TPU v7x, 256 devices: a whole 4x4x8 slice. The times are simulated.
256 devices in a mesh: seq: 64 (over z, x, core), heads: 4 (over y).
Axes of the slice: x: 4, y: 4, z: 8, core: 2. Of those that a mesh axis runs over, the one named last changes fastest.
Arguments:
- q_delta: bfloat16 [8192, 4096], P('seq', 'heads'), may hold values from -6 to 6
- k_delta: bfloat16 [8192, 4096], P('seq', 'heads'), may hold values from -6 to 6
- v_delta: bfloat16 [8192, 4096], P('seq', 'heads'), may hold values from -6 to 6
- decay: float32 [32, 8192], P('heads', 'seq'), may hold values from 0 to 2
- beta: float32 [32, 8192], P('heads', 'seq'), may hold values from 0 to 1
- gain: float32 [128], replicated, may hold values from 0.1 to 1.9
- attn_weight: bfloat16 [32, 128, 384], P('heads'), may hold values from -5 to 5
- out_weight: bfloat16 [4096, 4096], P('heads'), may hold values from -0.09375 to 0.09375
Outputs:
- block_out: bfloat16 [8192, 4096], P(('seq', 'heads'))
All inputs are finite; a program needn't handle non-finite values.
Results may differ from a plain program's by a relative error of at most 0.0142.
Values may be sent and summed in bfloat16 or wider, within the bound.
No kernel may reach another device: no remote copies, remote signals or barrier semaphores. Data moves between devices by JAX's collectives and lax.ppermute only.
A program may use at most 256 MiB of HBM per device.

v0:
```python
import jax
import jax.numpy as jnp
from jax import lax
from jax.sharding import PartitionSpec as P

WINDOW = 1024


def prefix_2(part, axis, combine, identity):
    place = lax.axis_index(axis)
    gathered = jax.tree.map(lambda a: lax.all_gather(a, axis), part)
    state = jax.tree.map(lambda a, e: jnp.zeros_like(a) + jnp.asarray(e, a.dtype), part, identity)

    def one(lap, state):
        return combine(
            state, jax.tree.map(lambda a: lax.dynamic_index_in_dim(a, lap, 0, False), gathered)
        )

    return lax.fori_loop(0, place, one, state)


def from_behind(block, axis, distance):
    devices = range(lax.axis_size(axis))
    route = [(i - distance, i) for i in devices if i - distance in devices]
    return lax.ppermute(block, axis, route)


def normalize(values, factor):
    return values * lax.rsqrt(jnp.sum(values * values, axis=-1, keepdims=True) + 1e-06) * factor


def matmul(pattern, left, right):
    return jnp.einsum(pattern, left, right, precision=lax.Precision.HIGHEST)


def sweep_state(initial, key_blocks, query_blocks, value_blocks, log_decay, strength, emit):
    block_rows = key_blocks.shape[2]
    line_position = lax.broadcasted_iota(jnp.int32, (block_rows, block_rows), 0)
    col_index = lax.broadcasted_iota(jnp.int32, (block_rows, block_rows), 1)
    lower_mask = line_position > col_index
    causal_mask = line_position >= col_index
    identity = jnp.eye(block_rows, dtype=jnp.float32)

    def step_forward(carried, segment_feed):
        current_keys, queries_now, values_now, logs_now, betas_now = segment_feed
        summed = jnp.cumsum(logs_now, axis=1)
        spread = summed[:, :, None] - summed[:, None, :]
        ratios = jnp.where(causal_mask, jnp.exp(jnp.where(causal_mask, spread, 0.0)), 0.0)
        intersection = matmul("htd,hsd->hts", current_keys, current_keys)
        lower_mix = jnp.where(lower_mask, ratios * intersection * betas_now[:, None, :], 0.0)
        decayed = jnp.exp(summed)[:, :, None]
        target = values_now - decayed * matmul("htd,hdw->htw", current_keys, carried)
        solved = jax.scipy.linalg.solve_triangular(
            identity + lower_mix, target, lower=True, unit_diagonal=True
        )
        tail_weight = jnp.exp(summed[:, -1:] - summed) * betas_now
        renewed = jnp.exp(summed[:, -1])[:, None, None] * carried + matmul(
            "hsd,hsw->hdw", current_keys, tail_weight[:, :, None] * solved
        )
        if emit:
            scored = (
                matmul("htd,hsd->hts", queries_now, current_keys) * ratios * betas_now[:, None, :]
            )
            result = decayed * matmul("htd,hdw->htw", queries_now, carried) + matmul(
                "hts,hsw->htw", scored, solved
            )
            return (renewed, result)
        return (renewed, None)

    return lax.scan(
        step_forward, initial, (key_blocks, query_blocks, value_blocks, log_decay, strength)
    )


def local(q_delta, k_delta, v_delta, decay, beta, gain, attn_weight, out_weight):
    length = q_delta.shape[0]
    heads_dev = attn_weight.shape[0]
    head_size = attn_weight.shape[1]
    block_rows = min(128, length)
    blocks = length // block_rows

    def by_heads(values):
        return values.astype(jnp.float32).reshape(length, heads_dev, head_size).transpose(1, 0, 2)

    def by_blocks(values):
        return values.reshape(heads_dev, blocks, block_rows, values.shape[-1]).transpose(1, 0, 2, 3)

    def per_block(values):
        return values.reshape(heads_dev, blocks, block_rows).transpose(1, 0, 2)

    probe_vectors = normalize(by_heads(q_delta), head_size ** (-0.5))
    key_rows = normalize(by_heads(k_delta), 1.0)
    values = by_heads(v_delta)
    log_decay = per_block(-decay)
    strength = per_block(beta)
    query_blocks = by_blocks(probe_vectors)
    key_blocks = by_blocks(key_rows)
    identity = jnp.broadcast_to(
        jnp.eye(head_size, dtype=jnp.float32), (heads_dev, head_size, head_size)
    )
    empty_state = jnp.zeros((heads_dev, head_size, head_size), jnp.float32)
    start_pair = jnp.concatenate([identity, empty_state], axis=-1)
    wide_values = by_blocks(jnp.concatenate([jnp.zeros_like(values), values], axis=-1))
    ending, unused = sweep_state(
        start_pair, key_blocks, query_blocks, wide_values, log_decay, strength, False
    )
    transition = ending[..., :head_size]
    local_state = ending[..., head_size:]

    def combine(earlier_tokens, later):
        return (
            matmul("hij,hjk->hik", later[0], earlier_tokens[0]),
            matmul("hij,hjk->hik", later[0], earlier_tokens[1]) + later[1],
        )

    prefix = prefix_2((transition, local_state), "seq", combine, (identity, empty_state))
    incoming = prefix[1]
    unused_state, direct = sweep_state(
        incoming, key_blocks, query_blocks, by_blocks(values), log_decay, strength, True
    )
    delta_out = direct.transpose(1, 0, 2, 3).reshape(heads_dev, length, head_size)
    normed = (
        delta_out
        * lax.rsqrt(jnp.mean(delta_out * delta_out, axis=-1, keepdims=True) + 1e-06)
        * gain
    ).astype(jnp.bfloat16)
    projected = jnp.einsum(
        "htd,hde->hte", normed, attn_weight, preferred_element_type=jnp.float32
    ).astype(jnp.bfloat16)
    query_two = projected[..., :head_size]
    key_two = projected[..., head_size : 2 * head_size]
    value_two = projected[..., 2 * head_size :]
    reach_devs = WINDOW // length
    received = [
        from_behind((key_two, value_two), "seq", offset) for offset in range(reach_devs, 0, -1)
    ]
    key_all = jnp.concatenate([shard_pair[0] for shard_pair in received] + [key_two], axis=1)
    value_all = jnp.concatenate([shard_pair[1] for shard_pair in received] + [value_two], axis=1)
    first_row = lax.axis_index("seq") * length
    query_block = min(512, length)
    key_span = query_block + WINDOW
    line_position = lax.broadcasted_iota(jnp.int32, (query_block, key_span), 0)
    col_index = lax.broadcasted_iota(jnp.int32, (query_block, key_span), 1)
    scores = jnp.einsum(
        "htd,hsd->hts", query_two, key_all, preferred_element_type=jnp.float32
    ) * head_size ** (-0.5)
    allowed = (
        (col_index > line_position)
        & (col_index <= line_position + WINDOW)
        & (col_index >= WINDOW - first_row - 0)
    )
    masked = jnp.where(allowed[None], scores, -1e30)
    row_maximum = jnp.max(masked, axis=-1, keepdims=True)
    raised = jnp.exp(masked - row_maximum)
    weights = (raised / jnp.sum(raised, axis=-1, keepdims=True)).astype(jnp.bfloat16)
    outputs = jnp.einsum(
        "hts,hsd->htd", weights, value_all, preferred_element_type=jnp.float32
    ).astype(jnp.bfloat16)
    flat_heads = outputs.transpose(1, 0, 2).reshape(length, heads_dev * head_size)
    return lax.psum_scatter(
        jnp.dot(flat_heads, out_weight, preferred_element_type=jnp.float32).astype(jnp.bfloat16),
        "heads",
        scatter_dimension=0,
        tiled=True,
    )


def solution(mesh):
    placed = (
        P("seq", "heads"),
        P("seq", "heads"),
        P("seq", "heads"),
        P("heads", "seq"),
        P("heads", "seq"),
        P(),
        P("heads", None, None),
        P("heads", None),
    )
    return jax.shard_map(
        local, mesh=mesh, in_specs=placed, out_specs=P(("seq", "heads"), None), check_vma=False
    )
```

profile of v0, /device:TPU:128, one launch (start us, length us, event | category | flops | bytes accessed | tf_op | source)
XLA Modules:
  0.0 647.1 jit_solution(2889973735242259828)
XLA Ops:
  11.2 2.5 fusion.22
  13.6 78.6 %custom-call.9 = f32[8,1,128,128]{2,3,1,0:T(8,128)S(1)} custom-call(f32[8,1,128,128]{3,2,1,0:T(8,128)S(1)} %fusion.22), custom_call_target="InvertDiagBlocksLowerTriangular" | custom-call | tf_op jit(solution)/shard_map/while/body/eval_jaxpr/jit(_solve_triangular)/vmap()/triangular_solve | solution.py:53
  99.0 138.9 %all-gather.5.cloned.1.call-done = f32[512,128,128]{2,1,0:T(8,128)} async-done(((f32[8,128,128]{2,1,0:T(8,128)}), f32[512,128,128]{2,1,0:T(8,128)}) %all-gather.5.cloned.1.call-update) | async-done | bytes 33554448 | tf_op jit(solution)/shard_map/all_gather | solution.py:11
  237.9 142.3 %all-gather.7.cloned.1.call-done = f32[512,128,128]{2,1,0:T(8,128)} async-done(((f32[8,128,128]{2,1,0:T(8,128)}), f32[512,128,128]{2,1,0:T(8,128)}) %all-gather.7.cloned.1.call-update) | async-done | bytes 33554448 | tf_op jit(solution)/shard_map/all_gather | solution.py:11
  380.2 61.8 %while.3 = (s32[]{:T(128)}, f32[8,128,128]{2,1,0:T(8,128)S(1)}, s32[]{:T(128)}, f32[64,8,128,128]{3,2,1,0:T(8,128)}, f32[64,8,128,128]{3,2,1,0:T(8,128)}, /*index=5*/s32[]{:T(128)}, s32[]{:T(128)}, s32[]{:T(128)}) while((s32[]{:T(128)}, f32[8,128,128]{2,1,0:T(8,128)S(1)}, s32[]{:T(128)}, f32[64,8,128,128]{3,2,1,0:T(8,128)}, ...), condition=%wide.region_4.5_spmd, body=%wide.region_3.4_spmd.sunk | while | flops 201457664 | bytes 3146871 | solution.py:19
  380.3 1.9 convolution_add_fusion.4
  382.2 1.9 convolution_add_fusion.4
  384.1 1.8 convolution_add_fusion.4
  386.1 1.9 convolution_add_fusion.4
  388.0 1.9 convolution_add_fusion.4
  389.9 1.9 convolution_add_fusion.4
  391.8 1.8 convolution_add_fusion.4
  393.8 1.9 convolution_add_fusion.4
  395.7 1.9 convolution_add_fusion.4
  397.6 1.8 convolution_add_fusion.4
  399.5 1.9 convolution_add_fusion.4
  401.5 1.9 convolution_add_fusion.4
  403.4 1.9 convolution_add_fusion.4
  405.3 1.8 convolution_add_fusion.4
  407.2 1.9 convolution_add_fusion.4
  409.2 1.9 convolution_add_fusion.4
  411.1 1.8 convolution_add_fusion.4
  413.0 1.9 convolution_add_fusion.4
  414.9 1.9 convolution_add_fusion.4
  416.9 1.9 convolution_add_fusion.4
  418.8 1.8 convolution_add_fusion.4
  420.7 1.9 convolution_add_fusion.4
  422.7 1.9 convolution_add_fusion.4
  424.6 1.8 convolution_add_fusion.4
  426.5 1.9 convolution_add_fusion.4
  428.4 1.9 convolution_add_fusion.4
  430.4 1.9 convolution_add_fusion.4
  432.3 1.8 convolution_add_fusion.4
  434.2 1.9 convolution_add_fusion.4
  436.1 1.9 convolution_add_fusion.4
  438.1 1.8 convolution_add_fusion.4
  440.0 1.9 convolution_add_fusion.4
  446.5 18.9 %collective-permute-start.8 = (bf16[8,128,128]{2,1,0:T(8,128)(2,1)S(1)}, bf16[8,128,128]{2,1,0:T(8,128)(2,1)S(1)}, u32[]{:S(2)}, u32[]{:S(2)}) collective-permute-start(bf16[8,128,128]{2,1,0:T(8,128)(2,1)S(1)} %get-tuple-element.125), channel_id=1, source_target_pairs={{0,32},{4,36},{8,40},{12,44},{16,48},{20,52},{24,56},{28,60},{32,6... | collective-permute-start | bytes 786440 | tf_op jit(solution)/shard_map/ppermute | solution.py:25
  465.3 15.8 %collective-permute-start.9 = (bf16[8,128,128]{2,1,0:T(8,128)(2,1)S(1)}, bf16[8,128,128]{2,1,0:T(8,128)(2,1)S(1)}, u32[]{:S(2)}, u32[]{:S(2)}) collective-permute-start(bf16[8,128,128]{2,1,0:T(8,128)(2,1)S(1)} %get-tuple-element.125), channel_id=1, source_target_pairs={{0,28},{4,32},{8,36},{12,40},{16,44},{20,48},{24,52},{28,56},{32,6... | collective-permute-start | bytes 786440 | tf_op jit(solution)/shard_map/ppermute | solution.py:25
  481.2 18.0 %collective-permute-start = (bf16[8,128,128]{2,1,0:T(8,128)(2,1)S(1)}, bf16[8,128,128]{2,1,0:T(8,128)(2,1)S(1)}, u32[]{:S(2)}, u32[]{:S(2)}) collective-permute-start(bf16[8,128,128]{2,1,0:T(8,128)(2,1)S(1)} %get-tuple-element.124), channel_id=1, source_target_pairs={{0,32},{4,36},{8,40},{12,44},{16,48},{20,52},{24,56},{28,60},{32,6... | collective-permute-start | bytes 786440 | tf_op jit(solution)/shard_map/ppermute | solution.py:25
  499.3 14.7 %collective-permute-start.10 = (bf16[8,128,128]{2,1,0:T(8,128)(2,1)S(1)}, bf16[8,128,128]{2,1,0:T(8,128)(2,1)S(1)}, u32[]{:S(2)}, u32[]{:S(2)}) collective-permute-start(bf16[8,128,128]{2,1,0:T(8,128)(2,1)S(1)} %get-tuple-element.125), channel_id=1, source_target_pairs={{0,24},{4,28},{8,32},{12,36},{16,40},{20,44},{24,48},{28,52},{32,5... | collective-permute-start | bytes 786440 | tf_op jit(solution)/shard_map/ppermute | solution.py:25
  514.1 1.9 collective-permute-start.11
  516.0 7.6 %collective-permute-start.12 = (bf16[8,128,128]{2,1,0:T(8,128)(2,1)S(1)}, bf16[8,128,128]{2,1,0:T(8,128)(2,1)S(1)}, u32[]{:S(2)}, u32[]{:S(2)}) collective-permute-start(bf16[8,128,128]{2,1,0:T(8,128)(2,1)S(1)} %get-tuple-element.125), channel_id=1, source_target_pairs={{0,16},{4,20},{8,24},{12,28},{16,32},{20,36},{24,40},{28,44},{32,4... | collective-permute-start | bytes 786440 | tf_op jit(solution)/shard_map/ppermute | solution.py:25
  523.6 1.9 collective-permute-start.13
  525.6 2.1 collective-permute-start.14
  527.8 3.5 collective-permute-start.15
  531.4 2.8 collective-permute-start.1
  534.2 8.1 %collective-permute-start.2 = (bf16[8,128,128]{2,1,0:T(8,128)(2,1)S(1)}, bf16[8,128,128]{2,1,0:T(8,128)(2,1)S(1)}, u32[]{:S(2)}, u32[]{:S(2)}) collective-permute-start(bf16[8,128,128]{2,1,0:T(8,128)(2,1)S(1)} %get-tuple-element.124), channel_id=1, source_target_pairs={{0,24},{4,28},{8,32},{12,36},{16,40},{20,44},{24,48},{28,52},{32,5... | collective-permute-start | bytes 786440 | tf_op jit(solution)/shard_map/ppermute | solution.py:25
  542.4 1.9 collective-permute-start.3
  544.4 3.0 collective-permute-done.14
  547.4 2.4 collective-permute-start.4
  549.8 1.5 collective-permute-done.15
  551.3 1.9 collective-permute-start.5
  553.3 4.1 collective-permute-start.6
  557.5 3.2 collective-permute-start.7
  560.8 1.7 collective-permute-done.4
  562.5 2.0 collective-permute-done.5
  564.6 16.5 %collective-permute-done.6 = bf16[8,128,128]{2,1,0:T(8,128)(2,1)S(1)} collective-permute-done((bf16[8,128,128]{2,1,0:T(8,128)(2,1)S(1)}, bf16[8,128,128]{2,1,0:T(8,128)(2,1)S(1)}, u32[]{:S(2)}, u32[]{:S(2)}) %collective-permute-start.6) | collective-permute-done | bytes 262176 | tf_op jit(solution)/shard_map/ppermute | solution.py:25
  581.1 4.8 collective-permute-done.7
  589.0 3.1 fusion.5
  592.2 3.5 exponential_reduce_fusion
  595.6 7.2 %fusion.23 = bf16[8,128,128]{1,2,0:T(8,128)(2,1)S(1)} fusion(bf16[8,1152,128]{2,1,0:T(8,128)(2,1)} %copy-done.5, f32[8,128]{1,0:T(8,128)S(1)} %exponential_reduce_fusion, f32[8,128,1152]{2,1,0:T(8,128)} %fusion.5), kind=kOutput, calls=%fused_computation.33 | convolution fusion | flops 305662080 | bytes 7344128 | tf_op jit(solution)/shard_map/hts,hsd->htd/dot_general | solution.py:156
  602.8 5.7 convolution_convert_fusion
  608.5 32.0 %reduce-scatter.2.cloned.1.call-done = bf16[32,4096]{1,0:T(8,128)(2,1)} async-done(((bf16[128,4096]{1,0:T(8,128)(2,1)}), bf16[32,4096]{1,0:T(8,128)(2,1)}) %reduce-scatter.2.cloned.1.call-update) | async-done | bytes 262160 | tf_op jit(solution)/shard_map/reduce_scatter | solution.py:160
  (112 shorter events, 20.6 us)
Async XLA Ops:
  6.5 439.4 %copy-start = (bf16[8,128,384]{2,1,0:T(8,128)(2,1)S(1)}, bf16[8,128,384]{2,1,0:T(8,128)(2,1)}, u32[]{:S(2)}) copy-start(bf16[8,128,384]{2,1,0:T(8,128)(2,1)} %param.16) | copy-start | bytes 2359300
  6.5 231.4 %all-gather.5.cloned.1.call-start = ((), (), s32[]{:S(2)}) async-start(), calls=%async_computation.2 | async-start | bytes 34078720 | tf_op jit(solution)/shard_map/all_gather | solution.py:11
  6.6 85.7 %copy-start.2 = (bf16[128,1024]{1,0:T(8,128)(2,1)S(1)}, bf16[128,1024]{1,0:T(8,128)(2,1)}, u32[]{:S(2)}) copy-start(bf16[128,1024]{1,0:T(8,128)(2,1)} %param.11) | copy-start | bytes 786436
  94.2 3.2 copy-start.4
  95.4 2.2 copy-start.6
  96.6 283.6 %all-gather.7.cloned.1.call-start = ((), (), s32[]{:S(2)}) async-start(), calls=%async_computation.3 | async-start | bytes 34078720 | tf_op jit(solution)/shard_map/all_gather | solution.py:11
  97.3 543.2 %reduce-scatter.2.cloned.1.call-start = ((), (), s32[]{:S(2)}) async-start(), calls=%async_computation.1 | async-start | bytes 1310720 | tf_op jit(solution)/shard_map/reduce_scatter | solution.py:160
  442.8 3.1 copy-start.7
  446.5 69.5 %collective-permute-start.8 = (bf16[8,128,128]{2,1,0:T(8,128)(2,1)S(1)}, bf16[8,128,128]{2,1,0:T(8,128)(2,1)S(1)}, u32[]{:S(2)}, u32[]{:S(2)}) collective-permute-start(bf16[8,128,128]{2,1,0:T(8,128)(2,1)S(1)} %get-tuple-element.125), channel_id=1, source_target_pairs={{0,32},{4,36},{8,40},{12,44},{16,48},{20,52},{24,56},{28,60},{32,6... | collective-permute-start | bytes 786440 | tf_op jit(solution)/shard_map/ppermute | solution.py:25
  465.3 60.2 %collective-permute-start.9 = (bf16[8,128,128]{2,1,0:T(8,128)(2,1)S(1)}, bf16[8,128,128]{2,1,0:T(8,128)(2,1)S(1)}, u32[]{:S(2)}, u32[]{:S(2)}) collective-permute-start(bf16[8,128,128]{2,1,0:T(8,128)(2,1)S(1)} %get-tuple-element.125), channel_id=1, source_target_pairs={{0,28},{4,32},{8,36},{12,40},{16,44},{20,48},{24,52},{28,56},{32,6... | collective-permute-start | bytes 786440 | tf_op jit(solution)/shard_map/ppermute | solution.py:25
  481.2 42.4 %collective-permute-start = (bf16[8,128,128]{2,1,0:T(8,128)(2,1)S(1)}, bf16[8,128,128]{2,1,0:T(8,128)(2,1)S(1)}, u32[]{:S(2)}, u32[]{:S(2)}) collective-permute-start(bf16[8,128,128]{2,1,0:T(8,128)(2,1)S(1)} %get-tuple-element.124), channel_id=1, source_target_pairs={{0,32},{4,36},{8,40},{12,44},{16,48},{20,52},{24,56},{28,60},{32,6... | collective-permute-start | bytes 786440 | tf_op jit(solution)/shard_map/ppermute | solution.py:25
  499.3 28.4 %collective-permute-start.10 = (bf16[8,128,128]{2,1,0:T(8,128)(2,1)S(1)}, bf16[8,128,128]{2,1,0:T(8,128)(2,1)S(1)}, u32[]{:S(2)}, u32[]{:S(2)}) collective-permute-start(bf16[8,128,128]{2,1,0:T(8,128)(2,1)S(1)} %get-tuple-element.125), channel_id=1, source_target_pairs={{0,24},{4,28},{8,32},{12,36},{16,40},{20,44},{24,48},{28,52},{32,5... | collective-permute-start | bytes 786440 | tf_op jit(solution)/shard_map/ppermute | solution.py:25
  514.1 17.3 %collective-permute-start.11 = (bf16[8,128,128]{2,1,0:T(8,128)(2,1)S(1)}, bf16[8,128,128]{2,1,0:T(8,128)(2,1)S(1)}, u32[]{:S(2)}, u32[]{:S(2)}) collective-permute-start(bf16[8,128,128]{2,1,0:T(8,128)(2,1)S(1)} %get-tuple-element.125), channel_id=1, source_target_pairs={{0,20},{4,24},{8,28},{12,32},{16,36},{20,40},{24,44},{28,48},{32,5... | collective-permute-start | bytes 786440 | tf_op jit(solution)/shard_map/ppermute | solution.py:25
  516.0 18.2 %collective-permute-start.12 = (bf16[8,128,128]{2,1,0:T(8,128)(2,1)S(1)}, bf16[8,128,128]{2,1,0:T(8,128)(2,1)S(1)}, u32[]{:S(2)}, u32[]{:S(2)}) collective-permute-start(bf16[8,128,128]{2,1,0:T(8,128)(2,1)S(1)} %get-tuple-element.125), channel_id=1, source_target_pairs={{0,16},{4,20},{8,24},{12,28},{16,32},{20,36},{24,40},{28,44},{32,4... | collective-permute-start | bytes 786440 | tf_op jit(solution)/shard_map/ppermute | solution.py:25
  523.6 18.8 %collective-permute-start.13 = (bf16[8,128,128]{2,1,0:T(8,128)(2,1)S(1)}, bf16[8,128,128]{2,1,0:T(8,128)(2,1)S(1)}, u32[]{:S(2)}, u32[]{:S(2)}) collective-permute-start(bf16[8,128,128]{2,1,0:T(8,128)(2,1)S(1)} %get-tuple-element.125), channel_id=1, source_target_pairs={{0,12},{4,16},{8,20},{12,24},{16,28},{20,32},{24,36},{28,40},{32,4... | collective-permute-start | bytes 786440 | tf_op jit(solution)/shard_map/ppermute | solution.py:25
  525.6 21.9 %collective-permute-start.14 = (bf16[8,128,128]{2,1,0:T(8,128)(2,1)S(1)}, bf16[8,128,128]{2,1,0:T(8,128)(2,1)S(1)}, u32[]{:S(2)}, u32[]{:S(2)}) collective-permute-start(bf16[8,128,128]{2,1,0:T(8,128)(2,1)S(1)} %get-tuple-element.125), channel_id=1, source_target_pairs={{0,8},{4,12},{8,16},{12,20},{16,24},{20,28},{24,32},{28,36},{32,40... | collective-permute-start | bytes 786440 | tf_op jit(solution)/shard_map/ppermute | solution.py:25
  527.8 23.5 %collective-permute-start.15 = (bf16[8,128,128]{2,1,0:T(8,128)(2,1)S(1)}, bf16[8,128,128]{2,1,0:T(8,128)(2,1)S(1)}, u32[]{:S(2)}, u32[]{:S(2)}) collective-permute-start(bf16[8,128,128]{2,1,0:T(8,128)(2,1)S(1)} %get-tuple-element.125), channel_id=1, source_target_pairs={{0,4},{4,8},{8,12},{12,16},{16,20},{20,24},{24,28},{28,32},{32,36}... | collective-permute-start | bytes 786440 | tf_op jit(solution)/shard_map/ppermute | solution.py:25
  531.4 21.9 %collective-permute-start.1 = (bf16[8,128,128]{2,1,0:T(8,128)(2,1)S(1)}, bf16[8,128,128]{2,1,0:T(8,128)(2,1)S(1)}, u32[]{:S(2)}, u32[]{:S(2)}) collective-permute-start(bf16[8,128,128]{2,1,0:T(8,128)(2,1)S(1)} %get-tuple-element.124), channel_id=1, source_target_pairs={{0,28},{4,32},{8,36},{12,40},{16,44},{20,48},{24,52},{28,56},{32,6... | collective-permute-start | bytes 786440 | tf_op jit(solution)/shard_map/ppermute | solution.py:25
  534.2 23.2 %collective-permute-start.2 = (bf16[8,128,128]{2,1,0:T(8,128)(2,1)S(1)}, bf16[8,128,128]{2,1,0:T(8,128)(2,1)S(1)}, u32[]{:S(2)}, u32[]{:S(2)}) collective-permute-start(bf16[8,128,128]{2,1,0:T(8,128)(2,1)S(1)} %get-tuple-element.124), channel_id=1, source_target_pairs={{0,24},{4,28},{8,32},{12,36},{16,40},{20,44},{24,48},{28,52},{32,5... | collective-permute-start | bytes 786440 | tf_op jit(solution)/shard_map/ppermute | solution.py:25
  542.4 18.3 %collective-permute-start.3 = (bf16[8,128,128]{2,1,0:T(8,128)(2,1)S(1)}, bf16[8,128,128]{2,1,0:T(8,128)(2,1)S(1)}, u32[]{:S(2)}, u32[]{:S(2)}) collective-permute-start(bf16[8,128,128]{2,1,0:T(8,128)(2,1)S(1)} %get-tuple-element.124), channel_id=1, source_target_pairs={{0,20},{4,24},{8,28},{12,32},{16,36},{20,40},{24,44},{28,48},{32,5... | collective-permute-start | bytes 786440 | tf_op jit(solution)/shard_map/ppermute | solution.py:25
  547.4 15.1 %collective-permute-start.4 = (bf16[8,128,128]{2,1,0:T(8,128)(2,1)S(1)}, bf16[8,128,128]{2,1,0:T(8,128)(2,1)S(1)}, u32[]{:S(2)}, u32[]{:S(2)}) collective-permute-start(bf16[8,128,128]{2,1,0:T(8,128)(2,1)S(1)} %get-tuple-element.124), channel_id=1, source_target_pairs={{0,16},{4,20},{8,24},{12,28},{16,32},{20,36},{24,40},{28,44},{32,4... | collective-permute-start | bytes 786440 | tf_op jit(solution)/shard_map/ppermute | solution.py:25
  551.3 13.3 %collective-permute-start.5 = (bf16[8,128,128]{2,1,0:T(8,128)(2,1)S(1)}, bf16[8,128,128]{2,1,0:T(8,128)(2,1)S(1)}, u32[]{:S(2)}, u32[]{:S(2)}) collective-permute-start(bf16[8,128,128]{2,1,0:T(8,128)(2,1)S(1)} %get-tuple-element.124), channel_id=1, source_target_pairs={{0,12},{4,16},{8,20},{12,24},{16,28},{20,32},{24,36},{28,40},{32,4... | collective-permute-start | bytes 786440 | tf_op jit(solution)/shard_map/ppermute | solution.py:25
  553.3 27.8 %collective-permute-start.6 = (bf16[8,128,128]{2,1,0:T(8,128)(2,1)S(1)}, bf16[8,128,128]{2,1,0:T(8,128)(2,1)S(1)}, u32[]{:S(2)}, u32[]{:S(2)}) collective-permute-start(bf16[8,128,128]{2,1,0:T(8,128)(2,1)S(1)} %get-tuple-element.124), channel_id=1, source_target_pairs={{0,8},{4,12},{8,16},{12,20},{16,24},{20,28},{24,32},{28,36},{32,40... | collective-permute-start | bytes 786440 | tf_op jit(solution)/shard_map/ppermute | solution.py:25
  557.5 28.4 %collective-permute-start.7 = (bf16[8,128,128]{2,1,0:T(8,128)(2,1)S(1)}, bf16[8,128,128]{2,1,0:T(8,128)(2,1)S(1)}, u32[]{:S(2)}, u32[]{:S(2)}) collective-permute-start(bf16[8,128,128]{2,1,0:T(8,128)(2,1)S(1)} %get-tuple-element.124), channel_id=1, source_target_pairs={{0,4},{4,8},{8,12},{12,16},{16,20},{20,24},{24,28},{28,32},{32,36}... | collective-permute-start | bytes 786440 | tf_op jit(solution)/shard_map/ppermute | solution.py:25
  586.1 1.4 copy-start.5
  587.5 1.5 copy-start.3
  602.8 37.8 %copy-start.1 = (bf16[8,128,384]{2,1,0:T(8,128)(2,1)S(1)}, bf16[8,128,384]{2,1,0:T(8,128)(2,1)}, u32[]{:S(2)}) copy-start(bf16[8,128,384]{2,1,0:T(8,128)(2,1)} %param.16) | copy-start | bytes 2359300
Sparse Core Ops, SparseCore 0:
  96.7 141.1 all-gather.4
  240.7 139.4 all-gather.6
  608.7 31.8 reduce-scatter.1
where the time goes:
time: 651 us; the launch traced here: 647 us
  waiting for transfers between devices  343 us (53%)
  starting transfers between devices  109 us (17%)
  matrix products  89.8 us (14%)
  other arithmetic  82.1 us (13%)
  between operations  13.7 us (2%)
  local copies, waits for them, and re-layouts  7.56 us (1%)
    all_gather x2, waiting for transfers between devices, prefix_2(): gathered = jax.tree.map(lambda a: lax.all_gather(a, axis), part)  281 us
    ppermute x16, starting transfers between devices, from_behind(): return lax.ppermute(block, axis, route)  109 us
    another operation x4, other arithmetic, step_forward(): jax.scipy.linalg.solve_triangular(identity + lower_mix, target, lower=Tru...  78.7 us
    dot_general x39, matrix products, matmul(): return jnp.einsum(pattern, left, right, precision=lax.Precision.HIGHEST)  67.9 us
    reduce_scatter x1, waiting for transfers between devices, local(): lax.psum_scatter(jnp.dot(flat_heads, out_weight, preferred_element_type=j...  32 us
    ppermute x16, waiting for transfers between devices, from_behind(): return lax.ppermute(block, axis, route)  29.5 us
  transfers between devices with their start and end apart: 19, of which 9 were waited for; matrix products, arithmetic and copies ran while one was open for 0% of the time, Pallas kernels for 0%

commit v1 on v0

v1 whole, which is shorter than its diff:
```python
import jax
import jax.numpy as jnp
from jax import lax
from jax.experimental import pallas as pl
from jax.experimental.pallas import tpu as pltpu
from jax.sharding import PartitionSpec as P

F32 = jnp.float32
BF16 = jnp.bfloat16
C = 128
PLANE = 8
PLANES = 8
BLK = 3 * C + 16
EPS = 1e-06
NEG = -1e30
VMEM_LIMIT = 48 * 1024 * 1024


def params():
    return pltpu.CompilerParams(vmem_limit_bytes=VMEM_LIMIT)


def cost(flops, nbytes, trans=0):
    return pl.CostEstimate(flops=int(flops), bytes_accessed=int(nbytes), transcendentals=int(trans))


def vmem():
    return pl.BlockSpec(memory_space=pltpu.VMEM)


def smem():
    return pl.BlockSpec(memory_space=pltpu.SMEM)


def split(a):
    hi = a.astype(BF16)
    lo = (a - hi.astype(F32)).astype(BF16)
    return hi, lo


def dot(a, b):
    return lax.dot_general(a, b, (((1,), (0,)), ((), ())), preferred_element_type=F32)


def dot_nt(a, b):
    return lax.dot_general(a, b, (((1,), (1,)), ((), ())), preferred_element_type=F32)


def dot_tn(a, b):
    return lax.dot_general(a, b, (((0,), (0,)), ((), ())), preferred_element_type=F32)


def mm(a, b):
    ah, al = split(a)
    bh, bl = split(b)
    return dot(ah, bh) + (dot(al, bh) + dot(ah, bl))


def mm_exact_right(a, b):
    ah, al = split(a)
    return dot(ah, b) + dot(al, b)


def iotas():
    row = lax.broadcasted_iota(jnp.int32, (C, C), 0)
    col = lax.broadcasted_iota(jnp.int32, (C, C), 1)
    return row, col


def pack_kernel(me_ref, q_ref, k_ref, v_ref, decay_ref, beta_ref, *rest):
    outs, scratch = rest[:PLANE], rest[PLANE]
    me = me_ref[0]

    def pieces(x):
        a = x.astype(BF16).astype(F32)
        b = (x - a).astype(BF16).astype(F32)
        c = ((x - a) - b).astype(BF16).astype(F32)
        return a, b, c

    for i, part in enumerate(pieces(decay_ref[...]) + pieces(beta_ref[...])):
        scratch[i] = part
    zeros = jnp.zeros((10, C), F32)
    for d in range(PLANE):
        head = jnp.bitwise_xor(me, d)
        cols = pl.ds(pl.multiple_of(head * C, C), C)
        out = outs[d]
        out[0:C, :] = k_ref[:, cols]
        out[C : 2 * C, :] = v_ref[:, cols]
        out[2 * C : 3 * C, :] = q_ref[:, cols]
        rows = [scratch[i, pl.ds(head, 1), :] for i in range(6)]
        out[3 * C :, :] = jnp.concatenate(rows + [zeros], axis=0).astype(BF16)


def pack(me, q, k, v, decay, beta):
    return pl.pallas_call(
        pack_kernel,
        out_shape=[jax.ShapeDtypeStruct((BLK, C), BF16)] * PLANE,
        in_specs=[smem()] + [vmem()] * 5,
        out_specs=[vmem()] * PLANE,
        scratch_shapes=[pltpu.VMEM((6, PLANE, C), F32)],
        compiler_params=params(),
        name="pack",
    )(me, q, k, v, decay, beta)


def gates(blocks):
    row, col = iotas()
    pieces = jnp.concatenate([b[3 * C :, :] for b in blocks], axis=0)
    upper = jnp.where(row <= col, 1.0, 0.0).astype(BF16)
    lower = jnp.where(row >= col, 1.0, 0.0).astype(BF16)
    eye = jnp.where(row == col, 1.0, 0.0).astype(BF16)
    along_row = dot(pieces, upper)
    along_col = dot_nt(jnp.concatenate([lower, eye], axis=0), pieces)
    plain = pieces.astype(F32)
    found = []
    for d in range(PLANE):
        o = 16 * d
        g_row = -(along_row[o : o + 1] + along_row[o + 1 : o + 2] + along_row[o + 2 : o + 3])
        b_row = plain[o + 3 : o + 4] + plain[o + 4 : o + 5] + plain[o + 5 : o + 6]
        g_col = -(
            along_col[:C, o : o + 1] + along_col[:C, o + 1 : o + 2] + along_col[:C, o + 2 : o + 3]
        )
        b_col = (
            along_col[C:, o + 3 : o + 4]
            + along_col[C:, o + 4 : o + 5]
            + along_col[C:, o + 5 : o + 6]
        )
        found.append((g_row, b_row, g_col, b_col))
    return found


def unit_lower_inverse(low, row, col):
    x = jnp.where(row == col, 1.0, 0.0) - jnp.where(
        (jnp.bitwise_xor(row, col) == 1) & (row > col), low, 0.0
    )
    size = 2
    while size < C:
        level = (row > col) & (jnp.bitwise_xor(row, col) >= size) & (
            jnp.bitwise_xor(row, col) < 2 * size
        )
        corner = jnp.where(level, low, 0.0)
        x = x - mm(mm(x, corner), x)
        size *= 2
    return x


def prep_kernel(me_ref, *refs):
    blocks = refs[:PLANE]
    mix_ref, wu_ref, ab_ref, level_ref = refs[PLANE : PLANE + 4]
    maps = refs[PLANE + 4]
    me = me_ref[0]
    row, col = iotas()
    eye = jnp.where(row == col, 1.0, 0.0)
    found = gates(blocks)
    for d in range(PLANE):
        g_row, b_row, g_col, b_col = found[d]
        keys = blocks[d][0:C, :]
        values = blocks[d][C : 2 * C, :]
        gram = dot_nt(keys, keys)
        diag = gram * eye
        r_col = lax.rsqrt(jnp.sum(diag, axis=1, keepdims=True) + EPS)
        r_row = lax.rsqrt(jnp.sum(diag, axis=0, keepdims=True) + EPS)
        ratio = jnp.where(row >= col, jnp.exp(jnp.minimum(g_col - g_row, 0.0)), 0.0)
        mix = ratio * (b_row * r_row)
        mix_ref[d] = mix
        low = jnp.where(row > col, mix * gram * r_col, 0.0)
        inverse = unit_lower_inverse(low, row, col)
        w = mm_exact_right(inverse * (jnp.exp(g_row) * r_row), keys)
        u = mm_exact_right(inverse, values)
        wu = jnp.concatenate([w, u], axis=1)
        wu_ref[d] = wu
        g_end = g_row[:, C - 1 : C]
        tail = jnp.exp(g_end - g_col) * b_col * r_col
        hi, lo = split(wu * tail)
        made = dot_tn(keys, hi) + dot_tn(keys, lo)
        chunk = jnp.bitwise_xor(me, d)
        maps[chunk] = jnp.concatenate([eye * jnp.exp(g_end) - made[:, :C], made[:, C:]], axis=1)

    def after(earlier, later):
        both = mm(later[:, :C], earlier)
        return jnp.concatenate([both[:, :C], both[:, C:] + later[:, C:]], axis=1)

    one = [maps[i] for i in range(PLANE)]
    two = [after(one[2 * i], one[2 * i + 1]) for i in range(4)]
    four = [after(two[2 * i], two[2 * i + 1]) for i in range(2)]
    ab_ref[...] = after(four[0], four[1])
    level_ref[0] = one[0]
    level_ref[1] = two[0]
    level_ref[2] = one[2]
    level_ref[3] = four[0]
    level_ref[4] = one[4]
    level_ref[5] = two[2]
    level_ref[6] = one[6]


def prep(me, blocks):
    return pl.pallas_call(
        prep_kernel,
        out_shape=[
            jax.ShapeDtypeStruct((PLANE, C, C), F32),
            jax.ShapeDtypeStruct((PLANE, C, 2 * C), F32),
            jax.ShapeDtypeStruct((C, 2 * C), F32),
            jax.ShapeDtypeStruct((7, C, 2 * C), F32),
        ],
        in_specs=[smem()] + [vmem()] * PLANE,
        out_specs=[vmem()] * 4,
        scratch_shapes=[pltpu.VMEM((PLANE, C, 2 * C), F32)],
        compiler_params=params(),
        cost_estimate=cost(2e9, 4e6),
        name="prep",
    )(me, *blocks)


def query_kernel(me_ref, *refs):
    blocks = refs[:PLANE]
    mix_ref, wu_ref, level_ref, no_ref, before = refs[PLANE:]
    me = me_ref[0]
    row, col = iotas()
    eye = jnp.where(row == col, 1.0, 0.0)

    def after(earlier, later):
        both = mm(later[:, :C], earlier)
        return jnp.concatenate([both[:, :C], both[:, C:] + later[:, C:]], axis=1)

    before[0] = jnp.concatenate([eye, jnp.zeros((C, C), F32)], axis=1)
    before[1] = level_ref[0]
    before[2] = level_ref[1]
    before[3] = after(level_ref[1], level_ref[2])
    before[4] = level_ref[3]
    before[5] = after(level_ref[3], level_ref[4])
    six = after(level_ref[3], level_ref[5])
    before[6] = six
    before[7] = after(six, level_ref[6])
    found = gates(blocks)
    for d in range(PLANE):
        g_row, b_row, g_col, b_col = found[d]
        keys = blocks[d][0:C, :]
        queries = blocks[d][2 * C : 3 * C, :]
        wide = queries.astype(F32)
        r_col = lax.rsqrt(jnp.sum(wide * wide, axis=1, keepdims=True) + EPS) * (C**-0.5)
        scored = dot_nt(queries, keys) * r_col * mix_ref[d]
        part = mm(scored, wu_ref[d])
        reach = wide * (r_col * jnp.exp(g_col)) - part[:, :C]
        chunk = jnp.bitwise_xor(me, d)
        both = mm(reach, before[chunk])
        rows = pl.ds(pl.multiple_of(chunk * C, C), C)
        no_ref[rows, :] = jnp.concatenate([both[:, :C], both[:, C:] + part[:, C:]], axis=1)


def query(me, blocks, mix, wu, level):
    return pl.pallas_call(
        query_kernel,
        out_shape=jax.ShapeDtypeStruct((PLANE * C, 2 * C), F32),
        in_specs=[smem()] + [vmem()] * (PLANE + 3),
        out_specs=vmem(),
        scratch_shapes=[pltpu.VMEM((PLANE, C, 2 * C), F32)],
        compiler_params=params(),
        cost_estimate=cost(1e9, 4e6),
        name="query",
    )(me, *blocks, mix, wu, level)


def norm_kernel(no_ref, gain_ref, *refs):
    maps, normed_ref = refs[:-1], refs[-1]
    state = maps[-1][:, C:]
    for ab in reversed(maps[:-1]):
        state = mm(ab[:, :C], state) + ab[:, C:]
    out = mm(no_ref[:, :C], state) + no_ref[:, C:]
    scale = lax.rsqrt(jnp.mean(out * out, axis=1, keepdims=True) + EPS)
    normed_ref[...] = (out * scale * gain_ref[...]).astype(BF16)


def norm(no, gain, maps):
    return pl.pallas_call(
        norm_kernel,
        out_shape=jax.ShapeDtypeStruct((PLANE * C, C), BF16),
        in_specs=[vmem()] * (2 + len(maps)),
        out_specs=vmem(),
        compiler_params=params(),
        cost_estimate=cost(2e8, 2e6),
        name="norm",
    )(no, gain, *maps)


QB = 256


def own_kernel(me_ref, normed_ref, weight_ref, acc_ref, stat_ref, q2_ref):
    proj = dot(normed_ref[...], weight_ref[0]).astype(BF16)
    q2_ref[...] = proj[:, :C]
    row = lax.broadcasted_iota(jnp.int32, (QB, QB), 0)
    col = lax.broadcasted_iota(jnp.int32, (QB, QB), 1)
    for i in range(PLANE * C // QB):
        at = i * QB
        q = proj[at : at + QB, :C]
        s = dot_nt(q, proj[: at + QB, C : 2 * C]) * (C**-0.5)
        last = jnp.where(col <= row, s[:, at:], NEG)
        s = last if i == 0 else jnp.concatenate([s[:, :at], last], axis=1)
        top = jnp.max(s, axis=1, keepdims=True)
        p = jnp.exp(s - top)
        total = jnp.sum(p, axis=1, keepdims=True)
        acc_ref[at : at + QB, :] = dot(p.astype(BF16), proj[: at + QB, 2 * C :])
        stat_ref[0, at : at + QB, :] = jnp.broadcast_to(top, (QB, C))
        stat_ref[1, at : at + QB, :] = jnp.broadcast_to(total, (QB, C))


def own(me, normed, weight):
    n = PLANE * C
    return pl.pallas_call(
        own_kernel,
        out_shape=[
            jax.ShapeDtypeStruct((n, C), F32),
            jax.ShapeDtypeStruct((2, n, C), F32),
            jax.ShapeDtypeStruct((n, C), BF16),
        ],
        grid_spec=pltpu.PrefetchScalarGridSpec(
            num_scalar_prefetch=1,
            grid=(1,),
            in_specs=[
                pl.BlockSpec((n, C), lambda i, me: (0, 0)),
                pl.BlockSpec((1, C, 3 * C), lambda i, me: (me[0], 0, 0)),
            ],
            out_specs=[
                pl.BlockSpec((n, C), lambda i, me: (0, 0)),
                pl.BlockSpec((2, n, C), lambda i, me: (0, 0, 0)),
                pl.BlockSpec((n, C), lambda i, me: (0, 0)),
            ],
        ),
        compiler_params=params(),
        cost_estimate=cost(1e9, 3e6, 6e5),
        name="own",
    )(me, normed, weight)


def halo_kernel(me_ref, halo_ref, weight_ref, acc_ref, stat_ref, q2_ref, *refs):
    outs, attended = refs[:PLANE], refs[PLANE]
    me, plane = me_ref[0], me_ref[1]
    proj = dot(halo_ref[...], weight_ref[0, :, C:]).astype(BF16)
    n = PLANE * C
    for i in range(n // QB):
        at = i * QB
        row = lax.broadcasted_iota(jnp.int32, (QB, n - at), 0)
        col = lax.broadcasted_iota(jnp.int32, (QB, n - at), 1)
        allowed = (col > row) & (plane > 0)
        s = dot_nt(q2_ref[at : at + QB, :], proj[at:, :C]) * (C**-0.5)
        s = jnp.where(allowed, s, NEG)
        before = stat_ref[0, at : at + QB, 0:1]
        top = jnp.maximum(jnp.max(s, axis=1, keepdims=True), before)
        p = jnp.where(allowed, jnp.exp(s - top), 0.0)
        keep = jnp.exp(before - top)
        total = jnp.sum(p, axis=1, keepdims=True) + keep * stat_ref[1, at : at + QB, 0:1]
        acc = acc_ref[at : at + QB, :] * keep + dot(p.astype(BF16), proj[at:, C:])
        attended[at : at + QB, :] = (acc / total).astype(BF16)
    for d in range(PLANE):
        chunk = jnp.bitwise_xor(me, d)
        outs[d][...] = attended[pl.ds(pl.multiple_of(chunk * C, C), C), :]


def halo_part(me, halo, weight, acc, stat, q2):
    n = PLANE * C
    return pl.pallas_call(
        halo_kernel,
        out_shape=[jax.ShapeDtypeStruct((C, C), BF16)] * PLANE,
        grid_spec=pltpu.PrefetchScalarGridSpec(
            num_scalar_prefetch=1,
            grid=(1,),
            in_specs=[
                pl.BlockSpec((n, C), lambda i, me: (0, 0)),
                pl.BlockSpec((1, C, 3 * C), lambda i, me: (me[0], 0, 0)),
                pl.BlockSpec((n, C), lambda i, me: (0, 0)),
                pl.BlockSpec((2, n, C), lambda i, me: (0, 0, 0)),
                pl.BlockSpec((n, C), lambda i, me: (0, 0)),
            ],
            out_specs=[pl.BlockSpec((C, C), lambda i, me: (0, 0))] * PLANE,
            scratch_shapes=[pltpu.VMEM((n, C), BF16)],
        ),
        compiler_params=params(),
        cost_estimate=cost(1e9, 3e6, 6e5),
        name="halo",
    )(me, halo, weight, acc, stat, q2)


COLS = 512


def project_kernel(me_ref, *refs):
    blocks = refs[:PLANE]
    weight_ref = refs[PLANE]
    outs = refs[PLANE + 1 : PLANE + 5]
    flat = refs[PLANE + 5]
    me, mine = me_ref[0], me_ref[2]

    @pl.when(pl.program_id(0) == 0)
    def _():
        for d in range(PLANE):
            head = jnp.bitwise_xor(me, d)
            cols = pl.ds(pl.multiple_of(head * C, C), C)
            for e in range(4):
                rows = pl.ds(pl.multiple_of(jnp.bitwise_xor(mine, e) * 32, 32), 32)
                flat[e * 32 : e * 32 + 32, cols] = blocks[d][rows, :]

    got = dot(flat[...], weight_ref[...])
    for e in range(4):
        outs[e][...] = got[e * 32 : e * 32 + 32].astype(outs[e].dtype)


def project(me, blocks, weight):
    depth, width = weight.shape
    return pl.pallas_call(
        project_kernel,
        out_shape=[jax.ShapeDtypeStruct((32, width), F32)]
        + [jax.ShapeDtypeStruct((32, width), BF16)] * 3,
        grid_spec=pltpu.PrefetchScalarGridSpec(
            num_scalar_prefetch=1,
            grid=(width // COLS,),
            in_specs=[pl.BlockSpec((C, C), lambda i, me: (0, 0))] * PLANE
            + [pl.BlockSpec((depth, COLS), lambda i, me: (0, i))],
            out_specs=[pl.BlockSpec((32, COLS), lambda i, me: (0, i))] * 4,
            scratch_shapes=[pltpu.VMEM((C, depth), BF16)],
        ),
        compiler_params=params(),
        cost_estimate=cost(1e9, 9e6),
        name="project",
    )(me, *blocks, weight)


def exchange(blocks):
    moved = [blocks[0]]
    for d in range(1, PLANE):
        route = [(s, s ^ d) for s in range(PLANE * PLANES)]
        moved.append(lax.ppermute(blocks[d], "seq", route))
    return moved


def later_plane(block, distance):
    n = PLANE * PLANES
    step = PLANE * distance
    return lax.ppermute(block, "seq", [(s, s + step) for s in range(n - step)])


def local(q_delta, k_delta, v_delta, decay, beta, gain, attn_weight, out_weight):
    place = lax.axis_index("seq")
    mine = lax.axis_index("heads")
    me = jnp.stack([place % PLANE, place // PLANE, mine]).astype(jnp.int32)
    blocks = exchange(pack(me, q_delta, k_delta, v_delta, decay, beta))
    mix, wu, ab, level = prep(me, blocks)
    maps = [later_plane(ab, distance) for distance in range(1, PLANES)]
    no = query(me, blocks, mix, wu, level)
    normed = norm(no, gain[None, :], maps)
    halo = later_plane(normed, 1)
    acc, stat, q2 = own(me, normed, attn_weight)
    attended = exchange(halo_part(me, halo, attn_weight, acc, stat, q2))
    sums = project(me, attended, out_weight)
    total = sums[0]
    for d in range(1, 4):
        got = lax.ppermute(sums[d], "heads", [(s, s ^ d) for s in range(4)])
        total = total + got.astype(F32)
    return total.astype(BF16)


def solution(mesh):
    placed = (
        P("seq", "heads"),
        P("seq", "heads"),
        P("seq", "heads"),
        P("heads", "seq"),
        P("heads", "seq"),
        P(),
        P("heads", None, None),
        P("heads", None),
    )
    return jax.shard_map(
        local, mesh=mesh, in_specs=placed, out_specs=P(("seq", "heads"), None), check_vma=False
    )
```

time: 651 us -> 131 us (0.20)
  waiting for transfers between devices: 343 us -> 32.6 us
  matrix products: 89.8 us -> 0 us
  other arithmetic: 82.1 us -> 0.89 us
  starting transfers between devices: 109 us -> 53.9 us
  Pallas kernels: 0 us -> 38.4 us
  between operations: 13.7 us -> 0.23 us
    all_gather x2 -> x0, waiting for transfers between devices: 281 us -> none  [prefix_2(): gathered = jax.tree.map(lambda a: lax.all_gather(a, axis), part)]
    dot_general x43 -> x0, matrix products: 84.3 us -> none  [the longest x39 67.9 us: matmul(): return jnp.einsum(pattern, left, right, precision=lax.Precision.HIGHEST)]
    another operation x5 -> x1, other arithmetic: 79 us -> 0.08 us  [local(): me = jnp.stack([place % PLANE, place // PLANE, mine]).astype(jnp.int32)]
    ppermute x16 -> x25, starting transfers between devices: 109 us -> 53.9 us  [the longest x8 32.8 us: later_plane(): return lax.ppermute(block, 'seq', [(s, s + step) for s in range(n - step)])]
    pallas_call x0 -> x7, Pallas kernels: none -> 38.4 us  [the longest x1 19.3 us: prep(): pl.pallas_call(prep_kernel, out_shape=[jax.ShapeDtypeStruct((PLANE, C, C)...]
    reduce_scatter x1 -> x0, waiting for transfers between devices: 32 us -> none  [local(): lax.psum_scatter(jnp.dot(flat_heads, out_weight, preferred_element_type=j...]
    ppermute x16 -> x25, waiting for transfers between devices: 29.5 us -> 32.6 us  [the longest x3 14.4 us: local(): got = lax.ppermute(sums[d], 'heads', [(s, s ^ d) for s in range(4)])]
  transfers between devices with their start and end apart: 19 -> 25, of which waited for: 9 -> 11; matrix products, arithmetic and copies ran while one was open for 0% -> 0% of each run, Pallas kernels for 0% -> 5%
where the time goes in v1:
time: 131 us; the launch traced here: 130 us
  starting transfers between devices  53.9 us (41%)
  Pallas kernels  38.4 us (29%)
  waiting for transfers between devices  32.6 us (25%)
  local copies, waits for them, and re-layouts  4.23 us (3%)
    ppermute x8, starting transfers between devices, later_plane(): return lax.ppermute(block, 'seq', [(s, s + step) for s in range(n - step)])  32.8 us
    pallas_call x1, Pallas kernels, prep(): pl.pallas_call(prep_kernel, out_shape=[jax.ShapeDtypeStruct((PLANE, C, C)...  19.3 us
    ppermute x14, starting transfers between devices, exchange(): moved.append(lax.ppermute(blocks[d], 'seq', route))  16.4 us
    ppermute x3, waiting for transfers between devices, local(): got = lax.ppermute(sums[d], 'heads', [(s, s ^ d) for s in range(4)])  14.4 us
    ppermute x14, waiting for transfers between devices, exchange(): moved.append(lax.ppermute(blocks[d], 'seq', route))  12.4 us
    pallas_call x1, Pallas kernels, project(): pl.pallas_call(project_kernel, out_shape=[jax.ShapeDtypeStruct((32, width...  7.52 us
    ppermute x8, waiting for transfers between devices, later_plane(): return lax.ppermute(block, 'seq', [(s, s + step) for s in range(n - step)])  5.82 us
    ppermute x3, starting transfers between devices, local(): got = lax.ppermute(sums[d], 'heads', [(s, s ^ d) for s in range(4)])  4.79 us
  transfers between devices with their start and end apart: 25, of which 11 were waited for; matrix products, arithmetic and copies ran while one was open for 0% of the time, Pallas kernels for 5%

profile of v1, /device:TPU:128, one launch (start us, length us, event | category | flops | bytes accessed | tf_op | source)
XLA Modules:
  0.0 130.3 jit_solution(11508391313991567400)
XLA Ops:
  0.0 0.1 pad_add_fusion.me_ref
  0.1 0.9 copy-done
  1.0 0.9 copy-done.1
  2.0 0.9 copy-done.2
  2.9 0.7 copy-done.3
  3.6 0.7 copy-done.4
  4.3 0.8 pack.1
  5.1 0.1 collective-permute-start
  5.2 1.6 %collective-permute-start.1 = (bf16[400,128]{1,0:T(8,128)(2,1)S(1)}, bf16[400,128]{1,0:T(8,128)(2,1)S(1)}, u32[]{:S(2)}, u32[]{:S(2)}) collective-permute-start(bf16[400,128]{1,0:T(8,128)(2,1)S(1)} %get-tuple-element.34), channel_id=1, source_target_pairs={{0,8},{4,12},{8,0},{12,4},{16,24},{20,28},{24,16},{28,20},{32,40},... | collective-permute-start | bytes 307208 | tf_op jit(solution)/shard_map/ppermute | solution.py:431
  6.8 0.3 collective-permute-start.2
  7.0 3.0 %collective-permute-start.3 = (bf16[400,128]{1,0:T(8,128)(2,1)S(1)}, bf16[400,128]{1,0:T(8,128)(2,1)S(1)}, u32[]{:S(2)}, u32[]{:S(2)}) collective-permute-start(bf16[400,128]{1,0:T(8,128)(2,1)S(1)} %get-tuple-element.36), channel_id=1, source_target_pairs={{0,16},{4,20},{8,24},{12,28},{16,0},{20,4},{24,8},{28,12},{32,48},... | collective-permute-start | bytes 307208 | tf_op jit(solution)/shard_map/ppermute | solution.py:431
  10.1 0.2 collective-permute-start.4
  10.3 0.0 collective-permute-done.refs_1_
  10.3 2.8 %collective-permute-start.5 = (bf16[400,128]{1,0:T(8,128)(2,1)S(1)}, bf16[400,128]{1,0:T(8,128)(2,1)S(1)}, u32[]{:S(2)}, u32[]{:S(2)}) collective-permute-start(bf16[400,128]{1,0:T(8,128)(2,1)S(1)} %get-tuple-element.38), channel_id=1, source_target_pairs={{0,24},{4,28},{8,16},{12,20},{16,8},{20,12},{24,0},{28,4},{32,56},... | collective-permute-start | bytes 307208 | tf_op jit(solution)/shard_map/ppermute | solution.py:431
  13.0 0.0 collective-permute-done.1.refs_2_
  13.0 0.2 collective-permute-start.6
  13.3 0.0 collective-permute-done.2.refs_3_
  13.3 4.4 %collective-permute-done.3.refs_4_ = bf16[400,128]{1,0:T(8,128)(2,1)S(1)} collective-permute-done((bf16[400,128]{1,0:T(8,128)(2,1)S(1)}, bf16[400,128]{1,0:T(8,128)(2,1)S(1)}, u32[]{:S(2)}, u32[]{:S(2)}) %collective-permute-start.3) | collective-permute-done | bytes 102432 | tf_op jit(solution)/shard_map/ppermute | solution.py:431
  17.6 1.2 collective-permute-done.4.refs_5_
  18.9 2.4 %collective-permute-done.5.refs_6_ = bf16[400,128]{1,0:T(8,128)(2,1)S(1)} collective-permute-done((bf16[400,128]{1,0:T(8,128)(2,1)S(1)}, bf16[400,128]{1,0:T(8,128)(2,1)S(1)}, u32[]{:S(2)}, u32[]{:S(2)}) %collective-permute-start.5) | collective-permute-done | bytes 102432 | tf_op jit(solution)/shard_map/ppermute | solution.py:431
  21.3 1.7 %collective-permute-done.6.refs_7_ = bf16[400,128]{1,0:T(8,128)(2,1)S(1)} collective-permute-done((bf16[400,128]{1,0:T(8,128)(2,1)S(1)}, bf16[400,128]{1,0:T(8,128)(2,1)S(1)}, u32[]{:S(2)}, u32[]{:S(2)}) %collective-permute-start.6) | collective-permute-done | bytes 102432 | tf_op jit(solution)/shard_map/ppermute | solution.py:431
  23.0 19.3 %prep.1 = (f32[8,128,128]{2,1,0:T(8,128)S(1)}, f32[8,128,256]{2,1,0:T(8,128)S(1)}, f32[128,256]{1,0:T(8,128)S(1)}, f32[7,128,256]{2,1,0:T(8,128)S(1)}) custom-call(s32[3]{0:T(128)S(1)} %pad_add_fusion.me_ref, bf16[400,128]{1,0:T(8,128)(2,1)S(1)} %get-tuple-element.32.refs_0_, bf16[400,128]{1,0:T(8,128)(2,1)S(1)} %collective-permute-done.refs_1_, ...), custom_call_target="tpu_custom_call" | custom-call | flops 2000000000 | bytes 4000000 | tf_op jit(solution)/shard_map/prep/pallas_call | solution.py:197
  42.3 0.7 collective-permute-start.13
  43.0 0.7 collective-permute-start.12
  43.6 0.7 collective-permute-start.11
  44.3 1.3 collective-permute-start.10
  45.6 5.7 %collective-permute-start.9 = (f32[128,256]{1,0:T(8,128)S(1)}, f32[128,256]{1,0:T(8,128)S(1)}, u32[]{:S(2)}, u32[]{:S(2)}) collective-permute-start(f32[128,256]{1,0:T(8,128)S(1)} %get-tuple-element.43), channel_id=1, source_target_pairs={{0,96},{4,100},{8,104},{12,108},{16,112},{20,116},{24,120},{28,124... | collective-permute-start | bytes 393224 | tf_op jit(solution)/shard_map/ppermute | solution.py:438
  51.3 0.0 collective-permute-done.13.refs_6_
  51.3 1.9 %collective-permute-start.8 = (f32[128,256]{1,0:T(8,128)S(1)}, f32[128,256]{1,0:T(8,128)S(1)}, u32[]{:S(2)}, u32[]{:S(2)}) collective-permute-start(f32[128,256]{1,0:T(8,128)S(1)} %get-tuple-element.43), channel_id=1, source_target_pairs={{0,64},{4,68},{8,72},{12,76},{16,80},{20,84},{24,88},{28,92},{32,9... | collective-permute-start | bytes 393224 | tf_op jit(solution)/shard_map/ppermute | solution.py:438
  53.3 0.0 collective-permute-done.12.refs_5_
  53.3 19.0 %collective-permute-start.7 = (f32[128,256]{1,0:T(8,128)S(1)}, f32[128,256]{1,0:T(8,128)S(1)}, u32[]{:S(2)}, u32[]{:S(2)}) collective-permute-start(f32[128,256]{1,0:T(8,128)S(1)} %get-tuple-element.43), channel_id=1, source_target_pairs={{0,32},{4,36},{8,40},{12,44},{16,48},{20,52},{24,56},{28,60},{32,6... | collective-permute-start | bytes 393224 | tf_op jit(solution)/shard_map/ppermute | solution.py:438
  72.3 3.7 %query.1.no_ref = f32[1024,256]{1,0:T(8,128)S(1)} custom-call(s32[3]{0:T(128)S(1)} %pad_add_fusion.me_ref, bf16[400,128]{1,0:T(8,128)(2,1)S(1)} %get-tuple-element.32.refs_0_, bf16[400,128]{1,0:T(8,128)(2,1)S(1)} %collective-permute-done.refs_1_, bf16[400,128]{1,0:T(8,128)(2,1)S(1)} %collective-permute-done.1.refs_2_, ...), custom_call_target="tpu_custom_call" | custom-call | flops 1000000000 | bytes 4000000 | tf_op jit(solution)/shard_map/query/pallas_call | solution.py:251
  76.0 0.0 collective-permute-done.11.refs_4_
  76.0 0.0 collective-permute-done.10.refs_3_
  76.0 0.0 collective-permute-done.9.refs_2_
  76.0 0.0 collective-permute-done.8.refs_1_
  76.0 0.0 collective-permute-done.7.refs_0_
  76.1 1.5 %norm.1.normed_ref = bf16[1024,128]{1,0:T(8,128)(2,1)S(1)} custom-call(f32[1024,256]{1,0:T(8,128)S(1)} %query.1.no_ref, f32[1,128]{1,0:T(1,128)S(1)} %bitcast.4, f32[128,256]{1,0:T(8,128)S(1)} %collective-permute-done.7.refs_0_, f32[128,256]{1,0:T(8,128)S(1)} %collective-permute-done.8.refs_1_, f32[128,256]{1,0:T(8,128)S(1)} %collective-permute-done.9.refs_2_, ...), custom_call_target="tpu_custom_call" | custom-call | flops 200000000 | bytes 2000000 | tf_op jit(solution)/shard_map/norm/pallas_call | solution.py:274
  77.6 2.9 %collective-permute-start.14 = (bf16[1024,128]{1,0:T(8,128)(2,1)S(1)}, bf16[1024,128]{1,0:T(8,128)(2,1)S(1)}, u32[]{:S(2)}, u32[]{:S(2)}) collective-permute-start(bf16[1024,128]{1,0:T(8,128)(2,1)S(1)} %norm.1.normed_ref), channel_id=1, source_target_pairs={{0,32},{4,36},{8,40},{12,44},{16,48},{20,52},{24,56},{28,60},{32,6... | collective-permute-start | bytes 786440 | tf_op jit(solution)/shard_map/ppermute | solution.py:438
  80.5 2.4 %own.1 = (f32[1024,128]{1,0:T(8,128)S(1)}, f32[2,1024,128]{2,1,0:T(8,128)S(1)}, bf16[1024,128]{1,0:T(8,128)(2,1)S(1)}) custom-call(s32[3]{0:T(128)S(1)} %pad_add_fusion.me_ref, bf16[1024,128]{1,0:T(8,128)(2,1)S(1)} %norm.1.normed_ref, bf16[8,128,384]{2,1,0:T(8,128)(2,1)S(1)} %copy-done.6), custom_call_target="tpu_custom_call" | custom-call | flops 1000000000 | bytes 3000000 | tf_op jit(solution)/shard_map/own/pallas_call | solution.py:309
  82.9 5.8 %collective-permute-done.14.halo_ref = bf16[1024,128]{1,0:T(8,128)(2,1)S(1)} collective-permute-done((bf16[1024,128]{1,0:T(8,128)(2,1)S(1)}, bf16[1024,128]{1,0:T(8,128)(2,1)S(1)}, u32[]{:S(2)}, u32[]{:S(2)}) %collective-permute-start.14) | collective-permute-done | bytes 262176 | tf_op jit(solution)/shard_map/ppermute | solution.py:438
  88.7 3.1 %halo.1 = (bf16[128,128]{1,0:T(8,128)(2,1)S(1)}, bf16[128,128]{1,0:T(8,128)(2,1)S(1)}, bf16[128,128]{1,0:T(8,128)(2,1)S(1)}, bf16[128,128]{1,0:T(8,128)(2,1)S(1)...) custom-call(s32[3]{0:T(128)S(1)} %pad_add_fusion.me_ref, ...), custom_call_target="tpu_custom_call" | custom-call | flops 1000000000 | bytes 3000000 | tf_op jit(solution)/shard_map/halo/pallas_call | solution.py:361
  91.8 0.1 collective-permute-start.15
  92.0 0.3 collective-permute-start.16
  92.3 1.5 %collective-permute-start.17 = (bf16[128,128]{1,0:T(8,128)(2,1)S(1)}, bf16[128,128]{1,0:T(8,128)(2,1)S(1)}, u32[]{:S(2)}, u32[]{:S(2)}) collective-permute-start(bf16[128,128]{1,0:T(8,128)(2,1)S(1)} %get-tuple-element.50), channel_id=1, source_target_pairs={{0,12},{4,8},{8,4},{12,0},{16,28},{20,24},{24,20},{28,16},{32,44},... | collective-permute-start | bytes 98312 | tf_op jit(solution)/shard_map/ppermute | solution.py:431
  93.8 1.5 %collective-permute-start.18 = (bf16[128,128]{1,0:T(8,128)(2,1)S(1)}, bf16[128,128]{1,0:T(8,128)(2,1)S(1)}, u32[]{:S(2)}, u32[]{:S(2)}) collective-permute-start(bf16[128,128]{1,0:T(8,128)(2,1)S(1)} %get-tuple-element.51), channel_id=1, source_target_pairs={{0,16},{4,20},{8,24},{12,28},{16,0},{20,4},{24,8},{28,12},{32,48},... | collective-permute-start | bytes 98312 | tf_op jit(solution)/shard_map/ppermute | solution.py:431
  95.3 1.8 %collective-permute-start.19 = (bf16[128,128]{1,0:T(8,128)(2,1)S(1)}, bf16[128,128]{1,0:T(8,128)(2,1)S(1)}, u32[]{:S(2)}, u32[]{:S(2)}) collective-permute-start(bf16[128,128]{1,0:T(8,128)(2,1)S(1)} %get-tuple-element.52), channel_id=1, source_target_pairs={{0,20},{4,16},{8,28},{12,24},{16,4},{20,0},{24,12},{28,8},{32,52},... | collective-permute-start | bytes 98312 | tf_op jit(solution)/shard_map/ppermute | solution.py:431
  97.0 0.0 collective-permute-done.15.refs_1_
  97.0 1.1 collective-permute-start.20
  98.2 0.0 collective-permute-done.16.refs_2_
  98.2 1.9 %collective-permute-start.21 = (bf16[128,128]{1,0:T(8,128)(2,1)S(1)}, bf16[128,128]{1,0:T(8,128)(2,1)S(1)}, u32[]{:S(2)}, u32[]{:S(2)}) collective-permute-start(bf16[128,128]{1,0:T(8,128)(2,1)S(1)} %get-tuple-element.54), channel_id=1, source_target_pairs={{0,28},{4,24},{8,20},{12,16},{16,12},{20,8},{24,4},{28,0},{32,60},... | collective-permute-start | bytes 98312 | tf_op jit(solution)/shard_map/ppermute | solution.py:431
  100.0 0.0 collective-permute-done.17.refs_3_
  100.1 0.0 collective-permute-done.18.refs_4_
  100.1 0.2 collective-permute-done.19.refs_5_
  100.2 1.9 %collective-permute-done.20.refs_6_ = bf16[128,128]{1,0:T(8,128)(2,1)S(1)} collective-permute-done((bf16[128,128]{1,0:T(8,128)(2,1)S(1)}, bf16[128,128]{1,0:T(8,128)(2,1)S(1)}, u32[]{:S(2)}, u32[]{:S(2)}) %collective-permute-start.20) | collective-permute-done | bytes 32800 | tf_op jit(solution)/shard_map/ppermute | solution.py:431
  102.2 0.5 collective-permute-done.21.refs_7_
  102.7 7.5 %project.1 = (f32[32,4096]{1,0:T(8,128)S(1)}, bf16[32,4096]{1,0:T(8,128)(2,1)S(1)}, bf16[32,4096]{1,0:T(8,128)(2,1)S(1)}, bf16[32,4096]{1,0:T(8,128)(2,1)S(1)}) custom-call(s32[3]{0:T(128)S(1)} %pad_add_fusion.me_ref, bf16[128,128]{1,0:T(8,128)(2,1)S(1)} %get-tuple-element.47.refs_0_, bf16[128,128]{1,0:T(8,128)(2,1)S(1)} %collective-permute-done.15.refs_1_, ...), custom_call_target="tpu_custom_call" | custom-call | flops 1000000000 | bytes 9000000 | tf_op jit(solution)/shard_map/project/pallas_call | solution.py:409
  110.2 1.7 %collective-permute-start.22 = (bf16[32,4096]{1,0:T(8,128)(2,1)S(1)}, bf16[32,4096]{1,0:T(8,128)(2,1)S(1)}, u32[]{:S(2)}, u32[]{:S(2)}) collective-permute-start(bf16[32,4096]{1,0:T(8,128)(2,1)S(1)} %get-tuple-element.56), channel_id=1, source_target_pairs={{0,1},{1,0},{2,3},{3,2},{4,5},{5,4},{6,7},{7,6},{8,9},{9,8},{10,11... | collective-permute-start | bytes 786440 | tf_op jit(solution)/shard_map/ppermute | solution.py:456
  111.9 2.9 %collective-permute-start.23 = (bf16[32,4096]{1,0:T(8,128)(2,1)S(1)}, bf16[32,4096]{1,0:T(8,128)(2,1)S(1)}, u32[]{:S(2)}, u32[]{:S(2)}) collective-permute-start(bf16[32,4096]{1,0:T(8,128)(2,1)S(1)} %get-tuple-element.57), channel_id=1, source_target_pairs={{0,2},{1,3},{2,0},{3,1},{4,6},{5,7},{6,4},{7,5},{8,10},{9,11},{10,... | collective-permute-start | bytes 786440 | tf_op jit(solution)/shard_map/ppermute | solution.py:456
  114.8 0.2 collective-permute-start.24
  115.0 4.5 %collective-permute-done.22 = bf16[32,4096]{1,0:T(8,128)(2,1)S(1)} collective-permute-done((bf16[32,4096]{1,0:T(8,128)(2,1)S(1)}, bf16[32,4096]{1,0:T(8,128)(2,1)S(1)}, u32[]{:S(2)}, u32[]{:S(2)}) %collective-permute-start.22) | collective-permute-done | bytes 262176 | tf_op jit(solution)/shard_map/ppermute | solution.py:456
  119.5 7.4 %collective-permute-done.23 = bf16[32,4096]{1,0:T(8,128)(2,1)S(1)} collective-permute-done((bf16[32,4096]{1,0:T(8,128)(2,1)S(1)}, bf16[32,4096]{1,0:T(8,128)(2,1)S(1)}, u32[]{:S(2)}, u32[]{:S(2)}) %collective-permute-start.23) | collective-permute-done | bytes 262176 | tf_op jit(solution)/shard_map/ppermute | solution.py:456
  126.9 2.6 %collective-permute-done.24 = bf16[32,4096]{1,0:T(8,128)(2,1)S(1)} collective-permute-done((bf16[32,4096]{1,0:T(8,128)(2,1)S(1)}, bf16[32,4096]{1,0:T(8,128)(2,1)S(1)}, u32[]{:S(2)}, u32[]{:S(2)}) %collective-permute-start.24) | collective-permute-done | bytes 262176 | tf_op jit(solution)/shard_map/ppermute | solution.py:456
  129.4 0.8 add_convert_fusion
  (9 shorter events, 0.0 us)
Async XLA Ops:
  0.0 76.1 %copy-start.5 = (f32[128]{0:T(128)S(1)}, f32[128]{0:T(128)}, u32[]{:S(2)}) copy-start(f32[128]{0:T(128)} %param.13) | copy-start | bytes 1540
  0.1 1.0 copy-start
  1.0 0.9 copy-start.1
  2.0 0.9 copy-start.2
  2.9 0.7 copy-start.3
  3.6 0.7 copy-start.4
  4.3 76.2 %copy-start.6 = (bf16[8,128,384]{2,1,0:T(8,128)(2,1)S(1)}, bf16[8,128,384]{2,1,0:T(8,128)(2,1)}, u32[]{:S(2)}) copy-start(bf16[8,128,384]{2,1,0:T(8,128)(2,1)} %weight_ref.3) | copy-start | bytes 2359300
  5.1 5.2 %collective-permute-start = (bf16[400,128]{1,0:T(8,128)(2,1)S(1)}, bf16[400,128]{1,0:T(8,128)(2,1)S(1)}, u32[]{:S(2)}, u32[]{:S(2)}) collective-permute-start(bf16[400,128]{1,0:T(8,128)(2,1)S(1)} %get-tuple-element.33), channel_id=1, source_target_pairs={{0,4},{4,0},{8,12},{12,8},{16,20},{20,16},{24,28},{28,24},{32,36},... | collective-permute-start | bytes 307208 | tf_op jit(solution)/shard_map/ppermute | solution.py:431
  5.2 7.9 %collective-permute-start.1 = (bf16[400,128]{1,0:T(8,128)(2,1)S(1)}, bf16[400,128]{1,0:T(8,128)(2,1)S(1)}, u32[]{:S(2)}, u32[]{:S(2)}) collective-permute-start(bf16[400,128]{1,0:T(8,128)(2,1)S(1)} %get-tuple-element.34), channel_id=1, source_target_pairs={{0,8},{4,12},{8,0},{12,4},{16,24},{20,28},{24,16},{28,20},{32,40},... | collective-permute-start | bytes 307208 | tf_op jit(solution)/shard_map/ppermute | solution.py:431
  6.8 6.5 %collective-permute-start.2 = (bf16[400,128]{1,0:T(8,128)(2,1)S(1)}, bf16[400,128]{1,0:T(8,128)(2,1)S(1)}, u32[]{:S(2)}, u32[]{:S(2)}) collective-permute-start(bf16[400,128]{1,0:T(8,128)(2,1)S(1)} %get-tuple-element.35), channel_id=1, source_target_pairs={{0,12},{4,8},{8,4},{12,0},{16,28},{20,24},{24,20},{28,16},{32,44},... | collective-permute-start | bytes 307208 | tf_op jit(solution)/shard_map/ppermute | solution.py:431
  7.0 10.6 %collective-permute-start.3 = (bf16[400,128]{1,0:T(8,128)(2,1)S(1)}, bf16[400,128]{1,0:T(8,128)(2,1)S(1)}, u32[]{:S(2)}, u32[]{:S(2)}) collective-permute-start(bf16[400,128]{1,0:T(8,128)(2,1)S(1)} %get-tuple-element.36), channel_id=1, source_target_pairs={{0,16},{4,20},{8,24},{12,28},{16,0},{20,4},{24,8},{28,12},{32,48},... | collective-permute-start | bytes 307208 | tf_op jit(solution)/shard_map/ppermute | solution.py:431
  10.1 8.8 %collective-permute-start.4 = (bf16[400,128]{1,0:T(8,128)(2,1)S(1)}, bf16[400,128]{1,0:T(8,128)(2,1)S(1)}, u32[]{:S(2)}, u32[]{:S(2)}) collective-permute-start(bf16[400,128]{1,0:T(8,128)(2,1)S(1)} %get-tuple-element.37), channel_id=1, source_target_pairs={{0,20},{4,16},{8,28},{12,24},{16,4},{20,0},{24,12},{28,8},{32,52},... | collective-permute-start | bytes 307208 | tf_op jit(solution)/shard_map/ppermute | solution.py:431
  10.3 11.0 %collective-permute-start.5 = (bf16[400,128]{1,0:T(8,128)(2,1)S(1)}, bf16[400,128]{1,0:T(8,128)(2,1)S(1)}, u32[]{:S(2)}, u32[]{:S(2)}) collective-permute-start(bf16[400,128]{1,0:T(8,128)(2,1)S(1)} %get-tuple-element.38), channel_id=1, source_target_pairs={{0,24},{4,28},{8,16},{12,20},{16,8},{20,12},{24,0},{28,4},{32,56},... | collective-permute-start | bytes 307208 | tf_op jit(solution)/shard_map/ppermute | solution.py:431
  13.0 9.9 %collective-permute-start.6 = (bf16[400,128]{1,0:T(8,128)(2,1)S(1)}, bf16[400,128]{1,0:T(8,128)(2,1)S(1)}, u32[]{:S(2)}, u32[]{:S(2)}) collective-permute-start(bf16[400,128]{1,0:T(8,128)(2,1)S(1)} %get-tuple-element.39), channel_id=1, source_target_pairs={{0,28},{4,24},{8,20},{12,16},{16,12},{20,8},{24,4},{28,0},{32,60},... | collective-permute-start | bytes 307208 | tf_op jit(solution)/shard_map/ppermute | solution.py:431
  42.3 9.0 %collective-permute-start.13 = (f32[128,256]{1,0:T(8,128)S(1)}, f32[128,256]{1,0:T(8,128)S(1)}, u32[]{:S(2)}, u32[]{:S(2)}) collective-permute-start(f32[128,256]{1,0:T(8,128)S(1)} %get-tuple-element.43), channel_id=1, source_target_pairs={{0,224},{4,228},{8,232},{12,236},{16,240},{20,244},{24,248},{28,25... | collective-permute-start | bytes 393224 | tf_op jit(solution)/shard_map/ppermute | solution.py:438
  43.0 10.3 %collective-permute-start.12 = (f32[128,256]{1,0:T(8,128)S(1)}, f32[128,256]{1,0:T(8,128)S(1)}, u32[]{:S(2)}, u32[]{:S(2)}) collective-permute-start(f32[128,256]{1,0:T(8,128)S(1)} %get-tuple-element.43), channel_id=1, source_target_pairs={{0,192},{4,196},{8,200},{12,204},{16,208},{20,212},{24,216},{28,22... | collective-permute-start | bytes 393224 | tf_op jit(solution)/shard_map/ppermute | solution.py:438
  43.6 32.4 %collective-permute-start.11 = (f32[128,256]{1,0:T(8,128)S(1)}, f32[128,256]{1,0:T(8,128)S(1)}, u32[]{:S(2)}, u32[]{:S(2)}) collective-permute-start(f32[128,256]{1,0:T(8,128)S(1)} %get-tuple-element.43), channel_id=1, source_target_pairs={{0,160},{4,164},{8,168},{12,172},{16,176},{20,180},{24,184},{28,18... | collective-permute-start | bytes 393224 | tf_op jit(solution)/shard_map/ppermute | solution.py:438
  44.3 31.7 %collective-permute-start.10 = (f32[128,256]{1,0:T(8,128)S(1)}, f32[128,256]{1,0:T(8,128)S(1)}, u32[]{:S(2)}, u32[]{:S(2)}) collective-permute-start(f32[128,256]{1,0:T(8,128)S(1)} %get-tuple-element.43), channel_id=1, source_target_pairs={{0,128},{4,132},{8,136},{12,140},{16,144},{20,148},{24,152},{28,15... | collective-permute-start | bytes 393224 | tf_op jit(solution)/shard_map/ppermute | solution.py:438
  45.6 30.4 %collective-permute-start.9 = (f32[128,256]{1,0:T(8,128)S(1)}, f32[128,256]{1,0:T(8,128)S(1)}, u32[]{:S(2)}, u32[]{:S(2)}) collective-permute-start(f32[128,256]{1,0:T(8,128)S(1)} %get-tuple-element.43), channel_id=1, source_target_pairs={{0,96},{4,100},{8,104},{12,108},{16,112},{20,116},{24,120},{28,124... | collective-permute-start | bytes 393224 | tf_op jit(solution)/shard_map/ppermute | solution.py:438
  51.3 24.7 %collective-permute-start.8 = (f32[128,256]{1,0:T(8,128)S(1)}, f32[128,256]{1,0:T(8,128)S(1)}, u32[]{:S(2)}, u32[]{:S(2)}) collective-permute-start(f32[128,256]{1,0:T(8,128)S(1)} %get-tuple-element.43), channel_id=1, source_target_pairs={{0,64},{4,68},{8,72},{12,76},{16,80},{20,84},{24,88},{28,92},{32,9... | collective-permute-start | bytes 393224 | tf_op jit(solution)/shard_map/ppermute | solution.py:438
  53.3 22.8 %collective-permute-start.7 = (f32[128,256]{1,0:T(8,128)S(1)}, f32[128,256]{1,0:T(8,128)S(1)}, u32[]{:S(2)}, u32[]{:S(2)}) collective-permute-start(f32[128,256]{1,0:T(8,128)S(1)} %get-tuple-element.43), channel_id=1, source_target_pairs={{0,32},{4,36},{8,40},{12,44},{16,48},{20,52},{24,56},{28,60},{32,6... | collective-permute-start | bytes 393224 | tf_op jit(solution)/shard_map/ppermute | solution.py:438
  77.6 11.2 %collective-permute-start.14 = (bf16[1024,128]{1,0:T(8,128)(2,1)S(1)}, bf16[1024,128]{1,0:T(8,128)(2,1)S(1)}, u32[]{:S(2)}, u32[]{:S(2)}) collective-permute-start(bf16[1024,128]{1,0:T(8,128)(2,1)S(1)} %norm.1.normed_ref), channel_id=1, source_target_pairs={{0,32},{4,36},{8,40},{12,44},{16,48},{20,52},{24,56},{28,60},{32,6... | collective-permute-start | bytes 786440 | tf_op jit(solution)/shard_map/ppermute | solution.py:438
  91.8 5.2 %collective-permute-start.15 = (bf16[128,128]{1,0:T(8,128)(2,1)S(1)}, bf16[128,128]{1,0:T(8,128)(2,1)S(1)}, u32[]{:S(2)}, u32[]{:S(2)}) collective-permute-start(bf16[128,128]{1,0:T(8,128)(2,1)S(1)} %get-tuple-element.48), channel_id=1, source_target_pairs={{0,4},{4,0},{8,12},{12,8},{16,20},{20,16},{24,28},{28,24},{32,36},... | collective-permute-start | bytes 98312 | tf_op jit(solution)/shard_map/ppermute | solution.py:431
  92.0 6.2 %collective-permute-start.16 = (bf16[128,128]{1,0:T(8,128)(2,1)S(1)}, bf16[128,128]{1,0:T(8,128)(2,1)S(1)}, u32[]{:S(2)}, u32[]{:S(2)}) collective-permute-start(bf16[128,128]{1,0:T(8,128)(2,1)S(1)} %get-tuple-element.49), channel_id=1, source_target_pairs={{0,8},{4,12},{8,0},{12,4},{16,24},{20,28},{24,16},{28,20},{32,40},... | collective-permute-start | bytes 98312 | tf_op jit(solution)/shard_map/ppermute | solution.py:431
  92.3 7.8 %collective-permute-start.17 = (bf16[128,128]{1,0:T(8,128)(2,1)S(1)}, bf16[128,128]{1,0:T(8,128)(2,1)S(1)}, u32[]{:S(2)}, u32[]{:S(2)}) collective-permute-start(bf16[128,128]{1,0:T(8,128)(2,1)S(1)} %get-tuple-element.50), channel_id=1, source_target_pairs={{0,12},{4,8},{8,4},{12,0},{16,28},{20,24},{24,20},{28,16},{32,44},... | collective-permute-start | bytes 98312 | tf_op jit(solution)/shard_map/ppermute | solution.py:431
  93.8 6.2 %collective-permute-start.18 = (bf16[128,128]{1,0:T(8,128)(2,1)S(1)}, bf16[128,128]{1,0:T(8,128)(2,1)S(1)}, u32[]{:S(2)}, u32[]{:S(2)}) collective-permute-start(bf16[128,128]{1,0:T(8,128)(2,1)S(1)} %get-tuple-element.51), channel_id=1, source_target_pairs={{0,16},{4,20},{8,24},{12,28},{16,0},{20,4},{24,8},{28,12},{32,48},... | collective-permute-start | bytes 98312 | tf_op jit(solution)/shard_map/ppermute | solution.py:431
  95.3 4.9 %collective-permute-start.19 = (bf16[128,128]{1,0:T(8,128)(2,1)S(1)}, bf16[128,128]{1,0:T(8,128)(2,1)S(1)}, u32[]{:S(2)}, u32[]{:S(2)}) collective-permute-start(bf16[128,128]{1,0:T(8,128)(2,1)S(1)} %get-tuple-element.52), channel_id=1, source_target_pairs={{0,20},{4,16},{8,28},{12,24},{16,4},{20,0},{24,12},{28,8},{32,52},... | collective-permute-start | bytes 98312 | tf_op jit(solution)/shard_map/ppermute | solution.py:431
  97.0 5.1 %collective-permute-start.20 = (bf16[128,128]{1,0:T(8,128)(2,1)S(1)}, bf16[128,128]{1,0:T(8,128)(2,1)S(1)}, u32[]{:S(2)}, u32[]{:S(2)}) collective-permute-start(bf16[128,128]{1,0:T(8,128)(2,1)S(1)} %get-tuple-element.53), channel_id=1, source_target_pairs={{0,24},{4,28},{8,16},{12,20},{16,8},{20,12},{24,0},{28,4},{32,56},... | collective-permute-start | bytes 98312 | tf_op jit(solution)/shard_map/ppermute | solution.py:431
  98.2 4.6 %collective-permute-start.21 = (bf16[128,128]{1,0:T(8,128)(2,1)S(1)}, bf16[128,128]{1,0:T(8,128)(2,1)S(1)}, u32[]{:S(2)}, u32[]{:S(2)}) collective-permute-start(bf16[128,128]{1,0:T(8,128)(2,1)S(1)} %get-tuple-element.54), channel_id=1, source_target_pairs={{0,28},{4,24},{8,20},{12,16},{16,12},{20,8},{24,4},{28,0},{32,60},... | collective-permute-start | bytes 98312 | tf_op jit(solution)/shard_map/ppermute | solution.py:431
  110.2 9.2 %collective-permute-start.22 = (bf16[32,4096]{1,0:T(8,128)(2,1)S(1)}, bf16[32,4096]{1,0:T(8,128)(2,1)S(1)}, u32[]{:S(2)}, u32[]{:S(2)}) collective-permute-start(bf16[32,4096]{1,0:T(8,128)(2,1)S(1)} %get-tuple-element.56), channel_id=1, source_target_pairs={{0,1},{1,0},{2,3},{3,2},{4,5},{5,4},{6,7},{7,6},{8,9},{9,8},{10,11... | collective-permute-start | bytes 786440 | tf_op jit(solution)/shard_map/ppermute | solution.py:456
  111.9 15.0 %collective-permute-start.23 = (bf16[32,4096]{1,0:T(8,128)(2,1)S(1)}, bf16[32,4096]{1,0:T(8,128)(2,1)S(1)}, u32[]{:S(2)}, u32[]{:S(2)}) collective-permute-start(bf16[32,4096]{1,0:T(8,128)(2,1)S(1)} %get-tuple-element.57), channel_id=1, source_target_pairs={{0,2},{1,3},{2,0},{3,1},{4,6},{5,7},{6,4},{7,5},{8,10},{9,11},{10,... | collective-permute-start | bytes 786440 | tf_op jit(solution)/shard_map/ppermute | solution.py:456
  114.8 14.6 %collective-permute-start.24 = (bf16[32,4096]{1,0:T(8,128)(2,1)S(1)}, bf16[32,4096]{1,0:T(8,128)(2,1)S(1)}, u32[]{:S(2)}, u32[]{:S(2)}) collective-permute-start(bf16[32,4096]{1,0:T(8,128)(2,1)S(1)} %get-tuple-element.58), channel_id=1, source_target_pairs={{0,3},{1,2},{2,1},{3,0},{4,7},{5,6},{6,5},{7,4},{8,11},{9,10},{10,... | collective-permute-start | bytes 786440 | tf_op jit(solution)/shard_map/ppermute | solution.py:456

commit v2 on v1

v2 whole, which is shorter than its diff:
```python
import jax
import jax.numpy as jnp
from jax import lax
from jax.experimental import pallas as pl
from jax.experimental.pallas import tpu as pltpu
from jax.sharding import PartitionSpec as P

F32 = jnp.float32
BF16 = jnp.bfloat16
C = 128
PLANE = 8
PLANES = 8
BLK = 2 * C + 16
B = 16
GROUP = 4
EPS = 1e-06
NEG = -1e30
VMEM_LIMIT = 24 * 1024 * 1024


def params():
    return pltpu.CompilerParams(vmem_limit_bytes=VMEM_LIMIT)


def cost(flops, nbytes, trans=0):
    return pl.CostEstimate(flops=int(flops), bytes_accessed=int(nbytes), transcendentals=int(trans))


def vmem():
    return pl.BlockSpec(memory_space=pltpu.VMEM)


def smem():
    return pl.BlockSpec(memory_space=pltpu.SMEM)


def split(a):
    hi = a.astype(BF16)
    lo = (a - hi.astype(F32)).astype(BF16)
    return hi, lo


def dot(a, b):
    return lax.dot_general(a, b, (((1,), (0,)), ((), ())), preferred_element_type=F32)


def dot_nt(a, b):
    return lax.dot_general(a, b, (((1,), (1,)), ((), ())), preferred_element_type=F32)


def dot_tn(a, b):
    return lax.dot_general(a, b, (((0,), (0,)), ((), ())), preferred_element_type=F32)


def mm(a, b):
    ah, al = split(a)
    bh, bl = split(b)
    left = jnp.concatenate([ah, al], axis=1)
    n = b.shape[1]
    if n > C:
        return dot(left, jnp.concatenate([bh, bh], axis=0)) + dot(ah, bl)
    pair = jnp.concatenate([bh, bl], axis=1)
    out = dot(left, jnp.concatenate([pair, pair], axis=0))
    return out[:, :n] + out[:, n:]


def mm_exact_right(a, b):
    ah, al = split(a)
    return dot(jnp.concatenate([ah, al], axis=1), jnp.concatenate([b, b], axis=0))


def iotas():
    row = lax.broadcasted_iota(jnp.int32, (C, C), 0)
    col = lax.broadcasted_iota(jnp.int32, (C, C), 1)
    return row, col


def pack_kernel(me_ref, q_ref, k_ref, v_ref, decay_ref, beta_ref, *rest):
    keep, send, keep_q, send_q, gate, raw, sems = rest
    me = me_ref[0]
    copies = [
        pltpu.make_async_copy(decay_ref, raw.at[0], sems.at[24]),
        pltpu.make_async_copy(beta_ref, raw.at[1], sems.at[25]),
    ]
    for d in range(PLANE):
        cols = pl.ds(pl.multiple_of(jnp.bitwise_xor(me, d) * C, C), C)
        out, out_q = (send, send_q) if d % 2 else (keep, keep_q)
        at = d // 2
        copies += [
            pltpu.make_async_copy(k_ref.at[:, cols], out.at[at, pl.ds(0, C)], sems.at[3 * d]),
            pltpu.make_async_copy(v_ref.at[:, cols], out.at[at, pl.ds(C, C)], sems.at[3 * d + 1]),
            pltpu.make_async_copy(q_ref.at[:, cols], out_q.at[at], sems.at[3 * d + 2]),
        ]
    for copy in copies:
        copy.start()
    copies[0].wait()
    copies[1].wait()
    for i in range(2):
        x = raw[i]
        for j in range(3):
            part = x.astype(BF16).astype(F32)
            gate[3 * i + j] = part
            x = x - part
    zeros = jnp.zeros((10, C), F32)
    for d in range(PLANE):
        head = jnp.bitwise_xor(me, d)
        rows = [gate[i, pl.ds(head, 1), :] for i in range(6)]
        out = send if d % 2 else keep
        out[d // 2, 2 * C :, :] = jnp.concatenate(rows + [zeros], axis=0).astype(BF16)
    for copy in copies[2:]:
        copy.wait()


def pack(me, q, k, v, decay, beta):
    any_space = pl.BlockSpec(memory_space=pl.ANY)
    wide = jax.ShapeDtypeStruct((4, BLK, C), BF16)
    thin = jax.ShapeDtypeStruct((4, C, C), BF16)
    return pl.pallas_call(
        pack_kernel,
        out_shape=[wide, wide, thin, thin],
        in_specs=[smem()] + [any_space] * 5,
        out_specs=[vmem()] * 4,
        scratch_shapes=[
            pltpu.VMEM((6, PLANE, C), F32),
            pltpu.VMEM((2, PLANE, C), F32),
            pltpu.SemaphoreType.DMA((26,)),
        ],
        compiler_params=params(),
        name="pack",
    )(me, q, k, v, decay, beta)


def gather_slots(refs, out_ref):
    keep, came = refs[0], refs[1]
    out_ref[0] = keep[0]
    out_ref[1] = came[0]
    for dx in range(1, 4):
        out_ref[2 * dx] = refs[dx + 1][0]
        out_ref[2 * dx + 1] = refs[dx + 1][1]


def gates(pieces):
    row, col = iotas()
    upper = jnp.where(row <= col, 1.0, 0.0).astype(BF16)
    lower = jnp.where(row >= col, 1.0, 0.0).astype(BF16)
    eye = jnp.where(row == col, 1.0, 0.0).astype(BF16)
    along_row = dot(pieces, upper)
    along_col = dot_nt(jnp.concatenate([lower, eye], axis=0), pieces)
    plain = pieces.astype(F32)
    g_row = -(along_row[0:1] + along_row[1:2] + along_row[2:3])
    b_row = plain[3:4] + plain[4:5] + plain[5:6]
    g_col = -(along_col[:C, 0:1] + along_col[:C, 1:2] + along_col[:C, 2:3])
    b_col = along_col[C:, 3:4] + along_col[C:, 4:5] + along_col[C:, 5:6]
    return g_row, b_row, g_col, b_col


def base_inverses(packed):
    row, col = iotas()
    high = packed.astype(BF16)
    rest = packed - high.astype(F32)
    mid = rest.astype(BF16)
    low = (rest - mid.astype(F32)).astype(BF16)
    three = jnp.concatenate([high, mid, low], axis=1)
    x = jnp.where(row % B == col % B, 1.0, 0.0)
    for j in range(B - 1):
        pick = jnp.where(row == col - col % B + j, 1.0, 0.0).astype(BF16)
        factor = dot(three, jnp.concatenate([pick, pick, pick], axis=0))
        line = x.reshape(PLANE, B, C)[:, j : j + 1, :]
        x = x - factor * jnp.broadcast_to(line, (PLANE, B, C)).reshape(C, C)
    return x


def after(earlier, later):
    both = mm(later[:, :C], earlier)
    return jnp.concatenate([both[:, :C], both[:, C:] + later[:, C:]], axis=1)


def prep_kernel(me_ref, *refs):
    kv_ref, mix_ref, wu_ref, ab_ref, level_ref = refs[5:10]
    maps, lows, packs, r_cols, ends = refs[10:]
    me = me_ref[0]
    row, col = iotas()
    gather_slots(refs[:5], kv_ref)
    blocks = (row // B) == (col // B)

    def first(step, _):
        for i in range(GROUP):
            d = step * GROUP + i
            keys = kv_ref[d, 0:C, :]
            g_row, b_row, g_col, b_col = gates(kv_ref[d, 2 * C :, :])
            gram = dot_nt(keys, keys)
            diag = jnp.where(row == col, gram, 0.0)
            r_col = lax.rsqrt(jnp.sum(diag, axis=1, keepdims=True) + EPS)
            r_row = lax.rsqrt(jnp.sum(diag, axis=0, keepdims=True) + EPS)
            ratio = jnp.where(row >= col, jnp.exp(jnp.minimum(g_col - g_row, 0.0)), 0.0)
            mix = ratio * (b_row * r_row)
            mix_ref[d] = mix
            low = jnp.where(row > col, mix * gram * r_col, 0.0)
            lows[d] = low
            held = jnp.where(blocks, low, 0.0)
            packed = held[0:B]
            for b in range(1, C // B):
                packed = packed + held[B * b : B * b + B]
            packs[pl.ds(pl.multiple_of(d * B, B), B), :] = packed
            g_end = g_row[:, C - 1 : C]
            tail = jnp.exp(g_end - g_col) * b_col * r_col
            fold = jnp.exp(g_row) * r_row
            r_cols[d, 0] = jnp.broadcast_to(tail, (C, C))
            r_cols[d, 1] = jnp.broadcast_to(fold, (C, C))
            ends[d] = jnp.broadcast_to(jnp.exp(g_end), (C, C))
        return _

    lax.fori_loop(0, PLANE // GROUP, first, 0)
    packs[...] = base_inverses(packs[...])

    def second(step, _):
        for i in range(GROUP):
            d = step * GROUP + i
            keys = kv_ref[d, 0:C, :]
            values = kv_ref[d, C : 2 * C, :]
            low = lows[d]
            x = packs[pl.ds(pl.multiple_of(d * B, B), B), :]
            x = jnp.where(blocks, jnp.concatenate([x] * (C // B), axis=0), 0.0)
            size = B
            while size < C:
                apart = jnp.bitwise_xor(row, col)
                corner = jnp.where((row > col) & (apart >= size) & (apart < 2 * size), low, 0.0)
                x = x - mm(mm(x, corner), x)
                size *= 2
            tail, fold = r_cols[d, 0], r_cols[d, 1]
            w = mm_exact_right(x * fold, keys)
            u = mm_exact_right(x, values)
            wu = jnp.concatenate([w, u], axis=1)
            wu_ref[d] = wu
            hi, lo = split(jnp.concatenate([w * tail, u * tail], axis=1))
            made = dot_tn(
                jnp.concatenate([keys, keys], axis=0), jnp.concatenate([hi, lo], axis=0)
            )
            g_end = ends[d]
            chunk = jnp.bitwise_xor(me, d)
            maps[chunk] = jnp.concatenate(
                [jnp.where(row == col, g_end, 0.0) - made[:, :C], made[:, C:]], axis=1
            )
        return _

    lax.fori_loop(0, PLANE // GROUP, second, 0)
    one = [maps[i] for i in range(PLANE)]
    two = [after(one[2 * i], one[2 * i + 1]) for i in range(4)]
    four = [after(two[2 * i], two[2 * i + 1]) for i in range(2)]
    ab_ref[...] = after(four[0], four[1]).astype(BF16)
    for i, part in enumerate((one[0], two[0], one[2], four[0], one[4], two[2], one[6])):
        level_ref[i] = part


def prep(me, slots):
    return pl.pallas_call(
        prep_kernel,
        out_shape=[
            jax.ShapeDtypeStruct((PLANE, BLK, C), BF16),
            jax.ShapeDtypeStruct((PLANE, C, C), F32),
            jax.ShapeDtypeStruct((PLANE, C, 2 * C), F32),
            jax.ShapeDtypeStruct((C, 2 * C), BF16),
            jax.ShapeDtypeStruct((7, C, 2 * C), F32),
        ],
        in_specs=[smem()] + [vmem()] * 5,
        out_specs=[vmem()] * 5,
        scratch_shapes=[
            pltpu.VMEM((PLANE, C, 2 * C), F32),
            pltpu.VMEM((PLANE, C, C), F32),
            pltpu.VMEM((C, C), F32),
            pltpu.VMEM((PLANE, 2, C, C), F32),
            pltpu.VMEM((PLANE, C, C), F32),
        ],
        compiler_params=params(),
        cost_estimate=cost(2e9, 4e6),
        name="prep",
    )(me, *slots)


def query_kernel(me_ref, *refs):
    kv_ref, mix_ref, wu_ref, level_ref, no_ref, queries_ref, before = refs[5:]
    me = me_ref[0]
    row, col = iotas()
    gather_slots(refs[:5], queries_ref)
    before[0] = jnp.concatenate([jnp.where(row == col, 1.0, 0.0), jnp.zeros((C, C), F32)], axis=1)
    before[1] = level_ref[0]
    before[2] = level_ref[1]
    before[3] = after(level_ref[1], level_ref[2])
    before[4] = level_ref[3]
    before[5] = after(level_ref[3], level_ref[4])
    six = after(level_ref[3], level_ref[5])
    before[6] = six
    before[7] = after(six, level_ref[6])

    def one(step, _):
        for i in range(GROUP):
            d = step * GROUP + i
            keys = kv_ref[d, 0:C, :]
            g_row, b_row, g_col, b_col = gates(kv_ref[d, 2 * C :, :])
            queries = queries_ref[d]
            wide = queries.astype(F32)
            r_col = lax.rsqrt(jnp.sum(wide * wide, axis=1, keepdims=True) + EPS) * (C**-0.5)
            scored = dot_nt(queries, keys) * r_col * mix_ref[d]
            part = mm(scored, wu_ref[d])
            reach = wide * (r_col * jnp.exp(g_col)) - part[:, :C]
            chunk = jnp.bitwise_xor(me, d)
            both = mm(reach, before[chunk])
            rows = pl.ds(pl.multiple_of(chunk * C, C), C)
            no_ref[rows, :] = jnp.concatenate([both[:, :C], both[:, C:] + part[:, C:]], axis=1)
        return _

    lax.fori_loop(0, PLANE // GROUP, one, 0)


def query(me, slots, kv, mix, wu, level):
    return pl.pallas_call(
        query_kernel,
        out_shape=jax.ShapeDtypeStruct((PLANE * C, 2 * C), F32),
        in_specs=[smem()] + [vmem()] * 9,
        out_specs=vmem(),
        scratch_shapes=[
            pltpu.VMEM((PLANE, C, C), BF16),
            pltpu.VMEM((PLANE, C, 2 * C), F32),
        ],
        compiler_params=params(),
        cost_estimate=cost(1e9, 4e6),
        name="query",
    )(me, *slots, kv, mix, wu, level)


def combine_kernel(own_ref, one_ref, two_ref, three_ref, out_ref, b_ref):
    def times(a, x):
        hi, lo = split(x)
        return dot(a, hi) + dot(a, lo)

    state = two_ref[:, C:].astype(F32) + dot(two_ref[:, :C], three_ref[...])
    state = one_ref[:, C:].astype(F32) + times(one_ref[:, :C], state)
    state = own_ref[:, C:].astype(F32) + times(own_ref[:, :C], state)
    reach = times(own_ref[:, :C], dot(one_ref[:, :C], two_ref[:, :C]))
    out_ref[:, :C] = reach.astype(BF16)
    out_ref[:, C:] = state.astype(BF16)
    b_ref[...] = state.astype(BF16)


def combine(own_map, one, two, three):
    return pl.pallas_call(
        combine_kernel,
        out_shape=[
            jax.ShapeDtypeStruct((C, 2 * C), BF16),
            jax.ShapeDtypeStruct((C, C), BF16),
        ],
        in_specs=[vmem()] * 4,
        out_specs=[vmem()] * 2,
        compiler_params=params(),
        name="combine",
    )(own_map, one, two, three)


def norm_kernel(no_ref, gain_ref, near_ref, far_ref, normed_ref):
    state = dot(near_ref[:, :C], far_ref[...]) + near_ref[:, C:].astype(F32)
    out = mm(no_ref[:, :C], state) + no_ref[:, C:]
    scale = lax.rsqrt(jnp.mean(out * out, axis=1, keepdims=True) + EPS)
    normed_ref[...] = (out * scale * gain_ref[...]).astype(BF16)


def norm(no, gain, near, far):
    return pl.pallas_call(
        norm_kernel,
        out_shape=jax.ShapeDtypeStruct((PLANE * C, C), BF16),
        in_specs=[vmem()] * 4,
        out_specs=vmem(),
        compiler_params=params(),
        cost_estimate=cost(2e8, 2e6),
        name="norm",
    )(no, gain, near, far)


QB = 256


def own_kernel(me_ref, normed_ref, weight_ref, acc_ref, stat_ref, q2_ref):
    proj = dot(normed_ref[...], weight_ref[0]).astype(BF16)
    q2_ref[...] = proj[:, :C]
    row = lax.broadcasted_iota(jnp.int32, (QB, QB), 0)
    col = lax.broadcasted_iota(jnp.int32, (QB, QB), 1)
    for i in range(PLANE * C // QB):
        at = i * QB
        q = proj[at : at + QB, :C]
        s = dot_nt(q, proj[: at + QB, C : 2 * C]) * (C**-0.5)
        last = jnp.where(col <= row, s[:, at:], NEG)
        s = last if i == 0 else jnp.concatenate([s[:, :at], last], axis=1)
        top = jnp.max(s, axis=1, keepdims=True)
        p = jnp.exp(s - top)
        total = jnp.sum(p, axis=1, keepdims=True)
        acc_ref[at : at + QB, :] = dot(p.astype(BF16), proj[: at + QB, 2 * C :])
        stat_ref[0, at : at + QB, :] = jnp.broadcast_to(top, (QB, C))
        stat_ref[1, at : at + QB, :] = jnp.broadcast_to(total, (QB, C))


def own(me, normed, weight):
    n = PLANE * C
    return pl.pallas_call(
        own_kernel,
        out_shape=[
            jax.ShapeDtypeStruct((n, C), F32),
            jax.ShapeDtypeStruct((2, n, C), F32),
            jax.ShapeDtypeStruct((n, C), BF16),
        ],
        grid_spec=pltpu.PrefetchScalarGridSpec(
            num_scalar_prefetch=1,
            grid=(1,),
            in_specs=[
                pl.BlockSpec((n, C), lambda i, me: (0, 0)),
                pl.BlockSpec((1, C, 3 * C), lambda i, me: (me[0], 0, 0)),
            ],
            out_specs=[
                pl.BlockSpec((n, C), lambda i, me: (0, 0)),
                pl.BlockSpec((2, n, C), lambda i, me: (0, 0, 0)),
                pl.BlockSpec((n, C), lambda i, me: (0, 0)),
            ],
        ),
        compiler_params=params(),
        cost_estimate=cost(1e9, 3e6, 6e5),
        name="own",
    )(me, normed, weight)


def halo_kernel(me_ref, halo_ref, weight_ref, acc_ref, stat_ref, q2_ref, *refs):
    keep, send, attended = refs
    me, plane = me_ref[0], me_ref[1]
    proj = dot(halo_ref[...], weight_ref[0, :, C:]).astype(BF16)
    n = PLANE * C
    for i in range(n // QB):
        at = i * QB
        row = lax.broadcasted_iota(jnp.int32, (QB, n - at), 0)
        col = lax.broadcasted_iota(jnp.int32, (QB, n - at), 1)
        allowed = (col > row) & (plane > 0)
        s = dot_nt(q2_ref[at : at + QB, :], proj[at:, :C]) * (C**-0.5)
        s = jnp.where(allowed, s, NEG)
        before = stat_ref[0, at : at + QB, 0:1]
        top = jnp.maximum(jnp.max(s, axis=1, keepdims=True), before)
        p = jnp.where(allowed, jnp.exp(s - top), 0.0)
        fade = jnp.exp(before - top)
        total = jnp.sum(p, axis=1, keepdims=True) + fade * stat_ref[1, at : at + QB, 0:1]
        acc = acc_ref[at : at + QB, :] * fade + dot(p.astype(BF16), proj[at:, C:])
        attended[at : at + QB, :] = (acc / total).astype(BF16)
    for d in range(PLANE):
        chunk = jnp.bitwise_xor(me, d)
        out = send if d % 2 else keep
        out[d // 2] = attended[pl.ds(pl.multiple_of(chunk * C, C), C), :]


def halo_part(me, halo, weight, acc, stat, q2):
    n = PLANE * C
    return pl.pallas_call(
        halo_kernel,
        out_shape=[jax.ShapeDtypeStruct((4, C, C), BF16)] * 2,
        grid_spec=pltpu.PrefetchScalarGridSpec(
            num_scalar_prefetch=1,
            grid=(1,),
            in_specs=[
                pl.BlockSpec((n, C), lambda i, me: (0, 0)),
                pl.BlockSpec((1, C, 3 * C), lambda i, me: (me[0], 0, 0)),
                pl.BlockSpec((n, C), lambda i, me: (0, 0)),
                pl.BlockSpec((2, n, C), lambda i, me: (0, 0, 0)),
                pl.BlockSpec((n, C), lambda i, me: (0, 0)),
            ],
            out_specs=[pl.BlockSpec((4, C, C), lambda i, me: (0, 0, 0))] * 2,
            scratch_shapes=[pltpu.VMEM((n, C), BF16)],
        ),
        compiler_params=params(),
        cost_estimate=cost(1e9, 3e6, 6e5),
        name="halo",
    )(me, halo, weight, acc, stat, q2)


COLS = 1024


def project_kernel(me_ref, *refs):
    slots, weight_ref, outs, flat = refs[:5], refs[5], refs[6:10], refs[10]
    me, mine = me_ref[0], me_ref[2]
    found = [slots[0].at[0], slots[1].at[0]]
    for dx in range(1, 4):
        found += [slots[dx + 1].at[0], slots[dx + 1].at[1]]
    for d in range(PLANE):
        cols = pl.ds(pl.multiple_of(jnp.bitwise_xor(me, d) * C, C), C)
        for e in range(4):
            rows = pl.ds(pl.multiple_of(jnp.bitwise_xor(mine, e) * 32, 32), 32)
            flat[e * 32 : e * 32 + 32, cols] = found[d][rows, :]

    def one(step, _):
        cols = pl.ds(pl.multiple_of(step * COLS, COLS), COLS)
        got = dot(flat[...], weight_ref[:, cols])
        for e in range(4):
            outs[e][:, cols] = got[e * 32 : e * 32 + 32].astype(outs[e].dtype)
        return _

    lax.fori_loop(0, weight_ref.shape[1] // COLS, one, 0)


def project(me, slots, weight):
    depth, width = weight.shape
    return pl.pallas_call(
        project_kernel,
        out_shape=[jax.ShapeDtypeStruct((32, width), F32)]
        + [jax.ShapeDtypeStruct((32, width), BF16)] * 3,
        in_specs=[smem()] + [vmem()] * 6,
        out_specs=[vmem()] * 4,
        scratch_shapes=[pltpu.VMEM((C, depth), BF16)],
        compiler_params=params(),
        cost_estimate=cost(1e9, 9e6),
        name="project",
    )(me, *slots, weight)


def swap(block, d):
    return lax.ppermute(block, "seq", [(s, s ^ d) for s in range(PLANE * PLANES)])


def exchange(keep, send):
    came = swap(send, 1)
    slots = [keep, came]
    for dx in (2, 1, 3):
        slots.append((dx, swap(jnp.stack([keep[dx], came[dx]]), 2 * dx)))
    return slots[:2] + [pair for _, pair in sorted(slots[2:], key=lambda item: item[0])]


def later_plane(block, distance, first=0, last=PLANES - 1):
    step = PLANE * distance
    route = []
    for z in range(first, last + 1):
        if z + distance < PLANES:
            route += [(z * PLANE + i, z * PLANE + i + step) for i in range(PLANE)]
    return lax.ppermute(block, "seq", route)


def local(q_delta, k_delta, v_delta, decay, beta, gain, attn_weight, out_weight):
    place = lax.axis_index("seq")
    mine = lax.axis_index("heads")
    me = jnp.stack([place % PLANE, place // PLANE, mine]).astype(jnp.int32)
    keep, send, keep_q, send_q = pack(me, q_delta, k_delta, v_delta, decay, beta)
    slots = exchange(keep, send)
    slots_q = exchange(keep_q, send_q)
    kv, mix, wu, ab, level = prep(me, slots)
    one = later_plane(ab, 1)
    two = later_plane(ab, 2)
    three = later_plane(ab[:, C:], 3, 0, 0)
    no = query(me, slots_q, kv, mix, wu, level)
    reach, state = combine(ab, one, two, three)
    near = later_plane(reach, 1)
    far = later_plane(state, 4, 1, 3)
    normed = norm(no, gain[None, :], near, far)
    halo = later_plane(normed, 1)
    acc, stat, q2 = own(me, normed, attn_weight)
    attended = exchange(*halo_part(me, halo, attn_weight, acc, stat, q2))
    sums = project(me, attended, out_weight)
    moved = {}
    for d in (2, 1, 3):
        moved[d] = lax.ppermute(sums[d], "heads", [(s, s ^ d) for s in range(4)])
    total = sums[0]
    for d in (1, 3, 2):
        total = total + moved[d].astype(F32)
    return total.astype(BF16)


def solution(mesh):
    placed = (
        P("seq", "heads"),
        P("seq", "heads"),
        P("seq", "heads"),
        P("heads", "seq"),
        P("heads", "seq"),
        P(),
        P("heads", None, None),
        P("heads", None),
    )
    return jax.shard_map(
        local, mesh=mesh, in_specs=placed, out_specs=P(("seq", "heads"), None), check_vma=False
    )
```

time: 131 us -> 102 us (0.78)
  the two profiles are of different devices: /device:TPU:128 before, /device:TPU:64 now
where the time goes in v2:
time: 102 us
  starting transfers between devices  42.5 us (42%)
  waiting for transfers between devices  28.1 us (28%)
  Pallas kernels  25.4 us (25%)
  local copies, waits for them, and re-layouts  4.31 us (4%)
    ppermute x6, starting transfers between devices, later_plane(): return lax.ppermute(block, 'seq', route)  22.4 us
    ppermute x12, starting transfers between devices, swap(): lax.ppermute(block, 'seq', [(s, s ^ d) for s in range(PLANE * PLANES)])  15.5 us
    ppermute x12, waiting for transfers between devices, swap(): lax.ppermute(block, 'seq', [(s, s ^ d) for s in range(PLANE * PLANES)])  13.3 us
    pallas_call x1, Pallas kernels, prep(): pl.pallas_call(prep_kernel, out_shape=[jax.ShapeDtypeStruct((PLANE, BLK,...  11.2 us
    ppermute x3, waiting for transfers between devices, local(): moved[d] = lax.ppermute(sums[d], 'heads', [(s, s ^ d) for s in range(4)])  10.3 us
    ppermute x3, starting transfers between devices, local(): moved[d] = lax.ppermute(sums[d], 'heads', [(s, s ^ d) for s in range(4)])  4.57 us
    ppermute x6, waiting for transfers between devices, later_plane(): return lax.ppermute(block, 'seq', route)  4.46 us
    unnamed x18, local copies, waits for them, and re-layouts  4.24 us
  transfers between devices with their start and end apart: 21, of which 12 were waited for; matrix products, arithmetic and copies ran while one was open for 0% of the time, Pallas kernels for 18%

profile of v2, /device:TPU:64, one launch (start us, length us, event | category | flops | bytes accessed | tf_op | source)
XLA Modules:
  0.0 101.6 jit_solution(3002867374353808001)
XLA Ops:
  0.0 0.0 copy-start.5
  0.0 0.1 pad_add_fusion.me_ref
  0.1 0.0 copy-start
  0.1 0.9 copy-done
  1.0 0.9 copy-done.1
  2.0 0.9 copy-done.2
  2.9 0.7 copy-done.3
  3.6 0.7 copy-done.4
  4.3 1.1 %pack.1 = (bf16[4,272,128]{2,1,0:T(8,128)(2,1)S(1)}, bf16[4,272,128]{2,1,0:T(8,128)(2,1)S(1)}, bf16[4,128,128]{2,1,0:T(8,128)(2,1)S(1)}, bf16[4,128,128]{2,1,0:T(8,128)(2,1)S(1)}) custom-call(s32[3]{0:T(128)S(1)} %pad_add_fusion.me_ref, bf16[128,1024]{1,0:T(8,128)(2,1)S(1)} %copy-done, bf16[128,1024]{1,0:T(8,128)(2,1)S(1)} %copy-done.1, ...), custom_call_target="tpu_custom_call" | custom-call | tf_op jit(solution)/shard_map/pack/pallas_call | solution.py:118
  5.4 0.1 collective-permute-start
  5.5 0.5 collective-permute-start.4
  6.0 0.8 collective-permute-done.refs_1_
  6.9 0.4 collective-permute-done.4.refs_1_
  7.3 1.6 %collective-permute-start.5 = (bf16[2,272,128]{2,1,0:T(8,128)(2,1)S(1)}, bf16[2,272,128]{2,1,0:T(8,128)(2,1)S(1)}, u32[]{:S(2)}, u32[]{:S(2)}) collective-permute-start(bf16[2,272,128]{2,1,0:T(8,128)(2,1)S(1)} %pad_maximum_fusion), channel_id=1, source_target_pairs={{0,8},{4,12},{8,0},{12,4},{16,24},{20,28},{24,16},{28,20},{32,40},... | collective-permute-start | bytes 417800 | tf_op jit(solution)/shard_map/ppermute | solution.py:518
  8.9 2.8 %collective-permute-start.6 = (bf16[2,272,128]{2,1,0:T(8,128)(2,1)S(1)}, bf16[2,272,128]{2,1,0:T(8,128)(2,1)S(1)}, u32[]{:S(2)}, u32[]{:S(2)}) collective-permute-start(bf16[2,272,128]{2,1,0:T(8,128)(2,1)S(1)} %pad_maximum_fusion.1), channel_id=1, source_target_pairs={{0,16},{4,20},{8,24},{12,28},{16,0},{20,4},{24,8},{28,12},{32,48},... | collective-permute-start | bytes 417800 | tf_op jit(solution)/shard_map/ppermute | solution.py:518
  11.7 0.6 collective-permute-start.7
  12.3 0.4 collective-permute-start.1
  12.7 4.0 %collective-permute-start.2 = (bf16[2,128,128]{2,1,0:T(8,128)(2,1)S(1)}, bf16[2,128,128]{2,1,0:T(8,128)(2,1)S(1)}, u32[]{:S(2)}, u32[]{:S(2)}) collective-permute-start(bf16[2,128,128]{2,1,0:T(8,128)(2,1)S(1)} %pad_maximum_fusion.4), channel_id=1, source_target_pairs={{0,16},{4,20},{8,24},{12,28},{16,0},{20,4},{24,8},{28,12},{32,48},... | collective-permute-start | bytes 196616 | tf_op jit(solution)/shard_map/ppermute | solution.py:518
  16.7 0.0 collective-permute-done.5.refs_2_
  16.7 2.4 %collective-permute-done.6.refs_3_ = bf16[2,272,128]{2,1,0:T(8,128)(2,1)S(1)} collective-permute-done((bf16[2,272,128]{2,1,0:T(8,128)(2,1)S(1)}, bf16[2,272,128]{2,1,0:T(8,128)(2,1)S(1)}, u32[]{:S(2)}, u32[]{:S(2)}) %collective-permute-start.6) | collective-permute-done | bytes 139296 | tf_op jit(solution)/shard_map/ppermute | solution.py:518
  19.1 3.4 %collective-permute-done.7.refs_4_ = bf16[2,272,128]{2,1,0:T(8,128)(2,1)S(1)} collective-permute-done((bf16[2,272,128]{2,1,0:T(8,128)(2,1)S(1)}, bf16[2,272,128]{2,1,0:T(8,128)(2,1)S(1)}, u32[]{:S(2)}, u32[]{:S(2)}) %collective-permute-start.7) | collective-permute-done | bytes 139296 | tf_op jit(solution)/shard_map/ppermute | solution.py:518
  22.5 11.2 %prep.1 = (bf16[8,272,128]{2,1,0:T(8,128)(2,1)S(1)}, f32[8,128,128]{2,1,0:T(8,128)S(1)}, f32[8,128,256]{2,1,0:T(8,128)S(1)}, bf16[128,256]{1,0:T(8,128)(2,1)S(1)}, f32[7,128,256]{2,1,0:T(8,128)S(1)}) custom-call(s32[3]{0:T(128)S(1)} %pad_add_fusion.me_ref, bf16[4,272,128]{2,1,0:T(8,128)(2,1)S(1)} %get-tuple-element.27.refs_0_, ...), custom_call_target="tpu_custom_call" | custom-call | flops 2000000000 | bytes 4000000 | tf_op jit(solution)/shard_map/prep/pallas_call | solution.py:256
  33.7 6.4 %collective-permute-start.9 = (bf16[128,256]{1,0:T(8,128)(2,1)S(1)}, bf16[128,256]{1,0:T(8,128)(2,1)S(1)}, u32[]{:S(2)}, u32[]{:S(2)}) collective-permute-start(bf16[128,256]{1,0:T(8,128)(2,1)S(1)} %get-tuple-element.33.own_ref), channel_id=1, source_target_pairs={{0,64},{4,68},{8,72},{12,76},{16,80},{20,84},{24,88},{28,92},{32,9... | collective-permute-start | bytes 196616 | tf_op jit(solution)/shard_map/ppermute | solution.py:535
  40.1 2.9 %collective-permute-start.8 = (bf16[128,256]{1,0:T(8,128)(2,1)S(1)}, bf16[128,256]{1,0:T(8,128)(2,1)S(1)}, u32[]{:S(2)}, u32[]{:S(2)}) collective-permute-start(bf16[128,256]{1,0:T(8,128)(2,1)S(1)} %get-tuple-element.33.own_ref), channel_id=1, source_target_pairs={{0,32},{4,36},{8,40},{12,44},{16,48},{20,52},{24,56},{28,60},{32,6... | collective-permute-start | bytes 196616 | tf_op jit(solution)/shard_map/ppermute | solution.py:535
  43.0 0.7 collective-permute-start.10
  43.7 0.0 collective-permute-done.10.three_ref
  43.7 0.6 collective-permute-start.3
  44.3 0.0 collective-permute-done.9.two_ref
  44.3 2.0 %collective-permute-done.8.one_ref = bf16[128,256]{1,0:T(8,128)(2,1)S(1)} collective-permute-done((bf16[128,256]{1,0:T(8,128)(2,1)S(1)}, bf16[128,256]{1,0:T(8,128)(2,1)S(1)}, u32[]{:S(2)}, u32[]{:S(2)}) %collective-permute-start.8) | collective-permute-done | bytes 65568 | tf_op jit(solution)/shard_map/ppermute | solution.py:535
  46.3 0.5 combine.1
  46.8 3.5 %collective-permute-start.12 = (bf16[128,128]{1,0:T(8,128)(2,1)S(1)}, bf16[128,128]{1,0:T(8,128)(2,1)S(1)}, u32[]{:S(2)}, u32[]{:S(2)}) collective-permute-start(bf16[128,128]{1,0:T(8,128)(2,1)S(1)} %get-tuple-element.35), channel_id=1, source_target_pairs={{32,160},{36,164},{40,168},{44,172},{48,176},{52,180},{56,184},{60... | collective-permute-start | bytes 98312 | tf_op jit(solution)/shard_map/ppermute | solution.py:535
  50.3 5.6 %collective-permute-start.11 = (bf16[128,256]{1,0:T(8,128)(2,1)S(1)}, bf16[128,256]{1,0:T(8,128)(2,1)S(1)}, u32[]{:S(2)}, u32[]{:S(2)}) collective-permute-start(bf16[128,256]{1,0:T(8,128)(2,1)S(1)} %get-tuple-element.34), channel_id=1, source_target_pairs={{0,32},{4,36},{8,40},{12,44},{16,48},{20,52},{24,56},{28,60},{32,6... | collective-permute-start | bytes 196616 | tf_op jit(solution)/shard_map/ppermute | solution.py:535
  55.9 0.0 collective-permute-done.1.refs_2_
  55.9 0.0 collective-permute-done.2.refs_3_
  55.9 0.0 collective-permute-done.3.refs_4_
  55.9 0.0 slice-start.1
  55.9 4.1 %query.1.no_ref = f32[1024,256]{1,0:T(8,128)S(1)} custom-call(s32[3]{0:T(128)S(1)} %pad_add_fusion.me_ref, bf16[4,128,128]{2,1,0:T(8,128)(2,1)S(1)} %get-tuple-element.25.refs_0_, bf16[4,128,128]{2,1,0:T(8,128)(2,1)S(1)} %collective-permute-done.refs_1_, bf16[2,128,128]{2,1,0:T(8,128)(2,1)S(1)} %collective-permute-done.1.refs_2_, ...), custom_call_target="tpu_custom_call" | custom-call | flops 1000000000 | bytes 4000000 | tf_op jit(solution)/shard_map/query/pallas_call | solution.py:316
  60.0 0.0 collective-permute-done.12.far_ref
  60.0 0.0 collective-permute-done.11.near_ref
  60.1 0.0 copy-done.5
  60.1 0.5 norm.1.normed_ref
  60.6 3.3 %collective-permute-start.13 = (bf16[1024,128]{1,0:T(8,128)(2,1)S(1)}, bf16[1024,128]{1,0:T(8,128)(2,1)S(1)}, u32[]{:S(2)}, u32[]{:S(2)}) collective-permute-start(bf16[1024,128]{1,0:T(8,128)(2,1)S(1)} %norm.1.normed_ref), channel_id=1, source_target_pairs={{0,32},{4,36},{8,40},{12,44},{16,48},{20,52},{24,56},{28,60},{32,6... | collective-permute-start | bytes 786440 | tf_op jit(solution)/shard_map/ppermute | solution.py:535
  63.9 0.0 copy-done.6
  63.9 2.4 %own.1 = (f32[1024,128]{1,0:T(8,128)S(1)}, f32[2,1024,128]{2,1,0:T(8,128)S(1)}, bf16[1024,128]{1,0:T(8,128)(2,1)S(1)}) custom-call(s32[3]{0:T(128)S(1)} %pad_add_fusion.me_ref, bf16[1024,128]{1,0:T(8,128)(2,1)S(1)} %norm.1.normed_ref, bf16[8,128,384]{2,1,0:T(8,128)(2,1)S(1)} %copy-done.6), custom_call_target="tpu_custom_call" | custom-call | flops 1000000000 | bytes 3000000 | tf_op jit(solution)/shard_map/own/pallas_call | solution.py:402
  66.4 2.5 %collective-permute-done.13.halo_ref = bf16[1024,128]{1,0:T(8,128)(2,1)S(1)} collective-permute-done((bf16[1024,128]{1,0:T(8,128)(2,1)S(1)}, bf16[1024,128]{1,0:T(8,128)(2,1)S(1)}, u32[]{:S(2)}, u32[]{:S(2)}) %collective-permute-start.13) | collective-permute-done | bytes 262176 | tf_op jit(solution)/shard_map/ppermute | solution.py:535
  68.9 3.1 %halo.1 = (bf16[4,128,128]{2,1,0:T(8,128)(2,1)S(1)}, bf16[4,128,128]{2,1,0:T(8,128)(2,1)S(1)}) custom-call(s32[3]{0:T(128)S(1)} %pad_add_fusion.me_ref, bf16[1024,128]{1,0:T(8,128)(2,1)S(1)} %collective-permute-done.13.halo_ref, bf16[8,128,384]{2,1,0:T(8,128)(2,1)S(1)} %copy-done.6, f32[1024,128]{1,0:T(8,128)S(1)} %get-tuple-element.36.acc_ref, ...), custom_call_target="tpu_custom_call" | custom-call | flops 1000000000 | bytes 3000000 | tf_op jit(solution)/shard_map/halo/pallas_call | solution.py:455
  72.0 0.1 collective-permute-start.14
  72.1 1.3 %collective-permute-done.14.refs_1_ = bf16[4,128,128]{2,1,0:T(8,128)(2,1)S(1)} collective-permute-done((bf16[4,128,128]{2,1,0:T(8,128)(2,1)S(1)}, bf16[4,128,128]{2,1,0:T(8,128)(2,1)S(1)}, u32[]{:S(2)}, u32[]{:S(2)}) %collective-permute-start.14) | collective-permute-done | bytes 131104 | tf_op jit(solution)/shard_map/ppermute | solution.py:518
  73.5 0.1 collective-permute-start.15
  73.6 4.3 %collective-permute-start.16 = (bf16[2,128,128]{2,1,0:T(8,128)(2,1)S(1)}, bf16[2,128,128]{2,1,0:T(8,128)(2,1)S(1)}, u32[]{:S(2)}, u32[]{:S(2)}) collective-permute-start(bf16[2,128,128]{2,1,0:T(8,128)(2,1)S(1)} %pad_maximum_fusion.7), channel_id=1, source_target_pairs={{0,16},{4,20},{8,24},{12,28},{16,0},{20,4},{24,8},{28,12},{32,48},... | collective-permute-start | bytes 196616 | tf_op jit(solution)/shard_map/ppermute | solution.py:518
  77.9 0.6 collective-permute-start.17
  78.4 0.0 collective-permute-done.15.refs_2_
  78.4 2.9 %collective-permute-done.16.refs_3_ = bf16[2,128,128]{2,1,0:T(8,128)(2,1)S(1)} collective-permute-done((bf16[2,128,128]{2,1,0:T(8,128)(2,1)S(1)}, bf16[2,128,128]{2,1,0:T(8,128)(2,1)S(1)}, u32[]{:S(2)}, u32[]{:S(2)}) %collective-permute-start.16) | collective-permute-done | bytes 65568 | tf_op jit(solution)/shard_map/ppermute | solution.py:518
  81.3 2.1 %collective-permute-done.17.refs_4_ = bf16[2,128,128]{2,1,0:T(8,128)(2,1)S(1)} collective-permute-done((bf16[2,128,128]{2,1,0:T(8,128)(2,1)S(1)}, bf16[2,128,128]{2,1,0:T(8,128)(2,1)S(1)}, u32[]{:S(2)}, u32[]{:S(2)}) %collective-permute-start.17) | collective-permute-done | bytes 65568 | tf_op jit(solution)/shard_map/ppermute | solution.py:518
  83.4 0.0 slice-done
  83.4 0.0 slice-done.1
  83.4 2.5 %project.1 = (f32[32,4096]{1,0:T(8,128)S(1)}, bf16[32,4096]{1,0:T(8,128)(2,1)S(1)}, bf16[32,4096]{1,0:T(8,128)(2,1)S(1)}, bf16[32,4096]{1,0:T(8,128)(2,1)S(1)}) custom-call(s32[3]{0:T(128)S(1)} %pad_add_fusion.me_ref, bf16[4,128,128]{2,1,0:T(8,128)(2,1)S(1)} %get-tuple-element.39.refs_0_, bf16[4,128,128]{2,1,0:T(8,128)(2,1)S(1)} %collective-permute-done.14.refs_1_, ...), custom_call_target="tpu_custom_call" | custom-call | flops 1000000000 | bytes 9000000 | tf_op jit(solution)/shard_map/project/pallas_call | solution.py:504
  85.9 1.7 %collective-permute-start.18 = (bf16[32,4096]{1,0:T(8,128)(2,1)S(1)}, bf16[32,4096]{1,0:T(8,128)(2,1)S(1)}, u32[]{:S(2)}, u32[]{:S(2)}) collective-permute-start(bf16[32,4096]{1,0:T(8,128)(2,1)S(1)} %get-tuple-element.42), channel_id=1, source_target_pairs={{0,1},{1,0},{2,3},{3,2},{4,5},{5,4},{6,7},{7,6},{8,9},{9,8},{10,11... | collective-permute-start | bytes 786440 | tf_op jit(solution)/shard_map/ppermute | solution.py:560
  87.6 2.2 %collective-permute-start.19 = (bf16[32,4096]{1,0:T(8,128)(2,1)S(1)}, bf16[32,4096]{1,0:T(8,128)(2,1)S(1)}, u32[]{:S(2)}, u32[]{:S(2)}) collective-permute-start(bf16[32,4096]{1,0:T(8,128)(2,1)S(1)} %get-tuple-element.43), channel_id=1, source_target_pairs={{0,3},{1,2},{2,1},{3,0},{4,7},{5,6},{6,5},{7,4},{8,11},{9,10},{10,... | collective-permute-start | bytes 786440 | tf_op jit(solution)/shard_map/ppermute | solution.py:560
  89.7 0.7 collective-permute-start.20
  90.5 4.7 %collective-permute-done.18 = bf16[32,4096]{1,0:T(8,128)(2,1)S(1)} collective-permute-done((bf16[32,4096]{1,0:T(8,128)(2,1)S(1)}, bf16[32,4096]{1,0:T(8,128)(2,1)S(1)}, u32[]{:S(2)}, u32[]{:S(2)}) %collective-permute-start.18) | collective-permute-done | bytes 262176 | tf_op jit(solution)/shard_map/ppermute | solution.py:560
  95.1 4.1 %collective-permute-done.19 = bf16[32,4096]{1,0:T(8,128)(2,1)S(1)} collective-permute-done((bf16[32,4096]{1,0:T(8,128)(2,1)S(1)}, bf16[32,4096]{1,0:T(8,128)(2,1)S(1)}, u32[]{:S(2)}, u32[]{:S(2)}) %collective-permute-start.19) | collective-permute-done | bytes 262176 | tf_op jit(solution)/shard_map/ppermute | solution.py:560
  99.2 1.5 %collective-permute-done.20 = bf16[32,4096]{1,0:T(8,128)(2,1)S(1)} collective-permute-done((bf16[32,4096]{1,0:T(8,128)(2,1)S(1)}, bf16[32,4096]{1,0:T(8,128)(2,1)S(1)}, u32[]{:S(2)}, u32[]{:S(2)}) %collective-permute-start.20) | collective-permute-done | bytes 262176 | tf_op jit(solution)/shard_map/ppermute | solution.py:560
  100.8 0.8 add_convert_fusion
  (23 shorter events, 0.2 us)
Async XLA Ops:
  0.0 60.1 %copy-start.5 = (f32[128]{0:T(128)S(1)}, f32[128]{0:T(128)}, u32[]{:S(2)}) copy-start(f32[128]{0:T(128)} %param.13) | copy-start | bytes 1540
  0.1 1.0 copy-start
  1.0 0.9 copy-start.1
  2.0 0.9 copy-start.2
  2.9 0.7 copy-start.3
  3.6 0.7 copy-start.4
  4.3 59.6 %copy-start.6 = (bf16[8,128,384]{2,1,0:T(8,128)(2,1)S(1)}, bf16[8,128,384]{2,1,0:T(8,128)(2,1)}, u32[]{:S(2)}) copy-start(bf16[8,128,384]{2,1,0:T(8,128)(2,1)} %weight_ref.3) | copy-start | bytes 2359300
  5.4 1.4 %collective-permute-start = (bf16[4,128,128]{2,1,0:T(8,128)(2,1)S(1)}, bf16[4,128,128]{2,1,0:T(8,128)(2,1)S(1)}, u32[]{:S(2)}, u32[]{:S(2)}) collective-permute-start(bf16[4,128,128]{2,1,0:T(8,128)(2,1)S(1)} %get-tuple-element.26), channel_id=1, source_target_pairs={{0,4},{4,0},{8,12},{12,8},{16,20},{20,16},{24,28},{28,24},{32,36},... | collective-permute-start | bytes 393224 | tf_op jit(solution)/shard_map/ppermute | solution.py:518
  5.5 1.7 %collective-permute-start.4 = (bf16[4,272,128]{2,1,0:T(8,128)(2,1)S(1)}, bf16[4,272,128]{2,1,0:T(8,128)(2,1)S(1)}, u32[]{:S(2)}, u32[]{:S(2)}) collective-permute-start(bf16[4,272,128]{2,1,0:T(8,128)(2,1)S(1)} %get-tuple-element.28), channel_id=1, source_target_pairs={{0,4},{4,0},{8,12},{12,8},{16,20},{20,16},{24,28},{28,24},{32,36},... | collective-permute-start | bytes 835592 | tf_op jit(solution)/shard_map/ppermute | solution.py:518
  7.3 9.4 %collective-permute-start.5 = (bf16[2,272,128]{2,1,0:T(8,128)(2,1)S(1)}, bf16[2,272,128]{2,1,0:T(8,128)(2,1)S(1)}, u32[]{:S(2)}, u32[]{:S(2)}) collective-permute-start(bf16[2,272,128]{2,1,0:T(8,128)(2,1)S(1)} %pad_maximum_fusion), channel_id=1, source_target_pairs={{0,8},{4,12},{8,0},{12,4},{16,24},{20,28},{24,16},{28,20},{32,40},... | collective-permute-start | bytes 417800 | tf_op jit(solution)/shard_map/ppermute | solution.py:518
  8.9 10.2 %collective-permute-start.6 = (bf16[2,272,128]{2,1,0:T(8,128)(2,1)S(1)}, bf16[2,272,128]{2,1,0:T(8,128)(2,1)S(1)}, u32[]{:S(2)}, u32[]{:S(2)}) collective-permute-start(bf16[2,272,128]{2,1,0:T(8,128)(2,1)S(1)} %pad_maximum_fusion.1), channel_id=1, source_target_pairs={{0,16},{4,20},{8,24},{12,28},{16,0},{20,4},{24,8},{28,12},{32,48},... | collective-permute-start | bytes 417800 | tf_op jit(solution)/shard_map/ppermute | solution.py:518
  11.7 10.8 %collective-permute-start.7 = (bf16[2,272,128]{2,1,0:T(8,128)(2,1)S(1)}, bf16[2,272,128]{2,1,0:T(8,128)(2,1)S(1)}, u32[]{:S(2)}, u32[]{:S(2)}) collective-permute-start(bf16[2,272,128]{2,1,0:T(8,128)(2,1)S(1)} %pad_maximum_fusion.2), channel_id=1, source_target_pairs={{0,24},{4,28},{8,16},{12,20},{16,8},{20,12},{24,0},{28,4},{32,56},... | collective-permute-start | bytes 417800 | tf_op jit(solution)/shard_map/ppermute | solution.py:518
  12.3 43.6 %collective-permute-start.1 = (bf16[2,128,128]{2,1,0:T(8,128)(2,1)S(1)}, bf16[2,128,128]{2,1,0:T(8,128)(2,1)S(1)}, u32[]{:S(2)}, u32[]{:S(2)}) collective-permute-start(bf16[2,128,128]{2,1,0:T(8,128)(2,1)S(1)} %pad_maximum_fusion.3), channel_id=1, source_target_pairs={{0,8},{4,12},{8,0},{12,4},{16,24},{20,28},{24,16},{28,20},{32,40},... | collective-permute-start | bytes 196616 | tf_op jit(solution)/shard_map/ppermute | solution.py:518
  12.7 43.2 %collective-permute-start.2 = (bf16[2,128,128]{2,1,0:T(8,128)(2,1)S(1)}, bf16[2,128,128]{2,1,0:T(8,128)(2,1)S(1)}, u32[]{:S(2)}, u32[]{:S(2)}) collective-permute-start(bf16[2,128,128]{2,1,0:T(8,128)(2,1)S(1)} %pad_maximum_fusion.4), channel_id=1, source_target_pairs={{0,16},{4,20},{8,24},{12,28},{16,0},{20,4},{24,8},{28,12},{32,48},... | collective-permute-start | bytes 196616 | tf_op jit(solution)/shard_map/ppermute | solution.py:518
  22.5 60.9 %slice-start = ((s8[8388608]{0:T(1024)(128)(4,1)}), s8[4194304]{0:T(1024)(128)(4,1)S(1)}, s32[]{:S(2)}) async-start(s8[8388608]{0:T(1024)(128)(4,1)} %bitcast.4), calls=%async_computation | async-start | bytes 8388608
  33.7 10.6 %collective-permute-start.9 = (bf16[128,256]{1,0:T(8,128)(2,1)S(1)}, bf16[128,256]{1,0:T(8,128)(2,1)S(1)}, u32[]{:S(2)}, u32[]{:S(2)}) collective-permute-start(bf16[128,256]{1,0:T(8,128)(2,1)S(1)} %get-tuple-element.33.own_ref), channel_id=1, source_target_pairs={{0,64},{4,68},{8,72},{12,76},{16,80},{20,84},{24,88},{28,92},{32,9... | collective-permute-start | bytes 196616 | tf_op jit(solution)/shard_map/ppermute | solution.py:535
  40.1 6.2 %collective-permute-start.8 = (bf16[128,256]{1,0:T(8,128)(2,1)S(1)}, bf16[128,256]{1,0:T(8,128)(2,1)S(1)}, u32[]{:S(2)}, u32[]{:S(2)}) collective-permute-start(bf16[128,256]{1,0:T(8,128)(2,1)S(1)} %get-tuple-element.33.own_ref), channel_id=1, source_target_pairs={{0,32},{4,36},{8,40},{12,44},{16,48},{20,52},{24,56},{28,60},{32,6... | collective-permute-start | bytes 196616 | tf_op jit(solution)/shard_map/ppermute | solution.py:535
  43.0 0.7 collective-permute-start.10
  43.7 12.2 %collective-permute-start.3 = (bf16[2,128,128]{2,1,0:T(8,128)(2,1)S(1)}, bf16[2,128,128]{2,1,0:T(8,128)(2,1)S(1)}, u32[]{:S(2)}, u32[]{:S(2)}) collective-permute-start(bf16[2,128,128]{2,1,0:T(8,128)(2,1)S(1)} %pad_maximum_fusion.5), channel_id=1, source_target_pairs={{0,24},{4,28},{8,16},{12,20},{16,8},{20,12},{24,0},{28,4},{32,56},... | collective-permute-start | bytes 196616 | tf_op jit(solution)/shard_map/ppermute | solution.py:518
  46.8 13.3 %collective-permute-start.12 = (bf16[128,128]{1,0:T(8,128)(2,1)S(1)}, bf16[128,128]{1,0:T(8,128)(2,1)S(1)}, u32[]{:S(2)}, u32[]{:S(2)}) collective-permute-start(bf16[128,128]{1,0:T(8,128)(2,1)S(1)} %get-tuple-element.35), channel_id=1, source_target_pairs={{32,160},{36,164},{40,168},{44,172},{48,176},{52,180},{56,184},{60... | collective-permute-start | bytes 98312 | tf_op jit(solution)/shard_map/ppermute | solution.py:535
  50.3 9.7 %collective-permute-start.11 = (bf16[128,256]{1,0:T(8,128)(2,1)S(1)}, bf16[128,256]{1,0:T(8,128)(2,1)S(1)}, u32[]{:S(2)}, u32[]{:S(2)}) collective-permute-start(bf16[128,256]{1,0:T(8,128)(2,1)S(1)} %get-tuple-element.34), channel_id=1, source_target_pairs={{0,32},{4,36},{8,40},{12,44},{16,48},{20,52},{24,56},{28,60},{32,6... | collective-permute-start | bytes 196616 | tf_op jit(solution)/shard_map/ppermute | solution.py:535
  55.9 27.5 %slice-start.1 = ((s8[8388608]{0:T(1024)(128)(4,1)}), s8[4194304]{0:T(1024)(128)(4,1)S(1)}, s32[]{:S(2)}) async-start(s8[8388608]{0:T(1024)(128)(4,1)} %bitcast.4), calls=%async_computation.1 | async-start | bytes 8388608
  60.6 8.3 %collective-permute-start.13 = (bf16[1024,128]{1,0:T(8,128)(2,1)S(1)}, bf16[1024,128]{1,0:T(8,128)(2,1)S(1)}, u32[]{:S(2)}, u32[]{:S(2)}) collective-permute-start(bf16[1024,128]{1,0:T(8,128)(2,1)S(1)} %norm.1.normed_ref), channel_id=1, source_target_pairs={{0,32},{4,36},{8,40},{12,44},{16,48},{20,52},{24,56},{28,60},{32,6... | collective-permute-start | bytes 786440 | tf_op jit(solution)/shard_map/ppermute | solution.py:535
  72.0 1.4 %collective-permute-start.14 = (bf16[4,128,128]{2,1,0:T(8,128)(2,1)S(1)}, bf16[4,128,128]{2,1,0:T(8,128)(2,1)S(1)}, u32[]{:S(2)}, u32[]{:S(2)}) collective-permute-start(bf16[4,128,128]{2,1,0:T(8,128)(2,1)S(1)} %get-tuple-element.40), channel_id=1, source_target_pairs={{0,4},{4,0},{8,12},{12,8},{16,20},{20,16},{24,28},{28,24},{32,36},... | collective-permute-start | bytes 393224 | tf_op jit(solution)/shard_map/ppermute | solution.py:518
  73.5 5.0 %collective-permute-start.15 = (bf16[2,128,128]{2,1,0:T(8,128)(2,1)S(1)}, bf16[2,128,128]{2,1,0:T(8,128)(2,1)S(1)}, u32[]{:S(2)}, u32[]{:S(2)}) collective-permute-start(bf16[2,128,128]{2,1,0:T(8,128)(2,1)S(1)} %pad_maximum_fusion.6), channel_id=1, source_target_pairs={{0,8},{4,12},{8,0},{12,4},{16,24},{20,28},{24,16},{28,20},{32,40},... | collective-permute-start | bytes 196616 | tf_op jit(solution)/shard_map/ppermute | solution.py:518
  73.6 7.7 %collective-permute-start.16 = (bf16[2,128,128]{2,1,0:T(8,128)(2,1)S(1)}, bf16[2,128,128]{2,1,0:T(8,128)(2,1)S(1)}, u32[]{:S(2)}, u32[]{:S(2)}) collective-permute-start(bf16[2,128,128]{2,1,0:T(8,128)(2,1)S(1)} %pad_maximum_fusion.7), channel_id=1, source_target_pairs={{0,16},{4,20},{8,24},{12,28},{16,0},{20,4},{24,8},{28,12},{32,48},... | collective-permute-start | bytes 196616 | tf_op jit(solution)/shard_map/ppermute | solution.py:518
  77.9 5.6 %collective-permute-start.17 = (bf16[2,128,128]{2,1,0:T(8,128)(2,1)S(1)}, bf16[2,128,128]{2,1,0:T(8,128)(2,1)S(1)}, u32[]{:S(2)}, u32[]{:S(2)}) collective-permute-start(bf16[2,128,128]{2,1,0:T(8,128)(2,1)S(1)} %pad_maximum_fusion.8), channel_id=1, source_target_pairs={{0,24},{4,28},{8,16},{12,20},{16,8},{20,12},{24,0},{28,4},{32,56},... | collective-permute-start | bytes 196616 | tf_op jit(solution)/shard_map/ppermute | solution.py:518
  85.9 9.3 %collective-permute-start.18 = (bf16[32,4096]{1,0:T(8,128)(2,1)S(1)}, bf16[32,4096]{1,0:T(8,128)(2,1)S(1)}, u32[]{:S(2)}, u32[]{:S(2)}) collective-permute-start(bf16[32,4096]{1,0:T(8,128)(2,1)S(1)} %get-tuple-element.42), channel_id=1, source_target_pairs={{0,1},{1,0},{2,3},{3,2},{4,5},{5,4},{6,7},{7,6},{8,9},{9,8},{10,11... | collective-permute-start | bytes 786440 | tf_op jit(solution)/shard_map/ppermute | solution.py:560
  87.6 11.7 %collective-permute-start.19 = (bf16[32,4096]{1,0:T(8,128)(2,1)S(1)}, bf16[32,4096]{1,0:T(8,128)(2,1)S(1)}, u32[]{:S(2)}, u32[]{:S(2)}) collective-permute-start(bf16[32,4096]{1,0:T(8,128)(2,1)S(1)} %get-tuple-element.43), channel_id=1, source_target_pairs={{0,3},{1,2},{2,1},{3,0},{4,7},{5,6},{6,5},{7,4},{8,11},{9,10},{10,... | collective-permute-start | bytes 786440 | tf_op jit(solution)/shard_map/ppermute | solution.py:560
  89.7 11.0 %collective-permute-start.20 = (bf16[32,4096]{1,0:T(8,128)(2,1)S(1)}, bf16[32,4096]{1,0:T(8,128)(2,1)S(1)}, u32[]{:S(2)}, u32[]{:S(2)}) collective-permute-start(bf16[32,4096]{1,0:T(8,128)(2,1)S(1)} %get-tuple-element.44), channel_id=1, source_target_pairs={{0,2},{1,3},{2,0},{3,1},{4,6},{5,7},{6,4},{7,5},{8,10},{9,11},{10,... | collective-permute-start | bytes 786440 | tf_op jit(solution)/shard_map/ppermute | solution.py:560

commit v3 on v2

--- a/solution.py
+++ b/solution.py
@@ -12,14 +12,13 @@
 PLANES = 8
 BLK = 2 * C + 16
 B = 16
-GROUP = 4
 EPS = 1e-06
 NEG = -1e30
 VMEM_LIMIT = 24 * 1024 * 1024
 
 
-def params():
-    return pltpu.CompilerParams(vmem_limit_bytes=VMEM_LIMIT)
+def params(limit=VMEM_LIMIT):
+    return pltpu.CompilerParams(vmem_limit_bytes=limit)
 
 
 def cost(flops, nbytes, trans=0):
@@ -112,7 +111,7 @@
 
 
 def pack(me, q, k, v, decay, beta):
-    any_space = pl.BlockSpec(memory_space=pl.ANY)
+    any_space = pl.BlockSpec(memory_space=pltpu.HBM)
     wide = jax.ShapeDtypeStruct((4, BLK, C), BF16)
     thin = jax.ShapeDtypeStruct((4, C, C), BF16)
     return pl.pallas_call(
@@ -125,7 +124,7 @@
             pltpu.VMEM((2, PLANE, C), F32),
             pltpu.SemaphoreType.DMA((26,)),
         ],
-        compiler_params=params(),
+        compiler_params=params(60 * 1024 * 1024),
         name="pack",
     )(me, q, k, v, decay, beta)
 
@@ -139,19 +138,30 @@
         out_ref[2 * dx + 1] = refs[dx + 1][1]
 
 
-def gates(pieces):
+def gates(kv_ref):
     row, col = iotas()
+    pieces = jnp.concatenate([kv_ref[d, 2 * C :, :] for d in range(PLANE)], axis=0)
     upper = jnp.where(row <= col, 1.0, 0.0).astype(BF16)
     lower = jnp.where(row >= col, 1.0, 0.0).astype(BF16)
     eye = jnp.where(row == col, 1.0, 0.0).astype(BF16)
     along_row = dot(pieces, upper)
     along_col = dot_nt(jnp.concatenate([lower, eye], axis=0), pieces)
     plain = pieces.astype(F32)
-    g_row = -(along_row[0:1] + along_row[1:2] + along_row[2:3])
-    b_row = plain[3:4] + plain[4:5] + plain[5:6]
-    g_col = -(along_col[:C, 0:1] + along_col[:C, 1:2] + along_col[:C, 2:3])
-    b_col = along_col[C:, 3:4] + along_col[C:, 4:5] + along_col[C:, 5:6]
-    return g_row, b_row, g_col, b_col
+    found = []
+    for d in range(PLANE):
+        o = 16 * d
+        g_row = -(along_row[o : o + 1] + along_row[o + 1 : o + 2] + along_row[o + 2 : o + 3])
+        b_row = plain[o + 3 : o + 4] + plain[o + 4 : o + 5] + plain[o + 5 : o + 6]
+        g_col = -(
+            along_col[:C, o : o + 1] + along_col[:C, o + 1 : o + 2] + along_col[:C, o + 2 : o + 3]
+        )
+        b_col = (
+            along_col[C:, o + 3 : o + 4]
+            + along_col[C:, o + 4 : o + 5]
+            + along_col[C:, o + 5 : o + 6]
+        )
+        found.append((g_row, b_row, g_col, b_col))
+    return found
 
 
 def base_inverses(packed):
@@ -177,74 +187,61 @@
 
 def prep_kernel(me_ref, *refs):
     kv_ref, mix_ref, wu_ref, ab_ref, level_ref = refs[5:10]
-    maps, lows, packs, r_cols, ends = refs[10:]
+    maps = refs[10]
     me = me_ref[0]
     row, col = iotas()
     gather_slots(refs[:5], kv_ref)
+    every = range(PLANE)
     blocks = (row // B) == (col // B)
-
-    def first(step, _):
-        for i in range(GROUP):
-            d = step * GROUP + i
-            keys = kv_ref[d, 0:C, :]
-            g_row, b_row, g_col, b_col = gates(kv_ref[d, 2 * C :, :])
-            gram = dot_nt(keys, keys)
-            diag = jnp.where(row == col, gram, 0.0)
-            r_col = lax.rsqrt(jnp.sum(diag, axis=1, keepdims=True) + EPS)
-            r_row = lax.rsqrt(jnp.sum(diag, axis=0, keepdims=True) + EPS)
-            ratio = jnp.where(row >= col, jnp.exp(jnp.minimum(g_col - g_row, 0.0)), 0.0)
-            mix = ratio * (b_row * r_row)
-            mix_ref[d] = mix
-            low = jnp.where(row > col, mix * gram * r_col, 0.0)
-            lows[d] = low
-            held = jnp.where(blocks, low, 0.0)
-            packed = held[0:B]
-            for b in range(1, C // B):
-                packed = packed + held[B * b : B * b + B]
-            packs[pl.ds(pl.multiple_of(d * B, B), B), :] = packed
-            g_end = g_row[:, C - 1 : C]
-            tail = jnp.exp(g_end - g_col) * b_col * r_col
-            fold = jnp.exp(g_row) * r_row
-            r_cols[d, 0] = jnp.broadcast_to(tail, (C, C))
-            r_cols[d, 1] = jnp.broadcast_to(fold, (C, C))
-            ends[d] = jnp.broadcast_to(jnp.exp(g_end), (C, C))
-        return _
-
-    lax.fori_loop(0, PLANE // GROUP, first, 0)
-    packs[...] = base_inverses(packs[...])
-
-    def second(step, _):
-        for i in range(GROUP):
-            d = step * GROUP + i
-            keys = kv_ref[d, 0:C, :]
-            values = kv_ref[d, C : 2 * C, :]
-            low = lows[d]
-            x = packs[pl.ds(pl.multiple_of(d * B, B), B), :]
-            x = jnp.where(blocks, jnp.concatenate([x] * (C // B), axis=0), 0.0)
-            size = B
-            while size < C:
-                apart = jnp.bitwise_xor(row, col)
-                corner = jnp.where((row > col) & (apart >= size) & (apart < 2 * size), low, 0.0)
-                x = x - mm(mm(x, corner), x)
-                size *= 2
-            tail, fold = r_cols[d, 0], r_cols[d, 1]
-            w = mm_exact_right(x * fold, keys)
-            u = mm_exact_right(x, values)
-            wu = jnp.concatenate([w, u], axis=1)
-            wu_ref[d] = wu
-            hi, lo = split(jnp.concatenate([w * tail, u * tail], axis=1))
-            made = dot_tn(
-                jnp.concatenate([keys, keys], axis=0), jnp.concatenate([hi, lo], axis=0)
-            )
-            g_end = ends[d]
-            chunk = jnp.bitwise_xor(me, d)
-            maps[chunk] = jnp.concatenate(
-                [jnp.where(row == col, g_end, 0.0) - made[:, :C], made[:, C:]], axis=1
-            )
-        return _
-
-    lax.fori_loop(0, PLANE // GROUP, second, 0)
-    one = [maps[i] for i in range(PLANE)]
+    apart = jnp.bitwise_xor(row, col)
+    found = gates(kv_ref)
+    keys = [kv_ref[d, 0:C, :] for d in every]
+    grams = [dot_nt(k, k) for k in keys]
+    diags = [jnp.where(row == col, g, 0.0) for g in grams]
+    r_cols = [lax.rsqrt(jnp.sum(g, axis=1, keepdims=True) + EPS) for g in diags]
+    r_rows = [lax.rsqrt(jnp.sum(g, axis=0, keepdims=True) + EPS) for g in diags]
+    lows, packs = [], []
+    for d in every:
+        g_row, b_row, g_col, _ = found[d]
+        ratio = jnp.where(row >= col, jnp.exp(jnp.minimum(g_col - g_row, 0.0)), 0.0)
+        mix = ratio * (b_row * r_rows[d])
+        mix_ref[d] = mix
+        low = jnp.where(row > col, mix * grams[d] * r_cols[d], 0.0)
+        lows.append(low)
+        held = jnp.where(blocks, low, 0.0)
+        packed = held[0:B]
+        for b in range(1, C // B):
+            packed = packed + held[B * b : B * b + B]
+        packs.append(packed)
+    base = base_inverses(jnp.concatenate(packs, axis=0))
+    inverse = [
+        jnp.where(blocks, jnp.concatenate([base[B * d : B * d + B]] * (C // B), axis=0), 0.0)
+        for d in every
+    ]
+    size = B
+    while size < C:
+        level = (row > col) & (apart >= size) & (apart < 2 * size)
+        half = [mm(x, jnp.where(level, low, 0.0)) for x, low in zip(inverse, lows)]
+        inverse = [x - mm(h, x) for x, h in zip(inverse, half)]
+        size *= 2
+    folded = [inverse[d] * (jnp.exp(found[d][0]) * r_rows[d]) for d in every]
+    values = [kv_ref[d, C : 2 * C, :] for d in every]
+    w = [mm_exact_right(folded[d], keys[d]) for d in every]
+    u = [mm_exact_right(inverse[d], values[d]) for d in every]
+    halves = []
+    for d in every:
+        wu = jnp.concatenate([w[d], u[d]], axis=1)
+        wu_ref[d] = wu
+        g_row, _, g_col, b_col = found[d]
+        tail = jnp.exp(g_row[:, C - 1 : C] - g_col) * b_col * r_cols[d]
+        halves.append(jnp.concatenate(split(wu * tail), axis=0))
+    made = [dot_tn(jnp.concatenate([keys[d], keys[d]], axis=0), halves[d]) for d in every]
+    for d in every:
+        g_end = found[d][0][:, C - 1 : C]
+        maps[jnp.bitwise_xor(me, d)] = jnp.concatenate(
+            [jnp.where(row == col, jnp.exp(g_end), 0.0) - made[d][:, :C], made[d][:, C:]], axis=1
+        )
+    one = [maps[i] for i in every]
     two = [after(one[2 * i], one[2 * i + 1]) for i in range(4)]
     four = [after(two[2 * i], two[2 * i + 1]) for i in range(2)]
     ab_ref[...] = after(four[0], four[1]).astype(BF16)
@@ -266,10 +263,6 @@
         out_specs=[vmem()] * 5,
         scratch_shapes=[
             pltpu.VMEM((PLANE, C, 2 * C), F32),
-            pltpu.VMEM((PLANE, C, C), F32),
-            pltpu.VMEM((C, C), F32),
-            pltpu.VMEM((PLANE, 2, C, C), F32),
-            pltpu.VMEM((PLANE, C, C), F32),
         ],
         compiler_params=params(),
         cost_estimate=cost(2e9, 4e6),
@@ -292,24 +285,27 @@
     before[6] = six
     before[7] = after(six, level_ref[6])
 
-    def one(step, _):
-        for i in range(GROUP):
-            d = step * GROUP + i
-            keys = kv_ref[d, 0:C, :]
-            g_row, b_row, g_col, b_col = gates(kv_ref[d, 2 * C :, :])
-            queries = queries_ref[d]
-            wide = queries.astype(F32)
-            r_col = lax.rsqrt(jnp.sum(wide * wide, axis=1, keepdims=True) + EPS) * (C**-0.5)
-            scored = dot_nt(queries, keys) * r_col * mix_ref[d]
-            part = mm(scored, wu_ref[d])
-            reach = wide * (r_col * jnp.exp(g_col)) - part[:, :C]
-            chunk = jnp.bitwise_xor(me, d)
-            both = mm(reach, before[chunk])
-            rows = pl.ds(pl.multiple_of(chunk * C, C), C)
-            no_ref[rows, :] = jnp.concatenate([both[:, :C], both[:, C:] + part[:, C:]], axis=1)
-        return _
-
-    lax.fori_loop(0, PLANE // GROUP, one, 0)
+    every = range(PLANE)
+    found = gates(kv_ref)
+    queries = [queries_ref[d] for d in every]
+    scored = [dot_nt(queries[d], kv_ref[d, 0:C, :]) for d in every]
+    r_cols = []
+    for q in queries:
+        wide = q.astype(F32)
+        r_cols.append(lax.rsqrt(jnp.sum(wide * wide, axis=1, keepdims=True) + EPS) * (C**-0.5))
+    scored = [scored[d] * r_cols[d] * mix_ref[d] for d in every]
+    parts = [mm(scored[d], wu_ref[d]) for d in every]
+    reach = [
+        queries[d].astype(F32) * (r_cols[d] * jnp.exp(found[d][2])) - parts[d][:, :C]
+        for d in every
+    ]
+    chunks = [jnp.bitwise_xor(me, d) for d in every]
+    both = [mm(reach[d], before[chunks[d]]) for d in every]
+    for d in every:
+        rows = pl.ds(pl.multiple_of(chunks[d] * C, C), C)
+        no_ref[rows, :] = jnp.concatenate(
+            [both[d][:, :C], both[d][:, C:] + parts[d][:, C:]], axis=1
+        )
 
 
 def query(me, slots, kv, mix, wu, level):
@@ -328,54 +324,57 @@
     )(me, *slots, kv, mix, wu, level)
 
 
-def combine_kernel(own_ref, one_ref, two_ref, three_ref, out_ref, b_ref):
-    def times(a, x):
-        hi, lo = split(x)
-        return dot(a, hi) + dot(a, lo)
-
-    state = two_ref[:, C:].astype(F32) + dot(two_ref[:, :C], three_ref[...])
-    state = one_ref[:, C:].astype(F32) + times(one_ref[:, :C], state)
-    state = own_ref[:, C:].astype(F32) + times(own_ref[:, :C], state)
-    reach = times(own_ref[:, :C], dot(one_ref[:, :C], two_ref[:, :C]))
-    out_ref[:, :C] = reach.astype(BF16)
-    out_ref[:, C:] = state.astype(BF16)
-    b_ref[...] = state.astype(BF16)
-
-
-def combine(own_map, one, two, three):
+def times(a, x):
+    hi, lo = split(x)
+    return dot(jnp.concatenate([a, a], axis=1), jnp.concatenate([hi, lo], axis=0))
+
+
+def combine_kernel(own_ref, one_ref, two_ref, before_ref, upto_ref):
+    a_one, a_own = one_ref[:, :C], own_ref[:, :C]
+    reach = dot(a_one, two_ref[:, :C])
+    state = one_ref[:, C:].astype(F32) + dot(a_one, two_ref[:, C:])
+    before_ref[:, :C] = reach
+    before_ref[:, C:] = state
+    upto_ref[:, :C] = times(a_own, reach).astype(BF16)
+    upto_ref[:, C:] = (own_ref[:, C:].astype(F32) + times(a_own, state)).astype(BF16)
+
+
+def combine(own_map, one, two):
     return pl.pallas_call(
         combine_kernel,
         out_shape=[
+            jax.ShapeDtypeStruct((C, 2 * C), F32),
             jax.ShapeDtypeStruct((C, 2 * C), BF16),
-            jax.ShapeDtypeStruct((C, C), BF16),
         ],
-        in_specs=[vmem()] * 4,
+        in_specs=[vmem()] * 3,
         out_specs=[vmem()] * 2,
         compiler_params=params(),
         name="combine",
-    )(own_map, one, two, three)
-
-
-def norm_kernel(no_ref, gain_ref, near_ref, far_ref, normed_ref):
-    state = dot(near_ref[:, :C], far_ref[...]) + near_ref[:, C:].astype(F32)
+    )(own_map, one, two)
+
+
+def norm_kernel(no_ref, gain_ref, before_ref, three_ref, six_ref, normed_ref):
+    state = three_ref[:, C:].astype(F32) + dot(three_ref[:, :C], six_ref[:, C:])
+    state = before_ref[:, C:] + mm(before_ref[:, :C], state)
     out = mm(no_ref[:, :C], state) + no_ref[:, C:]
     scale = lax.rsqrt(jnp.mean(out * out, axis=1, keepdims=True) + EPS)
     normed_ref[...] = (out * scale * gain_ref[...]).astype(BF16)
 
 
-def norm(no, gain, near, far):
+def norm(no, gain, before, three, six):
     return pl.pallas_call(
         norm_kernel,
         out_shape=jax.ShapeDtypeStruct((PLANE * C, C), BF16),
-        in_specs=[vmem()] * 4,
+        in_specs=[vmem()] * 5,
         out_specs=vmem(),
         compiler_params=params(),
         cost_estimate=cost(2e8, 2e6),
         name="norm",
-    )(no, gain, near, far)
+    )(no, gain, before, three, six)
 
 
 QB = 256
+SCALE = C**-0.5 * 1.4426950408889634
 
 
 def own_kernel(me_ref, normed_ref, weight_ref, acc_ref, stat_ref, q2_ref):
@@ -383,18 +382,18 @@
     q2_ref[...] = proj[:, :C]
     row = lax.broadcasted_iota(jnp.int32, (QB, QB), 0)
     col = lax.broadcasted_iota(jnp.int32, (QB, QB), 1)
-    for i in range(PLANE * C // QB):
-        at = i * QB
-        q = proj[at : at + QB, :C]
-        s = dot_nt(q, proj[: at + QB, C : 2 * C]) * (C**-0.5)
-        last = jnp.where(col <= row, s[:, at:], NEG)
-        s = last if i == 0 else jnp.concatenate([s[:, :at], last], axis=1)
-        top = jnp.max(s, axis=1, keepdims=True)
-        p = jnp.exp(s - top)
-        total = jnp.sum(p, axis=1, keepdims=True)
-        acc_ref[at : at + QB, :] = dot(p.astype(BF16), proj[: at + QB, 2 * C :])
-        stat_ref[0, at : at + QB, :] = jnp.broadcast_to(top, (QB, C))
-        stat_ref[1, at : at + QB, :] = jnp.broadcast_to(total, (QB, C))
+    starts = range(0, PLANE * C, QB)
+    scores = [dot_nt(proj[at : at + QB, :C], proj[: at + QB, C : 2 * C]) for at in starts]
+    for i, at in enumerate(starts):
+        last = jnp.where(col <= row, scores[i][:, at:], NEG)
+        scores[i] = last if i == 0 else jnp.concatenate([scores[i][:, :at], last], axis=1)
+    tops = [jnp.max(s, axis=1, keepdims=True) for s in scores]
+    raised = [jnp.exp2((s - top) * SCALE) for s, top in zip(scores, tops)]
+    totals = [jnp.sum(p, axis=1, keepdims=True) for p in raised]
+    for i, at in enumerate(starts):
+        acc_ref[at : at + QB, :] = dot(raised[i].astype(BF16), proj[: at + QB, 2 * C :])
+        stat_ref[0, at : at + QB, :] = jnp.broadcast_to(tops[i], (QB, C))
+        stat_ref[1, at : at + QB, :] = jnp.broadcast_to(totals[i], (QB, C))
 
 
 def own(me, normed, weight):
@@ -430,20 +429,30 @@
     me, plane = me_ref[0], me_ref[1]
     proj = dot(halo_ref[...], weight_ref[0, :, C:]).astype(BF16)
     n = PLANE * C
-    for i in range(n // QB):
-        at = i * QB
-        row = lax.broadcasted_iota(jnp.int32, (QB, n - at), 0)
-        col = lax.broadcasted_iota(jnp.int32, (QB, n - at), 1)
-        allowed = (col > row) & (plane > 0)
-        s = dot_nt(q2_ref[at : at + QB, :], proj[at:, :C]) * (C**-0.5)
-        s = jnp.where(allowed, s, NEG)
-        before = stat_ref[0, at : at + QB, 0:1]
-        top = jnp.maximum(jnp.max(s, axis=1, keepdims=True), before)
-        p = jnp.where(allowed, jnp.exp(s - top), 0.0)
-        fade = jnp.exp(before - top)
-        total = jnp.sum(p, axis=1, keepdims=True) + fade * stat_ref[1, at : at + QB, 0:1]
-        acc = acc_ref[at : at + QB, :] * fade + dot(p.astype(BF16), proj[at:, C:])
-        attended[at : at + QB, :] = (acc / total).astype(BF16)
+    row = lax.broadcasted_iota(jnp.int32, (QB, QB), 0)
+    col = lax.broadcasted_iota(jnp.int32, (QB, QB), 1)
+    starts = range(0, n, QB)
+    floor = jnp.where(plane > 0, 0.0, NEG)
+    scores = [dot_nt(q2_ref[at : at + QB, :], proj[at:, :C]) for at in starts]
+    for i, at in enumerate(starts):
+        first = jnp.where(col > row, scores[i][:, :QB], NEG)
+        scores[i] = (
+            first if at + QB == n else jnp.concatenate([first, scores[i][:, QB:]], axis=1)
+        )
+    before = [stat_ref[0, at : at + QB, 0:1] for at in starts]
+    tops = [
+        jnp.maximum(jnp.max(s, axis=1, keepdims=True) + floor, old)
+        for s, old in zip(scores, before)
+    ]
+    raised = [jnp.exp2((s - (top - floor)) * SCALE) for s, top in zip(scores, tops)]
+    fades = [jnp.exp2((old - top) * SCALE) for old, top in zip(before, tops)]
+    totals = [
+        jnp.sum(raised[i], axis=1, keepdims=True) + fades[i] * stat_ref[1, at : at + QB, 0:1]
+        for i, at in enumerate(starts)
+    ]
+    for i, at in enumerate(starts):
+        acc = acc_ref[at : at + QB, :] * fades[i] + dot(raised[i].astype(BF16), proj[at:, C:])
+        attended[at : at + QB, :] = (acc / totals[i]).astype(BF16)
     for d in range(PLANE):
         chunk = jnp.bitwise_xor(me, d)
         out = send if d % 2 else keep
@@ -526,12 +535,9 @@
     return slots[:2] + [pair for _, pair in sorted(slots[2:], key=lambda item: item[0])]
 
 
-def later_plane(block, distance, first=0, last=PLANES - 1):
+def later_plane(block, distance):
     step = PLANE * distance
-    route = []
-    for z in range(first, last + 1):
-        if z + distance < PLANES:
-            route += [(z * PLANE + i, z * PLANE + i + step) for i in range(PLANE)]
+    route = [(s, s + step) for s in range(PLANE * PLANES - step)]
     return lax.ppermute(block, "seq", route)
 
 
@@ -541,16 +547,16 @@
     me = jnp.stack([place % PLANE, place // PLANE, mine]).astype(jnp.int32)
     keep, send, keep_q, send_q = pack(me, q_delta, k_delta, v_delta, decay, beta)
     slots = exchange(keep, send)
-    slots_q = exchange(keep_q, send_q)
     kv, mix, wu, ab, level = prep(me, slots)
     one = later_plane(ab, 1)
     two = later_plane(ab, 2)
-    three = later_plane(ab[:, C:], 3, 0, 0)
+    keep_q, send_q, _ = lax.optimization_barrier((keep_q, send_q, ab))
+    slots_q = exchange(keep_q, send_q)
     no = query(me, slots_q, kv, mix, wu, level)
-    reach, state = combine(ab, one, two, three)
-    near = later_plane(reach, 1)
-    far = later_plane(state, 4, 1, 3)
-    normed = norm(no, gain[None, :], near, far)
+    before, upto = combine(ab, one, two)
+    three = later_plane(upto, 3)
+    six = later_plane(upto, 6)
+    normed = norm(no, gain[None, :], before, three, six)
     halo = later_plane(normed, 1)
     acc, stat, q2 = own(me, normed, attn_weight)
     attended = exchange(*halo_part(me, halo, attn_weight, acc, stat, q2))

time: 102 us -> 91 us (0.89)
  the two profiles are of different devices: /device:TPU:64 before, /device:TPU:128 now
where the time goes in v3:
time: 91 us; the launch traced here: 89.9 us
  waiting for transfers between devices  33.9 us (37%)
  starting transfers between devices  32.8 us (36%)
  Pallas kernels  18.6 us (20%)
  local copies, waits for them, and re-layouts  2.7 us (3%)
  other arithmetic  1.57 us (2%)
    ppermute x12, starting transfers between devices, swap(): lax.ppermute(block, 'seq', [(s, s ^ d) for s in range(PLANE * PLANES)])  15.1 us
    ppermute x12, waiting for transfers between devices, swap(): lax.ppermute(block, 'seq', [(s, s ^ d) for s in range(PLANE * PLANES)])  14.7 us
    ppermute x5, starting transfers between devices, later_plane(): return lax.ppermute(block, 'seq', route)  13.4 us
    ppermute x3, waiting for transfers between devices, local(): moved[d] = lax.ppermute(sums[d], 'heads', [(s, s ^ d) for s in range(4)])  10.2 us
    ppermute x5, waiting for transfers between devices, later_plane(): return lax.ppermute(block, 'seq', route)  8.98 us
    ppermute x3, starting transfers between devices, local(): moved[d] = lax.ppermute(sums[d], 'heads', [(s, s ^ d) for s in range(4)])  4.34 us
    pallas_call x1, Pallas kernels, halo_part(): pl.pallas_call(halo_kernel, out_shape=[jax.ShapeDtypeStruct((4, C, C), BF...  4.22 us
    pallas_call x1, Pallas kernels, prep(): pl.pallas_call(prep_kernel, out_shape=[jax.ShapeDtypeStruct((PLANE, BLK,...  4.05 us
  transfers between devices with their start and end apart: 20, of which 13 were waited for; matrix products, arithmetic and copies ran while one was open for 1% of the time, Pallas kernels for 5%

profile of v3, /device:TPU:128, one launch (start us, length us, event | category | flops | bytes accessed | tf_op | source)
XLA Modules:
  0.0 89.9 jit_solution(14806477719765140927)
XLA Ops:
  0.0 0.7 pad_add_fusion.me_ref
  0.7 3.0 %pack.1 = (bf16[4,272,128]{2,1,0:T(8,128)(2,1)}, bf16[4,272,128]{2,1,0:T(8,128)(2,1)}, bf16[4,128,128]{2,1,0:T(8,128)(2,1)}, bf16[4,128,128]{2,1,0:T(8,128)(2,1)}) custom-call(s32[3]{0:T(128)} %pad_add_fusion.me_ref, bf16[128,1024]{1,0:T(8,128)(2,1)} %q_ref.1, bf16[128,1024]{1,0:T(8,128)(2,1)} %k_ref.1, bf16[128,1024]{1,0:T(8,128)(2,1)} %v_ref.1, ...), custom_call_target="tpu_custom_call" | custom-call | tf_op jit(solution)/shard_map/pack/pallas_call | solution.py:117
  3.7 0.0 copy-start.6
  3.7 0.0 copy-start
  3.7 0.1 collective-permute-start
  3.8 1.0 %fusion = (bf16[1,272,128]{2,1,0:T(8,128)(2,1)S(1)}, bf16[1,272,128]{2,1,0:T(8,128)(2,1)S(1)}, bf16[1,272,128]{2,1,0:T(8,128)(2,1)S(1)}) fusion(bf16[4,272,128]{2,1,0:T(8,128)(2,1)} %get-tuple-element.29.refs_0_), kind=kLoop, calls=%fused_computation.11 | loop fusion | bytes 417792 | tf_op jit(solution)/shard_map/slice | solution.py:534
  4.8 0.8 collective-permute-done.refs_1_
  5.6 1.6 %collective-permute-start.1 = (bf16[2,272,128]{2,1,0:T(8,128)(2,1)S(1)}, bf16[2,272,128]{2,1,0:T(8,128)(2,1)S(1)}, u32[]{:S(2)}, u32[]{:S(2)}) collective-permute-start(bf16[2,272,128]{2,1,0:T(8,128)(2,1)S(1)} %pad_maximum_fusion), channel_id=1, source_target_pairs={{0,8},{4,12},{8,0},{12,4},{16,24},{20,28},{24,16},{28,20},{32,40},... | collective-permute-start | bytes 417800 | tf_op jit(solution)/shard_map/ppermute | solution.py:527
  7.2 2.8 %collective-permute-start.2 = (bf16[2,272,128]{2,1,0:T(8,128)(2,1)S(1)}, bf16[2,272,128]{2,1,0:T(8,128)(2,1)S(1)}, u32[]{:S(2)}, u32[]{:S(2)}) collective-permute-start(bf16[2,272,128]{2,1,0:T(8,128)(2,1)S(1)} %pad_maximum_fusion.1), channel_id=1, source_target_pairs={{0,16},{4,20},{8,24},{12,28},{16,0},{20,4},{24,8},{28,12},{32,48},... | collective-permute-start | bytes 417800 | tf_op jit(solution)/shard_map/ppermute | solution.py:527
  10.0 0.6 collective-permute-start.3
  10.6 1.5 %collective-permute-done.1.refs_2_ = bf16[2,272,128]{2,1,0:T(8,128)(2,1)S(1)} collective-permute-done((bf16[2,272,128]{2,1,0:T(8,128)(2,1)S(1)}, bf16[2,272,128]{2,1,0:T(8,128)(2,1)S(1)}, u32[]{:S(2)}, u32[]{:S(2)}) %collective-permute-start.1) | collective-permute-done | bytes 139296 | tf_op jit(solution)/shard_map/ppermute | solution.py:527
  12.1 4.6 %collective-permute-done.2.refs_3_ = bf16[2,272,128]{2,1,0:T(8,128)(2,1)S(1)} collective-permute-done((bf16[2,272,128]{2,1,0:T(8,128)(2,1)S(1)}, bf16[2,272,128]{2,1,0:T(8,128)(2,1)S(1)}, u32[]{:S(2)}, u32[]{:S(2)}) %collective-permute-start.2) | collective-permute-done | bytes 139296 | tf_op jit(solution)/shard_map/ppermute | solution.py:527
  16.7 2.4 %collective-permute-done.3.refs_4_ = bf16[2,272,128]{2,1,0:T(8,128)(2,1)S(1)} collective-permute-done((bf16[2,272,128]{2,1,0:T(8,128)(2,1)S(1)}, bf16[2,272,128]{2,1,0:T(8,128)(2,1)S(1)}, u32[]{:S(2)}, u32[]{:S(2)}) %collective-permute-start.3) | collective-permute-done | bytes 139296 | tf_op jit(solution)/shard_map/ppermute | solution.py:527
  19.1 1.0 %copy-done.1 = bf16[4,272,128]{2,1,0:T(8,128)(2,1)S(1)} copy-done((bf16[4,272,128]{2,1,0:T(8,128)(2,1)S(1)}, bf16[4,272,128]{2,1,0:T(8,128)(2,1)}, u32[]{:S(2)}) %copy-start.1) | copy-done | bytes 278552
  20.1 0.7 copy-done.2
  20.8 4.1 %prep.1 = (bf16[8,272,128]{2,1,0:T(8,128)(2,1)S(1)}, f32[8,128,128]{2,1,0:T(8,128)S(1)}, f32[8,128,256]{2,1,0:T(8,128)S(1)}, bf16[128,256]{1,0:T(8,128)(2,1)S(1)}, f32[7,128,256]{2,1,0:T(8,128)S(1)}) custom-call(s32[3]{0:T(128)S(1)} %copy-done.2, bf16[4,272,128]{2,1,0:T(8,128)(2,1)S(1)} %copy-done.1, bf16[4,272,128]{2,1,0:T(8,128)(2,1)S(1)} %collective-permute-done.refs_1_, ...), custom_call_target="tpu_custom_call" | custom-call | flops 2000000000 | bytes 4000000 | tf_op jit(solution)/shard_map/prep/pallas_call | solution.py:253
  24.8 0.0 slice-start
  24.8 3.2 %collective-permute-start.8 = (bf16[128,256]{1,0:T(8,128)(2,1)S(1)}, bf16[128,256]{1,0:T(8,128)(2,1)S(1)}, u32[]{:S(2)}, u32[]{:S(2)}) collective-permute-start(bf16[128,256]{1,0:T(8,128)(2,1)S(1)} %get-tuple-element.31.own_ref), channel_id=1, source_target_pairs={{0,32},{4,36},{8,40},{12,44},{16,48},{20,52},{24,56},{28,60},{32,6... | collective-permute-start | bytes 196616 | tf_op jit(solution)/shard_map/ppermute | solution.py:541
  28.0 3.4 %collective-permute-start.9 = (bf16[128,256]{1,0:T(8,128)(2,1)S(1)}, bf16[128,256]{1,0:T(8,128)(2,1)S(1)}, u32[]{:S(2)}, u32[]{:S(2)}) collective-permute-start(bf16[128,256]{1,0:T(8,128)(2,1)S(1)} %get-tuple-element.31.own_ref), channel_id=1, source_target_pairs={{0,64},{4,68},{8,72},{12,76},{16,80},{20,84},{24,88},{28,92},{32,9... | collective-permute-start | bytes 196616 | tf_op jit(solution)/shard_map/ppermute | solution.py:541
  31.4 0.0 copy-done.6
  31.4 0.1 collective-permute-start.4
  31.5 0.0 copy-done
  31.6 1.3 %collective-permute-done.4.refs_1_ = bf16[4,128,128]{2,1,0:T(8,128)(2,1)S(1)} collective-permute-done((bf16[4,128,128]{2,1,0:T(8,128)(2,1)S(1)}, bf16[4,128,128]{2,1,0:T(8,128)(2,1)S(1)}, u32[]{:S(2)}, u32[]{:S(2)}) %collective-permute-start.4) | collective-permute-done | bytes 131104 | tf_op jit(solution)/shard_map/ppermute | solution.py:527
  32.9 0.1 collective-permute-start.5
  33.0 2.1 %collective-permute-start.6 = (bf16[2,128,128]{2,1,0:T(8,128)(2,1)S(1)}, bf16[2,128,128]{2,1,0:T(8,128)(2,1)S(1)}, u32[]{:S(2)}, u32[]{:S(2)}) collective-permute-start(bf16[2,128,128]{2,1,0:T(8,128)(2,1)S(1)} %pad_maximum_fusion.4), channel_id=1, source_target_pairs={{0,16},{4,20},{8,24},{12,28},{16,0},{20,4},{24,8},{28,12},{32,48},... | collective-permute-start | bytes 196616 | tf_op jit(solution)/shard_map/ppermute | solution.py:527
  35.1 2.8 %collective-permute-start.7 = (bf16[2,128,128]{2,1,0:T(8,128)(2,1)S(1)}, bf16[2,128,128]{2,1,0:T(8,128)(2,1)S(1)}, u32[]{:S(2)}, u32[]{:S(2)}) collective-permute-start(bf16[2,128,128]{2,1,0:T(8,128)(2,1)S(1)} %pad_maximum_fusion.5), channel_id=1, source_target_pairs={{0,24},{4,28},{8,16},{12,20},{16,8},{20,12},{24,0},{28,4},{32,56},... | collective-permute-start | bytes 196616 | tf_op jit(solution)/shard_map/ppermute | solution.py:527
  37.9 0.0 collective-permute-done.8.one_ref
  37.9 0.0 collective-permute-done.9.two_ref
  37.9 0.3 combine.1
  38.2 1.9 %collective-permute-start.10 = (bf16[128,256]{1,0:T(8,128)(2,1)S(1)}, bf16[128,256]{1,0:T(8,128)(2,1)S(1)}, u32[]{:S(2)}, u32[]{:S(2)}) collective-permute-start(bf16[128,256]{1,0:T(8,128)(2,1)S(1)} %get-tuple-element.39), channel_id=1, source_target_pairs={{0,96},{4,100},{8,104},{12,108},{16,112},{20,116},{24,120},{28,124... | collective-permute-start | bytes 196616 | tf_op jit(solution)/shard_map/ppermute | solution.py:541
  40.1 0.7 collective-permute-start.11
  40.8 0.0 collective-permute-done.5.refs_2_
  40.8 0.0 collective-permute-done.6.refs_3_
  40.8 0.0 collective-permute-done.7.refs_4_
  40.8 0.0 copy-done.3
  40.8 1.9 %query.1.no_ref = f32[1024,256]{1,0:T(8,128)S(1)} custom-call(s32[3]{0:T(128)S(1)} %copy-done.3, bf16[4,128,128]{2,1,0:T(8,128)(2,1)S(1)} %copy-done, bf16[4,128,128]{2,1,0:T(8,128)(2,1)S(1)} %collective-permute-done.4.refs_1_, bf16[2,128,128]{2,1,0:T(8,128)(2,1)S(1)} %collective-permute-done.5.refs_2_, ...), custom_call_target="tpu_custom_call" | custom-call | flops 1000000000 | bytes 4000000 | tf_op jit(solution)/shard_map/query/pallas_call | solution.py:312
  42.8 5.3 %collective-permute-done.10.three_ref = bf16[128,256]{1,0:T(8,128)(2,1)S(1)} collective-permute-done((bf16[128,256]{1,0:T(8,128)(2,1)S(1)}, bf16[128,256]{1,0:T(8,128)(2,1)S(1)}, u32[]{:S(2)}, u32[]{:S(2)}) %collective-permute-start.10) | collective-permute-done | bytes 65568 | tf_op jit(solution)/shard_map/ppermute | solution.py:541
  48.1 0.0 collective-permute-done.11.six_ref
  48.1 0.0 copy-done.4
  48.1 0.7 norm.1.normed_ref
  48.8 0.0 slice-start.1
  48.8 4.2 %collective-permute-start.12 = (bf16[1024,128]{1,0:T(8,128)(2,1)S(1)}, bf16[1024,128]{1,0:T(8,128)(2,1)S(1)}, u32[]{:S(2)}, u32[]{:S(2)}) collective-permute-start(bf16[1024,128]{1,0:T(8,128)(2,1)S(1)} %norm.1.normed_ref), channel_id=1, source_target_pairs={{0,32},{4,36},{8,40},{12,44},{16,48},{20,52},{24,56},{28,60},{32,6... | collective-permute-start | bytes 786440 | tf_op jit(solution)/shard_map/ppermute | solution.py:541
  53.1 0.0 copy-done.5
  53.1 1.9 %own.1 = (f32[1024,128]{1,0:T(8,128)S(1)}, f32[2,1024,128]{2,1,0:T(8,128)S(1)}, bf16[1024,128]{1,0:T(8,128)(2,1)S(1)}) custom-call(s32[3]{0:T(128)S(1)} %copy-done.3, bf16[1024,128]{1,0:T(8,128)(2,1)S(1)} %norm.1.normed_ref, bf16[8,128,384]{2,1,0:T(8,128)(2,1)S(1)} %copy-done.5), custom_call_target="tpu_custom_call" | custom-call | flops 1000000000 | bytes 3000000 | tf_op jit(solution)/shard_map/own/pallas_call | solution.py:401
  54.9 3.7 %collective-permute-done.12.halo_ref = bf16[1024,128]{1,0:T(8,128)(2,1)S(1)} collective-permute-done((bf16[1024,128]{1,0:T(8,128)(2,1)S(1)}, bf16[1024,128]{1,0:T(8,128)(2,1)S(1)}, u32[]{:S(2)}, u32[]{:S(2)}) %collective-permute-start.12) | collective-permute-done | bytes 262176 | tf_op jit(solution)/shard_map/ppermute | solution.py:541
  58.6 4.2 %halo.1 = (bf16[4,128,128]{2,1,0:T(8,128)(2,1)S(1)}, bf16[4,128,128]{2,1,0:T(8,128)(2,1)S(1)}) custom-call(s32[3]{0:T(128)S(1)} %copy-done.3, bf16[1024,128]{1,0:T(8,128)(2,1)S(1)} %collective-permute-done.12.halo_ref, bf16[8,128,384]{2,1,0:T(8,128)(2,1)S(1)} %copy-done.5, f32[1024,128]{1,0:T(8,128)S(1)} %get-tuple-element.40.acc_ref, ...), custom_call_target="tpu_custom_call" | custom-call | flops 1000000000 | bytes 3000000 | tf_op jit(solution)/shard_map/halo/pallas_call | solution.py:464
  62.9 0.1 collective-permute-start.13
  63.0 1.3 %collective-permute-done.13.refs_1_ = bf16[4,128,128]{2,1,0:T(8,128)(2,1)S(1)} collective-permute-done((bf16[4,128,128]{2,1,0:T(8,128)(2,1)S(1)}, bf16[4,128,128]{2,1,0:T(8,128)(2,1)S(1)}, u32[]{:S(2)}, u32[]{:S(2)}) %collective-permute-start.13) | collective-permute-done | bytes 131104 | tf_op jit(solution)/shard_map/ppermute | solution.py:527
  64.3 0.1 collective-permute-start.14
  64.4 2.1 %collective-permute-start.15 = (bf16[2,128,128]{2,1,0:T(8,128)(2,1)S(1)}, bf16[2,128,128]{2,1,0:T(8,128)(2,1)S(1)}, u32[]{:S(2)}, u32[]{:S(2)}) collective-permute-start(bf16[2,128,128]{2,1,0:T(8,128)(2,1)S(1)} %pad_maximum_fusion.7), channel_id=1, source_target_pairs={{0,16},{4,20},{8,24},{12,28},{16,0},{20,4},{24,8},{28,12},{32,48},... | collective-permute-start | bytes 196616 | tf_op jit(solution)/shard_map/ppermute | solution.py:527
  66.5 2.8 %collective-permute-start.16 = (bf16[2,128,128]{2,1,0:T(8,128)(2,1)S(1)}, bf16[2,128,128]{2,1,0:T(8,128)(2,1)S(1)}, u32[]{:S(2)}, u32[]{:S(2)}) collective-permute-start(bf16[2,128,128]{2,1,0:T(8,128)(2,1)S(1)} %pad_maximum_fusion.8), channel_id=1, source_target_pairs={{0,24},{4,28},{8,16},{12,20},{16,8},{20,12},{24,0},{28,4},{32,56},... | collective-permute-start | bytes 196616 | tf_op jit(solution)/shard_map/ppermute | solution.py:527
  69.3 0.0 collective-permute-done.14.refs_2_
  69.3 1.0 %collective-permute-done.15.refs_3_ = bf16[2,128,128]{2,1,0:T(8,128)(2,1)S(1)} collective-permute-done((bf16[2,128,128]{2,1,0:T(8,128)(2,1)S(1)}, bf16[2,128,128]{2,1,0:T(8,128)(2,1)S(1)}, u32[]{:S(2)}, u32[]{:S(2)}) %collective-permute-start.15) | collective-permute-done | bytes 65568 | tf_op jit(solution)/shard_map/ppermute | solution.py:527
  70.3 1.7 %collective-permute-done.16.refs_4_ = bf16[2,128,128]{2,1,0:T(8,128)(2,1)S(1)} collective-permute-done((bf16[2,128,128]{2,1,0:T(8,128)(2,1)S(1)}, bf16[2,128,128]{2,1,0:T(8,128)(2,1)S(1)}, u32[]{:S(2)}, u32[]{:S(2)}) %collective-permute-start.16) | collective-permute-done | bytes 65568 | tf_op jit(solution)/shard_map/ppermute | solution.py:527
  72.1 0.0 slice-done
  72.1 0.0 slice-done.1
  72.1 2.4 %project.1 = (f32[32,4096]{1,0:T(8,128)S(1)}, bf16[32,4096]{1,0:T(8,128)(2,1)S(1)}, bf16[32,4096]{1,0:T(8,128)(2,1)S(1)}, bf16[32,4096]{1,0:T(8,128)(2,1)S(1)}) custom-call(s32[3]{0:T(128)S(1)} %copy-done.3, bf16[4,128,128]{2,1,0:T(8,128)(2,1)S(1)} %get-tuple-element.43.refs_0_, bf16[4,128,128]{2,1,0:T(8,128)(2,1)S(1)} %collective-permute-done.13.refs_1_, ...), custom_call_target="tpu_custom_call" | custom-call | flops 1000000000 | bytes 9000000 | tf_op jit(solution)/shard_map/project/pallas_call | solution.py:513
  74.5 3.3 %collective-permute-start.19 = (bf16[32,4096]{1,0:T(8,128)(2,1)S(1)}, bf16[32,4096]{1,0:T(8,128)(2,1)S(1)}, u32[]{:S(2)}, u32[]{:S(2)}) collective-permute-start(bf16[32,4096]{1,0:T(8,128)(2,1)S(1)} %get-tuple-element.48), channel_id=1, source_target_pairs={{0,2},{1,3},{2,0},{3,1},{4,6},{5,7},{6,4},{7,5},{8,10},{9,11},{10,... | collective-permute-start | bytes 786440 | tf_op jit(solution)/shard_map/ppermute | solution.py:566
  77.8 1.1 %collective-permute-start.18 = (bf16[32,4096]{1,0:T(8,128)(2,1)S(1)}, bf16[32,4096]{1,0:T(8,128)(2,1)S(1)}, u32[]{:S(2)}, u32[]{:S(2)}) collective-permute-start(bf16[32,4096]{1,0:T(8,128)(2,1)S(1)} %get-tuple-element.47), channel_id=1, source_target_pairs={{0,3},{1,2},{2,1},{3,0},{4,7},{5,6},{6,5},{7,4},{8,11},{9,10},{10,... | collective-permute-start | bytes 786440 | tf_op jit(solution)/shard_map/ppermute | solution.py:566
  78.9 0.0 collective-permute-start.17
  78.9 6.0 %collective-permute-done.19 = bf16[32,4096]{1,0:T(8,128)(2,1)S(1)} collective-permute-done((bf16[32,4096]{1,0:T(8,128)(2,1)S(1)}, bf16[32,4096]{1,0:T(8,128)(2,1)S(1)}, u32[]{:S(2)}, u32[]{:S(2)}) %collective-permute-start.19) | collective-permute-done | bytes 262176 | tf_op jit(solution)/shard_map/ppermute | solution.py:566
  84.8 3.9 %collective-permute-done.18 = bf16[32,4096]{1,0:T(8,128)(2,1)S(1)} collective-permute-done((bf16[32,4096]{1,0:T(8,128)(2,1)S(1)}, bf16[32,4096]{1,0:T(8,128)(2,1)S(1)}, u32[]{:S(2)}, u32[]{:S(2)}) %collective-permute-start.18) | collective-permute-done | bytes 262176 | tf_op jit(solution)/shard_map/ppermute | solution.py:566
  88.7 0.4 collective-permute-done.17
  89.1 0.8 add_convert_fusion
  (20 shorter events, 0.2 us)
Async XLA Ops:
  0.0 48.1 %copy-start.4 = (f32[128]{0:T(128)S(1)}, f32[128]{0:T(128)}, u32[]{:S(2)}) copy-start(f32[128]{0:T(128)} %param.13) | copy-start | bytes 1540
  0.7 40.2 %copy-start.3 = (s32[3]{0:T(128)S(1)}, s32[3]{0:T(128)}, u32[]{:S(2)}) copy-start(s32[3]{0:T(128)} %pad_add_fusion.me_ref) | copy-start | bytes 40
  0.7 52.4 %copy-start.5 = (bf16[8,128,384]{2,1,0:T(8,128)(2,1)S(1)}, bf16[8,128,384]{2,1,0:T(8,128)(2,1)}, u32[]{:S(2)}) copy-start(bf16[8,128,384]{2,1,0:T(8,128)(2,1)} %weight_ref.3) | copy-start | bytes 2359300
  3.7 27.7 %copy-start.6 = (bf16[4,128,128]{2,1,0:T(8,128)(2,1)S(1)}, bf16[4,128,128]{2,1,0:T(8,128)(2,1)}, u32[]{:S(2)}) copy-start(bf16[4,128,128]{2,1,0:T(8,128)(2,1)} %get-tuple-element.33) | copy-start | bytes 393220
  3.7 27.8 %copy-start = (bf16[4,128,128]{2,1,0:T(8,128)(2,1)S(1)}, bf16[4,128,128]{2,1,0:T(8,128)(2,1)}, u32[]{:S(2)}) copy-start(bf16[4,128,128]{2,1,0:T(8,128)(2,1)} %get-tuple-element.32.refs_0_) | copy-start | bytes 393220
  3.7 1.9 %collective-permute-start = (bf16[4,272,128]{2,1,0:T(8,128)(2,1)}, bf16[4,272,128]{2,1,0:T(8,128)(2,1)S(1)}, u32[]{:S(2)}, u32[]{:S(2)}) collective-permute-start(bf16[4,272,128]{2,1,0:T(8,128)(2,1)} %get-tuple-element.30), channel_id=1, source_target_pairs={{0,4},{4,0},{8,12},{12,8},{16,20},{20,16},{24,28},{28,24},{32,36},... | collective-permute-start | bytes 835592 | tf_op jit(solution)/shard_map/ppermute | solution.py:527
  5.6 6.5 %collective-permute-start.1 = (bf16[2,272,128]{2,1,0:T(8,128)(2,1)S(1)}, bf16[2,272,128]{2,1,0:T(8,128)(2,1)S(1)}, u32[]{:S(2)}, u32[]{:S(2)}) collective-permute-start(bf16[2,272,128]{2,1,0:T(8,128)(2,1)S(1)} %pad_maximum_fusion), channel_id=1, source_target_pairs={{0,8},{4,12},{8,0},{12,4},{16,24},{20,28},{24,16},{28,20},{32,40},... | collective-permute-start | bytes 417800 | tf_op jit(solution)/shard_map/ppermute | solution.py:527
  7.2 9.5 %collective-permute-start.2 = (bf16[2,272,128]{2,1,0:T(8,128)(2,1)S(1)}, bf16[2,272,128]{2,1,0:T(8,128)(2,1)S(1)}, u32[]{:S(2)}, u32[]{:S(2)}) collective-permute-start(bf16[2,272,128]{2,1,0:T(8,128)(2,1)S(1)} %pad_maximum_fusion.1), channel_id=1, source_target_pairs={{0,16},{4,20},{8,24},{12,28},{16,0},{20,4},{24,8},{28,12},{32,48},... | collective-permute-start | bytes 417800 | tf_op jit(solution)/shard_map/ppermute | solution.py:527
  10.0 9.1 %collective-permute-start.3 = (bf16[2,272,128]{2,1,0:T(8,128)(2,1)S(1)}, bf16[2,272,128]{2,1,0:T(8,128)(2,1)S(1)}, u32[]{:S(2)}, u32[]{:S(2)}) collective-permute-start(bf16[2,272,128]{2,1,0:T(8,128)(2,1)S(1)} %pad_maximum_fusion.2), channel_id=1, source_target_pairs={{0,24},{4,28},{8,16},{12,20},{16,8},{20,12},{24,0},{28,4},{32,56},... | collective-permute-start | bytes 417800 | tf_op jit(solution)/shard_map/ppermute | solution.py:527
  19.1 1.0 %copy-start.1 = (bf16[4,272,128]{2,1,0:T(8,128)(2,1)S(1)}, bf16[4,272,128]{2,1,0:T(8,128)(2,1)}, u32[]{:S(2)}) copy-start(bf16[4,272,128]{2,1,0:T(8,128)(2,1)} %get-tuple-element.29.refs_0_) | copy-start | bytes 835588
  20.1 0.7 copy-start.2
  24.8 47.3 %slice-start = ((s8[8388608]{0:T(1024)(128)(4,1)}), s8[4194304]{0:T(1024)(128)(4,1)S(1)}, s32[]{:S(2)}) async-start(s8[8388608]{0:T(1024)(128)(4,1)} %bitcast.4), calls=%async_computation | async-start | bytes 8388608
  24.8 13.0 %collective-permute-start.8 = (bf16[128,256]{1,0:T(8,128)(2,1)S(1)}, bf16[128,256]{1,0:T(8,128)(2,1)S(1)}, u32[]{:S(2)}, u32[]{:S(2)}) collective-permute-start(bf16[128,256]{1,0:T(8,128)(2,1)S(1)} %get-tuple-element.31.own_ref), channel_id=1, source_target_pairs={{0,32},{4,36},{8,40},{12,44},{16,48},{20,52},{24,56},{28,60},{32,6... | collective-permute-start | bytes 196616 | tf_op jit(solution)/shard_map/ppermute | solution.py:541
  28.0 9.8 %collective-permute-start.9 = (bf16[128,256]{1,0:T(8,128)(2,1)S(1)}, bf16[128,256]{1,0:T(8,128)(2,1)S(1)}, u32[]{:S(2)}, u32[]{:S(2)}) collective-permute-start(bf16[128,256]{1,0:T(8,128)(2,1)S(1)} %get-tuple-element.31.own_ref), channel_id=1, source_target_pairs={{0,64},{4,68},{8,72},{12,76},{16,80},{20,84},{24,88},{28,92},{32,9... | collective-permute-start | bytes 196616 | tf_op jit(solution)/shard_map/ppermute | solution.py:541
  31.4 1.4 %collective-permute-start.4 = (bf16[4,128,128]{2,1,0:T(8,128)(2,1)S(1)}, bf16[4,128,128]{2,1,0:T(8,128)(2,1)S(1)}, u32[]{:S(2)}, u32[]{:S(2)}) collective-permute-start(bf16[4,128,128]{2,1,0:T(8,128)(2,1)S(1)} %copy-done.6), channel_id=1, source_target_pairs={{0,4},{4,0},{8,12},{12,8},{16,20},{20,16},{24,28},{28,24},{32,36},... | collective-permute-start | bytes 393224 | tf_op jit(solution)/shard_map/ppermute | solution.py:527
  32.9 7.9 %collective-permute-start.5 = (bf16[2,128,128]{2,1,0:T(8,128)(2,1)S(1)}, bf16[2,128,128]{2,1,0:T(8,128)(2,1)S(1)}, u32[]{:S(2)}, u32[]{:S(2)}) collective-permute-start(bf16[2,128,128]{2,1,0:T(8,128)(2,1)S(1)} %pad_maximum_fusion.3), channel_id=1, source_target_pairs={{0,8},{4,12},{8,0},{12,4},{16,24},{20,28},{24,16},{28,20},{32,40},... | collective-permute-start | bytes 196616 | tf_op jit(solution)/shard_map/ppermute | solution.py:527
  33.0 7.8 %collective-permute-start.6 = (bf16[2,128,128]{2,1,0:T(8,128)(2,1)S(1)}, bf16[2,128,128]{2,1,0:T(8,128)(2,1)S(1)}, u32[]{:S(2)}, u32[]{:S(2)}) collective-permute-start(bf16[2,128,128]{2,1,0:T(8,128)(2,1)S(1)} %pad_maximum_fusion.4), channel_id=1, source_target_pairs={{0,16},{4,20},{8,24},{12,28},{16,0},{20,4},{24,8},{28,12},{32,48},... | collective-permute-start | bytes 196616 | tf_op jit(solution)/shard_map/ppermute | solution.py:527
  35.1 5.7 %collective-permute-start.7 = (bf16[2,128,128]{2,1,0:T(8,128)(2,1)S(1)}, bf16[2,128,128]{2,1,0:T(8,128)(2,1)S(1)}, u32[]{:S(2)}, u32[]{:S(2)}) collective-permute-start(bf16[2,128,128]{2,1,0:T(8,128)(2,1)S(1)} %pad_maximum_fusion.5), channel_id=1, source_target_pairs={{0,24},{4,28},{8,16},{12,20},{16,8},{20,12},{24,0},{28,4},{32,56},... | collective-permute-start | bytes 196616 | tf_op jit(solution)/shard_map/ppermute | solution.py:527
  38.2 9.9 %collective-permute-start.10 = (bf16[128,256]{1,0:T(8,128)(2,1)S(1)}, bf16[128,256]{1,0:T(8,128)(2,1)S(1)}, u32[]{:S(2)}, u32[]{:S(2)}) collective-permute-start(bf16[128,256]{1,0:T(8,128)(2,1)S(1)} %get-tuple-element.39), channel_id=1, source_target_pairs={{0,96},{4,100},{8,104},{12,108},{16,112},{20,116},{24,120},{28,124... | collective-permute-start | bytes 196616 | tf_op jit(solution)/shard_map/ppermute | solution.py:541
  40.1 8.0 %collective-permute-start.11 = (bf16[128,256]{1,0:T(8,128)(2,1)S(1)}, bf16[128,256]{1,0:T(8,128)(2,1)S(1)}, u32[]{:S(2)}, u32[]{:S(2)}) collective-permute-start(bf16[128,256]{1,0:T(8,128)(2,1)S(1)} %get-tuple-element.39), channel_id=1, source_target_pairs={{0,192},{4,196},{8,200},{12,204},{16,208},{20,212},{24,216},{28,22... | collective-permute-start | bytes 196616 | tf_op jit(solution)/shard_map/ppermute | solution.py:541
  48.8 23.3 %slice-start.1 = ((s8[8388608]{0:T(1024)(128)(4,1)}), s8[4194304]{0:T(1024)(128)(4,1)S(1)}, s32[]{:S(2)}) async-start(s8[8388608]{0:T(1024)(128)(4,1)} %bitcast.4), calls=%async_computation.1 | async-start | bytes 8388608
  48.8 9.8 %collective-permute-start.12 = (bf16[1024,128]{1,0:T(8,128)(2,1)S(1)}, bf16[1024,128]{1,0:T(8,128)(2,1)S(1)}, u32[]{:S(2)}, u32[]{:S(2)}) collective-permute-start(bf16[1024,128]{1,0:T(8,128)(2,1)S(1)} %norm.1.normed_ref), channel_id=1, source_target_pairs={{0,32},{4,36},{8,40},{12,44},{16,48},{20,52},{24,56},{28,60},{32,6... | collective-permute-start | bytes 786440 | tf_op jit(solution)/shard_map/ppermute | solution.py:541
  62.9 1.4 %collective-permute-start.13 = (bf16[4,128,128]{2,1,0:T(8,128)(2,1)S(1)}, bf16[4,128,128]{2,1,0:T(8,128)(2,1)S(1)}, u32[]{:S(2)}, u32[]{:S(2)}) collective-permute-start(bf16[4,128,128]{2,1,0:T(8,128)(2,1)S(1)} %get-tuple-element.44), channel_id=1, source_target_pairs={{0,4},{4,0},{8,12},{12,8},{16,20},{20,16},{24,28},{28,24},{32,36},... | collective-permute-start | bytes 393224 | tf_op jit(solution)/shard_map/ppermute | solution.py:527
  64.3 5.0 %collective-permute-start.14 = (bf16[2,128,128]{2,1,0:T(8,128)(2,1)S(1)}, bf16[2,128,128]{2,1,0:T(8,128)(2,1)S(1)}, u32[]{:S(2)}, u32[]{:S(2)}) collective-permute-start(bf16[2,128,128]{2,1,0:T(8,128)(2,1)S(1)} %pad_maximum_fusion.6), channel_id=1, source_target_pairs={{0,8},{4,12},{8,0},{12,4},{16,24},{20,28},{24,16},{28,20},{32,40},... | collective-permute-start | bytes 196616 | tf_op jit(solution)/shard_map/ppermute | solution.py:527
  64.4 5.9 %collective-permute-start.15 = (bf16[2,128,128]{2,1,0:T(8,128)(2,1)S(1)}, bf16[2,128,128]{2,1,0:T(8,128)(2,1)S(1)}, u32[]{:S(2)}, u32[]{:S(2)}) collective-permute-start(bf16[2,128,128]{2,1,0:T(8,128)(2,1)S(1)} %pad_maximum_fusion.7), channel_id=1, source_target_pairs={{0,16},{4,20},{8,24},{12,28},{16,0},{20,4},{24,8},{28,12},{32,48},... | collective-permute-start | bytes 196616 | tf_op jit(solution)/shard_map/ppermute | solution.py:527
  66.5 5.6 %collective-permute-start.16 = (bf16[2,128,128]{2,1,0:T(8,128)(2,1)S(1)}, bf16[2,128,128]{2,1,0:T(8,128)(2,1)S(1)}, u32[]{:S(2)}, u32[]{:S(2)}) collective-permute-start(bf16[2,128,128]{2,1,0:T(8,128)(2,1)S(1)} %pad_maximum_fusion.8), channel_id=1, source_target_pairs={{0,24},{4,28},{8,16},{12,20},{16,8},{20,12},{24,0},{28,4},{32,56},... | collective-permute-start | bytes 196616 | tf_op jit(solution)/shard_map/ppermute | solution.py:527
  74.5 10.3 %collective-permute-start.19 = (bf16[32,4096]{1,0:T(8,128)(2,1)S(1)}, bf16[32,4096]{1,0:T(8,128)(2,1)S(1)}, u32[]{:S(2)}, u32[]{:S(2)}) collective-permute-start(bf16[32,4096]{1,0:T(8,128)(2,1)S(1)} %get-tuple-element.48), channel_id=1, source_target_pairs={{0,2},{1,3},{2,0},{3,1},{4,6},{5,7},{6,4},{7,5},{8,10},{9,11},{10,... | collective-permute-start | bytes 786440 | tf_op jit(solution)/shard_map/ppermute | solution.py:566
  77.8 10.9 %collective-permute-start.18 = (bf16[32,4096]{1,0:T(8,128)(2,1)S(1)}, bf16[32,4096]{1,0:T(8,128)(2,1)S(1)}, u32[]{:S(2)}, u32[]{:S(2)}) collective-permute-start(bf16[32,4096]{1,0:T(8,128)(2,1)S(1)} %get-tuple-element.47), channel_id=1, source_target_pairs={{0,3},{1,2},{2,1},{3,0},{4,7},{5,6},{6,5},{7,4},{8,11},{9,10},{10,... | collective-permute-start | bytes 786440 | tf_op jit(solution)/shard_map/ppermute | solution.py:566
  78.9 10.2 %collective-permute-start.17 = (bf16[32,4096]{1,0:T(8,128)(2,1)S(1)}, bf16[32,4096]{1,0:T(8,128)(2,1)S(1)}, u32[]{:S(2)}, u32[]{:S(2)}) collective-permute-start(bf16[32,4096]{1,0:T(8,128)(2,1)S(1)} %get-tuple-element.46), channel_id=1, source_target_pairs={{0,1},{1,0},{2,3},{3,2},{4,5},{5,4},{6,7},{7,6},{8,9},{9,8},{10,11... | collective-permute-start | bytes 786440 | tf_op jit(solution)/shard_map/ppermute | solution.py:566

commit v4 on v3

--- a/solution.py
+++ b/solution.py
@@ -29,10 +29,6 @@
     return pl.BlockSpec(memory_space=pltpu.VMEM)
 
 
-def smem():
-    return pl.BlockSpec(memory_space=pltpu.SMEM)
-
-
 def split(a):
     hi = a.astype(BF16)
     lo = (a - hi.astype(F32)).astype(BF16)
@@ -74,9 +70,9 @@
     return row, col
 
 
-def pack_kernel(me_ref, q_ref, k_ref, v_ref, decay_ref, beta_ref, *rest):
+def pack_kernel(q_ref, k_ref, v_ref, decay_ref, beta_ref, *rest):
     keep, send, keep_q, send_q, gate, raw, sems = rest
-    me = me_ref[0]
+    me = lax.axis_index("seq") % PLANE
     copies = [
         pltpu.make_async_copy(decay_ref, raw.at[0], sems.at[24]),
         pltpu.make_async_copy(beta_ref, raw.at[1], sems.at[25]),
@@ -110,23 +106,23 @@
         copy.wait()
 
 
-def pack(me, q, k, v, decay, beta):
+def pack(q, k, v, decay, beta):
     any_space = pl.BlockSpec(memory_space=pltpu.HBM)
     wide = jax.ShapeDtypeStruct((4, BLK, C), BF16)
     thin = jax.ShapeDtypeStruct((4, C, C), BF16)
     return pl.pallas_call(
         pack_kernel,
         out_shape=[wide, wide, thin, thin],
-        in_specs=[smem()] + [any_space] * 5,
+        in_specs=[any_space] * 5,
         out_specs=[vmem()] * 4,
         scratch_shapes=[
             pltpu.VMEM((6, PLANE, C), F32),
             pltpu.VMEM((2, PLANE, C), F32),
             pltpu.SemaphoreType.DMA((26,)),
         ],
-        compiler_params=params(60 * 1024 * 1024),
+        compiler_params=params(),
         name="pack",
-    )(me, q, k, v, decay, beta)
+    )(*[pltpu.with_memory_space_constraint(x, pltpu.HBM) for x in (q, k, v, decay, beta)])
 
 
 def gather_slots(refs, out_ref):
@@ -185,10 +181,10 @@
     return jnp.concatenate([both[:, :C], both[:, C:] + later[:, C:]], axis=1)
 
 
-def prep_kernel(me_ref, *refs):
+def prep_kernel(*refs):
     kv_ref, mix_ref, wu_ref, ab_ref, level_ref = refs[5:10]
     maps = refs[10]
-    me = me_ref[0]
+    me = lax.axis_index("seq") % PLANE
     row, col = iotas()
     gather_slots(refs[:5], kv_ref)
     every = range(PLANE)
@@ -249,7 +245,7 @@
         level_ref[i] = part
 
 
-def prep(me, slots):
+def prep(slots):
     return pl.pallas_call(
         prep_kernel,
         out_shape=[
@@ -259,7 +255,7 @@
             jax.ShapeDtypeStruct((C, 2 * C), BF16),
             jax.ShapeDtypeStruct((7, C, 2 * C), F32),
         ],
-        in_specs=[smem()] + [vmem()] * 5,
+        in_specs=[vmem()] * 5,
         out_specs=[vmem()] * 5,
         scratch_shapes=[
             pltpu.VMEM((PLANE, C, 2 * C), F32),
@@ -267,12 +263,12 @@
         compiler_params=params(),
         cost_estimate=cost(2e9, 4e6),
         name="prep",
-    )(me, *slots)
-
-
-def query_kernel(me_ref, *refs):
+    )(*slots)
+
+
+def query_kernel(*refs):
     kv_ref, mix_ref, wu_ref, level_ref, no_ref, queries_ref, before = refs[5:]
-    me = me_ref[0]
+    me = lax.axis_index("seq") % PLANE
     row, col = iotas()
     gather_slots(refs[:5], queries_ref)
     before[0] = jnp.concatenate([jnp.where(row == col, 1.0, 0.0), jnp.zeros((C, C), F32)], axis=1)
@@ -308,11 +304,11 @@
         )
 
 
-def query(me, slots, kv, mix, wu, level):
+def query(slots, kv, mix, wu, level):
     return pl.pallas_call(
         query_kernel,
         out_shape=jax.ShapeDtypeStruct((PLANE * C, 2 * C), F32),
-        in_specs=[smem()] + [vmem()] * 9,
+        in_specs=[vmem()] * 9,
         out_specs=vmem(),
         scratch_shapes=[
             pltpu.VMEM((PLANE, C, C), BF16),
@@ -321,7 +317,7 @@
         compiler_params=params(),
         cost_estimate=cost(1e9, 4e6),
         name="query",
-    )(me, *slots, kv, mix, wu, level)
+    )(*slots, kv, mix, wu, level)
 
 
 def times(a, x):
@@ -377,26 +373,55 @@
 SCALE = C**-0.5 * 1.4426950408889634
 
 
-def own_kernel(me_ref, normed_ref, weight_ref, acc_ref, stat_ref, q2_ref):
-    proj = dot(normed_ref[...], weight_ref[0]).astype(BF16)
-    q2_ref[...] = proj[:, :C]
+def squares():
     row = lax.broadcasted_iota(jnp.int32, (QB, QB), 0)
     col = lax.broadcasted_iota(jnp.int32, (QB, QB), 1)
+    return row, col
+
+
+def row_max(parts):
+    top = jnp.max(parts[0], axis=1, keepdims=True)
+    for part in parts[1:]:
+        top = jnp.maximum(top, jnp.max(part, axis=1, keepdims=True))
+    return top
+
+
+def row_sum(parts):
+    total = jnp.sum(parts[0], axis=1, keepdims=True)
+    for part in parts[1:]:
+        total = total + jnp.sum(part, axis=1, keepdims=True)
+    return total
+
+
+def weighted(parts, values):
+    out = dot(parts[0].astype(BF16), values[0])
+    for part, value in zip(parts[1:], values[1:]):
+        out = out + dot(part.astype(BF16), value)
+    return out
+
+
+def own_kernel(normed_ref, weight_ref, acc_ref, stat_ref, q2_ref):
+    me = lax.axis_index("seq") % PLANE
+    proj = dot(normed_ref[...], weight_ref[me]).astype(BF16)
+    q2_ref[...] = proj[:, :C]
+    row, col = squares()
     starts = range(0, PLANE * C, QB)
-    scores = [dot_nt(proj[at : at + QB, :C], proj[: at + QB, C : 2 * C]) for at in starts]
+    spans = [[(at, at + QB)] + ([(0, at)] if at else []) for at in starts]
+    scores = [
+        [dot_nt(proj[at : at + QB, :C], proj[a:b, C : 2 * C]) for a, b in span]
+        for at, span in zip(starts, spans)
+    ]
+    scores = [[jnp.where(col <= row, parts[0], NEG)] + parts[1:] for parts in scores]
+    tops = [row_max(parts) for parts in scores]
+    raised = [[jnp.exp2((s - top) * SCALE) for s in parts] for parts, top in zip(scores, tops)]
     for i, at in enumerate(starts):
-        last = jnp.where(col <= row, scores[i][:, at:], NEG)
-        scores[i] = last if i == 0 else jnp.concatenate([scores[i][:, :at], last], axis=1)
-    tops = [jnp.max(s, axis=1, keepdims=True) for s in scores]
-    raised = [jnp.exp2((s - top) * SCALE) for s, top in zip(scores, tops)]
-    totals = [jnp.sum(p, axis=1, keepdims=True) for p in raised]
-    for i, at in enumerate(starts):
-        acc_ref[at : at + QB, :] = dot(raised[i].astype(BF16), proj[: at + QB, 2 * C :])
-        stat_ref[0, at : at + QB, :] = jnp.broadcast_to(tops[i], (QB, C))
-        stat_ref[1, at : at + QB, :] = jnp.broadcast_to(totals[i], (QB, C))
-
-
-def own(me, normed, weight):
+        rows = slice(at, at + QB)
+        acc_ref[rows, :] = weighted(raised[i], [proj[a:b, 2 * C :] for a, b in spans[i]])
+        stat_ref[0, rows, :] = jnp.broadcast_to(tops[i], (QB, C))
+        stat_ref[1, rows, :] = jnp.broadcast_to(row_sum(raised[i]), (QB, C))
+
+
+def own(normed, weight):
     n = PLANE * C
     return pl.pallas_call(
         own_kernel,
@@ -405,90 +430,67 @@
             jax.ShapeDtypeStruct((2, n, C), F32),
             jax.ShapeDtypeStruct((n, C), BF16),
         ],
-        grid_spec=pltpu.PrefetchScalarGridSpec(
-            num_scalar_prefetch=1,
-            grid=(1,),
-            in_specs=[
-                pl.BlockSpec((n, C), lambda i, me: (0, 0)),
-                pl.BlockSpec((1, C, 3 * C), lambda i, me: (me[0], 0, 0)),
-            ],
-            out_specs=[
-                pl.BlockSpec((n, C), lambda i, me: (0, 0)),
-                pl.BlockSpec((2, n, C), lambda i, me: (0, 0, 0)),
-                pl.BlockSpec((n, C), lambda i, me: (0, 0)),
-            ],
-        ),
+        in_specs=[vmem()] * 2,
+        out_specs=[vmem()] * 3,
         compiler_params=params(),
         cost_estimate=cost(1e9, 3e6, 6e5),
         name="own",
-    )(me, normed, weight)
-
-
-def halo_kernel(me_ref, halo_ref, weight_ref, acc_ref, stat_ref, q2_ref, *refs):
-    keep, send, attended = refs
-    me, plane = me_ref[0], me_ref[1]
-    proj = dot(halo_ref[...], weight_ref[0, :, C:]).astype(BF16)
+    )(normed, weight)
+
+
+def halo_kernel(halo_ref, weight_ref, acc_ref, stat_ref, q2_ref, keep, send, attended):
+    place = lax.axis_index("seq")
+    me, plane = place % PLANE, place // PLANE
+    proj = dot(halo_ref[...], weight_ref[me, :, C:]).astype(BF16)
     n = PLANE * C
-    row = lax.broadcasted_iota(jnp.int32, (QB, QB), 0)
-    col = lax.broadcasted_iota(jnp.int32, (QB, QB), 1)
+    row, col = squares()
     starts = range(0, n, QB)
+    spans = [[(at, at + QB)] + ([(at + QB, n)] if at + QB < n else []) for at in starts]
     floor = jnp.where(plane > 0, 0.0, NEG)
-    scores = [dot_nt(q2_ref[at : at + QB, :], proj[at:, :C]) for at in starts]
+    scores = [
+        [dot_nt(q2_ref[at : at + QB, :], proj[a:b, :C]) for a, b in span]
+        for at, span in zip(starts, spans)
+    ]
+    scores = [[jnp.where(col > row, parts[0], NEG)] + parts[1:] for parts in scores]
+    before = [stat_ref[0, at : at + QB, 0:1] for at in starts]
+    tops = [jnp.maximum(row_max(parts) + floor, old) for parts, old in zip(scores, before)]
+    raised = [
+        [jnp.exp2((s - (top - floor)) * SCALE) for s in parts] for parts, top in zip(scores, tops)
+    ]
+    fades = [jnp.exp2((old - top) * SCALE) for old, top in zip(before, tops)]
     for i, at in enumerate(starts):
-        first = jnp.where(col > row, scores[i][:, :QB], NEG)
-        scores[i] = (
-            first if at + QB == n else jnp.concatenate([first, scores[i][:, QB:]], axis=1)
+        rows = slice(at, at + QB)
+        total = row_sum(raised[i]) + fades[i] * stat_ref[1, rows, 0:1]
+        acc = acc_ref[rows, :] * fades[i] + weighted(
+            raised[i], [proj[a:b, C:] for a, b in spans[i]]
         )
-    before = [stat_ref[0, at : at + QB, 0:1] for at in starts]
-    tops = [
-        jnp.maximum(jnp.max(s, axis=1, keepdims=True) + floor, old)
-        for s, old in zip(scores, before)
-    ]
-    raised = [jnp.exp2((s - (top - floor)) * SCALE) for s, top in zip(scores, tops)]
-    fades = [jnp.exp2((old - top) * SCALE) for old, top in zip(before, tops)]
-    totals = [
-        jnp.sum(raised[i], axis=1, keepdims=True) + fades[i] * stat_ref[1, at : at + QB, 0:1]
-        for i, at in enumerate(starts)
-    ]
-    for i, at in enumerate(starts):
-        acc = acc_ref[at : at + QB, :] * fades[i] + dot(raised[i].astype(BF16), proj[at:, C:])
-        attended[at : at + QB, :] = (acc / totals[i]).astype(BF16)
+        attended[rows, :] = (acc / total).astype(BF16)
     for d in range(PLANE):
         chunk = jnp.bitwise_xor(me, d)
         out = send if d % 2 else keep
         out[d // 2] = attended[pl.ds(pl.multiple_of(chunk * C, C), C), :]
 
 
-def halo_part(me, halo, weight, acc, stat, q2):
+def halo_part(halo, weight, acc, stat, q2):
     n = PLANE * C
     return pl.pallas_call(
         halo_kernel,
         out_shape=[jax.ShapeDtypeStruct((4, C, C), BF16)] * 2,
-        grid_spec=pltpu.PrefetchScalarGridSpec(
-            num_scalar_prefetch=1,
-            grid=(1,),
-            in_specs=[
-                pl.BlockSpec((n, C), lambda i, me: (0, 0)),
-                pl.BlockSpec((1, C, 3 * C), lambda i, me: (me[0], 0, 0)),
-                pl.BlockSpec((n, C), lambda i, me: (0, 0)),
-                pl.BlockSpec((2, n, C), lambda i, me: (0, 0, 0)),
-                pl.BlockSpec((n, C), lambda i, me: (0, 0)),
-            ],
-            out_specs=[pl.BlockSpec((4, C, C), lambda i, me: (0, 0, 0))] * 2,
-            scratch_shapes=[pltpu.VMEM((n, C), BF16)],
-        ),
+        in_specs=[vmem()] * 5,
+        out_specs=[vmem()] * 2,
+        scratch_shapes=[pltpu.VMEM((n, C), BF16)],
         compiler_params=params(),
         cost_estimate=cost(1e9, 3e6, 6e5),
         name="halo",
-    )(me, halo, weight, acc, stat, q2)
+    )(halo, weight, acc, stat, q2)
 
 
 COLS = 1024
 
 
-def project_kernel(me_ref, *refs):
+def project_kernel(*refs):
     slots, weight_ref, outs, flat = refs[:5], refs[5], refs[6:10], refs[10]
-    me, mine = me_ref[0], me_ref[2]
+    me, mine = lax.axis_index("seq") % PLANE, lax.axis_index("heads")
     found = [slots[0].at[0], slots[1].at[0]]
     for dx in range(1, 4):
         found += [slots[dx + 1].at[0], slots[dx + 1].at[1]]
@@ -508,19 +510,19 @@
     lax.fori_loop(0, weight_ref.shape[1] // COLS, one, 0)
 
 
-def project(me, slots, weight):
+def project(slots, weight):
     depth, width = weight.shape
     return pl.pallas_call(
         project_kernel,
         out_shape=[jax.ShapeDtypeStruct((32, width), F32)]
         + [jax.ShapeDtypeStruct((32, width), BF16)] * 3,
-        in_specs=[smem()] + [vmem()] * 6,
+        in_specs=[vmem()] * 6,
         out_specs=[vmem()] * 4,
         scratch_shapes=[pltpu.VMEM((C, depth), BF16)],
         compiler_params=params(),
         cost_estimate=cost(1e9, 9e6),
         name="project",
-    )(me, *slots, weight)
+    )(*slots, weight)
 
 
 def swap(block, d):
@@ -542,25 +544,21 @@
 
 
 def local(q_delta, k_delta, v_delta, decay, beta, gain, attn_weight, out_weight):
-    place = lax.axis_index("seq")
-    mine = lax.axis_index("heads")
-    me = jnp.stack([place % PLANE, place // PLANE, mine]).astype(jnp.int32)
-    keep, send, keep_q, send_q = pack(me, q_delta, k_delta, v_delta, decay, beta)
+    keep, send, keep_q, send_q = pack(q_delta, k_delta, v_delta, decay, beta)
     slots = exchange(keep, send)
-    kv, mix, wu, ab, level = prep(me, slots)
+    slots_q = exchange(keep_q, send_q)
+    kv, mix, wu, ab, level = prep(slots)
     one = later_plane(ab, 1)
     two = later_plane(ab, 2)
-    keep_q, send_q, _ = lax.optimization_barrier((keep_q, send_q, ab))
-    slots_q = exchange(keep_q, send_q)
-    no = query(me, slots_q, kv, mix, wu, level)
+    no = query(slots_q, kv, mix, wu, level)
     before, upto = combine(ab, one, two)
     three = later_plane(upto, 3)
     six = later_plane(upto, 6)
     normed = norm(no, gain[None, :], before, three, six)
     halo = later_plane(normed, 1)
-    acc, stat, q2 = own(me, normed, attn_weight)
-    attended = exchange(*halo_part(me, halo, attn_weight, acc, stat, q2))
-    sums = project(me, attended, out_weight)
+    acc, stat, q2 = own(normed, attn_weight)
+    attended = exchange(*halo_part(halo, attn_weight, acc, stat, q2))
+    sums = project(attended, out_weight)
     moved = {}
     for d in (2, 1, 3):
         moved[d] = lax.ppermute(sums[d], "heads", [(s, s ^ d) for s in range(4)])

time: 91 us -> 84.8 us (0.932)
  Pallas kernels: 18.6 us -> 14.7 us
  local copies, waits for them, and re-layouts: 2.7 us -> 0.08 us
  waiting for transfers between devices: 33.9 us -> 35.7 us
    ppermute x5, waiting for transfers between devices: 8.98 us -> 14 us  [later_plane(): return lax.ppermute(block, 'seq', route)]
    ppermute x12, waiting for transfers between devices: 14.7 us -> 11 us  [swap(): lax.ppermute(block, 'seq', [(s, s ^ d) for s in range(PLANE * PLANES)])]
    unnamed x18 -> x8, local copies, waits for them, and re-layouts: 1.66 us -> 0.02 us
    pallas_call x1, Pallas kernels: 3.03 us -> 1.43 us  [pack(): pl.pallas_call(pack_kernel, out_shape=[wide, wide, thin, thin], in_specs=...]
    slice x6, local copies, waits for them, and re-layouts: 1.04 us -> 0.06 us  [exchange(): slots.append((dx, swap(jnp.stack([keep[dx], came[dx]]), 2 * dx)))]
  transfers between devices with their start and end apart: 20 -> 20, of which waited for: 13 -> 14; matrix products, arithmetic and copies ran while one was open for 1% -> 0% of each run, Pallas kernels for 5% -> 8%
where the time goes in v4:
time: 84.8 us; the launch traced here: 84.6 us
  waiting for transfers between devices  35.7 us (42%)
  starting transfers between devices  32.9 us (39%)
  Pallas kernels  14.7 us (17%)
  other arithmetic  0.91 us (1%)
    ppermute x12, starting transfers between devices, swap(): lax.ppermute(block, 'seq', [(s, s ^ d) for s in range(PLANE * PLANES)])  15.5 us
    ppermute x5, waiting for transfers between devices, later_plane(): return lax.ppermute(block, 'seq', route)  14 us
    ppermute x5, starting transfers between devices, later_plane(): return lax.ppermute(block, 'seq', route)  12.8 us
    ppermute x12, waiting for transfers between devices, swap(): lax.ppermute(block, 'seq', [(s, s ^ d) for s in range(PLANE * PLANES)])  11 us
    ppermute x3, waiting for transfers between devices, local(): moved[d] = lax.ppermute(sums[d], 'heads', [(s, s ^ d) for s in range(4)])  10.7 us
    ppermute x3, starting transfers between devices, local(): moved[d] = lax.ppermute(sums[d], 'heads', [(s, s ^ d) for s in range(4)])  4.57 us
    pallas_call x1, Pallas kernels, halo_part(): pl.pallas_call(halo_kernel, out_shape=[jax.ShapeDtypeStruct((4, C, C), BF...  4.27 us
    pallas_call x1, Pallas kernels, prep(): pl.pallas_call(prep_kernel, out_shape=[jax.ShapeDtypeStruct((PLANE, BLK,...  3.51 us
  transfers between devices with their start and end apart: 20, of which 14 were waited for; matrix products, arithmetic and copies ran while one was open for 0% of the time, Pallas kernels for 8%

profile of v4, /device:TPU:128, one launch (start us, length us, event | category | flops | bytes accessed | tf_op | source)
XLA Modules:
  0.0 84.6 jit_solution(15115792235008018146)
XLA Ops:
  0.0 0.0 copy-start
  0.0 0.0 copy-start.1
  0.0 1.4 %pack.1 = (bf16[4,272,128]{2,1,0:T(8,128)(2,1)S(1)}, bf16[4,272,128]{2,1,0:T(8,128)(2,1)S(1)}, bf16[4,128,128]{2,1,0:T(8,128)(2,1)S(1)}, bf16[4,128,128]{2,1,0:T(8,128)(2,1)S(1)}) custom-call(bf16[128,1024]{1,0:T(8,128)(2,1)} %q_ref.1, bf16[128,1024]{1,0:T(8,128)(2,1)} %k_ref.1, bf16[128,1024]{1,0:T(8,128)(2,1)} %v_ref.1, f32[8,128]{1,0:T(8,128)} %decay_ref.1, ...), custom_call_target="tpu_custom_call" | custom-call | tf_op jit(solution)/shard_map/pack/pallas_call | solution.py:113
  1.4 0.1 collective-permute-start
  1.5 0.5 collective-permute-start.4
  2.1 0.8 collective-permute-done.refs_1_
  2.9 0.4 collective-permute-done.4.refs_1_
  3.3 1.6 %collective-permute-start.5 = (bf16[2,272,128]{2,1,0:T(8,128)(2,1)S(1)}, bf16[2,272,128]{2,1,0:T(8,128)(2,1)S(1)}, u32[]{:S(2)}, u32[]{:S(2)}) collective-permute-start(bf16[2,272,128]{2,1,0:T(8,128)(2,1)S(1)} %pad_maximum_fusion), channel_id=1, source_target_pairs={{0,8},{4,12},{8,0},{12,4},{16,24},{20,28},{24,16},{28,20},{32,40},... | collective-permute-start | bytes 417800 | tf_op jit(solution)/shard_map/ppermute | solution.py:529
  4.9 2.8 %collective-permute-start.6 = (bf16[2,272,128]{2,1,0:T(8,128)(2,1)S(1)}, bf16[2,272,128]{2,1,0:T(8,128)(2,1)S(1)}, u32[]{:S(2)}, u32[]{:S(2)}) collective-permute-start(bf16[2,272,128]{2,1,0:T(8,128)(2,1)S(1)} %pad_maximum_fusion.1), channel_id=1, source_target_pairs={{0,16},{4,20},{8,24},{12,28},{16,0},{20,4},{24,8},{28,12},{32,48},... | collective-permute-start | bytes 417800 | tf_op jit(solution)/shard_map/ppermute | solution.py:529
  7.8 0.6 collective-permute-start.7
  8.3 0.4 collective-permute-start.1
  8.7 4.0 %collective-permute-start.2 = (bf16[2,128,128]{2,1,0:T(8,128)(2,1)S(1)}, bf16[2,128,128]{2,1,0:T(8,128)(2,1)S(1)}, u32[]{:S(2)}, u32[]{:S(2)}) collective-permute-start(bf16[2,128,128]{2,1,0:T(8,128)(2,1)S(1)} %pad_maximum_fusion.4), channel_id=1, source_target_pairs={{0,16},{4,20},{8,24},{12,28},{16,0},{20,4},{24,8},{28,12},{32,48},... | collective-permute-start | bytes 196616 | tf_op jit(solution)/shard_map/ppermute | solution.py:529
  12.7 0.0 collective-permute-done.5.refs_2_
  12.7 2.4 %collective-permute-done.6.refs_3_ = bf16[2,272,128]{2,1,0:T(8,128)(2,1)S(1)} collective-permute-done((bf16[2,272,128]{2,1,0:T(8,128)(2,1)S(1)}, bf16[2,272,128]{2,1,0:T(8,128)(2,1)S(1)}, u32[]{:S(2)}, u32[]{:S(2)}) %collective-permute-start.6) | collective-permute-done | bytes 139296 | tf_op jit(solution)/shard_map/ppermute | solution.py:529
  15.1 3.4 %collective-permute-done.7.refs_4_ = bf16[2,272,128]{2,1,0:T(8,128)(2,1)S(1)} collective-permute-done((bf16[2,272,128]{2,1,0:T(8,128)(2,1)S(1)}, bf16[2,272,128]{2,1,0:T(8,128)(2,1)S(1)}, u32[]{:S(2)}, u32[]{:S(2)}) %collective-permute-start.7) | collective-permute-done | bytes 139296 | tf_op jit(solution)/shard_map/ppermute | solution.py:529
  18.5 0.0 slice-start
  18.5 3.5 %prep.1 = (bf16[8,272,128]{2,1,0:T(8,128)(2,1)S(1)}, f32[8,128,128]{2,1,0:T(8,128)S(1)}, f32[8,128,256]{2,1,0:T(8,128)S(1)}, bf16[128,256]{1,0:T(8,128)(2,1)S(1)}, f32[7,128,256]{2,1,0:T(8,128)S(1)}) custom-call(bf16[4,272,128]{2,1,0:T(8,128)(2,1)S(1)} %get-tuple-element.27.refs_0_, bf16[4,272,128]{2,1,0:T(8,128)(2,1)S(1)} %collective-permute-done.4.refs_1_, ...), custom_call_target="tpu_custom_call" | custom-call | flops 2000000000 | bytes 4000000 | tf_op jit(solution)/shard_map/prep/pallas_call | solution.py:249
  22.0 3.4 %collective-permute-start.9 = (bf16[128,256]{1,0:T(8,128)(2,1)S(1)}, bf16[128,256]{1,0:T(8,128)(2,1)S(1)}, u32[]{:S(2)}, u32[]{:S(2)}) collective-permute-start(bf16[128,256]{1,0:T(8,128)(2,1)S(1)} %get-tuple-element.33.own_ref), channel_id=1, source_target_pairs={{0,64},{4,68},{8,72},{12,76},{16,80},{20,84},{24,88},{28,92},{32,9... | collective-permute-start | bytes 196616 | tf_op jit(solution)/shard_map/ppermute | solution.py:543
  25.4 2.9 %collective-permute-start.8 = (bf16[128,256]{1,0:T(8,128)(2,1)S(1)}, bf16[128,256]{1,0:T(8,128)(2,1)S(1)}, u32[]{:S(2)}, u32[]{:S(2)}) collective-permute-start(bf16[128,256]{1,0:T(8,128)(2,1)S(1)} %get-tuple-element.33.own_ref), channel_id=1, source_target_pairs={{0,32},{4,36},{8,40},{12,44},{16,48},{20,52},{24,56},{28,60},{32,6... | collective-permute-start | bytes 196616 | tf_op jit(solution)/shard_map/ppermute | solution.py:543
  28.4 0.6 collective-permute-start.3
  28.9 1.4 %collective-permute-done.9.two_ref = bf16[128,256]{1,0:T(8,128)(2,1)S(1)} collective-permute-done((bf16[128,256]{1,0:T(8,128)(2,1)S(1)}, bf16[128,256]{1,0:T(8,128)(2,1)S(1)}, u32[]{:S(2)}, u32[]{:S(2)}) %collective-permute-start.9) | collective-permute-done | bytes 65568 | tf_op jit(solution)/shard_map/ppermute | solution.py:543
  30.4 2.4 %collective-permute-done.8.one_ref = bf16[128,256]{1,0:T(8,128)(2,1)S(1)} collective-permute-done((bf16[128,256]{1,0:T(8,128)(2,1)S(1)}, bf16[128,256]{1,0:T(8,128)(2,1)S(1)}, u32[]{:S(2)}, u32[]{:S(2)}) %collective-permute-start.8) | collective-permute-done | bytes 65568 | tf_op jit(solution)/shard_map/ppermute | solution.py:543
  32.8 0.3 combine.1
  33.1 0.7 collective-permute-start.11
  33.8 1.9 %collective-permute-start.10 = (bf16[128,256]{1,0:T(8,128)(2,1)S(1)}, bf16[128,256]{1,0:T(8,128)(2,1)S(1)}, u32[]{:S(2)}, u32[]{:S(2)}) collective-permute-start(bf16[128,256]{1,0:T(8,128)(2,1)S(1)} %get-tuple-element.35), channel_id=1, source_target_pairs={{0,96},{4,100},{8,104},{12,108},{16,112},{20,116},{24,120},{28,124... | collective-permute-start | bytes 196616 | tf_op jit(solution)/shard_map/ppermute | solution.py:543
  35.7 0.0 collective-permute-done.1.refs_2_
  35.7 0.0 collective-permute-done.2.refs_3_
  35.7 0.0 collective-permute-done.3.refs_4_
  35.8 0.0 slice-start.1
  35.8 1.3 %query.1.no_ref = f32[1024,256]{1,0:T(8,128)S(1)} custom-call(bf16[4,128,128]{2,1,0:T(8,128)(2,1)S(1)} %get-tuple-element.25.refs_0_, bf16[4,128,128]{2,1,0:T(8,128)(2,1)S(1)} %collective-permute-done.refs_1_, bf16[2,128,128]{2,1,0:T(8,128)(2,1)S(1)} %collective-permute-done.1.refs_2_, bf16[2,128,128]{2,1,0:T(8,128)(2,1)S(1)} %collective-permute-done.2.refs_3_, ...), custom_call_target="tpu_custom_call" | custom-call | flops 1000000000 | bytes 4000000 | tf_op jit(solution)/shard_map/query/pallas_call | solution.py:308
  37.1 0.0 collective-permute-done.11.six_ref
  37.1 5.9 %collective-permute-done.10.three_ref = bf16[128,256]{1,0:T(8,128)(2,1)S(1)} collective-permute-done((bf16[128,256]{1,0:T(8,128)(2,1)S(1)}, bf16[128,256]{1,0:T(8,128)(2,1)S(1)}, u32[]{:S(2)}, u32[]{:S(2)}) %collective-permute-start.10) | collective-permute-done | bytes 65568 | tf_op jit(solution)/shard_map/ppermute | solution.py:543
  43.0 0.0 copy-done
  43.0 0.7 norm.1.normed_ref
  43.7 3.9 %collective-permute-start.12 = (bf16[1024,128]{1,0:T(8,128)(2,1)S(1)}, bf16[1024,128]{1,0:T(8,128)(2,1)S(1)}, u32[]{:S(2)}, u32[]{:S(2)}) collective-permute-start(bf16[1024,128]{1,0:T(8,128)(2,1)S(1)} %norm.1.normed_ref), channel_id=1, source_target_pairs={{0,32},{4,36},{8,40},{12,44},{16,48},{20,52},{24,56},{28,60},{32,6... | collective-permute-start | bytes 786440 | tf_op jit(solution)/shard_map/ppermute | solution.py:543
  47.6 0.0 copy-done.1
  47.6 1.3 %own.1 = (f32[1024,128]{1,0:T(8,128)S(1)}, f32[2,1024,128]{2,1,0:T(8,128)S(1)}, bf16[1024,128]{1,0:T(8,128)(2,1)S(1)}) custom-call(bf16[1024,128]{1,0:T(8,128)(2,1)S(1)} %norm.1.normed_ref, bf16[8,128,384]{2,1,0:T(8,128)(2,1)S(1)} %copy-done.1), custom_call_target="tpu_custom_call" | custom-call | flops 1000000000 | bytes 3000000 | tf_op jit(solution)/shard_map/own/pallas_call | solution.py:426
  48.9 4.3 %collective-permute-done.12.halo_ref = bf16[1024,128]{1,0:T(8,128)(2,1)S(1)} collective-permute-done((bf16[1024,128]{1,0:T(8,128)(2,1)S(1)}, bf16[1024,128]{1,0:T(8,128)(2,1)S(1)}, u32[]{:S(2)}, u32[]{:S(2)}) %collective-permute-start.12) | collective-permute-done | bytes 262176 | tf_op jit(solution)/shard_map/ppermute | solution.py:543
  53.2 4.3 %halo.1 = (bf16[4,128,128]{2,1,0:T(8,128)(2,1)S(1)}, bf16[4,128,128]{2,1,0:T(8,128)(2,1)S(1)}) custom-call(bf16[1024,128]{1,0:T(8,128)(2,1)S(1)} %collective-permute-done.12.halo_ref, bf16[8,128,384]{2,1,0:T(8,128)(2,1)S(1)} %copy-done.1, f32[1024,128]{1,0:T(8,128)S(1)} %get-tuple-element.36.acc_ref, f32[2,1024,128]{2,1,0:T(8,128)S(1)} %get-tuple-element.37.stat_ref, ...), custom_call_target="tpu_custom_call" | custom-call | flops 1000000000 | bytes 3000000 | tf_op jit(solution)/shard_map/halo/pallas_call | solution.py:476
  57.5 0.1 collective-permute-start.13
  57.6 1.3 %collective-permute-done.13.refs_1_ = bf16[4,128,128]{2,1,0:T(8,128)(2,1)S(1)} collective-permute-done((bf16[4,128,128]{2,1,0:T(8,128)(2,1)S(1)}, bf16[4,128,128]{2,1,0:T(8,128)(2,1)S(1)}, u32[]{:S(2)}, u32[]{:S(2)}) %collective-permute-start.13) | collective-permute-done | bytes 131104 | tf_op jit(solution)/shard_map/ppermute | solution.py:529
  58.9 0.1 collective-permute-start.14
  59.0 2.0 %collective-permute-start.15 = (bf16[2,128,128]{2,1,0:T(8,128)(2,1)S(1)}, bf16[2,128,128]{2,1,0:T(8,128)(2,1)S(1)}, u32[]{:S(2)}, u32[]{:S(2)}) collective-permute-start(bf16[2,128,128]{2,1,0:T(8,128)(2,1)S(1)} %pad_maximum_fusion.7), channel_id=1, source_target_pairs={{0,16},{4,20},{8,24},{12,28},{16,0},{20,4},{24,8},{28,12},{32,48},... | collective-permute-start | bytes 196616 | tf_op jit(solution)/shard_map/ppermute | solution.py:529
  61.1 2.8 %collective-permute-start.16 = (bf16[2,128,128]{2,1,0:T(8,128)(2,1)S(1)}, bf16[2,128,128]{2,1,0:T(8,128)(2,1)S(1)}, u32[]{:S(2)}, u32[]{:S(2)}) collective-permute-start(bf16[2,128,128]{2,1,0:T(8,128)(2,1)S(1)} %pad_maximum_fusion.8), channel_id=1, source_target_pairs={{0,24},{4,28},{8,16},{12,20},{16,8},{20,12},{24,0},{28,4},{32,56},... | collective-permute-start | bytes 196616 | tf_op jit(solution)/shard_map/ppermute | solution.py:529
  63.9 0.0 collective-permute-done.14.refs_2_
  63.9 1.0 %collective-permute-done.15.refs_3_ = bf16[2,128,128]{2,1,0:T(8,128)(2,1)S(1)} collective-permute-done((bf16[2,128,128]{2,1,0:T(8,128)(2,1)S(1)}, bf16[2,128,128]{2,1,0:T(8,128)(2,1)S(1)}, u32[]{:S(2)}, u32[]{:S(2)}) %collective-permute-start.15) | collective-permute-done | bytes 65568 | tf_op jit(solution)/shard_map/ppermute | solution.py:529
  64.9 1.7 %collective-permute-done.16.refs_4_ = bf16[2,128,128]{2,1,0:T(8,128)(2,1)S(1)} collective-permute-done((bf16[2,128,128]{2,1,0:T(8,128)(2,1)S(1)}, bf16[2,128,128]{2,1,0:T(8,128)(2,1)S(1)}, u32[]{:S(2)}, u32[]{:S(2)}) %collective-permute-start.16) | collective-permute-done | bytes 65568 | tf_op jit(solution)/shard_map/ppermute | solution.py:529
  66.6 0.0 slice-done
  66.6 0.0 slice-done.1
  66.6 1.9 %project.1 = (f32[32,4096]{1,0:T(8,128)S(1)}, bf16[32,4096]{1,0:T(8,128)(2,1)S(1)}, bf16[32,4096]{1,0:T(8,128)(2,1)S(1)}, bf16[32,4096]{1,0:T(8,128)(2,1)S(1)}) custom-call(bf16[4,128,128]{2,1,0:T(8,128)(2,1)S(1)} %get-tuple-element.39.refs_0_, bf16[4,128,128]{2,1,0:T(8,128)(2,1)S(1)} %collective-permute-done.13.refs_1_, ...), custom_call_target="tpu_custom_call" | custom-call | flops 1000000000 | bytes 9000000 | tf_op jit(solution)/shard_map/project/pallas_call | solution.py:515
  68.5 1.7 %collective-permute-start.17 = (bf16[32,4096]{1,0:T(8,128)(2,1)S(1)}, bf16[32,4096]{1,0:T(8,128)(2,1)S(1)}, u32[]{:S(2)}, u32[]{:S(2)}) collective-permute-start(bf16[32,4096]{1,0:T(8,128)(2,1)S(1)} %get-tuple-element.42), channel_id=1, source_target_pairs={{0,1},{1,0},{2,3},{3,2},{4,5},{5,4},{6,7},{7,6},{8,9},{9,8},{10,11... | collective-permute-start | bytes 786440 | tf_op jit(solution)/shard_map/ppermute | solution.py:564
  70.2 2.2 %collective-permute-start.18 = (bf16[32,4096]{1,0:T(8,128)(2,1)S(1)}, bf16[32,4096]{1,0:T(8,128)(2,1)S(1)}, u32[]{:S(2)}, u32[]{:S(2)}) collective-permute-start(bf16[32,4096]{1,0:T(8,128)(2,1)S(1)} %get-tuple-element.43), channel_id=1, source_target_pairs={{0,3},{1,2},{2,1},{3,0},{4,7},{5,6},{6,5},{7,4},{8,11},{9,10},{10,... | collective-permute-start | bytes 786440 | tf_op jit(solution)/shard_map/ppermute | solution.py:564
  72.4 0.7 collective-permute-start.19
  73.1 4.8 %collective-permute-done.17 = bf16[32,4096]{1,0:T(8,128)(2,1)S(1)} collective-permute-done((bf16[32,4096]{1,0:T(8,128)(2,1)S(1)}, bf16[32,4096]{1,0:T(8,128)(2,1)S(1)}, u32[]{:S(2)}, u32[]{:S(2)}) %collective-permute-start.17) | collective-permute-done | bytes 262176 | tf_op jit(solution)/shard_map/ppermute | solution.py:564
  77.8 4.4 %collective-permute-done.18 = bf16[32,4096]{1,0:T(8,128)(2,1)S(1)} collective-permute-done((bf16[32,4096]{1,0:T(8,128)(2,1)S(1)}, bf16[32,4096]{1,0:T(8,128)(2,1)S(1)}, u32[]{:S(2)}, u32[]{:S(2)}) %collective-permute-start.18) | collective-permute-done | bytes 262176 | tf_op jit(solution)/shard_map/ppermute | solution.py:564
  82.2 1.5 %collective-permute-done.19 = bf16[32,4096]{1,0:T(8,128)(2,1)S(1)} collective-permute-done((bf16[32,4096]{1,0:T(8,128)(2,1)S(1)}, bf16[32,4096]{1,0:T(8,128)(2,1)S(1)}, u32[]{:S(2)}, u32[]{:S(2)}) %collective-permute-start.19) | collective-permute-done | bytes 262176 | tf_op jit(solution)/shard_map/ppermute | solution.py:564
  83.7 0.8 add_convert_fusion
  (16 shorter events, 0.2 us)
Async XLA Ops:
  0.0 43.0 %copy-start = (f32[128]{0:T(128)S(1)}, f32[128]{0:T(128)}, u32[]{:S(2)}) copy-start(f32[128]{0:T(128)} %param.13) | copy-start | bytes 1540
  0.0 47.6 %copy-start.1 = (bf16[8,128,384]{2,1,0:T(8,128)(2,1)S(1)}, bf16[8,128,384]{2,1,0:T(8,128)(2,1)}, u32[]{:S(2)}) copy-start(bf16[8,128,384]{2,1,0:T(8,128)(2,1)} %weight_ref.3) | copy-start | bytes 2359300
  1.4 1.4 %collective-permute-start = (bf16[4,128,128]{2,1,0:T(8,128)(2,1)S(1)}, bf16[4,128,128]{2,1,0:T(8,128)(2,1)S(1)}, u32[]{:S(2)}, u32[]{:S(2)}) collective-permute-start(bf16[4,128,128]{2,1,0:T(8,128)(2,1)S(1)} %get-tuple-element.26), channel_id=1, source_target_pairs={{0,4},{4,0},{8,12},{12,8},{16,20},{20,16},{24,28},{28,24},{32,36},... | collective-permute-start | bytes 393224 | tf_op jit(solution)/shard_map/ppermute | solution.py:529
  1.5 1.7 %collective-permute-start.4 = (bf16[4,272,128]{2,1,0:T(8,128)(2,1)S(1)}, bf16[4,272,128]{2,1,0:T(8,128)(2,1)S(1)}, u32[]{:S(2)}, u32[]{:S(2)}) collective-permute-start(bf16[4,272,128]{2,1,0:T(8,128)(2,1)S(1)} %get-tuple-element.28), channel_id=1, source_target_pairs={{0,4},{4,0},{8,12},{12,8},{16,20},{20,16},{24,28},{28,24},{32,36},... | collective-permute-start | bytes 835592 | tf_op jit(solution)/shard_map/ppermute | solution.py:529
  3.3 9.4 %collective-permute-start.5 = (bf16[2,272,128]{2,1,0:T(8,128)(2,1)S(1)}, bf16[2,272,128]{2,1,0:T(8,128)(2,1)S(1)}, u32[]{:S(2)}, u32[]{:S(2)}) collective-permute-start(bf16[2,272,128]{2,1,0:T(8,128)(2,1)S(1)} %pad_maximum_fusion), channel_id=1, source_target_pairs={{0,8},{4,12},{8,0},{12,4},{16,24},{20,28},{24,16},{28,20},{32,40},... | collective-permute-start | bytes 417800 | tf_op jit(solution)/shard_map/ppermute | solution.py:529
  4.9 10.2 %collective-permute-start.6 = (bf16[2,272,128]{2,1,0:T(8,128)(2,1)S(1)}, bf16[2,272,128]{2,1,0:T(8,128)(2,1)S(1)}, u32[]{:S(2)}, u32[]{:S(2)}) collective-permute-start(bf16[2,272,128]{2,1,0:T(8,128)(2,1)S(1)} %pad_maximum_fusion.1), channel_id=1, source_target_pairs={{0,16},{4,20},{8,24},{12,28},{16,0},{20,4},{24,8},{28,12},{32,48},... | collective-permute-start | bytes 417800 | tf_op jit(solution)/shard_map/ppermute | solution.py:529
  7.8 10.8 %collective-permute-start.7 = (bf16[2,272,128]{2,1,0:T(8,128)(2,1)S(1)}, bf16[2,272,128]{2,1,0:T(8,128)(2,1)S(1)}, u32[]{:S(2)}, u32[]{:S(2)}) collective-permute-start(bf16[2,272,128]{2,1,0:T(8,128)(2,1)S(1)} %pad_maximum_fusion.2), channel_id=1, source_target_pairs={{0,24},{4,28},{8,16},{12,20},{16,8},{20,12},{24,0},{28,4},{32,56},... | collective-permute-start | bytes 417800 | tf_op jit(solution)/shard_map/ppermute | solution.py:529
  8.3 27.4 %collective-permute-start.1 = (bf16[2,128,128]{2,1,0:T(8,128)(2,1)S(1)}, bf16[2,128,128]{2,1,0:T(8,128)(2,1)S(1)}, u32[]{:S(2)}, u32[]{:S(2)}) collective-permute-start(bf16[2,128,128]{2,1,0:T(8,128)(2,1)S(1)} %pad_maximum_fusion.3), channel_id=1, source_target_pairs={{0,8},{4,12},{8,0},{12,4},{16,24},{20,28},{24,16},{28,20},{32,40},... | collective-permute-start | bytes 196616 | tf_op jit(solution)/shard_map/ppermute | solution.py:529
  8.7 27.0 %collective-permute-start.2 = (bf16[2,128,128]{2,1,0:T(8,128)(2,1)S(1)}, bf16[2,128,128]{2,1,0:T(8,128)(2,1)S(1)}, u32[]{:S(2)}, u32[]{:S(2)}) collective-permute-start(bf16[2,128,128]{2,1,0:T(8,128)(2,1)S(1)} %pad_maximum_fusion.4), channel_id=1, source_target_pairs={{0,16},{4,20},{8,24},{12,28},{16,0},{20,4},{24,8},{28,12},{32,48},... | collective-permute-start | bytes 196616 | tf_op jit(solution)/shard_map/ppermute | solution.py:529
  18.5 48.1 %slice-start = ((s8[8388608]{0:T(1024)(128)(4,1)}), s8[4194304]{0:T(1024)(128)(4,1)S(1)}, s32[]{:S(2)}) async-start(s8[8388608]{0:T(1024)(128)(4,1)} %bitcast.1), calls=%async_computation | async-start | bytes 8388608
  22.0 8.3 %collective-permute-start.9 = (bf16[128,256]{1,0:T(8,128)(2,1)S(1)}, bf16[128,256]{1,0:T(8,128)(2,1)S(1)}, u32[]{:S(2)}, u32[]{:S(2)}) collective-permute-start(bf16[128,256]{1,0:T(8,128)(2,1)S(1)} %get-tuple-element.33.own_ref), channel_id=1, source_target_pairs={{0,64},{4,68},{8,72},{12,76},{16,80},{20,84},{24,88},{28,92},{32,9... | collective-permute-start | bytes 196616 | tf_op jit(solution)/shard_map/ppermute | solution.py:543
  25.4 7.4 %collective-permute-start.8 = (bf16[128,256]{1,0:T(8,128)(2,1)S(1)}, bf16[128,256]{1,0:T(8,128)(2,1)S(1)}, u32[]{:S(2)}, u32[]{:S(2)}) collective-permute-start(bf16[128,256]{1,0:T(8,128)(2,1)S(1)} %get-tuple-element.33.own_ref), channel_id=1, source_target_pairs={{0,32},{4,36},{8,40},{12,44},{16,48},{20,52},{24,56},{28,60},{32,6... | collective-permute-start | bytes 196616 | tf_op jit(solution)/shard_map/ppermute | solution.py:543
  28.4 7.4 %collective-permute-start.3 = (bf16[2,128,128]{2,1,0:T(8,128)(2,1)S(1)}, bf16[2,128,128]{2,1,0:T(8,128)(2,1)S(1)}, u32[]{:S(2)}, u32[]{:S(2)}) collective-permute-start(bf16[2,128,128]{2,1,0:T(8,128)(2,1)S(1)} %pad_maximum_fusion.5), channel_id=1, source_target_pairs={{0,24},{4,28},{8,16},{12,20},{16,8},{20,12},{24,0},{28,4},{32,56},... | collective-permute-start | bytes 196616 | tf_op jit(solution)/shard_map/ppermute | solution.py:529
  33.1 4.0 %collective-permute-start.11 = (bf16[128,256]{1,0:T(8,128)(2,1)S(1)}, bf16[128,256]{1,0:T(8,128)(2,1)S(1)}, u32[]{:S(2)}, u32[]{:S(2)}) collective-permute-start(bf16[128,256]{1,0:T(8,128)(2,1)S(1)} %get-tuple-element.35), channel_id=1, source_target_pairs={{0,192},{4,196},{8,200},{12,204},{16,208},{20,212},{24,216},{28,22... | collective-permute-start | bytes 196616 | tf_op jit(solution)/shard_map/ppermute | solution.py:543
  33.8 9.2 %collective-permute-start.10 = (bf16[128,256]{1,0:T(8,128)(2,1)S(1)}, bf16[128,256]{1,0:T(8,128)(2,1)S(1)}, u32[]{:S(2)}, u32[]{:S(2)}) collective-permute-start(bf16[128,256]{1,0:T(8,128)(2,1)S(1)} %get-tuple-element.35), channel_id=1, source_target_pairs={{0,96},{4,100},{8,104},{12,108},{16,112},{20,116},{24,120},{28,124... | collective-permute-start | bytes 196616 | tf_op jit(solution)/shard_map/ppermute | solution.py:543
  35.8 30.9 %slice-start.1 = ((s8[8388608]{0:T(1024)(128)(4,1)}), s8[4194304]{0:T(1024)(128)(4,1)S(1)}, s32[]{:S(2)}) async-start(s8[8388608]{0:T(1024)(128)(4,1)} %bitcast.1), calls=%async_computation.1 | async-start | bytes 8388608
  43.7 9.5 %collective-permute-start.12 = (bf16[1024,128]{1,0:T(8,128)(2,1)S(1)}, bf16[1024,128]{1,0:T(8,128)(2,1)S(1)}, u32[]{:S(2)}, u32[]{:S(2)}) collective-permute-start(bf16[1024,128]{1,0:T(8,128)(2,1)S(1)} %norm.1.normed_ref), channel_id=1, source_target_pairs={{0,32},{4,36},{8,40},{12,44},{16,48},{20,52},{24,56},{28,60},{32,6... | collective-permute-start | bytes 786440 | tf_op jit(solution)/shard_map/ppermute | solution.py:543
  57.5 1.4 %collective-permute-start.13 = (bf16[4,128,128]{2,1,0:T(8,128)(2,1)S(1)}, bf16[4,128,128]{2,1,0:T(8,128)(2,1)S(1)}, u32[]{:S(2)}, u32[]{:S(2)}) collective-permute-start(bf16[4,128,128]{2,1,0:T(8,128)(2,1)S(1)} %get-tuple-element.40), channel_id=1, source_target_pairs={{0,4},{4,0},{8,12},{12,8},{16,20},{20,16},{24,28},{28,24},{32,36},... | collective-permute-start | bytes 393224 | tf_op jit(solution)/shard_map/ppermute | solution.py:529
  58.9 5.0 %collective-permute-start.14 = (bf16[2,128,128]{2,1,0:T(8,128)(2,1)S(1)}, bf16[2,128,128]{2,1,0:T(8,128)(2,1)S(1)}, u32[]{:S(2)}, u32[]{:S(2)}) collective-permute-start(bf16[2,128,128]{2,1,0:T(8,128)(2,1)S(1)} %pad_maximum_fusion.6), channel_id=1, source_target_pairs={{0,8},{4,12},{8,0},{12,4},{16,24},{20,28},{24,16},{28,20},{32,40},... | collective-permute-start | bytes 196616 | tf_op jit(solution)/shard_map/ppermute | solution.py:529
  59.0 5.9 %collective-permute-start.15 = (bf16[2,128,128]{2,1,0:T(8,128)(2,1)S(1)}, bf16[2,128,128]{2,1,0:T(8,128)(2,1)S(1)}, u32[]{:S(2)}, u32[]{:S(2)}) collective-permute-start(bf16[2,128,128]{2,1,0:T(8,128)(2,1)S(1)} %pad_maximum_fusion.7), channel_id=1, source_target_pairs={{0,16},{4,20},{8,24},{12,28},{16,0},{20,4},{24,8},{28,12},{32,48},... | collective-permute-start | bytes 196616 | tf_op jit(solution)/shard_map/ppermute | solution.py:529
  61.1 5.6 %collective-permute-start.16 = (bf16[2,128,128]{2,1,0:T(8,128)(2,1)S(1)}, bf16[2,128,128]{2,1,0:T(8,128)(2,1)S(1)}, u32[]{:S(2)}, u32[]{:S(2)}) collective-permute-start(bf16[2,128,128]{2,1,0:T(8,128)(2,1)S(1)} %pad_maximum_fusion.8), channel_id=1, source_target_pairs={{0,24},{4,28},{8,16},{12,20},{16,8},{20,12},{24,0},{28,4},{32,56},... | collective-permute-start | bytes 196616 | tf_op jit(solution)/shard_map/ppermute | solution.py:529
  68.5 9.3 %collective-permute-start.17 = (bf16[32,4096]{1,0:T(8,128)(2,1)S(1)}, bf16[32,4096]{1,0:T(8,128)(2,1)S(1)}, u32[]{:S(2)}, u32[]{:S(2)}) collective-permute-start(bf16[32,4096]{1,0:T(8,128)(2,1)S(1)} %get-tuple-element.42), channel_id=1, source_target_pairs={{0,1},{1,0},{2,3},{3,2},{4,5},{5,4},{6,7},{7,6},{8,9},{9,8},{10,11... | collective-permute-start | bytes 786440 | tf_op jit(solution)/shard_map/ppermute | solution.py:564
  70.2 12.1 %collective-permute-start.18 = (bf16[32,4096]{1,0:T(8,128)(2,1)S(1)}, bf16[32,4096]{1,0:T(8,128)(2,1)S(1)}, u32[]{:S(2)}, u32[]{:S(2)}) collective-permute-start(bf16[32,4096]{1,0:T(8,128)(2,1)S(1)} %get-tuple-element.43), channel_id=1, source_target_pairs={{0,3},{1,2},{2,1},{3,0},{4,7},{5,6},{6,5},{7,4},{8,11},{9,10},{10,... | collective-permute-start | bytes 786440 | tf_op jit(solution)/shard_map/ppermute | solution.py:564
  72.4 11.4 %collective-permute-start.19 = (bf16[32,4096]{1,0:T(8,128)(2,1)S(1)}, bf16[32,4096]{1,0:T(8,128)(2,1)S(1)}, u32[]{:S(2)}, u32[]{:S(2)}) collective-permute-start(bf16[32,4096]{1,0:T(8,128)(2,1)S(1)} %get-tuple-element.44), channel_id=1, source_target_pairs={{0,2},{1,3},{2,0},{3,1},{4,6},{5,7},{6,4},{7,5},{8,10},{9,11},{10,... | collective-permute-start | bytes 786440 | tf_op jit(solution)/shard_map/ppermute | solution.py:564

commit v5 on v4

--- a/solution.py
+++ b/solution.py
@@ -400,6 +400,10 @@
     return out
 
 
+def tiled(column, like):
+    return jnp.concatenate([column] * (like.shape[1] // C), axis=1)
+
+
 def own_kernel(normed_ref, weight_ref, acc_ref, stat_ref, q2_ref):
     me = lax.axis_index("seq") % PLANE
     proj = dot(normed_ref[...], weight_ref[me]).astype(BF16)
@@ -452,15 +456,16 @@
         for at, span in zip(starts, spans)
     ]
     scores = [[jnp.where(col > row, parts[0], NEG)] + parts[1:] for parts in scores]
-    before = [stat_ref[0, at : at + QB, 0:1] for at in starts]
+    before = [stat_ref[0, at : at + QB, :] for at in starts]
     tops = [jnp.maximum(row_max(parts) + floor, old) for parts, old in zip(scores, before)]
     raised = [
-        [jnp.exp2((s - (top - floor)) * SCALE) for s in parts] for parts, top in zip(scores, tops)
+        [jnp.exp2((s - tiled(top - floor, s)) * SCALE) for s in parts]
+        for parts, top in zip(scores, tops)
     ]
     fades = [jnp.exp2((old - top) * SCALE) for old, top in zip(before, tops)]
     for i, at in enumerate(starts):
         rows = slice(at, at + QB)
-        total = row_sum(raised[i]) + fades[i] * stat_ref[1, rows, 0:1]
+        total = row_sum(raised[i]) + fades[i] * stat_ref[1, rows, :]
         acc = acc_ref[rows, :] * fades[i] + weighted(
             raised[i], [proj[a:b, C:] for a, b in spans[i]]
         )

time: 84.8 us -> 82 us (0.967)
  Pallas kernels: 14.7 us -> 12 us
    pallas_call x1, Pallas kernels: 4.27 us -> 1.49 us  [halo_part(): pl.pallas_call(halo_kernel, out_shape=[jax.ShapeDtypeStruct((4, C, C), BF...]
where the time goes in v5:
time: 82 us; the launch traced here: 81.8 us
  waiting for transfers between devices  35.7 us (44%)
  starting transfers between devices  32.9 us (40%)
  Pallas kernels  12 us (15%)
  other arithmetic  0.91 us (1%)
    ppermute x12, starting transfers between devices, swap(): lax.ppermute(block, 'seq', [(s, s ^ d) for s in range(PLANE * PLANES)])  15.5 us
    ppermute x5, waiting for transfers between devices, later_plane(): return lax.ppermute(block, 'seq', route)  14 us
    ppermute x5, starting transfers between devices, later_plane(): return lax.ppermute(block, 'seq', route)  12.8 us
    ppermute x12, waiting for transfers between devices, swap(): lax.ppermute(block, 'seq', [(s, s ^ d) for s in range(PLANE * PLANES)])  11 us
    ppermute x3, waiting for transfers between devices, local(): moved[d] = lax.ppermute(sums[d], 'heads', [(s, s ^ d) for s in range(4)])  10.7 us
    ppermute x3, starting transfers between devices, local(): moved[d] = lax.ppermute(sums[d], 'heads', [(s, s ^ d) for s in range(4)])  4.58 us
    pallas_call x1, Pallas kernels, prep(): pl.pallas_call(prep_kernel, out_shape=[jax.ShapeDtypeStruct((PLANE, BLK,...  3.51 us
    pallas_call x1, Pallas kernels, project(): pl.pallas_call(project_kernel, out_shape=[jax.ShapeDtypeStruct((32, width...  1.87 us
  transfers between devices with their start and end apart: 20, of which 14 were waited for; matrix products, arithmetic and copies ran while one was open for 0% of the time, Pallas kernels for 8%

profile of v5, /device:TPU:128, one launch (start us, length us, event | category | flops | bytes accessed | tf_op | source)
XLA Modules:
  0.0 81.8 jit_solution(1915291166594462802)
XLA Ops:
  0.0 0.0 copy-start
  0.0 0.0 copy-start.1
  0.0 1.4 %pack.1 = (bf16[4,272,128]{2,1,0:T(8,128)(2,1)S(1)}, bf16[4,272,128]{2,1,0:T(8,128)(2,1)S(1)}, bf16[4,128,128]{2,1,0:T(8,128)(2,1)S(1)}, bf16[4,128,128]{2,1,0:T(8,128)(2,1)S(1)}) custom-call(bf16[128,1024]{1,0:T(8,128)(2,1)} %q_ref.1, bf16[128,1024]{1,0:T(8,128)(2,1)} %k_ref.1, bf16[128,1024]{1,0:T(8,128)(2,1)} %v_ref.1, f32[8,128]{1,0:T(8,128)} %decay_ref.1, ...), custom_call_target="tpu_custom_call" | custom-call | tf_op jit(solution)/shard_map/pack/pallas_call | solution.py:113
  1.4 0.1 collective-permute-start
  1.5 0.5 collective-permute-start.4
  2.1 0.8 collective-permute-done.refs_1_
  2.9 0.4 collective-permute-done.4.refs_1_
  3.3 1.6 %collective-permute-start.5 = (bf16[2,272,128]{2,1,0:T(8,128)(2,1)S(1)}, bf16[2,272,128]{2,1,0:T(8,128)(2,1)S(1)}, u32[]{:S(2)}, u32[]{:S(2)}) collective-permute-start(bf16[2,272,128]{2,1,0:T(8,128)(2,1)S(1)} %pad_maximum_fusion), channel_id=1, source_target_pairs={{0,8},{4,12},{8,0},{12,4},{16,24},{20,28},{24,16},{28,20},{32,40},... | collective-permute-start | bytes 417800 | tf_op jit(solution)/shard_map/ppermute | solution.py:534
  4.9 2.8 %collective-permute-start.6 = (bf16[2,272,128]{2,1,0:T(8,128)(2,1)S(1)}, bf16[2,272,128]{2,1,0:T(8,128)(2,1)S(1)}, u32[]{:S(2)}, u32[]{:S(2)}) collective-permute-start(bf16[2,272,128]{2,1,0:T(8,128)(2,1)S(1)} %pad_maximum_fusion.1), channel_id=1, source_target_pairs={{0,16},{4,20},{8,24},{12,28},{16,0},{20,4},{24,8},{28,12},{32,48},... | collective-permute-start | bytes 417800 | tf_op jit(solution)/shard_map/ppermute | solution.py:534
  7.8 0.6 collective-permute-start.7
  8.3 0.4 collective-permute-start.1
  8.7 4.0 %collective-permute-start.2 = (bf16[2,128,128]{2,1,0:T(8,128)(2,1)S(1)}, bf16[2,128,128]{2,1,0:T(8,128)(2,1)S(1)}, u32[]{:S(2)}, u32[]{:S(2)}) collective-permute-start(bf16[2,128,128]{2,1,0:T(8,128)(2,1)S(1)} %pad_maximum_fusion.4), channel_id=1, source_target_pairs={{0,16},{4,20},{8,24},{12,28},{16,0},{20,4},{24,8},{28,12},{32,48},... | collective-permute-start | bytes 196616 | tf_op jit(solution)/shard_map/ppermute | solution.py:534
  12.7 0.0 collective-permute-done.5.refs_2_
  12.7 2.4 %collective-permute-done.6.refs_3_ = bf16[2,272,128]{2,1,0:T(8,128)(2,1)S(1)} collective-permute-done((bf16[2,272,128]{2,1,0:T(8,128)(2,1)S(1)}, bf16[2,272,128]{2,1,0:T(8,128)(2,1)S(1)}, u32[]{:S(2)}, u32[]{:S(2)}) %collective-permute-start.6) | collective-permute-done | bytes 139296 | tf_op jit(solution)/shard_map/ppermute | solution.py:534
  15.1 3.4 %collective-permute-done.7.refs_4_ = bf16[2,272,128]{2,1,0:T(8,128)(2,1)S(1)} collective-permute-done((bf16[2,272,128]{2,1,0:T(8,128)(2,1)S(1)}, bf16[2,272,128]{2,1,0:T(8,128)(2,1)S(1)}, u32[]{:S(2)}, u32[]{:S(2)}) %collective-permute-start.7) | collective-permute-done | bytes 139296 | tf_op jit(solution)/shard_map/ppermute | solution.py:534
  18.5 0.0 slice-start
  18.5 3.5 %prep.1 = (bf16[8,272,128]{2,1,0:T(8,128)(2,1)S(1)}, f32[8,128,128]{2,1,0:T(8,128)S(1)}, f32[8,128,256]{2,1,0:T(8,128)S(1)}, bf16[128,256]{1,0:T(8,128)(2,1)S(1)}, f32[7,128,256]{2,1,0:T(8,128)S(1)}) custom-call(bf16[4,272,128]{2,1,0:T(8,128)(2,1)S(1)} %get-tuple-element.27.refs_0_, bf16[4,272,128]{2,1,0:T(8,128)(2,1)S(1)} %collective-permute-done.4.refs_1_, ...), custom_call_target="tpu_custom_call" | custom-call | flops 2000000000 | bytes 4000000 | tf_op jit(solution)/shard_map/prep/pallas_call | solution.py:249
  22.0 3.4 %collective-permute-start.9 = (bf16[128,256]{1,0:T(8,128)(2,1)S(1)}, bf16[128,256]{1,0:T(8,128)(2,1)S(1)}, u32[]{:S(2)}, u32[]{:S(2)}) collective-permute-start(bf16[128,256]{1,0:T(8,128)(2,1)S(1)} %get-tuple-element.33.own_ref), channel_id=1, source_target_pairs={{0,64},{4,68},{8,72},{12,76},{16,80},{20,84},{24,88},{28,92},{32,9... | collective-permute-start | bytes 196616 | tf_op jit(solution)/shard_map/ppermute | solution.py:548
  25.4 2.9 %collective-permute-start.8 = (bf16[128,256]{1,0:T(8,128)(2,1)S(1)}, bf16[128,256]{1,0:T(8,128)(2,1)S(1)}, u32[]{:S(2)}, u32[]{:S(2)}) collective-permute-start(bf16[128,256]{1,0:T(8,128)(2,1)S(1)} %get-tuple-element.33.own_ref), channel_id=1, source_target_pairs={{0,32},{4,36},{8,40},{12,44},{16,48},{20,52},{24,56},{28,60},{32,6... | collective-permute-start | bytes 196616 | tf_op jit(solution)/shard_map/ppermute | solution.py:548
  28.4 0.6 collective-permute-start.3
  28.9 1.4 %collective-permute-done.9.two_ref = bf16[128,256]{1,0:T(8,128)(2,1)S(1)} collective-permute-done((bf16[128,256]{1,0:T(8,128)(2,1)S(1)}, bf16[128,256]{1,0:T(8,128)(2,1)S(1)}, u32[]{:S(2)}, u32[]{:S(2)}) %collective-permute-start.9) | collective-permute-done | bytes 65568 | tf_op jit(solution)/shard_map/ppermute | solution.py:548
  30.4 2.4 %collective-permute-done.8.one_ref = bf16[128,256]{1,0:T(8,128)(2,1)S(1)} collective-permute-done((bf16[128,256]{1,0:T(8,128)(2,1)S(1)}, bf16[128,256]{1,0:T(8,128)(2,1)S(1)}, u32[]{:S(2)}, u32[]{:S(2)}) %collective-permute-start.8) | collective-permute-done | bytes 65568 | tf_op jit(solution)/shard_map/ppermute | solution.py:548
  32.8 0.3 combine.1
  33.1 0.7 collective-permute-start.11
  33.8 1.9 %collective-permute-start.10 = (bf16[128,256]{1,0:T(8,128)(2,1)S(1)}, bf16[128,256]{1,0:T(8,128)(2,1)S(1)}, u32[]{:S(2)}, u32[]{:S(2)}) collective-permute-start(bf16[128,256]{1,0:T(8,128)(2,1)S(1)} %get-tuple-element.35), channel_id=1, source_target_pairs={{0,96},{4,100},{8,104},{12,108},{16,112},{20,116},{24,120},{28,124... | collective-permute-start | bytes 196616 | tf_op jit(solution)/shard_map/ppermute | solution.py:548
  35.7 0.0 collective-permute-done.1.refs_2_
  35.7 0.0 collective-permute-done.2.refs_3_
  35.7 0.0 collective-permute-done.3.refs_4_
  35.8 0.0 slice-start.1
  35.8 1.3 %query.1.no_ref = f32[1024,256]{1,0:T(8,128)S(1)} custom-call(bf16[4,128,128]{2,1,0:T(8,128)(2,1)S(1)} %get-tuple-element.25.refs_0_, bf16[4,128,128]{2,1,0:T(8,128)(2,1)S(1)} %collective-permute-done.refs_1_, bf16[2,128,128]{2,1,0:T(8,128)(2,1)S(1)} %collective-permute-done.1.refs_2_, bf16[2,128,128]{2,1,0:T(8,128)(2,1)S(1)} %collective-permute-done.2.refs_3_, ...), custom_call_target="tpu_custom_call" | custom-call | flops 1000000000 | bytes 4000000 | tf_op jit(solution)/shard_map/query/pallas_call | solution.py:308
  37.1 0.0 collective-permute-done.11.six_ref
  37.1 5.9 %collective-permute-done.10.three_ref = bf16[128,256]{1,0:T(8,128)(2,1)S(1)} collective-permute-done((bf16[128,256]{1,0:T(8,128)(2,1)S(1)}, bf16[128,256]{1,0:T(8,128)(2,1)S(1)}, u32[]{:S(2)}, u32[]{:S(2)}) %collective-permute-start.10) | collective-permute-done | bytes 65568 | tf_op jit(solution)/shard_map/ppermute | solution.py:548
  43.0 0.0 copy-done
  43.0 0.7 norm.1.normed_ref
  43.7 3.9 %collective-permute-start.12 = (bf16[1024,128]{1,0:T(8,128)(2,1)S(1)}, bf16[1024,128]{1,0:T(8,128)(2,1)S(1)}, u32[]{:S(2)}, u32[]{:S(2)}) collective-permute-start(bf16[1024,128]{1,0:T(8,128)(2,1)S(1)} %norm.1.normed_ref), channel_id=1, source_target_pairs={{0,32},{4,36},{8,40},{12,44},{16,48},{20,52},{24,56},{28,60},{32,6... | collective-permute-start | bytes 786440 | tf_op jit(solution)/shard_map/ppermute | solution.py:548
  47.6 0.0 copy-done.1
  47.6 1.3 %own.1 = (f32[1024,128]{1,0:T(8,128)S(1)}, f32[2,1024,128]{2,1,0:T(8,128)S(1)}, bf16[1024,128]{1,0:T(8,128)(2,1)S(1)}) custom-call(bf16[1024,128]{1,0:T(8,128)(2,1)S(1)} %norm.1.normed_ref, bf16[8,128,384]{2,1,0:T(8,128)(2,1)S(1)} %copy-done.1), custom_call_target="tpu_custom_call" | custom-call | flops 1000000000 | bytes 3000000 | tf_op jit(solution)/shard_map/own/pallas_call | solution.py:430
  48.9 4.3 %collective-permute-done.12.halo_ref = bf16[1024,128]{1,0:T(8,128)(2,1)S(1)} collective-permute-done((bf16[1024,128]{1,0:T(8,128)(2,1)S(1)}, bf16[1024,128]{1,0:T(8,128)(2,1)S(1)}, u32[]{:S(2)}, u32[]{:S(2)}) %collective-permute-start.12) | collective-permute-done | bytes 262176 | tf_op jit(solution)/shard_map/ppermute | solution.py:548
  53.2 1.5 %halo.1 = (bf16[4,128,128]{2,1,0:T(8,128)(2,1)S(1)}, bf16[4,128,128]{2,1,0:T(8,128)(2,1)S(1)}) custom-call(bf16[1024,128]{1,0:T(8,128)(2,1)S(1)} %collective-permute-done.12.halo_ref, bf16[8,128,384]{2,1,0:T(8,128)(2,1)S(1)} %copy-done.1, f32[1024,128]{1,0:T(8,128)S(1)} %get-tuple-element.36.acc_ref, f32[2,1024,128]{2,1,0:T(8,128)S(1)} %get-tuple-element.37.stat_ref, ...), custom_call_target="tpu_custom_call" | custom-call | flops 1000000000 | bytes 3000000 | tf_op jit(solution)/shard_map/halo/pallas_call | solution.py:481
  54.7 0.1 collective-permute-start.13
  54.8 1.3 %collective-permute-done.13.refs_1_ = bf16[4,128,128]{2,1,0:T(8,128)(2,1)S(1)} collective-permute-done((bf16[4,128,128]{2,1,0:T(8,128)(2,1)S(1)}, bf16[4,128,128]{2,1,0:T(8,128)(2,1)S(1)}, u32[]{:S(2)}, u32[]{:S(2)}) %collective-permute-start.13) | collective-permute-done | bytes 131104 | tf_op jit(solution)/shard_map/ppermute | solution.py:534
  56.2 0.1 collective-permute-start.14
  56.3 2.0 %collective-permute-start.15 = (bf16[2,128,128]{2,1,0:T(8,128)(2,1)S(1)}, bf16[2,128,128]{2,1,0:T(8,128)(2,1)S(1)}, u32[]{:S(2)}, u32[]{:S(2)}) collective-permute-start(bf16[2,128,128]{2,1,0:T(8,128)(2,1)S(1)} %pad_maximum_fusion.7), channel_id=1, source_target_pairs={{0,16},{4,20},{8,24},{12,28},{16,0},{20,4},{24,8},{28,12},{32,48},... | collective-permute-start | bytes 196616 | tf_op jit(solution)/shard_map/ppermute | solution.py:534
  58.3 2.8 %collective-permute-start.16 = (bf16[2,128,128]{2,1,0:T(8,128)(2,1)S(1)}, bf16[2,128,128]{2,1,0:T(8,128)(2,1)S(1)}, u32[]{:S(2)}, u32[]{:S(2)}) collective-permute-start(bf16[2,128,128]{2,1,0:T(8,128)(2,1)S(1)} %pad_maximum_fusion.8), channel_id=1, source_target_pairs={{0,24},{4,28},{8,16},{12,20},{16,8},{20,12},{24,0},{28,4},{32,56},... | collective-permute-start | bytes 196616 | tf_op jit(solution)/shard_map/ppermute | solution.py:534
  61.1 0.0 collective-permute-done.14.refs_2_
  61.1 1.0 %collective-permute-done.15.refs_3_ = bf16[2,128,128]{2,1,0:T(8,128)(2,1)S(1)} collective-permute-done((bf16[2,128,128]{2,1,0:T(8,128)(2,1)S(1)}, bf16[2,128,128]{2,1,0:T(8,128)(2,1)S(1)}, u32[]{:S(2)}, u32[]{:S(2)}) %collective-permute-start.15) | collective-permute-done | bytes 65568 | tf_op jit(solution)/shard_map/ppermute | solution.py:534
  62.2 1.7 %collective-permute-done.16.refs_4_ = bf16[2,128,128]{2,1,0:T(8,128)(2,1)S(1)} collective-permute-done((bf16[2,128,128]{2,1,0:T(8,128)(2,1)S(1)}, bf16[2,128,128]{2,1,0:T(8,128)(2,1)S(1)}, u32[]{:S(2)}, u32[]{:S(2)}) %collective-permute-start.16) | collective-permute-done | bytes 65568 | tf_op jit(solution)/shard_map/ppermute | solution.py:534
  63.8 0.0 slice-done
  63.8 0.0 slice-done.1
  63.9 1.9 %project.1 = (f32[32,4096]{1,0:T(8,128)S(1)}, bf16[32,4096]{1,0:T(8,128)(2,1)S(1)}, bf16[32,4096]{1,0:T(8,128)(2,1)S(1)}, bf16[32,4096]{1,0:T(8,128)(2,1)S(1)}) custom-call(bf16[4,128,128]{2,1,0:T(8,128)(2,1)S(1)} %get-tuple-element.39.refs_0_, bf16[4,128,128]{2,1,0:T(8,128)(2,1)S(1)} %collective-permute-done.13.refs_1_, ...), custom_call_target="tpu_custom_call" | custom-call | flops 1000000000 | bytes 9000000 | tf_op jit(solution)/shard_map/project/pallas_call | solution.py:520
  65.7 1.7 %collective-permute-start.17 = (bf16[32,4096]{1,0:T(8,128)(2,1)S(1)}, bf16[32,4096]{1,0:T(8,128)(2,1)S(1)}, u32[]{:S(2)}, u32[]{:S(2)}) collective-permute-start(bf16[32,4096]{1,0:T(8,128)(2,1)S(1)} %get-tuple-element.42), channel_id=1, source_target_pairs={{0,1},{1,0},{2,3},{3,2},{4,5},{5,4},{6,7},{7,6},{8,9},{9,8},{10,11... | collective-permute-start | bytes 786440 | tf_op jit(solution)/shard_map/ppermute | solution.py:569
  67.4 2.2 %collective-permute-start.18 = (bf16[32,4096]{1,0:T(8,128)(2,1)S(1)}, bf16[32,4096]{1,0:T(8,128)(2,1)S(1)}, u32[]{:S(2)}, u32[]{:S(2)}) collective-permute-start(bf16[32,4096]{1,0:T(8,128)(2,1)S(1)} %get-tuple-element.43), channel_id=1, source_target_pairs={{0,3},{1,2},{2,1},{3,0},{4,7},{5,6},{6,5},{7,4},{8,11},{9,10},{10,... | collective-permute-start | bytes 786440 | tf_op jit(solution)/shard_map/ppermute | solution.py:569
  69.6 0.7 collective-permute-start.19
  70.3 4.8 %collective-permute-done.17 = bf16[32,4096]{1,0:T(8,128)(2,1)S(1)} collective-permute-done((bf16[32,4096]{1,0:T(8,128)(2,1)S(1)}, bf16[32,4096]{1,0:T(8,128)(2,1)S(1)}, u32[]{:S(2)}, u32[]{:S(2)}) %collective-permute-start.17) | collective-permute-done | bytes 262176 | tf_op jit(solution)/shard_map/ppermute | solution.py:569
  75.1 4.4 %collective-permute-done.18 = bf16[32,4096]{1,0:T(8,128)(2,1)S(1)} collective-permute-done((bf16[32,4096]{1,0:T(8,128)(2,1)S(1)}, bf16[32,4096]{1,0:T(8,128)(2,1)S(1)}, u32[]{:S(2)}, u32[]{:S(2)}) %collective-permute-start.18) | collective-permute-done | bytes 262176 | tf_op jit(solution)/shard_map/ppermute | solution.py:569
  79.5 1.5 %collective-permute-done.19 = bf16[32,4096]{1,0:T(8,128)(2,1)S(1)} collective-permute-done((bf16[32,4096]{1,0:T(8,128)(2,1)S(1)}, bf16[32,4096]{1,0:T(8,128)(2,1)S(1)}, u32[]{:S(2)}, u32[]{:S(2)}) %collective-permute-start.19) | collective-permute-done | bytes 262176 | tf_op jit(solution)/shard_map/ppermute | solution.py:569
  81.0 0.8 add_convert_fusion
  (16 shorter events, 0.2 us)
Async XLA Ops:
  0.0 43.0 %copy-start = (f32[128]{0:T(128)S(1)}, f32[128]{0:T(128)}, u32[]{:S(2)}) copy-start(f32[128]{0:T(128)} %param.13) | copy-start | bytes 1540
  0.0 47.6 %copy-start.1 = (bf16[8,128,384]{2,1,0:T(8,128)(2,1)S(1)}, bf16[8,128,384]{2,1,0:T(8,128)(2,1)}, u32[]{:S(2)}) copy-start(bf16[8,128,384]{2,1,0:T(8,128)(2,1)} %weight_ref.3) | copy-start | bytes 2359300
  1.4 1.4 %collective-permute-start = (bf16[4,128,128]{2,1,0:T(8,128)(2,1)S(1)}, bf16[4,128,128]{2,1,0:T(8,128)(2,1)S(1)}, u32[]{:S(2)}, u32[]{:S(2)}) collective-permute-start(bf16[4,128,128]{2,1,0:T(8,128)(2,1)S(1)} %get-tuple-element.26), channel_id=1, source_target_pairs={{0,4},{4,0},{8,12},{12,8},{16,20},{20,16},{24,28},{28,24},{32,36},... | collective-permute-start | bytes 393224 | tf_op jit(solution)/shard_map/ppermute | solution.py:534
  1.5 1.7 %collective-permute-start.4 = (bf16[4,272,128]{2,1,0:T(8,128)(2,1)S(1)}, bf16[4,272,128]{2,1,0:T(8,128)(2,1)S(1)}, u32[]{:S(2)}, u32[]{:S(2)}) collective-permute-start(bf16[4,272,128]{2,1,0:T(8,128)(2,1)S(1)} %get-tuple-element.28), channel_id=1, source_target_pairs={{0,4},{4,0},{8,12},{12,8},{16,20},{20,16},{24,28},{28,24},{32,36},... | collective-permute-start | bytes 835592 | tf_op jit(solution)/shard_map/ppermute | solution.py:534
  3.3 9.4 %collective-permute-start.5 = (bf16[2,272,128]{2,1,0:T(8,128)(2,1)S(1)}, bf16[2,272,128]{2,1,0:T(8,128)(2,1)S(1)}, u32[]{:S(2)}, u32[]{:S(2)}) collective-permute-start(bf16[2,272,128]{2,1,0:T(8,128)(2,1)S(1)} %pad_maximum_fusion), channel_id=1, source_target_pairs={{0,8},{4,12},{8,0},{12,4},{16,24},{20,28},{24,16},{28,20},{32,40},... | collective-permute-start | bytes 417800 | tf_op jit(solution)/shard_map/ppermute | solution.py:534
  4.9 10.2 %collective-permute-start.6 = (bf16[2,272,128]{2,1,0:T(8,128)(2,1)S(1)}, bf16[2,272,128]{2,1,0:T(8,128)(2,1)S(1)}, u32[]{:S(2)}, u32[]{:S(2)}) collective-permute-start(bf16[2,272,128]{2,1,0:T(8,128)(2,1)S(1)} %pad_maximum_fusion.1), channel_id=1, source_target_pairs={{0,16},{4,20},{8,24},{12,28},{16,0},{20,4},{24,8},{28,12},{32,48},... | collective-permute-start | bytes 417800 | tf_op jit(solution)/shard_map/ppermute | solution.py:534
  7.8 10.8 %collective-permute-start.7 = (bf16[2,272,128]{2,1,0:T(8,128)(2,1)S(1)}, bf16[2,272,128]{2,1,0:T(8,128)(2,1)S(1)}, u32[]{:S(2)}, u32[]{:S(2)}) collective-permute-start(bf16[2,272,128]{2,1,0:T(8,128)(2,1)S(1)} %pad_maximum_fusion.2), channel_id=1, source_target_pairs={{0,24},{4,28},{8,16},{12,20},{16,8},{20,12},{24,0},{28,4},{32,56},... | collective-permute-start | bytes 417800 | tf_op jit(solution)/shard_map/ppermute | solution.py:534
  8.3 27.4 %collective-permute-start.1 = (bf16[2,128,128]{2,1,0:T(8,128)(2,1)S(1)}, bf16[2,128,128]{2,1,0:T(8,128)(2,1)S(1)}, u32[]{:S(2)}, u32[]{:S(2)}) collective-permute-start(bf16[2,128,128]{2,1,0:T(8,128)(2,1)S(1)} %pad_maximum_fusion.3), channel_id=1, source_target_pairs={{0,8},{4,12},{8,0},{12,4},{16,24},{20,28},{24,16},{28,20},{32,40},... | collective-permute-start | bytes 196616 | tf_op jit(solution)/shard_map/ppermute | solution.py:534
  8.7 27.0 %collective-permute-start.2 = (bf16[2,128,128]{2,1,0:T(8,128)(2,1)S(1)}, bf16[2,128,128]{2,1,0:T(8,128)(2,1)S(1)}, u32[]{:S(2)}, u32[]{:S(2)}) collective-permute-start(bf16[2,128,128]{2,1,0:T(8,128)(2,1)S(1)} %pad_maximum_fusion.4), channel_id=1, source_target_pairs={{0,16},{4,20},{8,24},{12,28},{16,0},{20,4},{24,8},{28,12},{32,48},... | collective-permute-start | bytes 196616 | tf_op jit(solution)/shard_map/ppermute | solution.py:534
  18.5 45.3 %slice-start = ((s8[8388608]{0:T(1024)(128)(4,1)}), s8[4194304]{0:T(1024)(128)(4,1)S(1)}, s32[]{:S(2)}) async-start(s8[8388608]{0:T(1024)(128)(4,1)} %bitcast.1), calls=%async_computation | async-start | bytes 8388608
  22.0 8.3 %collective-permute-start.9 = (bf16[128,256]{1,0:T(8,128)(2,1)S(1)}, bf16[128,256]{1,0:T(8,128)(2,1)S(1)}, u32[]{:S(2)}, u32[]{:S(2)}) collective-permute-start(bf16[128,256]{1,0:T(8,128)(2,1)S(1)} %get-tuple-element.33.own_ref), channel_id=1, source_target_pairs={{0,64},{4,68},{8,72},{12,76},{16,80},{20,84},{24,88},{28,92},{32,9... | collective-permute-start | bytes 196616 | tf_op jit(solution)/shard_map/ppermute | solution.py:548
  25.4 7.4 %collective-permute-start.8 = (bf16[128,256]{1,0:T(8,128)(2,1)S(1)}, bf16[128,256]{1,0:T(8,128)(2,1)S(1)}, u32[]{:S(2)}, u32[]{:S(2)}) collective-permute-start(bf16[128,256]{1,0:T(8,128)(2,1)S(1)} %get-tuple-element.33.own_ref), channel_id=1, source_target_pairs={{0,32},{4,36},{8,40},{12,44},{16,48},{20,52},{24,56},{28,60},{32,6... | collective-permute-start | bytes 196616 | tf_op jit(solution)/shard_map/ppermute | solution.py:548
  28.4 7.4 %collective-permute-start.3 = (bf16[2,128,128]{2,1,0:T(8,128)(2,1)S(1)}, bf16[2,128,128]{2,1,0:T(8,128)(2,1)S(1)}, u32[]{:S(2)}, u32[]{:S(2)}) collective-permute-start(bf16[2,128,128]{2,1,0:T(8,128)(2,1)S(1)} %pad_maximum_fusion.5), channel_id=1, source_target_pairs={{0,24},{4,28},{8,16},{12,20},{16,8},{20,12},{24,0},{28,4},{32,56},... | collective-permute-start | bytes 196616 | tf_op jit(solution)/shard_map/ppermute | solution.py:534
  33.1 4.0 %collective-permute-start.11 = (bf16[128,256]{1,0:T(8,128)(2,1)S(1)}, bf16[128,256]{1,0:T(8,128)(2,1)S(1)}, u32[]{:S(2)}, u32[]{:S(2)}) collective-permute-start(bf16[128,256]{1,0:T(8,128)(2,1)S(1)} %get-tuple-element.35), channel_id=1, source_target_pairs={{0,192},{4,196},{8,200},{12,204},{16,208},{20,212},{24,216},{28,22... | collective-permute-start | bytes 196616 | tf_op jit(solution)/shard_map/ppermute | solution.py:548
  33.8 9.2 %collective-permute-start.10 = (bf16[128,256]{1,0:T(8,128)(2,1)S(1)}, bf16[128,256]{1,0:T(8,128)(2,1)S(1)}, u32[]{:S(2)}, u32[]{:S(2)}) collective-permute-start(bf16[128,256]{1,0:T(8,128)(2,1)S(1)} %get-tuple-element.35), channel_id=1, source_target_pairs={{0,96},{4,100},{8,104},{12,108},{16,112},{20,116},{24,120},{28,124... | collective-permute-start | bytes 196616 | tf_op jit(solution)/shard_map/ppermute | solution.py:548
  35.8 28.1 %slice-start.1 = ((s8[8388608]{0:T(1024)(128)(4,1)}), s8[4194304]{0:T(1024)(128)(4,1)S(1)}, s32[]{:S(2)}) async-start(s8[8388608]{0:T(1024)(128)(4,1)} %bitcast.1), calls=%async_computation.1 | async-start | bytes 8388608
  43.7 9.5 %collective-permute-start.12 = (bf16[1024,128]{1,0:T(8,128)(2,1)S(1)}, bf16[1024,128]{1,0:T(8,128)(2,1)S(1)}, u32[]{:S(2)}, u32[]{:S(2)}) collective-permute-start(bf16[1024,128]{1,0:T(8,128)(2,1)S(1)} %norm.1.normed_ref), channel_id=1, source_target_pairs={{0,32},{4,36},{8,40},{12,44},{16,48},{20,52},{24,56},{28,60},{32,6... | collective-permute-start | bytes 786440 | tf_op jit(solution)/shard_map/ppermute | solution.py:548
  54.7 1.4 %collective-permute-start.13 = (bf16[4,128,128]{2,1,0:T(8,128)(2,1)S(1)}, bf16[4,128,128]{2,1,0:T(8,128)(2,1)S(1)}, u32[]{:S(2)}, u32[]{:S(2)}) collective-permute-start(bf16[4,128,128]{2,1,0:T(8,128)(2,1)S(1)} %get-tuple-element.40), channel_id=1, source_target_pairs={{0,4},{4,0},{8,12},{12,8},{16,20},{20,16},{24,28},{28,24},{32,36},... | collective-permute-start | bytes 393224 | tf_op jit(solution)/shard_map/ppermute | solution.py:534
  56.2 5.0 %collective-permute-start.14 = (bf16[2,128,128]{2,1,0:T(8,128)(2,1)S(1)}, bf16[2,128,128]{2,1,0:T(8,128)(2,1)S(1)}, u32[]{:S(2)}, u32[]{:S(2)}) collective-permute-start(bf16[2,128,128]{2,1,0:T(8,128)(2,1)S(1)} %pad_maximum_fusion.6), channel_id=1, source_target_pairs={{0,8},{4,12},{8,0},{12,4},{16,24},{20,28},{24,16},{28,20},{32,40},... | collective-permute-start | bytes 196616 | tf_op jit(solution)/shard_map/ppermute | solution.py:534
  56.3 5.9 %collective-permute-start.15 = (bf16[2,128,128]{2,1,0:T(8,128)(2,1)S(1)}, bf16[2,128,128]{2,1,0:T(8,128)(2,1)S(1)}, u32[]{:S(2)}, u32[]{:S(2)}) collective-permute-start(bf16[2,128,128]{2,1,0:T(8,128)(2,1)S(1)} %pad_maximum_fusion.7), channel_id=1, source_target_pairs={{0,16},{4,20},{8,24},{12,28},{16,0},{20,4},{24,8},{28,12},{32,48},... | collective-permute-start | bytes 196616 | tf_op jit(solution)/shard_map/ppermute | solution.py:534
  58.3 5.6 %collective-permute-start.16 = (bf16[2,128,128]{2,1,0:T(8,128)(2,1)S(1)}, bf16[2,128,128]{2,1,0:T(8,128)(2,1)S(1)}, u32[]{:S(2)}, u32[]{:S(2)}) collective-permute-start(bf16[2,128,128]{2,1,0:T(8,128)(2,1)S(1)} %pad_maximum_fusion.8), channel_id=1, source_target_pairs={{0,24},{4,28},{8,16},{12,20},{16,8},{20,12},{24,0},{28,4},{32,56},... | collective-permute-start | bytes 196616 | tf_op jit(solution)/shard_map/ppermute | solution.py:534
  65.7 9.3 %collective-permute-start.17 = (bf16[32,4096]{1,0:T(8,128)(2,1)S(1)}, bf16[32,4096]{1,0:T(8,128)(2,1)S(1)}, u32[]{:S(2)}, u32[]{:S(2)}) collective-permute-start(bf16[32,4096]{1,0:T(8,128)(2,1)S(1)} %get-tuple-element.42), channel_id=1, source_target_pairs={{0,1},{1,0},{2,3},{3,2},{4,5},{5,4},{6,7},{7,6},{8,9},{9,8},{10,11... | collective-permute-start | bytes 786440 | tf_op jit(solution)/shard_map/ppermute | solution.py:569
  67.4 12.1 %collective-permute-start.18 = (bf16[32,4096]{1,0:T(8,128)(2,1)S(1)}, bf16[32,4096]{1,0:T(8,128)(2,1)S(1)}, u32[]{:S(2)}, u32[]{:S(2)}) collective-permute-start(bf16[32,4096]{1,0:T(8,128)(2,1)S(1)} %get-tuple-element.43), channel_id=1, source_target_pairs={{0,3},{1,2},{2,1},{3,0},{4,7},{5,6},{6,5},{7,4},{8,11},{9,10},{10,... | collective-permute-start | bytes 786440 | tf_op jit(solution)/shard_map/ppermute | solution.py:569
  69.6 11.4 %collective-permute-start.19 = (bf16[32,4096]{1,0:T(8,128)(2,1)S(1)}, bf16[32,4096]{1,0:T(8,128)(2,1)S(1)}, u32[]{:S(2)}, u32[]{:S(2)}) collective-permute-start(bf16[32,4096]{1,0:T(8,128)(2,1)S(1)} %get-tuple-element.44), channel_id=1, source_target_pairs={{0,2},{1,3},{2,0},{3,1},{4,6},{5,7},{6,4},{7,5},{8,10},{9,11},{10,... | collective-permute-start | bytes 786440 | tf_op jit(solution)/shard_map/ppermute | solution.py:569

commit v6 on v5

--- a/solution.py
+++ b/solution.py
@@ -10,7 +10,7 @@
 C = 128
 PLANE = 8
 PLANES = 8
-BLK = 2 * C + 16
+BLK = 3 * C + 16
 B = 16
 EPS = 1e-06
 NEG = -1e30
@@ -71,7 +71,7 @@
 
 
 def pack_kernel(q_ref, k_ref, v_ref, decay_ref, beta_ref, *rest):
-    keep, send, keep_q, send_q, gate, raw, sems = rest
+    keep, send, gate, raw, sems = rest
     me = lax.axis_index("seq") % PLANE
     copies = [
         pltpu.make_async_copy(decay_ref, raw.at[0], sems.at[24]),
@@ -79,12 +79,12 @@
     ]
     for d in range(PLANE):
         cols = pl.ds(pl.multiple_of(jnp.bitwise_xor(me, d) * C, C), C)
-        out, out_q = (send, send_q) if d % 2 else (keep, keep_q)
+        out = send if d % 2 else keep
         at = d // 2
         copies += [
             pltpu.make_async_copy(k_ref.at[:, cols], out.at[at, pl.ds(0, C)], sems.at[3 * d]),
             pltpu.make_async_copy(v_ref.at[:, cols], out.at[at, pl.ds(C, C)], sems.at[3 * d + 1]),
-            pltpu.make_async_copy(q_ref.at[:, cols], out_q.at[at], sems.at[3 * d + 2]),
+            pltpu.make_async_copy(q_ref.at[:, cols], out.at[at, pl.ds(2 * C, C)], sems.at[3 * d + 2]),
         ]
     for copy in copies:
         copy.start()
@@ -101,7 +101,7 @@
         head = jnp.bitwise_xor(me, d)
         rows = [gate[i, pl.ds(head, 1), :] for i in range(6)]
         out = send if d % 2 else keep
-        out[d // 2, 2 * C :, :] = jnp.concatenate(rows + [zeros], axis=0).astype(BF16)
+        out[d // 2, 3 * C :, :] = jnp.concatenate(rows + [zeros], axis=0).astype(BF16)
     for copy in copies[2:]:
         copy.wait()
 
@@ -109,12 +109,11 @@
 def pack(q, k, v, decay, beta):
     any_space = pl.BlockSpec(memory_space=pltpu.HBM)
     wide = jax.ShapeDtypeStruct((4, BLK, C), BF16)
-    thin = jax.ShapeDtypeStruct((4, C, C), BF16)
     return pl.pallas_call(
         pack_kernel,
-        out_shape=[wide, wide, thin, thin],
+        out_shape=[wide, wide],
         in_specs=[any_space] * 5,
-        out_specs=[vmem()] * 4,
+        out_specs=[vmem()] * 2,
         scratch_shapes=[
             pltpu.VMEM((6, PLANE, C), F32),
             pltpu.VMEM((2, PLANE, C), F32),
@@ -136,7 +135,7 @@
 
 def gates(kv_ref):
     row, col = iotas()
-    pieces = jnp.concatenate([kv_ref[d, 2 * C :, :] for d in range(PLANE)], axis=0)
+    pieces = jnp.concatenate([kv_ref[d, 3 * C :, :] for d in range(PLANE)], axis=0)
     upper = jnp.where(row <= col, 1.0, 0.0).astype(BF16)
     lower = jnp.where(row >= col, 1.0, 0.0).astype(BF16)
     eye = jnp.where(row == col, 1.0, 0.0).astype(BF16)
@@ -267,10 +266,9 @@
 
 
 def query_kernel(*refs):
-    kv_ref, mix_ref, wu_ref, level_ref, no_ref, queries_ref, before = refs[5:]
+    kv_ref, mix_ref, wu_ref, level_ref, no_ref, before = refs
     me = lax.axis_index("seq") % PLANE
     row, col = iotas()
-    gather_slots(refs[:5], queries_ref)
     before[0] = jnp.concatenate([jnp.where(row == col, 1.0, 0.0), jnp.zeros((C, C), F32)], axis=1)
     before[1] = level_ref[0]
     before[2] = level_ref[1]
@@ -283,7 +281,7 @@
 
     every = range(PLANE)
     found = gates(kv_ref)
-    queries = [queries_ref[d] for d in every]
+    queries = [kv_ref[d, 2 * C : 3 * C, :] for d in every]
     scored = [dot_nt(queries[d], kv_ref[d, 0:C, :]) for d in every]
     r_cols = []
     for q in queries:
@@ -304,20 +302,19 @@
         )
 
 
-def query(slots, kv, mix, wu, level):
+def query(kv, mix, wu, level):
     return pl.pallas_call(
         query_kernel,
         out_shape=jax.ShapeDtypeStruct((PLANE * C, 2 * C), F32),
-        in_specs=[vmem()] * 9,
+        in_specs=[vmem()] * 4,
         out_specs=vmem(),
         scratch_shapes=[
-            pltpu.VMEM((PLANE, C, C), BF16),
             pltpu.VMEM((PLANE, C, 2 * C), F32),
         ],
         compiler_params=params(),
         cost_estimate=cost(1e9, 4e6),
         name="query",
-    )(*slots, kv, mix, wu, level)
+    )(kv, mix, wu, level)
 
 
 def times(a, x):
@@ -325,14 +322,16 @@
     return dot(jnp.concatenate([a, a], axis=1), jnp.concatenate([hi, lo], axis=0))
 
 
-def combine_kernel(own_ref, one_ref, two_ref, before_ref, upto_ref):
+def combine_kernel(own_ref, one_ref, two_ref, before_ref, upto_ref, only_ref):
     a_one, a_own = one_ref[:, :C], own_ref[:, :C]
     reach = dot(a_one, two_ref[:, :C])
     state = one_ref[:, C:].astype(F32) + dot(a_one, two_ref[:, C:])
     before_ref[:, :C] = reach
     before_ref[:, C:] = state
     upto_ref[:, :C] = times(a_own, reach).astype(BF16)
-    upto_ref[:, C:] = (own_ref[:, C:].astype(F32) + times(a_own, state)).astype(BF16)
+    total = (own_ref[:, C:].astype(F32) + times(a_own, state)).astype(BF16)
+    upto_ref[:, C:] = total
+    only_ref[...] = total
 
 
 def combine(own_map, one, two):
@@ -341,16 +340,17 @@
         out_shape=[
             jax.ShapeDtypeStruct((C, 2 * C), F32),
             jax.ShapeDtypeStruct((C, 2 * C), BF16),
+            jax.ShapeDtypeStruct((C, C), BF16),
         ],
         in_specs=[vmem()] * 3,
-        out_specs=[vmem()] * 2,
+        out_specs=[vmem()] * 3,
         compiler_params=params(),
         name="combine",
     )(own_map, one, two)
 
 
 def norm_kernel(no_ref, gain_ref, before_ref, three_ref, six_ref, normed_ref):
-    state = three_ref[:, C:].astype(F32) + dot(three_ref[:, :C], six_ref[:, C:])
+    state = three_ref[:, C:].astype(F32) + dot(three_ref[:, :C], six_ref[...])
     state = before_ref[:, C:] + mm(before_ref[:, :C], state)
     out = mm(no_ref[:, :C], state) + no_ref[:, C:]
     scale = lax.rsqrt(jnp.mean(out * out, axis=1, keepdims=True) + EPS)
@@ -493,41 +493,64 @@
 COLS = 1024
 
 
-def project_kernel(*refs):
-    slots, weight_ref, outs, flat = refs[:5], refs[5], refs[6:10], refs[10]
-    me, mine = lax.axis_index("seq") % PLANE, lax.axis_index("heads")
-    found = [slots[0].at[0], slots[1].at[0]]
-    for dx in range(1, 4):
-        found += [slots[dx + 1].at[0], slots[dx + 1].at[1]]
-    for d in range(PLANE):
-        cols = pl.ds(pl.multiple_of(jnp.bitwise_xor(me, d) * C, C), C)
-        for e in range(4):
-            rows = pl.ds(pl.multiple_of(jnp.bitwise_xor(mine, e) * 32, 32), 32)
-            flat[e * 32 : e * 32 + 32, cols] = found[d][rows, :]
-
-    def one(step, _):
-        cols = pl.ds(pl.multiple_of(step * COLS, COLS), COLS)
-        got = dot(flat[...], weight_ref[:, cols])
+def pair_part(first, second, dx):
+    core, mine = lax.axis_index("seq") % 2, lax.axis_index("heads")
+    rows = [pl.ds(pl.multiple_of(jnp.bitwise_xor(mine, e) * 32, 32), 32) for e in range(4)]
+    one = jnp.concatenate([first[r, :] for r in rows], axis=0)
+    two = jnp.concatenate([second[r, :] for r in rows], axis=0)
+    swapped = core > 0
+    left = jnp.where(swapped, two.astype(F32), one.astype(F32)).astype(BF16)
+    right = jnp.where(swapped, one.astype(F32), two.astype(F32)).astype(BF16)
+    chip = lax.axis_index("seq") % PLANE // 2
+    at = pl.multiple_of(jnp.bitwise_xor(chip, dx) * 2 * C, 2 * C)
+    return jnp.concatenate([left, right], axis=1), pl.ds(at, 2 * C)
+
+
+def early_kernel(keep, came, one, two, weight_ref, acc_ref):
+    parts = [
+        pair_part(keep.at[0], came.at[0], 0),
+        pair_part(two.at[0], two.at[1], 2),
+        pair_part(one.at[0], one.at[1], 1),
+    ]
+    for at in range(0, weight_ref.shape[1], COLS):
+        cols = slice(at, at + COLS)
+        got = dot(parts[0][0], weight_ref[parts[0][1], cols])
+        for part, rows in parts[1:]:
+            got = got + dot(part, weight_ref[rows, cols])
+        acc_ref[:, cols] = got
+
+
+def late_kernel(three, weight_ref, acc_ref, *outs):
+    part, rows = pair_part(three.at[0], three.at[1], 3)
+    for at in range(0, weight_ref.shape[1], COLS):
+        cols = slice(at, at + COLS)
+        got = acc_ref[:, cols] + dot(part, weight_ref[rows, cols])
         for e in range(4):
             outs[e][:, cols] = got[e * 32 : e * 32 + 32].astype(outs[e].dtype)
-        return _
-
-    lax.fori_loop(0, weight_ref.shape[1] // COLS, one, 0)
 
 
 def project(slots, weight):
-    depth, width = weight.shape
-    return pl.pallas_call(
-        project_kernel,
+    width = weight.shape[1]
+    keep, came, one, two, three = slots
+    acc = pl.pallas_call(
+        early_kernel,
+        out_shape=jax.ShapeDtypeStruct((C, width), F32),
+        in_specs=[vmem()] * 5,
+        out_specs=vmem(),
+        compiler_params=params(),
+        cost_estimate=cost(8e8, 8e6),
+        name="early",
+    )(keep, came, one, two, weight)
+    return pl.pallas_call(
+        late_kernel,
         out_shape=[jax.ShapeDtypeStruct((32, width), F32)]
         + [jax.ShapeDtypeStruct((32, width), BF16)] * 3,
-        in_specs=[vmem()] * 6,
+        in_specs=[vmem()] * 3,
         out_specs=[vmem()] * 4,
-        scratch_shapes=[pltpu.VMEM((C, depth), BF16)],
-        compiler_params=params(),
-        cost_estimate=cost(1e9, 9e6),
-        name="project",
-    )(*slots, weight)
+        compiler_params=params(),
+        cost_estimate=cost(3e8, 4e6),
+        name="late",
+    )(three, weight, acc)
 
 
 def swap(block, d):
@@ -549,16 +572,13 @@
 
 
 def local(q_delta, k_delta, v_delta, decay, beta, gain, attn_weight, out_weight):
-    keep, send, keep_q, send_q = pack(q_delta, k_delta, v_delta, decay, beta)
-    slots = exchange(keep, send)
-    slots_q = exchange(keep_q, send_q)
-    kv, mix, wu, ab, level = prep(slots)
+    kv, mix, wu, ab, level = prep(exchange(*pack(q_delta, k_delta, v_delta, decay, beta)))
     one = later_plane(ab, 1)
     two = later_plane(ab, 2)
-    no = query(slots_q, kv, mix, wu, level)
-    before, upto = combine(ab, one, two)
+    no = query(kv, mix, wu, level)
+    before, upto, only = combine(ab, one, two)
     three = later_plane(upto, 3)
-    six = later_plane(upto, 6)
+    six = later_plane(only, 6)
     normed = norm(no, gain[None, :], before, three, six)
     halo = later_plane(normed, 1)
     acc, stat, q2 = own(normed, attn_weight)

time: 82 us -> 82.2 us (level)
  waiting for transfers between devices: 35.7 us -> 43.4 us
  starting transfers between devices: 32.9 us -> 25.9 us
    ppermute x12 -> x8, waiting for transfers between devices: 11 us -> 16.4 us  [swap(): lax.ppermute(block, 'seq', [(s, s ^ d) for s in range(PLANE * PLANES)])]
    ppermute x12 -> x8, starting transfers between devices: 15.5 us -> 10.3 us  [swap(): lax.ppermute(block, 'seq', [(s, s ^ d) for s in range(PLANE * PLANES)])]
    ppermute x5, waiting for transfers between devices: 14 us -> 16.4 us  [later_plane(): return lax.ppermute(block, 'seq', route)]
    ppermute x5, starting transfers between devices: 12.8 us -> 11 us  [later_plane(): return lax.ppermute(block, 'seq', route)]
    pallas_call x2 -> x3, Pallas kernels: 3.3 us -> 2.87 us  [the longest x1 1.43 us: pack(): pl.pallas_call(pack_kernel, out_shape=[wide, wide], in_specs=[any_space]...]
  transfers between devices with their start and end apart: 20 -> 16, of which waited for: 14 -> 14; matrix products, arithmetic and copies ran while one was open for 0% -> 0% of each run, Pallas kernels for 8% -> 4%
where the time goes in v6:
time: 82.2 us; the launch traced here: 82 us
  waiting for transfers between devices  43.4 us (53%)
  starting transfers between devices  25.9 us (32%)
  Pallas kernels  11.5 us (14%)
  other arithmetic  0.91 us (1%)
    ppermute x8, waiting for transfers between devices, swap(): lax.ppermute(block, 'seq', [(s, s ^ d) for s in range(PLANE * PLANES)])  16.4 us
    ppermute x5, waiting for transfers between devices, later_plane(): return lax.ppermute(block, 'seq', route)  16.4 us
    ppermute x5, starting transfers between devices, later_plane(): return lax.ppermute(block, 'seq', route)  11 us
    ppermute x3, waiting for transfers between devices, local(): moved[d] = lax.ppermute(sums[d], 'heads', [(s, s ^ d) for s in range(4)])  10.7 us
    ppermute x8, starting transfers between devices, swap(): lax.ppermute(block, 'seq', [(s, s ^ d) for s in range(PLANE * PLANES)])  10.3 us
    ppermute x3, starting transfers between devices, local(): moved[d] = lax.ppermute(sums[d], 'heads', [(s, s ^ d) for s in range(4)])  4.56 us
    pallas_call x1, Pallas kernels, prep(): pl.pallas_call(prep_kernel, out_shape=[jax.ShapeDtypeStruct((PLANE, BLK,...  3.51 us
  transfers between devices with their start and end apart: 16, of which 14 were waited for; matrix products, arithmetic and copies ran while one was open for 0% of the time, Pallas kernels for 4%

profile of v6, /device:TPU:128, one launch (start us, length us, event | category | flops | bytes accessed | tf_op | source)
XLA Modules:
  0.0 82.0 jit_solution(9524246634068740563)
XLA Ops:
  0.0 0.0 copy-start
  0.0 0.0 copy-start.1
  0.0 1.4 %pack.1 = (bf16[4,400,128]{2,1,0:T(8,128)(2,1)S(1)}, bf16[4,400,128]{2,1,0:T(8,128)(2,1)S(1)}) custom-call(bf16[128,1024]{1,0:T(8,128)(2,1)} %q_ref.1, bf16[128,1024]{1,0:T(8,128)(2,1)} %k_ref.1, bf16[128,1024]{1,0:T(8,128)(2,1)} %v_ref.1, f32[8,128]{1,0:T(8,128)} %decay_ref.1, f32[8,128]{1,0:T(8,128)} %beta_ref.1), custom_call_target="tpu_custom_call" | custom-call | tf_op jit(solution)/shard_map/pack/pallas_call | solution.py:112
  1.4 0.1 collective-permute-start
  1.6 1.7 %collective-permute-done.refs_1_ = bf16[4,400,128]{2,1,0:T(8,128)(2,1)S(1)} collective-permute-done((bf16[4,400,128]{2,1,0:T(8,128)(2,1)S(1)}, bf16[4,400,128]{2,1,0:T(8,128)(2,1)S(1)}, u32[]{:S(2)}, u32[]{:S(2)}) %collective-permute-start) | collective-permute-done | bytes 409632 | tf_op jit(solution)/shard_map/ppermute | solution.py:557
  3.3 1.6 %collective-permute-start.1 = (bf16[2,400,128]{2,1,0:T(8,128)(2,1)S(1)}, bf16[2,400,128]{2,1,0:T(8,128)(2,1)S(1)}, u32[]{:S(2)}, u32[]{:S(2)}) collective-permute-start(bf16[2,400,128]{2,1,0:T(8,128)(2,1)S(1)} %pad_maximum_fusion), channel_id=1, source_target_pairs={{0,8},{4,12},{8,0},{12,4},{16,24},{20,28},{24,16},{28,20},{32,40},... | collective-permute-start | bytes 614408 | tf_op jit(solution)/shard_map/ppermute | solution.py:557
  4.9 2.8 %collective-permute-start.2 = (bf16[2,400,128]{2,1,0:T(8,128)(2,1)S(1)}, bf16[2,400,128]{2,1,0:T(8,128)(2,1)S(1)}, u32[]{:S(2)}, u32[]{:S(2)}) collective-permute-start(bf16[2,400,128]{2,1,0:T(8,128)(2,1)S(1)} %pad_maximum_fusion.1), channel_id=1, source_target_pairs={{0,16},{4,20},{8,24},{12,28},{16,0},{20,4},{24,8},{28,12},{32,48},... | collective-permute-start | bytes 614408 | tf_op jit(solution)/shard_map/ppermute | solution.py:557
  7.8 0.6 collective-permute-start.3
  8.3 3.0 %collective-permute-done.1.refs_2_ = bf16[2,400,128]{2,1,0:T(8,128)(2,1)S(1)} collective-permute-done((bf16[2,400,128]{2,1,0:T(8,128)(2,1)S(1)}, bf16[2,400,128]{2,1,0:T(8,128)(2,1)S(1)}, u32[]{:S(2)}, u32[]{:S(2)}) %collective-permute-start.1) | collective-permute-done | bytes 204832 | tf_op jit(solution)/shard_map/ppermute | solution.py:557
  11.3 5.9 %collective-permute-done.2.refs_3_ = bf16[2,400,128]{2,1,0:T(8,128)(2,1)S(1)} collective-permute-done((bf16[2,400,128]{2,1,0:T(8,128)(2,1)S(1)}, bf16[2,400,128]{2,1,0:T(8,128)(2,1)S(1)}, u32[]{:S(2)}, u32[]{:S(2)}) %collective-permute-start.2) | collective-permute-done | bytes 204832 | tf_op jit(solution)/shard_map/ppermute | solution.py:557
  17.2 2.8 %collective-permute-done.3.refs_4_ = bf16[2,400,128]{2,1,0:T(8,128)(2,1)S(1)} collective-permute-done((bf16[2,400,128]{2,1,0:T(8,128)(2,1)S(1)}, bf16[2,400,128]{2,1,0:T(8,128)(2,1)S(1)}, u32[]{:S(2)}, u32[]{:S(2)}) %collective-permute-start.3) | collective-permute-done | bytes 204832 | tf_op jit(solution)/shard_map/ppermute | solution.py:557
  20.0 0.0 slice-start
  20.0 3.5 %prep.1 = (bf16[8,400,128]{2,1,0:T(8,128)(2,1)S(1)}, f32[8,128,128]{2,1,0:T(8,128)S(1)}, f32[8,128,256]{2,1,0:T(8,128)S(1)}, bf16[128,256]{1,0:T(8,128)(2,1)S(1)}, f32[7,128,256]{2,1,0:T(8,128)S(1)}) custom-call(bf16[4,400,128]{2,1,0:T(8,128)(2,1)S(1)} %get-tuple-element.24.refs_0_, bf16[4,400,128]{2,1,0:T(8,128)(2,1)S(1)} %collective-permute-done.refs_1_, ...), custom_call_target="tpu_custom_call" | custom-call | flops 2000000000 | bytes 4000000 | tf_op jit(solution)/shard_map/prep/pallas_call | solution.py:248
  23.5 3.4 %collective-permute-start.5 = (bf16[128,256]{1,0:T(8,128)(2,1)S(1)}, bf16[128,256]{1,0:T(8,128)(2,1)S(1)}, u32[]{:S(2)}, u32[]{:S(2)}) collective-permute-start(bf16[128,256]{1,0:T(8,128)(2,1)S(1)} %get-tuple-element.30.own_ref), channel_id=1, source_target_pairs={{0,64},{4,68},{8,72},{12,76},{16,80},{20,84},{24,88},{28,92},{32,9... | collective-permute-start | bytes 196616 | tf_op jit(solution)/shard_map/ppermute | solution.py:571
  26.9 2.9 %collective-permute-start.4 = (bf16[128,256]{1,0:T(8,128)(2,1)S(1)}, bf16[128,256]{1,0:T(8,128)(2,1)S(1)}, u32[]{:S(2)}, u32[]{:S(2)}) collective-permute-start(bf16[128,256]{1,0:T(8,128)(2,1)S(1)} %get-tuple-element.30.own_ref), channel_id=1, source_target_pairs={{0,32},{4,36},{8,40},{12,44},{16,48},{20,52},{24,56},{28,60},{32,6... | collective-permute-start | bytes 196616 | tf_op jit(solution)/shard_map/ppermute | solution.py:571
  29.9 2.0 %collective-permute-done.5.two_ref = bf16[128,256]{1,0:T(8,128)(2,1)S(1)} collective-permute-done((bf16[128,256]{1,0:T(8,128)(2,1)S(1)}, bf16[128,256]{1,0:T(8,128)(2,1)S(1)}, u32[]{:S(2)}, u32[]{:S(2)}) %collective-permute-start.5) | collective-permute-done | bytes 65568 | tf_op jit(solution)/shard_map/ppermute | solution.py:571
  31.8 2.5 %collective-permute-done.4.one_ref = bf16[128,256]{1,0:T(8,128)(2,1)S(1)} collective-permute-done((bf16[128,256]{1,0:T(8,128)(2,1)S(1)}, bf16[128,256]{1,0:T(8,128)(2,1)S(1)}, u32[]{:S(2)}, u32[]{:S(2)}) %collective-permute-start.4) | collective-permute-done | bytes 65568 | tf_op jit(solution)/shard_map/ppermute | solution.py:571
  34.3 0.3 combine.1
  34.6 0.7 collective-permute-start.7
  35.3 2.1 %collective-permute-start.6 = (bf16[128,256]{1,0:T(8,128)(2,1)S(1)}, bf16[128,256]{1,0:T(8,128)(2,1)S(1)}, u32[]{:S(2)}, u32[]{:S(2)}) collective-permute-start(bf16[128,256]{1,0:T(8,128)(2,1)S(1)} %get-tuple-element.32), channel_id=1, source_target_pairs={{0,96},{4,100},{8,104},{12,108},{16,112},{20,116},{24,120},{28,124... | collective-permute-start | bytes 196616 | tf_op jit(solution)/shard_map/ppermute | solution.py:571
  37.4 0.0 slice-start.1
  37.5 1.3 %query.1.no_ref = f32[1024,256]{1,0:T(8,128)S(1)} custom-call(bf16[8,400,128]{2,1,0:T(8,128)(2,1)S(1)} %get-tuple-element.26.refs_0_, f32[8,128,128]{2,1,0:T(8,128)S(1)} %get-tuple-element.27.refs_1_, f32[8,128,256]{2,1,0:T(8,128)S(1)} %get-tuple-element.28.refs_2_, f32[7,128,256]{2,1,0:T(8,128)S(1)} %get-tuple-element.29.refs_3_), custom_call_target="tpu_custom_call" | custom-call | flops 1000000000 | bytes 4000000 | tf_op jit(solution)/shard_map/query/pallas_call | solution.py:306
  38.8 0.0 collective-permute-done.7.six_ref
  38.8 5.7 %collective-permute-done.6.three_ref = bf16[128,256]{1,0:T(8,128)(2,1)S(1)} collective-permute-done((bf16[128,256]{1,0:T(8,128)(2,1)S(1)}, bf16[128,256]{1,0:T(8,128)(2,1)S(1)}, u32[]{:S(2)}, u32[]{:S(2)}) %collective-permute-start.6) | collective-permute-done | bytes 65568 | tf_op jit(solution)/shard_map/ppermute | solution.py:571
  44.5 0.0 copy-done
  44.5 0.7 norm.1.normed_ref
  45.2 1.9 %collective-permute-start.8 = (bf16[1024,128]{1,0:T(8,128)(2,1)S(1)}, bf16[1024,128]{1,0:T(8,128)(2,1)S(1)}, u32[]{:S(2)}, u32[]{:S(2)}) collective-permute-start(bf16[1024,128]{1,0:T(8,128)(2,1)S(1)} %norm.1.normed_ref), channel_id=1, source_target_pairs={{0,32},{4,36},{8,40},{12,44},{16,48},{20,52},{24,56},{28,60},{32,6... | collective-permute-start | bytes 786440 | tf_op jit(solution)/shard_map/ppermute | solution.py:571
  47.1 0.0 copy-done.1
  47.1 1.3 %own.1 = (f32[1024,128]{1,0:T(8,128)S(1)}, f32[2,1024,128]{2,1,0:T(8,128)S(1)}, bf16[1024,128]{1,0:T(8,128)(2,1)S(1)}) custom-call(bf16[1024,128]{1,0:T(8,128)(2,1)S(1)} %norm.1.normed_ref, bf16[8,128,384]{2,1,0:T(8,128)(2,1)S(1)} %copy-done.1), custom_call_target="tpu_custom_call" | custom-call | flops 1000000000 | bytes 3000000 | tf_op jit(solution)/shard_map/own/pallas_call | solution.py:430
  48.4 6.2 %collective-permute-done.8.halo_ref = bf16[1024,128]{1,0:T(8,128)(2,1)S(1)} collective-permute-done((bf16[1024,128]{1,0:T(8,128)(2,1)S(1)}, bf16[1024,128]{1,0:T(8,128)(2,1)S(1)}, u32[]{:S(2)}, u32[]{:S(2)}) %collective-permute-start.8) | collective-permute-done | bytes 262176 | tf_op jit(solution)/shard_map/ppermute | solution.py:571
  54.7 1.5 %halo.1 = (bf16[4,128,128]{2,1,0:T(8,128)(2,1)S(1)}, bf16[4,128,128]{2,1,0:T(8,128)(2,1)S(1)}) custom-call(bf16[1024,128]{1,0:T(8,128)(2,1)S(1)} %collective-permute-done.8.halo_ref, bf16[8,128,384]{2,1,0:T(8,128)(2,1)S(1)} %copy-done.1, f32[1024,128]{1,0:T(8,128)S(1)} %get-tuple-element.34.acc_ref, f32[2,1024,128]{2,1,0:T(8,128)S(1)} %get-tuple-element.35.stat_ref, ...), custom_call_target="tpu_custom_call" | custom-call | flops 1000000000 | bytes 3000000 | tf_op jit(solution)/shard_map/halo/pallas_call | solution.py:481
  56.2 0.1 collective-permute-start.9
  56.3 1.3 %collective-permute-done.9.came = bf16[4,128,128]{2,1,0:T(8,128)(2,1)S(1)} collective-permute-done((bf16[4,128,128]{2,1,0:T(8,128)(2,1)S(1)}, bf16[4,128,128]{2,1,0:T(8,128)(2,1)S(1)}, u32[]{:S(2)}, u32[]{:S(2)}) %collective-permute-start.9) | collective-permute-done | bytes 131104 | tf_op jit(solution)/shard_map/ppermute | solution.py:557
  57.6 0.1 collective-permute-start.11
  57.7 2.2 %collective-permute-start.12 = (bf16[2,128,128]{2,1,0:T(8,128)(2,1)S(1)}, bf16[2,128,128]{2,1,0:T(8,128)(2,1)S(1)}, u32[]{:S(2)}, u32[]{:S(2)}) collective-permute-start(bf16[2,128,128]{2,1,0:T(8,128)(2,1)S(1)} %pad_maximum_fusion.5), channel_id=1, source_target_pairs={{0,16},{4,20},{8,24},{12,28},{16,0},{20,4},{24,8},{28,12},{32,48},... | collective-permute-start | bytes 196616 | tf_op jit(solution)/shard_map/ppermute | solution.py:557
  59.9 2.8 %collective-permute-start.10 = (bf16[2,128,128]{2,1,0:T(8,128)(2,1)S(1)}, bf16[2,128,128]{2,1,0:T(8,128)(2,1)S(1)}, u32[]{:S(2)}, u32[]{:S(2)}) collective-permute-start(bf16[2,128,128]{2,1,0:T(8,128)(2,1)S(1)} %pad_maximum_fusion.3), channel_id=1, source_target_pairs={{0,24},{4,28},{8,16},{12,20},{16,8},{20,12},{24,0},{28,4},{32,56},... | collective-permute-start | bytes 196616 | tf_op jit(solution)/shard_map/ppermute | solution.py:557
  62.8 0.0 collective-permute-done.11.one
  62.8 1.0 %collective-permute-done.12.two = bf16[2,128,128]{2,1,0:T(8,128)(2,1)S(1)} collective-permute-done((bf16[2,128,128]{2,1,0:T(8,128)(2,1)S(1)}, bf16[2,128,128]{2,1,0:T(8,128)(2,1)S(1)}, u32[]{:S(2)}, u32[]{:S(2)}) %collective-permute-start.12) | collective-permute-done | bytes 65568 | tf_op jit(solution)/shard_map/ppermute | solution.py:557
  63.8 0.0 slice-done
  63.8 0.0 slice-done.1
  63.8 1.0 %early.1.acc_ref = f32[128,4096]{1,0:T(8,128)S(1)} custom-call(bf16[4,128,128]{2,1,0:T(8,128)(2,1)S(1)} %get-tuple-element.37.keep, bf16[4,128,128]{2,1,0:T(8,128)(2,1)S(1)} %collective-permute-done.9.came, bf16[2,128,128]{2,1,0:T(8,128)(2,1)S(1)} %collective-permute-done.11.one, bf16[2,128,128]{2,1,0:T(8,128)(2,1)S(1)} %collective-permute-done.12.two, ...), custom_call_target="tpu_custom_call" | custom-call | flops 800000000 | bytes 8000000 | tf_op jit(solution)/shard_map/early/pallas_call | solution.py:535
  64.8 0.7 collective-permute-done.10.three
  65.5 0.4 late.1
  65.9 1.7 %collective-permute-start.13 = (bf16[32,4096]{1,0:T(8,128)(2,1)S(1)}, bf16[32,4096]{1,0:T(8,128)(2,1)S(1)}, u32[]{:S(2)}, u32[]{:S(2)}) collective-permute-start(bf16[32,4096]{1,0:T(8,128)(2,1)S(1)} %get-tuple-element.40), channel_id=1, source_target_pairs={{0,1},{1,0},{2,3},{3,2},{4,5},{5,4},{6,7},{7,6},{8,9},{9,8},{10,11... | collective-permute-start | bytes 786440 | tf_op jit(solution)/shard_map/ppermute | solution.py:589
  67.6 2.2 %collective-permute-start.14 = (bf16[32,4096]{1,0:T(8,128)(2,1)S(1)}, bf16[32,4096]{1,0:T(8,128)(2,1)S(1)}, u32[]{:S(2)}, u32[]{:S(2)}) collective-permute-start(bf16[32,4096]{1,0:T(8,128)(2,1)S(1)} %get-tuple-element.41), channel_id=1, source_target_pairs={{0,3},{1,2},{2,1},{3,0},{4,7},{5,6},{6,5},{7,4},{8,11},{9,10},{10,... | collective-permute-start | bytes 786440 | tf_op jit(solution)/shard_map/ppermute | solution.py:589
  69.8 0.7 collective-permute-start.15
  70.5 4.8 %collective-permute-done.13 = bf16[32,4096]{1,0:T(8,128)(2,1)S(1)} collective-permute-done((bf16[32,4096]{1,0:T(8,128)(2,1)S(1)}, bf16[32,4096]{1,0:T(8,128)(2,1)S(1)}, u32[]{:S(2)}, u32[]{:S(2)}) %collective-permute-start.13) | collective-permute-done | bytes 262176 | tf_op jit(solution)/shard_map/ppermute | solution.py:589
  75.3 4.4 %collective-permute-done.14 = bf16[32,4096]{1,0:T(8,128)(2,1)S(1)} collective-permute-done((bf16[32,4096]{1,0:T(8,128)(2,1)S(1)}, bf16[32,4096]{1,0:T(8,128)(2,1)S(1)}, u32[]{:S(2)}, u32[]{:S(2)}) %collective-permute-start.14) | collective-permute-done | bytes 262176 | tf_op jit(solution)/shard_map/ppermute | solution.py:589
  79.7 1.5 %collective-permute-done.15 = bf16[32,4096]{1,0:T(8,128)(2,1)S(1)} collective-permute-done((bf16[32,4096]{1,0:T(8,128)(2,1)S(1)}, bf16[32,4096]{1,0:T(8,128)(2,1)S(1)}, u32[]{:S(2)}, u32[]{:S(2)}) %collective-permute-start.15) | collective-permute-done | bytes 262176 | tf_op jit(solution)/shard_map/ppermute | solution.py:589
  81.2 0.8 add_convert_fusion
  (11 shorter events, 0.1 us)
Async XLA Ops:
  0.0 44.5 %copy-start = (f32[128]{0:T(128)S(1)}, f32[128]{0:T(128)}, u32[]{:S(2)}) copy-start(f32[128]{0:T(128)} %param.13) | copy-start | bytes 1540
  0.0 47.1 %copy-start.1 = (bf16[8,128,384]{2,1,0:T(8,128)(2,1)S(1)}, bf16[8,128,384]{2,1,0:T(8,128)(2,1)}, u32[]{:S(2)}) copy-start(bf16[8,128,384]{2,1,0:T(8,128)(2,1)} %weight_ref.5) | copy-start | bytes 2359300
  1.4 1.8 %collective-permute-start = (bf16[4,400,128]{2,1,0:T(8,128)(2,1)S(1)}, bf16[4,400,128]{2,1,0:T(8,128)(2,1)S(1)}, u32[]{:S(2)}, u32[]{:S(2)}) collective-permute-start(bf16[4,400,128]{2,1,0:T(8,128)(2,1)S(1)} %get-tuple-element.25), channel_id=1, source_target_pairs={{0,4},{4,0},{8,12},{12,8},{16,20},{20,16},{24,28},{28,24},{32,36},... | collective-permute-start | bytes 1228808 | tf_op jit(solution)/shard_map/ppermute | solution.py:557
  3.3 8.0 %collective-permute-start.1 = (bf16[2,400,128]{2,1,0:T(8,128)(2,1)S(1)}, bf16[2,400,128]{2,1,0:T(8,128)(2,1)S(1)}, u32[]{:S(2)}, u32[]{:S(2)}) collective-permute-start(bf16[2,400,128]{2,1,0:T(8,128)(2,1)S(1)} %pad_maximum_fusion), channel_id=1, source_target_pairs={{0,8},{4,12},{8,0},{12,4},{16,24},{20,28},{24,16},{28,20},{32,40},... | collective-permute-start | bytes 614408 | tf_op jit(solution)/shard_map/ppermute | solution.py:557
  4.9 12.3 %collective-permute-start.2 = (bf16[2,400,128]{2,1,0:T(8,128)(2,1)S(1)}, bf16[2,400,128]{2,1,0:T(8,128)(2,1)S(1)}, u32[]{:S(2)}, u32[]{:S(2)}) collective-permute-start(bf16[2,400,128]{2,1,0:T(8,128)(2,1)S(1)} %pad_maximum_fusion.1), channel_id=1, source_target_pairs={{0,16},{4,20},{8,24},{12,28},{16,0},{20,4},{24,8},{28,12},{32,48},... | collective-permute-start | bytes 614408 | tf_op jit(solution)/shard_map/ppermute | solution.py:557
  7.8 12.2 %collective-permute-start.3 = (bf16[2,400,128]{2,1,0:T(8,128)(2,1)S(1)}, bf16[2,400,128]{2,1,0:T(8,128)(2,1)S(1)}, u32[]{:S(2)}, u32[]{:S(2)}) collective-permute-start(bf16[2,400,128]{2,1,0:T(8,128)(2,1)S(1)} %pad_maximum_fusion.2), channel_id=1, source_target_pairs={{0,24},{4,28},{8,16},{12,20},{16,8},{20,12},{24,0},{28,4},{32,56},... | collective-permute-start | bytes 614408 | tf_op jit(solution)/shard_map/ppermute | solution.py:557
  20.0 43.8 %slice-start = ((s8[8388608]{0:T(1024)(128)(4,1)}), s8[4194304]{0:T(1024)(128)(4,1)S(1)}, s32[]{:S(2)}) async-start(s8[8388608]{0:T(1024)(128)(4,1)} %bitcast.1), calls=%async_computation | async-start | bytes 8388608
  23.5 8.3 %collective-permute-start.5 = (bf16[128,256]{1,0:T(8,128)(2,1)S(1)}, bf16[128,256]{1,0:T(8,128)(2,1)S(1)}, u32[]{:S(2)}, u32[]{:S(2)}) collective-permute-start(bf16[128,256]{1,0:T(8,128)(2,1)S(1)} %get-tuple-element.30.own_ref), channel_id=1, source_target_pairs={{0,64},{4,68},{8,72},{12,76},{16,80},{20,84},{24,88},{28,92},{32,9... | collective-permute-start | bytes 196616 | tf_op jit(solution)/shard_map/ppermute | solution.py:571
  26.9 7.4 %collective-permute-start.4 = (bf16[128,256]{1,0:T(8,128)(2,1)S(1)}, bf16[128,256]{1,0:T(8,128)(2,1)S(1)}, u32[]{:S(2)}, u32[]{:S(2)}) collective-permute-start(bf16[128,256]{1,0:T(8,128)(2,1)S(1)} %get-tuple-element.30.own_ref), channel_id=1, source_target_pairs={{0,32},{4,36},{8,40},{12,44},{16,48},{20,52},{24,56},{28,60},{32,6... | collective-permute-start | bytes 196616 | tf_op jit(solution)/shard_map/ppermute | solution.py:571
  34.6 4.2 %collective-permute-start.7 = (bf16[128,128]{1,0:T(8,128)(2,1)S(1)}, bf16[128,128]{1,0:T(8,128)(2,1)S(1)}, u32[]{:S(2)}, u32[]{:S(2)}) collective-permute-start(bf16[128,128]{1,0:T(8,128)(2,1)S(1)} %get-tuple-element.33), channel_id=1, source_target_pairs={{0,192},{4,196},{8,200},{12,204},{16,208},{20,212},{24,216},{28,22... | collective-permute-start | bytes 98312 | tf_op jit(solution)/shard_map/ppermute | solution.py:571
  35.3 9.2 %collective-permute-start.6 = (bf16[128,256]{1,0:T(8,128)(2,1)S(1)}, bf16[128,256]{1,0:T(8,128)(2,1)S(1)}, u32[]{:S(2)}, u32[]{:S(2)}) collective-permute-start(bf16[128,256]{1,0:T(8,128)(2,1)S(1)} %get-tuple-element.32), channel_id=1, source_target_pairs={{0,96},{4,100},{8,104},{12,108},{16,112},{20,116},{24,120},{28,124... | collective-permute-start | bytes 196616 | tf_op jit(solution)/shard_map/ppermute | solution.py:571
  37.4 26.4 %slice-start.1 = ((s8[8388608]{0:T(1024)(128)(4,1)}), s8[4194304]{0:T(1024)(128)(4,1)S(1)}, s32[]{:S(2)}) async-start(s8[8388608]{0:T(1024)(128)(4,1)} %bitcast.1), calls=%async_computation.1 | async-start | bytes 8388608
  45.2 9.5 %collective-permute-start.8 = (bf16[1024,128]{1,0:T(8,128)(2,1)S(1)}, bf16[1024,128]{1,0:T(8,128)(2,1)S(1)}, u32[]{:S(2)}, u32[]{:S(2)}) collective-permute-start(bf16[1024,128]{1,0:T(8,128)(2,1)S(1)} %norm.1.normed_ref), channel_id=1, source_target_pairs={{0,32},{4,36},{8,40},{12,44},{16,48},{20,52},{24,56},{28,60},{32,6... | collective-permute-start | bytes 786440 | tf_op jit(solution)/shard_map/ppermute | solution.py:571
  56.2 1.4 %collective-permute-start.9 = (bf16[4,128,128]{2,1,0:T(8,128)(2,1)S(1)}, bf16[4,128,128]{2,1,0:T(8,128)(2,1)S(1)}, u32[]{:S(2)}, u32[]{:S(2)}) collective-permute-start(bf16[4,128,128]{2,1,0:T(8,128)(2,1)S(1)} %get-tuple-element.38), channel_id=1, source_target_pairs={{0,4},{4,0},{8,12},{12,8},{16,20},{20,16},{24,28},{28,24},{32,36},... | collective-permute-start | bytes 393224 | tf_op jit(solution)/shard_map/ppermute | solution.py:557
  57.6 5.2 %collective-permute-start.11 = (bf16[2,128,128]{2,1,0:T(8,128)(2,1)S(1)}, bf16[2,128,128]{2,1,0:T(8,128)(2,1)S(1)}, u32[]{:S(2)}, u32[]{:S(2)}) collective-permute-start(bf16[2,128,128]{2,1,0:T(8,128)(2,1)S(1)} %pad_maximum_fusion.4), channel_id=1, source_target_pairs={{0,8},{4,12},{8,0},{12,4},{16,24},{20,28},{24,16},{28,20},{32,40},... | collective-permute-start | bytes 196616 | tf_op jit(solution)/shard_map/ppermute | solution.py:557
  57.7 6.1 %collective-permute-start.12 = (bf16[2,128,128]{2,1,0:T(8,128)(2,1)S(1)}, bf16[2,128,128]{2,1,0:T(8,128)(2,1)S(1)}, u32[]{:S(2)}, u32[]{:S(2)}) collective-permute-start(bf16[2,128,128]{2,1,0:T(8,128)(2,1)S(1)} %pad_maximum_fusion.5), channel_id=1, source_target_pairs={{0,16},{4,20},{8,24},{12,28},{16,0},{20,4},{24,8},{28,12},{32,48},... | collective-permute-start | bytes 196616 | tf_op jit(solution)/shard_map/ppermute | solution.py:557
  59.9 5.6 %collective-permute-start.10 = (bf16[2,128,128]{2,1,0:T(8,128)(2,1)S(1)}, bf16[2,128,128]{2,1,0:T(8,128)(2,1)S(1)}, u32[]{:S(2)}, u32[]{:S(2)}) collective-permute-start(bf16[2,128,128]{2,1,0:T(8,128)(2,1)S(1)} %pad_maximum_fusion.3), channel_id=1, source_target_pairs={{0,24},{4,28},{8,16},{12,20},{16,8},{20,12},{24,0},{28,4},{32,56},... | collective-permute-start | bytes 196616 | tf_op jit(solution)/shard_map/ppermute | solution.py:557
  65.9 9.3 %collective-permute-start.13 = (bf16[32,4096]{1,0:T(8,128)(2,1)S(1)}, bf16[32,4096]{1,0:T(8,128)(2,1)S(1)}, u32[]{:S(2)}, u32[]{:S(2)}) collective-permute-start(bf16[32,4096]{1,0:T(8,128)(2,1)S(1)} %get-tuple-element.40), channel_id=1, source_target_pairs={{0,1},{1,0},{2,3},{3,2},{4,5},{5,4},{6,7},{7,6},{8,9},{9,8},{10,11... | collective-permute-start | bytes 786440 | tf_op jit(solution)/shard_map/ppermute | solution.py:589
  67.6 12.1 %collective-permute-start.14 = (bf16[32,4096]{1,0:T(8,128)(2,1)S(1)}, bf16[32,4096]{1,0:T(8,128)(2,1)S(1)}, u32[]{:S(2)}, u32[]{:S(2)}) collective-permute-start(bf16[32,4096]{1,0:T(8,128)(2,1)S(1)} %get-tuple-element.41), channel_id=1, source_target_pairs={{0,3},{1,2},{2,1},{3,0},{4,7},{5,6},{6,5},{7,4},{8,11},{9,10},{10,... | collective-permute-start | bytes 786440 | tf_op jit(solution)/shard_map/ppermute | solution.py:589
  69.8 11.4 %collective-permute-start.15 = (bf16[32,4096]{1,0:T(8,128)(2,1)S(1)}, bf16[32,4096]{1,0:T(8,128)(2,1)S(1)}, u32[]{:S(2)}, u32[]{:S(2)}) collective-permute-start(bf16[32,4096]{1,0:T(8,128)(2,1)S(1)} %get-tuple-element.42), channel_id=1, source_target_pairs={{0,2},{1,3},{2,0},{3,1},{4,6},{5,7},{6,4},{7,5},{8,10},{9,11},{10,... | collective-permute-start | bytes 786440 | tf_op jit(solution)/shard_map/ppermute | solution.py:589

commit v7 on v6

--- a/solution.py
+++ b/solution.py
@@ -10,7 +10,7 @@
 C = 128
 PLANE = 8
 PLANES = 8
-BLK = 3 * C + 16
+KROWS = C + 16
 B = 16
 EPS = 1e-06
 NEG = -1e30
@@ -71,7 +71,7 @@
 
 
 def pack_kernel(q_ref, k_ref, v_ref, decay_ref, beta_ref, *rest):
-    keep, send, gate, raw, sems = rest
+    keep_k, send_k, keep, send, gate, raw, sems = rest
     me = lax.axis_index("seq") % PLANE
     copies = [
         pltpu.make_async_copy(decay_ref, raw.at[0], sems.at[24]),
@@ -79,12 +79,12 @@
     ]
     for d in range(PLANE):
         cols = pl.ds(pl.multiple_of(jnp.bitwise_xor(me, d) * C, C), C)
-        out = send if d % 2 else keep
+        out_k, out = (send_k, send) if d % 2 else (keep_k, keep)
         at = d // 2
         copies += [
-            pltpu.make_async_copy(k_ref.at[:, cols], out.at[at, pl.ds(0, C)], sems.at[3 * d]),
-            pltpu.make_async_copy(v_ref.at[:, cols], out.at[at, pl.ds(C, C)], sems.at[3 * d + 1]),
-            pltpu.make_async_copy(q_ref.at[:, cols], out.at[at, pl.ds(2 * C, C)], sems.at[3 * d + 2]),
+            pltpu.make_async_copy(k_ref.at[:, cols], out_k.at[at, pl.ds(0, C)], sems.at[3 * d]),
+            pltpu.make_async_copy(v_ref.at[:, cols], out.at[at, pl.ds(0, C)], sems.at[3 * d + 1]),
+            pltpu.make_async_copy(q_ref.at[:, cols], out.at[at, pl.ds(C, C)], sems.at[3 * d + 2]),
         ]
     for copy in copies:
         copy.start()
@@ -100,20 +100,21 @@
     for d in range(PLANE):
         head = jnp.bitwise_xor(me, d)
         rows = [gate[i, pl.ds(head, 1), :] for i in range(6)]
-        out = send if d % 2 else keep
-        out[d // 2, 3 * C :, :] = jnp.concatenate(rows + [zeros], axis=0).astype(BF16)
+        out = send_k if d % 2 else keep_k
+        out[d // 2, C:, :] = jnp.concatenate(rows + [zeros], axis=0).astype(BF16)
     for copy in copies[2:]:
         copy.wait()
 
 
 def pack(q, k, v, decay, beta):
     any_space = pl.BlockSpec(memory_space=pltpu.HBM)
-    wide = jax.ShapeDtypeStruct((4, BLK, C), BF16)
+    first = jax.ShapeDtypeStruct((4, KROWS, C), BF16)
+    wide = jax.ShapeDtypeStruct((4, 2 * C, C), BF16)
     return pl.pallas_call(
         pack_kernel,
-        out_shape=[wide, wide],
+        out_shape=[first, first, wide, wide],
         in_specs=[any_space] * 5,
-        out_specs=[vmem()] * 2,
+        out_specs=[vmem()] * 4,
         scratch_shapes=[
             pltpu.VMEM((6, PLANE, C), F32),
             pltpu.VMEM((2, PLANE, C), F32),
@@ -133,9 +134,9 @@
         out_ref[2 * dx + 1] = refs[dx + 1][1]
 
 
-def gates(kv_ref):
+def gates(k_ref):
     row, col = iotas()
-    pieces = jnp.concatenate([kv_ref[d, 3 * C :, :] for d in range(PLANE)], axis=0)
+    pieces = jnp.concatenate([k_ref[d, C:, :] for d in range(PLANE)], axis=0)
     upper = jnp.where(row <= col, 1.0, 0.0).astype(BF16)
     lower = jnp.where(row >= col, 1.0, 0.0).astype(BF16)
     eye = jnp.where(row == col, 1.0, 0.0).astype(BF16)
@@ -180,17 +181,17 @@
     return jnp.concatenate([both[:, :C], both[:, C:] + later[:, C:]], axis=1)
 
 
-def prep_kernel(*refs):
-    kv_ref, mix_ref, wu_ref, ab_ref, level_ref = refs[5:10]
-    maps = refs[10]
+def key_kernel(*refs):
+    k_ref, mix_ref, inverse_ref, w_ref, tail_ref, reach_ref = refs[5:11]
+    maps = refs[11]
     me = lax.axis_index("seq") % PLANE
     row, col = iotas()
-    gather_slots(refs[:5], kv_ref)
+    gather_slots(refs[:5], k_ref)
     every = range(PLANE)
     blocks = (row // B) == (col // B)
     apart = jnp.bitwise_xor(row, col)
-    found = gates(kv_ref)
-    keys = [kv_ref[d, 0:C, :] for d in every]
+    found = gates(k_ref)
+    keys = [k_ref[d, 0:C, :] for d in every]
     grams = [dot_nt(k, k) for k in keys]
     diags = [jnp.where(row == col, g, 0.0) for g in grams]
     r_cols = [lax.rsqrt(jnp.sum(g, axis=1, keepdims=True) + EPS) for g in diags]
@@ -220,53 +221,91 @@
         inverse = [x - mm(h, x) for x, h in zip(inverse, half)]
         size *= 2
     folded = [inverse[d] * (jnp.exp(found[d][0]) * r_rows[d]) for d in every]
-    values = [kv_ref[d, C : 2 * C, :] for d in every]
     w = [mm_exact_right(folded[d], keys[d]) for d in every]
-    u = [mm_exact_right(inverse[d], values[d]) for d in every]
     halves = []
     for d in every:
-        wu = jnp.concatenate([w[d], u[d]], axis=1)
-        wu_ref[d] = wu
         g_row, _, g_col, b_col = found[d]
-        tail = jnp.exp(g_row[:, C - 1 : C] - g_col) * b_col * r_cols[d]
-        halves.append(jnp.concatenate(split(wu * tail), axis=0))
+        tail = jnp.broadcast_to(jnp.exp(g_row[:, C - 1 : C] - g_col) * b_col * r_cols[d], (C, C))
+        inverse_ref[d] = inverse[d]
+        w_ref[d] = w[d]
+        tail_ref[d] = tail
+        halves.append(jnp.concatenate(split(w[d] * tail), axis=0))
     made = [dot_tn(jnp.concatenate([keys[d], keys[d]], axis=0), halves[d]) for d in every]
     for d in every:
         g_end = found[d][0][:, C - 1 : C]
-        maps[jnp.bitwise_xor(me, d)] = jnp.concatenate(
-            [jnp.where(row == col, jnp.exp(g_end), 0.0) - made[d][:, :C], made[d][:, C:]], axis=1
-        )
+        maps[jnp.bitwise_xor(me, d)] = jnp.where(row == col, jnp.exp(g_end), 0.0) - made[d]
     one = [maps[i] for i in every]
-    two = [after(one[2 * i], one[2 * i + 1]) for i in range(4)]
-    four = [after(two[2 * i], two[2 * i + 1]) for i in range(2)]
-    ab_ref[...] = after(four[0], four[1]).astype(BF16)
-    for i, part in enumerate((one[0], two[0], one[2], four[0], one[4], two[2], one[6])):
-        level_ref[i] = part
-
-
-def prep(slots):
-    return pl.pallas_call(
-        prep_kernel,
+    two = [mm(one[2 * i + 1], one[2 * i]) for i in range(4)]
+    four = [mm(two[2 * i + 1], two[2 * i]) for i in range(2)]
+    for i, part in enumerate(one + two + four + [mm(four[1], four[0])]):
+        reach_ref[i] = part
+
+
+def value_kernel(*refs):
+    k_ref, inverse_ref, w_ref, tail_ref, reach_ref, vq_ref, wu_ref, ab_ref, level_ref, states = (
+        refs[5:]
+    )
+    me = lax.axis_index("seq") % PLANE
+    gather_slots(refs[:5], vq_ref)
+    every = range(PLANE)
+    u = [mm_exact_right(inverse_ref[d], vq_ref[d, 0:C, :]) for d in every]
+    halves = []
+    for d in every:
+        wu_ref[d, :, :C] = w_ref[d]
+        wu_ref[d, :, C:] = u[d]
+        halves.append(jnp.concatenate(split(u[d] * tail_ref[d]), axis=0))
+    keys = [k_ref[d, 0:C, :] for d in every]
+    made = [dot_tn(jnp.concatenate([keys[d], keys[d]], axis=0), halves[d]) for d in every]
+    for d in every:
+        states[jnp.bitwise_xor(me, d)] = made[d]
+    one = [states[i] for i in every]
+    two = [mm(reach_ref[2 * i + 1], one[2 * i]) + one[2 * i + 1] for i in range(4)]
+    four = [mm(reach_ref[8 + 2 * i + 1], two[2 * i]) + two[2 * i + 1] for i in range(2)]
+    last = mm(reach_ref[13], four[0]) + four[1]
+    ab_ref[:, :C] = reach_ref[14].astype(BF16)
+    ab_ref[:, C:] = last.astype(BF16)
+    both = ((0, one[0]), (8, two[0]), (2, one[2]), (12, four[0]), (4, one[4]), (10, two[2]), (6, one[6]))
+    for i, (at, state) in enumerate(both):
+        level_ref[i, :, :C] = reach_ref[at]
+        level_ref[i, :, C:] = state
+
+
+def key_part(slots):
+    square = jax.ShapeDtypeStruct((PLANE, C, C), F32)
+    return pl.pallas_call(
+        key_kernel,
+        out_shape=[jax.ShapeDtypeStruct((PLANE, KROWS, C), BF16)]
+        + [square] * 4
+        + [jax.ShapeDtypeStruct((15, C, C), F32)],
+        in_specs=[vmem()] * 5,
+        out_specs=[vmem()] * 6,
+        scratch_shapes=[pltpu.VMEM((PLANE, C, C), F32)],
+        compiler_params=params(),
+        cost_estimate=cost(2e9, 4e6),
+        name="keys",
+    )(*slots)
+
+
+def value_part(slots, k, inverse, w, tail, reach):
+    return pl.pallas_call(
+        value_kernel,
         out_shape=[
-            jax.ShapeDtypeStruct((PLANE, BLK, C), BF16),
-            jax.ShapeDtypeStruct((PLANE, C, C), F32),
+            jax.ShapeDtypeStruct((PLANE, 2 * C, C), BF16),
             jax.ShapeDtypeStruct((PLANE, C, 2 * C), F32),
             jax.ShapeDtypeStruct((C, 2 * C), BF16),
             jax.ShapeDtypeStruct((7, C, 2 * C), F32),
         ],
-        in_specs=[vmem()] * 5,
-        out_specs=[vmem()] * 5,
-        scratch_shapes=[
-            pltpu.VMEM((PLANE, C, 2 * C), F32),
-        ],
-        compiler_params=params(),
-        cost_estimate=cost(2e9, 4e6),
-        name="prep",
-    )(*slots)
+        in_specs=[vmem()] * 10,
+        out_specs=[vmem()] * 4,
+        scratch_shapes=[pltpu.VMEM((PLANE, C, C), F32)],
+        compiler_params=params(),
+        cost_estimate=cost(1e9, 4e6),
+        name="values",
+    )(*slots, k, inverse, w, tail, reach)
 
 
 def query_kernel(*refs):
-    kv_ref, mix_ref, wu_ref, level_ref, no_ref, before = refs
+    k_ref, vq_ref, mix_ref, wu_ref, level_ref, no_ref, before = refs
     me = lax.axis_index("seq") % PLANE
     row, col = iotas()
     before[0] = jnp.concatenate([jnp.where(row == col, 1.0, 0.0), jnp.zeros((C, C), F32)], axis=1)
@@ -280,9 +319,9 @@
     before[7] = after(six, level_ref[6])
 
     every = range(PLANE)
-    found = gates(kv_ref)
-    queries = [kv_ref[d, 2 * C : 3 * C, :] for d in every]
-    scored = [dot_nt(queries[d], kv_ref[d, 0:C, :]) for d in every]
+    found = gates(k_ref)
+    queries = [vq_ref[d, C : 2 * C, :] for d in every]
+    scored = [dot_nt(queries[d], k_ref[d, 0:C, :]) for d in every]
     r_cols = []
     for q in queries:
         wide = q.astype(F32)
@@ -302,11 +341,11 @@
         )
 
 
-def query(kv, mix, wu, level):
+def query(k, vq, mix, wu, level):
     return pl.pallas_call(
         query_kernel,
         out_shape=jax.ShapeDtypeStruct((PLANE * C, 2 * C), F32),
-        in_specs=[vmem()] * 4,
+        in_specs=[vmem()] * 5,
         out_specs=vmem(),
         scratch_shapes=[
             pltpu.VMEM((PLANE, C, 2 * C), F32),
@@ -314,7 +353,7 @@
         compiler_params=params(),
         cost_estimate=cost(1e9, 4e6),
         name="query",
-    )(kv, mix, wu, level)
+    )(k, vq, mix, wu, level)
 
 
 def times(a, x):
@@ -442,7 +481,8 @@
     )(normed, weight)
 
 
-def halo_kernel(halo_ref, weight_ref, acc_ref, stat_ref, q2_ref, keep, send, attended):
+def halo_kernel(halo_ref, weight_ref, acc_ref, stat_ref, q2_ref, *refs):
+    outs, attended = refs[:4], refs[4]
     place = lax.axis_index("seq")
     me, plane = place % PLANE, place // PLANE
     proj = dot(halo_ref[...], weight_ref[me, :, C:]).astype(BF16)
@@ -472,17 +512,16 @@
         attended[rows, :] = (acc / total).astype(BF16)
     for d in range(PLANE):
         chunk = jnp.bitwise_xor(me, d)
-        out = send if d % 2 else keep
-        out[d // 2] = attended[pl.ds(pl.multiple_of(chunk * C, C), C), :]
+        outs[d // 2][d % 2] = attended[pl.ds(pl.multiple_of(chunk * C, C), C), :]
 
 
 def halo_part(halo, weight, acc, stat, q2):
     n = PLANE * C
     return pl.pallas_call(
         halo_kernel,
-        out_shape=[jax.ShapeDtypeStruct((4, C, C), BF16)] * 2,
+        out_shape=[jax.ShapeDtypeStruct((2, C, C), BF16)] * 4,
         in_specs=[vmem()] * 5,
-        out_specs=[vmem()] * 2,
+        out_specs=[vmem()] * 4,
         scratch_shapes=[pltpu.VMEM((n, C), BF16)],
         compiler_params=params(),
         cost_estimate=cost(1e9, 3e6, 6e5),
@@ -506,11 +545,11 @@
     return jnp.concatenate([left, right], axis=1), pl.ds(at, 2 * C)
 
 
-def early_kernel(keep, came, one, two, weight_ref, acc_ref):
+def early_kernel(own_pair, own_came, two, two_came, one, one_came, weight_ref, acc_ref):
     parts = [
-        pair_part(keep.at[0], came.at[0], 0),
-        pair_part(two.at[0], two.at[1], 2),
-        pair_part(one.at[0], one.at[1], 1),
+        pair_part(own_pair.at[0], own_came, 0),
+        pair_part(two.at[0], two_came, 2),
+        pair_part(one.at[0], one_came, 1),
     ]
     for at in range(0, weight_ref.shape[1], COLS):
         cols = slice(at, at + COLS)
@@ -520,8 +559,8 @@
         acc_ref[:, cols] = got
 
 
-def late_kernel(three, weight_ref, acc_ref, *outs):
-    part, rows = pair_part(three.at[0], three.at[1], 3)
+def late_kernel(three, three_came, weight_ref, acc_ref, *outs):
+    part, rows = pair_part(three.at[0], three_came, 3)
     for at in range(0, weight_ref.shape[1], COLS):
         cols = slice(at, at + COLS)
         got = acc_ref[:, cols] + dot(part, weight_ref[rows, cols])
@@ -531,26 +570,26 @@
 
 def project(slots, weight):
     width = weight.shape[1]
-    keep, came, one, two, three = slots
+    (own_pair, one, two, three), (own_came, one_came, two_came, three_came) = slots
     acc = pl.pallas_call(
         early_kernel,
         out_shape=jax.ShapeDtypeStruct((C, width), F32),
-        in_specs=[vmem()] * 5,
+        in_specs=[vmem()] * 7,
         out_specs=vmem(),
         compiler_params=params(),
         cost_estimate=cost(8e8, 8e6),
         name="early",
-    )(keep, came, one, two, weight)
+    )(own_pair, own_came, two, two_came, one, one_came, weight)
     return pl.pallas_call(
         late_kernel,
         out_shape=[jax.ShapeDtypeStruct((32, width), F32)]
         + [jax.ShapeDtypeStruct((32, width), BF16)] * 3,
-        in_specs=[vmem()] * 3,
+        in_specs=[vmem()] * 4,
         out_specs=[vmem()] * 4,
         compiler_params=params(),
         cost_estimate=cost(3e8, 4e6),
         name="late",
-    )(three, weight, acc)
+    )(three, three_came, weight, acc)
 
 
 def swap(block, d):
@@ -565,6 +604,13 @@
     return slots[:2] + [pair for _, pair in sorted(slots[2:], key=lambda item: item[0])]
 
 
+def exchange_back(pairs):
+    found = {dx: swap(pairs[dx], 2 * dx) for dx in (2, 1, 3)}
+    found[0] = pairs[0]
+    came = {dx: swap(found[dx][1], 1) for dx in (0, 2, 1, 3)}
+    return [found[dx] for dx in range(4)], [came[dx] for dx in range(4)]
+
+
 def later_plane(block, distance):
     step = PLANE * distance
     route = [(s, s + step) for s in range(PLANE * PLANES - step)]
@@ -572,17 +618,21 @@
 
 
 def local(q_delta, k_delta, v_delta, decay, beta, gain, attn_weight, out_weight):
-    kv, mix, wu, ab, level = prep(exchange(*pack(q_delta, k_delta, v_delta, decay, beta)))
+    keep_k, send_k, keep, send = pack(q_delta, k_delta, v_delta, decay, beta)
+    slots_k = exchange(keep_k, send_k)
+    slots = exchange(keep, send)
+    k, mix, inverse, w, tail, reach = key_part(slots_k)
+    vq, wu, ab, level = value_part(slots, k, inverse, w, tail, reach)
     one = later_plane(ab, 1)
     two = later_plane(ab, 2)
-    no = query(kv, mix, wu, level)
+    no = query(k, vq, mix, wu, level)
     before, upto, only = combine(ab, one, two)
     three = later_plane(upto, 3)
     six = later_plane(only, 6)
     normed = norm(no, gain[None, :], before, three, six)
     halo = later_plane(normed, 1)
     acc, stat, q2 = own(normed, attn_weight)
-    attended = exchange(*halo_part(halo, attn_weight, acc, stat, q2))
+    attended = exchange_back(halo_part(halo, attn_weight, acc, stat, q2))
     sums = project(attended, out_weight)
     moved = {}
     for d in (2, 1, 3):

time: 82.2 us -> 80.4 us (0.978)
  waiting for transfers between devices: 43.4 us -> 36.5 us
  starting transfers between devices: 25.9 us -> 30.3 us
    ppermute x8 -> x15, waiting for transfers between devices: 16.4 us -> 8.02 us  [swap(): lax.ppermute(block, 'seq', [(s, s ^ d) for s in range(PLANE * PLANES)])]
    ppermute x8 -> x15, starting transfers between devices: 10.3 us -> 14.3 us  [swap(): lax.ppermute(block, 'seq', [(s, s ^ d) for s in range(PLANE * PLANES)])]
    ppermute x3, waiting for transfers between devices: 10.7 us -> 12.2 us  [local(): moved[d] = lax.ppermute(sums[d], 'heads', [(s, s ^ d) for s in range(4)])]
    pallas_call x3 -> x4, Pallas kernels: 6.44 us -> 7.19 us  [the longest x1 3.3 us: key_part(): pl.pallas_call(key_kernel, out_shape=[jax.ShapeDtypeStruct((PLANE, KROWS,...]
  transfers between devices with their start and end apart: 16 -> 23, of which waited for: 14 -> 14; matrix products, arithmetic and copies ran while one was open for 0% -> 0% of each run, Pallas kernels for 4% -> 9%
where the time goes in v7:
time: 80.4 us; the launch traced here: 80.2 us
  waiting for transfers between devices  36.5 us (45%)
  starting transfers between devices  30.3 us (38%)
  Pallas kernels  12.2 us (15%)
  other arithmetic  0.89 us (1%)
    ppermute x5, waiting for transfers between devices, later_plane(): return lax.ppermute(block, 'seq', route)  16.3 us
    ppermute x15, starting transfers between devices, swap(): lax.ppermute(block, 'seq', [(s, s ^ d) for s in range(PLANE * PLANES)])  14.3 us
    ppermute x3, waiting for transfers between devices, local(): moved[d] = lax.ppermute(sums[d], 'heads', [(s, s ^ d) for s in range(4)])  12.2 us
    ppermute x5, starting transfers between devices, later_plane(): return lax.ppermute(block, 'seq', route)  11.4 us
    ppermute x15, waiting for transfers between devices, swap(): lax.ppermute(block, 'seq', [(s, s ^ d) for s in range(PLANE * PLANES)])  8.02 us
    ppermute x3, starting transfers between devices, local(): moved[d] = lax.ppermute(sums[d], 'heads', [(s, s ^ d) for s in range(4)])  4.57 us
    pallas_call x1, Pallas kernels, key_part(): pl.pallas_call(key_kernel, out_shape=[jax.ShapeDtypeStruct((PLANE, KROWS,...  3.3 us
  transfers between devices with their start and end apart: 23, of which 14 were waited for; matrix products, arithmetic and copies ran while one was open for 0% of the time, Pallas kernels for 9%

profile of v7, /device:TPU:128, one launch (start us, length us, event | category | flops | bytes accessed | tf_op | source)
XLA Modules:
  0.0 80.2 jit_solution(7045677382080290427)
XLA Ops:
  0.0 1.4 %pack.1 = (bf16[4,144,128]{2,1,0:T(8,128)(2,1)S(1)}, bf16[4,144,128]{2,1,0:T(8,128)(2,1)S(1)}, bf16[4,256,128]{2,1,0:T(8,128)(2,1)S(1)}, bf16[4,256,128]{2,1,0:T(8,128)(2,1)S(1)}) custom-call(bf16[128,1024]{1,0:T(8,128)(2,1)} %q_ref.1, bf16[128,1024]{1,0:T(8,128)(2,1)} %k_ref.1, bf16[128,1024]{1,0:T(8,128)(2,1)} %v_ref.1, f32[8,128]{1,0:T(8,128)} %decay_ref.1, ...), custom_call_target="tpu_custom_call" | custom-call | tf_op jit(solution)/shard_map/pack/pallas_call | solution.py:113
  1.4 0.1 collective-permute-start
  1.5 0.5 collective-permute-start.4
  2.0 0.8 %collective-permute-done.refs_1_ = bf16[4,144,128]{2,1,0:T(8,128)(2,1)S(1)} collective-permute-done((bf16[4,144,128]{2,1,0:T(8,128)(2,1)S(1)}, bf16[4,144,128]{2,1,0:T(8,128)(2,1)S(1)}, u32[]{:S(2)}, u32[]{:S(2)}) %collective-permute-start) | collective-permute-done | bytes 147488 | tf_op jit(solution)/shard_map/ppermute | solution.py:596
  2.9 1.6 %collective-permute-start.1 = (bf16[2,144,128]{2,1,0:T(8,128)(2,1)S(1)}, bf16[2,144,128]{2,1,0:T(8,128)(2,1)S(1)}, u32[]{:S(2)}, u32[]{:S(2)}) collective-permute-start(bf16[2,144,128]{2,1,0:T(8,128)(2,1)S(1)} %pad_maximum_fusion.3), channel_id=1, source_target_pairs={{0,8},{4,12},{8,0},{12,4},{16,24},{20,28},{24,16},{28,20},{32,40},... | collective-permute-start | bytes 221192 | tf_op jit(solution)/shard_map/ppermute | solution.py:596
  4.4 2.8 %collective-permute-start.2 = (bf16[2,144,128]{2,1,0:T(8,128)(2,1)S(1)}, bf16[2,144,128]{2,1,0:T(8,128)(2,1)S(1)}, u32[]{:S(2)}, u32[]{:S(2)}) collective-permute-start(bf16[2,144,128]{2,1,0:T(8,128)(2,1)S(1)} %pad_maximum_fusion.4), channel_id=1, source_target_pairs={{0,16},{4,20},{8,24},{12,28},{16,0},{20,4},{24,8},{28,12},{32,48},... | collective-permute-start | bytes 221192 | tf_op jit(solution)/shard_map/ppermute | solution.py:596
  7.3 0.0 copy-start
  7.3 0.6 collective-permute-start.3
  7.9 0.0 collective-permute-done.4.refs_1_
  7.9 0.4 collective-permute-start.5
  8.3 4.0 %collective-permute-start.6 = (bf16[2,256,128]{2,1,0:T(8,128)(2,1)S(1)}, bf16[2,256,128]{2,1,0:T(8,128)(2,1)S(1)}, u32[]{:S(2)}, u32[]{:S(2)}) collective-permute-start(bf16[2,256,128]{2,1,0:T(8,128)(2,1)S(1)} %pad_maximum_fusion.1), channel_id=1, source_target_pairs={{0,16},{4,20},{8,24},{12,28},{16,0},{20,4},{24,8},{28,12},{32,48},... | collective-permute-start | bytes 393224 | tf_op jit(solution)/shard_map/ppermute | solution.py:596
  12.3 0.0 copy-start.1
  12.3 0.0 collective-permute-done.1.refs_2_
  12.3 0.6 collective-permute-start.7
  12.9 0.0 collective-permute-done.2.refs_3_
  12.9 0.0 collective-permute-done.3.refs_4_
  12.9 3.3 %keys.1 = (bf16[8,144,128]{2,1,0:T(8,128)(2,1)S(1)}, f32[8,128,128]{2,1,0:T(8,128)S(1)}, f32[8,128,128]{2,1,0:T(8,128)S(1)}, f32[8,128,128]{2,1,0:T(8,128)S(1)},...) custom-call(bf16[4,144,128]{2,1,0:T(8,128)(2,1)S(1)} %get-tuple-element.33.refs_0_, ...), custom_call_target="tpu_custom_call" | custom-call | flops 2000000000 | bytes 4000000 | tf_op jit(solution)/shard_map/keys/pallas_call | solution.py:275
  16.2 0.0 collective-permute-done.5.refs_2_
  16.3 1.5 %collective-permute-done.6.refs_3_ = bf16[2,256,128]{2,1,0:T(8,128)(2,1)S(1)} collective-permute-done((bf16[2,256,128]{2,1,0:T(8,128)(2,1)S(1)}, bf16[2,256,128]{2,1,0:T(8,128)(2,1)S(1)}, u32[]{:S(2)}, u32[]{:S(2)}) %collective-permute-start.6) | collective-permute-done | bytes 131104 | tf_op jit(solution)/shard_map/ppermute | solution.py:596
  17.8 1.9 %collective-permute-done.7.refs_4_ = bf16[2,256,128]{2,1,0:T(8,128)(2,1)S(1)} collective-permute-done((bf16[2,256,128]{2,1,0:T(8,128)(2,1)S(1)}, bf16[2,256,128]{2,1,0:T(8,128)(2,1)S(1)}, u32[]{:S(2)}, u32[]{:S(2)}) %collective-permute-start.7) | collective-permute-done | bytes 131104 | tf_op jit(solution)/shard_map/ppermute | solution.py:596
  19.7 0.0 slice-start
  19.7 1.0 %values.1 = (bf16[8,256,128]{2,1,0:T(8,128)(2,1)S(1)}, f32[8,128,256]{2,1,0:T(8,128)S(1)}, bf16[128,256]{1,0:T(8,128)(2,1)S(1)}, f32[7,128,256]{2,1,0:T(8,128)S(1)}) custom-call(bf16[4,256,128]{2,1,0:T(8,128)(2,1)S(1)} %get-tuple-element.36.refs_0_, bf16[4,256,128]{2,1,0:T(8,128)(2,1)S(1)} %collective-permute-done.4.refs_1_, ...), custom_call_target="tpu_custom_call" | custom-call | flops 1000000000 | bytes 4000000 | tf_op jit(solution)/shard_map/values/pallas_call | solution.py:290
  20.7 3.5 %collective-permute-start.9 = (bf16[128,256]{1,0:T(8,128)(2,1)S(1)}, bf16[128,256]{1,0:T(8,128)(2,1)S(1)}, u32[]{:S(2)}, u32[]{:S(2)}) collective-permute-start(bf16[128,256]{1,0:T(8,128)(2,1)S(1)} %get-tuple-element.46.own_ref), channel_id=1, source_target_pairs={{0,64},{4,68},{8,72},{12,76},{16,80},{20,84},{24,88},{28,92},{32,9... | collective-permute-start | bytes 196616 | tf_op jit(solution)/shard_map/ppermute | solution.py:617
  24.3 2.9 %collective-permute-start.8 = (bf16[128,256]{1,0:T(8,128)(2,1)S(1)}, bf16[128,256]{1,0:T(8,128)(2,1)S(1)}, u32[]{:S(2)}, u32[]{:S(2)}) collective-permute-start(bf16[128,256]{1,0:T(8,128)(2,1)S(1)} %get-tuple-element.46.own_ref), channel_id=1, source_target_pairs={{0,32},{4,36},{8,40},{12,44},{16,48},{20,52},{24,56},{28,60},{32,6... | collective-permute-start | bytes 196616 | tf_op jit(solution)/shard_map/ppermute | solution.py:617
  27.2 1.9 %collective-permute-done.9.two_ref = bf16[128,256]{1,0:T(8,128)(2,1)S(1)} collective-permute-done((bf16[128,256]{1,0:T(8,128)(2,1)S(1)}, bf16[128,256]{1,0:T(8,128)(2,1)S(1)}, u32[]{:S(2)}, u32[]{:S(2)}) %collective-permute-start.9) | collective-permute-done | bytes 65568 | tf_op jit(solution)/shard_map/ppermute | solution.py:617
  29.1 2.5 %collective-permute-done.8.one_ref = bf16[128,256]{1,0:T(8,128)(2,1)S(1)} collective-permute-done((bf16[128,256]{1,0:T(8,128)(2,1)S(1)}, bf16[128,256]{1,0:T(8,128)(2,1)S(1)}, u32[]{:S(2)}, u32[]{:S(2)}) %collective-permute-start.8) | collective-permute-done | bytes 65568 | tf_op jit(solution)/shard_map/ppermute | solution.py:617
  31.6 0.3 combine.1
  31.9 0.7 collective-permute-start.11
  32.6 2.1 %collective-permute-start.10 = (bf16[128,256]{1,0:T(8,128)(2,1)S(1)}, bf16[128,256]{1,0:T(8,128)(2,1)S(1)}, u32[]{:S(2)}, u32[]{:S(2)}) collective-permute-start(bf16[128,256]{1,0:T(8,128)(2,1)S(1)} %get-tuple-element.48), channel_id=1, source_target_pairs={{0,96},{4,100},{8,104},{12,108},{16,112},{20,116},{24,120},{28,124... | collective-permute-start | bytes 196616 | tf_op jit(solution)/shard_map/ppermute | solution.py:617
  34.7 1.3 %query.1.no_ref = f32[1024,256]{1,0:T(8,128)S(1)} custom-call(bf16[8,144,128]{2,1,0:T(8,128)(2,1)S(1)} %get-tuple-element.35.refs_5_.refs_0_, bf16[8,256,128]{2,1,0:T(8,128)(2,1)S(1)} %get-tuple-element.42.refs_1_, f32[8,128,128]{2,1,0:T(8,128)S(1)} %get-tuple-element.43.refs_2_, f32[8,128,256]{2,1,0:T(8,128)S(1)} %get-tuple-element.44.refs_3_, ...), custom_call_target="tpu_custom_call" | custom-call | flops 1000000000 | bytes 4000000 | tf_op jit(solution)/shard_map/query/pallas_call | solution.py:345
  36.0 0.0 collective-permute-done.11.six_ref
  36.0 5.8 %collective-permute-done.10.three_ref = bf16[128,256]{1,0:T(8,128)(2,1)S(1)} collective-permute-done((bf16[128,256]{1,0:T(8,128)(2,1)S(1)}, bf16[128,256]{1,0:T(8,128)(2,1)S(1)}, u32[]{:S(2)}, u32[]{:S(2)}) %collective-permute-start.10) | collective-permute-done | bytes 65568 | tf_op jit(solution)/shard_map/ppermute | solution.py:617
  41.8 0.0 copy-done
  41.8 0.7 norm.1.normed_ref
  42.5 2.3 %collective-permute-start.12 = (bf16[1024,128]{1,0:T(8,128)(2,1)S(1)}, bf16[1024,128]{1,0:T(8,128)(2,1)S(1)}, u32[]{:S(2)}, u32[]{:S(2)}) collective-permute-start(bf16[1024,128]{1,0:T(8,128)(2,1)S(1)} %norm.1.normed_ref), channel_id=1, source_target_pairs={{0,32},{4,36},{8,40},{12,44},{16,48},{20,52},{24,56},{28,60},{32,6... | collective-permute-start | bytes 786440 | tf_op jit(solution)/shard_map/ppermute | solution.py:617
  44.8 0.0 copy-done.1
  44.8 1.3 %own.1 = (f32[1024,128]{1,0:T(8,128)S(1)}, f32[2,1024,128]{2,1,0:T(8,128)S(1)}, bf16[1024,128]{1,0:T(8,128)(2,1)S(1)}) custom-call(bf16[1024,128]{1,0:T(8,128)(2,1)S(1)} %norm.1.normed_ref, bf16[8,128,384]{2,1,0:T(8,128)(2,1)S(1)} %copy-done.1), custom_call_target="tpu_custom_call" | custom-call | flops 1000000000 | bytes 3000000 | tf_op jit(solution)/shard_map/own/pallas_call | solution.py:469
  46.1 6.0 %collective-permute-done.12.halo_ref = bf16[1024,128]{1,0:T(8,128)(2,1)S(1)} collective-permute-done((bf16[1024,128]{1,0:T(8,128)(2,1)S(1)}, bf16[1024,128]{1,0:T(8,128)(2,1)S(1)}, u32[]{:S(2)}, u32[]{:S(2)}) %collective-permute-start.12) | collective-permute-done | bytes 262176 | tf_op jit(solution)/shard_map/ppermute | solution.py:617
  52.1 1.5 %halo.1 = (bf16[2,128,128]{2,1,0:T(8,128)(2,1)S(1)}, bf16[2,128,128]{2,1,0:T(8,128)(2,1)S(1)}, bf16[2,128,128]{2,1,0:T(8,128)(2,1)S(1)}, bf16[2,128,128]{2,1,0:T(8,128)(2,1)S(1)}) custom-call(bf16[1024,128]{1,0:T(8,128)(2,1)S(1)} %collective-permute-done.12.halo_ref, bf16[8,128,384]{2,1,0:T(8,128)(2,1)S(1)} %copy-done.1, ...), custom_call_target="tpu_custom_call" | custom-call | flops 1000000000 | bytes 3000000 | tf_op jit(solution)/shard_map/halo/pallas_call | solution.py:520
  53.6 0.9 %collective-permute-start.16 = (bf16[2,128,128]{2,1,0:T(8,128)(2,1)S(1)}, bf16[2,128,128]{2,1,0:T(8,128)(2,1)S(1)}, u32[]{:S(2)}, u32[]{:S(2)}) collective-permute-start(bf16[2,128,128]{2,1,0:T(8,128)(2,1)S(1)} %get-tuple-element.55), channel_id=1, source_target_pairs={{0,16},{4,20},{8,24},{12,28},{16,0},{20,4},{24,8},{28,12},{32,48},... | collective-permute-start | bytes 196616 | tf_op jit(solution)/shard_map/ppermute | solution.py:596
  54.5 0.0 collective-permute-start.15
  54.6 1.1 %collective-permute-start.13 = (bf16[2,128,128]{2,1,0:T(8,128)(2,1)S(1)}, bf16[2,128,128]{2,1,0:T(8,128)(2,1)S(1)}, u32[]{:S(2)}, u32[]{:S(2)}) collective-permute-start(bf16[2,128,128]{2,1,0:T(8,128)(2,1)S(1)} %get-tuple-element.53), channel_id=1, source_target_pairs={{0,24},{4,28},{8,16},{12,20},{16,8},{20,12},{24,0},{28,4},{32,56},... | collective-permute-start | bytes 196616 | tf_op jit(solution)/shard_map/ppermute | solution.py:596
  55.7 1.5 %collective-permute-start.18 = (bf16[2,128,128]{2,1,0:T(8,128)(2,1)S(1)}, bf16[2,128,128]{2,1,0:T(8,128)(2,1)S(1)}, u32[]{:S(2)}, u32[]{:S(2)}) collective-permute-start(bf16[2,128,128]{2,1,0:T(8,128)(2,1)S(1)} %get-tuple-element.56), channel_id=1, source_target_pairs={{0,8},{4,12},{8,0},{12,4},{16,24},{20,28},{24,16},{28,20},{32,40},... | collective-permute-start | bytes 196616 | tf_op jit(solution)/shard_map/ppermute | solution.py:596
  57.2 2.3 %collective-permute-done.16.two = bf16[2,128,128]{2,1,0:T(8,128)(2,1)S(1)} collective-permute-done((bf16[2,128,128]{2,1,0:T(8,128)(2,1)S(1)}, bf16[2,128,128]{2,1,0:T(8,128)(2,1)S(1)}, u32[]{:S(2)}, u32[]{:S(2)}) %collective-permute-start.16) | collective-permute-done | bytes 65568 | tf_op jit(solution)/shard_map/ppermute | solution.py:596
  59.5 0.0 collective-permute-start.17
  59.5 0.4 collective-permute-done.18.one
  59.9 0.1 collective-permute-start.19
  60.1 0.8 %collective-permute-done.13.three = bf16[2,128,128]{2,1,0:T(8,128)(2,1)S(1)} collective-permute-done((bf16[2,128,128]{2,1,0:T(8,128)(2,1)S(1)}, bf16[2,128,128]{2,1,0:T(8,128)(2,1)S(1)}, u32[]{:S(2)}, u32[]{:S(2)}) %collective-permute-start.13) | collective-permute-done | bytes 65568 | tf_op jit(solution)/shard_map/ppermute | solution.py:596
  60.9 0.1 collective-permute-start.14
  61.0 0.0 collective-permute-done.15.own_came
  61.0 0.0 collective-permute-done.17.two_came
  61.0 0.2 collective-permute-done.19.one_came
  61.1 0.0 slice-done
  61.1 0.0 slice-done.1
  61.2 1.0 %early.1.acc_ref = f32[128,4096]{1,0:T(8,128)S(1)} custom-call(bf16[2,128,128]{2,1,0:T(8,128)(2,1)S(1)} %get-tuple-element.54.own_pair, bf16[128,128]{1,0:T(8,128)(2,1)S(1)} %collective-permute-done.15.own_came, bf16[2,128,128]{2,1,0:T(8,128)(2,1)S(1)} %collective-permute-done.16.two, bf16[128,128]{1,0:T(8,128)(2,1)S(1)} %collective-permute-done.17.two_came, ...), custom_call_target="tpu_custom_call" | custom-call | flops 800000000 | bytes 8000000 | tf_op jit(solution)/shard_map/early/pallas_call | solution.py:574
  62.1 0.0 collective-permute-done.14.three_came
  62.2 0.5 late.1
  62.6 1.7 %collective-permute-start.20 = (bf16[32,4096]{1,0:T(8,128)(2,1)S(1)}, bf16[32,4096]{1,0:T(8,128)(2,1)S(1)}, u32[]{:S(2)}, u32[]{:S(2)}) collective-permute-start(bf16[32,4096]{1,0:T(8,128)(2,1)S(1)} %get-tuple-element.58), channel_id=1, source_target_pairs={{0,1},{1,0},{2,3},{3,2},{4,5},{5,4},{6,7},{7,6},{8,9},{9,8},{10,11... | collective-permute-start | bytes 786440 | tf_op jit(solution)/shard_map/ppermute | solution.py:639
  64.3 2.2 %collective-permute-start.21 = (bf16[32,4096]{1,0:T(8,128)(2,1)S(1)}, bf16[32,4096]{1,0:T(8,128)(2,1)S(1)}, u32[]{:S(2)}, u32[]{:S(2)}) collective-permute-start(bf16[32,4096]{1,0:T(8,128)(2,1)S(1)} %get-tuple-element.59), channel_id=1, source_target_pairs={{0,3},{1,2},{2,1},{3,0},{4,7},{5,6},{6,5},{7,4},{8,11},{9,10},{10,... | collective-permute-start | bytes 786440 | tf_op jit(solution)/shard_map/ppermute | solution.py:639
  66.5 0.7 collective-permute-start.22
  67.2 4.6 %collective-permute-done.20 = bf16[32,4096]{1,0:T(8,128)(2,1)S(1)} collective-permute-done((bf16[32,4096]{1,0:T(8,128)(2,1)S(1)}, bf16[32,4096]{1,0:T(8,128)(2,1)S(1)}, u32[]{:S(2)}, u32[]{:S(2)}) %collective-permute-start.20) | collective-permute-done | bytes 262176 | tf_op jit(solution)/shard_map/ppermute | solution.py:639
  71.8 6.0 %collective-permute-done.21 = bf16[32,4096]{1,0:T(8,128)(2,1)S(1)} collective-permute-done((bf16[32,4096]{1,0:T(8,128)(2,1)S(1)}, bf16[32,4096]{1,0:T(8,128)(2,1)S(1)}, u32[]{:S(2)}, u32[]{:S(2)}) %collective-permute-start.21) | collective-permute-done | bytes 262176 | tf_op jit(solution)/shard_map/ppermute | solution.py:639
  77.8 1.5 %collective-permute-done.22 = bf16[32,4096]{1,0:T(8,128)(2,1)S(1)} collective-permute-done((bf16[32,4096]{1,0:T(8,128)(2,1)S(1)}, bf16[32,4096]{1,0:T(8,128)(2,1)S(1)}, u32[]{:S(2)}, u32[]{:S(2)}) %collective-permute-start.22) | collective-permute-done | bytes 262176 | tf_op jit(solution)/shard_map/ppermute | solution.py:639
  79.4 0.8 %add_convert_fusion = bf16[32,4096]{1,0:T(8,128)(2,1)} fusion(bf16[32,4096]{1,0:T(8,128)(2,1)S(1)} %collective-permute-done.22, bf16[32,4096]{1,0:T(8,128)(2,1)S(1)} %collective-permute-done.21, f32[32,4096]{1,0:T(8,128)S(1)} %get-tuple-element.57, bf16[32,4096]{1,0:T(8,128)(2,1)S(1)} %collective-permute-done.20), kind=kLoop, calls=%fused_computation | loop fusion | flops 917504 | bytes 1572864 | tf_op jit(solution)/shard_map/convert_element_type | solution.py:643
  (16 shorter events, 0.1 us)
Async XLA Ops:
  1.4 1.5 %collective-permute-start = (bf16[4,144,128]{2,1,0:T(8,128)(2,1)S(1)}, bf16[4,144,128]{2,1,0:T(8,128)(2,1)S(1)}, u32[]{:S(2)}, u32[]{:S(2)}) collective-permute-start(bf16[4,144,128]{2,1,0:T(8,128)(2,1)S(1)} %get-tuple-element.34), channel_id=1, source_target_pairs={{0,4},{4,0},{8,12},{12,8},{16,20},{20,16},{24,28},{28,24},{32,36},... | collective-permute-start | bytes 442376 | tf_op jit(solution)/shard_map/ppermute | solution.py:596
  1.5 6.4 %collective-permute-start.4 = (bf16[4,256,128]{2,1,0:T(8,128)(2,1)S(1)}, bf16[4,256,128]{2,1,0:T(8,128)(2,1)S(1)}, u32[]{:S(2)}, u32[]{:S(2)}) collective-permute-start(bf16[4,256,128]{2,1,0:T(8,128)(2,1)S(1)} %get-tuple-element.37), channel_id=1, source_target_pairs={{0,4},{4,0},{8,12},{12,8},{16,20},{20,16},{24,28},{28,24},{32,36},... | collective-permute-start | bytes 786440 | tf_op jit(solution)/shard_map/ppermute | solution.py:596
  2.9 9.5 %collective-permute-start.1 = (bf16[2,144,128]{2,1,0:T(8,128)(2,1)S(1)}, bf16[2,144,128]{2,1,0:T(8,128)(2,1)S(1)}, u32[]{:S(2)}, u32[]{:S(2)}) collective-permute-start(bf16[2,144,128]{2,1,0:T(8,128)(2,1)S(1)} %pad_maximum_fusion.3), channel_id=1, source_target_pairs={{0,8},{4,12},{8,0},{12,4},{16,24},{20,28},{24,16},{28,20},{32,40},... | collective-permute-start | bytes 221192 | tf_op jit(solution)/shard_map/ppermute | solution.py:596
  4.4 8.5 %collective-permute-start.2 = (bf16[2,144,128]{2,1,0:T(8,128)(2,1)S(1)}, bf16[2,144,128]{2,1,0:T(8,128)(2,1)S(1)}, u32[]{:S(2)}, u32[]{:S(2)}) collective-permute-start(bf16[2,144,128]{2,1,0:T(8,128)(2,1)S(1)} %pad_maximum_fusion.4), channel_id=1, source_target_pairs={{0,16},{4,20},{8,24},{12,28},{16,0},{20,4},{24,8},{28,12},{32,48},... | collective-permute-start | bytes 221192 | tf_op jit(solution)/shard_map/ppermute | solution.py:596
  7.3 34.5 %copy-start = (f32[128]{0:T(128)S(1)}, f32[128]{0:T(128)}, u32[]{:S(2)}) copy-start(f32[128]{0:T(128)} %param.13) | copy-start | bytes 1540
  7.3 5.7 %collective-permute-start.3 = (bf16[2,144,128]{2,1,0:T(8,128)(2,1)S(1)}, bf16[2,144,128]{2,1,0:T(8,128)(2,1)S(1)}, u32[]{:S(2)}, u32[]{:S(2)}) collective-permute-start(bf16[2,144,128]{2,1,0:T(8,128)(2,1)S(1)} %pad_maximum_fusion.5), channel_id=1, source_target_pairs={{0,24},{4,28},{8,16},{12,20},{16,8},{20,12},{24,0},{28,4},{32,56},... | collective-permute-start | bytes 221192 | tf_op jit(solution)/shard_map/ppermute | solution.py:596
  7.9 8.3 %collective-permute-start.5 = (bf16[2,256,128]{2,1,0:T(8,128)(2,1)S(1)}, bf16[2,256,128]{2,1,0:T(8,128)(2,1)S(1)}, u32[]{:S(2)}, u32[]{:S(2)}) collective-permute-start(bf16[2,256,128]{2,1,0:T(8,128)(2,1)S(1)} %pad_maximum_fusion), channel_id=1, source_target_pairs={{0,8},{4,12},{8,0},{12,4},{16,24},{20,28},{24,16},{28,20},{32,40},... | collective-permute-start | bytes 393224 | tf_op jit(solution)/shard_map/ppermute | solution.py:596
  8.3 9.5 %collective-permute-start.6 = (bf16[2,256,128]{2,1,0:T(8,128)(2,1)S(1)}, bf16[2,256,128]{2,1,0:T(8,128)(2,1)S(1)}, u32[]{:S(2)}, u32[]{:S(2)}) collective-permute-start(bf16[2,256,128]{2,1,0:T(8,128)(2,1)S(1)} %pad_maximum_fusion.1), channel_id=1, source_target_pairs={{0,16},{4,20},{8,24},{12,28},{16,0},{20,4},{24,8},{28,12},{32,48},... | collective-permute-start | bytes 393224 | tf_op jit(solution)/shard_map/ppermute | solution.py:596
  12.3 32.5 %copy-start.1 = (bf16[8,128,384]{2,1,0:T(8,128)(2,1)S(1)}, bf16[8,128,384]{2,1,0:T(8,128)(2,1)}, u32[]{:S(2)}) copy-start(bf16[8,128,384]{2,1,0:T(8,128)(2,1)} %weight_ref.5) | copy-start | bytes 2359300
  12.3 7.3 %collective-permute-start.7 = (bf16[2,256,128]{2,1,0:T(8,128)(2,1)S(1)}, bf16[2,256,128]{2,1,0:T(8,128)(2,1)S(1)}, u32[]{:S(2)}, u32[]{:S(2)}) collective-permute-start(bf16[2,256,128]{2,1,0:T(8,128)(2,1)S(1)} %pad_maximum_fusion.2), channel_id=1, source_target_pairs={{0,24},{4,28},{8,16},{12,20},{16,8},{20,12},{24,0},{28,4},{32,56},... | collective-permute-start | bytes 393224 | tf_op jit(solution)/shard_map/ppermute | solution.py:596
  19.7 41.5 %slice-start = ((s8[8388608]{0:T(1024)(128)(4,1)}), s8[4194304]{0:T(1024)(128)(4,1)S(1)}, s32[]{:S(2)}) async-start(s8[8388608]{0:T(1024)(128)(4,1)} %bitcast.9), calls=%async_computation | async-start | bytes 8388608
  20.7 8.4 %collective-permute-start.9 = (bf16[128,256]{1,0:T(8,128)(2,1)S(1)}, bf16[128,256]{1,0:T(8,128)(2,1)S(1)}, u32[]{:S(2)}, u32[]{:S(2)}) collective-permute-start(bf16[128,256]{1,0:T(8,128)(2,1)S(1)} %get-tuple-element.46.own_ref), channel_id=1, source_target_pairs={{0,64},{4,68},{8,72},{12,76},{16,80},{20,84},{24,88},{28,92},{32,9... | collective-permute-start | bytes 196616 | tf_op jit(solution)/shard_map/ppermute | solution.py:617
  24.3 7.4 %collective-permute-start.8 = (bf16[128,256]{1,0:T(8,128)(2,1)S(1)}, bf16[128,256]{1,0:T(8,128)(2,1)S(1)}, u32[]{:S(2)}, u32[]{:S(2)}) collective-permute-start(bf16[128,256]{1,0:T(8,128)(2,1)S(1)} %get-tuple-element.46.own_ref), channel_id=1, source_target_pairs={{0,32},{4,36},{8,40},{12,44},{16,48},{20,52},{24,56},{28,60},{32,6... | collective-permute-start | bytes 196616 | tf_op jit(solution)/shard_map/ppermute | solution.py:617
  31.9 4.0 %collective-permute-start.11 = (bf16[128,128]{1,0:T(8,128)(2,1)S(1)}, bf16[128,128]{1,0:T(8,128)(2,1)S(1)}, u32[]{:S(2)}, u32[]{:S(2)}) collective-permute-start(bf16[128,128]{1,0:T(8,128)(2,1)S(1)} %get-tuple-element.49), channel_id=1, source_target_pairs={{0,192},{4,196},{8,200},{12,204},{16,208},{20,212},{24,216},{28,22... | collective-permute-start | bytes 98312 | tf_op jit(solution)/shard_map/ppermute | solution.py:617
  32.6 9.2 %collective-permute-start.10 = (bf16[128,256]{1,0:T(8,128)(2,1)S(1)}, bf16[128,256]{1,0:T(8,128)(2,1)S(1)}, u32[]{:S(2)}, u32[]{:S(2)}) collective-permute-start(bf16[128,256]{1,0:T(8,128)(2,1)S(1)} %get-tuple-element.48), channel_id=1, source_target_pairs={{0,96},{4,100},{8,104},{12,108},{16,112},{20,116},{24,120},{28,124... | collective-permute-start | bytes 196616 | tf_op jit(solution)/shard_map/ppermute | solution.py:617
  41.8 19.4 %slice-start.1 = ((s8[8388608]{0:T(1024)(128)(4,1)}), s8[4194304]{0:T(1024)(128)(4,1)S(1)}, s32[]{:S(2)}) async-start(s8[8388608]{0:T(1024)(128)(4,1)} %bitcast.9), calls=%async_computation.1 | async-start | bytes 8388608
  42.5 9.6 %collective-permute-start.12 = (bf16[1024,128]{1,0:T(8,128)(2,1)S(1)}, bf16[1024,128]{1,0:T(8,128)(2,1)S(1)}, u32[]{:S(2)}, u32[]{:S(2)}) collective-permute-start(bf16[1024,128]{1,0:T(8,128)(2,1)S(1)} %norm.1.normed_ref), channel_id=1, source_target_pairs={{0,32},{4,36},{8,40},{12,44},{16,48},{20,52},{24,56},{28,60},{32,6... | collective-permute-start | bytes 786440 | tf_op jit(solution)/shard_map/ppermute | solution.py:617
  53.6 5.9 %collective-permute-start.16 = (bf16[2,128,128]{2,1,0:T(8,128)(2,1)S(1)}, bf16[2,128,128]{2,1,0:T(8,128)(2,1)S(1)}, u32[]{:S(2)}, u32[]{:S(2)}) collective-permute-start(bf16[2,128,128]{2,1,0:T(8,128)(2,1)S(1)} %get-tuple-element.55), channel_id=1, source_target_pairs={{0,16},{4,20},{8,24},{12,28},{16,0},{20,4},{24,8},{28,12},{32,48},... | collective-permute-start | bytes 196616 | tf_op jit(solution)/shard_map/ppermute | solution.py:596
  54.5 6.4 %collective-permute-start.15 = (bf16[128,128]{1,0:T(8,128)(2,1)S(1)}, bf16[128,128]{1,0:T(8,128)(2,1)S(1)}, u32[]{:S(2)}, u32[]{:S(2)}) collective-permute-start(bf16[128,128]{1,0:T(8,128)(2,1)S(1)} %slice_bitcast_fusion.3), channel_id=1, source_target_pairs={{0,4},{4,0},{8,12},{12,8},{16,20},{20,16},{24,28},{28,24},{32,36},... | collective-permute-start | bytes 98312 | tf_op jit(solution)/shard_map/ppermute | solution.py:596
  54.6 6.3 %collective-permute-start.13 = (bf16[2,128,128]{2,1,0:T(8,128)(2,1)S(1)}, bf16[2,128,128]{2,1,0:T(8,128)(2,1)S(1)}, u32[]{:S(2)}, u32[]{:S(2)}) collective-permute-start(bf16[2,128,128]{2,1,0:T(8,128)(2,1)S(1)} %get-tuple-element.53), channel_id=1, source_target_pairs={{0,24},{4,28},{8,16},{12,20},{16,8},{20,12},{24,0},{28,4},{32,56},... | collective-permute-start | bytes 196616 | tf_op jit(solution)/shard_map/ppermute | solution.py:596
  55.7 4.3 %collective-permute-start.18 = (bf16[2,128,128]{2,1,0:T(8,128)(2,1)S(1)}, bf16[2,128,128]{2,1,0:T(8,128)(2,1)S(1)}, u32[]{:S(2)}, u32[]{:S(2)}) collective-permute-start(bf16[2,128,128]{2,1,0:T(8,128)(2,1)S(1)} %get-tuple-element.56), channel_id=1, source_target_pairs={{0,8},{4,12},{8,0},{12,4},{16,24},{20,28},{24,16},{28,20},{32,40},... | collective-permute-start | bytes 196616 | tf_op jit(solution)/shard_map/ppermute | solution.py:596
  59.5 1.4 %collective-permute-start.17 = (bf16[128,128]{1,0:T(8,128)(2,1)S(1)}, bf16[128,128]{1,0:T(8,128)(2,1)S(1)}, u32[]{:S(2)}, u32[]{:S(2)}) collective-permute-start(bf16[128,128]{1,0:T(8,128)(2,1)S(1)} %slice_bitcast_fusion.1), channel_id=1, source_target_pairs={{0,4},{4,0},{8,12},{12,8},{16,20},{20,16},{24,28},{28,24},{32,36},... | collective-permute-start | bytes 98312 | tf_op jit(solution)/shard_map/ppermute | solution.py:596
  59.9 1.2 %collective-permute-start.19 = (bf16[128,128]{1,0:T(8,128)(2,1)S(1)}, bf16[128,128]{1,0:T(8,128)(2,1)S(1)}, u32[]{:S(2)}, u32[]{:S(2)}) collective-permute-start(bf16[128,128]{1,0:T(8,128)(2,1)S(1)} %slice_bitcast_fusion), channel_id=1, source_target_pairs={{0,4},{4,0},{8,12},{12,8},{16,20},{20,16},{24,28},{28,24},{32,36},... | collective-permute-start | bytes 98312 | tf_op jit(solution)/shard_map/ppermute | solution.py:596
  60.9 1.3 %collective-permute-start.14 = (bf16[128,128]{1,0:T(8,128)(2,1)S(1)}, bf16[128,128]{1,0:T(8,128)(2,1)S(1)}, u32[]{:S(2)}, u32[]{:S(2)}) collective-permute-start(bf16[128,128]{1,0:T(8,128)(2,1)S(1)} %slice_bitcast_fusion.2), channel_id=1, source_target_pairs={{0,4},{4,0},{8,12},{12,8},{16,20},{20,16},{24,28},{28,24},{32,36},... | collective-permute-start | bytes 98312 | tf_op jit(solution)/shard_map/ppermute | solution.py:596
  62.6 9.2 %collective-permute-start.20 = (bf16[32,4096]{1,0:T(8,128)(2,1)S(1)}, bf16[32,4096]{1,0:T(8,128)(2,1)S(1)}, u32[]{:S(2)}, u32[]{:S(2)}) collective-permute-start(bf16[32,4096]{1,0:T(8,128)(2,1)S(1)} %get-tuple-element.58), channel_id=1, source_target_pairs={{0,1},{1,0},{2,3},{3,2},{4,5},{5,4},{6,7},{7,6},{8,9},{9,8},{10,11... | collective-permute-start | bytes 786440 | tf_op jit(solution)/shard_map/ppermute | solution.py:639
  64.3 13.5 %collective-permute-start.21 = (bf16[32,4096]{1,0:T(8,128)(2,1)S(1)}, bf16[32,4096]{1,0:T(8,128)(2,1)S(1)}, u32[]{:S(2)}, u32[]{:S(2)}) collective-permute-start(bf16[32,4096]{1,0:T(8,128)(2,1)S(1)} %get-tuple-element.59), channel_id=1, source_target_pairs={{0,3},{1,2},{2,1},{3,0},{4,7},{5,6},{6,5},{7,4},{8,11},{9,10},{10,... | collective-permute-start | bytes 786440 | tf_op jit(solution)/shard_map/ppermute | solution.py:639
  66.5 12.9 %collective-permute-start.22 = (bf16[32,4096]{1,0:T(8,128)(2,1)S(1)}, bf16[32,4096]{1,0:T(8,128)(2,1)S(1)}, u32[]{:S(2)}, u32[]{:S(2)}) collective-permute-start(bf16[32,4096]{1,0:T(8,128)(2,1)S(1)} %get-tuple-element.60), channel_id=1, source_target_pairs={{0,2},{1,3},{2,0},{3,1},{4,6},{5,7},{6,4},{7,5},{8,10},{9,11},{10,... | collective-permute-start | bytes 786440 | tf_op jit(solution)/shard_map/ppermute | solution.py:639

commit v8 on v7

--- a/solution.py
+++ b/solution.py
@@ -361,16 +361,14 @@
     return dot(jnp.concatenate([a, a], axis=1), jnp.concatenate([hi, lo], axis=0))
 
 
-def combine_kernel(own_ref, one_ref, two_ref, before_ref, upto_ref, only_ref):
+def combine_kernel(own_ref, one_ref, two_ref, before_ref, upto_ref):
     a_one, a_own = one_ref[:, :C], own_ref[:, :C]
     reach = dot(a_one, two_ref[:, :C])
     state = one_ref[:, C:].astype(F32) + dot(a_one, two_ref[:, C:])
     before_ref[:, :C] = reach
     before_ref[:, C:] = state
     upto_ref[:, :C] = times(a_own, reach).astype(BF16)
-    total = (own_ref[:, C:].astype(F32) + times(a_own, state)).astype(BF16)
-    upto_ref[:, C:] = total
-    only_ref[...] = total
+    upto_ref[:, C:] = (own_ref[:, C:].astype(F32) + times(a_own, state)).astype(BF16)
 
 
 def combine(own_map, one, two):
@@ -379,24 +377,23 @@
         out_shape=[
             jax.ShapeDtypeStruct((C, 2 * C), F32),
             jax.ShapeDtypeStruct((C, 2 * C), BF16),
-            jax.ShapeDtypeStruct((C, C), BF16),
         ],
         in_specs=[vmem()] * 3,
-        out_specs=[vmem()] * 3,
+        out_specs=[vmem()] * 2,
         compiler_params=params(),
         name="combine",
     )(own_map, one, two)
 
 
-def norm_kernel(no_ref, gain_ref, before_ref, three_ref, six_ref, normed_ref):
-    state = three_ref[:, C:].astype(F32) + dot(three_ref[:, :C], six_ref[...])
+def norm_kernel(no_ref, gain_ref, before_ref, six_ref, three_ref, normed_ref):
+    state = three_ref[:, C:].astype(F32) + dot(three_ref[:, :C], six_ref[:, C:])
     state = before_ref[:, C:] + mm(before_ref[:, :C], state)
     out = mm(no_ref[:, :C], state) + no_ref[:, C:]
     scale = lax.rsqrt(jnp.mean(out * out, axis=1, keepdims=True) + EPS)
     normed_ref[...] = (out * scale * gain_ref[...]).astype(BF16)
 
 
-def norm(no, gain, before, three, six):
+def norm(no, gain, before, six, three):
     return pl.pallas_call(
         norm_kernel,
         out_shape=jax.ShapeDtypeStruct((PLANE * C, C), BF16),
@@ -405,7 +402,7 @@
         compiler_params=params(),
         cost_estimate=cost(2e8, 2e6),
         name="norm",
-    )(no, gain, before, three, six)
+    )(no, gain, before, six, three)
 
 
 QB = 256
@@ -606,8 +603,8 @@
 
 def exchange_back(pairs):
     found = {dx: swap(pairs[dx], 2 * dx) for dx in (2, 1, 3)}
-    found[0] = pairs[0]
-    came = {dx: swap(found[dx][1], 1) for dx in (0, 2, 1, 3)}
+    found[0], found[2] = lax.optimization_barrier((pairs[0], found[2]))
+    came = {dx: swap(found[dx][1], 1) for dx in (2, 0, 1, 3)}
     return [found[dx] for dx in range(4)], [came[dx] for dx in range(4)]
 
 
@@ -626,10 +623,10 @@
     one = later_plane(ab, 1)
     two = later_plane(ab, 2)
     no = query(k, vq, mix, wu, level)
-    before, upto, only = combine(ab, one, two)
+    before, upto = combine(ab, one, two)
+    six = later_plane(upto, 6)
     three = later_plane(upto, 3)
-    six = later_plane(only, 6)
-    normed = norm(no, gain[None, :], before, three, six)
+    normed = norm(no, gain[None, :], before, six, three)
     halo = later_plane(normed, 1)
     acc, stat, q2 = own(normed, attn_weight)
     attended = exchange_back(halo_part(halo, attn_weight, acc, stat, q2))

time: 80.4 us -> 80.4 us (level)
  waiting for transfers between devices: 36.5 us -> 35.2 us
    ppermute x15, starting transfers between devices: 14.3 us -> 15.2 us  [swap(): lax.ppermute(block, 'seq', [(s, s ^ d) for s in range(PLANE * PLANES)])]
where the time goes in v8:
time: 80.4 us; the launch traced here: 79.6 us
  waiting for transfers between devices  35.2 us (44%)
  starting transfers between devices  31 us (39%)
  Pallas kernels  12.2 us (15%)
  other arithmetic  0.89 us (1%)
    ppermute x5, waiting for transfers between devices, later_plane(): return lax.ppermute(block, 'seq', route)  15.8 us
    ppermute x15, starting transfers between devices, swap(): lax.ppermute(block, 'seq', [(s, s ^ d) for s in range(PLANE * PLANES)])  15.2 us
    ppermute x3, waiting for transfers between devices, local(): moved[d] = lax.ppermute(sums[d], 'heads', [(s, s ^ d) for s in range(4)])  12 us
    ppermute x5, starting transfers between devices, later_plane(): return lax.ppermute(block, 'seq', route)  11.3 us
    ppermute x15, waiting for transfers between devices, swap(): lax.ppermute(block, 'seq', [(s, s ^ d) for s in range(PLANE * PLANES)])  7.37 us
    ppermute x3, starting transfers between devices, local(): moved[d] = lax.ppermute(sums[d], 'heads', [(s, s ^ d) for s in range(4)])  4.57 us
    pallas_call x1, Pallas kernels, key_part(): pl.pallas_call(key_kernel, out_shape=[jax.ShapeDtypeStruct((PLANE, KROWS,...  3.3 us
  transfers between devices with their start and end apart: 23, of which 14 were waited for; matrix products, arithmetic and copies ran while one was open for 0% of the time, Pallas kernels for 9%

profile of v8, /device:TPU:128, one launch (start us, length us, event | category | flops | bytes accessed | tf_op | source)
XLA Modules:
  0.0 79.6 jit_solution(13166157418226441599)
XLA Ops:
  0.0 1.4 %pack.1 = (bf16[4,144,128]{2,1,0:T(8,128)(2,1)S(1)}, bf16[4,144,128]{2,1,0:T(8,128)(2,1)S(1)}, bf16[4,256,128]{2,1,0:T(8,128)(2,1)S(1)}, bf16[4,256,128]{2,1,0:T(8,128)(2,1)S(1)}) custom-call(bf16[128,1024]{1,0:T(8,128)(2,1)} %q_ref.1, bf16[128,1024]{1,0:T(8,128)(2,1)} %k_ref.1, bf16[128,1024]{1,0:T(8,128)(2,1)} %v_ref.1, f32[8,128]{1,0:T(8,128)} %decay_ref.1, ...), custom_call_target="tpu_custom_call" | custom-call | tf_op jit(solution)/shard_map/pack/pallas_call | solution.py:113
  1.4 0.1 collective-permute-start
  1.5 0.5 collective-permute-start.4
  2.0 0.8 %collective-permute-done.refs_1_ = bf16[4,144,128]{2,1,0:T(8,128)(2,1)S(1)} collective-permute-done((bf16[4,144,128]{2,1,0:T(8,128)(2,1)S(1)}, bf16[4,144,128]{2,1,0:T(8,128)(2,1)S(1)}, u32[]{:S(2)}, u32[]{:S(2)}) %collective-permute-start) | collective-permute-done | bytes 147488 | tf_op jit(solution)/shard_map/ppermute | solution.py:593
  2.9 1.6 %collective-permute-start.1 = (bf16[2,144,128]{2,1,0:T(8,128)(2,1)S(1)}, bf16[2,144,128]{2,1,0:T(8,128)(2,1)S(1)}, u32[]{:S(2)}, u32[]{:S(2)}) collective-permute-start(bf16[2,144,128]{2,1,0:T(8,128)(2,1)S(1)} %pad_maximum_fusion.3), channel_id=1, source_target_pairs={{0,8},{4,12},{8,0},{12,4},{16,24},{20,28},{24,16},{28,20},{32,40},... | collective-permute-start | bytes 221192 | tf_op jit(solution)/shard_map/ppermute | solution.py:593
  4.4 2.8 %collective-permute-start.2 = (bf16[2,144,128]{2,1,0:T(8,128)(2,1)S(1)}, bf16[2,144,128]{2,1,0:T(8,128)(2,1)S(1)}, u32[]{:S(2)}, u32[]{:S(2)}) collective-permute-start(bf16[2,144,128]{2,1,0:T(8,128)(2,1)S(1)} %pad_maximum_fusion.4), channel_id=1, source_target_pairs={{0,16},{4,20},{8,24},{12,28},{16,0},{20,4},{24,8},{28,12},{32,48},... | collective-permute-start | bytes 221192 | tf_op jit(solution)/shard_map/ppermute | solution.py:593
  7.3 0.0 copy-start
  7.3 0.6 collective-permute-start.3
  7.9 0.0 collective-permute-done.4.refs_1_
  7.9 0.4 collective-permute-start.5
  8.3 4.0 %collective-permute-start.6 = (bf16[2,256,128]{2,1,0:T(8,128)(2,1)S(1)}, bf16[2,256,128]{2,1,0:T(8,128)(2,1)S(1)}, u32[]{:S(2)}, u32[]{:S(2)}) collective-permute-start(bf16[2,256,128]{2,1,0:T(8,128)(2,1)S(1)} %pad_maximum_fusion.1), channel_id=1, source_target_pairs={{0,16},{4,20},{8,24},{12,28},{16,0},{20,4},{24,8},{28,12},{32,48},... | collective-permute-start | bytes 393224 | tf_op jit(solution)/shard_map/ppermute | solution.py:593
  12.3 0.0 copy-start.1
  12.3 0.0 collective-permute-done.1.refs_2_
  12.3 0.6 collective-permute-start.7
  12.9 0.0 collective-permute-done.2.refs_3_
  12.9 0.0 collective-permute-done.3.refs_4_
  12.9 3.3 %keys.1 = (bf16[8,144,128]{2,1,0:T(8,128)(2,1)S(1)}, f32[8,128,128]{2,1,0:T(8,128)S(1)}, f32[8,128,128]{2,1,0:T(8,128)S(1)}, f32[8,128,128]{2,1,0:T(8,128)S(1)},...) custom-call(bf16[4,144,128]{2,1,0:T(8,128)(2,1)S(1)} %get-tuple-element.34.refs_0_, ...), custom_call_target="tpu_custom_call" | custom-call | flops 2000000000 | bytes 4000000 | tf_op jit(solution)/shard_map/keys/pallas_call | solution.py:275
  16.2 0.0 collective-permute-done.5.refs_2_
  16.3 1.5 %collective-permute-done.6.refs_3_ = bf16[2,256,128]{2,1,0:T(8,128)(2,1)S(1)} collective-permute-done((bf16[2,256,128]{2,1,0:T(8,128)(2,1)S(1)}, bf16[2,256,128]{2,1,0:T(8,128)(2,1)S(1)}, u32[]{:S(2)}, u32[]{:S(2)}) %collective-permute-start.6) | collective-permute-done | bytes 131104 | tf_op jit(solution)/shard_map/ppermute | solution.py:593
  17.8 1.9 %collective-permute-done.7.refs_4_ = bf16[2,256,128]{2,1,0:T(8,128)(2,1)S(1)} collective-permute-done((bf16[2,256,128]{2,1,0:T(8,128)(2,1)S(1)}, bf16[2,256,128]{2,1,0:T(8,128)(2,1)S(1)}, u32[]{:S(2)}, u32[]{:S(2)}) %collective-permute-start.7) | collective-permute-done | bytes 131104 | tf_op jit(solution)/shard_map/ppermute | solution.py:593
  19.7 0.0 slice-start
  19.7 1.0 %values.1 = (bf16[8,256,128]{2,1,0:T(8,128)(2,1)S(1)}, f32[8,128,256]{2,1,0:T(8,128)S(1)}, bf16[128,256]{1,0:T(8,128)(2,1)S(1)}, f32[7,128,256]{2,1,0:T(8,128)S(1)}) custom-call(bf16[4,256,128]{2,1,0:T(8,128)(2,1)S(1)} %get-tuple-element.37.refs_0_, bf16[4,256,128]{2,1,0:T(8,128)(2,1)S(1)} %collective-permute-done.4.refs_1_, ...), custom_call_target="tpu_custom_call" | custom-call | flops 1000000000 | bytes 4000000 | tf_op jit(solution)/shard_map/values/pallas_call | solution.py:290
  20.7 3.5 %collective-permute-start.9 = (bf16[128,256]{1,0:T(8,128)(2,1)S(1)}, bf16[128,256]{1,0:T(8,128)(2,1)S(1)}, u32[]{:S(2)}, u32[]{:S(2)}) collective-permute-start(bf16[128,256]{1,0:T(8,128)(2,1)S(1)} %get-tuple-element.47.own_ref), channel_id=1, source_target_pairs={{0,64},{4,68},{8,72},{12,76},{16,80},{20,84},{24,88},{28,92},{32,9... | collective-permute-start | bytes 196616 | tf_op jit(solution)/shard_map/ppermute | solution.py:614
  24.3 2.9 %collective-permute-start.8 = (bf16[128,256]{1,0:T(8,128)(2,1)S(1)}, bf16[128,256]{1,0:T(8,128)(2,1)S(1)}, u32[]{:S(2)}, u32[]{:S(2)}) collective-permute-start(bf16[128,256]{1,0:T(8,128)(2,1)S(1)} %get-tuple-element.47.own_ref), channel_id=1, source_target_pairs={{0,32},{4,36},{8,40},{12,44},{16,48},{20,52},{24,56},{28,60},{32,6... | collective-permute-start | bytes 196616 | tf_op jit(solution)/shard_map/ppermute | solution.py:614
  27.2 1.9 %collective-permute-done.9.two_ref = bf16[128,256]{1,0:T(8,128)(2,1)S(1)} collective-permute-done((bf16[128,256]{1,0:T(8,128)(2,1)S(1)}, bf16[128,256]{1,0:T(8,128)(2,1)S(1)}, u32[]{:S(2)}, u32[]{:S(2)}) %collective-permute-start.9) | collective-permute-done | bytes 65568 | tf_op jit(solution)/shard_map/ppermute | solution.py:614
  29.1 2.5 %collective-permute-done.8.one_ref = bf16[128,256]{1,0:T(8,128)(2,1)S(1)} collective-permute-done((bf16[128,256]{1,0:T(8,128)(2,1)S(1)}, bf16[128,256]{1,0:T(8,128)(2,1)S(1)}, u32[]{:S(2)}, u32[]{:S(2)}) %collective-permute-start.8) | collective-permute-done | bytes 65568 | tf_op jit(solution)/shard_map/ppermute | solution.py:614
  31.6 0.3 combine.1
  31.9 1.9 %collective-permute-start.11 = (bf16[128,256]{1,0:T(8,128)(2,1)S(1)}, bf16[128,256]{1,0:T(8,128)(2,1)S(1)}, u32[]{:S(2)}, u32[]{:S(2)}) collective-permute-start(bf16[128,256]{1,0:T(8,128)(2,1)S(1)} %get-tuple-element.49), channel_id=1, source_target_pairs={{0,96},{4,100},{8,104},{12,108},{16,112},{20,116},{24,120},{28,124... | collective-permute-start | bytes 196616 | tf_op jit(solution)/shard_map/ppermute | solution.py:614
  33.9 0.7 collective-permute-start.10
  34.5 1.3 %query.1.no_ref = f32[1024,256]{1,0:T(8,128)S(1)} custom-call(bf16[8,144,128]{2,1,0:T(8,128)(2,1)S(1)} %get-tuple-element.36.refs_5_.refs_0_, bf16[8,256,128]{2,1,0:T(8,128)(2,1)S(1)} %get-tuple-element.43.refs_1_, f32[8,128,128]{2,1,0:T(8,128)S(1)} %get-tuple-element.44.refs_2_, f32[8,128,256]{2,1,0:T(8,128)S(1)} %get-tuple-element.45.refs_3_, ...), custom_call_target="tpu_custom_call" | custom-call | flops 1000000000 | bytes 4000000 | tf_op jit(solution)/shard_map/query/pallas_call | solution.py:345
  35.8 5.3 %collective-permute-done.11.three_ref = bf16[128,256]{1,0:T(8,128)(2,1)S(1)} collective-permute-done((bf16[128,256]{1,0:T(8,128)(2,1)S(1)}, bf16[128,256]{1,0:T(8,128)(2,1)S(1)}, u32[]{:S(2)}, u32[]{:S(2)}) %collective-permute-start.11) | collective-permute-done | bytes 65568 | tf_op jit(solution)/shard_map/ppermute | solution.py:614
  41.1 0.0 collective-permute-done.10.six_ref
  41.1 0.0 copy-done
  41.1 0.7 norm.1.normed_ref
  41.9 2.3 %collective-permute-start.12 = (bf16[1024,128]{1,0:T(8,128)(2,1)S(1)}, bf16[1024,128]{1,0:T(8,128)(2,1)S(1)}, u32[]{:S(2)}, u32[]{:S(2)}) collective-permute-start(bf16[1024,128]{1,0:T(8,128)(2,1)S(1)} %norm.1.normed_ref), channel_id=1, source_target_pairs={{0,32},{4,36},{8,40},{12,44},{16,48},{20,52},{24,56},{28,60},{32,6... | collective-permute-start | bytes 786440 | tf_op jit(solution)/shard_map/ppermute | solution.py:614
  44.1 0.0 copy-done.1
  44.1 1.3 %own.1 = (f32[1024,128]{1,0:T(8,128)S(1)}, f32[2,1024,128]{2,1,0:T(8,128)S(1)}, bf16[1024,128]{1,0:T(8,128)(2,1)S(1)}) custom-call(bf16[1024,128]{1,0:T(8,128)(2,1)S(1)} %norm.1.normed_ref, bf16[8,128,384]{2,1,0:T(8,128)(2,1)S(1)} %copy-done.1), custom_call_target="tpu_custom_call" | custom-call | flops 1000000000 | bytes 3000000 | tf_op jit(solution)/shard_map/own/pallas_call | solution.py:466
  45.4 6.0 %collective-permute-done.12.halo_ref = bf16[1024,128]{1,0:T(8,128)(2,1)S(1)} collective-permute-done((bf16[1024,128]{1,0:T(8,128)(2,1)S(1)}, bf16[1024,128]{1,0:T(8,128)(2,1)S(1)}, u32[]{:S(2)}, u32[]{:S(2)}) %collective-permute-start.12) | collective-permute-done | bytes 262176 | tf_op jit(solution)/shard_map/ppermute | solution.py:614
  51.5 1.5 %halo.1 = (bf16[2,128,128]{2,1,0:T(8,128)(2,1)S(1)}, bf16[2,128,128]{2,1,0:T(8,128)(2,1)S(1)}, bf16[2,128,128]{2,1,0:T(8,128)(2,1)S(1)}, bf16[2,128,128]{2,1,0:T(8,128)(2,1)S(1)}) custom-call(bf16[1024,128]{1,0:T(8,128)(2,1)S(1)} %collective-permute-done.12.halo_ref, bf16[8,128,384]{2,1,0:T(8,128)(2,1)S(1)} %copy-done.1, ...), custom_call_target="tpu_custom_call" | custom-call | flops 1000000000 | bytes 3000000 | tf_op jit(solution)/shard_map/halo/pallas_call | solution.py:517
  53.0 0.2 collective-permute-start.15
  53.2 1.8 %collective-permute-start.13 = (bf16[2,128,128]{2,1,0:T(8,128)(2,1)S(1)}, bf16[2,128,128]{2,1,0:T(8,128)(2,1)S(1)}, u32[]{:S(2)}, u32[]{:S(2)}) collective-permute-start(bf16[2,128,128]{2,1,0:T(8,128)(2,1)S(1)} %get-tuple-element.53), channel_id=1, source_target_pairs={{0,24},{4,28},{8,16},{12,20},{16,8},{20,12},{24,0},{28,4},{32,56},... | collective-permute-start | bytes 196616 | tf_op jit(solution)/shard_map/ppermute | solution.py:593
  55.0 1.5 %collective-permute-start.18 = (bf16[2,128,128]{2,1,0:T(8,128)(2,1)S(1)}, bf16[2,128,128]{2,1,0:T(8,128)(2,1)S(1)}, u32[]{:S(2)}, u32[]{:S(2)}) collective-permute-start(bf16[2,128,128]{2,1,0:T(8,128)(2,1)S(1)} %get-tuple-element.58), channel_id=1, source_target_pairs={{0,8},{4,12},{8,0},{12,4},{16,24},{20,28},{24,16},{28,20},{32,40},... | collective-permute-start | bytes 196616 | tf_op jit(solution)/shard_map/ppermute | solution.py:593
  56.5 2.4 %collective-permute-done.15.two = bf16[2,128,128]{2,1,0:T(8,128)(2,1)S(1)} collective-permute-done((bf16[2,128,128]{2,1,0:T(8,128)(2,1)S(1)}, bf16[2,128,128]{2,1,0:T(8,128)(2,1)S(1)}, u32[]{:S(2)}, u32[]{:S(2)}) %collective-permute-start.15) | collective-permute-done | bytes 65568 | tf_op jit(solution)/shard_map/ppermute | solution.py:593
  58.9 0.1 collective-permute-start.17
  59.0 0.5 collective-permute-start.16
  59.5 0.0 collective-permute-done.18.one
  59.5 0.1 collective-permute-start.19
  59.7 0.0 collective-permute-done.13.three
  59.7 0.4 collective-permute-start.14
  60.1 0.2 collective-permute-done.17.two_came
  60.2 0.2 collective-permute-done.16.own_came
  60.4 0.4 collective-permute-done.19.one_came
  60.7 0.0 slice-done
  60.7 0.0 slice-done.1
  60.7 1.0 %early.1.acc_ref = f32[128,4096]{1,0:T(8,128)S(1)} custom-call(bf16[2,128,128]{2,1,0:T(8,128)(2,1)S(1)} %get-tuple-element.56.own_pair, bf16[128,128]{1,0:T(8,128)(2,1)S(1)} %collective-permute-done.16.own_came, bf16[2,128,128]{2,1,0:T(8,128)(2,1)S(1)} %collective-permute-done.15.two, bf16[128,128]{1,0:T(8,128)(2,1)S(1)} %collective-permute-done.17.two_came, ...), custom_call_target="tpu_custom_call" | custom-call | flops 800000000 | bytes 8000000 | tf_op jit(solution)/shard_map/early/pallas_call | solution.py:571
  61.7 0.0 collective-permute-done.14.three_came
  61.8 0.5 late.1
  62.2 1.7 %collective-permute-start.20 = (bf16[32,4096]{1,0:T(8,128)(2,1)S(1)}, bf16[32,4096]{1,0:T(8,128)(2,1)S(1)}, u32[]{:S(2)}, u32[]{:S(2)}) collective-permute-start(bf16[32,4096]{1,0:T(8,128)(2,1)S(1)} %get-tuple-element.60), channel_id=1, source_target_pairs={{0,1},{1,0},{2,3},{3,2},{4,5},{5,4},{6,7},{7,6},{8,9},{9,8},{10,11... | collective-permute-start | bytes 786440 | tf_op jit(solution)/shard_map/ppermute | solution.py:636
  63.9 2.2 %collective-permute-start.21 = (bf16[32,4096]{1,0:T(8,128)(2,1)S(1)}, bf16[32,4096]{1,0:T(8,128)(2,1)S(1)}, u32[]{:S(2)}, u32[]{:S(2)}) collective-permute-start(bf16[32,4096]{1,0:T(8,128)(2,1)S(1)} %get-tuple-element.61), channel_id=1, source_target_pairs={{0,3},{1,2},{2,1},{3,0},{4,7},{5,6},{6,5},{7,4},{8,11},{9,10},{10,... | collective-permute-start | bytes 786440 | tf_op jit(solution)/shard_map/ppermute | solution.py:636
  66.1 0.7 collective-permute-start.22
  66.8 4.7 %collective-permute-done.20 = bf16[32,4096]{1,0:T(8,128)(2,1)S(1)} collective-permute-done((bf16[32,4096]{1,0:T(8,128)(2,1)S(1)}, bf16[32,4096]{1,0:T(8,128)(2,1)S(1)}, u32[]{:S(2)}, u32[]{:S(2)}) %collective-permute-start.20) | collective-permute-done | bytes 262176 | tf_op jit(solution)/shard_map/ppermute | solution.py:636
  71.5 5.8 %collective-permute-done.21 = bf16[32,4096]{1,0:T(8,128)(2,1)S(1)} collective-permute-done((bf16[32,4096]{1,0:T(8,128)(2,1)S(1)}, bf16[32,4096]{1,0:T(8,128)(2,1)S(1)}, u32[]{:S(2)}, u32[]{:S(2)}) %collective-permute-start.21) | collective-permute-done | bytes 262176 | tf_op jit(solution)/shard_map/ppermute | solution.py:636
  77.3 1.5 %collective-permute-done.22 = bf16[32,4096]{1,0:T(8,128)(2,1)S(1)} collective-permute-done((bf16[32,4096]{1,0:T(8,128)(2,1)S(1)}, bf16[32,4096]{1,0:T(8,128)(2,1)S(1)}, u32[]{:S(2)}, u32[]{:S(2)}) %collective-permute-start.22) | collective-permute-done | bytes 262176 | tf_op jit(solution)/shard_map/ppermute | solution.py:636
  78.8 0.8 %add_convert_fusion = bf16[32,4096]{1,0:T(8,128)(2,1)} fusion(bf16[32,4096]{1,0:T(8,128)(2,1)S(1)} %collective-permute-done.22, bf16[32,4096]{1,0:T(8,128)(2,1)S(1)} %collective-permute-done.21, f32[32,4096]{1,0:T(8,128)S(1)} %get-tuple-element.59, bf16[32,4096]{1,0:T(8,128)(2,1)S(1)} %collective-permute-done.20), kind=kLoop, calls=%fused_computation | loop fusion | flops 917504 | bytes 1572864 | tf_op jit(solution)/shard_map/convert_element_type | solution.py:640
  (16 shorter events, 0.1 us)
Async XLA Ops:
  1.4 1.5 %collective-permute-start = (bf16[4,144,128]{2,1,0:T(8,128)(2,1)S(1)}, bf16[4,144,128]{2,1,0:T(8,128)(2,1)S(1)}, u32[]{:S(2)}, u32[]{:S(2)}) collective-permute-start(bf16[4,144,128]{2,1,0:T(8,128)(2,1)S(1)} %get-tuple-element.35), channel_id=1, source_target_pairs={{0,4},{4,0},{8,12},{12,8},{16,20},{20,16},{24,28},{28,24},{32,36},... | collective-permute-start | bytes 442376 | tf_op jit(solution)/shard_map/ppermute | solution.py:593
  1.5 6.4 %collective-permute-start.4 = (bf16[4,256,128]{2,1,0:T(8,128)(2,1)S(1)}, bf16[4,256,128]{2,1,0:T(8,128)(2,1)S(1)}, u32[]{:S(2)}, u32[]{:S(2)}) collective-permute-start(bf16[4,256,128]{2,1,0:T(8,128)(2,1)S(1)} %get-tuple-element.38), channel_id=1, source_target_pairs={{0,4},{4,0},{8,12},{12,8},{16,20},{20,16},{24,28},{28,24},{32,36},... | collective-permute-start | bytes 786440 | tf_op jit(solution)/shard_map/ppermute | solution.py:593
  2.9 9.5 %collective-permute-start.1 = (bf16[2,144,128]{2,1,0:T(8,128)(2,1)S(1)}, bf16[2,144,128]{2,1,0:T(8,128)(2,1)S(1)}, u32[]{:S(2)}, u32[]{:S(2)}) collective-permute-start(bf16[2,144,128]{2,1,0:T(8,128)(2,1)S(1)} %pad_maximum_fusion.3), channel_id=1, source_target_pairs={{0,8},{4,12},{8,0},{12,4},{16,24},{20,28},{24,16},{28,20},{32,40},... | collective-permute-start | bytes 221192 | tf_op jit(solution)/shard_map/ppermute | solution.py:593
  4.4 8.5 %collective-permute-start.2 = (bf16[2,144,128]{2,1,0:T(8,128)(2,1)S(1)}, bf16[2,144,128]{2,1,0:T(8,128)(2,1)S(1)}, u32[]{:S(2)}, u32[]{:S(2)}) collective-permute-start(bf16[2,144,128]{2,1,0:T(8,128)(2,1)S(1)} %pad_maximum_fusion.4), channel_id=1, source_target_pairs={{0,16},{4,20},{8,24},{12,28},{16,0},{20,4},{24,8},{28,12},{32,48},... | collective-permute-start | bytes 221192 | tf_op jit(solution)/shard_map/ppermute | solution.py:593
  7.3 33.8 %copy-start = (f32[128]{0:T(128)S(1)}, f32[128]{0:T(128)}, u32[]{:S(2)}) copy-start(f32[128]{0:T(128)} %param.13) | copy-start | bytes 1540
  7.3 5.7 %collective-permute-start.3 = (bf16[2,144,128]{2,1,0:T(8,128)(2,1)S(1)}, bf16[2,144,128]{2,1,0:T(8,128)(2,1)S(1)}, u32[]{:S(2)}, u32[]{:S(2)}) collective-permute-start(bf16[2,144,128]{2,1,0:T(8,128)(2,1)S(1)} %pad_maximum_fusion.5), channel_id=1, source_target_pairs={{0,24},{4,28},{8,16},{12,20},{16,8},{20,12},{24,0},{28,4},{32,56},... | collective-permute-start | bytes 221192 | tf_op jit(solution)/shard_map/ppermute | solution.py:593
  7.9 8.3 %collective-permute-start.5 = (bf16[2,256,128]{2,1,0:T(8,128)(2,1)S(1)}, bf16[2,256,128]{2,1,0:T(8,128)(2,1)S(1)}, u32[]{:S(2)}, u32[]{:S(2)}) collective-permute-start(bf16[2,256,128]{2,1,0:T(8,128)(2,1)S(1)} %pad_maximum_fusion), channel_id=1, source_target_pairs={{0,8},{4,12},{8,0},{12,4},{16,24},{20,28},{24,16},{28,20},{32,40},... | collective-permute-start | bytes 393224 | tf_op jit(solution)/shard_map/ppermute | solution.py:593
  8.3 9.5 %collective-permute-start.6 = (bf16[2,256,128]{2,1,0:T(8,128)(2,1)S(1)}, bf16[2,256,128]{2,1,0:T(8,128)(2,1)S(1)}, u32[]{:S(2)}, u32[]{:S(2)}) collective-permute-start(bf16[2,256,128]{2,1,0:T(8,128)(2,1)S(1)} %pad_maximum_fusion.1), channel_id=1, source_target_pairs={{0,16},{4,20},{8,24},{12,28},{16,0},{20,4},{24,8},{28,12},{32,48},... | collective-permute-start | bytes 393224 | tf_op jit(solution)/shard_map/ppermute | solution.py:593
  12.3 31.8 %copy-start.1 = (bf16[8,128,384]{2,1,0:T(8,128)(2,1)S(1)}, bf16[8,128,384]{2,1,0:T(8,128)(2,1)}, u32[]{:S(2)}) copy-start(bf16[8,128,384]{2,1,0:T(8,128)(2,1)} %weight_ref.5) | copy-start | bytes 2359300
  12.3 7.3 %collective-permute-start.7 = (bf16[2,256,128]{2,1,0:T(8,128)(2,1)S(1)}, bf16[2,256,128]{2,1,0:T(8,128)(2,1)S(1)}, u32[]{:S(2)}, u32[]{:S(2)}) collective-permute-start(bf16[2,256,128]{2,1,0:T(8,128)(2,1)S(1)} %pad_maximum_fusion.2), channel_id=1, source_target_pairs={{0,24},{4,28},{8,16},{12,20},{16,8},{20,12},{24,0},{28,4},{32,56},... | collective-permute-start | bytes 393224 | tf_op jit(solution)/shard_map/ppermute | solution.py:593
  19.7 41.1 %slice-start = ((s8[8388608]{0:T(1024)(128)(4,1)}), s8[4194304]{0:T(1024)(128)(4,1)S(1)}, s32[]{:S(2)}) async-start(s8[8388608]{0:T(1024)(128)(4,1)} %bitcast.9), calls=%async_computation | async-start | bytes 8388608
  20.7 8.4 %collective-permute-start.9 = (bf16[128,256]{1,0:T(8,128)(2,1)S(1)}, bf16[128,256]{1,0:T(8,128)(2,1)S(1)}, u32[]{:S(2)}, u32[]{:S(2)}) collective-permute-start(bf16[128,256]{1,0:T(8,128)(2,1)S(1)} %get-tuple-element.47.own_ref), channel_id=1, source_target_pairs={{0,64},{4,68},{8,72},{12,76},{16,80},{20,84},{24,88},{28,92},{32,9... | collective-permute-start | bytes 196616 | tf_op jit(solution)/shard_map/ppermute | solution.py:614
  24.3 7.4 %collective-permute-start.8 = (bf16[128,256]{1,0:T(8,128)(2,1)S(1)}, bf16[128,256]{1,0:T(8,128)(2,1)S(1)}, u32[]{:S(2)}, u32[]{:S(2)}) collective-permute-start(bf16[128,256]{1,0:T(8,128)(2,1)S(1)} %get-tuple-element.47.own_ref), channel_id=1, source_target_pairs={{0,32},{4,36},{8,40},{12,44},{16,48},{20,52},{24,56},{28,60},{32,6... | collective-permute-start | bytes 196616 | tf_op jit(solution)/shard_map/ppermute | solution.py:614
  31.9 9.2 %collective-permute-start.11 = (bf16[128,256]{1,0:T(8,128)(2,1)S(1)}, bf16[128,256]{1,0:T(8,128)(2,1)S(1)}, u32[]{:S(2)}, u32[]{:S(2)}) collective-permute-start(bf16[128,256]{1,0:T(8,128)(2,1)S(1)} %get-tuple-element.49), channel_id=1, source_target_pairs={{0,96},{4,100},{8,104},{12,108},{16,112},{20,116},{24,120},{28,124... | collective-permute-start | bytes 196616 | tf_op jit(solution)/shard_map/ppermute | solution.py:614
  33.9 7.2 %collective-permute-start.10 = (bf16[128,256]{1,0:T(8,128)(2,1)S(1)}, bf16[128,256]{1,0:T(8,128)(2,1)S(1)}, u32[]{:S(2)}, u32[]{:S(2)}) collective-permute-start(bf16[128,256]{1,0:T(8,128)(2,1)S(1)} %get-tuple-element.49), channel_id=1, source_target_pairs={{0,192},{4,196},{8,200},{12,204},{16,208},{20,212},{24,216},{28,22... | collective-permute-start | bytes 196616 | tf_op jit(solution)/shard_map/ppermute | solution.py:614
  41.1 19.6 %slice-start.1 = ((s8[8388608]{0:T(1024)(128)(4,1)}), s8[4194304]{0:T(1024)(128)(4,1)S(1)}, s32[]{:S(2)}) async-start(s8[8388608]{0:T(1024)(128)(4,1)} %bitcast.9), calls=%async_computation.1 | async-start | bytes 8388608
  41.9 9.6 %collective-permute-start.12 = (bf16[1024,128]{1,0:T(8,128)(2,1)S(1)}, bf16[1024,128]{1,0:T(8,128)(2,1)S(1)}, u32[]{:S(2)}, u32[]{:S(2)}) collective-permute-start(bf16[1024,128]{1,0:T(8,128)(2,1)S(1)} %norm.1.normed_ref), channel_id=1, source_target_pairs={{0,32},{4,36},{8,40},{12,44},{16,48},{20,52},{24,56},{28,60},{32,6... | collective-permute-start | bytes 786440 | tf_op jit(solution)/shard_map/ppermute | solution.py:614
  53.0 6.0 %collective-permute-start.15 = (bf16[2,128,128]{2,1,0:T(8,128)(2,1)S(1)}, bf16[2,128,128]{2,1,0:T(8,128)(2,1)S(1)}, u32[]{:S(2)}, u32[]{:S(2)}) collective-permute-start(bf16[2,128,128]{2,1,0:T(8,128)(2,1)S(1)} %get-tuple-element.55), channel_id=1, source_target_pairs={{0,16},{4,20},{8,24},{12,28},{16,0},{20,4},{24,8},{28,12},{32,48},... | collective-permute-start | bytes 196616 | tf_op jit(solution)/shard_map/ppermute | solution.py:593
  53.2 6.5 %collective-permute-start.13 = (bf16[2,128,128]{2,1,0:T(8,128)(2,1)S(1)}, bf16[2,128,128]{2,1,0:T(8,128)(2,1)S(1)}, u32[]{:S(2)}, u32[]{:S(2)}) collective-permute-start(bf16[2,128,128]{2,1,0:T(8,128)(2,1)S(1)} %get-tuple-element.53), channel_id=1, source_target_pairs={{0,24},{4,28},{8,16},{12,20},{16,8},{20,12},{24,0},{28,4},{32,56},... | collective-permute-start | bytes 196616 | tf_op jit(solution)/shard_map/ppermute | solution.py:593
  55.0 4.5 %collective-permute-start.18 = (bf16[2,128,128]{2,1,0:T(8,128)(2,1)S(1)}, bf16[2,128,128]{2,1,0:T(8,128)(2,1)S(1)}, u32[]{:S(2)}, u32[]{:S(2)}) collective-permute-start(bf16[2,128,128]{2,1,0:T(8,128)(2,1)S(1)} %get-tuple-element.58), channel_id=1, source_target_pairs={{0,8},{4,12},{8,0},{12,4},{16,24},{20,28},{24,16},{28,20},{32,40},... | collective-permute-start | bytes 196616 | tf_op jit(solution)/shard_map/ppermute | solution.py:593
  58.9 1.3 %collective-permute-start.17 = (bf16[128,128]{1,0:T(8,128)(2,1)S(1)}, bf16[128,128]{1,0:T(8,128)(2,1)S(1)}, u32[]{:S(2)}, u32[]{:S(2)}) collective-permute-start(bf16[128,128]{1,0:T(8,128)(2,1)S(1)} %slice_bitcast_fusion.2), channel_id=1, source_target_pairs={{0,4},{4,0},{8,12},{12,8},{16,20},{20,16},{24,28},{28,24},{32,36},... | collective-permute-start | bytes 98312 | tf_op jit(solution)/shard_map/ppermute | solution.py:593
  59.0 1.4 %collective-permute-start.16 = (bf16[128,128]{1,0:T(8,128)(2,1)S(1)}, bf16[128,128]{1,0:T(8,128)(2,1)S(1)}, u32[]{:S(2)}, u32[]{:S(2)}) collective-permute-start(bf16[128,128]{1,0:T(8,128)(2,1)S(1)} %slice_bitcast_fusion.3), channel_id=1, source_target_pairs={{0,4},{4,0},{8,12},{12,8},{16,20},{20,16},{24,28},{28,24},{32,36},... | collective-permute-start | bytes 98312 | tf_op jit(solution)/shard_map/ppermute | solution.py:593
  59.5 1.2 %collective-permute-start.19 = (bf16[128,128]{1,0:T(8,128)(2,1)S(1)}, bf16[128,128]{1,0:T(8,128)(2,1)S(1)}, u32[]{:S(2)}, u32[]{:S(2)}) collective-permute-start(bf16[128,128]{1,0:T(8,128)(2,1)S(1)} %slice_bitcast_fusion), channel_id=1, source_target_pairs={{0,4},{4,0},{8,12},{12,8},{16,20},{20,16},{24,28},{28,24},{32,36},... | collective-permute-start | bytes 98312 | tf_op jit(solution)/shard_map/ppermute | solution.py:593
  59.7 2.1 %collective-permute-start.14 = (bf16[128,128]{1,0:T(8,128)(2,1)S(1)}, bf16[128,128]{1,0:T(8,128)(2,1)S(1)}, u32[]{:S(2)}, u32[]{:S(2)}) collective-permute-start(bf16[128,128]{1,0:T(8,128)(2,1)S(1)} %slice_bitcast_fusion.1), channel_id=1, source_target_pairs={{0,4},{4,0},{8,12},{12,8},{16,20},{20,16},{24,28},{28,24},{32,36},... | collective-permute-start | bytes 98312 | tf_op jit(solution)/shard_map/ppermute | solution.py:593
  62.2 9.2 %collective-permute-start.20 = (bf16[32,4096]{1,0:T(8,128)(2,1)S(1)}, bf16[32,4096]{1,0:T(8,128)(2,1)S(1)}, u32[]{:S(2)}, u32[]{:S(2)}) collective-permute-start(bf16[32,4096]{1,0:T(8,128)(2,1)S(1)} %get-tuple-element.60), channel_id=1, source_target_pairs={{0,1},{1,0},{2,3},{3,2},{4,5},{5,4},{6,7},{7,6},{8,9},{9,8},{10,11... | collective-permute-start | bytes 786440 | tf_op jit(solution)/shard_map/ppermute | solution.py:636
  63.9 13.4 %collective-permute-start.21 = (bf16[32,4096]{1,0:T(8,128)(2,1)S(1)}, bf16[32,4096]{1,0:T(8,128)(2,1)S(1)}, u32[]{:S(2)}, u32[]{:S(2)}) collective-permute-start(bf16[32,4096]{1,0:T(8,128)(2,1)S(1)} %get-tuple-element.61), channel_id=1, source_target_pairs={{0,3},{1,2},{2,1},{3,0},{4,7},{5,6},{6,5},{7,4},{8,11},{9,10},{10,... | collective-permute-start | bytes 786440 | tf_op jit(solution)/shard_map/ppermute | solution.py:636
  66.1 12.7 %collective-permute-start.22 = (bf16[32,4096]{1,0:T(8,128)(2,1)S(1)}, bf16[32,4096]{1,0:T(8,128)(2,1)S(1)}, u32[]{:S(2)}, u32[]{:S(2)}) collective-permute-start(bf16[32,4096]{1,0:T(8,128)(2,1)S(1)} %get-tuple-element.62), channel_id=1, source_target_pairs={{0,2},{1,3},{2,0},{3,1},{4,6},{5,7},{6,4},{7,5},{8,10},{9,11},{10,... | collective-permute-start | bytes 786440 | tf_op jit(solution)/shard_map/ppermute | solution.py:636

commit v9 on v8

--- a/solution.py
+++ b/solution.py
@@ -125,10 +125,10 @@
     )(*[pltpu.with_memory_space_constraint(x, pltpu.HBM) for x in (q, k, v, decay, beta)])
 
 
-def gather_slots(refs, out_ref):
+def gather_slots(refs, out_ref, part=None):
     keep, came = refs[0], refs[1]
-    out_ref[0] = keep[0]
-    out_ref[1] = came[0]
+    out_ref[0] = keep[0] if part is None else keep[0, part, :]
+    out_ref[1] = came[0] if part is None else came[0, part, :]
     for dx in range(1, 4):
         out_ref[2 * dx] = refs[dx + 1][0]
         out_ref[2 * dx + 1] = refs[dx + 1][1]
@@ -242,13 +242,12 @@
 
 
 def value_kernel(*refs):
-    k_ref, inverse_ref, w_ref, tail_ref, reach_ref, vq_ref, wu_ref, ab_ref, level_ref, states = (
-        refs[5:]
-    )
+    k_ref, inverse_ref, w_ref, tail_ref, reach_ref = refs[5:10]
+    wu_ref, ab_ref, level_ref, states, v_ref = refs[10:]
     me = lax.axis_index("seq") % PLANE
-    gather_slots(refs[:5], vq_ref)
+    gather_slots(refs[:5], v_ref, slice(0, C))
     every = range(PLANE)
-    u = [mm_exact_right(inverse_ref[d], vq_ref[d, 0:C, :]) for d in every]
+    u = [mm_exact_right(inverse_ref[d], v_ref[d]) for d in every]
     halves = []
     for d in every:
         wu_ref[d, :, :C] = w_ref[d]
@@ -290,14 +289,13 @@
     return pl.pallas_call(
         value_kernel,
         out_shape=[
-            jax.ShapeDtypeStruct((PLANE, 2 * C, C), BF16),
             jax.ShapeDtypeStruct((PLANE, C, 2 * C), F32),
             jax.ShapeDtypeStruct((C, 2 * C), BF16),
             jax.ShapeDtypeStruct((7, C, 2 * C), F32),
         ],
         in_specs=[vmem()] * 10,
-        out_specs=[vmem()] * 4,
-        scratch_shapes=[pltpu.VMEM((PLANE, C, C), F32)],
+        out_specs=[vmem()] * 3,
+        scratch_shapes=[pltpu.VMEM((PLANE, C, C), F32), pltpu.VMEM((PLANE, C, C), BF16)],
         compiler_params=params(),
         cost_estimate=cost(1e9, 4e6),
         name="values",
@@ -305,7 +303,8 @@
 
 
 def query_kernel(*refs):
-    k_ref, vq_ref, mix_ref, wu_ref, level_ref, no_ref, before = refs
+    k_ref, mix_ref, wu_ref, level_ref, no_ref, before, q_ref = refs[5:]
+    gather_slots(refs[:5], q_ref, slice(C, 2 * C))
     me = lax.axis_index("seq") % PLANE
     row, col = iotas()
     before[0] = jnp.concatenate([jnp.where(row == col, 1.0, 0.0), jnp.zeros((C, C), F32)], axis=1)
@@ -320,7 +319,7 @@
 
     every = range(PLANE)
     found = gates(k_ref)
-    queries = [vq_ref[d, C : 2 * C, :] for d in every]
+    queries = [q_ref[d] for d in every]
     scored = [dot_nt(queries[d], k_ref[d, 0:C, :]) for d in every]
     r_cols = []
     for q in queries:
@@ -341,19 +340,20 @@
         )
 
 
-def query(k, vq, mix, wu, level):
+def query(slots, k, mix, wu, level):
     return pl.pallas_call(
         query_kernel,
         out_shape=jax.ShapeDtypeStruct((PLANE * C, 2 * C), F32),
-        in_specs=[vmem()] * 5,
+        in_specs=[vmem()] * 9,
         out_specs=vmem(),
         scratch_shapes=[
             pltpu.VMEM((PLANE, C, 2 * C), F32),
+            pltpu.VMEM((PLANE, C, C), BF16),
         ],
         compiler_params=params(),
         cost_estimate=cost(1e9, 4e6),
         name="query",
-    )(k, vq, mix, wu, level)
+    )(*slots, k, mix, wu, level)
 
 
 def times(a, x):
@@ -479,7 +479,7 @@
 
 
 def halo_kernel(halo_ref, weight_ref, acc_ref, stat_ref, q2_ref, *refs):
-    outs, attended = refs[:4], refs[4]
+    keep, send, attended = refs
     place = lax.axis_index("seq")
     me, plane = place % PLANE, place // PLANE
     proj = dot(halo_ref[...], weight_ref[me, :, C:]).astype(BF16)
@@ -509,16 +509,17 @@
         attended[rows, :] = (acc / total).astype(BF16)
     for d in range(PLANE):
         chunk = jnp.bitwise_xor(me, d)
-        outs[d // 2][d % 2] = attended[pl.ds(pl.multiple_of(chunk * C, C), C), :]
+        out = send if d % 2 else keep
+        out[d // 2] = attended[pl.ds(pl.multiple_of(chunk * C, C), C), :]
 
 
 def halo_part(halo, weight, acc, stat, q2):
     n = PLANE * C
     return pl.pallas_call(
         halo_kernel,
-        out_shape=[jax.ShapeDtypeStruct((2, C, C), BF16)] * 4,
+        out_shape=[jax.ShapeDtypeStruct((4, C, C), BF16)] * 2,
         in_specs=[vmem()] * 5,
-        out_specs=[vmem()] * 4,
+        out_specs=[vmem()] * 2,
         scratch_shapes=[pltpu.VMEM((n, C), BF16)],
         compiler_params=params(),
         cost_estimate=cost(1e9, 3e6, 6e5),
@@ -542,11 +543,11 @@
     return jnp.concatenate([left, right], axis=1), pl.ds(at, 2 * C)
 
 
-def early_kernel(own_pair, own_came, two, two_came, one, one_came, weight_ref, acc_ref):
+def early_kernel(keep, came, one, two, weight_ref, acc_ref):
     parts = [
-        pair_part(own_pair.at[0], own_came, 0),
-        pair_part(two.at[0], two_came, 2),
-        pair_part(one.at[0], one_came, 1),
+        pair_part(keep.at[0], came.at[0], 0),
+        pair_part(two.at[0], two.at[1], 2),
+        pair_part(one.at[0], one.at[1], 1),
     ]
     for at in range(0, weight_ref.shape[1], COLS):
         cols = slice(at, at + COLS)
@@ -556,8 +557,8 @@
         acc_ref[:, cols] = got
 
 
-def late_kernel(three, three_came, weight_ref, acc_ref, *outs):
-    part, rows = pair_part(three.at[0], three_came, 3)
+def late_kernel(three, weight_ref, acc_ref, *outs):
+    part, rows = pair_part(three.at[0], three.at[1], 3)
     for at in range(0, weight_ref.shape[1], COLS):
         cols = slice(at, at + COLS)
         got = acc_ref[:, cols] + dot(part, weight_ref[rows, cols])
@@ -567,45 +568,41 @@
 
 def project(slots, weight):
     width = weight.shape[1]
-    (own_pair, one, two, three), (own_came, one_came, two_came, three_came) = slots
+    keep, came, one, two, three = slots
     acc = pl.pallas_call(
         early_kernel,
         out_shape=jax.ShapeDtypeStruct((C, width), F32),
-        in_specs=[vmem()] * 7,
+        in_specs=[vmem()] * 5,
         out_specs=vmem(),
         compiler_params=params(),
         cost_estimate=cost(8e8, 8e6),
         name="early",
-    )(own_pair, own_came, two, two_came, one, one_came, weight)
+    )(keep, came, one, two, weight)
     return pl.pallas_call(
         late_kernel,
         out_shape=[jax.ShapeDtypeStruct((32, width), F32)]
         + [jax.ShapeDtypeStruct((32, width), BF16)] * 3,
-        in_specs=[vmem()] * 4,
+        in_specs=[vmem()] * 3,
         out_specs=[vmem()] * 4,
         compiler_params=params(),
         cost_estimate=cost(3e8, 4e6),
         name="late",
-    )(three, three_came, weight, acc)
+    )(three, weight, acc)
 
 
 def swap(block, d):
     return lax.ppermute(block, "seq", [(s, s ^ d) for s in range(PLANE * PLANES)])
 
 
+def along_x(keep, came, part=slice(None)):
+    pairs = {}
+    for dx in (2, 1, 3):
+        pairs[dx] = swap(jnp.stack([keep[dx, part], came[dx, part]]), 2 * dx)
+    return [keep, came] + [pairs[dx] for dx in (1, 2, 3)]
+
+
 def exchange(keep, send):
-    came = swap(send, 1)
-    slots = [keep, came]
-    for dx in (2, 1, 3):
-        slots.append((dx, swap(jnp.stack([keep[dx], came[dx]]), 2 * dx)))
-    return slots[:2] + [pair for _, pair in sorted(slots[2:], key=lambda item: item[0])]
-
-
-def exchange_back(pairs):
-    found = {dx: swap(pairs[dx], 2 * dx) for dx in (2, 1, 3)}
-    found[0], found[2] = lax.optimization_barrier((pairs[0], found[2]))
-    came = {dx: swap(found[dx][1], 1) for dx in (2, 0, 1, 3)}
-    return [found[dx] for dx in range(4)], [came[dx] for dx in range(4)]
+    return along_x(keep, swap(send, 1))
 
 
 def later_plane(block, distance):
@@ -617,19 +614,22 @@
 def local(q_delta, k_delta, v_delta, decay, beta, gain, attn_weight, out_weight):
     keep_k, send_k, keep, send = pack(q_delta, k_delta, v_delta, decay, beta)
     slots_k = exchange(keep_k, send_k)
-    slots = exchange(keep, send)
+    came = swap(send, 1)
+    slots_v = along_x(keep, came, slice(0, C))
     k, mix, inverse, w, tail, reach = key_part(slots_k)
-    vq, wu, ab, level = value_part(slots, k, inverse, w, tail, reach)
+    wu, ab, level = value_part(slots_v, k, inverse, w, tail, reach)
     one = later_plane(ab, 1)
     two = later_plane(ab, 2)
-    no = query(k, vq, mix, wu, level)
+    keep_q, came_q, _ = lax.optimization_barrier((keep, came, ab))
+    slots_q = along_x(keep_q, came_q, slice(C, 2 * C))
+    no = query(slots_q, k, mix, wu, level)
     before, upto = combine(ab, one, two)
     six = later_plane(upto, 6)
     three = later_plane(upto, 3)
     normed = norm(no, gain[None, :], before, six, three)
     halo = later_plane(normed, 1)
     acc, stat, q2 = own(normed, attn_weight)
-    attended = exchange_back(halo_part(halo, attn_weight, acc, stat, q2))
+    attended = exchange(*halo_part(halo, attn_weight, acc, stat, q2))
     sums = project(attended, out_weight)
     moved = {}
     for d in (2, 1, 3):

time: 80.4 us -> 79.1 us (0.984)
  waiting for transfers between devices: 35.2 us -> 28.7 us
  starting transfers between devices: 31 us -> 36.6 us
    ppermute x15, starting transfers between devices: 15.2 us -> 20.5 us  [swap(): lax.ppermute(block, 'seq', [(s, s ^ d) for s in range(PLANE * PLANES)])]
    ppermute x5, waiting for transfers between devices: 15.8 us -> 11.9 us  [later_plane(): return lax.ppermute(block, 'seq', route)]
    ppermute x3, waiting for transfers between devices: 12 us -> 10.5 us  [local(): moved[d] = lax.ppermute(sums[d], 'heads', [(s, s ^ d) for s in range(4)])]
    ppermute x15, waiting for transfers between devices: 7.37 us -> 6.26 us  [swap(): lax.ppermute(block, 'seq', [(s, s ^ d) for s in range(PLANE * PLANES)])]
  transfers between devices with their start and end apart: 23 -> 23, of which waited for: 14 -> 12; matrix products, arithmetic and copies ran while one was open for 0% -> 0% of each run, Pallas kernels for 9% -> 9%
where the time goes in v9:
time: 79.1 us; the launch traced here: 78.8 us
  starting transfers between devices  36.6 us (46%)
  waiting for transfers between devices  28.7 us (36%)
  Pallas kernels  12.3 us (16%)
  other arithmetic  0.92 us (1%)
    ppermute x15, starting transfers between devices, swap(): lax.ppermute(block, 'seq', [(s, s ^ d) for s in range(PLANE * PLANES)])  20.5 us
    ppermute x5, waiting for transfers between devices, later_plane(): return lax.ppermute(block, 'seq', route)  11.9 us
    ppermute x5, starting transfers between devices, later_plane(): return lax.ppermute(block, 'seq', route)  11.5 us
    ppermute x3, waiting for transfers between devices, local(): moved[d] = lax.ppermute(sums[d], 'heads', [(s, s ^ d) for s in range(4)])  10.5 us
    ppermute x15, waiting for transfers between devices, swap(): lax.ppermute(block, 'seq', [(s, s ^ d) for s in range(PLANE * PLANES)])  6.26 us
    ppermute x3, starting transfers between devices, local(): moved[d] = lax.ppermute(sums[d], 'heads', [(s, s ^ d) for s in range(4)])  4.57 us
    pallas_call x1, Pallas kernels, key_part(): pl.pallas_call(key_kernel, out_shape=[jax.ShapeDtypeStruct((PLANE, KROWS,...  3.3 us
  transfers between devices with their start and end apart: 23, of which 12 were waited for; matrix products, arithmetic and copies ran while one was open for 0% of the time, Pallas kernels for 9%

profile of v9, /device:TPU:128, one launch (start us, length us, event | category | flops | bytes accessed | tf_op | source)
XLA Modules:
  0.0 78.8 jit_solution(8775167652039872605)
XLA Ops:
  0.0 1.4 %pack.1 = (bf16[4,144,128]{2,1,0:T(8,128)(2,1)S(1)}, bf16[4,144,128]{2,1,0:T(8,128)(2,1)S(1)}, bf16[4,256,128]{2,1,0:T(8,128)(2,1)S(1)}, bf16[4,256,128]{2,1,0:T(8,128)(2,1)S(1)}) custom-call(bf16[128,1024]{1,0:T(8,128)(2,1)} %q_ref.1, bf16[128,1024]{1,0:T(8,128)(2,1)} %k_ref.1, bf16[128,1024]{1,0:T(8,128)(2,1)} %v_ref.1, f32[8,128]{1,0:T(8,128)} %decay_ref.1, ...), custom_call_target="tpu_custom_call" | custom-call | tf_op jit(solution)/shard_map/pack/pallas_call | solution.py:113
  1.4 0.1 collective-permute-start.4
  1.5 0.5 collective-permute-start
  2.0 0.8 %collective-permute-done.4.refs_1_ = bf16[4,144,128]{2,1,0:T(8,128)(2,1)S(1)} collective-permute-done((bf16[4,144,128]{2,1,0:T(8,128)(2,1)S(1)}, bf16[4,144,128]{2,1,0:T(8,128)(2,1)S(1)}, u32[]{:S(2)}, u32[]{:S(2)}) %collective-permute-start.4) | collective-permute-done | bytes 147488 | tf_op jit(solution)/shard_map/ppermute | solution.py:594
  2.9 1.6 %collective-permute-start.5 = (bf16[2,144,128]{2,1,0:T(8,128)(2,1)S(1)}, bf16[2,144,128]{2,1,0:T(8,128)(2,1)S(1)}, u32[]{:S(2)}, u32[]{:S(2)}) collective-permute-start(bf16[2,144,128]{2,1,0:T(8,128)(2,1)S(1)} %pad_maximum_fusion), channel_id=1, source_target_pairs={{0,8},{4,12},{8,0},{12,4},{16,24},{20,28},{24,16},{28,20},{32,40},... | collective-permute-start | bytes 221192 | tf_op jit(solution)/shard_map/ppermute | solution.py:594
  4.4 2.8 %collective-permute-start.6 = (bf16[2,144,128]{2,1,0:T(8,128)(2,1)S(1)}, bf16[2,144,128]{2,1,0:T(8,128)(2,1)S(1)}, u32[]{:S(2)}, u32[]{:S(2)}) collective-permute-start(bf16[2,144,128]{2,1,0:T(8,128)(2,1)S(1)} %pad_maximum_fusion.1), channel_id=1, source_target_pairs={{0,16},{4,20},{8,24},{12,28},{16,0},{20,4},{24,8},{28,12},{32,48},... | collective-permute-start | bytes 221192 | tf_op jit(solution)/shard_map/ppermute | solution.py:594
  7.3 0.6 collective-permute-start.7
  7.8 0.0 collective-permute-done.refs_1_
  7.9 0.4 collective-permute-start.1
  8.2 4.0 %collective-permute-start.2 = (bf16[2,128,128]{2,1,0:T(8,128)(2,1)S(1)}, bf16[2,128,128]{2,1,0:T(8,128)(2,1)S(1)}, u32[]{:S(2)}, u32[]{:S(2)}) collective-permute-start(bf16[2,128,128]{2,1,0:T(8,128)(2,1)S(1)} %pad_maximum_fusion.4), channel_id=1, source_target_pairs={{0,16},{4,20},{8,24},{12,28},{16,0},{20,4},{24,8},{28,12},{32,48},... | collective-permute-start | bytes 196616 | tf_op jit(solution)/shard_map/ppermute | solution.py:594
  12.3 0.0 copy-start.1
  12.3 0.0 collective-permute-done.5.refs_2_
  12.3 0.6 collective-permute-start.3
  12.9 0.0 collective-permute-done.6.refs_3_
  12.9 0.8 collective-permute-done.7.refs_4_
  13.6 3.3 %keys.1 = (bf16[8,144,128]{2,1,0:T(8,128)(2,1)S(1)}, f32[8,128,128]{2,1,0:T(8,128)S(1)}, f32[8,128,128]{2,1,0:T(8,128)S(1)}, f32[8,128,128]{2,1,0:T(8,128)S(1)},...) custom-call(bf16[4,144,128]{2,1,0:T(8,128)(2,1)S(1)} %get-tuple-element.33.refs_0_, ...), custom_call_target="tpu_custom_call" | custom-call | flops 2000000000 | bytes 4000000 | tf_op jit(solution)/shard_map/keys/pallas_call | solution.py:274
  16.9 0.0 collective-permute-done.1.refs_2_
  16.9 0.0 collective-permute-done.2.refs_3_
  17.0 0.9 %collective-permute-done.3.refs_4_ = bf16[2,128,128]{2,1,0:T(8,128)(2,1)S(1)} collective-permute-done((bf16[2,128,128]{2,1,0:T(8,128)(2,1)S(1)}, bf16[2,128,128]{2,1,0:T(8,128)(2,1)S(1)}, u32[]{:S(2)}, u32[]{:S(2)}) %collective-permute-start.3) | collective-permute-done | bytes 65568 | tf_op jit(solution)/shard_map/ppermute | solution.py:594
  17.9 1.0 %values.1 = (f32[8,128,256]{2,1,0:T(8,128)S(1)}, bf16[128,256]{1,0:T(8,128)(2,1)S(1)}, f32[7,128,256]{2,1,0:T(8,128)S(1)}) custom-call(bf16[4,256,128]{2,1,0:T(8,128)(2,1)S(1)} %get-tuple-element.41.refs_0_, bf16[4,256,128]{2,1,0:T(8,128)(2,1)S(1)} %collective-permute-done.refs_1_, bf16[2,128,128]{2,1,0:T(8,128)(2,1)S(1)} %collective-permute-done.1.refs_2_, ...), custom_call_target="tpu_custom_call" | custom-call | flops 1000000000 | bytes 4000000 | tf_op jit(solution)/shard_map/values/pallas_call | solution.py:289
  18.9 0.0 slice-start
  18.9 3.6 %collective-permute-start.12 = (bf16[128,256]{1,0:T(8,128)(2,1)S(1)}, bf16[128,256]{1,0:T(8,128)(2,1)S(1)}, u32[]{:S(2)}, u32[]{:S(2)}) collective-permute-start(bf16[128,256]{1,0:T(8,128)(2,1)S(1)} %get-tuple-element.40.own_ref), channel_id=1, source_target_pairs={{0,64},{4,68},{8,72},{12,76},{16,80},{20,84},{24,88},{28,92},{32,9... | collective-permute-start | bytes 196616 | tf_op jit(solution)/shard_map/ppermute | solution.py:611
  22.6 2.9 %collective-permute-start.11 = (bf16[128,256]{1,0:T(8,128)(2,1)S(1)}, bf16[128,256]{1,0:T(8,128)(2,1)S(1)}, u32[]{:S(2)}, u32[]{:S(2)}) collective-permute-start(bf16[128,256]{1,0:T(8,128)(2,1)S(1)} %get-tuple-element.40.own_ref), channel_id=1, source_target_pairs={{0,32},{4,36},{8,40},{12,44},{16,48},{20,52},{24,56},{28,60},{32,6... | collective-permute-start | bytes 196616 | tf_op jit(solution)/shard_map/ppermute | solution.py:611
  25.6 0.1 collective-permute-start.8
  25.7 2.6 %collective-permute-start.9 = (bf16[2,128,128]{2,1,0:T(8,128)(2,1)S(1)}, bf16[2,128,128]{2,1,0:T(8,128)(2,1)S(1)}, u32[]{:S(2)}, u32[]{:S(2)}) collective-permute-start(bf16[2,128,128]{2,1,0:T(8,128)(2,1)S(1)} %pad_maximum_fusion.7), channel_id=1, source_target_pairs={{0,16},{4,20},{8,24},{12,28},{16,0},{20,4},{24,8},{28,12},{32,48},... | collective-permute-start | bytes 196616 | tf_op jit(solution)/shard_map/ppermute | solution.py:594
  28.3 2.2 %collective-permute-start.10 = (bf16[2,128,128]{2,1,0:T(8,128)(2,1)S(1)}, bf16[2,128,128]{2,1,0:T(8,128)(2,1)S(1)}, u32[]{:S(2)}, u32[]{:S(2)}) collective-permute-start(bf16[2,128,128]{2,1,0:T(8,128)(2,1)S(1)} %pad_maximum_fusion.8), channel_id=1, source_target_pairs={{0,24},{4,28},{8,16},{12,20},{16,8},{20,12},{24,0},{28,4},{32,56},... | collective-permute-start | bytes 196616 | tf_op jit(solution)/shard_map/ppermute | solution.py:594
  30.5 0.0 collective-permute-done.12.two_ref
  30.5 0.0 collective-permute-done.11.one_ref
  30.5 0.3 combine.1
  30.9 1.9 %collective-permute-start.14 = (bf16[128,256]{1,0:T(8,128)(2,1)S(1)}, bf16[128,256]{1,0:T(8,128)(2,1)S(1)}, u32[]{:S(2)}, u32[]{:S(2)}) collective-permute-start(bf16[128,256]{1,0:T(8,128)(2,1)S(1)} %get-tuple-element.47), channel_id=1, source_target_pairs={{0,96},{4,100},{8,104},{12,108},{16,112},{20,116},{24,120},{28,124... | collective-permute-start | bytes 196616 | tf_op jit(solution)/shard_map/ppermute | solution.py:611
  32.8 0.8 %collective-permute-start.13 = (bf16[128,256]{1,0:T(8,128)(2,1)S(1)}, bf16[128,256]{1,0:T(8,128)(2,1)S(1)}, u32[]{:S(2)}, u32[]{:S(2)}) collective-permute-start(bf16[128,256]{1,0:T(8,128)(2,1)S(1)} %get-tuple-element.47), channel_id=1, source_target_pairs={{0,192},{4,196},{8,200},{12,204},{16,208},{20,212},{24,216},{28,22... | collective-permute-start | bytes 196616 | tf_op jit(solution)/shard_map/ppermute | solution.py:611
  33.6 0.0 collective-permute-done.8.refs_2_
  33.6 0.0 collective-permute-done.9.refs_3_
  33.7 0.2 collective-permute-done.10.refs_4_
  33.9 1.3 %query.1.no_ref = f32[1024,256]{1,0:T(8,128)S(1)} custom-call(bf16[4,256,128]{2,1,0:T(8,128)(2,1)S(1)} %get-tuple-element.41.refs_0_, bf16[4,256,128]{2,1,0:T(8,128)(2,1)S(1)} %collective-permute-done.refs_1_, bf16[2,128,128]{2,1,0:T(8,128)(2,1)S(1)} %collective-permute-done.8.refs_2_, bf16[2,128,128]{2,1,0:T(8,128)(2,1)S(1)} %collective-permute-done.9.refs_3_, ...), custom_call_target="tpu_custom_call" | custom-call | flops 1000000000 | bytes 4000000 | tf_op jit(solution)/shard_map/query/pallas_call | solution.py:344
  35.2 5.7 %collective-permute-done.14.three_ref = bf16[128,256]{1,0:T(8,128)(2,1)S(1)} collective-permute-done((bf16[128,256]{1,0:T(8,128)(2,1)S(1)}, bf16[128,256]{1,0:T(8,128)(2,1)S(1)}, u32[]{:S(2)}, u32[]{:S(2)}) %collective-permute-start.14) | collective-permute-done | bytes 65568 | tf_op jit(solution)/shard_map/ppermute | solution.py:611
  40.9 0.0 collective-permute-done.13.six_ref
  40.9 0.0 copy-done
  40.9 0.7 norm.1.normed_ref
  41.6 0.0 slice-start.1
  41.6 2.2 %collective-permute-start.15 = (bf16[1024,128]{1,0:T(8,128)(2,1)S(1)}, bf16[1024,128]{1,0:T(8,128)(2,1)S(1)}, u32[]{:S(2)}, u32[]{:S(2)}) collective-permute-start(bf16[1024,128]{1,0:T(8,128)(2,1)S(1)} %norm.1.normed_ref), channel_id=1, source_target_pairs={{0,32},{4,36},{8,40},{12,44},{16,48},{20,52},{24,56},{28,60},{32,6... | collective-permute-start | bytes 786440 | tf_op jit(solution)/shard_map/ppermute | solution.py:611
  43.8 0.0 copy-done.1
  43.8 1.3 %own.1 = (f32[1024,128]{1,0:T(8,128)S(1)}, f32[2,1024,128]{2,1,0:T(8,128)S(1)}, bf16[1024,128]{1,0:T(8,128)(2,1)S(1)}) custom-call(bf16[1024,128]{1,0:T(8,128)(2,1)S(1)} %norm.1.normed_ref, bf16[8,128,384]{2,1,0:T(8,128)(2,1)S(1)} %copy-done.1), custom_call_target="tpu_custom_call" | custom-call | flops 1000000000 | bytes 3000000 | tf_op jit(solution)/shard_map/own/pallas_call | solution.py:466
  45.1 6.3 %collective-permute-done.15.halo_ref = bf16[1024,128]{1,0:T(8,128)(2,1)S(1)} collective-permute-done((bf16[1024,128]{1,0:T(8,128)(2,1)S(1)}, bf16[1024,128]{1,0:T(8,128)(2,1)S(1)}, u32[]{:S(2)}, u32[]{:S(2)}) %collective-permute-start.15) | collective-permute-done | bytes 262176 | tf_op jit(solution)/shard_map/ppermute | solution.py:611
  51.3 1.5 %halo.1 = (bf16[4,128,128]{2,1,0:T(8,128)(2,1)S(1)}, bf16[4,128,128]{2,1,0:T(8,128)(2,1)S(1)}) custom-call(bf16[1024,128]{1,0:T(8,128)(2,1)S(1)} %collective-permute-done.15.halo_ref, bf16[8,128,384]{2,1,0:T(8,128)(2,1)S(1)} %copy-done.1, f32[1024,128]{1,0:T(8,128)S(1)} %get-tuple-element.48.acc_ref, f32[2,1024,128]{2,1,0:T(8,128)S(1)} %get-tuple-element.49.stat_ref, ...), custom_call_target="tpu_custom_call" | custom-call | flops 1000000000 | bytes 3000000 | tf_op jit(solution)/shard_map/halo/pallas_call | solution.py:518
  52.8 0.1 collective-permute-start.16
  53.0 1.3 %collective-permute-done.16.came = bf16[4,128,128]{2,1,0:T(8,128)(2,1)S(1)} collective-permute-done((bf16[4,128,128]{2,1,0:T(8,128)(2,1)S(1)}, bf16[4,128,128]{2,1,0:T(8,128)(2,1)S(1)}, u32[]{:S(2)}, u32[]{:S(2)}) %collective-permute-start.16) | collective-permute-done | bytes 131104 | tf_op jit(solution)/shard_map/ppermute | solution.py:594
  54.3 0.1 collective-permute-start.18
  54.4 2.5 %collective-permute-start.19 = (bf16[2,128,128]{2,1,0:T(8,128)(2,1)S(1)}, bf16[2,128,128]{2,1,0:T(8,128)(2,1)S(1)}, u32[]{:S(2)}, u32[]{:S(2)}) collective-permute-start(bf16[2,128,128]{2,1,0:T(8,128)(2,1)S(1)} %pad_maximum_fusion.11), channel_id=1, source_target_pairs={{0,16},{4,20},{8,24},{12,28},{16,0},{20,4},{24,8},{28,12},{32,48},... | collective-permute-start | bytes 196616 | tf_op jit(solution)/shard_map/ppermute | solution.py:594
  56.9 2.3 %collective-permute-start.17 = (bf16[2,128,128]{2,1,0:T(8,128)(2,1)S(1)}, bf16[2,128,128]{2,1,0:T(8,128)(2,1)S(1)}, u32[]{:S(2)}, u32[]{:S(2)}) collective-permute-start(bf16[2,128,128]{2,1,0:T(8,128)(2,1)S(1)} %pad_maximum_fusion.9), channel_id=1, source_target_pairs={{0,24},{4,28},{8,16},{12,20},{16,8},{20,12},{24,0},{28,4},{32,56},... | collective-permute-start | bytes 196616 | tf_op jit(solution)/shard_map/ppermute | solution.py:594
  59.3 0.0 collective-permute-done.18.one
  59.3 1.2 %collective-permute-done.19.two = bf16[2,128,128]{2,1,0:T(8,128)(2,1)S(1)} collective-permute-done((bf16[2,128,128]{2,1,0:T(8,128)(2,1)S(1)}, bf16[2,128,128]{2,1,0:T(8,128)(2,1)S(1)}, u32[]{:S(2)}, u32[]{:S(2)}) %collective-permute-start.19) | collective-permute-done | bytes 65568 | tf_op jit(solution)/shard_map/ppermute | solution.py:594
  60.5 0.0 slice-done
  60.5 0.0 slice-done.1
  60.5 1.0 %early.1.acc_ref = f32[128,4096]{1,0:T(8,128)S(1)} custom-call(bf16[4,128,128]{2,1,0:T(8,128)(2,1)S(1)} %get-tuple-element.51.keep, bf16[4,128,128]{2,1,0:T(8,128)(2,1)S(1)} %collective-permute-done.16.came, bf16[2,128,128]{2,1,0:T(8,128)(2,1)S(1)} %collective-permute-done.18.one, bf16[2,128,128]{2,1,0:T(8,128)(2,1)S(1)} %collective-permute-done.19.two, ...), custom_call_target="tpu_custom_call" | custom-call | flops 800000000 | bytes 8000000 | tf_op jit(solution)/shard_map/early/pallas_call | solution.py:572
  61.5 1.0 %collective-permute-done.17.three = bf16[2,128,128]{2,1,0:T(8,128)(2,1)S(1)} collective-permute-done((bf16[2,128,128]{2,1,0:T(8,128)(2,1)S(1)}, bf16[2,128,128]{2,1,0:T(8,128)(2,1)S(1)}, u32[]{:S(2)}, u32[]{:S(2)}) %collective-permute-start.17) | collective-permute-done | bytes 65568 | tf_op jit(solution)/shard_map/ppermute | solution.py:594
  62.5 0.5 late.1
  62.9 1.7 %collective-permute-start.20 = (bf16[32,4096]{1,0:T(8,128)(2,1)S(1)}, bf16[32,4096]{1,0:T(8,128)(2,1)S(1)}, u32[]{:S(2)}, u32[]{:S(2)}) collective-permute-start(bf16[32,4096]{1,0:T(8,128)(2,1)S(1)} %get-tuple-element.54), channel_id=1, source_target_pairs={{0,1},{1,0},{2,3},{3,2},{4,5},{5,4},{6,7},{7,6},{8,9},{9,8},{10,11... | collective-permute-start | bytes 786440 | tf_op jit(solution)/shard_map/ppermute | solution.py:636
  64.6 2.2 %collective-permute-start.21 = (bf16[32,4096]{1,0:T(8,128)(2,1)S(1)}, bf16[32,4096]{1,0:T(8,128)(2,1)S(1)}, u32[]{:S(2)}, u32[]{:S(2)}) collective-permute-start(bf16[32,4096]{1,0:T(8,128)(2,1)S(1)} %get-tuple-element.55), channel_id=1, source_target_pairs={{0,3},{1,2},{2,1},{3,0},{4,7},{5,6},{6,5},{7,4},{8,11},{9,10},{10,... | collective-permute-start | bytes 786440 | tf_op jit(solution)/shard_map/ppermute | solution.py:636
  66.8 0.7 collective-permute-start.22
  67.5 4.8 %collective-permute-done.20 = bf16[32,4096]{1,0:T(8,128)(2,1)S(1)} collective-permute-done((bf16[32,4096]{1,0:T(8,128)(2,1)S(1)}, bf16[32,4096]{1,0:T(8,128)(2,1)S(1)}, u32[]{:S(2)}, u32[]{:S(2)}) %collective-permute-start.20) | collective-permute-done | bytes 262176 | tf_op jit(solution)/shard_map/ppermute | solution.py:636
  72.3 4.2 %collective-permute-done.21 = bf16[32,4096]{1,0:T(8,128)(2,1)S(1)} collective-permute-done((bf16[32,4096]{1,0:T(8,128)(2,1)S(1)}, bf16[32,4096]{1,0:T(8,128)(2,1)S(1)}, u32[]{:S(2)}, u32[]{:S(2)}) %collective-permute-start.21) | collective-permute-done | bytes 262176 | tf_op jit(solution)/shard_map/ppermute | solution.py:636
  76.5 1.5 %collective-permute-done.22 = bf16[32,4096]{1,0:T(8,128)(2,1)S(1)} collective-permute-done((bf16[32,4096]{1,0:T(8,128)(2,1)S(1)}, bf16[32,4096]{1,0:T(8,128)(2,1)S(1)}, u32[]{:S(2)}, u32[]{:S(2)}) %collective-permute-start.22) | collective-permute-done | bytes 262176 | tf_op jit(solution)/shard_map/ppermute | solution.py:636
  78.0 0.8 %add_convert_fusion = bf16[32,4096]{1,0:T(8,128)(2,1)} fusion(bf16[32,4096]{1,0:T(8,128)(2,1)S(1)} %collective-permute-done.22, bf16[32,4096]{1,0:T(8,128)(2,1)S(1)} %collective-permute-done.21, f32[32,4096]{1,0:T(8,128)S(1)} %get-tuple-element.53, bf16[32,4096]{1,0:T(8,128)(2,1)S(1)} %collective-permute-done.20), kind=kLoop, calls=%fused_computation | loop fusion | flops 917504 | bytes 1572864 | tf_op jit(solution)/shard_map/convert_element_type | solution.py:640
  (21 shorter events, 0.2 us)
Async XLA Ops:
  1.4 1.5 %collective-permute-start.4 = (bf16[4,144,128]{2,1,0:T(8,128)(2,1)S(1)}, bf16[4,144,128]{2,1,0:T(8,128)(2,1)S(1)}, u32[]{:S(2)}, u32[]{:S(2)}) collective-permute-start(bf16[4,144,128]{2,1,0:T(8,128)(2,1)S(1)} %get-tuple-element.34), channel_id=1, source_target_pairs={{0,4},{4,0},{8,12},{12,8},{16,20},{20,16},{24,28},{28,24},{32,36},... | collective-permute-start | bytes 442376 | tf_op jit(solution)/shard_map/ppermute | solution.py:594
  1.5 6.4 %collective-permute-start = (bf16[4,256,128]{2,1,0:T(8,128)(2,1)S(1)}, bf16[4,256,128]{2,1,0:T(8,128)(2,1)S(1)}, u32[]{:S(2)}, u32[]{:S(2)}) collective-permute-start(bf16[4,256,128]{2,1,0:T(8,128)(2,1)S(1)} %get-tuple-element.32), channel_id=1, source_target_pairs={{0,4},{4,0},{8,12},{12,8},{16,20},{20,16},{24,28},{28,24},{32,36},... | collective-permute-start | bytes 786440 | tf_op jit(solution)/shard_map/ppermute | solution.py:594
  2.9 9.4 %collective-permute-start.5 = (bf16[2,144,128]{2,1,0:T(8,128)(2,1)S(1)}, bf16[2,144,128]{2,1,0:T(8,128)(2,1)S(1)}, u32[]{:S(2)}, u32[]{:S(2)}) collective-permute-start(bf16[2,144,128]{2,1,0:T(8,128)(2,1)S(1)} %pad_maximum_fusion), channel_id=1, source_target_pairs={{0,8},{4,12},{8,0},{12,4},{16,24},{20,28},{24,16},{28,20},{32,40},... | collective-permute-start | bytes 221192 | tf_op jit(solution)/shard_map/ppermute | solution.py:594
  4.4 8.4 %collective-permute-start.6 = (bf16[2,144,128]{2,1,0:T(8,128)(2,1)S(1)}, bf16[2,144,128]{2,1,0:T(8,128)(2,1)S(1)}, u32[]{:S(2)}, u32[]{:S(2)}) collective-permute-start(bf16[2,144,128]{2,1,0:T(8,128)(2,1)S(1)} %pad_maximum_fusion.1), channel_id=1, source_target_pairs={{0,16},{4,20},{8,24},{12,28},{16,0},{20,4},{24,8},{28,12},{32,48},... | collective-permute-start | bytes 221192 | tf_op jit(solution)/shard_map/ppermute | solution.py:594
  7.3 6.4 %collective-permute-start.7 = (bf16[2,144,128]{2,1,0:T(8,128)(2,1)S(1)}, bf16[2,144,128]{2,1,0:T(8,128)(2,1)S(1)}, u32[]{:S(2)}, u32[]{:S(2)}) collective-permute-start(bf16[2,144,128]{2,1,0:T(8,128)(2,1)S(1)} %pad_maximum_fusion.2), channel_id=1, source_target_pairs={{0,24},{4,28},{8,16},{12,20},{16,8},{20,12},{24,0},{28,4},{32,56},... | collective-permute-start | bytes 221192 | tf_op jit(solution)/shard_map/ppermute | solution.py:594
  7.9 9.1 %collective-permute-start.1 = (bf16[2,128,128]{2,1,0:T(8,128)(2,1)S(1)}, bf16[2,128,128]{2,1,0:T(8,128)(2,1)S(1)}, u32[]{:S(2)}, u32[]{:S(2)}) collective-permute-start(bf16[2,128,128]{2,1,0:T(8,128)(2,1)S(1)} %pad_maximum_fusion.3), channel_id=1, source_target_pairs={{0,8},{4,12},{8,0},{12,4},{16,24},{20,28},{24,16},{28,20},{32,40},... | collective-permute-start | bytes 196616 | tf_op jit(solution)/shard_map/ppermute | solution.py:594
  8.2 8.7 %collective-permute-start.2 = (bf16[2,128,128]{2,1,0:T(8,128)(2,1)S(1)}, bf16[2,128,128]{2,1,0:T(8,128)(2,1)S(1)}, u32[]{:S(2)}, u32[]{:S(2)}) collective-permute-start(bf16[2,128,128]{2,1,0:T(8,128)(2,1)S(1)} %pad_maximum_fusion.4), channel_id=1, source_target_pairs={{0,16},{4,20},{8,24},{12,28},{16,0},{20,4},{24,8},{28,12},{32,48},... | collective-permute-start | bytes 196616 | tf_op jit(solution)/shard_map/ppermute | solution.py:594
  12.3 28.6 %copy-start = (f32[128]{0:T(128)S(1)}, f32[128]{0:T(128)}, u32[]{:S(2)}) copy-start(f32[128]{0:T(128)} %param.13) | copy-start | bytes 1540
  12.3 31.5 %copy-start.1 = (bf16[8,128,384]{2,1,0:T(8,128)(2,1)S(1)}, bf16[8,128,384]{2,1,0:T(8,128)(2,1)}, u32[]{:S(2)}) copy-start(bf16[8,128,384]{2,1,0:T(8,128)(2,1)} %weight_ref.5) | copy-start | bytes 2359300
  12.3 5.6 %collective-permute-start.3 = (bf16[2,128,128]{2,1,0:T(8,128)(2,1)S(1)}, bf16[2,128,128]{2,1,0:T(8,128)(2,1)S(1)}, u32[]{:S(2)}, u32[]{:S(2)}) collective-permute-start(bf16[2,128,128]{2,1,0:T(8,128)(2,1)S(1)} %pad_maximum_fusion.5), channel_id=1, source_target_pairs={{0,24},{4,28},{8,16},{12,20},{16,8},{20,12},{24,0},{28,4},{32,56},... | collective-permute-start | bytes 196616 | tf_op jit(solution)/shard_map/ppermute | solution.py:594
  18.9 41.6 %slice-start = ((s8[8388608]{0:T(1024)(128)(4,1)}), s8[4194304]{0:T(1024)(128)(4,1)S(1)}, s32[]{:S(2)}) async-start(s8[8388608]{0:T(1024)(128)(4,1)} %bitcast.1), calls=%async_computation | async-start | bytes 8388608
  18.9 11.6 %collective-permute-start.12 = (bf16[128,256]{1,0:T(8,128)(2,1)S(1)}, bf16[128,256]{1,0:T(8,128)(2,1)S(1)}, u32[]{:S(2)}, u32[]{:S(2)}) collective-permute-start(bf16[128,256]{1,0:T(8,128)(2,1)S(1)} %get-tuple-element.40.own_ref), channel_id=1, source_target_pairs={{0,64},{4,68},{8,72},{12,76},{16,80},{20,84},{24,88},{28,92},{32,9... | collective-permute-start | bytes 196616 | tf_op jit(solution)/shard_map/ppermute | solution.py:611
  22.6 7.9 %collective-permute-start.11 = (bf16[128,256]{1,0:T(8,128)(2,1)S(1)}, bf16[128,256]{1,0:T(8,128)(2,1)S(1)}, u32[]{:S(2)}, u32[]{:S(2)}) collective-permute-start(bf16[128,256]{1,0:T(8,128)(2,1)S(1)} %get-tuple-element.40.own_ref), channel_id=1, source_target_pairs={{0,32},{4,36},{8,40},{12,44},{16,48},{20,52},{24,56},{28,60},{32,6... | collective-permute-start | bytes 196616 | tf_op jit(solution)/shard_map/ppermute | solution.py:611
  25.6 8.1 %collective-permute-start.8 = (bf16[2,128,128]{2,1,0:T(8,128)(2,1)S(1)}, bf16[2,128,128]{2,1,0:T(8,128)(2,1)S(1)}, u32[]{:S(2)}, u32[]{:S(2)}) collective-permute-start(bf16[2,128,128]{2,1,0:T(8,128)(2,1)S(1)} %pad_maximum_fusion.6), channel_id=1, source_target_pairs={{0,8},{4,12},{8,0},{12,4},{16,24},{20,28},{24,16},{28,20},{32,40},... | collective-permute-start | bytes 196616 | tf_op jit(solution)/shard_map/ppermute | solution.py:594
  25.7 8.0 %collective-permute-start.9 = (bf16[2,128,128]{2,1,0:T(8,128)(2,1)S(1)}, bf16[2,128,128]{2,1,0:T(8,128)(2,1)S(1)}, u32[]{:S(2)}, u32[]{:S(2)}) collective-permute-start(bf16[2,128,128]{2,1,0:T(8,128)(2,1)S(1)} %pad_maximum_fusion.7), channel_id=1, source_target_pairs={{0,16},{4,20},{8,24},{12,28},{16,0},{20,4},{24,8},{28,12},{32,48},... | collective-permute-start | bytes 196616 | tf_op jit(solution)/shard_map/ppermute | solution.py:594
  28.3 5.6 %collective-permute-start.10 = (bf16[2,128,128]{2,1,0:T(8,128)(2,1)S(1)}, bf16[2,128,128]{2,1,0:T(8,128)(2,1)S(1)}, u32[]{:S(2)}, u32[]{:S(2)}) collective-permute-start(bf16[2,128,128]{2,1,0:T(8,128)(2,1)S(1)} %pad_maximum_fusion.8), channel_id=1, source_target_pairs={{0,24},{4,28},{8,16},{12,20},{16,8},{20,12},{24,0},{28,4},{32,56},... | collective-permute-start | bytes 196616 | tf_op jit(solution)/shard_map/ppermute | solution.py:594
  30.9 10.0 %collective-permute-start.14 = (bf16[128,256]{1,0:T(8,128)(2,1)S(1)}, bf16[128,256]{1,0:T(8,128)(2,1)S(1)}, u32[]{:S(2)}, u32[]{:S(2)}) collective-permute-start(bf16[128,256]{1,0:T(8,128)(2,1)S(1)} %get-tuple-element.47), channel_id=1, source_target_pairs={{0,96},{4,100},{8,104},{12,108},{16,112},{20,116},{24,120},{28,124... | collective-permute-start | bytes 196616 | tf_op jit(solution)/shard_map/ppermute | solution.py:611
  32.8 8.1 %collective-permute-start.13 = (bf16[128,256]{1,0:T(8,128)(2,1)S(1)}, bf16[128,256]{1,0:T(8,128)(2,1)S(1)}, u32[]{:S(2)}, u32[]{:S(2)}) collective-permute-start(bf16[128,256]{1,0:T(8,128)(2,1)S(1)} %get-tuple-element.47), channel_id=1, source_target_pairs={{0,192},{4,196},{8,200},{12,204},{16,208},{20,212},{24,216},{28,22... | collective-permute-start | bytes 196616 | tf_op jit(solution)/shard_map/ppermute | solution.py:611
  41.6 18.9 %slice-start.1 = ((s8[8388608]{0:T(1024)(128)(4,1)}), s8[4194304]{0:T(1024)(128)(4,1)S(1)}, s32[]{:S(2)}) async-start(s8[8388608]{0:T(1024)(128)(4,1)} %bitcast.1), calls=%async_computation.1 | async-start | bytes 8388608
  41.6 9.7 %collective-permute-start.15 = (bf16[1024,128]{1,0:T(8,128)(2,1)S(1)}, bf16[1024,128]{1,0:T(8,128)(2,1)S(1)}, u32[]{:S(2)}, u32[]{:S(2)}) collective-permute-start(bf16[1024,128]{1,0:T(8,128)(2,1)S(1)} %norm.1.normed_ref), channel_id=1, source_target_pairs={{0,32},{4,36},{8,40},{12,44},{16,48},{20,52},{24,56},{28,60},{32,6... | collective-permute-start | bytes 786440 | tf_op jit(solution)/shard_map/ppermute | solution.py:611
  52.8 1.4 %collective-permute-start.16 = (bf16[4,128,128]{2,1,0:T(8,128)(2,1)S(1)}, bf16[4,128,128]{2,1,0:T(8,128)(2,1)S(1)}, u32[]{:S(2)}, u32[]{:S(2)}) collective-permute-start(bf16[4,128,128]{2,1,0:T(8,128)(2,1)S(1)} %get-tuple-element.52), channel_id=1, source_target_pairs={{0,4},{4,0},{8,12},{12,8},{16,20},{20,16},{24,28},{28,24},{32,36},... | collective-permute-start | bytes 393224 | tf_op jit(solution)/shard_map/ppermute | solution.py:594
  54.3 5.0 %collective-permute-start.18 = (bf16[2,128,128]{2,1,0:T(8,128)(2,1)S(1)}, bf16[2,128,128]{2,1,0:T(8,128)(2,1)S(1)}, u32[]{:S(2)}, u32[]{:S(2)}) collective-permute-start(bf16[2,128,128]{2,1,0:T(8,128)(2,1)S(1)} %pad_maximum_fusion.10), channel_id=1, source_target_pairs={{0,8},{4,12},{8,0},{12,4},{16,24},{20,28},{24,16},{28,20},{32,40},... | collective-permute-start | bytes 196616 | tf_op jit(solution)/shard_map/ppermute | solution.py:594
  54.4 6.1 %collective-permute-start.19 = (bf16[2,128,128]{2,1,0:T(8,128)(2,1)S(1)}, bf16[2,128,128]{2,1,0:T(8,128)(2,1)S(1)}, u32[]{:S(2)}, u32[]{:S(2)}) collective-permute-start(bf16[2,128,128]{2,1,0:T(8,128)(2,1)S(1)} %pad_maximum_fusion.11), channel_id=1, source_target_pairs={{0,16},{4,20},{8,24},{12,28},{16,0},{20,4},{24,8},{28,12},{32,48},... | collective-permute-start | bytes 196616 | tf_op jit(solution)/shard_map/ppermute | solution.py:594
  56.9 5.6 %collective-permute-start.17 = (bf16[2,128,128]{2,1,0:T(8,128)(2,1)S(1)}, bf16[2,128,128]{2,1,0:T(8,128)(2,1)S(1)}, u32[]{:S(2)}, u32[]{:S(2)}) collective-permute-start(bf16[2,128,128]{2,1,0:T(8,128)(2,1)S(1)} %pad_maximum_fusion.9), channel_id=1, source_target_pairs={{0,24},{4,28},{8,16},{12,20},{16,8},{20,12},{24,0},{28,4},{32,56},... | collective-permute-start | bytes 196616 | tf_op jit(solution)/shard_map/ppermute | solution.py:594
  62.9 9.3 %collective-permute-start.20 = (bf16[32,4096]{1,0:T(8,128)(2,1)S(1)}, bf16[32,4096]{1,0:T(8,128)(2,1)S(1)}, u32[]{:S(2)}, u32[]{:S(2)}) collective-permute-start(bf16[32,4096]{1,0:T(8,128)(2,1)S(1)} %get-tuple-element.54), channel_id=1, source_target_pairs={{0,1},{1,0},{2,3},{3,2},{4,5},{5,4},{6,7},{7,6},{8,9},{9,8},{10,11... | collective-permute-start | bytes 786440 | tf_op jit(solution)/shard_map/ppermute | solution.py:636
  64.6 11.9 %collective-permute-start.21 = (bf16[32,4096]{1,0:T(8,128)(2,1)S(1)}, bf16[32,4096]{1,0:T(8,128)(2,1)S(1)}, u32[]{:S(2)}, u32[]{:S(2)}) collective-permute-start(bf16[32,4096]{1,0:T(8,128)(2,1)S(1)} %get-tuple-element.55), channel_id=1, source_target_pairs={{0,3},{1,2},{2,1},{3,0},{4,7},{5,6},{6,5},{7,4},{8,11},{9,10},{10,... | collective-permute-start | bytes 786440 | tf_op jit(solution)/shard_map/ppermute | solution.py:636
  66.8 11.2 %collective-permute-start.22 = (bf16[32,4096]{1,0:T(8,128)(2,1)S(1)}, bf16[32,4096]{1,0:T(8,128)(2,1)S(1)}, u32[]{:S(2)}, u32[]{:S(2)}) collective-permute-start(bf16[32,4096]{1,0:T(8,128)(2,1)S(1)} %get-tuple-element.56), channel_id=1, source_target_pairs={{0,2},{1,3},{2,0},{3,1},{4,6},{5,7},{6,4},{7,5},{8,10},{9,11},{10,... | collective-permute-start | bytes 786440 | tf_op jit(solution)/shard_map/ppermute | solution.py:636

commit v10 on v9

--- a/solution.py
+++ b/solution.py
@@ -532,7 +532,7 @@
 
 def pair_part(first, second, dx):
     core, mine = lax.axis_index("seq") % 2, lax.axis_index("heads")
-    rows = [pl.ds(pl.multiple_of(jnp.bitwise_xor(mine, e) * 32, 32), 32) for e in range(4)]
+    rows = [pl.ds(pl.multiple_of(lax.rem(mine + e, 4) * 32, 32), 32) for e in range(4)]
     one = jnp.concatenate([first[r, :] for r in rows], axis=0)
     two = jnp.concatenate([second[r, :] for r in rows], axis=0)
     swapped = core > 0
@@ -557,13 +557,23 @@
         acc_ref[:, cols] = got
 
 
-def late_kernel(three, weight_ref, acc_ref, *outs):
+def late_kernel(three, weight_ref, acc_ref, own_ref, right_ref, left_ref, *outs):
     part, rows = pair_part(three.at[0], three.at[1], 3)
-    for at in range(0, weight_ref.shape[1], COLS):
+    far_right, far_left, plain_right, plain_left = outs
+    half = weight_ref.shape[1] // 2
+    for at in range(0, 2 * half, COLS):
         cols = slice(at, at + COLS)
         got = acc_ref[:, cols] + dot(part, weight_ref[rows, cols])
-        for e in range(4):
-            outs[e][:, cols] = got[e * 32 : e * 32 + 32].astype(outs[e].dtype)
+        own_ref[:, cols] = got[0:32]
+        if at < half:
+            right_ref[:, cols] = got[32:64]
+            far_right[:, cols] = got[64:96].astype(BF16)
+            plain_left[:, cols] = got[96:128].astype(BF16)
+        else:
+            cols = slice(at - half, at - half + COLS)
+            plain_right[:, cols] = got[32:64].astype(BF16)
+            far_left[:, cols] = got[64:96].astype(BF16)
+            left_ref[:, cols] = got[96:128]
 
 
 def project(slots, weight):
@@ -581,9 +591,10 @@
     return pl.pallas_call(
         late_kernel,
         out_shape=[jax.ShapeDtypeStruct((32, width), F32)]
-        + [jax.ShapeDtypeStruct((32, width), BF16)] * 3,
+        + [jax.ShapeDtypeStruct((32, width // 2), F32)] * 2
+        + [jax.ShapeDtypeStruct((32, width // 2), BF16)] * 4,
         in_specs=[vmem()] * 3,
-        out_specs=[vmem()] * 4,
+        out_specs=[vmem()] * 7,
         compiler_params=params(),
         cost_estimate=cost(3e8, 4e6),
         name="late",
@@ -630,14 +641,24 @@
     halo = later_plane(normed, 1)
     acc, stat, q2 = own(normed, attn_weight)
     attended = exchange(*halo_part(halo, attn_weight, acc, stat, q2))
-    sums = project(attended, out_weight)
-    moved = {}
-    for d in (2, 1, 3):
-        moved[d] = lax.ppermute(sums[d], "heads", [(s, s ^ d) for s in range(4)])
-    total = sums[0]
-    for d in (1, 3, 2):
-        total = total + moved[d].astype(F32)
-    return total.astype(BF16)
+    return sum_over_heads(*project(attended, out_weight))
+
+
+def sum_over_heads(own_sum, right, left, far_right, far_left, plain_right, plain_left):
+    def turn(block, step):
+        return lax.ppermute(block, "heads", [(s, (s + step) % 4) for s in range(4)])
+
+    passed_right = turn(far_right, 1)
+    passed_left = turn(far_left, 3)
+    plain_right = turn(plain_right, 1)
+    plain_left = turn(plain_left, 3)
+    right = turn((right + passed_right.astype(F32)).astype(BF16), 1)
+    left = turn((left + passed_left.astype(F32)).astype(BF16), 3)
+    others = jnp.concatenate(
+        [right.astype(F32) + plain_left.astype(F32), left.astype(F32) + plain_right.astype(F32)],
+        axis=1,
+    )
+    return (own_sum + others).astype(BF16)
 
 
 def solution(mesh):

time: 79.1 us -> 78.5 us (level)
  waiting for transfers between devices: 28.7 us -> 22.4 us
  starting transfers between devices: 36.6 us -> 41.6 us
    ppermute x3 -> x6, waiting for transfers between devices: 10.5 us -> 4.24 us  [turn(): return lax.ppermute(block, 'heads', [(s, (s + step) % 4) for s in range(4)])]
    ppermute x3 -> x6, starting transfers between devices: 4.57 us -> 9.58 us  [turn(): return lax.ppermute(block, 'heads', [(s, (s + step) % 4) for s in range(4)])]
  transfers between devices with their start and end apart: 23 -> 26, of which waited for: 12 -> 13; matrix products, arithmetic and copies ran while one was open for 0% -> 0% of each run, Pallas kernels for 9% -> 9%
where the time goes in v10:
time: 78.5 us; the launch traced here: 77.6 us
  starting transfers between devices  41.6 us (53%)
  waiting for transfers between devices  22.4 us (29%)
  Pallas kernels  12.3 us (16%)
  other arithmetic  0.96 us (1%)
    ppermute x15, starting transfers between devices, swap(): lax.ppermute(block, 'seq', [(s, s ^ d) for s in range(PLANE * PLANES)])  20.5 us
    ppermute x5, waiting for transfers between devices, later_plane(): return lax.ppermute(block, 'seq', route)  11.9 us
    ppermute x5, starting transfers between devices, later_plane(): return lax.ppermute(block, 'seq', route)  11.5 us
    ppermute x6, starting transfers between devices, turn(): return lax.ppermute(block, 'heads', [(s, (s + step) % 4) for s in range(4)])  9.58 us
    ppermute x15, waiting for transfers between devices, swap(): lax.ppermute(block, 'seq', [(s, s ^ d) for s in range(PLANE * PLANES)])  6.26 us
    ppermute x6, waiting for transfers between devices, turn(): return lax.ppermute(block, 'heads', [(s, (s + step) % 4) for s in range(4)])  4.24 us
    pallas_call x1, Pallas kernels, key_part(): pl.pallas_call(key_kernel, out_shape=[jax.ShapeDtypeStruct((PLANE, KROWS,...  3.3 us
  transfers between devices with their start and end apart: 26, of which 13 were waited for; matrix products, arithmetic and copies ran while one was open for 0% of the time, Pallas kernels for 9%

profile of v10, /device:TPU:128, one launch (start us, length us, event | category | flops | bytes accessed | tf_op | source)
XLA Modules:
  0.0 77.6 jit_solution(12621337746444392334)
XLA Ops:
  0.0 1.4 %pack.1 = (bf16[4,144,128]{2,1,0:T(8,128)(2,1)S(1)}, bf16[4,144,128]{2,1,0:T(8,128)(2,1)S(1)}, bf16[4,256,128]{2,1,0:T(8,128)(2,1)S(1)}, bf16[4,256,128]{2,1,0:T(8,128)(2,1)S(1)}) custom-call(bf16[128,1024]{1,0:T(8,128)(2,1)} %q_ref.1, bf16[128,1024]{1,0:T(8,128)(2,1)} %k_ref.1, bf16[128,1024]{1,0:T(8,128)(2,1)} %v_ref.1, f32[8,128]{1,0:T(8,128)} %decay_ref.1, ...), custom_call_target="tpu_custom_call" | custom-call | tf_op jit(solution)/shard_map/pack/pallas_call | solution.py:113
  1.4 0.1 collective-permute-start.4
  1.5 0.5 collective-permute-start
  2.0 0.8 %collective-permute-done.4.refs_1_ = bf16[4,144,128]{2,1,0:T(8,128)(2,1)S(1)} collective-permute-done((bf16[4,144,128]{2,1,0:T(8,128)(2,1)S(1)}, bf16[4,144,128]{2,1,0:T(8,128)(2,1)S(1)}, u32[]{:S(2)}, u32[]{:S(2)}) %collective-permute-start.4) | collective-permute-done | bytes 147488 | tf_op jit(solution)/shard_map/ppermute | solution.py:605
  2.9 1.6 %collective-permute-start.5 = (bf16[2,144,128]{2,1,0:T(8,128)(2,1)S(1)}, bf16[2,144,128]{2,1,0:T(8,128)(2,1)S(1)}, u32[]{:S(2)}, u32[]{:S(2)}) collective-permute-start(bf16[2,144,128]{2,1,0:T(8,128)(2,1)S(1)} %pad_maximum_fusion), channel_id=1, source_target_pairs={{0,8},{4,12},{8,0},{12,4},{16,24},{20,28},{24,16},{28,20},{32,40},... | collective-permute-start | bytes 221192 | tf_op jit(solution)/shard_map/ppermute | solution.py:605
  4.4 2.8 %collective-permute-start.6 = (bf16[2,144,128]{2,1,0:T(8,128)(2,1)S(1)}, bf16[2,144,128]{2,1,0:T(8,128)(2,1)S(1)}, u32[]{:S(2)}, u32[]{:S(2)}) collective-permute-start(bf16[2,144,128]{2,1,0:T(8,128)(2,1)S(1)} %pad_maximum_fusion.1), channel_id=1, source_target_pairs={{0,16},{4,20},{8,24},{12,28},{16,0},{20,4},{24,8},{28,12},{32,48},... | collective-permute-start | bytes 221192 | tf_op jit(solution)/shard_map/ppermute | solution.py:605
  7.3 0.6 collective-permute-start.7
  7.8 0.0 collective-permute-done.refs_1_
  7.9 0.4 collective-permute-start.1
  8.2 4.0 %collective-permute-start.2 = (bf16[2,128,128]{2,1,0:T(8,128)(2,1)S(1)}, bf16[2,128,128]{2,1,0:T(8,128)(2,1)S(1)}, u32[]{:S(2)}, u32[]{:S(2)}) collective-permute-start(bf16[2,128,128]{2,1,0:T(8,128)(2,1)S(1)} %pad_maximum_fusion.4), channel_id=1, source_target_pairs={{0,16},{4,20},{8,24},{12,28},{16,0},{20,4},{24,8},{28,12},{32,48},... | collective-permute-start | bytes 196616 | tf_op jit(solution)/shard_map/ppermute | solution.py:605
  12.3 0.0 copy-start.1
  12.3 0.0 collective-permute-done.5.refs_2_
  12.3 0.6 collective-permute-start.3
  12.9 0.0 collective-permute-done.6.refs_3_
  12.9 0.8 collective-permute-done.7.refs_4_
  13.6 3.3 %keys.1 = (bf16[8,144,128]{2,1,0:T(8,128)(2,1)S(1)}, f32[8,128,128]{2,1,0:T(8,128)S(1)}, f32[8,128,128]{2,1,0:T(8,128)S(1)}, f32[8,128,128]{2,1,0:T(8,128)S(1)},...) custom-call(bf16[4,144,128]{2,1,0:T(8,128)(2,1)S(1)} %get-tuple-element.36.refs_0_, ...), custom_call_target="tpu_custom_call" | custom-call | flops 2000000000 | bytes 4000000 | tf_op jit(solution)/shard_map/keys/pallas_call | solution.py:274
  16.9 0.0 collective-permute-done.1.refs_2_
  16.9 0.0 collective-permute-done.2.refs_3_
  17.0 0.9 %collective-permute-done.3.refs_4_ = bf16[2,128,128]{2,1,0:T(8,128)(2,1)S(1)} collective-permute-done((bf16[2,128,128]{2,1,0:T(8,128)(2,1)S(1)}, bf16[2,128,128]{2,1,0:T(8,128)(2,1)S(1)}, u32[]{:S(2)}, u32[]{:S(2)}) %collective-permute-start.3) | collective-permute-done | bytes 65568 | tf_op jit(solution)/shard_map/ppermute | solution.py:605
  17.9 1.0 %values.1 = (f32[8,128,256]{2,1,0:T(8,128)S(1)}, bf16[128,256]{1,0:T(8,128)(2,1)S(1)}, f32[7,128,256]{2,1,0:T(8,128)S(1)}) custom-call(bf16[4,256,128]{2,1,0:T(8,128)(2,1)S(1)} %get-tuple-element.44.refs_0_, bf16[4,256,128]{2,1,0:T(8,128)(2,1)S(1)} %collective-permute-done.refs_1_, bf16[2,128,128]{2,1,0:T(8,128)(2,1)S(1)} %collective-permute-done.1.refs_2_, ...), custom_call_target="tpu_custom_call" | custom-call | flops 1000000000 | bytes 4000000 | tf_op jit(solution)/shard_map/values/pallas_call | solution.py:289
  18.9 0.0 slice-start
  18.9 3.6 %collective-permute-start.12 = (bf16[128,256]{1,0:T(8,128)(2,1)S(1)}, bf16[128,256]{1,0:T(8,128)(2,1)S(1)}, u32[]{:S(2)}, u32[]{:S(2)}) collective-permute-start(bf16[128,256]{1,0:T(8,128)(2,1)S(1)} %get-tuple-element.43.own_ref), channel_id=1, source_target_pairs={{0,64},{4,68},{8,72},{12,76},{16,80},{20,84},{24,88},{28,92},{32,9... | collective-permute-start | bytes 196616 | tf_op jit(solution)/shard_map/ppermute | solution.py:622
  22.6 2.9 %collective-permute-start.11 = (bf16[128,256]{1,0:T(8,128)(2,1)S(1)}, bf16[128,256]{1,0:T(8,128)(2,1)S(1)}, u32[]{:S(2)}, u32[]{:S(2)}) collective-permute-start(bf16[128,256]{1,0:T(8,128)(2,1)S(1)} %get-tuple-element.43.own_ref), channel_id=1, source_target_pairs={{0,32},{4,36},{8,40},{12,44},{16,48},{20,52},{24,56},{28,60},{32,6... | collective-permute-start | bytes 196616 | tf_op jit(solution)/shard_map/ppermute | solution.py:622
  25.6 0.1 collective-permute-start.8
  25.7 2.6 %collective-permute-start.9 = (bf16[2,128,128]{2,1,0:T(8,128)(2,1)S(1)}, bf16[2,128,128]{2,1,0:T(8,128)(2,1)S(1)}, u32[]{:S(2)}, u32[]{:S(2)}) collective-permute-start(bf16[2,128,128]{2,1,0:T(8,128)(2,1)S(1)} %pad_maximum_fusion.7), channel_id=1, source_target_pairs={{0,16},{4,20},{8,24},{12,28},{16,0},{20,4},{24,8},{28,12},{32,48},... | collective-permute-start | bytes 196616 | tf_op jit(solution)/shard_map/ppermute | solution.py:605
  28.3 2.2 %collective-permute-start.10 = (bf16[2,128,128]{2,1,0:T(8,128)(2,1)S(1)}, bf16[2,128,128]{2,1,0:T(8,128)(2,1)S(1)}, u32[]{:S(2)}, u32[]{:S(2)}) collective-permute-start(bf16[2,128,128]{2,1,0:T(8,128)(2,1)S(1)} %pad_maximum_fusion.8), channel_id=1, source_target_pairs={{0,24},{4,28},{8,16},{12,20},{16,8},{20,12},{24,0},{28,4},{32,56},... | collective-permute-start | bytes 196616 | tf_op jit(solution)/shard_map/ppermute | solution.py:605
  30.5 0.0 collective-permute-done.12.two_ref
  30.5 0.3 combine.1
  30.9 1.9 %collective-permute-start.14 = (bf16[128,256]{1,0:T(8,128)(2,1)S(1)}, bf16[128,256]{1,0:T(8,128)(2,1)S(1)}, u32[]{:S(2)}, u32[]{:S(2)}) collective-permute-start(bf16[128,256]{1,0:T(8,128)(2,1)S(1)} %get-tuple-element.50), channel_id=1, source_target_pairs={{0,96},{4,100},{8,104},{12,108},{16,112},{20,116},{24,120},{28,124... | collective-permute-start | bytes 196616 | tf_op jit(solution)/shard_map/ppermute | solution.py:622
  32.8 0.8 %collective-permute-start.13 = (bf16[128,256]{1,0:T(8,128)(2,1)S(1)}, bf16[128,256]{1,0:T(8,128)(2,1)S(1)}, u32[]{:S(2)}, u32[]{:S(2)}) collective-permute-start(bf16[128,256]{1,0:T(8,128)(2,1)S(1)} %get-tuple-element.50), channel_id=1, source_target_pairs={{0,192},{4,196},{8,200},{12,204},{16,208},{20,212},{24,216},{28,22... | collective-permute-start | bytes 196616 | tf_op jit(solution)/shard_map/ppermute | solution.py:622
  33.6 0.0 collective-permute-done.8.refs_2_
  33.6 0.0 collective-permute-done.9.refs_3_
  33.7 0.2 collective-permute-done.10.refs_4_
  33.9 1.3 %query.1.no_ref = f32[1024,256]{1,0:T(8,128)S(1)} custom-call(bf16[4,256,128]{2,1,0:T(8,128)(2,1)S(1)} %get-tuple-element.44.refs_0_, bf16[4,256,128]{2,1,0:T(8,128)(2,1)S(1)} %collective-permute-done.refs_1_, bf16[2,128,128]{2,1,0:T(8,128)(2,1)S(1)} %collective-permute-done.8.refs_2_, bf16[2,128,128]{2,1,0:T(8,128)(2,1)S(1)} %collective-permute-done.9.refs_3_, ...), custom_call_target="tpu_custom_call" | custom-call | flops 1000000000 | bytes 4000000 | tf_op jit(solution)/shard_map/query/pallas_call | solution.py:344
  35.2 5.7 %collective-permute-done.14.three_ref = bf16[128,256]{1,0:T(8,128)(2,1)S(1)} collective-permute-done((bf16[128,256]{1,0:T(8,128)(2,1)S(1)}, bf16[128,256]{1,0:T(8,128)(2,1)S(1)}, u32[]{:S(2)}, u32[]{:S(2)}) %collective-permute-start.14) | collective-permute-done | bytes 65568 | tf_op jit(solution)/shard_map/ppermute | solution.py:622
  40.9 0.0 collective-permute-done.13.six_ref
  40.9 0.7 norm.1.normed_ref
  41.6 0.0 slice-start.1
  41.6 2.2 %collective-permute-start.15 = (bf16[1024,128]{1,0:T(8,128)(2,1)S(1)}, bf16[1024,128]{1,0:T(8,128)(2,1)S(1)}, u32[]{:S(2)}, u32[]{:S(2)}) collective-permute-start(bf16[1024,128]{1,0:T(8,128)(2,1)S(1)} %norm.1.normed_ref), channel_id=1, source_target_pairs={{0,32},{4,36},{8,40},{12,44},{16,48},{20,52},{24,56},{28,60},{32,6... | collective-permute-start | bytes 786440 | tf_op jit(solution)/shard_map/ppermute | solution.py:622
  43.8 1.3 %own.1 = (f32[1024,128]{1,0:T(8,128)S(1)}, f32[2,1024,128]{2,1,0:T(8,128)S(1)}, bf16[1024,128]{1,0:T(8,128)(2,1)S(1)}) custom-call(bf16[1024,128]{1,0:T(8,128)(2,1)S(1)} %norm.1.normed_ref, bf16[8,128,384]{2,1,0:T(8,128)(2,1)S(1)} %copy-done.1), custom_call_target="tpu_custom_call" | custom-call | flops 1000000000 | bytes 3000000 | tf_op jit(solution)/shard_map/own/pallas_call | solution.py:466
  45.1 6.3 %collective-permute-done.15.halo_ref = bf16[1024,128]{1,0:T(8,128)(2,1)S(1)} collective-permute-done((bf16[1024,128]{1,0:T(8,128)(2,1)S(1)}, bf16[1024,128]{1,0:T(8,128)(2,1)S(1)}, u32[]{:S(2)}, u32[]{:S(2)}) %collective-permute-start.15) | collective-permute-done | bytes 262176 | tf_op jit(solution)/shard_map/ppermute | solution.py:622
  51.3 1.5 %halo.1 = (bf16[4,128,128]{2,1,0:T(8,128)(2,1)S(1)}, bf16[4,128,128]{2,1,0:T(8,128)(2,1)S(1)}) custom-call(bf16[1024,128]{1,0:T(8,128)(2,1)S(1)} %collective-permute-done.15.halo_ref, bf16[8,128,384]{2,1,0:T(8,128)(2,1)S(1)} %copy-done.1, f32[1024,128]{1,0:T(8,128)S(1)} %get-tuple-element.51.acc_ref, f32[2,1024,128]{2,1,0:T(8,128)S(1)} %get-tuple-element.52.stat_ref, ...), custom_call_target="tpu_custom_call" | custom-call | flops 1000000000 | bytes 3000000 | tf_op jit(solution)/shard_map/halo/pallas_call | solution.py:518
  52.8 0.1 collective-permute-start.16
  53.0 1.3 %collective-permute-done.16.came = bf16[4,128,128]{2,1,0:T(8,128)(2,1)S(1)} collective-permute-done((bf16[4,128,128]{2,1,0:T(8,128)(2,1)S(1)}, bf16[4,128,128]{2,1,0:T(8,128)(2,1)S(1)}, u32[]{:S(2)}, u32[]{:S(2)}) %collective-permute-start.16) | collective-permute-done | bytes 131104 | tf_op jit(solution)/shard_map/ppermute | solution.py:605
  54.3 0.1 collective-permute-start.18
  54.4 2.5 %collective-permute-start.19 = (bf16[2,128,128]{2,1,0:T(8,128)(2,1)S(1)}, bf16[2,128,128]{2,1,0:T(8,128)(2,1)S(1)}, u32[]{:S(2)}, u32[]{:S(2)}) collective-permute-start(bf16[2,128,128]{2,1,0:T(8,128)(2,1)S(1)} %pad_maximum_fusion.11), channel_id=1, source_target_pairs={{0,16},{4,20},{8,24},{12,28},{16,0},{20,4},{24,8},{28,12},{32,48},... | collective-permute-start | bytes 196616 | tf_op jit(solution)/shard_map/ppermute | solution.py:605
  56.9 2.3 %collective-permute-start.17 = (bf16[2,128,128]{2,1,0:T(8,128)(2,1)S(1)}, bf16[2,128,128]{2,1,0:T(8,128)(2,1)S(1)}, u32[]{:S(2)}, u32[]{:S(2)}) collective-permute-start(bf16[2,128,128]{2,1,0:T(8,128)(2,1)S(1)} %pad_maximum_fusion.9), channel_id=1, source_target_pairs={{0,24},{4,28},{8,16},{12,20},{16,8},{20,12},{24,0},{28,4},{32,56},... | collective-permute-start | bytes 196616 | tf_op jit(solution)/shard_map/ppermute | solution.py:605
  59.3 1.2 %collective-permute-done.19.two = bf16[2,128,128]{2,1,0:T(8,128)(2,1)S(1)} collective-permute-done((bf16[2,128,128]{2,1,0:T(8,128)(2,1)S(1)}, bf16[2,128,128]{2,1,0:T(8,128)(2,1)S(1)}, u32[]{:S(2)}, u32[]{:S(2)}) %collective-permute-start.19) | collective-permute-done | bytes 65568 | tf_op jit(solution)/shard_map/ppermute | solution.py:605
  60.5 1.0 %early.1.acc_ref = f32[128,4096]{1,0:T(8,128)S(1)} custom-call(bf16[4,128,128]{2,1,0:T(8,128)(2,1)S(1)} %get-tuple-element.54.keep, bf16[4,128,128]{2,1,0:T(8,128)(2,1)S(1)} %collective-permute-done.16.came, bf16[2,128,128]{2,1,0:T(8,128)(2,1)S(1)} %collective-permute-done.18.one, bf16[2,128,128]{2,1,0:T(8,128)(2,1)S(1)} %collective-permute-done.19.two, ...), custom_call_target="tpu_custom_call" | custom-call | flops 800000000 | bytes 8000000 | tf_op jit(solution)/shard_map/early/pallas_call | solution.py:582
  61.5 1.0 %collective-permute-done.17.three = bf16[2,128,128]{2,1,0:T(8,128)(2,1)S(1)} collective-permute-done((bf16[2,128,128]{2,1,0:T(8,128)(2,1)S(1)}, bf16[2,128,128]{2,1,0:T(8,128)(2,1)S(1)}, u32[]{:S(2)}, u32[]{:S(2)}) %collective-permute-start.17) | collective-permute-done | bytes 65568 | tf_op jit(solution)/shard_map/ppermute | solution.py:605
  62.5 0.4 late.1
  62.9 1.7 %collective-permute-start.20 = (bf16[32,2048]{1,0:T(8,128)(2,1)S(1)}, bf16[32,2048]{1,0:T(8,128)(2,1)S(1)}, u32[]{:S(2)}, u32[]{:S(2)}) collective-permute-start(bf16[32,2048]{1,0:T(8,128)(2,1)S(1)} %get-tuple-element.58), channel_id=1, source_target_pairs={{0,1},{1,2},{2,3},{3,0},{4,5},{5,6},{6,7},{7,4},{8,9},{9,10},{10,1... | collective-permute-start | bytes 393224 | tf_op jit(solution)/shard_map/ppermute | solution.py:649
  64.6 1.7 %collective-permute-start.22 = (bf16[32,2048]{1,0:T(8,128)(2,1)S(1)}, bf16[32,2048]{1,0:T(8,128)(2,1)S(1)}, u32[]{:S(2)}, u32[]{:S(2)}) collective-permute-start(bf16[32,2048]{1,0:T(8,128)(2,1)S(1)} %get-tuple-element.59), channel_id=1, source_target_pairs={{0,3},{1,0},{2,1},{3,2},{4,7},{5,4},{6,5},{7,6},{8,11},{9,8},{10,9... | collective-permute-start | bytes 393224 | tf_op jit(solution)/shard_map/ppermute | solution.py:649
  66.2 1.8 %collective-permute-start.23 = (bf16[32,2048]{1,0:T(8,128)(2,1)S(1)}, bf16[32,2048]{1,0:T(8,128)(2,1)S(1)}, u32[]{:S(2)}, u32[]{:S(2)}) collective-permute-start(bf16[32,2048]{1,0:T(8,128)(2,1)S(1)} %get-tuple-element.61), channel_id=1, source_target_pairs={{0,3},{1,0},{2,1},{3,2},{4,7},{5,4},{6,5},{7,6},{8,11},{9,8},{10,9... | collective-permute-start | bytes 393224 | tf_op jit(solution)/shard_map/ppermute | solution.py:649
  68.1 0.2 collective-permute-start.25
  68.3 0.9 %collective-permute-done.20 = bf16[32,2048]{1,0:T(8,128)(2,1)S(1)} collective-permute-done((bf16[32,2048]{1,0:T(8,128)(2,1)S(1)}, bf16[32,2048]{1,0:T(8,128)(2,1)S(1)}, u32[]{:S(2)}, u32[]{:S(2)}) %collective-permute-start.20) | collective-permute-done | bytes 131104 | tf_op jit(solution)/shard_map/ppermute | solution.py:649
  69.2 1.2 %collective-permute-start.21 = (bf16[32,2048]{1,0:T(8,128)(2,1)S(1)}, bf16[32,2048]{1,0:T(8,128)(2,1)S(1)}, u32[]{:S(2)}, u32[]{:S(2)}) collective-permute-start(bf16[32,2048]{1,0:T(8,128)(2,1)S(1)} %add_convert_fusion.1), channel_id=1, source_target_pairs={{0,1},{1,2},{2,3},{3,0},{4,5},{5,6},{6,7},{7,4},{8,9},{9,10},{10,1... | collective-permute-start | bytes 393224 | tf_op jit(solution)/shard_map/ppermute | solution.py:649
  70.4 0.8 %collective-permute-done.23 = bf16[32,2048]{1,0:T(8,128)(2,1)S(1)} collective-permute-done((bf16[32,2048]{1,0:T(8,128)(2,1)S(1)}, bf16[32,2048]{1,0:T(8,128)(2,1)S(1)}, u32[]{:S(2)}, u32[]{:S(2)}) %collective-permute-start.23) | collective-permute-done | bytes 131104 | tf_op jit(solution)/shard_map/ppermute | solution.py:649
  71.3 3.0 %collective-permute-start.24 = (bf16[32,2048]{1,0:T(8,128)(2,1)S(1)}, bf16[32,2048]{1,0:T(8,128)(2,1)S(1)}, u32[]{:S(2)}, u32[]{:S(2)}) collective-permute-start(bf16[32,2048]{1,0:T(8,128)(2,1)S(1)} %add_convert_fusion), channel_id=1, source_target_pairs={{0,3},{1,0},{2,1},{3,2},{4,7},{5,4},{6,5},{7,6},{8,11},{9,8},{10,9... | collective-permute-start | bytes 393224 | tf_op jit(solution)/shard_map/ppermute | solution.py:649
  74.3 0.0 collective-permute-done.22
  74.3 1.3 %collective-permute-done.21 = bf16[32,2048]{1,0:T(8,128)(2,1)S(1)} collective-permute-done((bf16[32,2048]{1,0:T(8,128)(2,1)S(1)}, bf16[32,2048]{1,0:T(8,128)(2,1)S(1)}, u32[]{:S(2)}, u32[]{:S(2)}) %collective-permute-start.21) | collective-permute-done | bytes 131104 | tf_op jit(solution)/shard_map/ppermute | solution.py:649
  75.7 0.0 collective-permute-done.25
  75.7 1.2 %collective-permute-done.24 = bf16[32,2048]{1,0:T(8,128)(2,1)S(1)} collective-permute-done((bf16[32,2048]{1,0:T(8,128)(2,1)S(1)}, bf16[32,2048]{1,0:T(8,128)(2,1)S(1)}, u32[]{:S(2)}, u32[]{:S(2)}) %collective-permute-start.24) | collective-permute-done | bytes 131104 | tf_op jit(solution)/shard_map/ppermute | solution.py:649
  76.9 0.8 fusion
  (31 shorter events, 0.3 us)
Async XLA Ops:
  1.4 1.5 %collective-permute-start.4 = (bf16[4,144,128]{2,1,0:T(8,128)(2,1)S(1)}, bf16[4,144,128]{2,1,0:T(8,128)(2,1)S(1)}, u32[]{:S(2)}, u32[]{:S(2)}) collective-permute-start(bf16[4,144,128]{2,1,0:T(8,128)(2,1)S(1)} %get-tuple-element.37), channel_id=1, source_target_pairs={{0,4},{4,0},{8,12},{12,8},{16,20},{20,16},{24,28},{28,24},{32,36},... | collective-permute-start | bytes 442376 | tf_op jit(solution)/shard_map/ppermute | solution.py:605
  1.5 6.4 %collective-permute-start = (bf16[4,256,128]{2,1,0:T(8,128)(2,1)S(1)}, bf16[4,256,128]{2,1,0:T(8,128)(2,1)S(1)}, u32[]{:S(2)}, u32[]{:S(2)}) collective-permute-start(bf16[4,256,128]{2,1,0:T(8,128)(2,1)S(1)} %get-tuple-element.35), channel_id=1, source_target_pairs={{0,4},{4,0},{8,12},{12,8},{16,20},{20,16},{24,28},{28,24},{32,36},... | collective-permute-start | bytes 786440 | tf_op jit(solution)/shard_map/ppermute | solution.py:605
  2.9 9.4 %collective-permute-start.5 = (bf16[2,144,128]{2,1,0:T(8,128)(2,1)S(1)}, bf16[2,144,128]{2,1,0:T(8,128)(2,1)S(1)}, u32[]{:S(2)}, u32[]{:S(2)}) collective-permute-start(bf16[2,144,128]{2,1,0:T(8,128)(2,1)S(1)} %pad_maximum_fusion), channel_id=1, source_target_pairs={{0,8},{4,12},{8,0},{12,4},{16,24},{20,28},{24,16},{28,20},{32,40},... | collective-permute-start | bytes 221192 | tf_op jit(solution)/shard_map/ppermute | solution.py:605
  4.4 8.4 %collective-permute-start.6 = (bf16[2,144,128]{2,1,0:T(8,128)(2,1)S(1)}, bf16[2,144,128]{2,1,0:T(8,128)(2,1)S(1)}, u32[]{:S(2)}, u32[]{:S(2)}) collective-permute-start(bf16[2,144,128]{2,1,0:T(8,128)(2,1)S(1)} %pad_maximum_fusion.1), channel_id=1, source_target_pairs={{0,16},{4,20},{8,24},{12,28},{16,0},{20,4},{24,8},{28,12},{32,48},... | collective-permute-start | bytes 221192 | tf_op jit(solution)/shard_map/ppermute | solution.py:605
  7.3 6.4 %collective-permute-start.7 = (bf16[2,144,128]{2,1,0:T(8,128)(2,1)S(1)}, bf16[2,144,128]{2,1,0:T(8,128)(2,1)S(1)}, u32[]{:S(2)}, u32[]{:S(2)}) collective-permute-start(bf16[2,144,128]{2,1,0:T(8,128)(2,1)S(1)} %pad_maximum_fusion.2), channel_id=1, source_target_pairs={{0,24},{4,28},{8,16},{12,20},{16,8},{20,12},{24,0},{28,4},{32,56},... | collective-permute-start | bytes 221192 | tf_op jit(solution)/shard_map/ppermute | solution.py:605
  7.9 9.1 %collective-permute-start.1 = (bf16[2,128,128]{2,1,0:T(8,128)(2,1)S(1)}, bf16[2,128,128]{2,1,0:T(8,128)(2,1)S(1)}, u32[]{:S(2)}, u32[]{:S(2)}) collective-permute-start(bf16[2,128,128]{2,1,0:T(8,128)(2,1)S(1)} %pad_maximum_fusion.3), channel_id=1, source_target_pairs={{0,8},{4,12},{8,0},{12,4},{16,24},{20,28},{24,16},{28,20},{32,40},... | collective-permute-start | bytes 196616 | tf_op jit(solution)/shard_map/ppermute | solution.py:605
  8.2 8.7 %collective-permute-start.2 = (bf16[2,128,128]{2,1,0:T(8,128)(2,1)S(1)}, bf16[2,128,128]{2,1,0:T(8,128)(2,1)S(1)}, u32[]{:S(2)}, u32[]{:S(2)}) collective-permute-start(bf16[2,128,128]{2,1,0:T(8,128)(2,1)S(1)} %pad_maximum_fusion.4), channel_id=1, source_target_pairs={{0,16},{4,20},{8,24},{12,28},{16,0},{20,4},{24,8},{28,12},{32,48},... | collective-permute-start | bytes 196616 | tf_op jit(solution)/shard_map/ppermute | solution.py:605
  12.3 28.6 %copy-start = (f32[128]{0:T(128)S(1)}, f32[128]{0:T(128)}, u32[]{:S(2)}) copy-start(f32[128]{0:T(128)} %param.13) | copy-start | bytes 1540
  12.3 31.5 %copy-start.1 = (bf16[8,128,384]{2,1,0:T(8,128)(2,1)S(1)}, bf16[8,128,384]{2,1,0:T(8,128)(2,1)}, u32[]{:S(2)}) copy-start(bf16[8,128,384]{2,1,0:T(8,128)(2,1)} %weight_ref.5) | copy-start | bytes 2359300
  12.3 5.6 %collective-permute-start.3 = (bf16[2,128,128]{2,1,0:T(8,128)(2,1)S(1)}, bf16[2,128,128]{2,1,0:T(8,128)(2,1)S(1)}, u32[]{:S(2)}, u32[]{:S(2)}) collective-permute-start(bf16[2,128,128]{2,1,0:T(8,128)(2,1)S(1)} %pad_maximum_fusion.5), channel_id=1, source_target_pairs={{0,24},{4,28},{8,16},{12,20},{16,8},{20,12},{24,0},{28,4},{32,56},... | collective-permute-start | bytes 196616 | tf_op jit(solution)/shard_map/ppermute | solution.py:605
  18.9 41.6 %slice-start = ((s8[8388608]{0:T(1024)(128)(4,1)}), s8[4194304]{0:T(1024)(128)(4,1)S(1)}, s32[]{:S(2)}) async-start(s8[8388608]{0:T(1024)(128)(4,1)} %bitcast.1), calls=%async_computation | async-start | bytes 8388608
  18.9 11.6 %collective-permute-start.12 = (bf16[128,256]{1,0:T(8,128)(2,1)S(1)}, bf16[128,256]{1,0:T(8,128)(2,1)S(1)}, u32[]{:S(2)}, u32[]{:S(2)}) collective-permute-start(bf16[128,256]{1,0:T(8,128)(2,1)S(1)} %get-tuple-element.43.own_ref), channel_id=1, source_target_pairs={{0,64},{4,68},{8,72},{12,76},{16,80},{20,84},{24,88},{28,92},{32,9... | collective-permute-start | bytes 196616 | tf_op jit(solution)/shard_map/ppermute | solution.py:622
  22.6 7.9 %collective-permute-start.11 = (bf16[128,256]{1,0:T(8,128)(2,1)S(1)}, bf16[128,256]{1,0:T(8,128)(2,1)S(1)}, u32[]{:S(2)}, u32[]{:S(2)}) collective-permute-start(bf16[128,256]{1,0:T(8,128)(2,1)S(1)} %get-tuple-element.43.own_ref), channel_id=1, source_target_pairs={{0,32},{4,36},{8,40},{12,44},{16,48},{20,52},{24,56},{28,60},{32,6... | collective-permute-start | bytes 196616 | tf_op jit(solution)/shard_map/ppermute | solution.py:622
  25.6 8.1 %collective-permute-start.8 = (bf16[2,128,128]{2,1,0:T(8,128)(2,1)S(1)}, bf16[2,128,128]{2,1,0:T(8,128)(2,1)S(1)}, u32[]{:S(2)}, u32[]{:S(2)}) collective-permute-start(bf16[2,128,128]{2,1,0:T(8,128)(2,1)S(1)} %pad_maximum_fusion.6), channel_id=1, source_target_pairs={{0,8},{4,12},{8,0},{12,4},{16,24},{20,28},{24,16},{28,20},{32,40},... | collective-permute-start | bytes 196616 | tf_op jit(solution)/shard_map/ppermute | solution.py:605
  25.7 8.0 %collective-permute-start.9 = (bf16[2,128,128]{2,1,0:T(8,128)(2,1)S(1)}, bf16[2,128,128]{2,1,0:T(8,128)(2,1)S(1)}, u32[]{:S(2)}, u32[]{:S(2)}) collective-permute-start(bf16[2,128,128]{2,1,0:T(8,128)(2,1)S(1)} %pad_maximum_fusion.7), channel_id=1, source_target_pairs={{0,16},{4,20},{8,24},{12,28},{16,0},{20,4},{24,8},{28,12},{32,48},... | collective-permute-start | bytes 196616 | tf_op jit(solution)/shard_map/ppermute | solution.py:605
  28.3 5.6 %collective-permute-start.10 = (bf16[2,128,128]{2,1,0:T(8,128)(2,1)S(1)}, bf16[2,128,128]{2,1,0:T(8,128)(2,1)S(1)}, u32[]{:S(2)}, u32[]{:S(2)}) collective-permute-start(bf16[2,128,128]{2,1,0:T(8,128)(2,1)S(1)} %pad_maximum_fusion.8), channel_id=1, source_target_pairs={{0,24},{4,28},{8,16},{12,20},{16,8},{20,12},{24,0},{28,4},{32,56},... | collective-permute-start | bytes 196616 | tf_op jit(solution)/shard_map/ppermute | solution.py:605
  30.9 10.0 %collective-permute-start.14 = (bf16[128,256]{1,0:T(8,128)(2,1)S(1)}, bf16[128,256]{1,0:T(8,128)(2,1)S(1)}, u32[]{:S(2)}, u32[]{:S(2)}) collective-permute-start(bf16[128,256]{1,0:T(8,128)(2,1)S(1)} %get-tuple-element.50), channel_id=1, source_target_pairs={{0,96},{4,100},{8,104},{12,108},{16,112},{20,116},{24,120},{28,124... | collective-permute-start | bytes 196616 | tf_op jit(solution)/shard_map/ppermute | solution.py:622
  32.8 8.1 %collective-permute-start.13 = (bf16[128,256]{1,0:T(8,128)(2,1)S(1)}, bf16[128,256]{1,0:T(8,128)(2,1)S(1)}, u32[]{:S(2)}, u32[]{:S(2)}) collective-permute-start(bf16[128,256]{1,0:T(8,128)(2,1)S(1)} %get-tuple-element.50), channel_id=1, source_target_pairs={{0,192},{4,196},{8,200},{12,204},{16,208},{20,212},{24,216},{28,22... | collective-permute-start | bytes 196616 | tf_op jit(solution)/shard_map/ppermute | solution.py:622
  41.6 18.9 %slice-start.1 = ((s8[8388608]{0:T(1024)(128)(4,1)}), s8[4194304]{0:T(1024)(128)(4,1)S(1)}, s32[]{:S(2)}) async-start(s8[8388608]{0:T(1024)(128)(4,1)} %bitcast.1), calls=%async_computation.1 | async-start | bytes 8388608
  41.6 9.7 %collective-permute-start.15 = (bf16[1024,128]{1,0:T(8,128)(2,1)S(1)}, bf16[1024,128]{1,0:T(8,128)(2,1)S(1)}, u32[]{:S(2)}, u32[]{:S(2)}) collective-permute-start(bf16[1024,128]{1,0:T(8,128)(2,1)S(1)} %norm.1.normed_ref), channel_id=1, source_target_pairs={{0,32},{4,36},{8,40},{12,44},{16,48},{20,52},{24,56},{28,60},{32,6... | collective-permute-start | bytes 786440 | tf_op jit(solution)/shard_map/ppermute | solution.py:622
  52.8 1.4 %collective-permute-start.16 = (bf16[4,128,128]{2,1,0:T(8,128)(2,1)S(1)}, bf16[4,128,128]{2,1,0:T(8,128)(2,1)S(1)}, u32[]{:S(2)}, u32[]{:S(2)}) collective-permute-start(bf16[4,128,128]{2,1,0:T(8,128)(2,1)S(1)} %get-tuple-element.55), channel_id=1, source_target_pairs={{0,4},{4,0},{8,12},{12,8},{16,20},{20,16},{24,28},{28,24},{32,36},... | collective-permute-start | bytes 393224 | tf_op jit(solution)/shard_map/ppermute | solution.py:605
  54.3 5.0 %collective-permute-start.18 = (bf16[2,128,128]{2,1,0:T(8,128)(2,1)S(1)}, bf16[2,128,128]{2,1,0:T(8,128)(2,1)S(1)}, u32[]{:S(2)}, u32[]{:S(2)}) collective-permute-start(bf16[2,128,128]{2,1,0:T(8,128)(2,1)S(1)} %pad_maximum_fusion.10), channel_id=1, source_target_pairs={{0,8},{4,12},{8,0},{12,4},{16,24},{20,28},{24,16},{28,20},{32,40},... | collective-permute-start | bytes 196616 | tf_op jit(solution)/shard_map/ppermute | solution.py:605
  54.4 6.1 %collective-permute-start.19 = (bf16[2,128,128]{2,1,0:T(8,128)(2,1)S(1)}, bf16[2,128,128]{2,1,0:T(8,128)(2,1)S(1)}, u32[]{:S(2)}, u32[]{:S(2)}) collective-permute-start(bf16[2,128,128]{2,1,0:T(8,128)(2,1)S(1)} %pad_maximum_fusion.11), channel_id=1, source_target_pairs={{0,16},{4,20},{8,24},{12,28},{16,0},{20,4},{24,8},{28,12},{32,48},... | collective-permute-start | bytes 196616 | tf_op jit(solution)/shard_map/ppermute | solution.py:605
  56.9 5.6 %collective-permute-start.17 = (bf16[2,128,128]{2,1,0:T(8,128)(2,1)S(1)}, bf16[2,128,128]{2,1,0:T(8,128)(2,1)S(1)}, u32[]{:S(2)}, u32[]{:S(2)}) collective-permute-start(bf16[2,128,128]{2,1,0:T(8,128)(2,1)S(1)} %pad_maximum_fusion.9), channel_id=1, source_target_pairs={{0,24},{4,28},{8,16},{12,20},{16,8},{20,12},{24,0},{28,4},{32,56},... | collective-permute-start | bytes 196616 | tf_op jit(solution)/shard_map/ppermute | solution.py:605
  62.9 6.3 %collective-permute-start.20 = (bf16[32,2048]{1,0:T(8,128)(2,1)S(1)}, bf16[32,2048]{1,0:T(8,128)(2,1)S(1)}, u32[]{:S(2)}, u32[]{:S(2)}) collective-permute-start(bf16[32,2048]{1,0:T(8,128)(2,1)S(1)} %get-tuple-element.58), channel_id=1, source_target_pairs={{0,1},{1,2},{2,3},{3,0},{4,5},{5,6},{6,7},{7,4},{8,9},{9,10},{10,1... | collective-permute-start | bytes 393224 | tf_op jit(solution)/shard_map/ppermute | solution.py:649
  64.6 9.8 %collective-permute-start.22 = (bf16[32,2048]{1,0:T(8,128)(2,1)S(1)}, bf16[32,2048]{1,0:T(8,128)(2,1)S(1)}, u32[]{:S(2)}, u32[]{:S(2)}) collective-permute-start(bf16[32,2048]{1,0:T(8,128)(2,1)S(1)} %get-tuple-element.59), channel_id=1, source_target_pairs={{0,3},{1,0},{2,1},{3,2},{4,7},{5,4},{6,5},{7,6},{8,11},{9,8},{10,9... | collective-permute-start | bytes 393224 | tf_op jit(solution)/shard_map/ppermute | solution.py:649
  66.2 5.0 %collective-permute-start.23 = (bf16[32,2048]{1,0:T(8,128)(2,1)S(1)}, bf16[32,2048]{1,0:T(8,128)(2,1)S(1)}, u32[]{:S(2)}, u32[]{:S(2)}) collective-permute-start(bf16[32,2048]{1,0:T(8,128)(2,1)S(1)} %get-tuple-element.61), channel_id=1, source_target_pairs={{0,3},{1,0},{2,1},{3,2},{4,7},{5,4},{6,5},{7,6},{8,11},{9,8},{10,9... | collective-permute-start | bytes 393224 | tf_op jit(solution)/shard_map/ppermute | solution.py:649
  68.1 7.6 %collective-permute-start.25 = (bf16[32,2048]{1,0:T(8,128)(2,1)S(1)}, bf16[32,2048]{1,0:T(8,128)(2,1)S(1)}, u32[]{:S(2)}, u32[]{:S(2)}) collective-permute-start(bf16[32,2048]{1,0:T(8,128)(2,1)S(1)} %get-tuple-element.62), channel_id=1, source_target_pairs={{0,1},{1,2},{2,3},{3,0},{4,5},{5,6},{6,7},{7,4},{8,9},{9,10},{10,1... | collective-permute-start | bytes 393224 | tf_op jit(solution)/shard_map/ppermute | solution.py:649
  69.2 6.4 %collective-permute-start.21 = (bf16[32,2048]{1,0:T(8,128)(2,1)S(1)}, bf16[32,2048]{1,0:T(8,128)(2,1)S(1)}, u32[]{:S(2)}, u32[]{:S(2)}) collective-permute-start(bf16[32,2048]{1,0:T(8,128)(2,1)S(1)} %add_convert_fusion.1), channel_id=1, source_target_pairs={{0,1},{1,2},{2,3},{3,0},{4,5},{5,6},{6,7},{7,4},{8,9},{9,10},{10,1... | collective-permute-start | bytes 393224 | tf_op jit(solution)/shard_map/ppermute | solution.py:649
  71.3 5.5 %collective-permute-start.24 = (bf16[32,2048]{1,0:T(8,128)(2,1)S(1)}, bf16[32,2048]{1,0:T(8,128)(2,1)S(1)}, u32[]{:S(2)}, u32[]{:S(2)}) collective-permute-start(bf16[32,2048]{1,0:T(8,128)(2,1)S(1)} %add_convert_fusion), channel_id=1, source_target_pairs={{0,3},{1,0},{2,1},{3,2},{4,7},{5,4},{6,5},{7,6},{8,11},{9,8},{10,9... | collective-permute-start | bytes 393224 | tf_op jit(solution)/shard_map/ppermute | solution.py:649

commit v11 on v10

--- a/solution.py
+++ b/solution.py
@@ -70,22 +70,20 @@
     return row, col
 
 
-def pack_kernel(q_ref, k_ref, v_ref, decay_ref, beta_ref, *rest):
-    keep_k, send_k, keep, send, gate, raw, sems = rest
+def head_columns(me, d):
+    return pl.ds(pl.multiple_of(jnp.bitwise_xor(me, d) * C, C), C)
+
+
+def pack_keys_kernel(k_ref, decay_ref, beta_ref, keep, send, gate, raw, sems):
     me = lax.axis_index("seq") % PLANE
     copies = [
-        pltpu.make_async_copy(decay_ref, raw.at[0], sems.at[24]),
-        pltpu.make_async_copy(beta_ref, raw.at[1], sems.at[25]),
+        pltpu.make_async_copy(decay_ref, raw.at[0], sems.at[8]),
+        pltpu.make_async_copy(beta_ref, raw.at[1], sems.at[9]),
     ]
     for d in range(PLANE):
-        cols = pl.ds(pl.multiple_of(jnp.bitwise_xor(me, d) * C, C), C)
-        out_k, out = (send_k, send) if d % 2 else (keep_k, keep)
-        at = d // 2
-        copies += [
-            pltpu.make_async_copy(k_ref.at[:, cols], out_k.at[at, pl.ds(0, C)], sems.at[3 * d]),
-            pltpu.make_async_copy(v_ref.at[:, cols], out.at[at, pl.ds(0, C)], sems.at[3 * d + 1]),
-            pltpu.make_async_copy(q_ref.at[:, cols], out.at[at, pl.ds(C, C)], sems.at[3 * d + 2]),
-        ]
+        out = send if d % 2 else keep
+        into = out.at[d // 2, pl.ds(0, C)]
+        copies.append(pltpu.make_async_copy(k_ref.at[:, head_columns(me, d)], into, sems.at[d]))
     for copy in copies:
         copy.start()
     copies[0].wait()
@@ -100,29 +98,57 @@
     for d in range(PLANE):
         head = jnp.bitwise_xor(me, d)
         rows = [gate[i, pl.ds(head, 1), :] for i in range(6)]
-        out = send_k if d % 2 else keep_k
+        out = send if d % 2 else keep
         out[d // 2, C:, :] = jnp.concatenate(rows + [zeros], axis=0).astype(BF16)
     for copy in copies[2:]:
         copy.wait()
 
 
-def pack(q, k, v, decay, beta):
-    any_space = pl.BlockSpec(memory_space=pltpu.HBM)
-    first = jax.ShapeDtypeStruct((4, KROWS, C), BF16)
-    wide = jax.ShapeDtypeStruct((4, 2 * C, C), BF16)
-    return pl.pallas_call(
-        pack_kernel,
-        out_shape=[first, first, wide, wide],
-        in_specs=[any_space] * 5,
-        out_specs=[vmem()] * 4,
+def pack_rest_kernel(q_ref, v_ref, keep, send, sems):
+    me = lax.axis_index("seq") % PLANE
+    copies = []
+    for d in range(PLANE):
+        out = send if d % 2 else keep
+        for part, ref in enumerate((v_ref, q_ref)):
+            into = out.at[d // 2, pl.ds(part * C, C)]
+            source = ref.at[:, head_columns(me, d)]
+            copies.append(pltpu.make_async_copy(source, into, sems.at[2 * d + part]))
+    for copy in copies:
+        copy.start()
+    for copy in copies:
+        copy.wait()
+
+
+def in_hbm(*arrays):
+    return [pltpu.with_memory_space_constraint(x, pltpu.HBM) for x in arrays]
+
+
+def pack_keys(k, decay, beta):
+    return pl.pallas_call(
+        pack_keys_kernel,
+        out_shape=[jax.ShapeDtypeStruct((4, KROWS, C), BF16)] * 2,
+        in_specs=[pl.BlockSpec(memory_space=pltpu.HBM)] * 3,
+        out_specs=[vmem()] * 2,
         scratch_shapes=[
             pltpu.VMEM((6, PLANE, C), F32),
             pltpu.VMEM((2, PLANE, C), F32),
-            pltpu.SemaphoreType.DMA((26,)),
+            pltpu.SemaphoreType.DMA((10,)),
         ],
         compiler_params=params(),
-        name="pack",
-    )(*[pltpu.with_memory_space_constraint(x, pltpu.HBM) for x in (q, k, v, decay, beta)])
+        name="pack_keys",
+    )(*in_hbm(k, decay, beta))
+
+
+def pack_rest(q, v):
+    return pl.pallas_call(
+        pack_rest_kernel,
+        out_shape=[jax.ShapeDtypeStruct((4, 2 * C, C), BF16)] * 2,
+        in_specs=[pl.BlockSpec(memory_space=pltpu.HBM)] * 2,
+        out_specs=[vmem()] * 2,
+        scratch_shapes=[pltpu.SemaphoreType.DMA((16,))],
+        compiler_params=params(),
+        name="pack_rest",
+    )(*in_hbm(q, v))
 
 
 def gather_slots(refs, out_ref, part=None):
@@ -182,8 +208,7 @@
 
 
 def key_kernel(*refs):
-    k_ref, mix_ref, inverse_ref, w_ref, tail_ref, reach_ref = refs[5:11]
-    maps = refs[11]
+    k_ref, mix_ref, inverse_ref, w_ref, tail_ref, reach_ref = refs[5:]
     me = lax.axis_index("seq") % PLANE
     row, col = iotas()
     gather_slots(refs[:5], k_ref)
@@ -233,12 +258,7 @@
     made = [dot_tn(jnp.concatenate([keys[d], keys[d]], axis=0), halves[d]) for d in every]
     for d in every:
         g_end = found[d][0][:, C - 1 : C]
-        maps[jnp.bitwise_xor(me, d)] = jnp.where(row == col, jnp.exp(g_end), 0.0) - made[d]
-    one = [maps[i] for i in every]
-    two = [mm(one[2 * i + 1], one[2 * i]) for i in range(4)]
-    four = [mm(two[2 * i + 1], two[2 * i]) for i in range(2)]
-    for i, part in enumerate(one + two + four + [mm(four[1], four[0])]):
-        reach_ref[i] = part
+        reach_ref[jnp.bitwise_xor(me, d)] = jnp.where(row == col, jnp.exp(g_end), 0.0) - made[d]
 
 
 def value_kernel(*refs):
@@ -247,7 +267,9 @@
     me = lax.axis_index("seq") % PLANE
     gather_slots(refs[:5], v_ref, slice(0, C))
     every = range(PLANE)
+    reach = [reach_ref[i] for i in every]
     u = [mm_exact_right(inverse_ref[d], v_ref[d]) for d in every]
+    reach_two = [mm(reach[2 * i + 1], reach[2 * i]) for i in range(4)]
     halves = []
     for d in every:
         wu_ref[d, :, :C] = w_ref[d]
@@ -255,17 +277,18 @@
         halves.append(jnp.concatenate(split(u[d] * tail_ref[d]), axis=0))
     keys = [k_ref[d, 0:C, :] for d in every]
     made = [dot_tn(jnp.concatenate([keys[d], keys[d]], axis=0), halves[d]) for d in every]
+    reach_four = [mm(reach_two[2 * i + 1], reach_two[2 * i]) for i in range(2)]
     for d in every:
         states[jnp.bitwise_xor(me, d)] = made[d]
     one = [states[i] for i in every]
-    two = [mm(reach_ref[2 * i + 1], one[2 * i]) + one[2 * i + 1] for i in range(4)]
-    four = [mm(reach_ref[8 + 2 * i + 1], two[2 * i]) + two[2 * i + 1] for i in range(2)]
-    last = mm(reach_ref[13], four[0]) + four[1]
-    ab_ref[:, :C] = reach_ref[14].astype(BF16)
-    ab_ref[:, C:] = last.astype(BF16)
-    both = ((0, one[0]), (8, two[0]), (2, one[2]), (12, four[0]), (4, one[4]), (10, two[2]), (6, one[6]))
-    for i, (at, state) in enumerate(both):
-        level_ref[i, :, :C] = reach_ref[at]
+    two = [mm(reach[2 * i + 1], one[2 * i]) + one[2 * i + 1] for i in range(4)]
+    ab_ref[:, :C] = mm(reach_four[1], reach_four[0]).astype(BF16)
+    four = [mm(reach_two[2 * i + 1], two[2 * i]) + two[2 * i + 1] for i in range(2)]
+    ab_ref[:, C:] = (mm(reach_four[1], four[0]) + four[1]).astype(BF16)
+    levels = [(reach[0], one[0]), (reach_two[0], two[0]), (reach[2], one[2])]
+    levels += [(reach_four[0], four[0]), (reach[4], one[4]), (reach_two[2], two[2])]
+    for i, (across, state) in enumerate(levels + [(reach[6], one[6])]):
+        level_ref[i, :, :C] = across
         level_ref[i, :, C:] = state
 
 
@@ -274,11 +297,9 @@
     return pl.pallas_call(
         key_kernel,
         out_shape=[jax.ShapeDtypeStruct((PLANE, KROWS, C), BF16)]
-        + [square] * 4
-        + [jax.ShapeDtypeStruct((15, C, C), F32)],
+        + [square] * 5,
         in_specs=[vmem()] * 5,
         out_specs=[vmem()] * 6,
-        scratch_shapes=[pltpu.VMEM((PLANE, C, C), F32)],
         compiler_params=params(),
         cost_estimate=cost(2e9, 4e6),
         name="keys",
@@ -479,7 +500,7 @@
 
 
 def halo_kernel(halo_ref, weight_ref, acc_ref, stat_ref, q2_ref, *refs):
-    keep, send, attended = refs
+    outs, attended = refs[:4], refs[4]
     place = lax.axis_index("seq")
     me, plane = place % PLANE, place // PLANE
     proj = dot(halo_ref[...], weight_ref[me, :, C:]).astype(BF16)
@@ -509,17 +530,16 @@
         attended[rows, :] = (acc / total).astype(BF16)
     for d in range(PLANE):
         chunk = jnp.bitwise_xor(me, d)
-        out = send if d % 2 else keep
-        out[d // 2] = attended[pl.ds(pl.multiple_of(chunk * C, C), C), :]
+        outs[d // 2][d % 2] = attended[pl.ds(pl.multiple_of(chunk * C, C), C), :]
 
 
 def halo_part(halo, weight, acc, stat, q2):
     n = PLANE * C
     return pl.pallas_call(
         halo_kernel,
-        out_shape=[jax.ShapeDtypeStruct((4, C, C), BF16)] * 2,
+        out_shape=[jax.ShapeDtypeStruct((2, C, C), BF16)] * 4,
         in_specs=[vmem()] * 5,
-        out_specs=[vmem()] * 2,
+        out_specs=[vmem()] * 4,
         scratch_shapes=[pltpu.VMEM((n, C), BF16)],
         compiler_params=params(),
         cost_estimate=cost(1e9, 3e6, 6e5),
@@ -543,12 +563,8 @@
     return jnp.concatenate([left, right], axis=1), pl.ds(at, 2 * C)
 
 
-def early_kernel(keep, came, one, two, weight_ref, acc_ref):
-    parts = [
-        pair_part(keep.at[0], came.at[0], 0),
-        pair_part(two.at[0], two.at[1], 2),
-        pair_part(one.at[0], one.at[1], 1),
-    ]
+def early_kernel(own_pair, own_came, two, two_came, weight_ref, acc_ref):
+    parts = [pair_part(own_pair.at[0], own_came, 0), pair_part(two.at[0], two_came, 2)]
     for at in range(0, weight_ref.shape[1], COLS):
         cols = slice(at, at + COLS)
         got = dot(parts[0][0], weight_ref[parts[0][1], cols])
@@ -557,13 +573,15 @@
         acc_ref[:, cols] = got
 
 
-def late_kernel(three, weight_ref, acc_ref, own_ref, right_ref, left_ref, *outs):
-    part, rows = pair_part(three.at[0], three.at[1], 3)
+def late_kernel(one, one_came, three, three_came, weight_ref, acc_ref, own_ref, right_ref, left_ref, *outs):
+    parts = [pair_part(one.at[0], one_came, 1), pair_part(three.at[0], three_came, 3)]
     far_right, far_left, plain_right, plain_left = outs
     half = weight_ref.shape[1] // 2
     for at in range(0, 2 * half, COLS):
         cols = slice(at, at + COLS)
-        got = acc_ref[:, cols] + dot(part, weight_ref[rows, cols])
+        got = acc_ref[:, cols]
+        for part, rows in parts:
+            got = got + dot(part, weight_ref[rows, cols])
         own_ref[:, cols] = got[0:32]
         if at < half:
             right_ref[:, cols] = got[32:64]
@@ -578,7 +596,7 @@
 
 def project(slots, weight):
     width = weight.shape[1]
-    keep, came, one, two, three = slots
+    (own_pair, one, two, three), (own_came, one_came, two_came, three_came) = slots
     acc = pl.pallas_call(
         early_kernel,
         out_shape=jax.ShapeDtypeStruct((C, width), F32),
@@ -587,18 +605,18 @@
         compiler_params=params(),
         cost_estimate=cost(8e8, 8e6),
         name="early",
-    )(keep, came, one, two, weight)
+    )(own_pair, own_came, two, two_came, weight)
     return pl.pallas_call(
         late_kernel,
         out_shape=[jax.ShapeDtypeStruct((32, width), F32)]
         + [jax.ShapeDtypeStruct((32, width // 2), F32)] * 2
         + [jax.ShapeDtypeStruct((32, width // 2), BF16)] * 4,
-        in_specs=[vmem()] * 3,
+        in_specs=[vmem()] * 6,
         out_specs=[vmem()] * 7,
         compiler_params=params(),
         cost_estimate=cost(3e8, 4e6),
         name="late",
-    )(three, weight, acc)
+    )(one, one_came, three, three_came, weight, acc)
 
 
 def swap(block, d):
@@ -616,6 +634,13 @@
     return along_x(keep, swap(send, 1))
 
 
+def exchange_back(pairs):
+    found = {dx: swap(pairs[dx], 2 * dx) for dx in (2, 1, 3)}
+    found[0], found[2] = lax.optimization_barrier((pairs[0], found[2]))
+    came = {dx: swap(found[dx][1], 1) for dx in (2, 0, 1, 3)}
+    return [found[dx] for dx in range(4)], [came[dx] for dx in range(4)]
+
+
 def later_plane(block, distance):
     step = PLANE * distance
     route = [(s, s + step) for s in range(PLANE * PLANES - step)]
@@ -623,8 +648,8 @@
 
 
 def local(q_delta, k_delta, v_delta, decay, beta, gain, attn_weight, out_weight):
-    keep_k, send_k, keep, send = pack(q_delta, k_delta, v_delta, decay, beta)
-    slots_k = exchange(keep_k, send_k)
+    slots_k = exchange(*pack_keys(k_delta, decay, beta))
+    keep, send = pack_rest(q_delta, v_delta)
     came = swap(send, 1)
     slots_v = along_x(keep, came, slice(0, C))
     k, mix, inverse, w, tail, reach = key_part(slots_k)
@@ -640,7 +665,7 @@
     normed = norm(no, gain[None, :], before, six, three)
     halo = later_plane(normed, 1)
     acc, stat, q2 = own(normed, attn_weight)
-    attended = exchange(*halo_part(halo, attn_weight, acc, stat, q2))
+    attended = exchange_back(halo_part(halo, attn_weight, acc, stat, q2))
     return sum_over_heads(*project(attended, out_weight))
 
 

time: 78.5 us -> 80 us (1.019)
  waiting for transfers between devices: 22.4 us -> 24.2 us
  starting transfers between devices: 41.6 us -> 40.3 us
    ppermute x6, waiting for transfers between devices: 4.24 us -> 6.66 us  [turn(): return lax.ppermute(block, 'heads', [(s, (s + step) % 4) for s in range(4)])]
    ppermute x15 -> x18, waiting for transfers between devices: 6.26 us -> 5.24 us  [swap(): lax.ppermute(block, 'seq', [(s, s ^ d) for s in range(PLANE * PLANES)])]
    pallas_call x2 -> x3, Pallas kernels: 2.85 us -> 3.65 us  [the longest x1 1.49 us: halo_part(): pl.pallas_call(halo_kernel, out_shape=[jax.ShapeDtypeStruct((2, C, C), BF...]
    ppermute x15 -> x18, starting transfers between devices: 20.5 us -> 20.4 us  [swap(): lax.ppermute(block, 'seq', [(s, s ^ d) for s in range(PLANE * PLANES)])]
  transfers between devices with their start and end apart: 26 -> 29, of which waited for: 13 -> 12; matrix products, arithmetic and copies ran while one was open for 0% -> 0% of each run, Pallas kernels for 9% -> 10%
where the time goes in v11:
time: 80 us; the launch traced here: 78.5 us
  starting transfers between devices  40.3 us (50%)
  waiting for transfers between devices  24.2 us (30%)
  Pallas kernels  12.6 us (16%)
  other arithmetic  0.95 us (1%)
    ppermute x18, starting transfers between devices, swap(): lax.ppermute(block, 'seq', [(s, s ^ d) for s in range(PLANE * PLANES)])  20.4 us
    ppermute x5, waiting for transfers between devices, later_plane(): return lax.ppermute(block, 'seq', route)  12.3 us
    ppermute x5, starting transfers between devices, later_plane(): return lax.ppermute(block, 'seq', route)  11.1 us
    ppermute x6, starting transfers between devices, turn(): return lax.ppermute(block, 'heads', [(s, (s + step) % 4) for s in range(4)])  8.82 us
    ppermute x6, waiting for transfers between devices, turn(): return lax.ppermute(block, 'heads', [(s, (s + step) % 4) for s in range(4)])  6.66 us
    ppermute x18, waiting for transfers between devices, swap(): lax.ppermute(block, 'seq', [(s, s ^ d) for s in range(PLANE * PLANES)])  5.24 us
    pallas_call x1, Pallas kernels, key_part(): pl.pallas_call(key_kernel, out_shape=[jax.ShapeDtypeStruct((PLANE, KROWS,...  2.71 us
  transfers between devices with their start and end apart: 29, of which 12 were waited for; matrix products, arithmetic and copies ran while one was open for 0% of the time, Pallas kernels for 10%

profile of v11, /device:TPU:128, one launch (start us, length us, event | category | flops | bytes accessed | tf_op | source)
XLA Modules:
  0.0 78.5 jit_solution(7178150841595675449)
XLA Ops:
  0.0 1.0 %pack_keys.1 = (bf16[4,144,128]{2,1,0:T(8,128)(2,1)S(1)}, bf16[4,144,128]{2,1,0:T(8,128)(2,1)S(1)}) custom-call(bf16[128,1024]{1,0:T(8,128)(2,1)} %k_ref.1, f32[8,128]{1,0:T(8,128)} %decay_ref.1, f32[8,128]{1,0:T(8,128)} %beta_ref.1), custom_call_target="tpu_custom_call" | custom-call | tf_op jit(solution)/shard_map/pack_keys/pallas_call | solution.py:127
  1.0 0.1 collective-permute-start.4
  1.1 1.2 %pack_rest.1 = (bf16[4,256,128]{2,1,0:T(8,128)(2,1)S(1)}, bf16[4,256,128]{2,1,0:T(8,128)(2,1)S(1)}) custom-call(bf16[128,1024]{1,0:T(8,128)(2,1)} %q_ref.1, bf16[128,1024]{1,0:T(8,128)(2,1)} %v_ref.1), custom_call_target="tpu_custom_call" | custom-call | tf_op jit(solution)/shard_map/pack_rest/pallas_call | solution.py:143
  2.3 0.6 collective-permute-start
  2.9 0.0 collective-permute-done.4.refs_1_
  2.9 1.6 %collective-permute-start.5 = (bf16[2,144,128]{2,1,0:T(8,128)(2,1)S(1)}, bf16[2,144,128]{2,1,0:T(8,128)(2,1)S(1)}, u32[]{:S(2)}, u32[]{:S(2)}) collective-permute-start(bf16[2,144,128]{2,1,0:T(8,128)(2,1)S(1)} %pad_maximum_fusion), channel_id=1, source_target_pairs={{0,8},{4,12},{8,0},{12,4},{16,24},{20,28},{24,16},{28,20},{32,40},... | collective-permute-start | bytes 221192 | tf_op jit(solution)/shard_map/ppermute | solution.py:623
  4.5 2.8 %collective-permute-start.6 = (bf16[2,144,128]{2,1,0:T(8,128)(2,1)S(1)}, bf16[2,144,128]{2,1,0:T(8,128)(2,1)S(1)}, u32[]{:S(2)}, u32[]{:S(2)}) collective-permute-start(bf16[2,144,128]{2,1,0:T(8,128)(2,1)S(1)} %pad_maximum_fusion.1), channel_id=1, source_target_pairs={{0,16},{4,20},{8,24},{12,28},{16,0},{20,4},{24,8},{28,12},{32,48},... | collective-permute-start | bytes 221192 | tf_op jit(solution)/shard_map/ppermute | solution.py:623
  7.3 0.6 collective-permute-start.7
  7.9 0.0 collective-permute-done.refs_1_
  7.9 0.4 collective-permute-start.1
  8.3 4.0 %collective-permute-start.2 = (bf16[2,128,128]{2,1,0:T(8,128)(2,1)S(1)}, bf16[2,128,128]{2,1,0:T(8,128)(2,1)S(1)}, u32[]{:S(2)}, u32[]{:S(2)}) collective-permute-start(bf16[2,128,128]{2,1,0:T(8,128)(2,1)S(1)} %pad_maximum_fusion.4), channel_id=1, source_target_pairs={{0,16},{4,20},{8,24},{12,28},{16,0},{20,4},{24,8},{28,12},{32,48},... | collective-permute-start | bytes 196616 | tf_op jit(solution)/shard_map/ppermute | solution.py:623
  12.3 0.0 copy-start.1
  12.4 0.0 collective-permute-done.5.refs_2_
  12.4 0.6 collective-permute-start.3
  12.9 0.0 collective-permute-done.6.refs_3_
  12.9 0.8 collective-permute-done.7.refs_4_
  13.7 2.7 %keys.1 = (bf16[8,144,128]{2,1,0:T(8,128)(2,1)S(1)}, f32[8,128,128]{2,1,0:T(8,128)S(1)}, f32[8,128,128]{2,1,0:T(8,128)S(1)}, f32[8,128,128]{2,1,0:T(8,128)S(1)},...) custom-call(bf16[4,144,128]{2,1,0:T(8,128)(2,1)S(1)} %get-tuple-element.40.refs_0_, ...), custom_call_target="tpu_custom_call" | custom-call | flops 2000000000 | bytes 4000000 | tf_op jit(solution)/shard_map/keys/pallas_call | solution.py:297
  16.4 0.0 collective-permute-done.2.refs_3_
  16.4 1.5 %collective-permute-done.3.refs_4_ = bf16[2,128,128]{2,1,0:T(8,128)(2,1)S(1)} collective-permute-done((bf16[2,128,128]{2,1,0:T(8,128)(2,1)S(1)}, bf16[2,128,128]{2,1,0:T(8,128)(2,1)S(1)}, u32[]{:S(2)}, u32[]{:S(2)}) %collective-permute-start.3) | collective-permute-done | bytes 65568 | tf_op jit(solution)/shard_map/ppermute | solution.py:623
  17.9 1.1 %values.1 = (f32[8,128,256]{2,1,0:T(8,128)S(1)}, bf16[128,256]{1,0:T(8,128)(2,1)S(1)}, f32[7,128,256]{2,1,0:T(8,128)S(1)}) custom-call(bf16[4,256,128]{2,1,0:T(8,128)(2,1)S(1)} %get-tuple-element.48.refs_0_, bf16[4,256,128]{2,1,0:T(8,128)(2,1)S(1)} %collective-permute-done.refs_1_, bf16[2,128,128]{2,1,0:T(8,128)(2,1)S(1)} %collective-permute-done.1.refs_2_, ...), custom_call_target="tpu_custom_call" | custom-call | flops 1000000000 | bytes 4000000 | tf_op jit(solution)/shard_map/values/pallas_call | solution.py:310
  19.1 3.5 %collective-permute-start.12 = (bf16[128,256]{1,0:T(8,128)(2,1)S(1)}, bf16[128,256]{1,0:T(8,128)(2,1)S(1)}, u32[]{:S(2)}, u32[]{:S(2)}) collective-permute-start(bf16[128,256]{1,0:T(8,128)(2,1)S(1)} %get-tuple-element.47.own_ref), channel_id=1, source_target_pairs={{0,64},{4,68},{8,72},{12,76},{16,80},{20,84},{24,88},{28,92},{32,9... | collective-permute-start | bytes 196616 | tf_op jit(solution)/shard_map/ppermute | solution.py:647
  22.6 2.9 %collective-permute-start.11 = (bf16[128,256]{1,0:T(8,128)(2,1)S(1)}, bf16[128,256]{1,0:T(8,128)(2,1)S(1)}, u32[]{:S(2)}, u32[]{:S(2)}) collective-permute-start(bf16[128,256]{1,0:T(8,128)(2,1)S(1)} %get-tuple-element.47.own_ref), channel_id=1, source_target_pairs={{0,32},{4,36},{8,40},{12,44},{16,48},{20,52},{24,56},{28,60},{32,6... | collective-permute-start | bytes 196616 | tf_op jit(solution)/shard_map/ppermute | solution.py:647
  25.6 0.1 collective-permute-start.8
  25.7 2.0 %collective-permute-start.9 = (bf16[2,128,128]{2,1,0:T(8,128)(2,1)S(1)}, bf16[2,128,128]{2,1,0:T(8,128)(2,1)S(1)}, u32[]{:S(2)}, u32[]{:S(2)}) collective-permute-start(bf16[2,128,128]{2,1,0:T(8,128)(2,1)S(1)} %pad_maximum_fusion.7), channel_id=1, source_target_pairs={{0,16},{4,20},{8,24},{12,28},{16,0},{20,4},{24,8},{28,12},{32,48},... | collective-permute-start | bytes 196616 | tf_op jit(solution)/shard_map/ppermute | solution.py:623
  27.7 2.8 %collective-permute-start.10 = (bf16[2,128,128]{2,1,0:T(8,128)(2,1)S(1)}, bf16[2,128,128]{2,1,0:T(8,128)(2,1)S(1)}, u32[]{:S(2)}, u32[]{:S(2)}) collective-permute-start(bf16[2,128,128]{2,1,0:T(8,128)(2,1)S(1)} %pad_maximum_fusion.8), channel_id=1, source_target_pairs={{0,24},{4,28},{8,16},{12,20},{16,8},{20,12},{24,0},{28,4},{32,56},... | collective-permute-start | bytes 196616 | tf_op jit(solution)/shard_map/ppermute | solution.py:623
  30.5 0.3 combine.1
  30.9 1.9 %collective-permute-start.14 = (bf16[128,256]{1,0:T(8,128)(2,1)S(1)}, bf16[128,256]{1,0:T(8,128)(2,1)S(1)}, u32[]{:S(2)}, u32[]{:S(2)}) collective-permute-start(bf16[128,256]{1,0:T(8,128)(2,1)S(1)} %get-tuple-element.54), channel_id=1, source_target_pairs={{0,96},{4,100},{8,104},{12,108},{16,112},{20,116},{24,120},{28,124... | collective-permute-start | bytes 196616 | tf_op jit(solution)/shard_map/ppermute | solution.py:647
  32.8 0.7 collective-permute-start.13
  33.5 0.0 collective-permute-done.8.refs_2_
  33.5 0.0 slice-start.1
  33.5 1.3 %query.1.no_ref = f32[1024,256]{1,0:T(8,128)S(1)} custom-call(bf16[4,256,128]{2,1,0:T(8,128)(2,1)S(1)} %get-tuple-element.48.refs_0_, bf16[4,256,128]{2,1,0:T(8,128)(2,1)S(1)} %collective-permute-done.refs_1_, bf16[2,128,128]{2,1,0:T(8,128)(2,1)S(1)} %collective-permute-done.8.refs_2_, bf16[2,128,128]{2,1,0:T(8,128)(2,1)S(1)} %collective-permute-done.9.refs_3_, ...), custom_call_target="tpu_custom_call" | custom-call | flops 1000000000 | bytes 4000000 | tf_op jit(solution)/shard_map/query/pallas_call | solution.py:365
  34.8 6.1 %collective-permute-done.14.three_ref = bf16[128,256]{1,0:T(8,128)(2,1)S(1)} collective-permute-done((bf16[128,256]{1,0:T(8,128)(2,1)S(1)}, bf16[128,256]{1,0:T(8,128)(2,1)S(1)}, u32[]{:S(2)}, u32[]{:S(2)}) %collective-permute-start.14) | collective-permute-done | bytes 65568 | tf_op jit(solution)/shard_map/ppermute | solution.py:647
  40.9 0.0 collective-permute-done.13.six_ref
  40.9 0.7 norm.1.normed_ref
  41.6 2.1 %collective-permute-start.15 = (bf16[1024,128]{1,0:T(8,128)(2,1)S(1)}, bf16[1024,128]{1,0:T(8,128)(2,1)S(1)}, u32[]{:S(2)}, u32[]{:S(2)}) collective-permute-start(bf16[1024,128]{1,0:T(8,128)(2,1)S(1)} %norm.1.normed_ref), channel_id=1, source_target_pairs={{0,32},{4,36},{8,40},{12,44},{16,48},{20,52},{24,56},{28,60},{32,6... | collective-permute-start | bytes 786440 | tf_op jit(solution)/shard_map/ppermute | solution.py:647
  43.7 1.3 %own.1 = (f32[1024,128]{1,0:T(8,128)S(1)}, f32[2,1024,128]{2,1,0:T(8,128)S(1)}, bf16[1024,128]{1,0:T(8,128)(2,1)S(1)}) custom-call(bf16[1024,128]{1,0:T(8,128)(2,1)S(1)} %norm.1.normed_ref, bf16[8,128,384]{2,1,0:T(8,128)(2,1)S(1)} %copy-done.1), custom_call_target="tpu_custom_call" | custom-call | flops 1000000000 | bytes 3000000 | tf_op jit(solution)/shard_map/own/pallas_call | solution.py:487
  45.0 6.3 %collective-permute-done.15.halo_ref = bf16[1024,128]{1,0:T(8,128)(2,1)S(1)} collective-permute-done((bf16[1024,128]{1,0:T(8,128)(2,1)S(1)}, bf16[1024,128]{1,0:T(8,128)(2,1)S(1)}, u32[]{:S(2)}, u32[]{:S(2)}) %collective-permute-start.15) | collective-permute-done | bytes 262176 | tf_op jit(solution)/shard_map/ppermute | solution.py:647
  51.3 1.5 %halo.1 = (bf16[2,128,128]{2,1,0:T(8,128)(2,1)S(1)}, bf16[2,128,128]{2,1,0:T(8,128)(2,1)S(1)}, bf16[2,128,128]{2,1,0:T(8,128)(2,1)S(1)}, bf16[2,128,128]{2,1,0:T(8,128)(2,1)S(1)}) custom-call(bf16[1024,128]{1,0:T(8,128)(2,1)S(1)} %collective-permute-done.15.halo_ref, bf16[8,128,384]{2,1,0:T(8,128)(2,1)S(1)} %copy-done.1, ...), custom_call_target="tpu_custom_call" | custom-call | flops 1000000000 | bytes 3000000 | tf_op jit(solution)/shard_map/halo/pallas_call | solution.py:538
  52.8 0.1 collective-permute-start.16
  52.9 0.4 collective-permute-start.18
  53.3 3.6 %collective-permute-start.20 = (bf16[2,128,128]{2,1,0:T(8,128)(2,1)S(1)}, bf16[2,128,128]{2,1,0:T(8,128)(2,1)S(1)}, u32[]{:S(2)}, u32[]{:S(2)}) collective-permute-start(bf16[2,128,128]{2,1,0:T(8,128)(2,1)S(1)} %get-tuple-element.61), channel_id=1, source_target_pairs={{0,16},{4,20},{8,24},{12,28},{16,0},{20,4},{24,8},{28,12},{32,48},... | collective-permute-start | bytes 196616 | tf_op jit(solution)/shard_map/ppermute | solution.py:623
  57.0 0.2 collective-permute-done.16.one
  57.1 0.0 collective-permute-start.17
  57.1 2.1 %collective-permute-done.20.two = bf16[2,128,128]{2,1,0:T(8,128)(2,1)S(1)} collective-permute-done((bf16[2,128,128]{2,1,0:T(8,128)(2,1)S(1)}, bf16[2,128,128]{2,1,0:T(8,128)(2,1)S(1)}, u32[]{:S(2)}, u32[]{:S(2)}) %collective-permute-start.20) | collective-permute-done | bytes 65568 | tf_op jit(solution)/shard_map/ppermute | solution.py:623
  59.2 0.1 collective-permute-start.22
  59.3 0.5 collective-permute-start.21
  59.8 0.0 collective-permute-done.18.three
  59.8 0.1 collective-permute-start.19
  59.9 0.6 collective-permute-done.22.two_came
  60.5 0.2 collective-permute-done.21.own_came
  60.7 0.7 early.1.acc_ref
  61.4 0.0 collective-permute-done.19.three_came
  61.4 0.7 late.1
  62.2 1.6 %collective-permute-start.23 = (bf16[32,2048]{1,0:T(8,128)(2,1)S(1)}, bf16[32,2048]{1,0:T(8,128)(2,1)S(1)}, u32[]{:S(2)}, u32[]{:S(2)}) collective-permute-start(bf16[32,2048]{1,0:T(8,128)(2,1)S(1)} %get-tuple-element.66), channel_id=1, source_target_pairs={{0,1},{1,2},{2,3},{3,0},{4,5},{5,6},{6,7},{7,4},{8,9},{9,10},{10,1... | collective-permute-start | bytes 393224 | tf_op jit(solution)/shard_map/ppermute | solution.py:674
  63.8 1.7 %collective-permute-start.25 = (bf16[32,2048]{1,0:T(8,128)(2,1)S(1)}, bf16[32,2048]{1,0:T(8,128)(2,1)S(1)}, u32[]{:S(2)}, u32[]{:S(2)}) collective-permute-start(bf16[32,2048]{1,0:T(8,128)(2,1)S(1)} %get-tuple-element.67), channel_id=1, source_target_pairs={{0,3},{1,0},{2,1},{3,2},{4,7},{5,4},{6,5},{7,6},{8,11},{9,8},{10,9... | collective-permute-start | bytes 393224 | tf_op jit(solution)/shard_map/ppermute | solution.py:674
  65.5 1.8 %collective-permute-start.26 = (bf16[32,2048]{1,0:T(8,128)(2,1)S(1)}, bf16[32,2048]{1,0:T(8,128)(2,1)S(1)}, u32[]{:S(2)}, u32[]{:S(2)}) collective-permute-start(bf16[32,2048]{1,0:T(8,128)(2,1)S(1)} %get-tuple-element.69), channel_id=1, source_target_pairs={{0,3},{1,0},{2,1},{3,2},{4,7},{5,4},{6,5},{7,6},{8,11},{9,8},{10,9... | collective-permute-start | bytes 393224 | tf_op jit(solution)/shard_map/ppermute | solution.py:674
  67.3 0.2 collective-permute-start.28
  67.5 1.8 %collective-permute-done.23 = bf16[32,2048]{1,0:T(8,128)(2,1)S(1)} collective-permute-done((bf16[32,2048]{1,0:T(8,128)(2,1)S(1)}, bf16[32,2048]{1,0:T(8,128)(2,1)S(1)}, u32[]{:S(2)}, u32[]{:S(2)}) %collective-permute-start.23) | collective-permute-done | bytes 131104 | tf_op jit(solution)/shard_map/ppermute | solution.py:674
  69.3 0.4 collective-permute-start.24
  69.7 2.4 %collective-permute-done.26 = bf16[32,2048]{1,0:T(8,128)(2,1)S(1)} collective-permute-done((bf16[32,2048]{1,0:T(8,128)(2,1)S(1)}, bf16[32,2048]{1,0:T(8,128)(2,1)S(1)}, u32[]{:S(2)}, u32[]{:S(2)}) %collective-permute-start.26) | collective-permute-done | bytes 131104 | tf_op jit(solution)/shard_map/ppermute | solution.py:674
  72.1 3.1 %collective-permute-start.27 = (bf16[32,2048]{1,0:T(8,128)(2,1)S(1)}, bf16[32,2048]{1,0:T(8,128)(2,1)S(1)}, u32[]{:S(2)}, u32[]{:S(2)}) collective-permute-start(bf16[32,2048]{1,0:T(8,128)(2,1)S(1)} %add_convert_fusion), channel_id=1, source_target_pairs={{0,3},{1,0},{2,1},{3,2},{4,7},{5,4},{6,5},{7,6},{8,11},{9,8},{10,9... | collective-permute-start | bytes 393224 | tf_op jit(solution)/shard_map/ppermute | solution.py:674
  75.2 1.0 %collective-permute-done.24 = bf16[32,2048]{1,0:T(8,128)(2,1)S(1)} collective-permute-done((bf16[32,2048]{1,0:T(8,128)(2,1)S(1)}, bf16[32,2048]{1,0:T(8,128)(2,1)S(1)}, u32[]{:S(2)}, u32[]{:S(2)}) %collective-permute-start.24) | collective-permute-done | bytes 131104 | tf_op jit(solution)/shard_map/ppermute | solution.py:674
  76.3 1.4 %collective-permute-done.27 = bf16[32,2048]{1,0:T(8,128)(2,1)S(1)} collective-permute-done((bf16[32,2048]{1,0:T(8,128)(2,1)S(1)}, bf16[32,2048]{1,0:T(8,128)(2,1)S(1)}, u32[]{:S(2)}, u32[]{:S(2)}) %collective-permute-start.27) | collective-permute-done | bytes 131104 | tf_op jit(solution)/shard_map/ppermute | solution.py:674
  77.8 0.8 fusion
  (37 shorter events, 0.3 us)
Async XLA Ops:
  1.0 1.9 %collective-permute-start.4 = (bf16[4,144,128]{2,1,0:T(8,128)(2,1)S(1)}, bf16[4,144,128]{2,1,0:T(8,128)(2,1)S(1)}, u32[]{:S(2)}, u32[]{:S(2)}) collective-permute-start(bf16[4,144,128]{2,1,0:T(8,128)(2,1)S(1)} %get-tuple-element.41), channel_id=1, source_target_pairs={{0,4},{4,0},{8,12},{12,8},{16,20},{20,16},{24,28},{28,24},{32,36},... | collective-permute-start | bytes 442376 | tf_op jit(solution)/shard_map/ppermute | solution.py:623
  2.3 5.6 %collective-permute-start = (bf16[4,256,128]{2,1,0:T(8,128)(2,1)S(1)}, bf16[4,256,128]{2,1,0:T(8,128)(2,1)S(1)}, u32[]{:S(2)}, u32[]{:S(2)}) collective-permute-start(bf16[4,256,128]{2,1,0:T(8,128)(2,1)S(1)} %get-tuple-element.39), channel_id=1, source_target_pairs={{0,4},{4,0},{8,12},{12,8},{16,20},{20,16},{24,28},{28,24},{32,36},... | collective-permute-start | bytes 786440 | tf_op jit(solution)/shard_map/ppermute | solution.py:623
  2.9 9.4 %collective-permute-start.5 = (bf16[2,144,128]{2,1,0:T(8,128)(2,1)S(1)}, bf16[2,144,128]{2,1,0:T(8,128)(2,1)S(1)}, u32[]{:S(2)}, u32[]{:S(2)}) collective-permute-start(bf16[2,144,128]{2,1,0:T(8,128)(2,1)S(1)} %pad_maximum_fusion), channel_id=1, source_target_pairs={{0,8},{4,12},{8,0},{12,4},{16,24},{20,28},{24,16},{28,20},{32,40},... | collective-permute-start | bytes 221192 | tf_op jit(solution)/shard_map/ppermute | solution.py:623
  4.5 8.4 %collective-permute-start.6 = (bf16[2,144,128]{2,1,0:T(8,128)(2,1)S(1)}, bf16[2,144,128]{2,1,0:T(8,128)(2,1)S(1)}, u32[]{:S(2)}, u32[]{:S(2)}) collective-permute-start(bf16[2,144,128]{2,1,0:T(8,128)(2,1)S(1)} %pad_maximum_fusion.1), channel_id=1, source_target_pairs={{0,16},{4,20},{8,24},{12,28},{16,0},{20,4},{24,8},{28,12},{32,48},... | collective-permute-start | bytes 221192 | tf_op jit(solution)/shard_map/ppermute | solution.py:623
  7.3 6.4 %collective-permute-start.7 = (bf16[2,144,128]{2,1,0:T(8,128)(2,1)S(1)}, bf16[2,144,128]{2,1,0:T(8,128)(2,1)S(1)}, u32[]{:S(2)}, u32[]{:S(2)}) collective-permute-start(bf16[2,144,128]{2,1,0:T(8,128)(2,1)S(1)} %pad_maximum_fusion.2), channel_id=1, source_target_pairs={{0,24},{4,28},{8,16},{12,20},{16,8},{20,12},{24,0},{28,4},{32,56},... | collective-permute-start | bytes 221192 | tf_op jit(solution)/shard_map/ppermute | solution.py:623
  7.9 8.5 %collective-permute-start.1 = (bf16[2,128,128]{2,1,0:T(8,128)(2,1)S(1)}, bf16[2,128,128]{2,1,0:T(8,128)(2,1)S(1)}, u32[]{:S(2)}, u32[]{:S(2)}) collective-permute-start(bf16[2,128,128]{2,1,0:T(8,128)(2,1)S(1)} %pad_maximum_fusion.3), channel_id=1, source_target_pairs={{0,8},{4,12},{8,0},{12,4},{16,24},{20,28},{24,16},{28,20},{32,40},... | collective-permute-start | bytes 196616 | tf_op jit(solution)/shard_map/ppermute | solution.py:623
  8.3 8.1 %collective-permute-start.2 = (bf16[2,128,128]{2,1,0:T(8,128)(2,1)S(1)}, bf16[2,128,128]{2,1,0:T(8,128)(2,1)S(1)}, u32[]{:S(2)}, u32[]{:S(2)}) collective-permute-start(bf16[2,128,128]{2,1,0:T(8,128)(2,1)S(1)} %pad_maximum_fusion.4), channel_id=1, source_target_pairs={{0,16},{4,20},{8,24},{12,28},{16,0},{20,4},{24,8},{28,12},{32,48},... | collective-permute-start | bytes 196616 | tf_op jit(solution)/shard_map/ppermute | solution.py:623
  12.3 28.6 %copy-start = (f32[128]{0:T(128)S(1)}, f32[128]{0:T(128)}, u32[]{:S(2)}) copy-start(f32[128]{0:T(128)} %param.13) | copy-start | bytes 1540
  12.3 31.4 %copy-start.1 = (bf16[8,128,384]{2,1,0:T(8,128)(2,1)S(1)}, bf16[8,128,384]{2,1,0:T(8,128)(2,1)}, u32[]{:S(2)}) copy-start(bf16[8,128,384]{2,1,0:T(8,128)(2,1)} %weight_ref.5) | copy-start | bytes 2359300
  12.4 5.6 %collective-permute-start.3 = (bf16[2,128,128]{2,1,0:T(8,128)(2,1)S(1)}, bf16[2,128,128]{2,1,0:T(8,128)(2,1)S(1)}, u32[]{:S(2)}, u32[]{:S(2)}) collective-permute-start(bf16[2,128,128]{2,1,0:T(8,128)(2,1)S(1)} %pad_maximum_fusion.5), channel_id=1, source_target_pairs={{0,24},{4,28},{8,16},{12,20},{16,8},{20,12},{24,0},{28,4},{32,56},... | collective-permute-start | bytes 196616 | tf_op jit(solution)/shard_map/ppermute | solution.py:623
  17.9 42.7 %slice-start = ((s8[8388608]{0:T(1024)(128)(4,1)}), s8[4194304]{0:T(1024)(128)(4,1)S(1)}, s32[]{:S(2)}) async-start(s8[8388608]{0:T(1024)(128)(4,1)} %bitcast.9), calls=%async_computation | async-start | bytes 8388608
  19.1 11.5 %collective-permute-start.12 = (bf16[128,256]{1,0:T(8,128)(2,1)S(1)}, bf16[128,256]{1,0:T(8,128)(2,1)S(1)}, u32[]{:S(2)}, u32[]{:S(2)}) collective-permute-start(bf16[128,256]{1,0:T(8,128)(2,1)S(1)} %get-tuple-element.47.own_ref), channel_id=1, source_target_pairs={{0,64},{4,68},{8,72},{12,76},{16,80},{20,84},{24,88},{28,92},{32,9... | collective-permute-start | bytes 196616 | tf_op jit(solution)/shard_map/ppermute | solution.py:647
  22.6 7.9 %collective-permute-start.11 = (bf16[128,256]{1,0:T(8,128)(2,1)S(1)}, bf16[128,256]{1,0:T(8,128)(2,1)S(1)}, u32[]{:S(2)}, u32[]{:S(2)}) collective-permute-start(bf16[128,256]{1,0:T(8,128)(2,1)S(1)} %get-tuple-element.47.own_ref), channel_id=1, source_target_pairs={{0,32},{4,36},{8,40},{12,44},{16,48},{20,52},{24,56},{28,60},{32,6... | collective-permute-start | bytes 196616 | tf_op jit(solution)/shard_map/ppermute | solution.py:647
  25.6 7.9 %collective-permute-start.8 = (bf16[2,128,128]{2,1,0:T(8,128)(2,1)S(1)}, bf16[2,128,128]{2,1,0:T(8,128)(2,1)S(1)}, u32[]{:S(2)}, u32[]{:S(2)}) collective-permute-start(bf16[2,128,128]{2,1,0:T(8,128)(2,1)S(1)} %pad_maximum_fusion.6), channel_id=1, source_target_pairs={{0,8},{4,12},{8,0},{12,4},{16,24},{20,28},{24,16},{28,20},{32,40},... | collective-permute-start | bytes 196616 | tf_op jit(solution)/shard_map/ppermute | solution.py:623
  25.7 7.8 %collective-permute-start.9 = (bf16[2,128,128]{2,1,0:T(8,128)(2,1)S(1)}, bf16[2,128,128]{2,1,0:T(8,128)(2,1)S(1)}, u32[]{:S(2)}, u32[]{:S(2)}) collective-permute-start(bf16[2,128,128]{2,1,0:T(8,128)(2,1)S(1)} %pad_maximum_fusion.7), channel_id=1, source_target_pairs={{0,16},{4,20},{8,24},{12,28},{16,0},{20,4},{24,8},{28,12},{32,48},... | collective-permute-start | bytes 196616 | tf_op jit(solution)/shard_map/ppermute | solution.py:623
  27.7 5.8 %collective-permute-start.10 = (bf16[2,128,128]{2,1,0:T(8,128)(2,1)S(1)}, bf16[2,128,128]{2,1,0:T(8,128)(2,1)S(1)}, u32[]{:S(2)}, u32[]{:S(2)}) collective-permute-start(bf16[2,128,128]{2,1,0:T(8,128)(2,1)S(1)} %pad_maximum_fusion.8), channel_id=1, source_target_pairs={{0,24},{4,28},{8,16},{12,20},{16,8},{20,12},{24,0},{28,4},{32,56},... | collective-permute-start | bytes 196616 | tf_op jit(solution)/shard_map/ppermute | solution.py:623
  30.9 10.0 %collective-permute-start.14 = (bf16[128,256]{1,0:T(8,128)(2,1)S(1)}, bf16[128,256]{1,0:T(8,128)(2,1)S(1)}, u32[]{:S(2)}, u32[]{:S(2)}) collective-permute-start(bf16[128,256]{1,0:T(8,128)(2,1)S(1)} %get-tuple-element.54), channel_id=1, source_target_pairs={{0,96},{4,100},{8,104},{12,108},{16,112},{20,116},{24,120},{28,124... | collective-permute-start | bytes 196616 | tf_op jit(solution)/shard_map/ppermute | solution.py:647
  32.8 8.1 %collective-permute-start.13 = (bf16[128,256]{1,0:T(8,128)(2,1)S(1)}, bf16[128,256]{1,0:T(8,128)(2,1)S(1)}, u32[]{:S(2)}, u32[]{:S(2)}) collective-permute-start(bf16[128,256]{1,0:T(8,128)(2,1)S(1)} %get-tuple-element.54), channel_id=1, source_target_pairs={{0,192},{4,196},{8,200},{12,204},{16,208},{20,212},{24,216},{28,22... | collective-permute-start | bytes 196616 | tf_op jit(solution)/shard_map/ppermute | solution.py:647
  33.5 27.2 %slice-start.1 = ((s8[8388608]{0:T(1024)(128)(4,1)}), s8[4194304]{0:T(1024)(128)(4,1)S(1)}, s32[]{:S(2)}) async-start(s8[8388608]{0:T(1024)(128)(4,1)} %bitcast.9), calls=%async_computation.1 | async-start | bytes 8388608
  41.6 9.7 %collective-permute-start.15 = (bf16[1024,128]{1,0:T(8,128)(2,1)S(1)}, bf16[1024,128]{1,0:T(8,128)(2,1)S(1)}, u32[]{:S(2)}, u32[]{:S(2)}) collective-permute-start(bf16[1024,128]{1,0:T(8,128)(2,1)S(1)} %norm.1.normed_ref), channel_id=1, source_target_pairs={{0,32},{4,36},{8,40},{12,44},{16,48},{20,52},{24,56},{28,60},{32,6... | collective-permute-start | bytes 786440 | tf_op jit(solution)/shard_map/ppermute | solution.py:647
  52.8 4.4 %collective-permute-start.16 = (bf16[2,128,128]{2,1,0:T(8,128)(2,1)S(1)}, bf16[2,128,128]{2,1,0:T(8,128)(2,1)S(1)}, u32[]{:S(2)}, u32[]{:S(2)}) collective-permute-start(bf16[2,128,128]{2,1,0:T(8,128)(2,1)S(1)} %get-tuple-element.58), channel_id=1, source_target_pairs={{0,8},{4,12},{8,0},{12,4},{16,24},{20,28},{24,16},{28,20},{32,40},... | collective-permute-start | bytes 196616 | tf_op jit(solution)/shard_map/ppermute | solution.py:623
  52.9 6.9 %collective-permute-start.18 = (bf16[2,128,128]{2,1,0:T(8,128)(2,1)S(1)}, bf16[2,128,128]{2,1,0:T(8,128)(2,1)S(1)}, u32[]{:S(2)}, u32[]{:S(2)}) collective-permute-start(bf16[2,128,128]{2,1,0:T(8,128)(2,1)S(1)} %get-tuple-element.59), channel_id=1, source_target_pairs={{0,24},{4,28},{8,16},{12,20},{16,8},{20,12},{24,0},{28,4},{32,56},... | collective-permute-start | bytes 196616 | tf_op jit(solution)/shard_map/ppermute | solution.py:623
  53.3 5.9 %collective-permute-start.20 = (bf16[2,128,128]{2,1,0:T(8,128)(2,1)S(1)}, bf16[2,128,128]{2,1,0:T(8,128)(2,1)S(1)}, u32[]{:S(2)}, u32[]{:S(2)}) collective-permute-start(bf16[2,128,128]{2,1,0:T(8,128)(2,1)S(1)} %get-tuple-element.61), channel_id=1, source_target_pairs={{0,16},{4,20},{8,24},{12,28},{16,0},{20,4},{24,8},{28,12},{32,48},... | collective-permute-start | bytes 196616 | tf_op jit(solution)/shard_map/ppermute | solution.py:623
  57.1 4.3 %collective-permute-start.17 = (bf16[128,128]{1,0:T(8,128)(2,1)S(1)}, bf16[128,128]{1,0:T(8,128)(2,1)S(1)}, u32[]{:S(2)}, u32[]{:S(2)}) collective-permute-start(bf16[128,128]{1,0:T(8,128)(2,1)S(1)} %slice_bitcast_fusion.1), channel_id=1, source_target_pairs={{0,4},{4,0},{8,12},{12,8},{16,20},{20,16},{24,28},{28,24},{32,36},... | collective-permute-start | bytes 98312 | tf_op jit(solution)/shard_map/ppermute | solution.py:623
  59.2 1.3 %collective-permute-start.22 = (bf16[128,128]{1,0:T(8,128)(2,1)S(1)}, bf16[128,128]{1,0:T(8,128)(2,1)S(1)}, u32[]{:S(2)}, u32[]{:S(2)}) collective-permute-start(bf16[128,128]{1,0:T(8,128)(2,1)S(1)} %slice_bitcast_fusion.2), channel_id=1, source_target_pairs={{0,4},{4,0},{8,12},{12,8},{16,20},{20,16},{24,28},{28,24},{32,36},... | collective-permute-start | bytes 98312 | tf_op jit(solution)/shard_map/ppermute | solution.py:623
  59.3 1.4 %collective-permute-start.21 = (bf16[128,128]{1,0:T(8,128)(2,1)S(1)}, bf16[128,128]{1,0:T(8,128)(2,1)S(1)}, u32[]{:S(2)}, u32[]{:S(2)}) collective-permute-start(bf16[128,128]{1,0:T(8,128)(2,1)S(1)} %slice_bitcast_fusion.3), channel_id=1, source_target_pairs={{0,4},{4,0},{8,12},{12,8},{16,20},{20,16},{24,28},{28,24},{32,36},... | collective-permute-start | bytes 98312 | tf_op jit(solution)/shard_map/ppermute | solution.py:623
  59.8 1.6 %collective-permute-start.19 = (bf16[128,128]{1,0:T(8,128)(2,1)S(1)}, bf16[128,128]{1,0:T(8,128)(2,1)S(1)}, u32[]{:S(2)}, u32[]{:S(2)}) collective-permute-start(bf16[128,128]{1,0:T(8,128)(2,1)S(1)} %slice_bitcast_fusion), channel_id=1, source_target_pairs={{0,4},{4,0},{8,12},{12,8},{16,20},{20,16},{24,28},{28,24},{32,36},... | collective-permute-start | bytes 98312 | tf_op jit(solution)/shard_map/ppermute | solution.py:623
  62.2 7.1 %collective-permute-start.23 = (bf16[32,2048]{1,0:T(8,128)(2,1)S(1)}, bf16[32,2048]{1,0:T(8,128)(2,1)S(1)}, u32[]{:S(2)}, u32[]{:S(2)}) collective-permute-start(bf16[32,2048]{1,0:T(8,128)(2,1)S(1)} %get-tuple-element.66), channel_id=1, source_target_pairs={{0,1},{1,2},{2,3},{3,0},{4,5},{5,6},{6,7},{7,4},{8,9},{9,10},{10,1... | collective-permute-start | bytes 393224 | tf_op jit(solution)/shard_map/ppermute | solution.py:674
  63.8 11.4 %collective-permute-start.25 = (bf16[32,2048]{1,0:T(8,128)(2,1)S(1)}, bf16[32,2048]{1,0:T(8,128)(2,1)S(1)}, u32[]{:S(2)}, u32[]{:S(2)}) collective-permute-start(bf16[32,2048]{1,0:T(8,128)(2,1)S(1)} %get-tuple-element.67), channel_id=1, source_target_pairs={{0,3},{1,0},{2,1},{3,2},{4,7},{5,4},{6,5},{7,6},{8,11},{9,8},{10,9... | collective-permute-start | bytes 393224 | tf_op jit(solution)/shard_map/ppermute | solution.py:674
  65.5 6.6 %collective-permute-start.26 = (bf16[32,2048]{1,0:T(8,128)(2,1)S(1)}, bf16[32,2048]{1,0:T(8,128)(2,1)S(1)}, u32[]{:S(2)}, u32[]{:S(2)}) collective-permute-start(bf16[32,2048]{1,0:T(8,128)(2,1)S(1)} %get-tuple-element.69), channel_id=1, source_target_pairs={{0,3},{1,0},{2,1},{3,2},{4,7},{5,4},{6,5},{7,6},{8,11},{9,8},{10,9... | collective-permute-start | bytes 393224 | tf_op jit(solution)/shard_map/ppermute | solution.py:674
  67.3 9.0 %collective-permute-start.28 = (bf16[32,2048]{1,0:T(8,128)(2,1)S(1)}, bf16[32,2048]{1,0:T(8,128)(2,1)S(1)}, u32[]{:S(2)}, u32[]{:S(2)}) collective-permute-start(bf16[32,2048]{1,0:T(8,128)(2,1)S(1)} %get-tuple-element.70), channel_id=1, source_target_pairs={{0,1},{1,2},{2,3},{3,0},{4,5},{5,6},{6,7},{7,4},{8,9},{9,10},{10,1... | collective-permute-start | bytes 393224 | tf_op jit(solution)/shard_map/ppermute | solution.py:674
  69.3 7.0 %collective-permute-start.24 = (bf16[32,2048]{1,0:T(8,128)(2,1)S(1)}, bf16[32,2048]{1,0:T(8,128)(2,1)S(1)}, u32[]{:S(2)}, u32[]{:S(2)}) collective-permute-start(bf16[32,2048]{1,0:T(8,128)(2,1)S(1)} %add_convert_fusion.1), channel_id=1, source_target_pairs={{0,1},{1,2},{2,3},{3,0},{4,5},{5,6},{6,7},{7,4},{8,9},{9,10},{10,1... | collective-permute-start | bytes 393224 | tf_op jit(solution)/shard_map/ppermute | solution.py:674
  72.1 5.6 %collective-permute-start.27 = (bf16[32,2048]{1,0:T(8,128)(2,1)S(1)}, bf16[32,2048]{1,0:T(8,128)(2,1)S(1)}, u32[]{:S(2)}, u32[]{:S(2)}) collective-permute-start(bf16[32,2048]{1,0:T(8,128)(2,1)S(1)} %add_convert_fusion), channel_id=1, source_target_pairs={{0,3},{1,0},{2,1},{3,2},{4,7},{5,4},{6,5},{7,6},{8,11},{9,8},{10,9... | collective-permute-start | bytes 393224 | tf_op jit(solution)/shard_map/ppermute | solution.py:674

commit v12 on v10

--- a/solution.py
+++ b/solution.py
@@ -182,8 +182,7 @@
 
 
 def key_kernel(*refs):
-    k_ref, mix_ref, inverse_ref, w_ref, tail_ref, reach_ref = refs[5:11]
-    maps = refs[11]
+    k_ref, mix_ref, inverse_ref, w_ref, tail_ref, reach_ref = refs[5:]
     me = lax.axis_index("seq") % PLANE
     row, col = iotas()
     gather_slots(refs[:5], k_ref)
@@ -233,12 +232,7 @@
     made = [dot_tn(jnp.concatenate([keys[d], keys[d]], axis=0), halves[d]) for d in every]
     for d in every:
         g_end = found[d][0][:, C - 1 : C]
-        maps[jnp.bitwise_xor(me, d)] = jnp.where(row == col, jnp.exp(g_end), 0.0) - made[d]
-    one = [maps[i] for i in every]
-    two = [mm(one[2 * i + 1], one[2 * i]) for i in range(4)]
-    four = [mm(two[2 * i + 1], two[2 * i]) for i in range(2)]
-    for i, part in enumerate(one + two + four + [mm(four[1], four[0])]):
-        reach_ref[i] = part
+        reach_ref[jnp.bitwise_xor(me, d)] = jnp.where(row == col, jnp.exp(g_end), 0.0) - made[d]
 
 
 def value_kernel(*refs):
@@ -247,7 +241,9 @@
     me = lax.axis_index("seq") % PLANE
     gather_slots(refs[:5], v_ref, slice(0, C))
     every = range(PLANE)
+    reach = [reach_ref[i] for i in every]
     u = [mm_exact_right(inverse_ref[d], v_ref[d]) for d in every]
+    reach_two = [mm(reach[2 * i + 1], reach[2 * i]) for i in range(4)]
     halves = []
     for d in every:
         wu_ref[d, :, :C] = w_ref[d]
@@ -255,17 +251,18 @@
         halves.append(jnp.concatenate(split(u[d] * tail_ref[d]), axis=0))
     keys = [k_ref[d, 0:C, :] for d in every]
     made = [dot_tn(jnp.concatenate([keys[d], keys[d]], axis=0), halves[d]) for d in every]
+    reach_four = [mm(reach_two[2 * i + 1], reach_two[2 * i]) for i in range(2)]
     for d in every:
         states[jnp.bitwise_xor(me, d)] = made[d]
     one = [states[i] for i in every]
-    two = [mm(reach_ref[2 * i + 1], one[2 * i]) + one[2 * i + 1] for i in range(4)]
-    four = [mm(reach_ref[8 + 2 * i + 1], two[2 * i]) + two[2 * i + 1] for i in range(2)]
-    last = mm(reach_ref[13], four[0]) + four[1]
-    ab_ref[:, :C] = reach_ref[14].astype(BF16)
-    ab_ref[:, C:] = last.astype(BF16)
-    both = ((0, one[0]), (8, two[0]), (2, one[2]), (12, four[0]), (4, one[4]), (10, two[2]), (6, one[6]))
-    for i, (at, state) in enumerate(both):
-        level_ref[i, :, :C] = reach_ref[at]
+    two = [mm(reach[2 * i + 1], one[2 * i]) + one[2 * i + 1] for i in range(4)]
+    ab_ref[:, :C] = mm(reach_four[1], reach_four[0]).astype(BF16)
+    four = [mm(reach_two[2 * i + 1], two[2 * i]) + two[2 * i + 1] for i in range(2)]
+    ab_ref[:, C:] = (mm(reach_four[1], four[0]) + four[1]).astype(BF16)
+    levels = [(reach[0], one[0]), (reach_two[0], two[0]), (reach[2], one[2])]
+    levels += [(reach_four[0], four[0]), (reach[4], one[4]), (reach_two[2], two[2])]
+    for i, (across, state) in enumerate(levels + [(reach[6], one[6])]):
+        level_ref[i, :, :C] = across
         level_ref[i, :, C:] = state
 
 
@@ -274,11 +271,9 @@
     return pl.pallas_call(
         key_kernel,
         out_shape=[jax.ShapeDtypeStruct((PLANE, KROWS, C), BF16)]
-        + [square] * 4
-        + [jax.ShapeDtypeStruct((15, C, C), F32)],
+        + [square] * 5,
         in_specs=[vmem()] * 5,
         out_specs=[vmem()] * 6,
-        scratch_shapes=[pltpu.VMEM((PLANE, C, C), F32)],
         compiler_params=params(),
         cost_estimate=cost(2e9, 4e6),
         name="keys",
@@ -650,6 +645,7 @@
 
     passed_right = turn(far_right, 1)
     passed_left = turn(far_left, 3)
+    passed_right, passed_left = lax.optimization_barrier((passed_right, passed_left))
     plain_right = turn(plain_right, 1)
     plain_left = turn(plain_left, 3)
     right = turn((right + passed_right.astype(F32)).astype(BF16), 1)

time: 78.5 us -> 77.3 us (0.985)
  starting transfers between devices: 41.6 us -> 40.7 us
  waiting for transfers between devices: 22.4 us -> 23.2 us
    ppermute x6, starting transfers between devices: 9.58 us -> 8.73 us  [turn(): return lax.ppermute(block, 'heads', [(s, (s + step) % 4) for s in range(4)])]
  transfers between devices with their start and end apart: 26 -> 26, of which waited for: 13 -> 12; matrix products, arithmetic and copies ran while one was open for 0% -> 0% of each run, Pallas kernels for 9% -> 9%
where the time goes in v12:
time: 77.3 us; the launch traced here: 77.1 us
  starting transfers between devices  40.7 us (53%)
  waiting for transfers between devices  23.2 us (30%)
  Pallas kernels  11.8 us (15%)
  other arithmetic  0.96 us (1%)
    ppermute x15, starting transfers between devices, swap(): lax.ppermute(block, 'seq', [(s, s ^ d) for s in range(PLANE * PLANES)])  20.5 us
    ppermute x5, waiting for transfers between devices, later_plane(): return lax.ppermute(block, 'seq', route)  12.1 us
    ppermute x5, starting transfers between devices, later_plane(): return lax.ppermute(block, 'seq', route)  11.5 us
    ppermute x6, starting transfers between devices, turn(): return lax.ppermute(block, 'heads', [(s, (s + step) % 4) for s in range(4)])  8.73 us
    ppermute x15, waiting for transfers between devices, swap(): lax.ppermute(block, 'seq', [(s, s ^ d) for s in range(PLANE * PLANES)])  6.05 us
    ppermute x6, waiting for transfers between devices, turn(): return lax.ppermute(block, 'heads', [(s, (s + step) % 4) for s in range(4)])  5 us
    pallas_call x1, Pallas kernels, key_part(): pl.pallas_call(key_kernel, out_shape=[jax.ShapeDtypeStruct((PLANE, KROWS,...  2.71 us
  transfers between devices with their start and end apart: 26, of which 12 were waited for; matrix products, arithmetic and copies ran while one was open for 0% of the time, Pallas kernels for 9%

profile of v12, /device:TPU:128, one launch (start us, length us, event | category | flops | bytes accessed | tf_op | source)
XLA Modules:
  0.0 77.1 jit_solution(7990501276959160510)
XLA Ops:
  0.0 1.4 %pack.1 = (bf16[4,144,128]{2,1,0:T(8,128)(2,1)S(1)}, bf16[4,144,128]{2,1,0:T(8,128)(2,1)S(1)}, bf16[4,256,128]{2,1,0:T(8,128)(2,1)S(1)}, bf16[4,256,128]{2,1,0:T(8,128)(2,1)S(1)}) custom-call(bf16[128,1024]{1,0:T(8,128)(2,1)} %q_ref.1, bf16[128,1024]{1,0:T(8,128)(2,1)} %k_ref.1, bf16[128,1024]{1,0:T(8,128)(2,1)} %v_ref.1, f32[8,128]{1,0:T(8,128)} %decay_ref.1, ...), custom_call_target="tpu_custom_call" | custom-call | tf_op jit(solution)/shard_map/pack/pallas_call | solution.py:113
  1.4 0.1 collective-permute-start.4
  1.5 0.5 collective-permute-start
  2.0 0.8 %collective-permute-done.4.refs_1_ = bf16[4,144,128]{2,1,0:T(8,128)(2,1)S(1)} collective-permute-done((bf16[4,144,128]{2,1,0:T(8,128)(2,1)S(1)}, bf16[4,144,128]{2,1,0:T(8,128)(2,1)S(1)}, u32[]{:S(2)}, u32[]{:S(2)}) %collective-permute-start.4) | collective-permute-done | bytes 147488 | tf_op jit(solution)/shard_map/ppermute | solution.py:600
  2.9 1.6 %collective-permute-start.5 = (bf16[2,144,128]{2,1,0:T(8,128)(2,1)S(1)}, bf16[2,144,128]{2,1,0:T(8,128)(2,1)S(1)}, u32[]{:S(2)}, u32[]{:S(2)}) collective-permute-start(bf16[2,144,128]{2,1,0:T(8,128)(2,1)S(1)} %pad_maximum_fusion), channel_id=1, source_target_pairs={{0,8},{4,12},{8,0},{12,4},{16,24},{20,28},{24,16},{28,20},{32,40},... | collective-permute-start | bytes 221192 | tf_op jit(solution)/shard_map/ppermute | solution.py:600
  4.4 2.8 %collective-permute-start.6 = (bf16[2,144,128]{2,1,0:T(8,128)(2,1)S(1)}, bf16[2,144,128]{2,1,0:T(8,128)(2,1)S(1)}, u32[]{:S(2)}, u32[]{:S(2)}) collective-permute-start(bf16[2,144,128]{2,1,0:T(8,128)(2,1)S(1)} %pad_maximum_fusion.1), channel_id=1, source_target_pairs={{0,16},{4,20},{8,24},{12,28},{16,0},{20,4},{24,8},{28,12},{32,48},... | collective-permute-start | bytes 221192 | tf_op jit(solution)/shard_map/ppermute | solution.py:600
  7.3 0.6 collective-permute-start.7
  7.8 0.0 collective-permute-done.refs_1_
  7.9 0.4 collective-permute-start.1
  8.2 4.0 %collective-permute-start.2 = (bf16[2,128,128]{2,1,0:T(8,128)(2,1)S(1)}, bf16[2,128,128]{2,1,0:T(8,128)(2,1)S(1)}, u32[]{:S(2)}, u32[]{:S(2)}) collective-permute-start(bf16[2,128,128]{2,1,0:T(8,128)(2,1)S(1)} %pad_maximum_fusion.4), channel_id=1, source_target_pairs={{0,16},{4,20},{8,24},{12,28},{16,0},{20,4},{24,8},{28,12},{32,48},... | collective-permute-start | bytes 196616 | tf_op jit(solution)/shard_map/ppermute | solution.py:600
  12.3 0.0 copy-start.1
  12.3 0.0 collective-permute-done.5.refs_2_
  12.3 0.6 collective-permute-start.3
  12.9 0.0 collective-permute-done.6.refs_3_
  12.9 0.8 collective-permute-done.7.refs_4_
  13.6 2.7 %keys.1 = (bf16[8,144,128]{2,1,0:T(8,128)(2,1)S(1)}, f32[8,128,128]{2,1,0:T(8,128)S(1)}, f32[8,128,128]{2,1,0:T(8,128)S(1)}, f32[8,128,128]{2,1,0:T(8,128)S(1)},...) custom-call(bf16[4,144,128]{2,1,0:T(8,128)(2,1)S(1)} %get-tuple-element.38.refs_0_, ...), custom_call_target="tpu_custom_call" | custom-call | flops 2000000000 | bytes 4000000 | tf_op jit(solution)/shard_map/keys/pallas_call | solution.py:271
  16.3 0.0 collective-permute-done.1.refs_2_
  16.4 0.0 collective-permute-done.2.refs_3_
  16.4 1.5 %collective-permute-done.3.refs_4_ = bf16[2,128,128]{2,1,0:T(8,128)(2,1)S(1)} collective-permute-done((bf16[2,128,128]{2,1,0:T(8,128)(2,1)S(1)}, bf16[2,128,128]{2,1,0:T(8,128)(2,1)S(1)}, u32[]{:S(2)}, u32[]{:S(2)}) %collective-permute-start.3) | collective-permute-done | bytes 65568 | tf_op jit(solution)/shard_map/ppermute | solution.py:600
  17.9 1.1 %values.1 = (f32[8,128,256]{2,1,0:T(8,128)S(1)}, bf16[128,256]{1,0:T(8,128)(2,1)S(1)}, f32[7,128,256]{2,1,0:T(8,128)S(1)}) custom-call(bf16[4,256,128]{2,1,0:T(8,128)(2,1)S(1)} %get-tuple-element.46.refs_0_, bf16[4,256,128]{2,1,0:T(8,128)(2,1)S(1)} %collective-permute-done.refs_1_, bf16[2,128,128]{2,1,0:T(8,128)(2,1)S(1)} %collective-permute-done.1.refs_2_, ...), custom_call_target="tpu_custom_call" | custom-call | flops 1000000000 | bytes 4000000 | tf_op jit(solution)/shard_map/values/pallas_call | solution.py:284
  19.0 0.0 slice-start
  19.0 3.6 %collective-permute-start.12 = (bf16[128,256]{1,0:T(8,128)(2,1)S(1)}, bf16[128,256]{1,0:T(8,128)(2,1)S(1)}, u32[]{:S(2)}, u32[]{:S(2)}) collective-permute-start(bf16[128,256]{1,0:T(8,128)(2,1)S(1)} %get-tuple-element.45.own_ref), channel_id=1, source_target_pairs={{0,64},{4,68},{8,72},{12,76},{16,80},{20,84},{24,88},{28,92},{32,9... | collective-permute-start | bytes 196616 | tf_op jit(solution)/shard_map/ppermute | solution.py:617
  22.7 2.9 %collective-permute-start.11 = (bf16[128,256]{1,0:T(8,128)(2,1)S(1)}, bf16[128,256]{1,0:T(8,128)(2,1)S(1)}, u32[]{:S(2)}, u32[]{:S(2)}) collective-permute-start(bf16[128,256]{1,0:T(8,128)(2,1)S(1)} %get-tuple-element.45.own_ref), channel_id=1, source_target_pairs={{0,32},{4,36},{8,40},{12,44},{16,48},{20,52},{24,56},{28,60},{32,6... | collective-permute-start | bytes 196616 | tf_op jit(solution)/shard_map/ppermute | solution.py:617
  25.6 0.1 collective-permute-start.8
  25.8 2.0 %collective-permute-start.9 = (bf16[2,128,128]{2,1,0:T(8,128)(2,1)S(1)}, bf16[2,128,128]{2,1,0:T(8,128)(2,1)S(1)}, u32[]{:S(2)}, u32[]{:S(2)}) collective-permute-start(bf16[2,128,128]{2,1,0:T(8,128)(2,1)S(1)} %pad_maximum_fusion.7), channel_id=1, source_target_pairs={{0,16},{4,20},{8,24},{12,28},{16,0},{20,4},{24,8},{28,12},{32,48},... | collective-permute-start | bytes 196616 | tf_op jit(solution)/shard_map/ppermute | solution.py:600
  27.8 2.8 %collective-permute-start.10 = (bf16[2,128,128]{2,1,0:T(8,128)(2,1)S(1)}, bf16[2,128,128]{2,1,0:T(8,128)(2,1)S(1)}, u32[]{:S(2)}, u32[]{:S(2)}) collective-permute-start(bf16[2,128,128]{2,1,0:T(8,128)(2,1)S(1)} %pad_maximum_fusion.8), channel_id=1, source_target_pairs={{0,24},{4,28},{8,16},{12,20},{16,8},{20,12},{24,0},{28,4},{32,56},... | collective-permute-start | bytes 196616 | tf_op jit(solution)/shard_map/ppermute | solution.py:600
  30.6 0.0 collective-permute-done.12.two_ref
  30.6 0.0 collective-permute-done.11.one_ref
  30.6 0.3 combine.1
  30.9 1.9 %collective-permute-start.14 = (bf16[128,256]{1,0:T(8,128)(2,1)S(1)}, bf16[128,256]{1,0:T(8,128)(2,1)S(1)}, u32[]{:S(2)}, u32[]{:S(2)}) collective-permute-start(bf16[128,256]{1,0:T(8,128)(2,1)S(1)} %get-tuple-element.52), channel_id=1, source_target_pairs={{0,96},{4,100},{8,104},{12,108},{16,112},{20,116},{24,120},{28,124... | collective-permute-start | bytes 196616 | tf_op jit(solution)/shard_map/ppermute | solution.py:617
  32.9 0.7 collective-permute-start.13
  33.5 0.0 collective-permute-done.8.refs_2_
  33.6 0.0 collective-permute-done.10.refs_4_
  33.6 1.3 %query.1.no_ref = f32[1024,256]{1,0:T(8,128)S(1)} custom-call(bf16[4,256,128]{2,1,0:T(8,128)(2,1)S(1)} %get-tuple-element.46.refs_0_, bf16[4,256,128]{2,1,0:T(8,128)(2,1)S(1)} %collective-permute-done.refs_1_, bf16[2,128,128]{2,1,0:T(8,128)(2,1)S(1)} %collective-permute-done.8.refs_2_, bf16[2,128,128]{2,1,0:T(8,128)(2,1)S(1)} %collective-permute-done.9.refs_3_, ...), custom_call_target="tpu_custom_call" | custom-call | flops 1000000000 | bytes 4000000 | tf_op jit(solution)/shard_map/query/pallas_call | solution.py:339
  34.9 6.0 %collective-permute-done.14.three_ref = bf16[128,256]{1,0:T(8,128)(2,1)S(1)} collective-permute-done((bf16[128,256]{1,0:T(8,128)(2,1)S(1)}, bf16[128,256]{1,0:T(8,128)(2,1)S(1)}, u32[]{:S(2)}, u32[]{:S(2)}) %collective-permute-start.14) | collective-permute-done | bytes 65568 | tf_op jit(solution)/shard_map/ppermute | solution.py:617
  40.9 0.0 collective-permute-done.13.six_ref
  40.9 0.7 norm.1.normed_ref
  41.7 0.0 slice-start.1
  41.7 2.4 %collective-permute-start.15 = (bf16[1024,128]{1,0:T(8,128)(2,1)S(1)}, bf16[1024,128]{1,0:T(8,128)(2,1)S(1)}, u32[]{:S(2)}, u32[]{:S(2)}) collective-permute-start(bf16[1024,128]{1,0:T(8,128)(2,1)S(1)} %norm.1.normed_ref), channel_id=1, source_target_pairs={{0,32},{4,36},{8,40},{12,44},{16,48},{20,52},{24,56},{28,60},{32,6... | collective-permute-start | bytes 786440 | tf_op jit(solution)/shard_map/ppermute | solution.py:617
  44.1 1.3 %own.1 = (f32[1024,128]{1,0:T(8,128)S(1)}, f32[2,1024,128]{2,1,0:T(8,128)S(1)}, bf16[1024,128]{1,0:T(8,128)(2,1)S(1)}) custom-call(bf16[1024,128]{1,0:T(8,128)(2,1)S(1)} %norm.1.normed_ref, bf16[8,128,384]{2,1,0:T(8,128)(2,1)S(1)} %copy-done.1), custom_call_target="tpu_custom_call" | custom-call | flops 1000000000 | bytes 3000000 | tf_op jit(solution)/shard_map/own/pallas_call | solution.py:461
  45.3 6.1 %collective-permute-done.15.halo_ref = bf16[1024,128]{1,0:T(8,128)(2,1)S(1)} collective-permute-done((bf16[1024,128]{1,0:T(8,128)(2,1)S(1)}, bf16[1024,128]{1,0:T(8,128)(2,1)S(1)}, u32[]{:S(2)}, u32[]{:S(2)}) %collective-permute-start.15) | collective-permute-done | bytes 262176 | tf_op jit(solution)/shard_map/ppermute | solution.py:617
  51.4 1.5 %halo.1 = (bf16[4,128,128]{2,1,0:T(8,128)(2,1)S(1)}, bf16[4,128,128]{2,1,0:T(8,128)(2,1)S(1)}) custom-call(bf16[1024,128]{1,0:T(8,128)(2,1)S(1)} %collective-permute-done.15.halo_ref, bf16[8,128,384]{2,1,0:T(8,128)(2,1)S(1)} %copy-done.1, f32[1024,128]{1,0:T(8,128)S(1)} %get-tuple-element.53.acc_ref, f32[2,1024,128]{2,1,0:T(8,128)S(1)} %get-tuple-element.54.stat_ref, ...), custom_call_target="tpu_custom_call" | custom-call | flops 1000000000 | bytes 3000000 | tf_op jit(solution)/shard_map/halo/pallas_call | solution.py:513
  52.9 0.1 collective-permute-start.16
  53.0 1.3 %collective-permute-done.16.came = bf16[4,128,128]{2,1,0:T(8,128)(2,1)S(1)} collective-permute-done((bf16[4,128,128]{2,1,0:T(8,128)(2,1)S(1)}, bf16[4,128,128]{2,1,0:T(8,128)(2,1)S(1)}, u32[]{:S(2)}, u32[]{:S(2)}) %collective-permute-start.16) | collective-permute-done | bytes 131104 | tf_op jit(solution)/shard_map/ppermute | solution.py:600
  54.4 0.1 collective-permute-start.18
  54.5 1.9 %collective-permute-start.19 = (bf16[2,128,128]{2,1,0:T(8,128)(2,1)S(1)}, bf16[2,128,128]{2,1,0:T(8,128)(2,1)S(1)}, u32[]{:S(2)}, u32[]{:S(2)}) collective-permute-start(bf16[2,128,128]{2,1,0:T(8,128)(2,1)S(1)} %pad_maximum_fusion.11), channel_id=1, source_target_pairs={{0,16},{4,20},{8,24},{12,28},{16,0},{20,4},{24,8},{28,12},{32,48},... | collective-permute-start | bytes 196616 | tf_op jit(solution)/shard_map/ppermute | solution.py:600
  56.4 2.9 %collective-permute-start.17 = (bf16[2,128,128]{2,1,0:T(8,128)(2,1)S(1)}, bf16[2,128,128]{2,1,0:T(8,128)(2,1)S(1)}, u32[]{:S(2)}, u32[]{:S(2)}) collective-permute-start(bf16[2,128,128]{2,1,0:T(8,128)(2,1)S(1)} %pad_maximum_fusion.9), channel_id=1, source_target_pairs={{0,24},{4,28},{8,16},{12,20},{16,8},{20,12},{24,0},{28,4},{32,56},... | collective-permute-start | bytes 196616 | tf_op jit(solution)/shard_map/ppermute | solution.py:600
  59.4 0.0 collective-permute-done.18.one
  59.4 1.1 %collective-permute-done.19.two = bf16[2,128,128]{2,1,0:T(8,128)(2,1)S(1)} collective-permute-done((bf16[2,128,128]{2,1,0:T(8,128)(2,1)S(1)}, bf16[2,128,128]{2,1,0:T(8,128)(2,1)S(1)}, u32[]{:S(2)}, u32[]{:S(2)}) %collective-permute-start.19) | collective-permute-done | bytes 65568 | tf_op jit(solution)/shard_map/ppermute | solution.py:600
  60.4 1.0 %early.1.acc_ref = f32[128,4096]{1,0:T(8,128)S(1)} custom-call(bf16[4,128,128]{2,1,0:T(8,128)(2,1)S(1)} %get-tuple-element.56.keep, bf16[4,128,128]{2,1,0:T(8,128)(2,1)S(1)} %collective-permute-done.16.came, bf16[2,128,128]{2,1,0:T(8,128)(2,1)S(1)} %collective-permute-done.18.one, bf16[2,128,128]{2,1,0:T(8,128)(2,1)S(1)} %collective-permute-done.19.two, ...), custom_call_target="tpu_custom_call" | custom-call | flops 800000000 | bytes 8000000 | tf_op jit(solution)/shard_map/early/pallas_call | solution.py:577
  61.4 0.6 collective-permute-done.17.three
  62.0 0.4 late.1
  62.4 1.6 %collective-permute-start.20 = (bf16[32,2048]{1,0:T(8,128)(2,1)S(1)}, bf16[32,2048]{1,0:T(8,128)(2,1)S(1)}, u32[]{:S(2)}, u32[]{:S(2)}) collective-permute-start(bf16[32,2048]{1,0:T(8,128)(2,1)S(1)} %get-tuple-element.60), channel_id=1, source_target_pairs={{0,1},{1,2},{2,3},{3,0},{4,5},{5,6},{6,7},{7,4},{8,9},{9,10},{10,1... | collective-permute-start | bytes 393224 | tf_op jit(solution)/shard_map/ppermute | solution.py:644
  64.1 1.7 %collective-permute-start.21 = (bf16[32,2048]{1,0:T(8,128)(2,1)S(1)}, bf16[32,2048]{1,0:T(8,128)(2,1)S(1)}, u32[]{:S(2)}, u32[]{:S(2)}) collective-permute-start(bf16[32,2048]{1,0:T(8,128)(2,1)S(1)} %get-tuple-element.61), channel_id=1, source_target_pairs={{0,3},{1,0},{2,1},{3,2},{4,7},{5,4},{6,5},{7,6},{8,11},{9,8},{10,9... | collective-permute-start | bytes 393224 | tf_op jit(solution)/shard_map/ppermute | solution.py:644
  65.8 1.8 %collective-permute-start.23 = (bf16[32,2048]{1,0:T(8,128)(2,1)S(1)}, bf16[32,2048]{1,0:T(8,128)(2,1)S(1)}, u32[]{:S(2)}, u32[]{:S(2)}) collective-permute-start(bf16[32,2048]{1,0:T(8,128)(2,1)S(1)} %get-tuple-element.63), channel_id=1, source_target_pairs={{0,3},{1,0},{2,1},{3,2},{4,7},{5,4},{6,5},{7,6},{8,11},{9,8},{10,9... | collective-permute-start | bytes 393224 | tf_op jit(solution)/shard_map/ppermute | solution.py:644
  67.6 0.2 collective-permute-start.25
  67.8 0.9 %collective-permute-done.20 = bf16[32,2048]{1,0:T(8,128)(2,1)S(1)} collective-permute-done((bf16[32,2048]{1,0:T(8,128)(2,1)S(1)}, bf16[32,2048]{1,0:T(8,128)(2,1)S(1)}, u32[]{:S(2)}, u32[]{:S(2)}) %collective-permute-start.20) | collective-permute-done | bytes 131104 | tf_op jit(solution)/shard_map/ppermute | solution.py:644
  68.7 0.9 %collective-permute-done.21 = bf16[32,2048]{1,0:T(8,128)(2,1)S(1)} collective-permute-done((bf16[32,2048]{1,0:T(8,128)(2,1)S(1)}, bf16[32,2048]{1,0:T(8,128)(2,1)S(1)}, u32[]{:S(2)}, u32[]{:S(2)}) %collective-permute-start.21) | collective-permute-done | bytes 131104 | tf_op jit(solution)/shard_map/ppermute | solution.py:644
  69.7 1.5 %collective-permute-start.22 = (bf16[32,2048]{1,0:T(8,128)(2,1)S(1)}, bf16[32,2048]{1,0:T(8,128)(2,1)S(1)}, u32[]{:S(2)}, u32[]{:S(2)}) collective-permute-start(bf16[32,2048]{1,0:T(8,128)(2,1)S(1)} %add_convert_fusion.1), channel_id=1, source_target_pairs={{0,1},{1,2},{2,3},{3,0},{4,5},{5,6},{6,7},{7,4},{8,9},{9,10},{10,1... | collective-permute-start | bytes 393224 | tf_op jit(solution)/shard_map/ppermute | solution.py:644
  71.2 1.9 %collective-permute-start.24 = (bf16[32,2048]{1,0:T(8,128)(2,1)S(1)}, bf16[32,2048]{1,0:T(8,128)(2,1)S(1)}, u32[]{:S(2)}, u32[]{:S(2)}) collective-permute-start(bf16[32,2048]{1,0:T(8,128)(2,1)S(1)} %add_convert_fusion), channel_id=1, source_target_pairs={{0,3},{1,0},{2,1},{3,2},{4,7},{5,4},{6,5},{7,6},{8,11},{9,8},{10,9... | collective-permute-start | bytes 393224 | tf_op jit(solution)/shard_map/ppermute | solution.py:644
  73.1 0.0 collective-permute-done.23
  73.1 2.8 %collective-permute-done.22 = bf16[32,2048]{1,0:T(8,128)(2,1)S(1)} collective-permute-done((bf16[32,2048]{1,0:T(8,128)(2,1)S(1)}, bf16[32,2048]{1,0:T(8,128)(2,1)S(1)}, u32[]{:S(2)}, u32[]{:S(2)}) %collective-permute-start.22) | collective-permute-done | bytes 131104 | tf_op jit(solution)/shard_map/ppermute | solution.py:644
  76.0 0.3 collective-permute-done.24
  76.3 0.8 fusion
  (31 shorter events, 0.3 us)
Async XLA Ops:
  1.4 1.5 %collective-permute-start.4 = (bf16[4,144,128]{2,1,0:T(8,128)(2,1)S(1)}, bf16[4,144,128]{2,1,0:T(8,128)(2,1)S(1)}, u32[]{:S(2)}, u32[]{:S(2)}) collective-permute-start(bf16[4,144,128]{2,1,0:T(8,128)(2,1)S(1)} %get-tuple-element.39), channel_id=1, source_target_pairs={{0,4},{4,0},{8,12},{12,8},{16,20},{20,16},{24,28},{28,24},{32,36},... | collective-permute-start | bytes 442376 | tf_op jit(solution)/shard_map/ppermute | solution.py:600
  1.5 6.4 %collective-permute-start = (bf16[4,256,128]{2,1,0:T(8,128)(2,1)S(1)}, bf16[4,256,128]{2,1,0:T(8,128)(2,1)S(1)}, u32[]{:S(2)}, u32[]{:S(2)}) collective-permute-start(bf16[4,256,128]{2,1,0:T(8,128)(2,1)S(1)} %get-tuple-element.37), channel_id=1, source_target_pairs={{0,4},{4,0},{8,12},{12,8},{16,20},{20,16},{24,28},{28,24},{32,36},... | collective-permute-start | bytes 786440 | tf_op jit(solution)/shard_map/ppermute | solution.py:600
  2.9 9.4 %collective-permute-start.5 = (bf16[2,144,128]{2,1,0:T(8,128)(2,1)S(1)}, bf16[2,144,128]{2,1,0:T(8,128)(2,1)S(1)}, u32[]{:S(2)}, u32[]{:S(2)}) collective-permute-start(bf16[2,144,128]{2,1,0:T(8,128)(2,1)S(1)} %pad_maximum_fusion), channel_id=1, source_target_pairs={{0,8},{4,12},{8,0},{12,4},{16,24},{20,28},{24,16},{28,20},{32,40},... | collective-permute-start | bytes 221192 | tf_op jit(solution)/shard_map/ppermute | solution.py:600
  4.4 8.4 %collective-permute-start.6 = (bf16[2,144,128]{2,1,0:T(8,128)(2,1)S(1)}, bf16[2,144,128]{2,1,0:T(8,128)(2,1)S(1)}, u32[]{:S(2)}, u32[]{:S(2)}) collective-permute-start(bf16[2,144,128]{2,1,0:T(8,128)(2,1)S(1)} %pad_maximum_fusion.1), channel_id=1, source_target_pairs={{0,16},{4,20},{8,24},{12,28},{16,0},{20,4},{24,8},{28,12},{32,48},... | collective-permute-start | bytes 221192 | tf_op jit(solution)/shard_map/ppermute | solution.py:600
  7.3 6.4 %collective-permute-start.7 = (bf16[2,144,128]{2,1,0:T(8,128)(2,1)S(1)}, bf16[2,144,128]{2,1,0:T(8,128)(2,1)S(1)}, u32[]{:S(2)}, u32[]{:S(2)}) collective-permute-start(bf16[2,144,128]{2,1,0:T(8,128)(2,1)S(1)} %pad_maximum_fusion.2), channel_id=1, source_target_pairs={{0,24},{4,28},{8,16},{12,20},{16,8},{20,12},{24,0},{28,4},{32,56},... | collective-permute-start | bytes 221192 | tf_op jit(solution)/shard_map/ppermute | solution.py:600
  7.9 8.5 %collective-permute-start.1 = (bf16[2,128,128]{2,1,0:T(8,128)(2,1)S(1)}, bf16[2,128,128]{2,1,0:T(8,128)(2,1)S(1)}, u32[]{:S(2)}, u32[]{:S(2)}) collective-permute-start(bf16[2,128,128]{2,1,0:T(8,128)(2,1)S(1)} %pad_maximum_fusion.3), channel_id=1, source_target_pairs={{0,8},{4,12},{8,0},{12,4},{16,24},{20,28},{24,16},{28,20},{32,40},... | collective-permute-start | bytes 196616 | tf_op jit(solution)/shard_map/ppermute | solution.py:600
  8.2 8.1 %collective-permute-start.2 = (bf16[2,128,128]{2,1,0:T(8,128)(2,1)S(1)}, bf16[2,128,128]{2,1,0:T(8,128)(2,1)S(1)}, u32[]{:S(2)}, u32[]{:S(2)}) collective-permute-start(bf16[2,128,128]{2,1,0:T(8,128)(2,1)S(1)} %pad_maximum_fusion.4), channel_id=1, source_target_pairs={{0,16},{4,20},{8,24},{12,28},{16,0},{20,4},{24,8},{28,12},{32,48},... | collective-permute-start | bytes 196616 | tf_op jit(solution)/shard_map/ppermute | solution.py:600
  12.3 28.7 %copy-start = (f32[128]{0:T(128)S(1)}, f32[128]{0:T(128)}, u32[]{:S(2)}) copy-start(f32[128]{0:T(128)} %param.13) | copy-start | bytes 1540
  12.3 31.8 %copy-start.1 = (bf16[8,128,384]{2,1,0:T(8,128)(2,1)S(1)}, bf16[8,128,384]{2,1,0:T(8,128)(2,1)}, u32[]{:S(2)}) copy-start(bf16[8,128,384]{2,1,0:T(8,128)(2,1)} %weight_ref.5) | copy-start | bytes 2359300
  12.3 5.6 %collective-permute-start.3 = (bf16[2,128,128]{2,1,0:T(8,128)(2,1)S(1)}, bf16[2,128,128]{2,1,0:T(8,128)(2,1)S(1)}, u32[]{:S(2)}, u32[]{:S(2)}) collective-permute-start(bf16[2,128,128]{2,1,0:T(8,128)(2,1)S(1)} %pad_maximum_fusion.5), channel_id=1, source_target_pairs={{0,24},{4,28},{8,16},{12,20},{16,8},{20,12},{24,0},{28,4},{32,56},... | collective-permute-start | bytes 196616 | tf_op jit(solution)/shard_map/ppermute | solution.py:600
  19.0 41.4 %slice-start = ((s8[8388608]{0:T(1024)(128)(4,1)}), s8[4194304]{0:T(1024)(128)(4,1)S(1)}, s32[]{:S(2)}) async-start(s8[8388608]{0:T(1024)(128)(4,1)} %bitcast.1), calls=%async_computation | async-start | bytes 8388608
  19.0 11.6 %collective-permute-start.12 = (bf16[128,256]{1,0:T(8,128)(2,1)S(1)}, bf16[128,256]{1,0:T(8,128)(2,1)S(1)}, u32[]{:S(2)}, u32[]{:S(2)}) collective-permute-start(bf16[128,256]{1,0:T(8,128)(2,1)S(1)} %get-tuple-element.45.own_ref), channel_id=1, source_target_pairs={{0,64},{4,68},{8,72},{12,76},{16,80},{20,84},{24,88},{28,92},{32,9... | collective-permute-start | bytes 196616 | tf_op jit(solution)/shard_map/ppermute | solution.py:617
  22.7 7.9 %collective-permute-start.11 = (bf16[128,256]{1,0:T(8,128)(2,1)S(1)}, bf16[128,256]{1,0:T(8,128)(2,1)S(1)}, u32[]{:S(2)}, u32[]{:S(2)}) collective-permute-start(bf16[128,256]{1,0:T(8,128)(2,1)S(1)} %get-tuple-element.45.own_ref), channel_id=1, source_target_pairs={{0,32},{4,36},{8,40},{12,44},{16,48},{20,52},{24,56},{28,60},{32,6... | collective-permute-start | bytes 196616 | tf_op jit(solution)/shard_map/ppermute | solution.py:617
  25.6 7.9 %collective-permute-start.8 = (bf16[2,128,128]{2,1,0:T(8,128)(2,1)S(1)}, bf16[2,128,128]{2,1,0:T(8,128)(2,1)S(1)}, u32[]{:S(2)}, u32[]{:S(2)}) collective-permute-start(bf16[2,128,128]{2,1,0:T(8,128)(2,1)S(1)} %pad_maximum_fusion.6), channel_id=1, source_target_pairs={{0,8},{4,12},{8,0},{12,4},{16,24},{20,28},{24,16},{28,20},{32,40},... | collective-permute-start | bytes 196616 | tf_op jit(solution)/shard_map/ppermute | solution.py:600
  25.8 7.8 %collective-permute-start.9 = (bf16[2,128,128]{2,1,0:T(8,128)(2,1)S(1)}, bf16[2,128,128]{2,1,0:T(8,128)(2,1)S(1)}, u32[]{:S(2)}, u32[]{:S(2)}) collective-permute-start(bf16[2,128,128]{2,1,0:T(8,128)(2,1)S(1)} %pad_maximum_fusion.7), channel_id=1, source_target_pairs={{0,16},{4,20},{8,24},{12,28},{16,0},{20,4},{24,8},{28,12},{32,48},... | collective-permute-start | bytes 196616 | tf_op jit(solution)/shard_map/ppermute | solution.py:600
  27.8 5.7 %collective-permute-start.10 = (bf16[2,128,128]{2,1,0:T(8,128)(2,1)S(1)}, bf16[2,128,128]{2,1,0:T(8,128)(2,1)S(1)}, u32[]{:S(2)}, u32[]{:S(2)}) collective-permute-start(bf16[2,128,128]{2,1,0:T(8,128)(2,1)S(1)} %pad_maximum_fusion.8), channel_id=1, source_target_pairs={{0,24},{4,28},{8,16},{12,20},{16,8},{20,12},{24,0},{28,4},{32,56},... | collective-permute-start | bytes 196616 | tf_op jit(solution)/shard_map/ppermute | solution.py:600
  30.9 10.0 %collective-permute-start.14 = (bf16[128,256]{1,0:T(8,128)(2,1)S(1)}, bf16[128,256]{1,0:T(8,128)(2,1)S(1)}, u32[]{:S(2)}, u32[]{:S(2)}) collective-permute-start(bf16[128,256]{1,0:T(8,128)(2,1)S(1)} %get-tuple-element.52), channel_id=1, source_target_pairs={{0,96},{4,100},{8,104},{12,108},{16,112},{20,116},{24,120},{28,124... | collective-permute-start | bytes 196616 | tf_op jit(solution)/shard_map/ppermute | solution.py:617
  32.9 8.1 %collective-permute-start.13 = (bf16[128,256]{1,0:T(8,128)(2,1)S(1)}, bf16[128,256]{1,0:T(8,128)(2,1)S(1)}, u32[]{:S(2)}, u32[]{:S(2)}) collective-permute-start(bf16[128,256]{1,0:T(8,128)(2,1)S(1)} %get-tuple-element.52), channel_id=1, source_target_pairs={{0,192},{4,196},{8,200},{12,204},{16,208},{20,212},{24,216},{28,22... | collective-permute-start | bytes 196616 | tf_op jit(solution)/shard_map/ppermute | solution.py:617
  41.7 18.7 %slice-start.1 = ((s8[8388608]{0:T(1024)(128)(4,1)}), s8[4194304]{0:T(1024)(128)(4,1)S(1)}, s32[]{:S(2)}) async-start(s8[8388608]{0:T(1024)(128)(4,1)} %bitcast.1), calls=%async_computation.1 | async-start | bytes 8388608
  41.7 9.7 %collective-permute-start.15 = (bf16[1024,128]{1,0:T(8,128)(2,1)S(1)}, bf16[1024,128]{1,0:T(8,128)(2,1)S(1)}, u32[]{:S(2)}, u32[]{:S(2)}) collective-permute-start(bf16[1024,128]{1,0:T(8,128)(2,1)S(1)} %norm.1.normed_ref), channel_id=1, source_target_pairs={{0,32},{4,36},{8,40},{12,44},{16,48},{20,52},{24,56},{28,60},{32,6... | collective-permute-start | bytes 786440 | tf_op jit(solution)/shard_map/ppermute | solution.py:617
  52.9 1.4 %collective-permute-start.16 = (bf16[4,128,128]{2,1,0:T(8,128)(2,1)S(1)}, bf16[4,128,128]{2,1,0:T(8,128)(2,1)S(1)}, u32[]{:S(2)}, u32[]{:S(2)}) collective-permute-start(bf16[4,128,128]{2,1,0:T(8,128)(2,1)S(1)} %get-tuple-element.57), channel_id=1, source_target_pairs={{0,4},{4,0},{8,12},{12,8},{16,20},{20,16},{24,28},{28,24},{32,36},... | collective-permute-start | bytes 393224 | tf_op jit(solution)/shard_map/ppermute | solution.py:600
  54.4 5.0 %collective-permute-start.18 = (bf16[2,128,128]{2,1,0:T(8,128)(2,1)S(1)}, bf16[2,128,128]{2,1,0:T(8,128)(2,1)S(1)}, u32[]{:S(2)}, u32[]{:S(2)}) collective-permute-start(bf16[2,128,128]{2,1,0:T(8,128)(2,1)S(1)} %pad_maximum_fusion.10), channel_id=1, source_target_pairs={{0,8},{4,12},{8,0},{12,4},{16,24},{20,28},{24,16},{28,20},{32,40},... | collective-permute-start | bytes 196616 | tf_op jit(solution)/shard_map/ppermute | solution.py:600
  54.5 5.9 %collective-permute-start.19 = (bf16[2,128,128]{2,1,0:T(8,128)(2,1)S(1)}, bf16[2,128,128]{2,1,0:T(8,128)(2,1)S(1)}, u32[]{:S(2)}, u32[]{:S(2)}) collective-permute-start(bf16[2,128,128]{2,1,0:T(8,128)(2,1)S(1)} %pad_maximum_fusion.11), channel_id=1, source_target_pairs={{0,16},{4,20},{8,24},{12,28},{16,0},{20,4},{24,8},{28,12},{32,48},... | collective-permute-start | bytes 196616 | tf_op jit(solution)/shard_map/ppermute | solution.py:600
  56.4 5.6 %collective-permute-start.17 = (bf16[2,128,128]{2,1,0:T(8,128)(2,1)S(1)}, bf16[2,128,128]{2,1,0:T(8,128)(2,1)S(1)}, u32[]{:S(2)}, u32[]{:S(2)}) collective-permute-start(bf16[2,128,128]{2,1,0:T(8,128)(2,1)S(1)} %pad_maximum_fusion.9), channel_id=1, source_target_pairs={{0,24},{4,28},{8,16},{12,20},{16,8},{20,12},{24,0},{28,4},{32,56},... | collective-permute-start | bytes 196616 | tf_op jit(solution)/shard_map/ppermute | solution.py:600
  62.4 6.3 %collective-permute-start.20 = (bf16[32,2048]{1,0:T(8,128)(2,1)S(1)}, bf16[32,2048]{1,0:T(8,128)(2,1)S(1)}, u32[]{:S(2)}, u32[]{:S(2)}) collective-permute-start(bf16[32,2048]{1,0:T(8,128)(2,1)S(1)} %get-tuple-element.60), channel_id=1, source_target_pairs={{0,1},{1,2},{2,3},{3,0},{4,5},{5,6},{6,7},{7,4},{8,9},{9,10},{10,1... | collective-permute-start | bytes 393224 | tf_op jit(solution)/shard_map/ppermute | solution.py:644
  64.1 5.6 %collective-permute-start.21 = (bf16[32,2048]{1,0:T(8,128)(2,1)S(1)}, bf16[32,2048]{1,0:T(8,128)(2,1)S(1)}, u32[]{:S(2)}, u32[]{:S(2)}) collective-permute-start(bf16[32,2048]{1,0:T(8,128)(2,1)S(1)} %get-tuple-element.61), channel_id=1, source_target_pairs={{0,3},{1,0},{2,1},{3,2},{4,7},{5,4},{6,5},{7,6},{8,11},{9,8},{10,9... | collective-permute-start | bytes 393224 | tf_op jit(solution)/shard_map/ppermute | solution.py:644
  65.8 7.3 %collective-permute-start.23 = (bf16[32,2048]{1,0:T(8,128)(2,1)S(1)}, bf16[32,2048]{1,0:T(8,128)(2,1)S(1)}, u32[]{:S(2)}, u32[]{:S(2)}) collective-permute-start(bf16[32,2048]{1,0:T(8,128)(2,1)S(1)} %get-tuple-element.63), channel_id=1, source_target_pairs={{0,3},{1,0},{2,1},{3,2},{4,7},{5,4},{6,5},{7,6},{8,11},{9,8},{10,9... | collective-permute-start | bytes 393224 | tf_op jit(solution)/shard_map/ppermute | solution.py:644
  67.6 8.4 %collective-permute-start.25 = (bf16[32,2048]{1,0:T(8,128)(2,1)S(1)}, bf16[32,2048]{1,0:T(8,128)(2,1)S(1)}, u32[]{:S(2)}, u32[]{:S(2)}) collective-permute-start(bf16[32,2048]{1,0:T(8,128)(2,1)S(1)} %get-tuple-element.66), channel_id=1, source_target_pairs={{0,1},{1,2},{2,3},{3,0},{4,5},{5,6},{6,7},{7,4},{8,9},{9,10},{10,1... | collective-permute-start | bytes 393224 | tf_op jit(solution)/shard_map/ppermute | solution.py:644
  69.7 6.3 %collective-permute-start.22 = (bf16[32,2048]{1,0:T(8,128)(2,1)S(1)}, bf16[32,2048]{1,0:T(8,128)(2,1)S(1)}, u32[]{:S(2)}, u32[]{:S(2)}) collective-permute-start(bf16[32,2048]{1,0:T(8,128)(2,1)S(1)} %add_convert_fusion.1), channel_id=1, source_target_pairs={{0,1},{1,2},{2,3},{3,0},{4,5},{5,6},{6,7},{7,4},{8,9},{9,10},{10,1... | collective-permute-start | bytes 393224 | tf_op jit(solution)/shard_map/ppermute | solution.py:644
  71.2 5.0 %collective-permute-start.24 = (bf16[32,2048]{1,0:T(8,128)(2,1)S(1)}, bf16[32,2048]{1,0:T(8,128)(2,1)S(1)}, u32[]{:S(2)}, u32[]{:S(2)}) collective-permute-start(bf16[32,2048]{1,0:T(8,128)(2,1)S(1)} %add_convert_fusion), channel_id=1, source_target_pairs={{0,3},{1,0},{2,1},{3,2},{4,7},{5,4},{6,5},{7,6},{8,11},{9,8},{10,9... | collective-permute-start | bytes 393224 | tf_op jit(solution)/shard_map/ppermute | solution.py:644

commit v13 on v12

--- a/solution.py
+++ b/solution.py
@@ -538,12 +538,8 @@
     return jnp.concatenate([left, right], axis=1), pl.ds(at, 2 * C)
 
 
-def early_kernel(keep, came, one, two, weight_ref, acc_ref):
-    parts = [
-        pair_part(keep.at[0], came.at[0], 0),
-        pair_part(two.at[0], two.at[1], 2),
-        pair_part(one.at[0], one.at[1], 1),
-    ]
+def early_kernel(keep, came, one, weight_ref, acc_ref):
+    parts = [pair_part(keep.at[0], came.at[0], 0), pair_part(one.at[0], one.at[1], 1)]
     for at in range(0, weight_ref.shape[1], COLS):
         cols = slice(at, at + COLS)
         got = dot(parts[0][0], weight_ref[parts[0][1], cols])
@@ -552,13 +548,15 @@
         acc_ref[:, cols] = got
 
 
-def late_kernel(three, weight_ref, acc_ref, own_ref, right_ref, left_ref, *outs):
-    part, rows = pair_part(three.at[0], three.at[1], 3)
+def late_kernel(two, three, weight_ref, acc_ref, own_ref, right_ref, left_ref, *outs):
+    parts = [pair_part(two.at[0], two.at[1], 2), pair_part(three.at[0], three.at[1], 3)]
     far_right, far_left, plain_right, plain_left = outs
     half = weight_ref.shape[1] // 2
     for at in range(0, 2 * half, COLS):
         cols = slice(at, at + COLS)
-        got = acc_ref[:, cols] + dot(part, weight_ref[rows, cols])
+        got = acc_ref[:, cols]
+        for part, rows in parts:
+            got = got + dot(part, weight_ref[rows, cols])
         own_ref[:, cols] = got[0:32]
         if at < half:
             right_ref[:, cols] = got[32:64]
@@ -577,33 +575,35 @@
     acc = pl.pallas_call(
         early_kernel,
         out_shape=jax.ShapeDtypeStruct((C, width), F32),
-        in_specs=[vmem()] * 5,
+        in_specs=[vmem()] * 4,
         out_specs=vmem(),
         compiler_params=params(),
-        cost_estimate=cost(8e8, 8e6),
+        cost_estimate=cost(5e8, 4e6),
         name="early",
-    )(keep, came, one, two, weight)
+    )(keep, came, one, weight)
     return pl.pallas_call(
         late_kernel,
         out_shape=[jax.ShapeDtypeStruct((32, width), F32)]
         + [jax.ShapeDtypeStruct((32, width // 2), F32)] * 2
         + [jax.ShapeDtypeStruct((32, width // 2), BF16)] * 4,
-        in_specs=[vmem()] * 3,
+        in_specs=[vmem()] * 4,
         out_specs=[vmem()] * 7,
         compiler_params=params(),
         cost_estimate=cost(3e8, 4e6),
         name="late",
-    )(three, weight, acc)
+    )(two, three, weight, acc)
 
 
 def swap(block, d):
     return lax.ppermute(block, "seq", [(s, s ^ d) for s in range(PLANE * PLANES)])
 
 
+def along_x_one(keep, came, dx, part):
+    return swap(jnp.stack([keep[dx, part], came[dx, part]]), 2 * dx)
+
+
 def along_x(keep, came, part=slice(None)):
-    pairs = {}
-    for dx in (2, 1, 3):
-        pairs[dx] = swap(jnp.stack([keep[dx, part], came[dx, part]]), 2 * dx)
+    pairs = {dx: along_x_one(keep, came, dx, part) for dx in (2, 1, 3)}
     return [keep, came] + [pairs[dx] for dx in (1, 2, 3)]
 
 
@@ -626,8 +626,9 @@
     wu, ab, level = value_part(slots_v, k, inverse, w, tail, reach)
     one = later_plane(ab, 1)
     two = later_plane(ab, 2)
+    q_part = slice(C, 2 * C)
     keep_q, came_q, _ = lax.optimization_barrier((keep, came, ab))
-    slots_q = along_x(keep_q, came_q, slice(C, 2 * C))
+    slots_q = along_x(keep_q, came_q, q_part)
     no = query(slots_q, k, mix, wu, level)
     before, upto = combine(ab, one, two)
     six = later_plane(upto, 6)

time: 77.3 us -> 77.5 us (level)
  waiting for transfers between devices: 23.2 us -> 24 us
  transfers between devices with their start and end apart: 26 -> 26, of which waited for: 12 -> 13; matrix products, arithmetic and copies ran while one was open for 0% -> 0% of each run, Pallas kernels for 9% -> 8%
where the time goes in v13:
time: 77.5 us; the launch traced here: 77.3 us
  starting transfers between devices  40.1 us (52%)
  waiting for transfers between devices  24 us (31%)
  Pallas kernels  11.8 us (15%)
  other arithmetic  0.97 us (1%)
    ppermute x15, starting transfers between devices, swap(): lax.ppermute(block, 'seq', [(s, s ^ d) for s in range(PLANE * PLANES)])  19.9 us
    ppermute x5, waiting for transfers between devices, later_plane(): return lax.ppermute(block, 'seq', route)  12.1 us
    ppermute x5, starting transfers between devices, later_plane(): return lax.ppermute(block, 'seq', route)  11.5 us
    ppermute x6, starting transfers between devices, turn(): return lax.ppermute(block, 'heads', [(s, (s + step) % 4) for s in range(4)])  8.73 us
    ppermute x15, waiting for transfers between devices, swap(): lax.ppermute(block, 'seq', [(s, s ^ d) for s in range(PLANE * PLANES)])  6.47 us
    ppermute x6, waiting for transfers between devices, turn(): return lax.ppermute(block, 'heads', [(s, (s + step) % 4) for s in range(4)])  5.41 us
    pallas_call x1, Pallas kernels, key_part(): pl.pallas_call(key_kernel, out_shape=[jax.ShapeDtypeStruct((PLANE, KROWS,...  2.71 us
  transfers between devices with their start and end apart: 26, of which 13 were waited for; matrix products, arithmetic and copies ran while one was open for 0% of the time, Pallas kernels for 8%

profile of v13, /device:TPU:128, one launch (start us, length us, event | category | flops | bytes accessed | tf_op | source)
XLA Modules:
  0.0 77.3 jit_solution(14399225310212582590)
XLA Ops:
  0.0 1.4 %pack.1 = (bf16[4,144,128]{2,1,0:T(8,128)(2,1)S(1)}, bf16[4,144,128]{2,1,0:T(8,128)(2,1)S(1)}, bf16[4,256,128]{2,1,0:T(8,128)(2,1)S(1)}, bf16[4,256,128]{2,1,0:T(8,128)(2,1)S(1)}) custom-call(bf16[128,1024]{1,0:T(8,128)(2,1)} %q_ref.1, bf16[128,1024]{1,0:T(8,128)(2,1)} %k_ref.1, bf16[128,1024]{1,0:T(8,128)(2,1)} %v_ref.1, f32[8,128]{1,0:T(8,128)} %decay_ref.1, ...), custom_call_target="tpu_custom_call" | custom-call | tf_op jit(solution)/shard_map/pack/pallas_call | solution.py:113
  1.4 0.1 collective-permute-start.4
  1.5 0.5 collective-permute-start
  2.0 0.8 %collective-permute-done.4.refs_1_ = bf16[4,144,128]{2,1,0:T(8,128)(2,1)S(1)} collective-permute-done((bf16[4,144,128]{2,1,0:T(8,128)(2,1)S(1)}, bf16[4,144,128]{2,1,0:T(8,128)(2,1)S(1)}, u32[]{:S(2)}, u32[]{:S(2)}) %collective-permute-start.4) | collective-permute-done | bytes 147488 | tf_op jit(solution)/shard_map/ppermute | solution.py:598
  2.9 1.6 %collective-permute-start.5 = (bf16[2,144,128]{2,1,0:T(8,128)(2,1)S(1)}, bf16[2,144,128]{2,1,0:T(8,128)(2,1)S(1)}, u32[]{:S(2)}, u32[]{:S(2)}) collective-permute-start(bf16[2,144,128]{2,1,0:T(8,128)(2,1)S(1)} %pad_maximum_fusion), channel_id=1, source_target_pairs={{0,8},{4,12},{8,0},{12,4},{16,24},{20,28},{24,16},{28,20},{32,40},... | collective-permute-start | bytes 221192 | tf_op jit(solution)/shard_map/ppermute | solution.py:598
  4.4 2.8 %collective-permute-start.6 = (bf16[2,144,128]{2,1,0:T(8,128)(2,1)S(1)}, bf16[2,144,128]{2,1,0:T(8,128)(2,1)S(1)}, u32[]{:S(2)}, u32[]{:S(2)}) collective-permute-start(bf16[2,144,128]{2,1,0:T(8,128)(2,1)S(1)} %pad_maximum_fusion.1), channel_id=1, source_target_pairs={{0,16},{4,20},{8,24},{12,28},{16,0},{20,4},{24,8},{28,12},{32,48},... | collective-permute-start | bytes 221192 | tf_op jit(solution)/shard_map/ppermute | solution.py:598
  7.3 0.6 collective-permute-start.7
  7.8 0.0 collective-permute-done.refs_1_
  7.9 0.4 collective-permute-start.1
  8.2 4.0 %collective-permute-start.2 = (bf16[2,128,128]{2,1,0:T(8,128)(2,1)S(1)}, bf16[2,128,128]{2,1,0:T(8,128)(2,1)S(1)}, u32[]{:S(2)}, u32[]{:S(2)}) collective-permute-start(bf16[2,128,128]{2,1,0:T(8,128)(2,1)S(1)} %pad_maximum_fusion.4), channel_id=1, source_target_pairs={{0,16},{4,20},{8,24},{12,28},{16,0},{20,4},{24,8},{28,12},{32,48},... | collective-permute-start | bytes 196616 | tf_op jit(solution)/shard_map/ppermute | solution.py:598
  12.3 0.0 copy-start.1
  12.3 0.0 collective-permute-done.5.refs_2_
  12.3 0.6 collective-permute-start.3
  12.9 0.0 collective-permute-done.6.refs_3_
  12.9 0.8 collective-permute-done.7.refs_4_
  13.6 2.7 %keys.1 = (bf16[8,144,128]{2,1,0:T(8,128)(2,1)S(1)}, f32[8,128,128]{2,1,0:T(8,128)S(1)}, f32[8,128,128]{2,1,0:T(8,128)S(1)}, f32[8,128,128]{2,1,0:T(8,128)S(1)},...) custom-call(bf16[4,144,128]{2,1,0:T(8,128)(2,1)S(1)} %get-tuple-element.38.refs_0_, ...), custom_call_target="tpu_custom_call" | custom-call | flops 2000000000 | bytes 4000000 | tf_op jit(solution)/shard_map/keys/pallas_call | solution.py:271
  16.3 0.0 collective-permute-done.1.refs_2_
  16.4 1.5 %collective-permute-done.3.refs_4_ = bf16[2,128,128]{2,1,0:T(8,128)(2,1)S(1)} collective-permute-done((bf16[2,128,128]{2,1,0:T(8,128)(2,1)S(1)}, bf16[2,128,128]{2,1,0:T(8,128)(2,1)S(1)}, u32[]{:S(2)}, u32[]{:S(2)}) %collective-permute-start.3) | collective-permute-done | bytes 65568 | tf_op jit(solution)/shard_map/ppermute | solution.py:598
  17.9 1.1 %values.1 = (f32[8,128,256]{2,1,0:T(8,128)S(1)}, bf16[128,256]{1,0:T(8,128)(2,1)S(1)}, f32[7,128,256]{2,1,0:T(8,128)S(1)}) custom-call(bf16[4,256,128]{2,1,0:T(8,128)(2,1)S(1)} %get-tuple-element.46.refs_0_, bf16[4,256,128]{2,1,0:T(8,128)(2,1)S(1)} %collective-permute-done.refs_1_, bf16[2,128,128]{2,1,0:T(8,128)(2,1)S(1)} %collective-permute-done.1.refs_2_, ...), custom_call_target="tpu_custom_call" | custom-call | flops 1000000000 | bytes 4000000 | tf_op jit(solution)/shard_map/values/pallas_call | solution.py:284
  19.0 0.0 slice-start
  19.0 3.6 %collective-permute-start.12 = (bf16[128,256]{1,0:T(8,128)(2,1)S(1)}, bf16[128,256]{1,0:T(8,128)(2,1)S(1)}, u32[]{:S(2)}, u32[]{:S(2)}) collective-permute-start(bf16[128,256]{1,0:T(8,128)(2,1)S(1)} %get-tuple-element.45.own_ref), channel_id=1, source_target_pairs={{0,64},{4,68},{8,72},{12,76},{16,80},{20,84},{24,88},{28,92},{32,9... | collective-permute-start | bytes 196616 | tf_op jit(solution)/shard_map/ppermute | solution.py:617
  22.7 2.9 %collective-permute-start.11 = (bf16[128,256]{1,0:T(8,128)(2,1)S(1)}, bf16[128,256]{1,0:T(8,128)(2,1)S(1)}, u32[]{:S(2)}, u32[]{:S(2)}) collective-permute-start(bf16[128,256]{1,0:T(8,128)(2,1)S(1)} %get-tuple-element.45.own_ref), channel_id=1, source_target_pairs={{0,32},{4,36},{8,40},{12,44},{16,48},{20,52},{24,56},{28,60},{32,6... | collective-permute-start | bytes 196616 | tf_op jit(solution)/shard_map/ppermute | solution.py:617
  25.6 0.1 collective-permute-start.8
  25.8 2.0 %collective-permute-start.9 = (bf16[2,128,128]{2,1,0:T(8,128)(2,1)S(1)}, bf16[2,128,128]{2,1,0:T(8,128)(2,1)S(1)}, u32[]{:S(2)}, u32[]{:S(2)}) collective-permute-start(bf16[2,128,128]{2,1,0:T(8,128)(2,1)S(1)} %pad_maximum_fusion.7), channel_id=1, source_target_pairs={{0,16},{4,20},{8,24},{12,28},{16,0},{20,4},{24,8},{28,12},{32,48},... | collective-permute-start | bytes 196616 | tf_op jit(solution)/shard_map/ppermute | solution.py:598
  27.8 2.8 %collective-permute-start.10 = (bf16[2,128,128]{2,1,0:T(8,128)(2,1)S(1)}, bf16[2,128,128]{2,1,0:T(8,128)(2,1)S(1)}, u32[]{:S(2)}, u32[]{:S(2)}) collective-permute-start(bf16[2,128,128]{2,1,0:T(8,128)(2,1)S(1)} %pad_maximum_fusion.8), channel_id=1, source_target_pairs={{0,24},{4,28},{8,16},{12,20},{16,8},{20,12},{24,0},{28,4},{32,56},... | collective-permute-start | bytes 196616 | tf_op jit(solution)/shard_map/ppermute | solution.py:598
  30.6 0.0 collective-permute-done.12.two_ref
  30.6 0.0 collective-permute-done.11.one_ref
  30.6 0.3 combine.1
  30.9 1.9 %collective-permute-start.14 = (bf16[128,256]{1,0:T(8,128)(2,1)S(1)}, bf16[128,256]{1,0:T(8,128)(2,1)S(1)}, u32[]{:S(2)}, u32[]{:S(2)}) collective-permute-start(bf16[128,256]{1,0:T(8,128)(2,1)S(1)} %get-tuple-element.52), channel_id=1, source_target_pairs={{0,96},{4,100},{8,104},{12,108},{16,112},{20,116},{24,120},{28,124... | collective-permute-start | bytes 196616 | tf_op jit(solution)/shard_map/ppermute | solution.py:617
  32.9 0.7 collective-permute-start.13
  33.5 0.0 collective-permute-done.8.refs_2_
  33.6 0.0 collective-permute-done.10.refs_4_
  33.6 1.3 %query.1.no_ref = f32[1024,256]{1,0:T(8,128)S(1)} custom-call(bf16[4,256,128]{2,1,0:T(8,128)(2,1)S(1)} %get-tuple-element.46.refs_0_, bf16[4,256,128]{2,1,0:T(8,128)(2,1)S(1)} %collective-permute-done.refs_1_, bf16[2,128,128]{2,1,0:T(8,128)(2,1)S(1)} %collective-permute-done.8.refs_2_, bf16[2,128,128]{2,1,0:T(8,128)(2,1)S(1)} %collective-permute-done.9.refs_3_, ...), custom_call_target="tpu_custom_call" | custom-call | flops 1000000000 | bytes 4000000 | tf_op jit(solution)/shard_map/query/pallas_call | solution.py:339
  34.9 6.0 %collective-permute-done.14.three_ref = bf16[128,256]{1,0:T(8,128)(2,1)S(1)} collective-permute-done((bf16[128,256]{1,0:T(8,128)(2,1)S(1)}, bf16[128,256]{1,0:T(8,128)(2,1)S(1)}, u32[]{:S(2)}, u32[]{:S(2)}) %collective-permute-start.14) | collective-permute-done | bytes 65568 | tf_op jit(solution)/shard_map/ppermute | solution.py:617
  40.9 0.0 collective-permute-done.13.six_ref
  40.9 0.7 norm.1.normed_ref
  41.7 0.0 slice-start.1
  41.7 2.4 %collective-permute-start.15 = (bf16[1024,128]{1,0:T(8,128)(2,1)S(1)}, bf16[1024,128]{1,0:T(8,128)(2,1)S(1)}, u32[]{:S(2)}, u32[]{:S(2)}) collective-permute-start(bf16[1024,128]{1,0:T(8,128)(2,1)S(1)} %norm.1.normed_ref), channel_id=1, source_target_pairs={{0,32},{4,36},{8,40},{12,44},{16,48},{20,52},{24,56},{28,60},{32,6... | collective-permute-start | bytes 786440 | tf_op jit(solution)/shard_map/ppermute | solution.py:617
  44.1 1.3 %own.1 = (f32[1024,128]{1,0:T(8,128)S(1)}, f32[2,1024,128]{2,1,0:T(8,128)S(1)}, bf16[1024,128]{1,0:T(8,128)(2,1)S(1)}) custom-call(bf16[1024,128]{1,0:T(8,128)(2,1)S(1)} %norm.1.normed_ref, bf16[8,128,384]{2,1,0:T(8,128)(2,1)S(1)} %copy-done.1), custom_call_target="tpu_custom_call" | custom-call | flops 1000000000 | bytes 3000000 | tf_op jit(solution)/shard_map/own/pallas_call | solution.py:461
  45.3 6.1 %collective-permute-done.15.halo_ref = bf16[1024,128]{1,0:T(8,128)(2,1)S(1)} collective-permute-done((bf16[1024,128]{1,0:T(8,128)(2,1)S(1)}, bf16[1024,128]{1,0:T(8,128)(2,1)S(1)}, u32[]{:S(2)}, u32[]{:S(2)}) %collective-permute-start.15) | collective-permute-done | bytes 262176 | tf_op jit(solution)/shard_map/ppermute | solution.py:617
  51.4 1.5 %halo.1 = (bf16[4,128,128]{2,1,0:T(8,128)(2,1)S(1)}, bf16[4,128,128]{2,1,0:T(8,128)(2,1)S(1)}) custom-call(bf16[1024,128]{1,0:T(8,128)(2,1)S(1)} %collective-permute-done.15.halo_ref, bf16[8,128,384]{2,1,0:T(8,128)(2,1)S(1)} %copy-done.1, f32[1024,128]{1,0:T(8,128)S(1)} %get-tuple-element.53.acc_ref, f32[2,1024,128]{2,1,0:T(8,128)S(1)} %get-tuple-element.54.stat_ref, ...), custom_call_target="tpu_custom_call" | custom-call | flops 1000000000 | bytes 3000000 | tf_op jit(solution)/shard_map/halo/pallas_call | solution.py:513
  52.9 0.1 collective-permute-start.16
  53.0 1.3 %collective-permute-done.16.came = bf16[4,128,128]{2,1,0:T(8,128)(2,1)S(1)} collective-permute-done((bf16[4,128,128]{2,1,0:T(8,128)(2,1)S(1)}, bf16[4,128,128]{2,1,0:T(8,128)(2,1)S(1)}, u32[]{:S(2)}, u32[]{:S(2)}) %collective-permute-start.16) | collective-permute-done | bytes 131104 | tf_op jit(solution)/shard_map/ppermute | solution.py:598
  54.4 0.1 collective-permute-start.17
  54.5 1.3 %collective-permute-start.19 = (bf16[2,128,128]{2,1,0:T(8,128)(2,1)S(1)}, bf16[2,128,128]{2,1,0:T(8,128)(2,1)S(1)}, u32[]{:S(2)}, u32[]{:S(2)}) collective-permute-start(bf16[2,128,128]{2,1,0:T(8,128)(2,1)S(1)} %pad_maximum_fusion.11), channel_id=1, source_target_pairs={{0,8},{4,12},{8,0},{12,4},{16,24},{20,28},{24,16},{28,20},{32,40},... | collective-permute-start | bytes 196616 | tf_op jit(solution)/shard_map/ppermute | solution.py:598
  55.8 2.9 %collective-permute-start.18 = (bf16[2,128,128]{2,1,0:T(8,128)(2,1)S(1)}, bf16[2,128,128]{2,1,0:T(8,128)(2,1)S(1)}, u32[]{:S(2)}, u32[]{:S(2)}) collective-permute-start(bf16[2,128,128]{2,1,0:T(8,128)(2,1)S(1)} %pad_maximum_fusion.10), channel_id=1, source_target_pairs={{0,24},{4,28},{8,16},{12,20},{16,8},{20,12},{24,0},{28,4},{32,56},... | collective-permute-start | bytes 196616 | tf_op jit(solution)/shard_map/ppermute | solution.py:598
  58.7 0.6 collective-permute-done.19.one
  59.4 0.7 early.1.acc_ref
  60.1 0.7 collective-permute-done.17.two
  60.8 0.7 collective-permute-done.18.three
  61.5 0.7 late.1
  62.3 1.7 %collective-permute-start.20 = (bf16[32,2048]{1,0:T(8,128)(2,1)S(1)}, bf16[32,2048]{1,0:T(8,128)(2,1)S(1)}, u32[]{:S(2)}, u32[]{:S(2)}) collective-permute-start(bf16[32,2048]{1,0:T(8,128)(2,1)S(1)} %get-tuple-element.60), channel_id=1, source_target_pairs={{0,1},{1,2},{2,3},{3,0},{4,5},{5,6},{6,7},{7,4},{8,9},{9,10},{10,1... | collective-permute-start | bytes 393224 | tf_op jit(solution)/shard_map/ppermute | solution.py:645
  63.9 1.7 %collective-permute-start.21 = (bf16[32,2048]{1,0:T(8,128)(2,1)S(1)}, bf16[32,2048]{1,0:T(8,128)(2,1)S(1)}, u32[]{:S(2)}, u32[]{:S(2)}) collective-permute-start(bf16[32,2048]{1,0:T(8,128)(2,1)S(1)} %get-tuple-element.61), channel_id=1, source_target_pairs={{0,3},{1,0},{2,1},{3,2},{4,7},{5,4},{6,5},{7,6},{8,11},{9,8},{10,9... | collective-permute-start | bytes 393224 | tf_op jit(solution)/shard_map/ppermute | solution.py:645
  65.6 1.8 %collective-permute-start.23 = (bf16[32,2048]{1,0:T(8,128)(2,1)S(1)}, bf16[32,2048]{1,0:T(8,128)(2,1)S(1)}, u32[]{:S(2)}, u32[]{:S(2)}) collective-permute-start(bf16[32,2048]{1,0:T(8,128)(2,1)S(1)} %get-tuple-element.63), channel_id=1, source_target_pairs={{0,3},{1,0},{2,1},{3,2},{4,7},{5,4},{6,5},{7,6},{8,11},{9,8},{10,9... | collective-permute-start | bytes 393224 | tf_op jit(solution)/shard_map/ppermute | solution.py:645
  67.4 0.2 collective-permute-start.25
  67.6 0.9 %collective-permute-done.20 = bf16[32,2048]{1,0:T(8,128)(2,1)S(1)} collective-permute-done((bf16[32,2048]{1,0:T(8,128)(2,1)S(1)}, bf16[32,2048]{1,0:T(8,128)(2,1)S(1)}, u32[]{:S(2)}, u32[]{:S(2)}) %collective-permute-start.20) | collective-permute-done | bytes 131104 | tf_op jit(solution)/shard_map/ppermute | solution.py:645
  68.5 1.4 %collective-permute-done.21 = bf16[32,2048]{1,0:T(8,128)(2,1)S(1)} collective-permute-done((bf16[32,2048]{1,0:T(8,128)(2,1)S(1)}, bf16[32,2048]{1,0:T(8,128)(2,1)S(1)}, u32[]{:S(2)}, u32[]{:S(2)}) %collective-permute-start.21) | collective-permute-done | bytes 131104 | tf_op jit(solution)/shard_map/ppermute | solution.py:645
  69.9 1.5 %collective-permute-start.22 = (bf16[32,2048]{1,0:T(8,128)(2,1)S(1)}, bf16[32,2048]{1,0:T(8,128)(2,1)S(1)}, u32[]{:S(2)}, u32[]{:S(2)}) collective-permute-start(bf16[32,2048]{1,0:T(8,128)(2,1)S(1)} %add_convert_fusion.1), channel_id=1, source_target_pairs={{0,1},{1,2},{2,3},{3,0},{4,5},{5,6},{6,7},{7,4},{8,9},{9,10},{10,1... | collective-permute-start | bytes 393224 | tf_op jit(solution)/shard_map/ppermute | solution.py:645
  71.5 1.9 %collective-permute-start.24 = (bf16[32,2048]{1,0:T(8,128)(2,1)S(1)}, bf16[32,2048]{1,0:T(8,128)(2,1)S(1)}, u32[]{:S(2)}, u32[]{:S(2)}) collective-permute-start(bf16[32,2048]{1,0:T(8,128)(2,1)S(1)} %add_convert_fusion), channel_id=1, source_target_pairs={{0,3},{1,0},{2,1},{3,2},{4,7},{5,4},{6,5},{7,6},{8,11},{9,8},{10,9... | collective-permute-start | bytes 393224 | tf_op jit(solution)/shard_map/ppermute | solution.py:645
  73.3 0.0 collective-permute-done.23
  73.3 2.8 %collective-permute-done.22 = bf16[32,2048]{1,0:T(8,128)(2,1)S(1)} collective-permute-done((bf16[32,2048]{1,0:T(8,128)(2,1)S(1)}, bf16[32,2048]{1,0:T(8,128)(2,1)S(1)}, u32[]{:S(2)}, u32[]{:S(2)}) %collective-permute-start.22) | collective-permute-done | bytes 131104 | tf_op jit(solution)/shard_map/ppermute | solution.py:645
  76.2 0.0 collective-permute-done.25
  76.2 0.3 collective-permute-done.24
  76.5 0.8 fusion
  (31 shorter events, 0.3 us)
Async XLA Ops:
  1.4 1.5 %collective-permute-start.4 = (bf16[4,144,128]{2,1,0:T(8,128)(2,1)S(1)}, bf16[4,144,128]{2,1,0:T(8,128)(2,1)S(1)}, u32[]{:S(2)}, u32[]{:S(2)}) collective-permute-start(bf16[4,144,128]{2,1,0:T(8,128)(2,1)S(1)} %get-tuple-element.39), channel_id=1, source_target_pairs={{0,4},{4,0},{8,12},{12,8},{16,20},{20,16},{24,28},{28,24},{32,36},... | collective-permute-start | bytes 442376 | tf_op jit(solution)/shard_map/ppermute | solution.py:598
  1.5 6.4 %collective-permute-start = (bf16[4,256,128]{2,1,0:T(8,128)(2,1)S(1)}, bf16[4,256,128]{2,1,0:T(8,128)(2,1)S(1)}, u32[]{:S(2)}, u32[]{:S(2)}) collective-permute-start(bf16[4,256,128]{2,1,0:T(8,128)(2,1)S(1)} %get-tuple-element.37), channel_id=1, source_target_pairs={{0,4},{4,0},{8,12},{12,8},{16,20},{20,16},{24,28},{28,24},{32,36},... | collective-permute-start | bytes 786440 | tf_op jit(solution)/shard_map/ppermute | solution.py:598
  2.9 9.4 %collective-permute-start.5 = (bf16[2,144,128]{2,1,0:T(8,128)(2,1)S(1)}, bf16[2,144,128]{2,1,0:T(8,128)(2,1)S(1)}, u32[]{:S(2)}, u32[]{:S(2)}) collective-permute-start(bf16[2,144,128]{2,1,0:T(8,128)(2,1)S(1)} %pad_maximum_fusion), channel_id=1, source_target_pairs={{0,8},{4,12},{8,0},{12,4},{16,24},{20,28},{24,16},{28,20},{32,40},... | collective-permute-start | bytes 221192 | tf_op jit(solution)/shard_map/ppermute | solution.py:598
  4.4 8.4 %collective-permute-start.6 = (bf16[2,144,128]{2,1,0:T(8,128)(2,1)S(1)}, bf16[2,144,128]{2,1,0:T(8,128)(2,1)S(1)}, u32[]{:S(2)}, u32[]{:S(2)}) collective-permute-start(bf16[2,144,128]{2,1,0:T(8,128)(2,1)S(1)} %pad_maximum_fusion.1), channel_id=1, source_target_pairs={{0,16},{4,20},{8,24},{12,28},{16,0},{20,4},{24,8},{28,12},{32,48},... | collective-permute-start | bytes 221192 | tf_op jit(solution)/shard_map/ppermute | solution.py:598
  7.3 6.4 %collective-permute-start.7 = (bf16[2,144,128]{2,1,0:T(8,128)(2,1)S(1)}, bf16[2,144,128]{2,1,0:T(8,128)(2,1)S(1)}, u32[]{:S(2)}, u32[]{:S(2)}) collective-permute-start(bf16[2,144,128]{2,1,0:T(8,128)(2,1)S(1)} %pad_maximum_fusion.2), channel_id=1, source_target_pairs={{0,24},{4,28},{8,16},{12,20},{16,8},{20,12},{24,0},{28,4},{32,56},... | collective-permute-start | bytes 221192 | tf_op jit(solution)/shard_map/ppermute | solution.py:598
  7.9 8.5 %collective-permute-start.1 = (bf16[2,128,128]{2,1,0:T(8,128)(2,1)S(1)}, bf16[2,128,128]{2,1,0:T(8,128)(2,1)S(1)}, u32[]{:S(2)}, u32[]{:S(2)}) collective-permute-start(bf16[2,128,128]{2,1,0:T(8,128)(2,1)S(1)} %pad_maximum_fusion.3), channel_id=1, source_target_pairs={{0,8},{4,12},{8,0},{12,4},{16,24},{20,28},{24,16},{28,20},{32,40},... | collective-permute-start | bytes 196616 | tf_op jit(solution)/shard_map/ppermute | solution.py:598
  8.2 8.1 %collective-permute-start.2 = (bf16[2,128,128]{2,1,0:T(8,128)(2,1)S(1)}, bf16[2,128,128]{2,1,0:T(8,128)(2,1)S(1)}, u32[]{:S(2)}, u32[]{:S(2)}) collective-permute-start(bf16[2,128,128]{2,1,0:T(8,128)(2,1)S(1)} %pad_maximum_fusion.4), channel_id=1, source_target_pairs={{0,16},{4,20},{8,24},{12,28},{16,0},{20,4},{24,8},{28,12},{32,48},... | collective-permute-start | bytes 196616 | tf_op jit(solution)/shard_map/ppermute | solution.py:598
  12.3 28.7 %copy-start = (f32[128]{0:T(128)S(1)}, f32[128]{0:T(128)}, u32[]{:S(2)}) copy-start(f32[128]{0:T(128)} %param.13) | copy-start | bytes 1540
  12.3 31.8 %copy-start.1 = (bf16[8,128,384]{2,1,0:T(8,128)(2,1)S(1)}, bf16[8,128,384]{2,1,0:T(8,128)(2,1)}, u32[]{:S(2)}) copy-start(bf16[8,128,384]{2,1,0:T(8,128)(2,1)} %weight_ref.5) | copy-start | bytes 2359300
  12.3 5.6 %collective-permute-start.3 = (bf16[2,128,128]{2,1,0:T(8,128)(2,1)S(1)}, bf16[2,128,128]{2,1,0:T(8,128)(2,1)S(1)}, u32[]{:S(2)}, u32[]{:S(2)}) collective-permute-start(bf16[2,128,128]{2,1,0:T(8,128)(2,1)S(1)} %pad_maximum_fusion.5), channel_id=1, source_target_pairs={{0,24},{4,28},{8,16},{12,20},{16,8},{20,12},{24,0},{28,4},{32,56},... | collective-permute-start | bytes 196616 | tf_op jit(solution)/shard_map/ppermute | solution.py:598
  19.0 40.4 %slice-start = ((s8[8388608]{0:T(1024)(128)(4,1)}), s8[4194304]{0:T(1024)(128)(4,1)S(1)}, s32[]{:S(2)}) async-start(s8[8388608]{0:T(1024)(128)(4,1)} %bitcast.1), calls=%async_computation | async-start | bytes 8388608
  19.0 11.6 %collective-permute-start.12 = (bf16[128,256]{1,0:T(8,128)(2,1)S(1)}, bf16[128,256]{1,0:T(8,128)(2,1)S(1)}, u32[]{:S(2)}, u32[]{:S(2)}) collective-permute-start(bf16[128,256]{1,0:T(8,128)(2,1)S(1)} %get-tuple-element.45.own_ref), channel_id=1, source_target_pairs={{0,64},{4,68},{8,72},{12,76},{16,80},{20,84},{24,88},{28,92},{32,9... | collective-permute-start | bytes 196616 | tf_op jit(solution)/shard_map/ppermute | solution.py:617
  22.7 7.9 %collective-permute-start.11 = (bf16[128,256]{1,0:T(8,128)(2,1)S(1)}, bf16[128,256]{1,0:T(8,128)(2,1)S(1)}, u32[]{:S(2)}, u32[]{:S(2)}) collective-permute-start(bf16[128,256]{1,0:T(8,128)(2,1)S(1)} %get-tuple-element.45.own_ref), channel_id=1, source_target_pairs={{0,32},{4,36},{8,40},{12,44},{16,48},{20,52},{24,56},{28,60},{32,6... | collective-permute-start | bytes 196616 | tf_op jit(solution)/shard_map/ppermute | solution.py:617
  25.6 7.9 %collective-permute-start.8 = (bf16[2,128,128]{2,1,0:T(8,128)(2,1)S(1)}, bf16[2,128,128]{2,1,0:T(8,128)(2,1)S(1)}, u32[]{:S(2)}, u32[]{:S(2)}) collective-permute-start(bf16[2,128,128]{2,1,0:T(8,128)(2,1)S(1)} %pad_maximum_fusion.6), channel_id=1, source_target_pairs={{0,8},{4,12},{8,0},{12,4},{16,24},{20,28},{24,16},{28,20},{32,40},... | collective-permute-start | bytes 196616 | tf_op jit(solution)/shard_map/ppermute | solution.py:598
  25.8 7.8 %collective-permute-start.9 = (bf16[2,128,128]{2,1,0:T(8,128)(2,1)S(1)}, bf16[2,128,128]{2,1,0:T(8,128)(2,1)S(1)}, u32[]{:S(2)}, u32[]{:S(2)}) collective-permute-start(bf16[2,128,128]{2,1,0:T(8,128)(2,1)S(1)} %pad_maximum_fusion.7), channel_id=1, source_target_pairs={{0,16},{4,20},{8,24},{12,28},{16,0},{20,4},{24,8},{28,12},{32,48},... | collective-permute-start | bytes 196616 | tf_op jit(solution)/shard_map/ppermute | solution.py:598
  27.8 5.7 %collective-permute-start.10 = (bf16[2,128,128]{2,1,0:T(8,128)(2,1)S(1)}, bf16[2,128,128]{2,1,0:T(8,128)(2,1)S(1)}, u32[]{:S(2)}, u32[]{:S(2)}) collective-permute-start(bf16[2,128,128]{2,1,0:T(8,128)(2,1)S(1)} %pad_maximum_fusion.8), channel_id=1, source_target_pairs={{0,24},{4,28},{8,16},{12,20},{16,8},{20,12},{24,0},{28,4},{32,56},... | collective-permute-start | bytes 196616 | tf_op jit(solution)/shard_map/ppermute | solution.py:598
  30.9 10.0 %collective-permute-start.14 = (bf16[128,256]{1,0:T(8,128)(2,1)S(1)}, bf16[128,256]{1,0:T(8,128)(2,1)S(1)}, u32[]{:S(2)}, u32[]{:S(2)}) collective-permute-start(bf16[128,256]{1,0:T(8,128)(2,1)S(1)} %get-tuple-element.52), channel_id=1, source_target_pairs={{0,96},{4,100},{8,104},{12,108},{16,112},{20,116},{24,120},{28,124... | collective-permute-start | bytes 196616 | tf_op jit(solution)/shard_map/ppermute | solution.py:617
  32.9 8.1 %collective-permute-start.13 = (bf16[128,256]{1,0:T(8,128)(2,1)S(1)}, bf16[128,256]{1,0:T(8,128)(2,1)S(1)}, u32[]{:S(2)}, u32[]{:S(2)}) collective-permute-start(bf16[128,256]{1,0:T(8,128)(2,1)S(1)} %get-tuple-element.52), channel_id=1, source_target_pairs={{0,192},{4,196},{8,200},{12,204},{16,208},{20,212},{24,216},{28,22... | collective-permute-start | bytes 196616 | tf_op jit(solution)/shard_map/ppermute | solution.py:617
  41.7 17.7 %slice-start.1 = ((s8[8388608]{0:T(1024)(128)(4,1)}), s8[4194304]{0:T(1024)(128)(4,1)S(1)}, s32[]{:S(2)}) async-start(s8[8388608]{0:T(1024)(128)(4,1)} %bitcast.1), calls=%async_computation.1 | async-start | bytes 8388608
  41.7 9.7 %collective-permute-start.15 = (bf16[1024,128]{1,0:T(8,128)(2,1)S(1)}, bf16[1024,128]{1,0:T(8,128)(2,1)S(1)}, u32[]{:S(2)}, u32[]{:S(2)}) collective-permute-start(bf16[1024,128]{1,0:T(8,128)(2,1)S(1)} %norm.1.normed_ref), channel_id=1, source_target_pairs={{0,32},{4,36},{8,40},{12,44},{16,48},{20,52},{24,56},{28,60},{32,6... | collective-permute-start | bytes 786440 | tf_op jit(solution)/shard_map/ppermute | solution.py:617
  52.9 1.4 %collective-permute-start.16 = (bf16[4,128,128]{2,1,0:T(8,128)(2,1)S(1)}, bf16[4,128,128]{2,1,0:T(8,128)(2,1)S(1)}, u32[]{:S(2)}, u32[]{:S(2)}) collective-permute-start(bf16[4,128,128]{2,1,0:T(8,128)(2,1)S(1)} %get-tuple-element.57), channel_id=1, source_target_pairs={{0,4},{4,0},{8,12},{12,8},{16,20},{20,16},{24,28},{28,24},{32,36},... | collective-permute-start | bytes 393224 | tf_op jit(solution)/shard_map/ppermute | solution.py:598
  54.4 6.4 %collective-permute-start.17 = (bf16[2,128,128]{2,1,0:T(8,128)(2,1)S(1)}, bf16[2,128,128]{2,1,0:T(8,128)(2,1)S(1)}, u32[]{:S(2)}, u32[]{:S(2)}) collective-permute-start(bf16[2,128,128]{2,1,0:T(8,128)(2,1)S(1)} %pad_maximum_fusion.9), channel_id=1, source_target_pairs={{0,16},{4,20},{8,24},{12,28},{16,0},{20,4},{24,8},{28,12},{32,48},... | collective-permute-start | bytes 196616 | tf_op jit(solution)/shard_map/ppermute | solution.py:598
  54.5 4.9 %collective-permute-start.19 = (bf16[2,128,128]{2,1,0:T(8,128)(2,1)S(1)}, bf16[2,128,128]{2,1,0:T(8,128)(2,1)S(1)}, u32[]{:S(2)}, u32[]{:S(2)}) collective-permute-start(bf16[2,128,128]{2,1,0:T(8,128)(2,1)S(1)} %pad_maximum_fusion.11), channel_id=1, source_target_pairs={{0,8},{4,12},{8,0},{12,4},{16,24},{20,28},{24,16},{28,20},{32,40},... | collective-permute-start | bytes 196616 | tf_op jit(solution)/shard_map/ppermute | solution.py:598
  55.8 5.7 %collective-permute-start.18 = (bf16[2,128,128]{2,1,0:T(8,128)(2,1)S(1)}, bf16[2,128,128]{2,1,0:T(8,128)(2,1)S(1)}, u32[]{:S(2)}, u32[]{:S(2)}) collective-permute-start(bf16[2,128,128]{2,1,0:T(8,128)(2,1)S(1)} %pad_maximum_fusion.10), channel_id=1, source_target_pairs={{0,24},{4,28},{8,16},{12,20},{16,8},{20,12},{24,0},{28,4},{32,56},... | collective-permute-start | bytes 196616 | tf_op jit(solution)/shard_map/ppermute | solution.py:598
  62.3 6.3 %collective-permute-start.20 = (bf16[32,2048]{1,0:T(8,128)(2,1)S(1)}, bf16[32,2048]{1,0:T(8,128)(2,1)S(1)}, u32[]{:S(2)}, u32[]{:S(2)}) collective-permute-start(bf16[32,2048]{1,0:T(8,128)(2,1)S(1)} %get-tuple-element.60), channel_id=1, source_target_pairs={{0,1},{1,2},{2,3},{3,0},{4,5},{5,6},{6,7},{7,4},{8,9},{9,10},{10,1... | collective-permute-start | bytes 393224 | tf_op jit(solution)/shard_map/ppermute | solution.py:645
  63.9 6.0 %collective-permute-start.21 = (bf16[32,2048]{1,0:T(8,128)(2,1)S(1)}, bf16[32,2048]{1,0:T(8,128)(2,1)S(1)}, u32[]{:S(2)}, u32[]{:S(2)}) collective-permute-start(bf16[32,2048]{1,0:T(8,128)(2,1)S(1)} %get-tuple-element.61), channel_id=1, source_target_pairs={{0,3},{1,0},{2,1},{3,2},{4,7},{5,4},{6,5},{7,6},{8,11},{9,8},{10,9... | collective-permute-start | bytes 393224 | tf_op jit(solution)/shard_map/ppermute | solution.py:645
  65.6 7.8 %collective-permute-start.23 = (bf16[32,2048]{1,0:T(8,128)(2,1)S(1)}, bf16[32,2048]{1,0:T(8,128)(2,1)S(1)}, u32[]{:S(2)}, u32[]{:S(2)}) collective-permute-start(bf16[32,2048]{1,0:T(8,128)(2,1)S(1)} %get-tuple-element.63), channel_id=1, source_target_pairs={{0,3},{1,0},{2,1},{3,2},{4,7},{5,4},{6,5},{7,6},{8,11},{9,8},{10,9... | collective-permute-start | bytes 393224 | tf_op jit(solution)/shard_map/ppermute | solution.py:645
  67.4 8.8 %collective-permute-start.25 = (bf16[32,2048]{1,0:T(8,128)(2,1)S(1)}, bf16[32,2048]{1,0:T(8,128)(2,1)S(1)}, u32[]{:S(2)}, u32[]{:S(2)}) collective-permute-start(bf16[32,2048]{1,0:T(8,128)(2,1)S(1)} %get-tuple-element.66), channel_id=1, source_target_pairs={{0,1},{1,2},{2,3},{3,0},{4,5},{5,6},{6,7},{7,4},{8,9},{9,10},{10,1... | collective-permute-start | bytes 393224 | tf_op jit(solution)/shard_map/ppermute | solution.py:645
  69.9 6.3 %collective-permute-start.22 = (bf16[32,2048]{1,0:T(8,128)(2,1)S(1)}, bf16[32,2048]{1,0:T(8,128)(2,1)S(1)}, u32[]{:S(2)}, u32[]{:S(2)}) collective-permute-start(bf16[32,2048]{1,0:T(8,128)(2,1)S(1)} %add_convert_fusion.1), channel_id=1, source_target_pairs={{0,1},{1,2},{2,3},{3,0},{4,5},{5,6},{6,7},{7,4},{8,9},{9,10},{10,1... | collective-permute-start | bytes 393224 | tf_op jit(solution)/shard_map/ppermute | solution.py:645
  71.5 5.0 %collective-permute-start.24 = (bf16[32,2048]{1,0:T(8,128)(2,1)S(1)}, bf16[32,2048]{1,0:T(8,128)(2,1)S(1)}, u32[]{:S(2)}, u32[]{:S(2)}) collective-permute-start(bf16[32,2048]{1,0:T(8,128)(2,1)S(1)} %add_convert_fusion), channel_id=1, source_target_pairs={{0,3},{1,0},{2,1},{3,2},{4,7},{5,4},{6,5},{7,6},{8,11},{9,8},{10,9... | collective-permute-start | bytes 393224 | tf_op jit(solution)/shard_map/ppermute | solution.py:645

commit v14 on v12

--- a/solution.py
+++ b/solution.py
@@ -356,7 +356,7 @@
     return dot(jnp.concatenate([a, a], axis=1), jnp.concatenate([hi, lo], axis=0))
 
 
-def combine_kernel(own_ref, one_ref, two_ref, before_ref, upto_ref):
+def combine_kernel(own_ref, two_ref, one_ref, before_ref, upto_ref):
     a_one, a_own = one_ref[:, :C], own_ref[:, :C]
     reach = dot(a_one, two_ref[:, :C])
     state = one_ref[:, C:].astype(F32) + dot(a_one, two_ref[:, C:])
@@ -366,7 +366,7 @@
     upto_ref[:, C:] = (own_ref[:, C:].astype(F32) + times(a_own, state)).astype(BF16)
 
 
-def combine(own_map, one, two):
+def combine(own_map, two, one):
     return pl.pallas_call(
         combine_kernel,
         out_shape=[
@@ -377,7 +377,7 @@
         out_specs=[vmem()] * 2,
         compiler_params=params(),
         name="combine",
-    )(own_map, one, two)
+    )(own_map, two, one)
 
 
 def norm_kernel(no_ref, gain_ref, before_ref, six_ref, three_ref, normed_ref):
@@ -629,7 +629,7 @@
     keep_q, came_q, _ = lax.optimization_barrier((keep, came, ab))
     slots_q = along_x(keep_q, came_q, slice(C, 2 * C))
     no = query(slots_q, k, mix, wu, level)
-    before, upto = combine(ab, one, two)
+    before, upto = combine(ab, two, one)
     six = later_plane(upto, 6)
     three = later_plane(upto, 3)
     normed = norm(no, gain[None, :], before, six, three)

time: 77.3 us -> 77.7 us (level)
  starting transfers between devices: 40.7 us -> 42.1 us
  waiting for transfers between devices: 23.2 us -> 22.2 us
    ppermute x5, starting transfers between devices: 11.5 us -> 12.9 us  [later_plane(): return lax.ppermute(block, 'seq', route)]
    ppermute x5, waiting for transfers between devices: 12.1 us -> 11.1 us  [later_plane(): return lax.ppermute(block, 'seq', route)]
  transfers between devices with their start and end apart: 26 -> 26, of which waited for: 12 -> 13; matrix products, arithmetic and copies ran while one was open for 0% -> 0% of each run, Pallas kernels for 9% -> 9%
where the time goes in v14:
time: 77.7 us; the launch traced here: 77.5 us
  starting transfers between devices  42.1 us (54%)
  waiting for transfers between devices  22.2 us (29%)
  Pallas kernels  11.8 us (15%)
  other arithmetic  0.96 us (1%)
    ppermute x15, starting transfers between devices, swap(): lax.ppermute(block, 'seq', [(s, s ^ d) for s in range(PLANE * PLANES)])  20.5 us
    ppermute x5, starting transfers between devices, later_plane(): return lax.ppermute(block, 'seq', route)  12.9 us
    ppermute x5, waiting for transfers between devices, later_plane(): return lax.ppermute(block, 'seq', route)  11.1 us
    ppermute x6, starting transfers between devices, turn(): return lax.ppermute(block, 'heads', [(s, (s + step) % 4) for s in range(4)])  8.73 us
    ppermute x15, waiting for transfers between devices, swap(): lax.ppermute(block, 'seq', [(s, s ^ d) for s in range(PLANE * PLANES)])  6.17 us
    ppermute x6, waiting for transfers between devices, turn(): return lax.ppermute(block, 'heads', [(s, (s + step) % 4) for s in range(4)])  4.87 us
    pallas_call x1, Pallas kernels, key_part(): pl.pallas_call(key_kernel, out_shape=[jax.ShapeDtypeStruct((PLANE, KROWS,...  2.71 us
  transfers between devices with their start and end apart: 26, of which 13 were waited for; matrix products, arithmetic and copies ran while one was open for 0% of the time, Pallas kernels for 9%

profile of v14, /device:TPU:128, one launch (start us, length us, event | category | flops | bytes accessed | tf_op | source)
XLA Modules:
  0.0 77.5 jit_solution(13480319060739826832)
XLA Ops:
  0.0 1.4 %pack.1 = (bf16[4,144,128]{2,1,0:T(8,128)(2,1)S(1)}, bf16[4,144,128]{2,1,0:T(8,128)(2,1)S(1)}, bf16[4,256,128]{2,1,0:T(8,128)(2,1)S(1)}, bf16[4,256,128]{2,1,0:T(8,128)(2,1)S(1)}) custom-call(bf16[128,1024]{1,0:T(8,128)(2,1)} %q_ref.1, bf16[128,1024]{1,0:T(8,128)(2,1)} %k_ref.1, bf16[128,1024]{1,0:T(8,128)(2,1)} %v_ref.1, f32[8,128]{1,0:T(8,128)} %decay_ref.1, ...), custom_call_target="tpu_custom_call" | custom-call | tf_op jit(solution)/shard_map/pack/pallas_call | solution.py:113
  1.4 0.1 collective-permute-start.4
  1.5 0.5 collective-permute-start
  2.0 0.8 %collective-permute-done.4.refs_1_ = bf16[4,144,128]{2,1,0:T(8,128)(2,1)S(1)} collective-permute-done((bf16[4,144,128]{2,1,0:T(8,128)(2,1)S(1)}, bf16[4,144,128]{2,1,0:T(8,128)(2,1)S(1)}, u32[]{:S(2)}, u32[]{:S(2)}) %collective-permute-start.4) | collective-permute-done | bytes 147488 | tf_op jit(solution)/shard_map/ppermute | solution.py:600
  2.9 1.6 %collective-permute-start.5 = (bf16[2,144,128]{2,1,0:T(8,128)(2,1)S(1)}, bf16[2,144,128]{2,1,0:T(8,128)(2,1)S(1)}, u32[]{:S(2)}, u32[]{:S(2)}) collective-permute-start(bf16[2,144,128]{2,1,0:T(8,128)(2,1)S(1)} %pad_maximum_fusion), channel_id=1, source_target_pairs={{0,8},{4,12},{8,0},{12,4},{16,24},{20,28},{24,16},{28,20},{32,40},... | collective-permute-start | bytes 221192 | tf_op jit(solution)/shard_map/ppermute | solution.py:600
  4.4 2.8 %collective-permute-start.6 = (bf16[2,144,128]{2,1,0:T(8,128)(2,1)S(1)}, bf16[2,144,128]{2,1,0:T(8,128)(2,1)S(1)}, u32[]{:S(2)}, u32[]{:S(2)}) collective-permute-start(bf16[2,144,128]{2,1,0:T(8,128)(2,1)S(1)} %pad_maximum_fusion.1), channel_id=1, source_target_pairs={{0,16},{4,20},{8,24},{12,28},{16,0},{20,4},{24,8},{28,12},{32,48},... | collective-permute-start | bytes 221192 | tf_op jit(solution)/shard_map/ppermute | solution.py:600
  7.3 0.6 collective-permute-start.7
  7.8 0.0 collective-permute-done.refs_1_
  7.9 0.4 collective-permute-start.1
  8.2 4.0 %collective-permute-start.2 = (bf16[2,128,128]{2,1,0:T(8,128)(2,1)S(1)}, bf16[2,128,128]{2,1,0:T(8,128)(2,1)S(1)}, u32[]{:S(2)}, u32[]{:S(2)}) collective-permute-start(bf16[2,128,128]{2,1,0:T(8,128)(2,1)S(1)} %pad_maximum_fusion.4), channel_id=1, source_target_pairs={{0,16},{4,20},{8,24},{12,28},{16,0},{20,4},{24,8},{28,12},{32,48},... | collective-permute-start | bytes 196616 | tf_op jit(solution)/shard_map/ppermute | solution.py:600
  12.3 0.0 copy-start.1
  12.3 0.0 collective-permute-done.5.refs_2_
  12.3 0.6 collective-permute-start.3
  12.9 0.0 collective-permute-done.6.refs_3_
  12.9 0.8 collective-permute-done.7.refs_4_
  13.6 2.7 %keys.1 = (bf16[8,144,128]{2,1,0:T(8,128)(2,1)S(1)}, f32[8,128,128]{2,1,0:T(8,128)S(1)}, f32[8,128,128]{2,1,0:T(8,128)S(1)}, f32[8,128,128]{2,1,0:T(8,128)S(1)},...) custom-call(bf16[4,144,128]{2,1,0:T(8,128)(2,1)S(1)} %get-tuple-element.38.refs_0_, ...), custom_call_target="tpu_custom_call" | custom-call | flops 2000000000 | bytes 4000000 | tf_op jit(solution)/shard_map/keys/pallas_call | solution.py:271
  16.3 0.0 collective-permute-done.1.refs_2_
  16.4 0.0 collective-permute-done.2.refs_3_
  16.4 1.5 %collective-permute-done.3.refs_4_ = bf16[2,128,128]{2,1,0:T(8,128)(2,1)S(1)} collective-permute-done((bf16[2,128,128]{2,1,0:T(8,128)(2,1)S(1)}, bf16[2,128,128]{2,1,0:T(8,128)(2,1)S(1)}, u32[]{:S(2)}, u32[]{:S(2)}) %collective-permute-start.3) | collective-permute-done | bytes 65568 | tf_op jit(solution)/shard_map/ppermute | solution.py:600
  17.9 1.1 %values.1 = (f32[8,128,256]{2,1,0:T(8,128)S(1)}, bf16[128,256]{1,0:T(8,128)(2,1)S(1)}, f32[7,128,256]{2,1,0:T(8,128)S(1)}) custom-call(bf16[4,256,128]{2,1,0:T(8,128)(2,1)S(1)} %get-tuple-element.46.refs_0_, bf16[4,256,128]{2,1,0:T(8,128)(2,1)S(1)} %collective-permute-done.refs_1_, bf16[2,128,128]{2,1,0:T(8,128)(2,1)S(1)} %collective-permute-done.1.refs_2_, ...), custom_call_target="tpu_custom_call" | custom-call | flops 1000000000 | bytes 4000000 | tf_op jit(solution)/shard_map/values/pallas_call | solution.py:284
  19.0 0.0 slice-start
  19.0 3.2 %collective-permute-start.12 = (bf16[128,256]{1,0:T(8,128)(2,1)S(1)}, bf16[128,256]{1,0:T(8,128)(2,1)S(1)}, u32[]{:S(2)}, u32[]{:S(2)}) collective-permute-start(bf16[128,256]{1,0:T(8,128)(2,1)S(1)} %get-tuple-element.45.own_ref), channel_id=1, source_target_pairs={{0,32},{4,36},{8,40},{12,44},{16,48},{20,52},{24,56},{28,60},{32,6... | collective-permute-start | bytes 196616 | tf_op jit(solution)/shard_map/ppermute | solution.py:617
  22.2 3.4 %collective-permute-start.11 = (bf16[128,256]{1,0:T(8,128)(2,1)S(1)}, bf16[128,256]{1,0:T(8,128)(2,1)S(1)}, u32[]{:S(2)}, u32[]{:S(2)}) collective-permute-start(bf16[128,256]{1,0:T(8,128)(2,1)S(1)} %get-tuple-element.45.own_ref), channel_id=1, source_target_pairs={{0,64},{4,68},{8,72},{12,76},{16,80},{20,84},{24,88},{28,92},{32,9... | collective-permute-start | bytes 196616 | tf_op jit(solution)/shard_map/ppermute | solution.py:617
  25.6 0.1 collective-permute-start.8
  25.8 2.0 %collective-permute-start.9 = (bf16[2,128,128]{2,1,0:T(8,128)(2,1)S(1)}, bf16[2,128,128]{2,1,0:T(8,128)(2,1)S(1)}, u32[]{:S(2)}, u32[]{:S(2)}) collective-permute-start(bf16[2,128,128]{2,1,0:T(8,128)(2,1)S(1)} %pad_maximum_fusion.7), channel_id=1, source_target_pairs={{0,16},{4,20},{8,24},{12,28},{16,0},{20,4},{24,8},{28,12},{32,48},... | collective-permute-start | bytes 196616 | tf_op jit(solution)/shard_map/ppermute | solution.py:600
  27.8 2.8 %collective-permute-start.10 = (bf16[2,128,128]{2,1,0:T(8,128)(2,1)S(1)}, bf16[2,128,128]{2,1,0:T(8,128)(2,1)S(1)}, u32[]{:S(2)}, u32[]{:S(2)}) collective-permute-start(bf16[2,128,128]{2,1,0:T(8,128)(2,1)S(1)} %pad_maximum_fusion.8), channel_id=1, source_target_pairs={{0,24},{4,28},{8,16},{12,20},{16,8},{20,12},{24,0},{28,4},{32,56},... | collective-permute-start | bytes 196616 | tf_op jit(solution)/shard_map/ppermute | solution.py:600
  30.6 0.0 collective-permute-done.12.one_ref
  30.6 0.6 collective-permute-done.11.two_ref
  31.2 0.3 combine.1
  31.5 1.9 %collective-permute-start.14 = (bf16[128,256]{1,0:T(8,128)(2,1)S(1)}, bf16[128,256]{1,0:T(8,128)(2,1)S(1)}, u32[]{:S(2)}, u32[]{:S(2)}) collective-permute-start(bf16[128,256]{1,0:T(8,128)(2,1)S(1)} %get-tuple-element.52), channel_id=1, source_target_pairs={{0,96},{4,100},{8,104},{12,108},{16,112},{20,116},{24,120},{28,124... | collective-permute-start | bytes 196616 | tf_op jit(solution)/shard_map/ppermute | solution.py:617
  33.4 0.7 collective-permute-start.13
  34.1 0.0 collective-permute-done.9.refs_3_
  34.1 0.0 collective-permute-done.10.refs_4_
  34.1 1.3 %query.1.no_ref = f32[1024,256]{1,0:T(8,128)S(1)} custom-call(bf16[4,256,128]{2,1,0:T(8,128)(2,1)S(1)} %get-tuple-element.46.refs_0_, bf16[4,256,128]{2,1,0:T(8,128)(2,1)S(1)} %collective-permute-done.refs_1_, bf16[2,128,128]{2,1,0:T(8,128)(2,1)S(1)} %collective-permute-done.8.refs_2_, bf16[2,128,128]{2,1,0:T(8,128)(2,1)S(1)} %collective-permute-done.9.refs_3_, ...), custom_call_target="tpu_custom_call" | custom-call | flops 1000000000 | bytes 4000000 | tf_op jit(solution)/shard_map/query/pallas_call | solution.py:339
  35.5 5.9 %collective-permute-done.14.three_ref = bf16[128,256]{1,0:T(8,128)(2,1)S(1)} collective-permute-done((bf16[128,256]{1,0:T(8,128)(2,1)S(1)}, bf16[128,256]{1,0:T(8,128)(2,1)S(1)}, u32[]{:S(2)}, u32[]{:S(2)}) %collective-permute-start.14) | collective-permute-done | bytes 65568 | tf_op jit(solution)/shard_map/ppermute | solution.py:617
  41.4 0.0 collective-permute-done.13.six_ref
  41.4 0.7 norm.1.normed_ref
  42.1 0.0 slice-start.1
  42.1 3.8 %collective-permute-start.15 = (bf16[1024,128]{1,0:T(8,128)(2,1)S(1)}, bf16[1024,128]{1,0:T(8,128)(2,1)S(1)}, u32[]{:S(2)}, u32[]{:S(2)}) collective-permute-start(bf16[1024,128]{1,0:T(8,128)(2,1)S(1)} %norm.1.normed_ref), channel_id=1, source_target_pairs={{0,32},{4,36},{8,40},{12,44},{16,48},{20,52},{24,56},{28,60},{32,6... | collective-permute-start | bytes 786440 | tf_op jit(solution)/shard_map/ppermute | solution.py:617
  45.9 1.3 %own.1 = (f32[1024,128]{1,0:T(8,128)S(1)}, f32[2,1024,128]{2,1,0:T(8,128)S(1)}, bf16[1024,128]{1,0:T(8,128)(2,1)S(1)}) custom-call(bf16[1024,128]{1,0:T(8,128)(2,1)S(1)} %norm.1.normed_ref, bf16[8,128,384]{2,1,0:T(8,128)(2,1)S(1)} %copy-done.1), custom_call_target="tpu_custom_call" | custom-call | flops 1000000000 | bytes 3000000 | tf_op jit(solution)/shard_map/own/pallas_call | solution.py:461
  47.2 4.6 %collective-permute-done.15.halo_ref = bf16[1024,128]{1,0:T(8,128)(2,1)S(1)} collective-permute-done((bf16[1024,128]{1,0:T(8,128)(2,1)S(1)}, bf16[1024,128]{1,0:T(8,128)(2,1)S(1)}, u32[]{:S(2)}, u32[]{:S(2)}) %collective-permute-start.15) | collective-permute-done | bytes 262176 | tf_op jit(solution)/shard_map/ppermute | solution.py:617
  51.9 1.5 %halo.1 = (bf16[4,128,128]{2,1,0:T(8,128)(2,1)S(1)}, bf16[4,128,128]{2,1,0:T(8,128)(2,1)S(1)}) custom-call(bf16[1024,128]{1,0:T(8,128)(2,1)S(1)} %collective-permute-done.15.halo_ref, bf16[8,128,384]{2,1,0:T(8,128)(2,1)S(1)} %copy-done.1, f32[1024,128]{1,0:T(8,128)S(1)} %get-tuple-element.53.acc_ref, f32[2,1024,128]{2,1,0:T(8,128)S(1)} %get-tuple-element.54.stat_ref, ...), custom_call_target="tpu_custom_call" | custom-call | flops 1000000000 | bytes 3000000 | tf_op jit(solution)/shard_map/halo/pallas_call | solution.py:513
  53.4 0.1 collective-permute-start.16
  53.5 1.3 %collective-permute-done.16.came = bf16[4,128,128]{2,1,0:T(8,128)(2,1)S(1)} collective-permute-done((bf16[4,128,128]{2,1,0:T(8,128)(2,1)S(1)}, bf16[4,128,128]{2,1,0:T(8,128)(2,1)S(1)}, u32[]{:S(2)}, u32[]{:S(2)}) %collective-permute-start.16) | collective-permute-done | bytes 131104 | tf_op jit(solution)/shard_map/ppermute | solution.py:600
  54.8 0.1 collective-permute-start.18
  54.9 2.0 %collective-permute-start.19 = (bf16[2,128,128]{2,1,0:T(8,128)(2,1)S(1)}, bf16[2,128,128]{2,1,0:T(8,128)(2,1)S(1)}, u32[]{:S(2)}, u32[]{:S(2)}) collective-permute-start(bf16[2,128,128]{2,1,0:T(8,128)(2,1)S(1)} %pad_maximum_fusion.11), channel_id=1, source_target_pairs={{0,16},{4,20},{8,24},{12,28},{16,0},{20,4},{24,8},{28,12},{32,48},... | collective-permute-start | bytes 196616 | tf_op jit(solution)/shard_map/ppermute | solution.py:600
  57.0 2.8 %collective-permute-start.17 = (bf16[2,128,128]{2,1,0:T(8,128)(2,1)S(1)}, bf16[2,128,128]{2,1,0:T(8,128)(2,1)S(1)}, u32[]{:S(2)}, u32[]{:S(2)}) collective-permute-start(bf16[2,128,128]{2,1,0:T(8,128)(2,1)S(1)} %pad_maximum_fusion.9), channel_id=1, source_target_pairs={{0,24},{4,28},{8,16},{12,20},{16,8},{20,12},{24,0},{28,4},{32,56},... | collective-permute-start | bytes 196616 | tf_op jit(solution)/shard_map/ppermute | solution.py:600
  59.8 0.0 collective-permute-done.18.one
  59.8 1.0 %collective-permute-done.19.two = bf16[2,128,128]{2,1,0:T(8,128)(2,1)S(1)} collective-permute-done((bf16[2,128,128]{2,1,0:T(8,128)(2,1)S(1)}, bf16[2,128,128]{2,1,0:T(8,128)(2,1)S(1)}, u32[]{:S(2)}, u32[]{:S(2)}) %collective-permute-start.19) | collective-permute-done | bytes 65568 | tf_op jit(solution)/shard_map/ppermute | solution.py:600
  60.8 1.0 %early.1.acc_ref = f32[128,4096]{1,0:T(8,128)S(1)} custom-call(bf16[4,128,128]{2,1,0:T(8,128)(2,1)S(1)} %get-tuple-element.56.keep, bf16[4,128,128]{2,1,0:T(8,128)(2,1)S(1)} %collective-permute-done.16.came, bf16[2,128,128]{2,1,0:T(8,128)(2,1)S(1)} %collective-permute-done.18.one, bf16[2,128,128]{2,1,0:T(8,128)(2,1)S(1)} %collective-permute-done.19.two, ...), custom_call_target="tpu_custom_call" | custom-call | flops 800000000 | bytes 8000000 | tf_op jit(solution)/shard_map/early/pallas_call | solution.py:577
  61.8 0.7 collective-permute-done.17.three
  62.5 0.5 late.1
  63.0 1.7 %collective-permute-start.20 = (bf16[32,2048]{1,0:T(8,128)(2,1)S(1)}, bf16[32,2048]{1,0:T(8,128)(2,1)S(1)}, u32[]{:S(2)}, u32[]{:S(2)}) collective-permute-start(bf16[32,2048]{1,0:T(8,128)(2,1)S(1)} %get-tuple-element.60), channel_id=1, source_target_pairs={{0,1},{1,2},{2,3},{3,0},{4,5},{5,6},{6,7},{7,4},{8,9},{9,10},{10,1... | collective-permute-start | bytes 393224 | tf_op jit(solution)/shard_map/ppermute | solution.py:644
  64.7 1.7 %collective-permute-start.21 = (bf16[32,2048]{1,0:T(8,128)(2,1)S(1)}, bf16[32,2048]{1,0:T(8,128)(2,1)S(1)}, u32[]{:S(2)}, u32[]{:S(2)}) collective-permute-start(bf16[32,2048]{1,0:T(8,128)(2,1)S(1)} %get-tuple-element.61), channel_id=1, source_target_pairs={{0,3},{1,0},{2,1},{3,2},{4,7},{5,4},{6,5},{7,6},{8,11},{9,8},{10,9... | collective-permute-start | bytes 393224 | tf_op jit(solution)/shard_map/ppermute | solution.py:644
  66.3 1.8 %collective-permute-start.23 = (bf16[32,2048]{1,0:T(8,128)(2,1)S(1)}, bf16[32,2048]{1,0:T(8,128)(2,1)S(1)}, u32[]{:S(2)}, u32[]{:S(2)}) collective-permute-start(bf16[32,2048]{1,0:T(8,128)(2,1)S(1)} %get-tuple-element.63), channel_id=1, source_target_pairs={{0,3},{1,0},{2,1},{3,2},{4,7},{5,4},{6,5},{7,6},{8,11},{9,8},{10,9... | collective-permute-start | bytes 393224 | tf_op jit(solution)/shard_map/ppermute | solution.py:644
  68.1 0.2 collective-permute-start.25
  68.3 0.9 %collective-permute-done.20 = bf16[32,2048]{1,0:T(8,128)(2,1)S(1)} collective-permute-done((bf16[32,2048]{1,0:T(8,128)(2,1)S(1)}, bf16[32,2048]{1,0:T(8,128)(2,1)S(1)}, u32[]{:S(2)}, u32[]{:S(2)}) %collective-permute-start.20) | collective-permute-done | bytes 131104 | tf_op jit(solution)/shard_map/ppermute | solution.py:644
  69.3 0.8 %collective-permute-done.21 = bf16[32,2048]{1,0:T(8,128)(2,1)S(1)} collective-permute-done((bf16[32,2048]{1,0:T(8,128)(2,1)S(1)}, bf16[32,2048]{1,0:T(8,128)(2,1)S(1)}, u32[]{:S(2)}, u32[]{:S(2)}) %collective-permute-start.21) | collective-permute-done | bytes 131104 | tf_op jit(solution)/shard_map/ppermute | solution.py:644
  70.1 1.5 %collective-permute-start.22 = (bf16[32,2048]{1,0:T(8,128)(2,1)S(1)}, bf16[32,2048]{1,0:T(8,128)(2,1)S(1)}, u32[]{:S(2)}, u32[]{:S(2)}) collective-permute-start(bf16[32,2048]{1,0:T(8,128)(2,1)S(1)} %add_convert_fusion.1), channel_id=1, source_target_pairs={{0,1},{1,2},{2,3},{3,0},{4,5},{5,6},{6,7},{7,4},{8,9},{9,10},{10,1... | collective-permute-start | bytes 393224 | tf_op jit(solution)/shard_map/ppermute | solution.py:644
  71.7 1.9 %collective-permute-start.24 = (bf16[32,2048]{1,0:T(8,128)(2,1)S(1)}, bf16[32,2048]{1,0:T(8,128)(2,1)S(1)}, u32[]{:S(2)}, u32[]{:S(2)}) collective-permute-start(bf16[32,2048]{1,0:T(8,128)(2,1)S(1)} %add_convert_fusion), channel_id=1, source_target_pairs={{0,3},{1,0},{2,1},{3,2},{4,7},{5,4},{6,5},{7,6},{8,11},{9,8},{10,9... | collective-permute-start | bytes 393224 | tf_op jit(solution)/shard_map/ppermute | solution.py:644
  73.5 0.0 collective-permute-done.23
  73.5 2.8 %collective-permute-done.22 = bf16[32,2048]{1,0:T(8,128)(2,1)S(1)} collective-permute-done((bf16[32,2048]{1,0:T(8,128)(2,1)S(1)}, bf16[32,2048]{1,0:T(8,128)(2,1)S(1)}, u32[]{:S(2)}, u32[]{:S(2)}) %collective-permute-start.22) | collective-permute-done | bytes 131104 | tf_op jit(solution)/shard_map/ppermute | solution.py:644
  76.4 0.3 collective-permute-done.24
  76.7 0.8 fusion
  (31 shorter events, 0.3 us)
Async XLA Ops:
  1.4 1.5 %collective-permute-start.4 = (bf16[4,144,128]{2,1,0:T(8,128)(2,1)S(1)}, bf16[4,144,128]{2,1,0:T(8,128)(2,1)S(1)}, u32[]{:S(2)}, u32[]{:S(2)}) collective-permute-start(bf16[4,144,128]{2,1,0:T(8,128)(2,1)S(1)} %get-tuple-element.39), channel_id=1, source_target_pairs={{0,4},{4,0},{8,12},{12,8},{16,20},{20,16},{24,28},{28,24},{32,36},... | collective-permute-start | bytes 442376 | tf_op jit(solution)/shard_map/ppermute | solution.py:600
  1.5 6.4 %collective-permute-start = (bf16[4,256,128]{2,1,0:T(8,128)(2,1)S(1)}, bf16[4,256,128]{2,1,0:T(8,128)(2,1)S(1)}, u32[]{:S(2)}, u32[]{:S(2)}) collective-permute-start(bf16[4,256,128]{2,1,0:T(8,128)(2,1)S(1)} %get-tuple-element.37), channel_id=1, source_target_pairs={{0,4},{4,0},{8,12},{12,8},{16,20},{20,16},{24,28},{28,24},{32,36},... | collective-permute-start | bytes 786440 | tf_op jit(solution)/shard_map/ppermute | solution.py:600
  2.9 9.4 %collective-permute-start.5 = (bf16[2,144,128]{2,1,0:T(8,128)(2,1)S(1)}, bf16[2,144,128]{2,1,0:T(8,128)(2,1)S(1)}, u32[]{:S(2)}, u32[]{:S(2)}) collective-permute-start(bf16[2,144,128]{2,1,0:T(8,128)(2,1)S(1)} %pad_maximum_fusion), channel_id=1, source_target_pairs={{0,8},{4,12},{8,0},{12,4},{16,24},{20,28},{24,16},{28,20},{32,40},... | collective-permute-start | bytes 221192 | tf_op jit(solution)/shard_map/ppermute | solution.py:600
  4.4 8.4 %collective-permute-start.6 = (bf16[2,144,128]{2,1,0:T(8,128)(2,1)S(1)}, bf16[2,144,128]{2,1,0:T(8,128)(2,1)S(1)}, u32[]{:S(2)}, u32[]{:S(2)}) collective-permute-start(bf16[2,144,128]{2,1,0:T(8,128)(2,1)S(1)} %pad_maximum_fusion.1), channel_id=1, source_target_pairs={{0,16},{4,20},{8,24},{12,28},{16,0},{20,4},{24,8},{28,12},{32,48},... | collective-permute-start | bytes 221192 | tf_op jit(solution)/shard_map/ppermute | solution.py:600
  7.3 6.4 %collective-permute-start.7 = (bf16[2,144,128]{2,1,0:T(8,128)(2,1)S(1)}, bf16[2,144,128]{2,1,0:T(8,128)(2,1)S(1)}, u32[]{:S(2)}, u32[]{:S(2)}) collective-permute-start(bf16[2,144,128]{2,1,0:T(8,128)(2,1)S(1)} %pad_maximum_fusion.2), channel_id=1, source_target_pairs={{0,24},{4,28},{8,16},{12,20},{16,8},{20,12},{24,0},{28,4},{32,56},... | collective-permute-start | bytes 221192 | tf_op jit(solution)/shard_map/ppermute | solution.py:600
  7.9 8.5 %collective-permute-start.1 = (bf16[2,128,128]{2,1,0:T(8,128)(2,1)S(1)}, bf16[2,128,128]{2,1,0:T(8,128)(2,1)S(1)}, u32[]{:S(2)}, u32[]{:S(2)}) collective-permute-start(bf16[2,128,128]{2,1,0:T(8,128)(2,1)S(1)} %pad_maximum_fusion.3), channel_id=1, source_target_pairs={{0,8},{4,12},{8,0},{12,4},{16,24},{20,28},{24,16},{28,20},{32,40},... | collective-permute-start | bytes 196616 | tf_op jit(solution)/shard_map/ppermute | solution.py:600
  8.2 8.1 %collective-permute-start.2 = (bf16[2,128,128]{2,1,0:T(8,128)(2,1)S(1)}, bf16[2,128,128]{2,1,0:T(8,128)(2,1)S(1)}, u32[]{:S(2)}, u32[]{:S(2)}) collective-permute-start(bf16[2,128,128]{2,1,0:T(8,128)(2,1)S(1)} %pad_maximum_fusion.4), channel_id=1, source_target_pairs={{0,16},{4,20},{8,24},{12,28},{16,0},{20,4},{24,8},{28,12},{32,48},... | collective-permute-start | bytes 196616 | tf_op jit(solution)/shard_map/ppermute | solution.py:600
  12.3 29.1 %copy-start = (f32[128]{0:T(128)S(1)}, f32[128]{0:T(128)}, u32[]{:S(2)}) copy-start(f32[128]{0:T(128)} %param.13) | copy-start | bytes 1540
  12.3 33.6 %copy-start.1 = (bf16[8,128,384]{2,1,0:T(8,128)(2,1)S(1)}, bf16[8,128,384]{2,1,0:T(8,128)(2,1)}, u32[]{:S(2)}) copy-start(bf16[8,128,384]{2,1,0:T(8,128)(2,1)} %weight_ref.5) | copy-start | bytes 2359300
  12.3 5.6 %collective-permute-start.3 = (bf16[2,128,128]{2,1,0:T(8,128)(2,1)S(1)}, bf16[2,128,128]{2,1,0:T(8,128)(2,1)S(1)}, u32[]{:S(2)}, u32[]{:S(2)}) collective-permute-start(bf16[2,128,128]{2,1,0:T(8,128)(2,1)S(1)} %pad_maximum_fusion.5), channel_id=1, source_target_pairs={{0,24},{4,28},{8,16},{12,20},{16,8},{20,12},{24,0},{28,4},{32,56},... | collective-permute-start | bytes 196616 | tf_op jit(solution)/shard_map/ppermute | solution.py:600
  19.0 41.8 %slice-start = ((s8[8388608]{0:T(1024)(128)(4,1)}), s8[4194304]{0:T(1024)(128)(4,1)S(1)}, s32[]{:S(2)}) async-start(s8[8388608]{0:T(1024)(128)(4,1)} %bitcast.1), calls=%async_computation | async-start | bytes 8388608
  19.0 11.6 %collective-permute-start.12 = (bf16[128,256]{1,0:T(8,128)(2,1)S(1)}, bf16[128,256]{1,0:T(8,128)(2,1)S(1)}, u32[]{:S(2)}, u32[]{:S(2)}) collective-permute-start(bf16[128,256]{1,0:T(8,128)(2,1)S(1)} %get-tuple-element.45.own_ref), channel_id=1, source_target_pairs={{0,32},{4,36},{8,40},{12,44},{16,48},{20,52},{24,56},{28,60},{32,6... | collective-permute-start | bytes 196616 | tf_op jit(solution)/shard_map/ppermute | solution.py:617
  22.2 9.0 %collective-permute-start.11 = (bf16[128,256]{1,0:T(8,128)(2,1)S(1)}, bf16[128,256]{1,0:T(8,128)(2,1)S(1)}, u32[]{:S(2)}, u32[]{:S(2)}) collective-permute-start(bf16[128,256]{1,0:T(8,128)(2,1)S(1)} %get-tuple-element.45.own_ref), channel_id=1, source_target_pairs={{0,64},{4,68},{8,72},{12,76},{16,80},{20,84},{24,88},{28,92},{32,9... | collective-permute-start | bytes 196616 | tf_op jit(solution)/shard_map/ppermute | solution.py:617
  25.6 8.5 %collective-permute-start.8 = (bf16[2,128,128]{2,1,0:T(8,128)(2,1)S(1)}, bf16[2,128,128]{2,1,0:T(8,128)(2,1)S(1)}, u32[]{:S(2)}, u32[]{:S(2)}) collective-permute-start(bf16[2,128,128]{2,1,0:T(8,128)(2,1)S(1)} %pad_maximum_fusion.6), channel_id=1, source_target_pairs={{0,8},{4,12},{8,0},{12,4},{16,24},{20,28},{24,16},{28,20},{32,40},... | collective-permute-start | bytes 196616 | tf_op jit(solution)/shard_map/ppermute | solution.py:600
  25.8 8.4 %collective-permute-start.9 = (bf16[2,128,128]{2,1,0:T(8,128)(2,1)S(1)}, bf16[2,128,128]{2,1,0:T(8,128)(2,1)S(1)}, u32[]{:S(2)}, u32[]{:S(2)}) collective-permute-start(bf16[2,128,128]{2,1,0:T(8,128)(2,1)S(1)} %pad_maximum_fusion.7), channel_id=1, source_target_pairs={{0,16},{4,20},{8,24},{12,28},{16,0},{20,4},{24,8},{28,12},{32,48},... | collective-permute-start | bytes 196616 | tf_op jit(solution)/shard_map/ppermute | solution.py:600
  27.8 6.3 %collective-permute-start.10 = (bf16[2,128,128]{2,1,0:T(8,128)(2,1)S(1)}, bf16[2,128,128]{2,1,0:T(8,128)(2,1)S(1)}, u32[]{:S(2)}, u32[]{:S(2)}) collective-permute-start(bf16[2,128,128]{2,1,0:T(8,128)(2,1)S(1)} %pad_maximum_fusion.8), channel_id=1, source_target_pairs={{0,24},{4,28},{8,16},{12,20},{16,8},{20,12},{24,0},{28,4},{32,56},... | collective-permute-start | bytes 196616 | tf_op jit(solution)/shard_map/ppermute | solution.py:600
  31.5 9.9 %collective-permute-start.14 = (bf16[128,256]{1,0:T(8,128)(2,1)S(1)}, bf16[128,256]{1,0:T(8,128)(2,1)S(1)}, u32[]{:S(2)}, u32[]{:S(2)}) collective-permute-start(bf16[128,256]{1,0:T(8,128)(2,1)S(1)} %get-tuple-element.52), channel_id=1, source_target_pairs={{0,96},{4,100},{8,104},{12,108},{16,112},{20,116},{24,120},{28,124... | collective-permute-start | bytes 196616 | tf_op jit(solution)/shard_map/ppermute | solution.py:617
  33.4 7.9 %collective-permute-start.13 = (bf16[128,256]{1,0:T(8,128)(2,1)S(1)}, bf16[128,256]{1,0:T(8,128)(2,1)S(1)}, u32[]{:S(2)}, u32[]{:S(2)}) collective-permute-start(bf16[128,256]{1,0:T(8,128)(2,1)S(1)} %get-tuple-element.52), channel_id=1, source_target_pairs={{0,192},{4,196},{8,200},{12,204},{16,208},{20,212},{24,216},{28,22... | collective-permute-start | bytes 196616 | tf_op jit(solution)/shard_map/ppermute | solution.py:617
  42.1 18.7 %slice-start.1 = ((s8[8388608]{0:T(1024)(128)(4,1)}), s8[4194304]{0:T(1024)(128)(4,1)S(1)}, s32[]{:S(2)}) async-start(s8[8388608]{0:T(1024)(128)(4,1)} %bitcast.1), calls=%async_computation.1 | async-start | bytes 8388608
  42.1 9.7 %collective-permute-start.15 = (bf16[1024,128]{1,0:T(8,128)(2,1)S(1)}, bf16[1024,128]{1,0:T(8,128)(2,1)S(1)}, u32[]{:S(2)}, u32[]{:S(2)}) collective-permute-start(bf16[1024,128]{1,0:T(8,128)(2,1)S(1)} %norm.1.normed_ref), channel_id=1, source_target_pairs={{0,32},{4,36},{8,40},{12,44},{16,48},{20,52},{24,56},{28,60},{32,6... | collective-permute-start | bytes 786440 | tf_op jit(solution)/shard_map/ppermute | solution.py:617
  53.4 1.4 %collective-permute-start.16 = (bf16[4,128,128]{2,1,0:T(8,128)(2,1)S(1)}, bf16[4,128,128]{2,1,0:T(8,128)(2,1)S(1)}, u32[]{:S(2)}, u32[]{:S(2)}) collective-permute-start(bf16[4,128,128]{2,1,0:T(8,128)(2,1)S(1)} %get-tuple-element.57), channel_id=1, source_target_pairs={{0,4},{4,0},{8,12},{12,8},{16,20},{20,16},{24,28},{28,24},{32,36},... | collective-permute-start | bytes 393224 | tf_op jit(solution)/shard_map/ppermute | solution.py:600
  54.8 5.0 %collective-permute-start.18 = (bf16[2,128,128]{2,1,0:T(8,128)(2,1)S(1)}, bf16[2,128,128]{2,1,0:T(8,128)(2,1)S(1)}, u32[]{:S(2)}, u32[]{:S(2)}) collective-permute-start(bf16[2,128,128]{2,1,0:T(8,128)(2,1)S(1)} %pad_maximum_fusion.10), channel_id=1, source_target_pairs={{0,8},{4,12},{8,0},{12,4},{16,24},{20,28},{24,16},{28,20},{32,40},... | collective-permute-start | bytes 196616 | tf_op jit(solution)/shard_map/ppermute | solution.py:600
  54.9 5.9 %collective-permute-start.19 = (bf16[2,128,128]{2,1,0:T(8,128)(2,1)S(1)}, bf16[2,128,128]{2,1,0:T(8,128)(2,1)S(1)}, u32[]{:S(2)}, u32[]{:S(2)}) collective-permute-start(bf16[2,128,128]{2,1,0:T(8,128)(2,1)S(1)} %pad_maximum_fusion.11), channel_id=1, source_target_pairs={{0,16},{4,20},{8,24},{12,28},{16,0},{20,4},{24,8},{28,12},{32,48},... | collective-permute-start | bytes 196616 | tf_op jit(solution)/shard_map/ppermute | solution.py:600
  57.0 5.6 %collective-permute-start.17 = (bf16[2,128,128]{2,1,0:T(8,128)(2,1)S(1)}, bf16[2,128,128]{2,1,0:T(8,128)(2,1)S(1)}, u32[]{:S(2)}, u32[]{:S(2)}) collective-permute-start(bf16[2,128,128]{2,1,0:T(8,128)(2,1)S(1)} %pad_maximum_fusion.9), channel_id=1, source_target_pairs={{0,24},{4,28},{8,16},{12,20},{16,8},{20,12},{24,0},{28,4},{32,56},... | collective-permute-start | bytes 196616 | tf_op jit(solution)/shard_map/ppermute | solution.py:600
  63.0 6.3 %collective-permute-start.20 = (bf16[32,2048]{1,0:T(8,128)(2,1)S(1)}, bf16[32,2048]{1,0:T(8,128)(2,1)S(1)}, u32[]{:S(2)}, u32[]{:S(2)}) collective-permute-start(bf16[32,2048]{1,0:T(8,128)(2,1)S(1)} %get-tuple-element.60), channel_id=1, source_target_pairs={{0,1},{1,2},{2,3},{3,0},{4,5},{5,6},{6,7},{7,4},{8,9},{9,10},{10,1... | collective-permute-start | bytes 393224 | tf_op jit(solution)/shard_map/ppermute | solution.py:644
  64.7 5.4 %collective-permute-start.21 = (bf16[32,2048]{1,0:T(8,128)(2,1)S(1)}, bf16[32,2048]{1,0:T(8,128)(2,1)S(1)}, u32[]{:S(2)}, u32[]{:S(2)}) collective-permute-start(bf16[32,2048]{1,0:T(8,128)(2,1)S(1)} %get-tuple-element.61), channel_id=1, source_target_pairs={{0,3},{1,0},{2,1},{3,2},{4,7},{5,4},{6,5},{7,6},{8,11},{9,8},{10,9... | collective-permute-start | bytes 393224 | tf_op jit(solution)/shard_map/ppermute | solution.py:644
  66.3 7.2 %collective-permute-start.23 = (bf16[32,2048]{1,0:T(8,128)(2,1)S(1)}, bf16[32,2048]{1,0:T(8,128)(2,1)S(1)}, u32[]{:S(2)}, u32[]{:S(2)}) collective-permute-start(bf16[32,2048]{1,0:T(8,128)(2,1)S(1)} %get-tuple-element.63), channel_id=1, source_target_pairs={{0,3},{1,0},{2,1},{3,2},{4,7},{5,4},{6,5},{7,6},{8,11},{9,8},{10,9... | collective-permute-start | bytes 393224 | tf_op jit(solution)/shard_map/ppermute | solution.py:644
  68.1 8.3 %collective-permute-start.25 = (bf16[32,2048]{1,0:T(8,128)(2,1)S(1)}, bf16[32,2048]{1,0:T(8,128)(2,1)S(1)}, u32[]{:S(2)}, u32[]{:S(2)}) collective-permute-start(bf16[32,2048]{1,0:T(8,128)(2,1)S(1)} %get-tuple-element.66), channel_id=1, source_target_pairs={{0,1},{1,2},{2,3},{3,0},{4,5},{5,6},{6,7},{7,4},{8,9},{9,10},{10,1... | collective-permute-start | bytes 393224 | tf_op jit(solution)/shard_map/ppermute | solution.py:644
  70.1 6.3 %collective-permute-start.22 = (bf16[32,2048]{1,0:T(8,128)(2,1)S(1)}, bf16[32,2048]{1,0:T(8,128)(2,1)S(1)}, u32[]{:S(2)}, u32[]{:S(2)}) collective-permute-start(bf16[32,2048]{1,0:T(8,128)(2,1)S(1)} %add_convert_fusion.1), channel_id=1, source_target_pairs={{0,1},{1,2},{2,3},{3,0},{4,5},{5,6},{6,7},{7,4},{8,9},{9,10},{10,1... | collective-permute-start | bytes 393224 | tf_op jit(solution)/shard_map/ppermute | solution.py:644
  71.7 5.0 %collective-permute-start.24 = (bf16[32,2048]{1,0:T(8,128)(2,1)S(1)}, bf16[32,2048]{1,0:T(8,128)(2,1)S(1)}, u32[]{:S(2)}, u32[]{:S(2)}) collective-permute-start(bf16[32,2048]{1,0:T(8,128)(2,1)S(1)} %add_convert_fusion), channel_id=1, source_target_pairs={{0,3},{1,0},{2,1},{3,2},{4,7},{5,4},{6,5},{7,6},{8,11},{9,8},{10,9... | collective-permute-start | bytes 393224 | tf_op jit(solution)/shard_map/ppermute | solution.py:644

commit v15 on v12

--- a/solution.py
+++ b/solution.py
@@ -12,6 +12,7 @@
 PLANES = 8
 KROWS = C + 16
 B = 16
+HALF = 512
 EPS = 1e-06
 NEG = -1e30
 VMEM_LIMIT = 24 * 1024 * 1024
@@ -380,20 +381,22 @@
     )(own_map, one, two)
 
 
-def norm_kernel(no_ref, gain_ref, before_ref, six_ref, three_ref, normed_ref):
+def norm_kernel(no_ref, gain_ref, before_ref, six_ref, three_ref, far_ref, near_ref):
     state = three_ref[:, C:].astype(F32) + dot(three_ref[:, :C], six_ref[:, C:])
     state = before_ref[:, C:] + mm(before_ref[:, :C], state)
     out = mm(no_ref[:, :C], state) + no_ref[:, C:]
     scale = lax.rsqrt(jnp.mean(out * out, axis=1, keepdims=True) + EPS)
-    normed_ref[...] = (out * scale * gain_ref[...]).astype(BF16)
+    normed = (out * scale * gain_ref[...]).astype(BF16)
+    far_ref[...] = normed[:HALF]
+    near_ref[...] = normed[HALF:]
 
 
 def norm(no, gain, before, six, three):
     return pl.pallas_call(
         norm_kernel,
-        out_shape=jax.ShapeDtypeStruct((PLANE * C, C), BF16),
+        out_shape=[jax.ShapeDtypeStruct((HALF, C), BF16)] * 2,
         in_specs=[vmem()] * 5,
-        out_specs=vmem(),
+        out_specs=[vmem()] * 2,
         compiler_params=params(),
         cost_estimate=cost(2e8, 2e6),
         name="norm",
@@ -435,9 +438,10 @@
     return jnp.concatenate([column] * (like.shape[1] // C), axis=1)
 
 
-def own_kernel(normed_ref, weight_ref, acc_ref, stat_ref, q2_ref):
+def own_kernel(far_ref, near_ref, weight_ref, acc_ref, stat_ref, q2_ref):
     me = lax.axis_index("seq") % PLANE
-    proj = dot(normed_ref[...], weight_ref[me]).astype(BF16)
+    normed = jnp.concatenate([far_ref[...], near_ref[...]], axis=0)
+    proj = dot(normed, weight_ref[me]).astype(BF16)
     q2_ref[...] = proj[:, :C]
     row, col = squares()
     starts = range(0, PLANE * C, QB)
@@ -456,7 +460,7 @@
         stat_ref[1, rows, :] = jnp.broadcast_to(row_sum(raised[i]), (QB, C))
 
 
-def own(normed, weight):
+def own(far, near, weight):
     n = PLANE * C
     return pl.pallas_call(
         own_kernel,
@@ -465,61 +469,97 @@
             jax.ShapeDtypeStruct((2, n, C), F32),
             jax.ShapeDtypeStruct((n, C), BF16),
         ],
-        in_specs=[vmem()] * 2,
+        in_specs=[vmem()] * 3,
         out_specs=[vmem()] * 3,
         compiler_params=params(),
         cost_estimate=cost(1e9, 3e6, 6e5),
         name="own",
-    )(normed, weight)
-
-
-def halo_kernel(halo_ref, weight_ref, acc_ref, stat_ref, q2_ref, *refs):
-    keep, send, attended = refs
+    )(far, near, weight)
+
+
+def add_halo(halo_ref, weight_ref, acc_ref, stat_ref, q2_ref, spans):
     place = lax.axis_index("seq")
     me, plane = place % PLANE, place // PLANE
     proj = dot(halo_ref[...], weight_ref[me, :, C:]).astype(BF16)
-    n = PLANE * C
     row, col = squares()
-    starts = range(0, n, QB)
-    spans = [[(at, at + QB)] + ([(at + QB, n)] if at + QB < n else []) for at in starts]
     floor = jnp.where(plane > 0, 0.0, NEG)
-    scores = [
-        [dot_nt(q2_ref[at : at + QB, :], proj[a:b, :C]) for a, b in span]
-        for at, span in zip(starts, spans)
-    ]
-    scores = [[jnp.where(col > row, parts[0], NEG)] + parts[1:] for parts in scores]
-    before = [stat_ref[0, at : at + QB, :] for at in starts]
+    scores = []
+    for at, masked, span in spans:
+        parts = [dot_nt(q2_ref[at : at + QB, :], proj[a:b, :C]) for a, b in span]
+        scores.append([jnp.where(col > row, parts[0], NEG)] + parts[1:] if masked else parts)
+    before = [stat_ref[0, at : at + QB, :] for at, _, _ in spans]
     tops = [jnp.maximum(row_max(parts) + floor, old) for parts, old in zip(scores, before)]
     raised = [
         [jnp.exp2((s - tiled(top - floor, s)) * SCALE) for s in parts]
         for parts, top in zip(scores, tops)
     ]
     fades = [jnp.exp2((old - top) * SCALE) for old, top in zip(before, tops)]
-    for i, at in enumerate(starts):
+    found = []
+    for i, (at, _, span) in enumerate(spans):
         rows = slice(at, at + QB)
         total = row_sum(raised[i]) + fades[i] * stat_ref[1, rows, :]
         acc = acc_ref[rows, :] * fades[i] + weighted(
-            raised[i], [proj[a:b, C:] for a, b in spans[i]]
+            raised[i], [proj[a:b, C:] for a, b in span]
         )
-        attended[rows, :] = (acc / total).astype(BF16)
+        found.append((tops[i], total, acc))
+    return found
+
+
+def near_kernel(halo_ref, weight_ref, acc_ref, stat_ref, q2_ref, new_acc, new_stat, done_ref):
+    whole = [(0, HALF)]
+    spans = [(0, False, whole), (QB, False, whole)]
+    spans += [(2 * QB, True, [(0, QB), (QB, HALF)]), (3 * QB, True, [(QB, HALF)])]
+    found = add_halo(halo_ref, weight_ref, acc_ref, stat_ref, q2_ref, spans)
+    for i, (top, total, acc) in enumerate(found):
+        if i < 2:
+            rows = slice(i * QB, i * QB + QB)
+            new_acc[rows, :] = acc
+            new_stat[0, rows, :] = top
+            new_stat[1, rows, :] = total
+        else:
+            done_ref[i * QB - HALF : i * QB - HALF + QB, :] = (acc / total).astype(BF16)
+
+
+def far_kernel(halo_ref, weight_ref, acc_ref, stat_ref, q2_ref, done_ref, keep, send, attended):
+    me = lax.axis_index("seq") % PLANE
+    spans = [(0, True, [(0, QB), (QB, HALF)]), (QB, True, [(QB, HALF)])]
+    found = add_halo(halo_ref, weight_ref, acc_ref, stat_ref, q2_ref, spans)
+    for i, (_, total, acc) in enumerate(found):
+        attended[i * QB : i * QB + QB, :] = (acc / total).astype(BF16)
+    attended[HALF:, :] = done_ref[...]
     for d in range(PLANE):
         chunk = jnp.bitwise_xor(me, d)
         out = send if d % 2 else keep
         out[d // 2] = attended[pl.ds(pl.multiple_of(chunk * C, C), C), :]
 
 
-def halo_part(halo, weight, acc, stat, q2):
-    n = PLANE * C
-    return pl.pallas_call(
-        halo_kernel,
+def near_part(halo, weight, acc, stat, q2):
+    return pl.pallas_call(
+        near_kernel,
+        out_shape=[
+            jax.ShapeDtypeStruct((HALF, C), F32),
+            jax.ShapeDtypeStruct((2, HALF, C), F32),
+            jax.ShapeDtypeStruct((HALF, C), BF16),
+        ],
+        in_specs=[vmem()] * 5,
+        out_specs=[vmem()] * 3,
+        compiler_params=params(),
+        cost_estimate=cost(8e8, 2e6, 4e5),
+        name="near",
+    )(halo, weight, acc, stat, q2)
+
+
+def far_part(halo, weight, acc, stat, q2, done):
+    return pl.pallas_call(
+        far_kernel,
         out_shape=[jax.ShapeDtypeStruct((4, C, C), BF16)] * 2,
-        in_specs=[vmem()] * 5,
+        in_specs=[vmem()] * 6,
         out_specs=[vmem()] * 2,
-        scratch_shapes=[pltpu.VMEM((n, C), BF16)],
-        compiler_params=params(),
-        cost_estimate=cost(1e9, 3e6, 6e5),
-        name="halo",
-    )(halo, weight, acc, stat, q2)
+        scratch_shapes=[pltpu.VMEM((PLANE * C, C), BF16)],
+        compiler_params=params(),
+        cost_estimate=cost(3e8, 2e6, 2e5),
+        name="far",
+    )(halo, weight, acc, stat, q2, done)
 
 
 COLS = 1024
@@ -632,10 +672,12 @@
     before, upto = combine(ab, one, two)
     six = later_plane(upto, 6)
     three = later_plane(upto, 3)
-    normed = norm(no, gain[None, :], before, six, three)
-    halo = later_plane(normed, 1)
-    acc, stat, q2 = own(normed, attn_weight)
-    attended = exchange(*halo_part(halo, attn_weight, acc, stat, q2))
+    far, near = norm(no, gain[None, :], before, six, three)
+    near_halo = later_plane(near, 1)
+    far_halo = later_plane(far, 1)
+    acc, stat, q2 = own(far, near, attn_weight)
+    acc, stat, done = near_part(near_halo, attn_weight, acc, stat, q2)
+    attended = exchange(*far_part(far_halo, attn_weight, acc, stat, q2, done))
     return sum_over_heads(*project(attended, out_weight))
 
 

time: 77.3 us -> 79.1 us (1.023)
  the two profiles are of different devices: /device:TPU:128 before, /device:TPU:96 now
where the time goes in v15:
time: 79.1 us; the launch traced here: 78.8 us
  starting transfers between devices  47.7 us (60%)
  waiting for transfers between devices  17.4 us (22%)
  Pallas kernels  12.3 us (16%)
  other arithmetic  0.96 us (1%)
    ppermute x15, starting transfers between devices, swap(): lax.ppermute(block, 'seq', [(s, s ^ d) for s in range(PLANE * PLANES)])  20.5 us
    ppermute x6, starting transfers between devices, later_plane(): return lax.ppermute(block, 'seq', route)  18.5 us
    ppermute x6, starting transfers between devices, turn(): return lax.ppermute(block, 'heads', [(s, (s + step) % 4) for s in range(4)])  8.73 us
    ppermute x6, waiting for transfers between devices, later_plane(): return lax.ppermute(block, 'seq', route)  6.38 us
    ppermute x15, waiting for transfers between devices, swap(): lax.ppermute(block, 'seq', [(s, s ^ d) for s in range(PLANE * PLANES)])  6.02 us
    ppermute x6, waiting for transfers between devices, turn(): return lax.ppermute(block, 'heads', [(s, (s + step) % 4) for s in range(4)])  5.03 us
    pallas_call x1, Pallas kernels, key_part(): pl.pallas_call(key_kernel, out_shape=[jax.ShapeDtypeStruct((PLANE, KROWS,...  2.71 us
  transfers between devices with their start and end apart: 27, of which 12 were waited for; matrix products, arithmetic and copies ran while one was open for 0% of the time, Pallas kernels for 10%

profile of v15, /device:TPU:96, one launch (start us, length us, event | category | flops | bytes accessed | tf_op | source)
XLA Modules:
  0.0 78.8 jit_solution(12367201819136437964)
XLA Ops:
  0.0 1.4 %pack.1 = (bf16[4,144,128]{2,1,0:T(8,128)(2,1)S(1)}, bf16[4,144,128]{2,1,0:T(8,128)(2,1)S(1)}, bf16[4,256,128]{2,1,0:T(8,128)(2,1)S(1)}, bf16[4,256,128]{2,1,0:T(8,128)(2,1)S(1)}) custom-call(bf16[128,1024]{1,0:T(8,128)(2,1)} %q_ref.1, bf16[128,1024]{1,0:T(8,128)(2,1)} %k_ref.1, bf16[128,1024]{1,0:T(8,128)(2,1)} %v_ref.1, f32[8,128]{1,0:T(8,128)} %decay_ref.1, ...), custom_call_target="tpu_custom_call" | custom-call | tf_op jit(solution)/shard_map/pack/pallas_call | solution.py:114
  1.4 0.1 collective-permute-start.4
  1.5 0.5 collective-permute-start
  2.0 0.8 %collective-permute-done.4.refs_1_ = bf16[4,144,128]{2,1,0:T(8,128)(2,1)S(1)} collective-permute-done((bf16[4,144,128]{2,1,0:T(8,128)(2,1)S(1)}, bf16[4,144,128]{2,1,0:T(8,128)(2,1)S(1)}, u32[]{:S(2)}, u32[]{:S(2)}) %collective-permute-start.4) | collective-permute-done | bytes 147488 | tf_op jit(solution)/shard_map/ppermute | solution.py:640
  2.9 1.6 %collective-permute-start.5 = (bf16[2,144,128]{2,1,0:T(8,128)(2,1)S(1)}, bf16[2,144,128]{2,1,0:T(8,128)(2,1)S(1)}, u32[]{:S(2)}, u32[]{:S(2)}) collective-permute-start(bf16[2,144,128]{2,1,0:T(8,128)(2,1)S(1)} %pad_maximum_fusion), channel_id=1, source_target_pairs={{0,8},{4,12},{8,0},{12,4},{16,24},{20,28},{24,16},{28,20},{32,40},... | collective-permute-start | bytes 221192 | tf_op jit(solution)/shard_map/ppermute | solution.py:640
  4.4 2.8 %collective-permute-start.6 = (bf16[2,144,128]{2,1,0:T(8,128)(2,1)S(1)}, bf16[2,144,128]{2,1,0:T(8,128)(2,1)S(1)}, u32[]{:S(2)}, u32[]{:S(2)}) collective-permute-start(bf16[2,144,128]{2,1,0:T(8,128)(2,1)S(1)} %pad_maximum_fusion.1), channel_id=1, source_target_pairs={{0,16},{4,20},{8,24},{12,28},{16,0},{20,4},{24,8},{28,12},{32,48},... | collective-permute-start | bytes 221192 | tf_op jit(solution)/shard_map/ppermute | solution.py:640
  7.3 0.6 collective-permute-start.7
  7.8 0.0 collective-permute-done.refs_1_
  7.9 0.4 collective-permute-start.1
  8.2 4.0 %collective-permute-start.2 = (bf16[2,128,128]{2,1,0:T(8,128)(2,1)S(1)}, bf16[2,128,128]{2,1,0:T(8,128)(2,1)S(1)}, u32[]{:S(2)}, u32[]{:S(2)}) collective-permute-start(bf16[2,128,128]{2,1,0:T(8,128)(2,1)S(1)} %pad_maximum_fusion.4), channel_id=1, source_target_pairs={{0,16},{4,20},{8,24},{12,28},{16,0},{20,4},{24,8},{28,12},{32,48},... | collective-permute-start | bytes 196616 | tf_op jit(solution)/shard_map/ppermute | solution.py:640
  12.3 0.0 copy-start
  12.3 0.6 collective-permute-start.3
  12.9 0.0 collective-permute-done.6.refs_3_
  12.9 0.8 collective-permute-done.7.refs_4_
  13.6 2.7 %keys.1 = (bf16[8,144,128]{2,1,0:T(8,128)(2,1)S(1)}, f32[8,128,128]{2,1,0:T(8,128)S(1)}, f32[8,128,128]{2,1,0:T(8,128)S(1)}, f32[8,128,128]{2,1,0:T(8,128)S(1)},...) custom-call(bf16[4,144,128]{2,1,0:T(8,128)(2,1)S(1)} %get-tuple-element.43.refs_0_, ...), custom_call_target="tpu_custom_call" | custom-call | flops 2000000000 | bytes 4000000 | tf_op jit(solution)/shard_map/keys/pallas_call | solution.py:272
  16.3 0.0 collective-permute-done.1.refs_2_
  16.4 0.0 collective-permute-done.2.refs_3_
  16.4 1.5 %collective-permute-done.3.refs_4_ = bf16[2,128,128]{2,1,0:T(8,128)(2,1)S(1)} collective-permute-done((bf16[2,128,128]{2,1,0:T(8,128)(2,1)S(1)}, bf16[2,128,128]{2,1,0:T(8,128)(2,1)S(1)}, u32[]{:S(2)}, u32[]{:S(2)}) %collective-permute-start.3) | collective-permute-done | bytes 65568 | tf_op jit(solution)/shard_map/ppermute | solution.py:640
  17.9 1.1 %values.1 = (f32[8,128,256]{2,1,0:T(8,128)S(1)}, bf16[128,256]{1,0:T(8,128)(2,1)S(1)}, f32[7,128,256]{2,1,0:T(8,128)S(1)}) custom-call(bf16[4,256,128]{2,1,0:T(8,128)(2,1)S(1)} %get-tuple-element.51.refs_0_, bf16[4,256,128]{2,1,0:T(8,128)(2,1)S(1)} %collective-permute-done.refs_1_, bf16[2,128,128]{2,1,0:T(8,128)(2,1)S(1)} %collective-permute-done.1.refs_2_, ...), custom_call_target="tpu_custom_call" | custom-call | flops 1000000000 | bytes 4000000 | tf_op jit(solution)/shard_map/values/pallas_call | solution.py:285
  19.0 0.0 slice-start
  19.0 5.8 %collective-permute-start.12 = (bf16[128,256]{1,0:T(8,128)(2,1)S(1)}, bf16[128,256]{1,0:T(8,128)(2,1)S(1)}, u32[]{:S(2)}, u32[]{:S(2)}) collective-permute-start(bf16[128,256]{1,0:T(8,128)(2,1)S(1)} %get-tuple-element.50.own_ref), channel_id=1, source_target_pairs={{0,64},{4,68},{8,72},{12,76},{16,80},{20,84},{24,88},{28,92},{32,9... | collective-permute-start | bytes 196616 | tf_op jit(solution)/shard_map/ppermute | solution.py:657
  24.8 2.9 %collective-permute-start.11 = (bf16[128,256]{1,0:T(8,128)(2,1)S(1)}, bf16[128,256]{1,0:T(8,128)(2,1)S(1)}, u32[]{:S(2)}, u32[]{:S(2)}) collective-permute-start(bf16[128,256]{1,0:T(8,128)(2,1)S(1)} %get-tuple-element.50.own_ref), channel_id=1, source_target_pairs={{0,32},{4,36},{8,40},{12,44},{16,48},{20,52},{24,56},{28,60},{32,6... | collective-permute-start | bytes 196616 | tf_op jit(solution)/shard_map/ppermute | solution.py:657
  27.8 0.1 collective-permute-start.8
  27.9 2.0 %collective-permute-start.9 = (bf16[2,128,128]{2,1,0:T(8,128)(2,1)S(1)}, bf16[2,128,128]{2,1,0:T(8,128)(2,1)S(1)}, u32[]{:S(2)}, u32[]{:S(2)}) collective-permute-start(bf16[2,128,128]{2,1,0:T(8,128)(2,1)S(1)} %pad_maximum_fusion.7), channel_id=1, source_target_pairs={{0,16},{4,20},{8,24},{12,28},{16,0},{20,4},{24,8},{28,12},{32,48},... | collective-permute-start | bytes 196616 | tf_op jit(solution)/shard_map/ppermute | solution.py:640
  29.9 2.8 %collective-permute-start.10 = (bf16[2,128,128]{2,1,0:T(8,128)(2,1)S(1)}, bf16[2,128,128]{2,1,0:T(8,128)(2,1)S(1)}, u32[]{:S(2)}, u32[]{:S(2)}) collective-permute-start(bf16[2,128,128]{2,1,0:T(8,128)(2,1)S(1)} %pad_maximum_fusion.8), channel_id=1, source_target_pairs={{0,24},{4,28},{8,16},{12,20},{16,8},{20,12},{24,0},{28,4},{32,56},... | collective-permute-start | bytes 196616 | tf_op jit(solution)/shard_map/ppermute | solution.py:640
  32.7 0.0 collective-permute-done.12.two_ref
  32.7 0.0 collective-permute-done.11.one_ref
  32.7 0.3 combine.1
  33.1 1.9 %collective-permute-start.14 = (bf16[128,256]{1,0:T(8,128)(2,1)S(1)}, bf16[128,256]{1,0:T(8,128)(2,1)S(1)}, u32[]{:S(2)}, u32[]{:S(2)}) collective-permute-start(bf16[128,256]{1,0:T(8,128)(2,1)S(1)} %get-tuple-element.57), channel_id=1, source_target_pairs={{0,96},{4,100},{8,104},{12,108},{16,112},{20,116},{24,120},{28,124... | collective-permute-start | bytes 196616 | tf_op jit(solution)/shard_map/ppermute | solution.py:657
  35.0 0.7 collective-permute-start.13
  35.7 0.0 collective-permute-done.9.refs_3_
  35.7 0.0 collective-permute-done.10.refs_4_
  35.7 1.3 %query.1.no_ref = f32[1024,256]{1,0:T(8,128)S(1)} custom-call(bf16[4,256,128]{2,1,0:T(8,128)(2,1)S(1)} %get-tuple-element.51.refs_0_, bf16[4,256,128]{2,1,0:T(8,128)(2,1)S(1)} %collective-permute-done.refs_1_, bf16[2,128,128]{2,1,0:T(8,128)(2,1)S(1)} %collective-permute-done.8.refs_2_, bf16[2,128,128]{2,1,0:T(8,128)(2,1)S(1)} %collective-permute-done.9.refs_3_, ...), custom_call_target="tpu_custom_call" | custom-call | flops 1000000000 | bytes 4000000 | tf_op jit(solution)/shard_map/query/pallas_call | solution.py:340
  37.0 4.1 %collective-permute-done.14.three_ref = bf16[128,256]{1,0:T(8,128)(2,1)S(1)} collective-permute-done((bf16[128,256]{1,0:T(8,128)(2,1)S(1)}, bf16[128,256]{1,0:T(8,128)(2,1)S(1)}, u32[]{:S(2)}, u32[]{:S(2)}) %collective-permute-start.14) | collective-permute-done | bytes 65568 | tf_op jit(solution)/shard_map/ppermute | solution.py:657
  41.1 0.7 norm.1
  41.8 4.9 %collective-permute-start.16 = (bf16[512,128]{1,0:T(8,128)(2,1)S(1)}, bf16[512,128]{1,0:T(8,128)(2,1)S(1)}, u32[]{:S(2)}, u32[]{:S(2)}) collective-permute-start(bf16[512,128]{1,0:T(8,128)(2,1)S(1)} %get-tuple-element.59.near_ref), channel_id=1, source_target_pairs={{0,32},{4,36},{8,40},{12,44},{16,48},{20,52},{24,56},{28,60},{32,6... | collective-permute-start | bytes 393224 | tf_op jit(solution)/shard_map/ppermute | solution.py:657
  46.7 0.0 slice-start.1
  46.8 2.4 %collective-permute-start.15 = (bf16[512,128]{1,0:T(8,128)(2,1)S(1)}, bf16[512,128]{1,0:T(8,128)(2,1)S(1)}, u32[]{:S(2)}, u32[]{:S(2)}) collective-permute-start(bf16[512,128]{1,0:T(8,128)(2,1)S(1)} %get-tuple-element.58.far_ref), channel_id=1, source_target_pairs={{0,32},{4,36},{8,40},{12,44},{16,48},{20,52},{24,56},{28,60},{32,6... | collective-permute-start | bytes 393224 | tf_op jit(solution)/shard_map/ppermute | solution.py:657
  49.1 1.3 %own.1 = (f32[1024,128]{1,0:T(8,128)S(1)}, f32[2,1024,128]{2,1,0:T(8,128)S(1)}, bf16[1024,128]{1,0:T(8,128)(2,1)S(1)}) custom-call(bf16[512,128]{1,0:T(8,128)(2,1)S(1)} %get-tuple-element.58.far_ref, bf16[512,128]{1,0:T(8,128)(2,1)S(1)} %get-tuple-element.59.near_ref, bf16[8,128,384]{2,1,0:T(8,128)(2,1)S(1)} %copy-done), custom_call_target="tpu_custom_call" | custom-call | flops 1000000000 | bytes 3000000 | tf_op jit(solution)/shard_map/own/pallas_call | solution.py:465
  50.4 1.2 %near.1 = (f32[512,128]{1,0:T(8,128)S(1)}, f32[2,512,128]{2,1,0:T(8,128)S(1)}, bf16[512,128]{1,0:T(8,128)(2,1)S(1)}) custom-call(bf16[512,128]{1,0:T(8,128)(2,1)S(1)} %collective-permute-done.16.halo_ref, bf16[8,128,384]{2,1,0:T(8,128)(2,1)S(1)} %copy-done, f32[1024,128]{1,0:T(8,128)S(1)} %get-tuple-element.60.acc_ref, ...), custom_call_target="tpu_custom_call" | custom-call | flops 800000000 | bytes 2000000 | tf_op jit(solution)/shard_map/near/pallas_call | solution.py:537
  51.6 2.3 %collective-permute-done.15.halo_ref = bf16[512,128]{1,0:T(8,128)(2,1)S(1)} collective-permute-done((bf16[512,128]{1,0:T(8,128)(2,1)S(1)}, bf16[512,128]{1,0:T(8,128)(2,1)S(1)}, u32[]{:S(2)}, u32[]{:S(2)}) %collective-permute-start.15) | collective-permute-done | bytes 131104 | tf_op jit(solution)/shard_map/ppermute | solution.py:657
  53.9 0.8 %far.1 = (bf16[4,128,128]{2,1,0:T(8,128)(2,1)S(1)}, bf16[4,128,128]{2,1,0:T(8,128)(2,1)S(1)}) custom-call(bf16[512,128]{1,0:T(8,128)(2,1)S(1)} %collective-permute-done.15.halo_ref, bf16[8,128,384]{2,1,0:T(8,128)(2,1)S(1)} %copy-done, f32[512,128]{1,0:T(8,128)S(1)} %get-tuple-element.63.acc_ref, f32[2,512,128]{2,1,0:T(8,128)S(1)} %get-tuple-element.64.stat_ref, ...), custom_call_target="tpu_custom_call" | custom-call | flops 300000000 | bytes 2000000 | tf_op jit(solution)/shard_map/far/pallas_call | solution.py:553
  54.7 0.1 collective-permute-start.17
  54.8 1.3 %collective-permute-done.17.came = bf16[4,128,128]{2,1,0:T(8,128)(2,1)S(1)} collective-permute-done((bf16[4,128,128]{2,1,0:T(8,128)(2,1)S(1)}, bf16[4,128,128]{2,1,0:T(8,128)(2,1)S(1)}, u32[]{:S(2)}, u32[]{:S(2)}) %collective-permute-start.17) | collective-permute-done | bytes 131104 | tf_op jit(solution)/shard_map/ppermute | solution.py:640
  56.2 0.1 collective-permute-start.19
  56.3 1.9 %collective-permute-start.20 = (bf16[2,128,128]{2,1,0:T(8,128)(2,1)S(1)}, bf16[2,128,128]{2,1,0:T(8,128)(2,1)S(1)}, u32[]{:S(2)}, u32[]{:S(2)}) collective-permute-start(bf16[2,128,128]{2,1,0:T(8,128)(2,1)S(1)} %pad_maximum_fusion.11), channel_id=1, source_target_pairs={{0,16},{4,20},{8,24},{12,28},{16,0},{20,4},{24,8},{28,12},{32,48},... | collective-permute-start | bytes 196616 | tf_op jit(solution)/shard_map/ppermute | solution.py:640
  58.2 3.0 %collective-permute-start.18 = (bf16[2,128,128]{2,1,0:T(8,128)(2,1)S(1)}, bf16[2,128,128]{2,1,0:T(8,128)(2,1)S(1)}, u32[]{:S(2)}, u32[]{:S(2)}) collective-permute-start(bf16[2,128,128]{2,1,0:T(8,128)(2,1)S(1)} %pad_maximum_fusion.9), channel_id=1, source_target_pairs={{0,24},{4,28},{8,16},{12,20},{16,8},{20,12},{24,0},{28,4},{32,56},... | collective-permute-start | bytes 196616 | tf_op jit(solution)/shard_map/ppermute | solution.py:640
  61.1 1.1 %collective-permute-done.20.two = bf16[2,128,128]{2,1,0:T(8,128)(2,1)S(1)} collective-permute-done((bf16[2,128,128]{2,1,0:T(8,128)(2,1)S(1)}, bf16[2,128,128]{2,1,0:T(8,128)(2,1)S(1)}, u32[]{:S(2)}, u32[]{:S(2)}) %collective-permute-start.20) | collective-permute-done | bytes 65568 | tf_op jit(solution)/shard_map/ppermute | solution.py:640
  62.2 1.0 %early.1.acc_ref = f32[128,4096]{1,0:T(8,128)S(1)} custom-call(bf16[4,128,128]{2,1,0:T(8,128)(2,1)S(1)} %get-tuple-element.66.keep, bf16[4,128,128]{2,1,0:T(8,128)(2,1)S(1)} %collective-permute-done.17.came, bf16[2,128,128]{2,1,0:T(8,128)(2,1)S(1)} %collective-permute-done.19.one, bf16[2,128,128]{2,1,0:T(8,128)(2,1)S(1)} %collective-permute-done.20.two, ...), custom_call_target="tpu_custom_call" | custom-call | flops 800000000 | bytes 8000000 | tf_op jit(solution)/shard_map/early/pallas_call | solution.py:617
  63.2 0.5 collective-permute-done.18.three
  63.7 0.4 late.1
  64.2 1.6 %collective-permute-start.21 = (bf16[32,2048]{1,0:T(8,128)(2,1)S(1)}, bf16[32,2048]{1,0:T(8,128)(2,1)S(1)}, u32[]{:S(2)}, u32[]{:S(2)}) collective-permute-start(bf16[32,2048]{1,0:T(8,128)(2,1)S(1)} %get-tuple-element.70), channel_id=1, source_target_pairs={{0,1},{1,2},{2,3},{3,0},{4,5},{5,6},{6,7},{7,4},{8,9},{9,10},{10,1... | collective-permute-start | bytes 393224 | tf_op jit(solution)/shard_map/ppermute | solution.py:686
  65.8 1.7 %collective-permute-start.22 = (bf16[32,2048]{1,0:T(8,128)(2,1)S(1)}, bf16[32,2048]{1,0:T(8,128)(2,1)S(1)}, u32[]{:S(2)}, u32[]{:S(2)}) collective-permute-start(bf16[32,2048]{1,0:T(8,128)(2,1)S(1)} %get-tuple-element.71), channel_id=1, source_target_pairs={{0,3},{1,0},{2,1},{3,2},{4,7},{5,4},{6,5},{7,6},{8,11},{9,8},{10,9... | collective-permute-start | bytes 393224 | tf_op jit(solution)/shard_map/ppermute | solution.py:686
  67.5 1.8 %collective-permute-start.24 = (bf16[32,2048]{1,0:T(8,128)(2,1)S(1)}, bf16[32,2048]{1,0:T(8,128)(2,1)S(1)}, u32[]{:S(2)}, u32[]{:S(2)}) collective-permute-start(bf16[32,2048]{1,0:T(8,128)(2,1)S(1)} %get-tuple-element.73), channel_id=1, source_target_pairs={{0,3},{1,0},{2,1},{3,2},{4,7},{5,4},{6,5},{7,6},{8,11},{9,8},{10,9... | collective-permute-start | bytes 393224 | tf_op jit(solution)/shard_map/ppermute | solution.py:686
  69.3 0.2 collective-permute-start.26
  69.5 0.9 %collective-permute-done.21 = bf16[32,2048]{1,0:T(8,128)(2,1)S(1)} collective-permute-done((bf16[32,2048]{1,0:T(8,128)(2,1)S(1)}, bf16[32,2048]{1,0:T(8,128)(2,1)S(1)}, u32[]{:S(2)}, u32[]{:S(2)}) %collective-permute-start.21) | collective-permute-done | bytes 131104 | tf_op jit(solution)/shard_map/ppermute | solution.py:686
  70.5 1.0 %collective-permute-done.22 = bf16[32,2048]{1,0:T(8,128)(2,1)S(1)} collective-permute-done((bf16[32,2048]{1,0:T(8,128)(2,1)S(1)}, bf16[32,2048]{1,0:T(8,128)(2,1)S(1)}, u32[]{:S(2)}, u32[]{:S(2)}) %collective-permute-start.22) | collective-permute-done | bytes 131104 | tf_op jit(solution)/shard_map/ppermute | solution.py:686
  71.5 1.5 %collective-permute-start.23 = (bf16[32,2048]{1,0:T(8,128)(2,1)S(1)}, bf16[32,2048]{1,0:T(8,128)(2,1)S(1)}, u32[]{:S(2)}, u32[]{:S(2)}) collective-permute-start(bf16[32,2048]{1,0:T(8,128)(2,1)S(1)} %add_convert_fusion.1), channel_id=1, source_target_pairs={{0,1},{1,2},{2,3},{3,0},{4,5},{5,6},{6,7},{7,4},{8,9},{9,10},{10,1... | collective-permute-start | bytes 393224 | tf_op jit(solution)/shard_map/ppermute | solution.py:686
  73.0 1.9 %collective-permute-start.25 = (bf16[32,2048]{1,0:T(8,128)(2,1)S(1)}, bf16[32,2048]{1,0:T(8,128)(2,1)S(1)}, u32[]{:S(2)}, u32[]{:S(2)}) collective-permute-start(bf16[32,2048]{1,0:T(8,128)(2,1)S(1)} %add_convert_fusion), channel_id=1, source_target_pairs={{0,3},{1,0},{2,1},{3,2},{4,7},{5,4},{6,5},{7,6},{8,11},{9,8},{10,9... | collective-permute-start | bytes 393224 | tf_op jit(solution)/shard_map/ppermute | solution.py:686
  74.9 0.0 collective-permute-done.24
  74.9 2.8 %collective-permute-done.23 = bf16[32,2048]{1,0:T(8,128)(2,1)S(1)} collective-permute-done((bf16[32,2048]{1,0:T(8,128)(2,1)S(1)}, bf16[32,2048]{1,0:T(8,128)(2,1)S(1)}, u32[]{:S(2)}, u32[]{:S(2)}) %collective-permute-start.23) | collective-permute-done | bytes 131104 | tf_op jit(solution)/shard_map/ppermute | solution.py:686
  77.7 0.0 collective-permute-done.26
  77.8 0.3 collective-permute-done.25
  78.1 0.8 fusion
  (34 shorter events, 0.3 us)
Async XLA Ops:
  1.4 1.5 %collective-permute-start.4 = (bf16[4,144,128]{2,1,0:T(8,128)(2,1)S(1)}, bf16[4,144,128]{2,1,0:T(8,128)(2,1)S(1)}, u32[]{:S(2)}, u32[]{:S(2)}) collective-permute-start(bf16[4,144,128]{2,1,0:T(8,128)(2,1)S(1)} %get-tuple-element.44), channel_id=1, source_target_pairs={{0,4},{4,0},{8,12},{12,8},{16,20},{20,16},{24,28},{28,24},{32,36},... | collective-permute-start | bytes 442376 | tf_op jit(solution)/shard_map/ppermute | solution.py:640
  1.5 6.4 %collective-permute-start = (bf16[4,256,128]{2,1,0:T(8,128)(2,1)S(1)}, bf16[4,256,128]{2,1,0:T(8,128)(2,1)S(1)}, u32[]{:S(2)}, u32[]{:S(2)}) collective-permute-start(bf16[4,256,128]{2,1,0:T(8,128)(2,1)S(1)} %get-tuple-element.42), channel_id=1, source_target_pairs={{0,4},{4,0},{8,12},{12,8},{16,20},{20,16},{24,28},{28,24},{32,36},... | collective-permute-start | bytes 786440 | tf_op jit(solution)/shard_map/ppermute | solution.py:640
  2.9 9.4 %collective-permute-start.5 = (bf16[2,144,128]{2,1,0:T(8,128)(2,1)S(1)}, bf16[2,144,128]{2,1,0:T(8,128)(2,1)S(1)}, u32[]{:S(2)}, u32[]{:S(2)}) collective-permute-start(bf16[2,144,128]{2,1,0:T(8,128)(2,1)S(1)} %pad_maximum_fusion), channel_id=1, source_target_pairs={{0,8},{4,12},{8,0},{12,4},{16,24},{20,28},{24,16},{28,20},{32,40},... | collective-permute-start | bytes 221192 | tf_op jit(solution)/shard_map/ppermute | solution.py:640
  4.4 8.4 %collective-permute-start.6 = (bf16[2,144,128]{2,1,0:T(8,128)(2,1)S(1)}, bf16[2,144,128]{2,1,0:T(8,128)(2,1)S(1)}, u32[]{:S(2)}, u32[]{:S(2)}) collective-permute-start(bf16[2,144,128]{2,1,0:T(8,128)(2,1)S(1)} %pad_maximum_fusion.1), channel_id=1, source_target_pairs={{0,16},{4,20},{8,24},{12,28},{16,0},{20,4},{24,8},{28,12},{32,48},... | collective-permute-start | bytes 221192 | tf_op jit(solution)/shard_map/ppermute | solution.py:640
  7.3 6.4 %collective-permute-start.7 = (bf16[2,144,128]{2,1,0:T(8,128)(2,1)S(1)}, bf16[2,144,128]{2,1,0:T(8,128)(2,1)S(1)}, u32[]{:S(2)}, u32[]{:S(2)}) collective-permute-start(bf16[2,144,128]{2,1,0:T(8,128)(2,1)S(1)} %pad_maximum_fusion.2), channel_id=1, source_target_pairs={{0,24},{4,28},{8,16},{12,20},{16,8},{20,12},{24,0},{28,4},{32,56},... | collective-permute-start | bytes 221192 | tf_op jit(solution)/shard_map/ppermute | solution.py:640
  7.9 8.5 %collective-permute-start.1 = (bf16[2,128,128]{2,1,0:T(8,128)(2,1)S(1)}, bf16[2,128,128]{2,1,0:T(8,128)(2,1)S(1)}, u32[]{:S(2)}, u32[]{:S(2)}) collective-permute-start(bf16[2,128,128]{2,1,0:T(8,128)(2,1)S(1)} %pad_maximum_fusion.3), channel_id=1, source_target_pairs={{0,8},{4,12},{8,0},{12,4},{16,24},{20,28},{24,16},{28,20},{32,40},... | collective-permute-start | bytes 196616 | tf_op jit(solution)/shard_map/ppermute | solution.py:640
  8.2 8.1 %collective-permute-start.2 = (bf16[2,128,128]{2,1,0:T(8,128)(2,1)S(1)}, bf16[2,128,128]{2,1,0:T(8,128)(2,1)S(1)}, u32[]{:S(2)}, u32[]{:S(2)}) collective-permute-start(bf16[2,128,128]{2,1,0:T(8,128)(2,1)S(1)} %pad_maximum_fusion.4), channel_id=1, source_target_pairs={{0,16},{4,20},{8,24},{12,28},{16,0},{20,4},{24,8},{28,12},{32,48},... | collective-permute-start | bytes 196616 | tf_op jit(solution)/shard_map/ppermute | solution.py:640
  12.3 28.9 %copy-start.1 = (f32[128]{0:T(128)S(1)}, f32[128]{0:T(128)}, u32[]{:S(2)}) copy-start(f32[128]{0:T(128)} %param.13) | copy-start | bytes 1540
  12.3 36.9 %copy-start = (bf16[8,128,384]{2,1,0:T(8,128)(2,1)S(1)}, bf16[8,128,384]{2,1,0:T(8,128)(2,1)}, u32[]{:S(2)}) copy-start(bf16[8,128,384]{2,1,0:T(8,128)(2,1)} %weight_ref.7) | copy-start | bytes 2359300
  12.3 5.6 %collective-permute-start.3 = (bf16[2,128,128]{2,1,0:T(8,128)(2,1)S(1)}, bf16[2,128,128]{2,1,0:T(8,128)(2,1)S(1)}, u32[]{:S(2)}, u32[]{:S(2)}) collective-permute-start(bf16[2,128,128]{2,1,0:T(8,128)(2,1)S(1)} %pad_maximum_fusion.5), channel_id=1, source_target_pairs={{0,24},{4,28},{8,16},{12,20},{16,8},{20,12},{24,0},{28,4},{32,56},... | collective-permute-start | bytes 196616 | tf_op jit(solution)/shard_map/ppermute | solution.py:640
  19.0 43.2 %slice-start = ((s8[8388608]{0:T(1024)(128)(4,1)}), s8[4194304]{0:T(1024)(128)(4,1)S(1)}, s32[]{:S(2)}) async-start(s8[8388608]{0:T(1024)(128)(4,1)} %bitcast.1), calls=%async_computation | async-start | bytes 8388608
  19.0 13.7 %collective-permute-start.12 = (bf16[128,256]{1,0:T(8,128)(2,1)S(1)}, bf16[128,256]{1,0:T(8,128)(2,1)S(1)}, u32[]{:S(2)}, u32[]{:S(2)}) collective-permute-start(bf16[128,256]{1,0:T(8,128)(2,1)S(1)} %get-tuple-element.50.own_ref), channel_id=1, source_target_pairs={{0,64},{4,68},{8,72},{12,76},{16,80},{20,84},{24,88},{28,92},{32,9... | collective-permute-start | bytes 196616 | tf_op jit(solution)/shard_map/ppermute | solution.py:657
  24.8 8.0 %collective-permute-start.11 = (bf16[128,256]{1,0:T(8,128)(2,1)S(1)}, bf16[128,256]{1,0:T(8,128)(2,1)S(1)}, u32[]{:S(2)}, u32[]{:S(2)}) collective-permute-start(bf16[128,256]{1,0:T(8,128)(2,1)S(1)} %get-tuple-element.50.own_ref), channel_id=1, source_target_pairs={{0,32},{4,36},{8,40},{12,44},{16,48},{20,52},{24,56},{28,60},{32,6... | collective-permute-start | bytes 196616 | tf_op jit(solution)/shard_map/ppermute | solution.py:657
  27.8 7.9 %collective-permute-start.8 = (bf16[2,128,128]{2,1,0:T(8,128)(2,1)S(1)}, bf16[2,128,128]{2,1,0:T(8,128)(2,1)S(1)}, u32[]{:S(2)}, u32[]{:S(2)}) collective-permute-start(bf16[2,128,128]{2,1,0:T(8,128)(2,1)S(1)} %pad_maximum_fusion.6), channel_id=1, source_target_pairs={{0,8},{4,12},{8,0},{12,4},{16,24},{20,28},{24,16},{28,20},{32,40},... | collective-permute-start | bytes 196616 | tf_op jit(solution)/shard_map/ppermute | solution.py:640
  27.9 7.8 %collective-permute-start.9 = (bf16[2,128,128]{2,1,0:T(8,128)(2,1)S(1)}, bf16[2,128,128]{2,1,0:T(8,128)(2,1)S(1)}, u32[]{:S(2)}, u32[]{:S(2)}) collective-permute-start(bf16[2,128,128]{2,1,0:T(8,128)(2,1)S(1)} %pad_maximum_fusion.7), channel_id=1, source_target_pairs={{0,16},{4,20},{8,24},{12,28},{16,0},{20,4},{24,8},{28,12},{32,48},... | collective-permute-start | bytes 196616 | tf_op jit(solution)/shard_map/ppermute | solution.py:640
  29.9 5.8 %collective-permute-start.10 = (bf16[2,128,128]{2,1,0:T(8,128)(2,1)S(1)}, bf16[2,128,128]{2,1,0:T(8,128)(2,1)S(1)}, u32[]{:S(2)}, u32[]{:S(2)}) collective-permute-start(bf16[2,128,128]{2,1,0:T(8,128)(2,1)S(1)} %pad_maximum_fusion.8), channel_id=1, source_target_pairs={{0,24},{4,28},{8,16},{12,20},{16,8},{20,12},{24,0},{28,4},{32,56},... | collective-permute-start | bytes 196616 | tf_op jit(solution)/shard_map/ppermute | solution.py:640
  33.1 8.1 %collective-permute-start.14 = (bf16[128,256]{1,0:T(8,128)(2,1)S(1)}, bf16[128,256]{1,0:T(8,128)(2,1)S(1)}, u32[]{:S(2)}, u32[]{:S(2)}) collective-permute-start(bf16[128,256]{1,0:T(8,128)(2,1)S(1)} %get-tuple-element.57), channel_id=1, source_target_pairs={{0,96},{4,100},{8,104},{12,108},{16,112},{20,116},{24,120},{28,124... | collective-permute-start | bytes 196616 | tf_op jit(solution)/shard_map/ppermute | solution.py:657
  35.0 6.1 %collective-permute-start.13 = (bf16[128,256]{1,0:T(8,128)(2,1)S(1)}, bf16[128,256]{1,0:T(8,128)(2,1)S(1)}, u32[]{:S(2)}, u32[]{:S(2)}) collective-permute-start(bf16[128,256]{1,0:T(8,128)(2,1)S(1)} %get-tuple-element.57), channel_id=1, source_target_pairs={{0,192},{4,196},{8,200},{12,204},{16,208},{20,212},{24,216},{28,22... | collective-permute-start | bytes 196616 | tf_op jit(solution)/shard_map/ppermute | solution.py:657
  41.8 8.6 %collective-permute-start.16 = (bf16[512,128]{1,0:T(8,128)(2,1)S(1)}, bf16[512,128]{1,0:T(8,128)(2,1)S(1)}, u32[]{:S(2)}, u32[]{:S(2)}) collective-permute-start(bf16[512,128]{1,0:T(8,128)(2,1)S(1)} %get-tuple-element.59.near_ref), channel_id=1, source_target_pairs={{0,32},{4,36},{8,40},{12,44},{16,48},{20,52},{24,56},{28,60},{32,6... | collective-permute-start | bytes 393224 | tf_op jit(solution)/shard_map/ppermute | solution.py:657
  46.7 15.5 %slice-start.1 = ((s8[8388608]{0:T(1024)(128)(4,1)}), s8[4194304]{0:T(1024)(128)(4,1)S(1)}, s32[]{:S(2)}) async-start(s8[8388608]{0:T(1024)(128)(4,1)} %bitcast.1), calls=%async_computation.1 | async-start | bytes 8388608
  46.8 7.1 %collective-permute-start.15 = (bf16[512,128]{1,0:T(8,128)(2,1)S(1)}, bf16[512,128]{1,0:T(8,128)(2,1)S(1)}, u32[]{:S(2)}, u32[]{:S(2)}) collective-permute-start(bf16[512,128]{1,0:T(8,128)(2,1)S(1)} %get-tuple-element.58.far_ref), channel_id=1, source_target_pairs={{0,32},{4,36},{8,40},{12,44},{16,48},{20,52},{24,56},{28,60},{32,6... | collective-permute-start | bytes 393224 | tf_op jit(solution)/shard_map/ppermute | solution.py:657
  54.7 1.4 %collective-permute-start.17 = (bf16[4,128,128]{2,1,0:T(8,128)(2,1)S(1)}, bf16[4,128,128]{2,1,0:T(8,128)(2,1)S(1)}, u32[]{:S(2)}, u32[]{:S(2)}) collective-permute-start(bf16[4,128,128]{2,1,0:T(8,128)(2,1)S(1)} %get-tuple-element.67), channel_id=1, source_target_pairs={{0,4},{4,0},{8,12},{12,8},{16,20},{20,16},{24,28},{28,24},{32,36},... | collective-permute-start | bytes 393224 | tf_op jit(solution)/shard_map/ppermute | solution.py:640
  56.2 5.0 %collective-permute-start.19 = (bf16[2,128,128]{2,1,0:T(8,128)(2,1)S(1)}, bf16[2,128,128]{2,1,0:T(8,128)(2,1)S(1)}, u32[]{:S(2)}, u32[]{:S(2)}) collective-permute-start(bf16[2,128,128]{2,1,0:T(8,128)(2,1)S(1)} %pad_maximum_fusion.10), channel_id=1, source_target_pairs={{0,8},{4,12},{8,0},{12,4},{16,24},{20,28},{24,16},{28,20},{32,40},... | collective-permute-start | bytes 196616 | tf_op jit(solution)/shard_map/ppermute | solution.py:640
  56.3 5.9 %collective-permute-start.20 = (bf16[2,128,128]{2,1,0:T(8,128)(2,1)S(1)}, bf16[2,128,128]{2,1,0:T(8,128)(2,1)S(1)}, u32[]{:S(2)}, u32[]{:S(2)}) collective-permute-start(bf16[2,128,128]{2,1,0:T(8,128)(2,1)S(1)} %pad_maximum_fusion.11), channel_id=1, source_target_pairs={{0,16},{4,20},{8,24},{12,28},{16,0},{20,4},{24,8},{28,12},{32,48},... | collective-permute-start | bytes 196616 | tf_op jit(solution)/shard_map/ppermute | solution.py:640
  58.2 5.6 %collective-permute-start.18 = (bf16[2,128,128]{2,1,0:T(8,128)(2,1)S(1)}, bf16[2,128,128]{2,1,0:T(8,128)(2,1)S(1)}, u32[]{:S(2)}, u32[]{:S(2)}) collective-permute-start(bf16[2,128,128]{2,1,0:T(8,128)(2,1)S(1)} %pad_maximum_fusion.9), channel_id=1, source_target_pairs={{0,24},{4,28},{8,16},{12,20},{16,8},{20,12},{24,0},{28,4},{32,56},... | collective-permute-start | bytes 196616 | tf_op jit(solution)/shard_map/ppermute | solution.py:640
  64.2 6.3 %collective-permute-start.21 = (bf16[32,2048]{1,0:T(8,128)(2,1)S(1)}, bf16[32,2048]{1,0:T(8,128)(2,1)S(1)}, u32[]{:S(2)}, u32[]{:S(2)}) collective-permute-start(bf16[32,2048]{1,0:T(8,128)(2,1)S(1)} %get-tuple-element.70), channel_id=1, source_target_pairs={{0,1},{1,2},{2,3},{3,0},{4,5},{5,6},{6,7},{7,4},{8,9},{9,10},{10,1... | collective-permute-start | bytes 393224 | tf_op jit(solution)/shard_map/ppermute | solution.py:686
  65.8 5.6 %collective-permute-start.22 = (bf16[32,2048]{1,0:T(8,128)(2,1)S(1)}, bf16[32,2048]{1,0:T(8,128)(2,1)S(1)}, u32[]{:S(2)}, u32[]{:S(2)}) collective-permute-start(bf16[32,2048]{1,0:T(8,128)(2,1)S(1)} %get-tuple-element.71), channel_id=1, source_target_pairs={{0,3},{1,0},{2,1},{3,2},{4,7},{5,4},{6,5},{7,6},{8,11},{9,8},{10,9... | collective-permute-start | bytes 393224 | tf_op jit(solution)/shard_map/ppermute | solution.py:686
  67.5 7.4 %collective-permute-start.24 = (bf16[32,2048]{1,0:T(8,128)(2,1)S(1)}, bf16[32,2048]{1,0:T(8,128)(2,1)S(1)}, u32[]{:S(2)}, u32[]{:S(2)}) collective-permute-start(bf16[32,2048]{1,0:T(8,128)(2,1)S(1)} %get-tuple-element.73), channel_id=1, source_target_pairs={{0,3},{1,0},{2,1},{3,2},{4,7},{5,4},{6,5},{7,6},{8,11},{9,8},{10,9... | collective-permute-start | bytes 393224 | tf_op jit(solution)/shard_map/ppermute | solution.py:686
  69.3 8.4 %collective-permute-start.26 = (bf16[32,2048]{1,0:T(8,128)(2,1)S(1)}, bf16[32,2048]{1,0:T(8,128)(2,1)S(1)}, u32[]{:S(2)}, u32[]{:S(2)}) collective-permute-start(bf16[32,2048]{1,0:T(8,128)(2,1)S(1)} %get-tuple-element.76), channel_id=1, source_target_pairs={{0,1},{1,2},{2,3},{3,0},{4,5},{5,6},{6,7},{7,4},{8,9},{9,10},{10,1... | collective-permute-start | bytes 393224 | tf_op jit(solution)/shard_map/ppermute | solution.py:686
  71.5 6.3 %collective-permute-start.23 = (bf16[32,2048]{1,0:T(8,128)(2,1)S(1)}, bf16[32,2048]{1,0:T(8,128)(2,1)S(1)}, u32[]{:S(2)}, u32[]{:S(2)}) collective-permute-start(bf16[32,2048]{1,0:T(8,128)(2,1)S(1)} %add_convert_fusion.1), channel_id=1, source_target_pairs={{0,1},{1,2},{2,3},{3,0},{4,5},{5,6},{6,7},{7,4},{8,9},{9,10},{10,1... | collective-permute-start | bytes 393224 | tf_op jit(solution)/shard_map/ppermute | solution.py:686
  73.0 5.0 %collective-permute-start.25 = (bf16[32,2048]{1,0:T(8,128)(2,1)S(1)}, bf16[32,2048]{1,0:T(8,128)(2,1)S(1)}, u32[]{:S(2)}, u32[]{:S(2)}) collective-permute-start(bf16[32,2048]{1,0:T(8,128)(2,1)S(1)} %add_convert_fusion), channel_id=1, source_target_pairs={{0,3},{1,0},{2,1},{3,2},{4,7},{5,4},{6,5},{7,6},{8,11},{9,8},{10,9... | collective-permute-start | bytes 393224 | tf_op jit(solution)/shard_map/ppermute | solution.py:686

commit v16 on v12

--- a/solution.py
+++ b/solution.py
@@ -298,7 +298,7 @@
 
 
 def query_kernel(*refs):
-    k_ref, mix_ref, wu_ref, level_ref, no_ref, before, q_ref = refs[5:]
+    k_ref, mix_ref, wu_ref, level_ref, n_ref, o_ref, before, q_ref = refs[5:]
     gather_slots(refs[:5], q_ref, slice(C, 2 * C))
     me = lax.axis_index("seq") % PLANE
     row, col = iotas()
@@ -330,17 +330,19 @@
     both = [mm(reach[d], before[chunks[d]]) for d in every]
     for d in every:
         rows = pl.ds(pl.multiple_of(chunks[d] * C, C), C)
-        no_ref[rows, :] = jnp.concatenate(
-            [both[d][:, :C], both[d][:, C:] + parts[d][:, C:]], axis=1
-        )
+        n_ref[rows, :] = jnp.concatenate(split(both[d][:, :C]), axis=1)
+        o_ref[rows, :] = both[d][:, C:] + parts[d][:, C:]
 
 
 def query(slots, k, mix, wu, level):
     return pl.pallas_call(
         query_kernel,
-        out_shape=jax.ShapeDtypeStruct((PLANE * C, 2 * C), F32),
+        out_shape=[
+            jax.ShapeDtypeStruct((PLANE * C, 2 * C), BF16),
+            jax.ShapeDtypeStruct((PLANE * C, C), F32),
+        ],
         in_specs=[vmem()] * 9,
-        out_specs=vmem(),
+        out_specs=[vmem()] * 2,
         scratch_shapes=[
             pltpu.VMEM((PLANE, C, 2 * C), F32),
             pltpu.VMEM((PLANE, C, C), BF16),
@@ -380,24 +382,26 @@
     )(own_map, one, two)
 
 
-def norm_kernel(no_ref, gain_ref, before_ref, six_ref, three_ref, normed_ref):
+def norm_kernel(n_ref, o_ref, gain_ref, before_ref, six_ref, three_ref, normed_ref):
     state = three_ref[:, C:].astype(F32) + dot(three_ref[:, :C], six_ref[:, C:])
     state = before_ref[:, C:] + mm(before_ref[:, :C], state)
-    out = mm(no_ref[:, :C], state) + no_ref[:, C:]
+    pair = jnp.concatenate(split(state), axis=1)
+    out = dot(n_ref[...], jnp.concatenate([pair, pair], axis=0))
+    out = out[:, :C] + out[:, C:] + o_ref[...]
     scale = lax.rsqrt(jnp.mean(out * out, axis=1, keepdims=True) + EPS)
     normed_ref[...] = (out * scale * gain_ref[...]).astype(BF16)
 
 
-def norm(no, gain, before, six, three):
+def norm(n, o, gain, before, six, three):
     return pl.pallas_call(
         norm_kernel,
         out_shape=jax.ShapeDtypeStruct((PLANE * C, C), BF16),
-        in_specs=[vmem()] * 5,
+        in_specs=[vmem()] * 6,
         out_specs=vmem(),
         compiler_params=params(),
         cost_estimate=cost(2e8, 2e6),
         name="norm",
-    )(no, gain, before, six, three)
+    )(n, o, gain, before, six, three)
 
 
 QB = 256
@@ -628,11 +632,11 @@
     two = later_plane(ab, 2)
     keep_q, came_q, _ = lax.optimization_barrier((keep, came, ab))
     slots_q = along_x(keep_q, came_q, slice(C, 2 * C))
-    no = query(slots_q, k, mix, wu, level)
+    n, o = query(slots_q, k, mix, wu, level)
     before, upto = combine(ab, one, two)
     six = later_plane(upto, 6)
     three = later_plane(upto, 3)
-    normed = norm(no, gain[None, :], before, six, three)
+    normed = norm(n, o, gain[None, :], before, six, three)
     halo = later_plane(normed, 1)
     acc, stat, q2 = own(normed, attn_weight)
     attended = exchange(*halo_part(halo, attn_weight, acc, stat, q2))

time: 77.3 us -> 77 us (level)
  no operation moved by 1% of the time
where the time goes in v16:
time: 77 us; the launch traced here: 76.8 us
  starting transfers between devices  40.5 us (53%)
  waiting for transfers between devices  23.1 us (30%)
  Pallas kernels  11.8 us (15%)
  other arithmetic  0.96 us (1%)
    ppermute x15, starting transfers between devices, swap(): lax.ppermute(block, 'seq', [(s, s ^ d) for s in range(PLANE * PLANES)])  20.5 us
    ppermute x5, waiting for transfers between devices, later_plane(): return lax.ppermute(block, 'seq', route)  12 us
    ppermute x5, starting transfers between devices, later_plane(): return lax.ppermute(block, 'seq', route)  11.3 us
    ppermute x6, starting transfers between devices, turn(): return lax.ppermute(block, 'heads', [(s, (s + step) % 4) for s in range(4)])  8.73 us
    ppermute x15, waiting for transfers between devices, swap(): lax.ppermute(block, 'seq', [(s, s ^ d) for s in range(PLANE * PLANES)])  6.08 us
    ppermute x6, waiting for transfers between devices, turn(): return lax.ppermute(block, 'heads', [(s, (s + step) % 4) for s in range(4)])  5 us
    pallas_call x1, Pallas kernels, key_part(): pl.pallas_call(key_kernel, out_shape=[jax.ShapeDtypeStruct((PLANE, KROWS,...  2.71 us
  transfers between devices with their start and end apart: 26, of which 12 were waited for; matrix products, arithmetic and copies ran while one was open for 0% of the time, Pallas kernels for 9%

profile of v16, /device:TPU:128, one launch (start us, length us, event | category | flops | bytes accessed | tf_op | source)
XLA Modules:
  0.0 76.8 jit_solution(1020313408678824250)
XLA Ops:
  0.0 1.4 %pack.1 = (bf16[4,144,128]{2,1,0:T(8,128)(2,1)S(1)}, bf16[4,144,128]{2,1,0:T(8,128)(2,1)S(1)}, bf16[4,256,128]{2,1,0:T(8,128)(2,1)S(1)}, bf16[4,256,128]{2,1,0:T(8,128)(2,1)S(1)}) custom-call(bf16[128,1024]{1,0:T(8,128)(2,1)} %q_ref.1, bf16[128,1024]{1,0:T(8,128)(2,1)} %k_ref.1, bf16[128,1024]{1,0:T(8,128)(2,1)} %v_ref.1, f32[8,128]{1,0:T(8,128)} %decay_ref.1, ...), custom_call_target="tpu_custom_call" | custom-call | tf_op jit(solution)/shard_map/pack/pallas_call | solution.py:113
  1.4 0.1 collective-permute-start.4
  1.5 0.5 collective-permute-start
  2.0 0.8 %collective-permute-done.4.refs_1_ = bf16[4,144,128]{2,1,0:T(8,128)(2,1)S(1)} collective-permute-done((bf16[4,144,128]{2,1,0:T(8,128)(2,1)S(1)}, bf16[4,144,128]{2,1,0:T(8,128)(2,1)S(1)}, u32[]{:S(2)}, u32[]{:S(2)}) %collective-permute-start.4) | collective-permute-done | bytes 147488 | tf_op jit(solution)/shard_map/ppermute | solution.py:604
  2.9 0.0 copy-start
  2.9 1.6 %collective-permute-start.5 = (bf16[2,144,128]{2,1,0:T(8,128)(2,1)S(1)}, bf16[2,144,128]{2,1,0:T(8,128)(2,1)S(1)}, u32[]{:S(2)}, u32[]{:S(2)}) collective-permute-start(bf16[2,144,128]{2,1,0:T(8,128)(2,1)S(1)} %pad_maximum_fusion), channel_id=1, source_target_pairs={{0,8},{4,12},{8,0},{12,4},{16,24},{20,28},{24,16},{28,20},{32,40},... | collective-permute-start | bytes 221192 | tf_op jit(solution)/shard_map/ppermute | solution.py:604
  4.5 2.8 %collective-permute-start.6 = (bf16[2,144,128]{2,1,0:T(8,128)(2,1)S(1)}, bf16[2,144,128]{2,1,0:T(8,128)(2,1)S(1)}, u32[]{:S(2)}, u32[]{:S(2)}) collective-permute-start(bf16[2,144,128]{2,1,0:T(8,128)(2,1)S(1)} %pad_maximum_fusion.1), channel_id=1, source_target_pairs={{0,16},{4,20},{8,24},{12,28},{16,0},{20,4},{24,8},{28,12},{32,48},... | collective-permute-start | bytes 221192 | tf_op jit(solution)/shard_map/ppermute | solution.py:604
  7.3 0.6 collective-permute-start.7
  7.9 0.0 collective-permute-done.refs_1_
  7.9 0.4 collective-permute-start.1
  8.3 4.0 %collective-permute-start.2 = (bf16[2,128,128]{2,1,0:T(8,128)(2,1)S(1)}, bf16[2,128,128]{2,1,0:T(8,128)(2,1)S(1)}, u32[]{:S(2)}, u32[]{:S(2)}) collective-permute-start(bf16[2,128,128]{2,1,0:T(8,128)(2,1)S(1)} %pad_maximum_fusion.4), channel_id=1, source_target_pairs={{0,16},{4,20},{8,24},{12,28},{16,0},{20,4},{24,8},{28,12},{32,48},... | collective-permute-start | bytes 196616 | tf_op jit(solution)/shard_map/ppermute | solution.py:604
  12.3 0.0 collective-permute-done.5.refs_2_
  12.3 0.6 collective-permute-start.3
  12.9 0.0 collective-permute-done.6.refs_3_
  12.9 0.8 collective-permute-done.7.refs_4_
  13.6 2.7 %keys.1 = (bf16[8,144,128]{2,1,0:T(8,128)(2,1)S(1)}, f32[8,128,128]{2,1,0:T(8,128)S(1)}, f32[8,128,128]{2,1,0:T(8,128)S(1)}, f32[8,128,128]{2,1,0:T(8,128)S(1)},...) custom-call(bf16[4,144,128]{2,1,0:T(8,128)(2,1)S(1)} %get-tuple-element.40.refs_0_, ...), custom_call_target="tpu_custom_call" | custom-call | flops 2000000000 | bytes 4000000 | tf_op jit(solution)/shard_map/keys/pallas_call | solution.py:271
  16.4 0.0 collective-permute-done.1.refs_2_
  16.4 0.0 collective-permute-done.2.refs_3_
  16.4 1.5 %collective-permute-done.3.refs_4_ = bf16[2,128,128]{2,1,0:T(8,128)(2,1)S(1)} collective-permute-done((bf16[2,128,128]{2,1,0:T(8,128)(2,1)S(1)}, bf16[2,128,128]{2,1,0:T(8,128)(2,1)S(1)}, u32[]{:S(2)}, u32[]{:S(2)}) %collective-permute-start.3) | collective-permute-done | bytes 65568 | tf_op jit(solution)/shard_map/ppermute | solution.py:604
  17.9 1.1 %values.1 = (f32[8,128,256]{2,1,0:T(8,128)S(1)}, bf16[128,256]{1,0:T(8,128)(2,1)S(1)}, f32[7,128,256]{2,1,0:T(8,128)S(1)}) custom-call(bf16[4,256,128]{2,1,0:T(8,128)(2,1)S(1)} %get-tuple-element.48.refs_0_, bf16[4,256,128]{2,1,0:T(8,128)(2,1)S(1)} %collective-permute-done.refs_1_, bf16[2,128,128]{2,1,0:T(8,128)(2,1)S(1)} %collective-permute-done.1.refs_2_, ...), custom_call_target="tpu_custom_call" | custom-call | flops 1000000000 | bytes 4000000 | tf_op jit(solution)/shard_map/values/pallas_call | solution.py:284
  19.0 3.5 %collective-permute-start.12 = (bf16[128,256]{1,0:T(8,128)(2,1)S(1)}, bf16[128,256]{1,0:T(8,128)(2,1)S(1)}, u32[]{:S(2)}, u32[]{:S(2)}) collective-permute-start(bf16[128,256]{1,0:T(8,128)(2,1)S(1)} %get-tuple-element.47.own_ref), channel_id=1, source_target_pairs={{0,64},{4,68},{8,72},{12,76},{16,80},{20,84},{24,88},{28,92},{32,9... | collective-permute-start | bytes 196616 | tf_op jit(solution)/shard_map/ppermute | solution.py:621
  22.5 2.9 %collective-permute-start.11 = (bf16[128,256]{1,0:T(8,128)(2,1)S(1)}, bf16[128,256]{1,0:T(8,128)(2,1)S(1)}, u32[]{:S(2)}, u32[]{:S(2)}) collective-permute-start(bf16[128,256]{1,0:T(8,128)(2,1)S(1)} %get-tuple-element.47.own_ref), channel_id=1, source_target_pairs={{0,32},{4,36},{8,40},{12,44},{16,48},{20,52},{24,56},{28,60},{32,6... | collective-permute-start | bytes 196616 | tf_op jit(solution)/shard_map/ppermute | solution.py:621
  25.5 0.1 collective-permute-start.8
  25.6 2.1 %collective-permute-start.9 = (bf16[2,128,128]{2,1,0:T(8,128)(2,1)S(1)}, bf16[2,128,128]{2,1,0:T(8,128)(2,1)S(1)}, u32[]{:S(2)}, u32[]{:S(2)}) collective-permute-start(bf16[2,128,128]{2,1,0:T(8,128)(2,1)S(1)} %pad_maximum_fusion.7), channel_id=1, source_target_pairs={{0,16},{4,20},{8,24},{12,28},{16,0},{20,4},{24,8},{28,12},{32,48},... | collective-permute-start | bytes 196616 | tf_op jit(solution)/shard_map/ppermute | solution.py:604
  27.7 2.8 %collective-permute-start.10 = (bf16[2,128,128]{2,1,0:T(8,128)(2,1)S(1)}, bf16[2,128,128]{2,1,0:T(8,128)(2,1)S(1)}, u32[]{:S(2)}, u32[]{:S(2)}) collective-permute-start(bf16[2,128,128]{2,1,0:T(8,128)(2,1)S(1)} %pad_maximum_fusion.8), channel_id=1, source_target_pairs={{0,24},{4,28},{8,16},{12,20},{16,8},{20,12},{24,0},{28,4},{32,56},... | collective-permute-start | bytes 196616 | tf_op jit(solution)/shard_map/ppermute | solution.py:604
  30.5 0.0 collective-permute-done.12.two_ref
  30.5 0.0 collective-permute-done.11.one_ref
  30.5 0.3 combine.1
  30.8 1.9 %collective-permute-start.14 = (bf16[128,256]{1,0:T(8,128)(2,1)S(1)}, bf16[128,256]{1,0:T(8,128)(2,1)S(1)}, u32[]{:S(2)}, u32[]{:S(2)}) collective-permute-start(bf16[128,256]{1,0:T(8,128)(2,1)S(1)} %get-tuple-element.56), channel_id=1, source_target_pairs={{0,96},{4,100},{8,104},{12,108},{16,112},{20,116},{24,120},{28,124... | collective-permute-start | bytes 196616 | tf_op jit(solution)/shard_map/ppermute | solution.py:621
  32.7 0.7 collective-permute-start.13
  33.4 0.0 collective-permute-done.8.refs_2_
  33.4 0.0 collective-permute-done.9.refs_3_
  33.4 0.0 collective-permute-done.10.refs_4_
  33.4 1.4 %query.1 = (bf16[1024,256]{1,0:T(8,128)(2,1)S(1)}, f32[1024,128]{1,0:T(8,128)S(1)}) custom-call(bf16[4,256,128]{2,1,0:T(8,128)(2,1)S(1)} %get-tuple-element.48.refs_0_, bf16[4,256,128]{2,1,0:T(8,128)(2,1)S(1)} %collective-permute-done.refs_1_, bf16[2,128,128]{2,1,0:T(8,128)(2,1)S(1)} %collective-permute-done.8.refs_2_, ...), custom_call_target="tpu_custom_call" | custom-call | flops 1000000000 | bytes 4000000 | tf_op jit(solution)/shard_map/query/pallas_call | solution.py:338
  34.8 6.0 %collective-permute-done.14.three_ref = bf16[128,256]{1,0:T(8,128)(2,1)S(1)} collective-permute-done((bf16[128,256]{1,0:T(8,128)(2,1)S(1)}, bf16[128,256]{1,0:T(8,128)(2,1)S(1)}, u32[]{:S(2)}, u32[]{:S(2)}) %collective-permute-start.14) | collective-permute-done | bytes 65568 | tf_op jit(solution)/shard_map/ppermute | solution.py:621
  40.8 0.0 collective-permute-done.13.six_ref
  40.8 0.7 norm.1.normed_ref
  41.5 2.2 %collective-permute-start.15 = (bf16[1024,128]{1,0:T(8,128)(2,1)S(1)}, bf16[1024,128]{1,0:T(8,128)(2,1)S(1)}, u32[]{:S(2)}, u32[]{:S(2)}) collective-permute-start(bf16[1024,128]{1,0:T(8,128)(2,1)S(1)} %norm.1.normed_ref), channel_id=1, source_target_pairs={{0,32},{4,36},{8,40},{12,44},{16,48},{20,52},{24,56},{28,60},{32,6... | collective-permute-start | bytes 786440 | tf_op jit(solution)/shard_map/ppermute | solution.py:621
  43.8 1.3 %own.1 = (f32[1024,128]{1,0:T(8,128)S(1)}, f32[2,1024,128]{2,1,0:T(8,128)S(1)}, bf16[1024,128]{1,0:T(8,128)(2,1)S(1)}) custom-call(bf16[1024,128]{1,0:T(8,128)(2,1)S(1)} %norm.1.normed_ref, bf16[8,128,384]{2,1,0:T(8,128)(2,1)S(1)} %copy-done.1), custom_call_target="tpu_custom_call" | custom-call | flops 1000000000 | bytes 3000000 | tf_op jit(solution)/shard_map/own/pallas_call | solution.py:465
  45.1 6.1 %collective-permute-done.15.halo_ref = bf16[1024,128]{1,0:T(8,128)(2,1)S(1)} collective-permute-done((bf16[1024,128]{1,0:T(8,128)(2,1)S(1)}, bf16[1024,128]{1,0:T(8,128)(2,1)S(1)}, u32[]{:S(2)}, u32[]{:S(2)}) %collective-permute-start.15) | collective-permute-done | bytes 262176 | tf_op jit(solution)/shard_map/ppermute | solution.py:621
  51.1 1.5 %halo.1 = (bf16[4,128,128]{2,1,0:T(8,128)(2,1)S(1)}, bf16[4,128,128]{2,1,0:T(8,128)(2,1)S(1)}) custom-call(bf16[1024,128]{1,0:T(8,128)(2,1)S(1)} %collective-permute-done.15.halo_ref, bf16[8,128,384]{2,1,0:T(8,128)(2,1)S(1)} %copy-done.1, f32[1024,128]{1,0:T(8,128)S(1)} %get-tuple-element.57.acc_ref, f32[2,1024,128]{2,1,0:T(8,128)S(1)} %get-tuple-element.58.stat_ref, ...), custom_call_target="tpu_custom_call" | custom-call | flops 1000000000 | bytes 3000000 | tf_op jit(solution)/shard_map/halo/pallas_call | solution.py:517
  52.6 0.1 collective-permute-start.16
  52.8 1.3 %collective-permute-done.16.came = bf16[4,128,128]{2,1,0:T(8,128)(2,1)S(1)} collective-permute-done((bf16[4,128,128]{2,1,0:T(8,128)(2,1)S(1)}, bf16[4,128,128]{2,1,0:T(8,128)(2,1)S(1)}, u32[]{:S(2)}, u32[]{:S(2)}) %collective-permute-start.16) | collective-permute-done | bytes 131104 | tf_op jit(solution)/shard_map/ppermute | solution.py:604
  54.1 0.1 collective-permute-start.18
  54.2 1.9 %collective-permute-start.19 = (bf16[2,128,128]{2,1,0:T(8,128)(2,1)S(1)}, bf16[2,128,128]{2,1,0:T(8,128)(2,1)S(1)}, u32[]{:S(2)}, u32[]{:S(2)}) collective-permute-start(bf16[2,128,128]{2,1,0:T(8,128)(2,1)S(1)} %pad_maximum_fusion.11), channel_id=1, source_target_pairs={{0,16},{4,20},{8,24},{12,28},{16,0},{20,4},{24,8},{28,12},{32,48},... | collective-permute-start | bytes 196616 | tf_op jit(solution)/shard_map/ppermute | solution.py:604
  56.2 2.9 %collective-permute-start.17 = (bf16[2,128,128]{2,1,0:T(8,128)(2,1)S(1)}, bf16[2,128,128]{2,1,0:T(8,128)(2,1)S(1)}, u32[]{:S(2)}, u32[]{:S(2)}) collective-permute-start(bf16[2,128,128]{2,1,0:T(8,128)(2,1)S(1)} %pad_maximum_fusion.9), channel_id=1, source_target_pairs={{0,24},{4,28},{8,16},{12,20},{16,8},{20,12},{24,0},{28,4},{32,56},... | collective-permute-start | bytes 196616 | tf_op jit(solution)/shard_map/ppermute | solution.py:604
  59.1 0.0 collective-permute-done.18.one
  59.1 1.0 %collective-permute-done.19.two = bf16[2,128,128]{2,1,0:T(8,128)(2,1)S(1)} collective-permute-done((bf16[2,128,128]{2,1,0:T(8,128)(2,1)S(1)}, bf16[2,128,128]{2,1,0:T(8,128)(2,1)S(1)}, u32[]{:S(2)}, u32[]{:S(2)}) %collective-permute-start.19) | collective-permute-done | bytes 65568 | tf_op jit(solution)/shard_map/ppermute | solution.py:604
  60.1 1.0 %early.1.acc_ref = f32[128,4096]{1,0:T(8,128)S(1)} custom-call(bf16[4,128,128]{2,1,0:T(8,128)(2,1)S(1)} %get-tuple-element.60.keep, bf16[4,128,128]{2,1,0:T(8,128)(2,1)S(1)} %collective-permute-done.16.came, bf16[2,128,128]{2,1,0:T(8,128)(2,1)S(1)} %collective-permute-done.18.one, bf16[2,128,128]{2,1,0:T(8,128)(2,1)S(1)} %collective-permute-done.19.two, ...), custom_call_target="tpu_custom_call" | custom-call | flops 800000000 | bytes 8000000 | tf_op jit(solution)/shard_map/early/pallas_call | solution.py:581
  61.1 0.6 collective-permute-done.17.three
  61.7 0.4 late.1
  62.2 1.7 %collective-permute-start.20 = (bf16[32,2048]{1,0:T(8,128)(2,1)S(1)}, bf16[32,2048]{1,0:T(8,128)(2,1)S(1)}, u32[]{:S(2)}, u32[]{:S(2)}) collective-permute-start(bf16[32,2048]{1,0:T(8,128)(2,1)S(1)} %get-tuple-element.64), channel_id=1, source_target_pairs={{0,1},{1,2},{2,3},{3,0},{4,5},{5,6},{6,7},{7,4},{8,9},{9,10},{10,1... | collective-permute-start | bytes 393224 | tf_op jit(solution)/shard_map/ppermute | solution.py:648
  63.8 1.7 %collective-permute-start.21 = (bf16[32,2048]{1,0:T(8,128)(2,1)S(1)}, bf16[32,2048]{1,0:T(8,128)(2,1)S(1)}, u32[]{:S(2)}, u32[]{:S(2)}) collective-permute-start(bf16[32,2048]{1,0:T(8,128)(2,1)S(1)} %get-tuple-element.65), channel_id=1, source_target_pairs={{0,3},{1,0},{2,1},{3,2},{4,7},{5,4},{6,5},{7,6},{8,11},{9,8},{10,9... | collective-permute-start | bytes 393224 | tf_op jit(solution)/shard_map/ppermute | solution.py:648
  65.5 1.8 %collective-permute-start.23 = (bf16[32,2048]{1,0:T(8,128)(2,1)S(1)}, bf16[32,2048]{1,0:T(8,128)(2,1)S(1)}, u32[]{:S(2)}, u32[]{:S(2)}) collective-permute-start(bf16[32,2048]{1,0:T(8,128)(2,1)S(1)} %get-tuple-element.67), channel_id=1, source_target_pairs={{0,3},{1,0},{2,1},{3,2},{4,7},{5,4},{6,5},{7,6},{8,11},{9,8},{10,9... | collective-permute-start | bytes 393224 | tf_op jit(solution)/shard_map/ppermute | solution.py:648
  67.3 0.2 collective-permute-start.25
  67.5 0.9 %collective-permute-done.20 = bf16[32,2048]{1,0:T(8,128)(2,1)S(1)} collective-permute-done((bf16[32,2048]{1,0:T(8,128)(2,1)S(1)}, bf16[32,2048]{1,0:T(8,128)(2,1)S(1)}, u32[]{:S(2)}, u32[]{:S(2)}) %collective-permute-start.20) | collective-permute-done | bytes 131104 | tf_op jit(solution)/shard_map/ppermute | solution.py:648
  68.4 0.9 %collective-permute-done.21 = bf16[32,2048]{1,0:T(8,128)(2,1)S(1)} collective-permute-done((bf16[32,2048]{1,0:T(8,128)(2,1)S(1)}, bf16[32,2048]{1,0:T(8,128)(2,1)S(1)}, u32[]{:S(2)}, u32[]{:S(2)}) %collective-permute-start.21) | collective-permute-done | bytes 131104 | tf_op jit(solution)/shard_map/ppermute | solution.py:648
  69.4 1.5 %collective-permute-start.22 = (bf16[32,2048]{1,0:T(8,128)(2,1)S(1)}, bf16[32,2048]{1,0:T(8,128)(2,1)S(1)}, u32[]{:S(2)}, u32[]{:S(2)}) collective-permute-start(bf16[32,2048]{1,0:T(8,128)(2,1)S(1)} %add_convert_fusion.1), channel_id=1, source_target_pairs={{0,1},{1,2},{2,3},{3,0},{4,5},{5,6},{6,7},{7,4},{8,9},{9,10},{10,1... | collective-permute-start | bytes 393224 | tf_op jit(solution)/shard_map/ppermute | solution.py:648
  71.0 1.9 %collective-permute-start.24 = (bf16[32,2048]{1,0:T(8,128)(2,1)S(1)}, bf16[32,2048]{1,0:T(8,128)(2,1)S(1)}, u32[]{:S(2)}, u32[]{:S(2)}) collective-permute-start(bf16[32,2048]{1,0:T(8,128)(2,1)S(1)} %add_convert_fusion), channel_id=1, source_target_pairs={{0,3},{1,0},{2,1},{3,2},{4,7},{5,4},{6,5},{7,6},{8,11},{9,8},{10,9... | collective-permute-start | bytes 393224 | tf_op jit(solution)/shard_map/ppermute | solution.py:648
  72.8 0.0 collective-permute-done.23
  72.8 2.8 %collective-permute-done.22 = bf16[32,2048]{1,0:T(8,128)(2,1)S(1)} collective-permute-done((bf16[32,2048]{1,0:T(8,128)(2,1)S(1)}, bf16[32,2048]{1,0:T(8,128)(2,1)S(1)}, u32[]{:S(2)}, u32[]{:S(2)}) %collective-permute-start.22) | collective-permute-done | bytes 131104 | tf_op jit(solution)/shard_map/ppermute | solution.py:648
  75.7 0.0 collective-permute-done.25
  75.7 0.3 collective-permute-done.24
  76.0 0.8 fusion
  (31 shorter events, 0.3 us)
Async XLA Ops:
  1.4 1.5 %collective-permute-start.4 = (bf16[4,144,128]{2,1,0:T(8,128)(2,1)S(1)}, bf16[4,144,128]{2,1,0:T(8,128)(2,1)S(1)}, u32[]{:S(2)}, u32[]{:S(2)}) collective-permute-start(bf16[4,144,128]{2,1,0:T(8,128)(2,1)S(1)} %get-tuple-element.41), channel_id=1, source_target_pairs={{0,4},{4,0},{8,12},{12,8},{16,20},{20,16},{24,28},{28,24},{32,36},... | collective-permute-start | bytes 442376 | tf_op jit(solution)/shard_map/ppermute | solution.py:604
  1.5 6.4 %collective-permute-start = (bf16[4,256,128]{2,1,0:T(8,128)(2,1)S(1)}, bf16[4,256,128]{2,1,0:T(8,128)(2,1)S(1)}, u32[]{:S(2)}, u32[]{:S(2)}) collective-permute-start(bf16[4,256,128]{2,1,0:T(8,128)(2,1)S(1)} %get-tuple-element.39), channel_id=1, source_target_pairs={{0,4},{4,0},{8,12},{12,8},{16,20},{20,16},{24,28},{28,24},{32,36},... | collective-permute-start | bytes 786440 | tf_op jit(solution)/shard_map/ppermute | solution.py:604
  2.9 38.0 %copy-start = (f32[128]{0:T(128)S(1)}, f32[128]{0:T(128)}, u32[]{:S(2)}) copy-start(f32[128]{0:T(128)} %param.13) | copy-start | bytes 1540
  2.9 9.4 %collective-permute-start.5 = (bf16[2,144,128]{2,1,0:T(8,128)(2,1)S(1)}, bf16[2,144,128]{2,1,0:T(8,128)(2,1)S(1)}, u32[]{:S(2)}, u32[]{:S(2)}) collective-permute-start(bf16[2,144,128]{2,1,0:T(8,128)(2,1)S(1)} %pad_maximum_fusion), channel_id=1, source_target_pairs={{0,8},{4,12},{8,0},{12,4},{16,24},{20,28},{24,16},{28,20},{32,40},... | collective-permute-start | bytes 221192 | tf_op jit(solution)/shard_map/ppermute | solution.py:604
  4.5 8.4 %collective-permute-start.6 = (bf16[2,144,128]{2,1,0:T(8,128)(2,1)S(1)}, bf16[2,144,128]{2,1,0:T(8,128)(2,1)S(1)}, u32[]{:S(2)}, u32[]{:S(2)}) collective-permute-start(bf16[2,144,128]{2,1,0:T(8,128)(2,1)S(1)} %pad_maximum_fusion.1), channel_id=1, source_target_pairs={{0,16},{4,20},{8,24},{12,28},{16,0},{20,4},{24,8},{28,12},{32,48},... | collective-permute-start | bytes 221192 | tf_op jit(solution)/shard_map/ppermute | solution.py:604
  7.3 6.4 %collective-permute-start.7 = (bf16[2,144,128]{2,1,0:T(8,128)(2,1)S(1)}, bf16[2,144,128]{2,1,0:T(8,128)(2,1)S(1)}, u32[]{:S(2)}, u32[]{:S(2)}) collective-permute-start(bf16[2,144,128]{2,1,0:T(8,128)(2,1)S(1)} %pad_maximum_fusion.2), channel_id=1, source_target_pairs={{0,24},{4,28},{8,16},{12,20},{16,8},{20,12},{24,0},{28,4},{32,56},... | collective-permute-start | bytes 221192 | tf_op jit(solution)/shard_map/ppermute | solution.py:604
  7.9 8.5 %collective-permute-start.1 = (bf16[2,128,128]{2,1,0:T(8,128)(2,1)S(1)}, bf16[2,128,128]{2,1,0:T(8,128)(2,1)S(1)}, u32[]{:S(2)}, u32[]{:S(2)}) collective-permute-start(bf16[2,128,128]{2,1,0:T(8,128)(2,1)S(1)} %pad_maximum_fusion.3), channel_id=1, source_target_pairs={{0,8},{4,12},{8,0},{12,4},{16,24},{20,28},{24,16},{28,20},{32,40},... | collective-permute-start | bytes 196616 | tf_op jit(solution)/shard_map/ppermute | solution.py:604
  8.3 8.1 %collective-permute-start.2 = (bf16[2,128,128]{2,1,0:T(8,128)(2,1)S(1)}, bf16[2,128,128]{2,1,0:T(8,128)(2,1)S(1)}, u32[]{:S(2)}, u32[]{:S(2)}) collective-permute-start(bf16[2,128,128]{2,1,0:T(8,128)(2,1)S(1)} %pad_maximum_fusion.4), channel_id=1, source_target_pairs={{0,16},{4,20},{8,24},{12,28},{16,0},{20,4},{24,8},{28,12},{32,48},... | collective-permute-start | bytes 196616 | tf_op jit(solution)/shard_map/ppermute | solution.py:604
  12.3 31.5 %copy-start.1 = (bf16[8,128,384]{2,1,0:T(8,128)(2,1)S(1)}, bf16[8,128,384]{2,1,0:T(8,128)(2,1)}, u32[]{:S(2)}) copy-start(bf16[8,128,384]{2,1,0:T(8,128)(2,1)} %weight_ref.5) | copy-start | bytes 2359300
  12.3 5.6 %collective-permute-start.3 = (bf16[2,128,128]{2,1,0:T(8,128)(2,1)S(1)}, bf16[2,128,128]{2,1,0:T(8,128)(2,1)S(1)}, u32[]{:S(2)}, u32[]{:S(2)}) collective-permute-start(bf16[2,128,128]{2,1,0:T(8,128)(2,1)S(1)} %pad_maximum_fusion.5), channel_id=1, source_target_pairs={{0,24},{4,28},{8,16},{12,20},{16,8},{20,12},{24,0},{28,4},{32,56},... | collective-permute-start | bytes 196616 | tf_op jit(solution)/shard_map/ppermute | solution.py:604
  17.9 42.3 %slice-start = ((s8[8388608]{0:T(1024)(128)(4,1)}), s8[4194304]{0:T(1024)(128)(4,1)S(1)}, s32[]{:S(2)}) async-start(s8[8388608]{0:T(1024)(128)(4,1)} %bitcast.1), calls=%async_computation | async-start | bytes 8388608
  19.0 11.5 %collective-permute-start.12 = (bf16[128,256]{1,0:T(8,128)(2,1)S(1)}, bf16[128,256]{1,0:T(8,128)(2,1)S(1)}, u32[]{:S(2)}, u32[]{:S(2)}) collective-permute-start(bf16[128,256]{1,0:T(8,128)(2,1)S(1)} %get-tuple-element.47.own_ref), channel_id=1, source_target_pairs={{0,64},{4,68},{8,72},{12,76},{16,80},{20,84},{24,88},{28,92},{32,9... | collective-permute-start | bytes 196616 | tf_op jit(solution)/shard_map/ppermute | solution.py:621
  22.5 7.9 %collective-permute-start.11 = (bf16[128,256]{1,0:T(8,128)(2,1)S(1)}, bf16[128,256]{1,0:T(8,128)(2,1)S(1)}, u32[]{:S(2)}, u32[]{:S(2)}) collective-permute-start(bf16[128,256]{1,0:T(8,128)(2,1)S(1)} %get-tuple-element.47.own_ref), channel_id=1, source_target_pairs={{0,32},{4,36},{8,40},{12,44},{16,48},{20,52},{24,56},{28,60},{32,6... | collective-permute-start | bytes 196616 | tf_op jit(solution)/shard_map/ppermute | solution.py:621
  25.5 7.9 %collective-permute-start.8 = (bf16[2,128,128]{2,1,0:T(8,128)(2,1)S(1)}, bf16[2,128,128]{2,1,0:T(8,128)(2,1)S(1)}, u32[]{:S(2)}, u32[]{:S(2)}) collective-permute-start(bf16[2,128,128]{2,1,0:T(8,128)(2,1)S(1)} %pad_maximum_fusion.6), channel_id=1, source_target_pairs={{0,8},{4,12},{8,0},{12,4},{16,24},{20,28},{24,16},{28,20},{32,40},... | collective-permute-start | bytes 196616 | tf_op jit(solution)/shard_map/ppermute | solution.py:604
  25.6 7.8 %collective-permute-start.9 = (bf16[2,128,128]{2,1,0:T(8,128)(2,1)S(1)}, bf16[2,128,128]{2,1,0:T(8,128)(2,1)S(1)}, u32[]{:S(2)}, u32[]{:S(2)}) collective-permute-start(bf16[2,128,128]{2,1,0:T(8,128)(2,1)S(1)} %pad_maximum_fusion.7), channel_id=1, source_target_pairs={{0,16},{4,20},{8,24},{12,28},{16,0},{20,4},{24,8},{28,12},{32,48},... | collective-permute-start | bytes 196616 | tf_op jit(solution)/shard_map/ppermute | solution.py:604
  27.7 5.7 %collective-permute-start.10 = (bf16[2,128,128]{2,1,0:T(8,128)(2,1)S(1)}, bf16[2,128,128]{2,1,0:T(8,128)(2,1)S(1)}, u32[]{:S(2)}, u32[]{:S(2)}) collective-permute-start(bf16[2,128,128]{2,1,0:T(8,128)(2,1)S(1)} %pad_maximum_fusion.8), channel_id=1, source_target_pairs={{0,24},{4,28},{8,16},{12,20},{16,8},{20,12},{24,0},{28,4},{32,56},... | collective-permute-start | bytes 196616 | tf_op jit(solution)/shard_map/ppermute | solution.py:604
  30.8 10.0 %collective-permute-start.14 = (bf16[128,256]{1,0:T(8,128)(2,1)S(1)}, bf16[128,256]{1,0:T(8,128)(2,1)S(1)}, u32[]{:S(2)}, u32[]{:S(2)}) collective-permute-start(bf16[128,256]{1,0:T(8,128)(2,1)S(1)} %get-tuple-element.56), channel_id=1, source_target_pairs={{0,96},{4,100},{8,104},{12,108},{16,112},{20,116},{24,120},{28,124... | collective-permute-start | bytes 196616 | tf_op jit(solution)/shard_map/ppermute | solution.py:621
  32.7 8.1 %collective-permute-start.13 = (bf16[128,256]{1,0:T(8,128)(2,1)S(1)}, bf16[128,256]{1,0:T(8,128)(2,1)S(1)}, u32[]{:S(2)}, u32[]{:S(2)}) collective-permute-start(bf16[128,256]{1,0:T(8,128)(2,1)S(1)} %get-tuple-element.56), channel_id=1, source_target_pairs={{0,192},{4,196},{8,200},{12,204},{16,208},{20,212},{24,216},{28,22... | collective-permute-start | bytes 196616 | tf_op jit(solution)/shard_map/ppermute | solution.py:621
  40.8 19.3 %slice-start.1 = ((s8[8388608]{0:T(1024)(128)(4,1)}), s8[4194304]{0:T(1024)(128)(4,1)S(1)}, s32[]{:S(2)}) async-start(s8[8388608]{0:T(1024)(128)(4,1)} %bitcast.1), calls=%async_computation.1 | async-start | bytes 8388608
  41.5 9.6 %collective-permute-start.15 = (bf16[1024,128]{1,0:T(8,128)(2,1)S(1)}, bf16[1024,128]{1,0:T(8,128)(2,1)S(1)}, u32[]{:S(2)}, u32[]{:S(2)}) collective-permute-start(bf16[1024,128]{1,0:T(8,128)(2,1)S(1)} %norm.1.normed_ref), channel_id=1, source_target_pairs={{0,32},{4,36},{8,40},{12,44},{16,48},{20,52},{24,56},{28,60},{32,6... | collective-permute-start | bytes 786440 | tf_op jit(solution)/shard_map/ppermute | solution.py:621
  52.6 1.4 %collective-permute-start.16 = (bf16[4,128,128]{2,1,0:T(8,128)(2,1)S(1)}, bf16[4,128,128]{2,1,0:T(8,128)(2,1)S(1)}, u32[]{:S(2)}, u32[]{:S(2)}) collective-permute-start(bf16[4,128,128]{2,1,0:T(8,128)(2,1)S(1)} %get-tuple-element.61), channel_id=1, source_target_pairs={{0,4},{4,0},{8,12},{12,8},{16,20},{20,16},{24,28},{28,24},{32,36},... | collective-permute-start | bytes 393224 | tf_op jit(solution)/shard_map/ppermute | solution.py:604
  54.1 5.0 %collective-permute-start.18 = (bf16[2,128,128]{2,1,0:T(8,128)(2,1)S(1)}, bf16[2,128,128]{2,1,0:T(8,128)(2,1)S(1)}, u32[]{:S(2)}, u32[]{:S(2)}) collective-permute-start(bf16[2,128,128]{2,1,0:T(8,128)(2,1)S(1)} %pad_maximum_fusion.10), channel_id=1, source_target_pairs={{0,8},{4,12},{8,0},{12,4},{16,24},{20,28},{24,16},{28,20},{32,40},... | collective-permute-start | bytes 196616 | tf_op jit(solution)/shard_map/ppermute | solution.py:604
  54.2 5.9 %collective-permute-start.19 = (bf16[2,128,128]{2,1,0:T(8,128)(2,1)S(1)}, bf16[2,128,128]{2,1,0:T(8,128)(2,1)S(1)}, u32[]{:S(2)}, u32[]{:S(2)}) collective-permute-start(bf16[2,128,128]{2,1,0:T(8,128)(2,1)S(1)} %pad_maximum_fusion.11), channel_id=1, source_target_pairs={{0,16},{4,20},{8,24},{12,28},{16,0},{20,4},{24,8},{28,12},{32,48},... | collective-permute-start | bytes 196616 | tf_op jit(solution)/shard_map/ppermute | solution.py:604
  56.2 5.6 %collective-permute-start.17 = (bf16[2,128,128]{2,1,0:T(8,128)(2,1)S(1)}, bf16[2,128,128]{2,1,0:T(8,128)(2,1)S(1)}, u32[]{:S(2)}, u32[]{:S(2)}) collective-permute-start(bf16[2,128,128]{2,1,0:T(8,128)(2,1)S(1)} %pad_maximum_fusion.9), channel_id=1, source_target_pairs={{0,24},{4,28},{8,16},{12,20},{16,8},{20,12},{24,0},{28,4},{32,56},... | collective-permute-start | bytes 196616 | tf_op jit(solution)/shard_map/ppermute | solution.py:604
  62.2 6.3 %collective-permute-start.20 = (bf16[32,2048]{1,0:T(8,128)(2,1)S(1)}, bf16[32,2048]{1,0:T(8,128)(2,1)S(1)}, u32[]{:S(2)}, u32[]{:S(2)}) collective-permute-start(bf16[32,2048]{1,0:T(8,128)(2,1)S(1)} %get-tuple-element.64), channel_id=1, source_target_pairs={{0,1},{1,2},{2,3},{3,0},{4,5},{5,6},{6,7},{7,4},{8,9},{9,10},{10,1... | collective-permute-start | bytes 393224 | tf_op jit(solution)/shard_map/ppermute | solution.py:648
  63.8 5.5 %collective-permute-start.21 = (bf16[32,2048]{1,0:T(8,128)(2,1)S(1)}, bf16[32,2048]{1,0:T(8,128)(2,1)S(1)}, u32[]{:S(2)}, u32[]{:S(2)}) collective-permute-start(bf16[32,2048]{1,0:T(8,128)(2,1)S(1)} %get-tuple-element.65), channel_id=1, source_target_pairs={{0,3},{1,0},{2,1},{3,2},{4,7},{5,4},{6,5},{7,6},{8,11},{9,8},{10,9... | collective-permute-start | bytes 393224 | tf_op jit(solution)/shard_map/ppermute | solution.py:648
  65.5 7.3 %collective-permute-start.23 = (bf16[32,2048]{1,0:T(8,128)(2,1)S(1)}, bf16[32,2048]{1,0:T(8,128)(2,1)S(1)}, u32[]{:S(2)}, u32[]{:S(2)}) collective-permute-start(bf16[32,2048]{1,0:T(8,128)(2,1)S(1)} %get-tuple-element.67), channel_id=1, source_target_pairs={{0,3},{1,0},{2,1},{3,2},{4,7},{5,4},{6,5},{7,6},{8,11},{9,8},{10,9... | collective-permute-start | bytes 393224 | tf_op jit(solution)/shard_map/ppermute | solution.py:648
  67.3 8.4 %collective-permute-start.25 = (bf16[32,2048]{1,0:T(8,128)(2,1)S(1)}, bf16[32,2048]{1,0:T(8,128)(2,1)S(1)}, u32[]{:S(2)}, u32[]{:S(2)}) collective-permute-start(bf16[32,2048]{1,0:T(8,128)(2,1)S(1)} %get-tuple-element.70), channel_id=1, source_target_pairs={{0,1},{1,2},{2,3},{3,0},{4,5},{5,6},{6,7},{7,4},{8,9},{9,10},{10,1... | collective-permute-start | bytes 393224 | tf_op jit(solution)/shard_map/ppermute | solution.py:648
  69.4 6.3 %collective-permute-start.22 = (bf16[32,2048]{1,0:T(8,128)(2,1)S(1)}, bf16[32,2048]{1,0:T(8,128)(2,1)S(1)}, u32[]{:S(2)}, u32[]{:S(2)}) collective-permute-start(bf16[32,2048]{1,0:T(8,128)(2,1)S(1)} %add_convert_fusion.1), channel_id=1, source_target_pairs={{0,1},{1,2},{2,3},{3,0},{4,5},{5,6},{6,7},{7,4},{8,9},{9,10},{10,1... | collective-permute-start | bytes 393224 | tf_op jit(solution)/shard_map/ppermute | solution.py:648
  71.0 5.0 %collective-permute-start.24 = (bf16[32,2048]{1,0:T(8,128)(2,1)S(1)}, bf16[32,2048]{1,0:T(8,128)(2,1)S(1)}, u32[]{:S(2)}, u32[]{:S(2)}) collective-permute-start(bf16[32,2048]{1,0:T(8,128)(2,1)S(1)} %add_convert_fusion), channel_id=1, source_target_pairs={{0,3},{1,0},{2,1},{3,2},{4,7},{5,4},{6,5},{7,6},{8,11},{9,8},{10,9... | collective-permute-start | bytes 393224 | tf_op jit(solution)/shard_map/ppermute | solution.py:648
